TPU v7x, 32 devices: a whole 2x2x4 slice. The times are simulated.
32 devices in a mesh: dp: 16 (over z, y, core), ctx: 2 (over x).
Axes of the slice: x: 2, y: 2, z: 4, core: 2. Of those that a mesh axis runs over, the one named last changes fastest.
Arguments:
- inputs: bfloat16 [16, 256, 1280], P(None, ('dp', 'ctx')), may hold values from -6 to 6
- cotangent: bfloat16 [16, 256, 1280], P(None, ('dp', 'ctx')), may hold values from -6 to 6
- w_query: float32 [1280, 1280], P(('dp', 'ctx')), may hold values from -0.15625 to 0.15625
- w_key: float32 [1280, 1280], P(('dp', 'ctx')), may hold values from -0.15625 to 0.15625
- w_value: float32 [1280, 1280], P(('dp', 'ctx')), may hold values from -0.15625 to 0.15625
- w_output: float32 [1280, 1280], P(('dp', 'ctx')), may hold values from -1.25 to 1.25
- w_up: float32 [1280, 1280], P(('dp', 'ctx')), may hold values from -0.15625 to 0.15625
- w_down: float32 [1280, 1280], P(('dp', 'ctx')), may hold values from -0.15625 to 0.15625
- attn_gain: float32 [1280], P(('dp', 'ctx')), may hold values from 0.1 to 1.9
- mlp_gain: float32 [1280], P(('dp', 'ctx')), may hold values from 0.1 to 1.9
- query_scale: float32 [1280], P(('dp', 'ctx')), may hold values from -1 to 1
- deal: int32 [16], replicated, may hold values from 0 to 15, each once
- lengths: int32 [16], replicated, may hold values from 64 to 256, as said below
Outputs:
- outputs: bfloat16 [16, 256, 1280], P(None, ('dp', 'ctx'))
- grad_inputs: bfloat16 [16, 256, 1280], P(None, ('dp', 'ctx'))
- grad_w_query: float32 [1280, 1280], P(('dp', 'ctx'))
- grad_w_key: float32 [1280, 1280], P(('dp', 'ctx'))
- grad_w_value: float32 [1280, 1280], P(('dp', 'ctx'))
- grad_w_output: float32 [1280, 1280], P(('dp', 'ctx'))
- grad_w_up: float32 [1280, 1280], P(('dp', 'ctx'))
- grad_w_down: float32 [1280, 1280], P(('dp', 'ctx'))
- grad_attn_gain: float32 [1280], P(('dp', 'ctx'))
- grad_mlp_gain: float32 [1280], P(('dp', 'ctx'))
- grad_query_scale: float32 [1280], P(('dp', 'ctx'))
Inputs may be any that keep to these rules, and one draw needn't show every extreme that they name: lengths[i] is the length of sequence deal[i]; one sequence has exactly 256.
All inputs are finite; a program needn't handle non-finite values.
Results may differ from a plain program's by a relative error of at most 0.028.
Values may be sent and summed in bfloat16 or wider, within the bound.
No kernel may reach another device: no remote copies, remote signals or barrier semaphores. Data moves between devices by JAX's collectives and lax.ppermute only.
A program may use at most 256 MiB of HBM per device.

v0:
```python
import math

import jax
import jax.numpy as jnp
from jax import lax
from jax.sharding import PartitionSpec as P

H = 16
HD = 80


def mult_trans(left, right):
    return lax.dot_general(
        left, right, (((1,), (1,)), ((), ())), preferred_element_type=jnp.float32
    )


def trans_mult(left, right):
    return lax.dot_general(
        left, right, (((0,), (0,)), ((), ())), preferred_element_type=jnp.float32
    )


def position_of(index, local_rows, piece_rows, groups):
    column = index // local_rows
    within = index % local_rows
    return (within // piece_rows * groups + column) * piece_rows + within % piece_rows


def norm_back(grad_hidden, normed, inverse, gain_value):
    grad_normed = grad_hidden * gain_value
    return inverse * (grad_normed - normed * jnp.mean(grad_normed * normed, axis=1, keepdims=True))


def per_device(
    inputs,
    cotangent,
    w_query,
    w_key,
    w_value,
    w_output,
    w_up,
    w_down,
    attn_gain,
    mlp_gain,
    query_scale,
    deal,
    lengths,
):
    groups = lax.axis_size("ctx")
    group_index = lax.axis_index("dp")
    ctx_index = lax.axis_index("ctx")
    head_count = H
    head_dim = HD
    piece_rows = inputs.shape[1]
    dealt_in = jnp.take(inputs, deal, axis=0)
    dealt_cot = jnp.take(cotangent, deal, axis=0)
    local_in, local_cot = (
        lax.all_to_all(dealt_in, "dp", split_axis=0, concat_axis=1, tiled=True),
        lax.all_to_all(dealt_cot, "dp", split_axis=0, concat_axis=1, tiled=True),
    )
    seq_count, local_rows, model_width = local_in.shape
    padded = local_rows * groups
    token_count = seq_count * local_rows
    my_lengths = lax.dynamic_slice_in_dim(lengths, group_index * seq_count, seq_count, 0)
    query_pos = position_of(
        ctx_index * local_rows + jnp.arange(local_rows, dtype=jnp.int32),
        local_rows,
        piece_rows,
        groups,
    )
    flat_in = local_in.reshape(token_count, model_width).astype(jnp.float32)
    flat_cot = local_cot.reshape(token_count, model_width)
    lowered = (
        w_query.astype(jnp.bfloat16),
        w_key.astype(jnp.bfloat16),
        w_value.astype(jnp.bfloat16),
        w_output.astype(jnp.bfloat16),
        w_up.astype(jnp.bfloat16),
        w_down.astype(jnp.bfloat16),
        attn_gain.astype(jnp.bfloat16),
        mlp_gain.astype(jnp.bfloat16),
        query_scale.astype(jnp.bfloat16),
    )
    gathered = (
        lax.all_gather(lowered[0], ("dp", "ctx"), axis=0, tiled=True),
        lax.all_gather(lowered[1], ("dp", "ctx"), axis=0, tiled=True),
        lax.all_gather(lowered[2], ("dp", "ctx"), axis=0, tiled=True),
        lax.all_gather(lowered[3], ("dp", "ctx"), axis=0, tiled=True),
        lax.all_gather(lowered[4], ("dp", "ctx"), axis=0, tiled=True),
        lax.all_gather(lowered[5], ("dp", "ctx"), axis=0, tiled=True),
        lax.all_gather(lowered[6], ("dp", "ctx"), axis=0, tiled=True),
        lax.all_gather(lowered[7], ("dp", "ctx"), axis=0, tiled=True),
        lax.all_gather(lowered[8], ("dp", "ctx"), axis=0, tiled=True),
    )
    (
        query_full,
        key_full,
        value_full,
        output_full,
        up_full,
        down_full,
        gain_one,
        gain_two,
        scale_raw,
    ) = gathered
    inv_one = lax.rsqrt(jnp.mean(flat_in * flat_in, axis=1, keepdims=True) + 1e-06)
    normed_one = flat_in * inv_one
    hidden_one = (normed_one * gain_one.astype(jnp.float32)).astype(jnp.bfloat16)
    scale_param = scale_raw.astype(jnp.float32)
    query_mult = 1.442695041 / math.sqrt(head_dim) * jax.nn.softplus(scale_param)
    query_pre = jnp.dot(hidden_one, query_full, preferred_element_type=jnp.float32)
    queries = (query_pre * query_mult).astype(jnp.bfloat16)
    keys_local = jnp.dot(hidden_one, key_full, preferred_element_type=jnp.float32).astype(
        jnp.bfloat16
    )
    values_local = jnp.dot(hidden_one, value_full, preferred_element_type=jnp.float32).astype(
        jnp.bfloat16
    )
    four_shape = (seq_count, local_rows, head_count, head_dim)
    query_four = queries.reshape(four_shape)
    keys_three = keys_local.reshape(seq_count, local_rows, model_width)
    values_three = values_local.reshape(seq_count, local_rows, model_width)

    def live_between(row_pos, key_pos):
        allowed = (key_pos[None, None, :] <= row_pos[None, :, None]) & (
            key_pos[None, None, :] < my_lengths[:, None, None]
        )
        return allowed[:, :, None, :]

    def live_mask(key_pos):
        return live_between(query_pos, key_pos)

    def attend_block(state_now, key_block, value_block, first_row):
        run_max, run_sum, run_acc = state_now
        block_len = key_block.shape[1]
        key_pos = position_of(
            first_row + jnp.arange(block_len, dtype=jnp.int32), local_rows, piece_rows, groups
        )
        key_four = key_block.reshape(seq_count, block_len, head_count, head_dim)
        value_four = value_block.reshape(seq_count, block_len, head_count, head_dim)
        scores = jnp.einsum(
            "srhd,skhd->srhk", query_four, key_four, preferred_element_type=jnp.float32
        )
        allowed = live_mask(key_pos)
        masked = jnp.where(allowed, scores, -1e30)
        new_max = jnp.maximum(run_max, jnp.max(masked, axis=3))
        weights_now = jnp.exp(jnp.where(allowed, masked - new_max[..., None], -1e30))
        factor = jnp.exp(run_max - new_max)
        new_sum = run_sum * factor + jnp.sum(weights_now, axis=3)
        added = jnp.einsum(
            "srhk,skhd->srhd",
            weights_now.astype(jnp.bfloat16),
            value_four,
            preferred_element_type=jnp.float32,
        )
        return (new_max, new_sum, run_acc * factor[..., None] + added)

    start_state = (
        jnp.full((seq_count, local_rows, head_count), -1e30, jnp.float32),
        jnp.zeros((seq_count, local_rows, head_count), jnp.float32),
        jnp.zeros(four_shape, jnp.float32),
    )
    key_piece = lax.all_gather(keys_three, "ctx", axis=1, tiled=True)
    value_piece = lax.all_gather(values_three, "ctx", axis=1, tiled=True)
    piece_len = key_piece.shape[1]
    fold_block_len = 512 if piece_len % 512 == 0 else piece_len

    def one_block(state_now, block_index):
        offset = block_index * fold_block_len
        key_block = lax.dynamic_slice_in_dim(key_piece, offset, fold_block_len, 1)
        value_block = lax.dynamic_slice_in_dim(value_piece, offset, fold_block_len, 1)
        return (attend_block(state_now, key_block, value_block, offset), None)

    result_state, unused = lax.scan(
        one_block, start_state, jnp.arange(piece_len // fold_block_len, dtype=jnp.int32)
    )
    run_max, run_sum, run_acc = result_state
    log_total = run_max + jnp.log(run_sum)
    attn_exact = run_acc / run_sum[..., None]
    attended = attn_exact.reshape(token_count, model_width).astype(jnp.bfloat16)
    middle = flat_in + jnp.dot(attended, output_full, preferred_element_type=jnp.float32)
    inv_two = lax.rsqrt(jnp.mean(middle * middle, axis=1, keepdims=True) + 1e-06)
    normed_two = middle * inv_two
    hidden_two = (normed_two * gain_two.astype(jnp.float32)).astype(jnp.bfloat16)
    up_pre = jnp.dot(hidden_two, up_full, preferred_element_type=jnp.float32)
    active = jax.nn.silu(up_pre).astype(jnp.bfloat16)
    result = (middle + jnp.dot(active, down_full, preferred_element_type=jnp.float32)).astype(
        jnp.bfloat16
    )
    back_weights = (
        lax.all_gather(lowered[0], ("dp", "ctx"), axis=0, tiled=True),
        lax.all_gather(lowered[1], ("dp", "ctx"), axis=0, tiled=True),
        lax.all_gather(lowered[2], ("dp", "ctx"), axis=0, tiled=True),
        lax.all_gather(lowered[3], ("dp", "ctx"), axis=0, tiled=True),
        lax.all_gather(lowered[4], ("dp", "ctx"), axis=0, tiled=True),
        lax.all_gather(lowered[5], ("dp", "ctx"), axis=0, tiled=True),
        lax.all_gather(lowered[6], ("dp", "ctx"), axis=0, tiled=True),
        lax.all_gather(lowered[7], ("dp", "ctx"), axis=0, tiled=True),
        lax.all_gather(lowered[8], ("dp", "ctx"), axis=0, tiled=True),
    )
    (
        query_back,
        key_back,
        value_back,
        output_back,
        up_back,
        down_back,
        gain_one_back,
        gain_two_back,
        scale_back,
    ) = back_weights
    cot_wide = flat_cot.astype(jnp.float32)
    grad_down = trans_mult(active, flat_cot)
    grad_active = mult_trans(flat_cot, down_back)
    sigma_up = jax.nn.sigmoid(up_pre)
    grad_up_pre = (grad_active * sigma_up * (1.0 + up_pre * (1.0 - sigma_up))).astype(jnp.bfloat16)
    grad_up = trans_mult(hidden_two, grad_up_pre)
    grad_hidden_two = mult_trans(grad_up_pre, up_back)
    grad_gain_two = jnp.sum(grad_hidden_two * normed_two, axis=0)
    grad_middle = cot_wide + norm_back(
        grad_hidden_two, normed_two, inv_two, gain_two_back.astype(jnp.float32)
    )
    grad_middle_low = grad_middle.astype(jnp.bfloat16)
    grad_output = trans_mult(attended, grad_middle_low)
    grad_attended = mult_trans(grad_middle_low, output_back).astype(jnp.bfloat16)
    grad_att_four = grad_attended.reshape(four_shape)
    delta_rows = jnp.sum(grad_att_four.astype(jnp.float32) * attn_exact, axis=3)
    key_all, value_all = (
        lax.all_gather(keys_three, "ctx", axis=1, tiled=True),
        lax.all_gather(values_three, "ctx", axis=1, tiled=True),
    )
    block_len = min(512, padded)

    def back_block(block_index, state_now):
        grad_query, grad_key_all, grad_value_all = state_now
        offset = block_index * block_len
        key_block = lax.dynamic_slice_in_dim(key_all, offset, block_len, 1).reshape(
            seq_count, block_len, head_count, head_dim
        )
        value_block = lax.dynamic_slice_in_dim(value_all, offset, block_len, 1).reshape(
            seq_count, block_len, head_count, head_dim
        )
        key_pos = position_of(
            offset + jnp.arange(block_len, dtype=jnp.int32), local_rows, piece_rows, groups
        )
        scores = jnp.einsum(
            "srhd,skhd->srhk", query_four, key_block, preferred_element_type=jnp.float32
        )
        probs = jnp.exp(jnp.where(live_mask(key_pos), scores - log_total[..., None], -1e30))
        grad_value_block = jnp.einsum(
            "srhk,srhd->skhd",
            probs.astype(jnp.bfloat16),
            grad_att_four,
            preferred_element_type=jnp.float32,
        )
        grad_probs = jnp.einsum(
            "srhd,skhd->srhk", grad_att_four, value_block, preferred_element_type=jnp.float32
        )
        grad_scores = (probs * (grad_probs - delta_rows[..., None])).astype(jnp.bfloat16)
        grad_query = grad_query + jnp.einsum(
            "srhk,skhd->srhd", grad_scores, key_block, preferred_element_type=jnp.float32
        )
        grad_key_block = jnp.einsum(
            "srhk,srhd->skhd", grad_scores, query_four, preferred_element_type=jnp.float32
        )
        grad_key_all = lax.dynamic_update_slice_in_dim(
            grad_key_all, grad_key_block.reshape(seq_count, block_len, model_width), offset, 1
        )
        grad_value_all = lax.dynamic_update_slice_in_dim(
            grad_value_all, grad_value_block.reshape(seq_count, block_len, model_width), offset, 1
        )
        return (grad_query, grad_key_all, grad_value_all)

    zero_all = jnp.zeros((seq_count, padded, model_width), jnp.float32)
    grad_query, grad_key_all, grad_value_all = lax.fori_loop(
        0, padded // block_len, back_block, (jnp.zeros(four_shape, jnp.float32), zero_all, zero_all)
    )
    grad_key_mine, grad_value_mine = (
        lax.psum_scatter(
            grad_key_all.astype(jnp.bfloat16), "ctx", scatter_dimension=1, tiled=True
        ).astype(jnp.float32),
        lax.psum_scatter(
            grad_value_all.astype(jnp.bfloat16), "ctx", scatter_dimension=1, tiled=True
        ).astype(jnp.float32),
    )
    grad_query_flat = grad_query.reshape(token_count, model_width)
    grad_query_pre = (grad_query_flat * query_mult).astype(jnp.bfloat16)
    grad_scale = (
        1.442695041
        / math.sqrt(head_dim)
        * jax.nn.sigmoid(scale_back.astype(jnp.float32))
        * jnp.sum(grad_query_flat * query_pre, axis=0)
    )
    grad_key_low = grad_key_mine.reshape(token_count, model_width).astype(jnp.bfloat16)
    grad_value_low = grad_value_mine.reshape(token_count, model_width).astype(jnp.bfloat16)
    grad_wq = trans_mult(hidden_one, grad_query_pre)
    grad_wk = trans_mult(hidden_one, grad_key_low)
    grad_wv = trans_mult(hidden_one, grad_value_low)
    grad_hidden_one = (
        mult_trans(grad_query_pre, query_back)
        + mult_trans(grad_key_low, key_back)
        + mult_trans(grad_value_low, value_back)
    )
    grad_gain_one = jnp.sum(grad_hidden_one * normed_one, axis=0)
    grad_in = grad_middle + norm_back(
        grad_hidden_one, normed_one, inv_one, gain_one_back.astype(jnp.float32)
    )
    matrix_stack = jnp.stack([grad_wq, grad_wk, grad_wv, grad_output, grad_up, grad_down], axis=0)
    vector_stack = jnp.stack([grad_gain_one, grad_gain_two, grad_scale], axis=0)
    matrix_sums, vector_sums = (
        lax.psum_scatter(matrix_stack, ("dp", "ctx"), scatter_dimension=1, tiled=True),
        lax.psum_scatter(vector_stack, ("dp", "ctx"), scatter_dimension=1, tiled=True),
    )
    out_local = result.reshape(seq_count, local_rows, model_width)
    grad_local = grad_in.astype(jnp.bfloat16).reshape(seq_count, local_rows, model_width)
    back_out, back_grad = (
        lax.all_to_all(out_local, "dp", split_axis=1, concat_axis=0, tiled=True),
        lax.all_to_all(grad_local, "dp", split_axis=1, concat_axis=0, tiled=True),
    )
    undo_order = jnp.zeros_like(deal).at[deal].set(jnp.arange(deal.shape[0], dtype=jnp.int32))
    final_out = jnp.take(back_out, undo_order, axis=0)
    final_grad = jnp.take(back_grad, undo_order, axis=0)
    return (
        final_out,
        final_grad,
        matrix_sums[0],
        matrix_sums[1],
        matrix_sums[2],
        matrix_sums[3],
        matrix_sums[4],
        matrix_sums[5],
        vector_sums[0],
        vector_sums[1],
        vector_sums[2],
    )


def solution(mesh):
    placed = (
        P(None, ("dp", "ctx"), None),
        P(None, ("dp", "ctx"), None),
        P(("dp", "ctx"), None),
        P(("dp", "ctx"), None),
        P(("dp", "ctx"), None),
        P(("dp", "ctx"), None),
        P(("dp", "ctx"), None),
        P(("dp", "ctx"), None),
        P(("dp", "ctx")),
        P(("dp", "ctx")),
        P(("dp", "ctx")),
        P(),
        P(),
    )
    return jax.shard_map(
        per_device,
        mesh=mesh,
        in_specs=placed,
        out_specs=(
            P(None, ("dp", "ctx"), None),
            P(None, ("dp", "ctx"), None),
            P(("dp", "ctx"), None),
            P(("dp", "ctx"), None),
            P(("dp", "ctx"), None),
            P(("dp", "ctx"), None),
            P(("dp", "ctx"), None),
            P(("dp", "ctx"), None),
            P(("dp", "ctx")),
            P(("dp", "ctx")),
            P(("dp", "ctx")),
        ),
        check_vma=False,
    )
```

profile of v0, /device:TPU:0, one launch (start us, length us, event | category | flops | bytes accessed | tf_op | source)
XLA Modules:
  0.0 829.5 jit_solution(9876260089558337992)
XLA Ops:
  7.3 1.6 convert_element_type.200
  9.0 1.6 convert_element_type.194
  10.7 1.6 convert_element_type.196
  12.3 1.6 convert_element_type.205
  14.0 1.6 convert_element_type.209
  15.6 1.6 convert_element_type.211
  19.8 1.0 broadcast_select_fusion.2
  20.7 7.4 all-to-all-start
  30.2 41.7 %all-reduce.4 = (bf16[1280]{0:T(1024)(128)(2,1)S(1)}, bf16[1280]{0:T(1024)(128)(2,1)S(1)}, bf16[1280]{0:T(1024)(128)(2,1)S(1)}) all-reduce(bf16[1280]{0:T(1024)(128)(2,1)S(1)} %dynamic-update-slice, bf16[1280]{0:T(1024)(128)(2,1)S(1)} %dynamic-update-slice.1, ...), channel_id=1, replica_groups=mesh['dp'=16,'ctx'=2] {'dp','ctx'}, use_global_device_ids=true, to_apply=%add | all-reduce | flops 3840 | bytes 15360
  72.1 5.0 all-to-all-start.2
  77.4 2.6 convolution_convert_fusion.1
  80.0 11.5 %all-gather.1 = bf16[256,1280]{1,0:T(8,128)(2,1)S(1)} all-gather(bf16[128,1280]{1,0:T(8,128)(2,1)S(1)} %convolution_convert_fusion.1), channel_id=3, replica_groups=mesh['dp'=16,'ctx'=2] {'ctx'}, dimensions={0}, use_global_device_ids=true | all-gather | bytes 983040 | tf_op jit(solution)/shard_map/all_gather | solution.py:165
  91.5 1.1 copy.64
  92.6 43.8 %all-gather.9.cloned.1.call-done = bf16[1280,1280]{1,0:T(8,128)(2,1)} async-done(((bf16[40,1280]{1,0:T(8,128)(2,1)}), bf16[1280,1280]{1,0:T(8,128)(2,1)}) %all-gather.9.cloned.1.call-update) | async-done | bytes 3276816 | tf_op jit(solution)/shard_map/all_gather | solution.py:87
  136.4 2.6 convolution_convert_fusion.2
  138.9 10.7 %all-gather = bf16[256,1280]{1,0:T(8,128)(2,1)S(1)} all-gather(bf16[128,1280]{1,0:T(8,128)(2,1)S(1)} %convolution_convert_fusion.2), channel_id=2, replica_groups=mesh['dp'=16,'ctx'=2] {'ctx'}, dimensions={0}, use_global_device_ids=true | all-gather | bytes 983040 | tf_op jit(solution)/shard_map/all_gather | solution.py:164
  149.9 48.1 %all-gather.11.cloned.1.call-done = bf16[1280,1280]{1,0:T(8,128)(2,1)} async-done(((bf16[40,1280]{1,0:T(8,128)(2,1)}), bf16[1280,1280]{1,0:T(8,128)(2,1)}) %all-gather.11.cloned.1.call-update) | async-done | bytes 3276816 | tf_op jit(solution)/shard_map/all_gather | solution.py:86
  198.1 3.4 multiply_convert_fusion.3
  202.4 1.5 fusion.14
  204.4 2.7 fusion.88
  207.0 52.6 %all-gather.15.cloned.1.call-done = bf16[1280,1280]{1,0:T(8,128)(2,1)} async-done(((bf16[40,1280]{1,0:T(8,128)(2,1)}), bf16[1280,1280]{1,0:T(8,128)(2,1)}) %all-gather.15.cloned.1.call-update) | async-done | bytes 3276816 | tf_op jit(solution)/shard_map/all_gather | solution.py:89
  259.6 2.8 multiply_reduce_fusion.4
  262.4 58.8 %all-gather.17.cloned.1.call-done = bf16[1280,1280]{1,0:T(8,128)(2,1)} async-done(((bf16[40,1280]{1,0:T(8,128)(2,1)}), bf16[1280,1280]{1,0:T(8,128)(2,1)}) %all-gather.17.cloned.1.call-update) | async-done | bytes 3276816 | tf_op jit(solution)/shard_map/all_gather | solution.py:90
  321.2 3.4 fusion.83
  324.6 58.2 %all-gather.19.cloned.1.call-done = bf16[1280,1280]{1,0:T(8,128)(2,1)} async-done(((bf16[40,1280]{1,0:T(8,128)(2,1)}), bf16[1280,1280]{1,0:T(8,128)(2,1)}) %all-gather.19.cloned.1.call-update) | async-done | bytes 3276816 | tf_op jit(solution)/shard_map/all_gather | solution.py:91
  382.8 3.4 fusion.8
  386.2 1.3 multiply_reduce_fusion.1
  388.7 1.9 convolution_convert_fusion
  390.6 1.2 copy.67
  391.8 2.0 copy.68
  393.8 1.4 multiply_reduce_fusion.2
  395.2 1.9 fusion.18
  397.1 1.0 copy-done.8
  398.0 1.3 convolution_convert_fusion.4
  399.4 3.7 copy.79
  403.1 2.2 copy.96
  405.4 1.4 convolution_convert_fusion.3
  406.9 3.9 copy.81
  410.8 2.2 copy.95
  413.4 1.2 fusion.46
  414.5 3.8 fusion.5
  418.4 2.0 reduce-scatter.11.cloned.1.call-done
  420.4 1.3 reshape_bitcast_fusion.1
  422.3 16.5 %reduce-scatter.13.cloned.1.call-done = bf16[128,1280]{1,0:T(8,128)(2,1)} async-done(((bf16[256,1280]{1,0:T(8,128)(2,1)}), bf16[128,1280]{1,0:T(8,128)(2,1)}) %reduce-scatter.13.cloned.1.call-update) | async-done | bytes 327696
  438.8 1.3 reshape_bitcast_fusion
  440.6 3.9 fusion.4
  444.5 3.8 fusion.3
  448.3 3.7 fusion.2
  452.0 3.9 fusion.1
  456.0 3.8 fusion
  459.8 2.6 fusion.9
  463.5 2.6 reduce.8
  466.9 5.6 all-to-all-start.1
  472.6 1.4 copy.70
  474.1 3.8 fusion.47
  478.0 1.2 convolution_add_fusion.1
  479.3 1.2 copy-done.5
  480.5 1.4 fusion.42
  482.7 2.6 reduce.7
  486.1 5.9 all-to-all-start.3
  493.1 40.0 %all-reduce.3 = f32[3,1280]{1,0:T(4,128)S(1)} all-reduce(f32[3,1280]{1,0:T(4,128)S(1)} %pad_maximum_fusion), channel_id=7, replica_groups=mesh['dp'=16,'ctx'=2] {'dp','ctx'}, use_global_device_ids=true, to_apply=%region_14.16.clone | all-reduce | flops 3840 | bytes 30720
  534.6 1.0 broadcast_select_fusion
  535.5 285.1 %reduce-scatter.9.cloned.1.call-done = f32[6,40,1280]{2,1,0:T(8,128)} async-done(((f32[6,1280,1280]{2,1,0:T(8,128)}), f32[6,40,1280]{2,1,0:T(8,128)}) %reduce-scatter.9.cloned.1.call-update) | async-done | bytes 1228816 | tf_op jit(solution)/shard_map/reduce_scatter | solution.py:312
  820.6 2.4 slice_bitcast_fusion
  (134 shorter events, 15.6 us)
Async XLA Ops:
  7.2 11.4 %copy-start = (bf16[16,8,1280]{2,1,0:T(8,128)(2,1)S(1)}, bf16[16,8,1280]{2,1,0:T(8,128)(2,1)}, u32[]{:S(2)}) copy-start(bf16[16,8,1280]{2,1,0:T(8,128)(2,1)} %param.16) | copy-start | bytes 983044
  7.2 12.6 %copy-start.21 = (s32[16]{0:T(128)S(1)}, s32[16]{0:T(128)}, u32[]{:S(2)}) copy-start(s32[16]{0:T(128)} %param.26) | copy-start | bytes 196
  7.2 12.0 %copy-start.20 = (bf16[16,8,1280]{2,1,0:T(8,128)(2,1)S(1)}, bf16[16,8,1280]{2,1,0:T(8,128)(2,1)}, u32[]{:S(2)}) copy-start(bf16[16,8,1280]{2,1,0:T(8,128)(2,1)} %param.15) | copy-start | bytes 983044
  7.2 20.9 %copy-start.22 = (s32[16]{0:T(128)S(1)}, s32[16]{0:T(128)}, u32[]{:S(2)}) copy-start(s32[16]{0:T(128)} %param.27) | copy-start | bytes 196
  7.2 22.2 %copy-start.23 = (f32[40]{0:T(128)S(1)}, f32[40]{0:T(128)}, u32[]{:S(2)}) copy-start(f32[40]{0:T(128)} %param.23) | copy-start | bytes 484
  7.2 22.2 %copy-start.24 = (f32[40]{0:T(128)S(1)}, f32[40]{0:T(128)}, u32[]{:S(2)}) copy-start(f32[40]{0:T(128)} %param.24) | copy-start | bytes 484
  7.2 22.2 %copy-start.25 = (f32[40]{0:T(128)S(1)}, f32[40]{0:T(128)}, u32[]{:S(2)}) copy-start(f32[40]{0:T(128)} %param.25) | copy-start | bytes 484
  7.3 70.2 %all-gather.13.cloned.1.call-start = ((), (), s32[]{:S(2)}) async-start(), calls=%async_computation.9 | async-start | bytes 3379200 | tf_op jit(solution)/shard_map/all_gather | solution.py:88
  9.0 127.4 %all-gather.9.cloned.1.call-start = ((), (), s32[]{:S(2)}) async-start(), calls=%async_computation.7 | async-start | bytes 3379200 | tf_op jit(solution)/shard_map/all_gather | solution.py:87
  10.6 187.5 %all-gather.11.cloned.1.call-start = ((), (), s32[]{:S(2)}) async-start(), calls=%async_computation.8 | async-start | bytes 3379200 | tf_op jit(solution)/shard_map/all_gather | solution.py:86
  12.3 247.4 %all-gather.15.cloned.1.call-start = ((), (), s32[]{:S(2)}) async-start(), calls=%async_computation.10 | async-start | bytes 3379200 | tf_op jit(solution)/shard_map/all_gather | solution.py:89
  13.9 307.3 %all-gather.17.cloned.1.call-start = ((), (), s32[]{:S(2)}) async-start(), calls=%async_computation.11 | async-start | bytes 3379200 | tf_op jit(solution)/shard_map/all_gather | solution.py:90
  15.6 367.2 %all-gather.19.cloned.1.call-start = ((), (), s32[]{:S(2)}) async-start(), calls=%async_computation.12 | async-start | bytes 3379200 | tf_op jit(solution)/shard_map/all_gather | solution.py:91
  20.7 51.3 %all-to-all-start = ((bf16[16,8,1280]{2,1,0:T(8,128)(2,1)}), bf16[16,8,1280]{2,1,0:T(8,128)(2,1)S(1)}, u32[]{:S(2)}, u32[]{:S(2)}) async-start(bf16[16,8,1280]{2,1,0:T(8,128)(2,1)} %get-tuple-element.100), calls=%async_computation | async-start | bytes 655360 | tf_op jit(solution)/shard_map/all_to_all | solution.py:59
  72.1 252.5 %all-to-all-start.2 = ((bf16[16,8,1280]{2,1,0:T(8,128)(2,1)}), bf16[16,8,1280]{2,1,0:T(8,128)(2,1)S(1)}, u32[]{:S(2)}, u32[]{:S(2)}) async-start(bf16[16,8,1280]{2,1,0:T(8,128)(2,1)} %get-tuple-element.99), calls=%async_computation.2 | async-start | bytes 655360 | tf_op jit(solution)/shard_map/all_to_all | solution.py:60
  77.1 343.3 %reduce-scatter.11.cloned.1.call-start = ((), (), s32[]{:S(2)}) async-start(), calls=%async_computation.14 | async-start | bytes 983040
  149.9 53.9 %copy-start.10 = (bf16[256,1280]{0,1:T(8,128)(2,1)}, bf16[256,1280]{0,1:T(8,128)(2,1)S(1)}, u32[]{:S(2)}) copy-start(bf16[256,1280]{0,1:T(8,128)(2,1)S(1)} %copy.62) | copy-start | bytes 1966084
  324.6 63.0 %copy-start.13 = (bf16[16,8,1280]{2,1,0:T(8,128)(2,1)}, bf16[16,8,1280]{2,1,0:T(8,128)(2,1)S(1)}, u32[]{:S(2)}) copy-start(bf16[16,8,1280]{2,1,0:T(8,128)(2,1)S(1)} %all-to-all-done.2) | copy-start | bytes 983044
  382.8 3.4 copy-start.4
  386.2 1.6 copy-start.18
  386.2 2.4 copy-start.3
  387.8 0.9 copy-start.6
  393.8 4.3 copy-start.15
  397.1 1.0 copy-start.8
  405.4 33.4 %reduce-scatter.13.cloned.1.call-start = ((), (), s32[]{:S(2)}) async-start(), calls=%async_computation.15 | async-start | bytes 983040
  406.9 6.5 copy-start.9
  406.9 6.5 copy-start.11
  413.0 407.6 %reduce-scatter.9.cloned.1.call-start = ((), (), s32[]{:S(2)}) async-start(), calls=%async_computation.13 | async-start | bytes 40550400 | tf_op jit(solution)/shard_map/reduce_scatter | solution.py:312
  444.5 3.8 copy-start.7
  444.5 3.8 copy-start.17
  448.3 3.7 copy-start.19
  452.0 3.9 copy-start.12
  452.0 3.9 copy-start.14
  462.4 11.5 %copy-start.16 = (f32[128,1280]{1,0:T(8,128)S(1)}, f32[128,1280]{1,0:T(8,128)}, u32[]{:S(2)}) copy-start(f32[128,1280]{1,0:T(8,128)} %get-tuple-element.102) | copy-start | bytes 1966084
  466.9 19.2 %all-to-all-start.1 = ((bf16[16,2,5120]{2,1,0:T(2,128)(2,1)}), bf16[16,2,5120]{2,1,0:T(2,128)(2,1)S(1)}, u32[]{:S(2)}, u32[]{:S(2)}) async-start(bf16[16,2,5120]{2,1,0:T(2,128)(2,1)} %reshape.683), calls=%async_computation.1 | async-start | bytes 655360 | tf_op jit(solution)/shard_map/all_to_all | solution.py:318
  473.9 4.0 copy-start.2
  478.0 2.5 copy-start.5
  486.1 47.5 %all-to-all-start.3 = ((bf16[16,2,5120]{2,1,0:T(2,128)(2,1)}), bf16[16,2,5120]{2,1,0:T(2,128)(2,1)S(1)}, u32[]{:S(2)}, u32[]{:S(2)}) async-start(bf16[16,2,5120]{2,1,0:T(2,128)(2,1)} %reshape.685), calls=%async_computation.3 | async-start | bytes 655360 | tf_op jit(solution)/shard_map/all_to_all | solution.py:319
  492.4 330.5 %copy-start.1 = (bf16[16,8,1280]{2,1,0:T(8,128)(2,1)S(1)}, bf16[16,8,1280]{2,1,0:T(8,128)(2,1)}, u32[]{:S(2)}) copy-start(bf16[16,8,1280]{2,1,0:T(8,128)(2,1)} %param.16) | copy-start | bytes 983044
Sparse Core Ops, SparseCore 0:
  11.5 63.0 all-gather.12
  78.0 58.2 all-gather.8
  139.8 58.2 all-gather.10
  201.4 58.2 all-gather.14
  262.9 58.2 all-gather.16
  324.5 58.2 all-gather.18
  405.5 14.8 reduce-scatter.10
  422.8 15.9 reduce-scatter.12
  459.9 360.5 reduce-scatter.8
where the time goes:
time: 831 us; the launch traced here: 830 us
  waiting for transfers between devices  565 us (68%)
  blocking collectives  104 us (13%)
  matrix products  63.4 us (8%)
  local copies, waits for them, and re-layouts  37 us (4%)
  starting transfers between devices  24.6 us (3%)
  other arithmetic  20.9 us (3%)
  between operations  14.5 us (2%)
    reduce_scatter x1, waiting for transfers between devices, per_device(): lax.psum_scatter(matrix_stack, ('dp', 'ctx'), scatter_dimension=1, tiled=...  285 us
    unnamed x2, blocking collectives  81.6 us
    all_gather x1, waiting for transfers between devices, per_device(): lax.all_gather(lowered[4], ('dp', 'ctx'), axis=0, tiled=True)  58.8 us
    all_gather x1, waiting for transfers between devices, per_device(): lax.all_gather(lowered[5], ('dp', 'ctx'), axis=0, tiled=True)  58.2 us
    all_gather x1, waiting for transfers between devices, per_device(): lax.all_gather(lowered[3], ('dp', 'ctx'), axis=0, tiled=True)  52.6 us
    all_gather x1, waiting for transfers between devices, per_device(): lax.all_gather(lowered[0], ('dp', 'ctx'), axis=0, tiled=True)  48.1 us
    all_gather x1, waiting for transfers between devices, per_device(): lax.all_gather(lowered[1], ('dp', 'ctx'), axis=0, tiled=True)  43.8 us
    dot_general x6, matrix products, trans_mult(): lax.dot_general(left, right, (((0,), (0,)), ((), ())), preferred_element_...  23 us
  transfers between devices with their start and end apart: 13, of which 8 were waited for; matrix products, arithmetic and copies ran while one was open for 9% of the time, Pallas kernels for 0%

commit v1 on v0

--- a/solution.py
+++ b/solution.py
@@ -3,7 +3,9 @@
 import jax
 import jax.numpy as jnp
 from jax import lax
-from jax.sharding import PartitionSpec as P
+from jax.experimental import pallas as pl
+from jax.experimental.pallas import tpu as pltpu
+from jax.sharding import Mesh, PartitionSpec as P
 
 H = 16
 HD = 80
@@ -53,16 +55,18 @@
     head_count = H
     head_dim = HD
     piece_rows = inputs.shape[1]
-    dealt_in = jnp.take(inputs, deal, axis=0)
-    dealt_cot = jnp.take(cotangent, deal, axis=0)
+    seq_numbers = jnp.arange(inputs.shape[0], dtype=jnp.int32)
+    seq_lengths = jnp.sum(
+        jnp.where(deal[None, :] == seq_numbers[:, None], lengths[None, :], 0), axis=1
+    )
     local_in, local_cot = (
-        lax.all_to_all(dealt_in, "dp", split_axis=0, concat_axis=1, tiled=True),
-        lax.all_to_all(dealt_cot, "dp", split_axis=0, concat_axis=1, tiled=True),
+        lax.all_to_all(inputs, "dp", split_axis=0, concat_axis=1, tiled=True),
+        lax.all_to_all(cotangent, "dp", split_axis=0, concat_axis=1, tiled=True),
     )
     seq_count, local_rows, model_width = local_in.shape
     padded = local_rows * groups
     token_count = seq_count * local_rows
-    my_lengths = lax.dynamic_slice_in_dim(lengths, group_index * seq_count, seq_count, 0)
+    my_lengths = lax.dynamic_slice_in_dim(seq_lengths, group_index * seq_count, seq_count, 0)
     query_pos = position_of(
         ctx_index * local_rows + jnp.arange(local_rows, dtype=jnp.int32),
         local_rows,
@@ -318,12 +322,9 @@
         lax.all_to_all(out_local, "dp", split_axis=1, concat_axis=0, tiled=True),
         lax.all_to_all(grad_local, "dp", split_axis=1, concat_axis=0, tiled=True),
     )
-    undo_order = jnp.zeros_like(deal).at[deal].set(jnp.arange(deal.shape[0], dtype=jnp.int32))
-    final_out = jnp.take(back_out, undo_order, axis=0)
-    final_grad = jnp.take(back_grad, undo_order, axis=0)
     return (
-        final_out,
-        final_grad,
+        back_out,
+        back_grad,
         matrix_sums[0],
         matrix_sums[1],
         matrix_sums[2],
@@ -336,38 +337,415 @@
     )
 
 
+LOG2E = 1.442695041
+CODES = (0, 1, 4, 5)
+
+
+def plane_shift(value, step):
+    if step == 1:
+        return lax.ppermute(value, "x", [(0, 1), (1, 0)])
+    if step == 2:
+        return lax.ppermute(value, "y", [(0, 1), (1, 0)])
+    return lax.ppermute(value, ("y", "x"), [(0, 3), (1, 2), (2, 1), (3, 0)])
+
+
+def core_swap(value):
+    return lax.ppermute(value, "core", [(0, 1), (1, 0)])
+
+
+def ring_shift(value, step):
+    return lax.ppermute(value, "z", [(i, (i + step) % 4) for i in range(4)])
+
+
+def pick(array, index):
+    return lax.dynamic_index_in_dim(array, index, 0, keepdims=False)
+
+
+def by_source(pieces, z_index):
+    own, one, two, three = pieces
+    line = jnp.stack([three, two, one, own, three, two, one])
+    return lax.dynamic_slice_in_dim(line, 3 - z_index, 4, 0)
+
+
+def pair(mine, other, index, axis):
+    first = index == 0
+    return jnp.stack([jnp.where(first, mine, other), jnp.where(first, other, mine)], axis=axis)
+
+
+def row_positions(shape, dim, z_index, plane_index):
+    row = lax.broadcasted_iota(jnp.int32, shape, dim)
+    chip = (row // 32) % 4
+    code = (chip % 2) + 4 * (chip // 2) + 2 * (row // 128)
+    hop = (row % 32) // 8
+    return 64 * ((z_index - hop) & 3) + 8 * (plane_index ^ code) + row % 8
+
+
+def live_pairs(info_ref, seq):
+    z_index, plane_index = info_ref[0], info_ref[1]
+    shape = (256, 256)
+    query_pos = row_positions(shape, 0, z_index, plane_index)
+    key_pos = row_positions(shape, 1, z_index, plane_index)
+    return (key_pos <= query_pos) & (key_pos < info_ref[2 + seq])
+
+
+def block_rows(near_ref, far_ref):
+    return jnp.concatenate([near_ref[...], far_ref[...]], axis=0).reshape(256, near_ref.shape[2])
+
+
+def soft_probs(query, key, live):
+    scores = mult_trans(query, key)
+    scores = jnp.where(live, scores, -1e30)
+    top = jnp.max(scores, axis=1, keepdims=True)
+    weights = jnp.where(live, jnp.exp(scores - top), 0.0)
+    return weights / jnp.sum(weights, axis=1, keepdims=True)
+
+
+def attend_kernel(info_ref, near_ref, far_ref, gain_ref, mult_ref, w_ref, pre_ref, att_near, att_far):
+    seq = pl.program_id(0)
+    live = live_pairs(info_ref, seq)
+    wide = block_rows(near_ref, far_ref).astype(jnp.float32)
+    inverse = lax.rsqrt(jnp.mean(wide * wide, axis=1, keepdims=True) + 1e-06)
+    hidden = (wide * inverse * gain_ref[...]).astype(jnp.bfloat16)
+    pre = jnp.dot(hidden, w_ref[...], preferred_element_type=jnp.float32)
+    pre_ref[...] = pre.reshape(2, 4, 32, 480)
+    query = (pre[:, 0:160] * mult_ref[...]).astype(jnp.bfloat16)
+    key = pre[:, 160:320].astype(jnp.bfloat16)
+    value = pre[:, 320:480].astype(jnp.bfloat16)
+    heads = []
+    for head in range(2):
+        part = slice(80 * head, 80 * head + 80)
+        probs = soft_probs(query[:, part], key[:, part], live).astype(jnp.bfloat16)
+        heads.append(jnp.dot(probs, value[:, part], preferred_element_type=jnp.float32))
+    att = jnp.concatenate(heads, axis=1).astype(jnp.bfloat16).reshape(2, 4, 32, 160)
+    att_near[...] = att[0]
+    att_far[...] = att[1]
+
+
+def attend_back_kernel(
+    info_ref, near_ref, far_ref, gain_ref, mult_ref, w_ref, pre_ref, grad_near, grad_far,
+    hid_near, hid_far, w_grad, gain_grad, scale_grad, w_acc, gain_acc, scale_acc,
+):
+    seq = pl.program_id(0)
+
+    @pl.when(seq == 0)
+    def _():
+        w_acc[...] = jnp.zeros_like(w_acc)
+        gain_acc[...] = jnp.zeros_like(gain_acc)
+        scale_acc[...] = jnp.zeros_like(scale_acc)
+
+    live = live_pairs(info_ref, seq)
+    wide = block_rows(near_ref, far_ref).astype(jnp.float32)
+    inverse = lax.rsqrt(jnp.mean(wide * wide, axis=1, keepdims=True) + 1e-06)
+    normed = wide * inverse
+    hidden = (normed * gain_ref[...]).astype(jnp.bfloat16)
+    pre = pre_ref[...].reshape(256, 480)
+    mult = mult_ref[...]
+    query = (pre[:, 0:160] * mult).astype(jnp.bfloat16)
+    key = pre[:, 160:320].astype(jnp.bfloat16)
+    value = pre[:, 320:480].astype(jnp.bfloat16)
+    grad_att = block_rows(grad_near, grad_far)
+    grad_q, grad_k, grad_v = [], [], []
+    for head in range(2):
+        part = slice(80 * head, 80 * head + 80)
+        probs = soft_probs(query[:, part], key[:, part], live)
+        grad_probs = mult_trans(grad_att[:, part], value[:, part])
+        delta = jnp.sum(probs * grad_probs, axis=1, keepdims=True)
+        grad_scores = (probs * (grad_probs - delta)).astype(jnp.bfloat16)
+        grad_v.append(trans_mult(probs.astype(jnp.bfloat16), grad_att[:, part]))
+        grad_q.append(jnp.dot(grad_scores, key[:, part], preferred_element_type=jnp.float32))
+        grad_k.append(trans_mult(grad_scores, query[:, part]))
+    grad_query = jnp.concatenate(grad_q, axis=1)
+    scale_acc[...] += jnp.sum(grad_query * pre[:, 0:160], axis=0, keepdims=True)
+    joined = jnp.concatenate([grad_query * mult] + grad_k + grad_v, axis=1).astype(jnp.bfloat16)
+    w_acc[...] += trans_mult(hidden, joined)
+    grad_hidden = mult_trans(joined, w_ref[...])
+    gain_acc[...] += jnp.sum(grad_hidden * normed, axis=0, keepdims=True)
+    low = grad_hidden.astype(jnp.bfloat16).reshape(2, 4, 32, 1280)
+    hid_near[...] = low[0]
+    hid_far[...] = low[1]
+
+    @pl.when(seq == 3)
+    def _():
+        w_grad[...] = w_acc[...].astype(jnp.bfloat16)
+        gain_grad[...] = gain_acc[...]
+        scale_grad[...] = scale_acc[...]
+
+
+def feed_kernel(
+    info_ref, x_ref, g_ref, att_0, att_1, att_2, att_3, gain_ref, wo_ref, up_ref, down_ref,
+    out_ref, act_ref, hid_ref, dup_ref, dm_ref, dmid_ref, datt_0, datt_1, datt_2, datt_3, gain_grad,
+):
+    plane_index = info_ref[1]
+    atts, datts = (att_0, att_1, att_2, att_3), (datt_0, datt_1, datt_2, datt_3)
+
+    def rows_of(chip, core):
+        source = plane_index ^ (CODES[chip] + 2 * core)
+        return pl.ds(pl.multiple_of(source * 160, 160), 160)
+
+    middle = x_ref[...].astype(jnp.float32)
+    for chip in range(4):
+        for core in range(2):
+            middle += jnp.dot(
+                atts[chip][core], wo_ref[rows_of(chip, core), :], preferred_element_type=jnp.float32
+            )
+    inverse = lax.rsqrt(jnp.mean(middle * middle, axis=1, keepdims=True) + 1e-06)
+    normed = middle * inverse
+    gain = gain_ref[...]
+    hidden = (normed * gain).astype(jnp.bfloat16)
+    hid_ref[...] = hidden
+    up = jnp.dot(hidden, up_ref[...], preferred_element_type=jnp.float32)
+    sigma = jax.nn.sigmoid(up)
+    active = (up * sigma).astype(jnp.bfloat16)
+    act_ref[...] = active
+    down = jnp.dot(active, down_ref[...], preferred_element_type=jnp.float32)
+    out_ref[...] = (middle + down).astype(jnp.bfloat16)
+    cot = g_ref[...]
+    grad_act = mult_trans(cot, down_ref[...])
+    grad_up = (grad_act * sigma * (1.0 + up * (1.0 - sigma))).astype(jnp.bfloat16)
+    dup_ref[...] = grad_up
+    grad_hidden = mult_trans(grad_up, up_ref[...])
+    gain_grad[...] = jnp.sum(grad_hidden * normed, axis=0, keepdims=True)
+    grad_mid = cot.astype(jnp.float32) + norm_back(grad_hidden, normed, inverse, gain)
+    dmid_ref[...] = grad_mid
+    low = grad_mid.astype(jnp.bfloat16)
+    dm_ref[...] = low
+    for chip in range(4):
+        for core in range(2):
+            datts[chip][core] = mult_trans(low, wo_ref[rows_of(chip, core), :]).astype(jnp.bfloat16)
+
+
+def whole(shape):
+    return pl.BlockSpec(shape, lambda *_: (0,) * len(shape))
+
+
+def seq_block(*lead, width):
+    count = len(lead)
+    return pl.BlockSpec((*lead, 32, width), lambda s, info: (*(0,) * count, s, 0))
+
+
+def planes(
+    inputs, cotangent, w_query, w_key, w_value, w_output, w_up, w_down,
+    attn_gain, mlp_gain, query_scale, deal, lengths,
+):
+    f32, bf16 = jnp.float32, jnp.bfloat16
+    z, y, c, x = (lax.axis_index(name) for name in ("z", "y", "core", "x"))
+    plane = 4 * y + 2 * c + x
+    width = 1280
+    seqs = jnp.arange(16, dtype=jnp.int32)
+    seq_lengths = jnp.sum(jnp.where(deal[None, :] == seqs[:, None], lengths[None, :], 0), axis=1)
+    my_lengths = lax.dynamic_slice_in_dim(seq_lengths, 4 * z, 4, 0)
+    info = jnp.concatenate([jnp.stack([z, plane]), my_lengths]).astype(jnp.int32)
+
+    vec = jnp.concatenate([attn_gain, mlp_gain, query_scale]).astype(bf16)
+    vec_block = jnp.zeros((1, 8, width), bf16).at[0, 0, :120].set(vec)
+    in_four = inputs.reshape(4, 4, 8, width)
+    cot_four = cotangent.reshape(4, 4, 8, width)
+    sent = [jnp.concatenate([pick(in_four, (z + k) % 4), vec_block]) for k in range(4)]
+    got = [sent[0]] + [ring_shift(sent[k], k) for k in (1, 2, 3)]
+    x_rows = jnp.stack([item[:4] for item in got], axis=1).reshape(128, width)
+    vec_rows = jnp.concatenate([item[4, :1] for item in got] + [jnp.zeros((4, width), bf16)])
+    own = jnp.concatenate([x_rows, vec_rows])
+
+    qkv = jnp.stack([w_query, w_key, w_value]).astype(bf16)
+    qkv = qkv.reshape(3, 40, 8, 160).transpose(2, 1, 0, 3).reshape(8, 40, 480)
+    qkv = lax.all_to_all(qkv, ("y", "core", "x"), split_axis=0, concat_axis=0, tiled=True)
+    qkv = qkv.reshape(320, 480)
+    w_qkv = by_source([qkv] + [ring_shift(qkv, k) for k in (1, 2, 3)], z).reshape(width, 480)
+
+    near = jnp.stack([own] + [plane_shift(own, step) for step in (1, 2, 3)])
+    far = core_swap(near)
+
+    big = jnp.stack([w_output, w_up, w_down]).astype(bf16)
+    big = lax.all_gather(big, "z", axis=0)
+    part_a, part_b = big[:2], big[2:]
+    part_a = pair(part_a, plane_shift(part_a, 1), x, 2)
+    part_b = pair(part_b, plane_shift(part_b, 2), y, 2)
+    part_a = pair(part_a, plane_shift(part_a, 2), y, 2)
+    part_b = pair(part_b, plane_shift(part_b, 1), x, 3)
+    big = jnp.concatenate([part_a, part_b])
+    other = core_swap(big)
+    w_out_full, w_up_full, w_down_full = (
+        pair(big[:, i], other[:, i], c, 2).reshape(width, width) for i in range(3)
+    )
+
+    vecs = jnp.stack([near[:, 128:132, :120], far[:, 128:132, :120]])
+    vecs = vecs.astype(f32).reshape(2, 2, 2, 4, 120)
+    vecs = jnp.where(c == 0, vecs, vecs[::-1])
+    vecs = jnp.where(y == 0, vecs, vecs[:, ::-1])
+    vecs = jnp.where(x == 0, vecs, vecs[:, :, ::-1])
+    fours = jnp.arange(4, dtype=jnp.int32)
+    from_hop = (z - fours[:, None]) % 4 == fours[None, :]
+    vecs = jnp.sum(jnp.where(from_hop[:, None, None, None, :, None], vecs[None], 0.0), axis=4)
+    vecs = vecs.reshape(4, 2, 2, 2, 3, 40).transpose(4, 0, 2, 1, 3, 5).reshape(3, width)
+    gain_one, gain_two = vecs[0:1], vecs[1:2]
+    my_scale = lax.dynamic_slice_in_dim(vecs[2:3], 160 * plane, 160, 1)
+    query_mult = LOG2E / math.sqrt(HD) * jax.nn.softplus(my_scale)
+
+    limit = pltpu.CompilerParams(vmem_limit_bytes=50 * 1024 * 1024)
+    pre, att_near, att_far = pl.pallas_call(
+        attend_kernel,
+        grid_spec=pltpu.PrefetchScalarGridSpec(
+            num_scalar_prefetch=1,
+            grid=(4,),
+            in_specs=[
+                seq_block(4, width=width), seq_block(4, width=width),
+                whole((1, width)), whole((1, 160)), whole((width, 480)),
+            ],
+            out_specs=[seq_block(2, 4, width=480), seq_block(4, width=160), seq_block(4, width=160)],
+        ),
+        out_shape=[
+            jax.ShapeDtypeStruct((2, 4, 128, 480), f32),
+            jax.ShapeDtypeStruct((4, 128, 160), bf16),
+            jax.ShapeDtypeStruct((4, 128, 160), bf16),
+        ],
+        compiler_params=limit,
+        cost_estimate=pl.CostEstimate(flops=1_500_000_000, bytes_accessed=8_000_000, transcendentals=600_000),
+        name="attend",
+    )(info, near, far, gain_one, query_mult, w_qkv)
+
+    att_pair = jnp.stack([att_near, core_swap(att_far)], axis=1)
+    atts = [att_pair[0]] + [plane_shift(att_pair[step], step) for step in (1, 2, 3)]
+
+    cot_sent = [pick(cot_four, (z + k) % 4) for k in range(4)]
+    cot_got = [cot_sent[0]] + [ring_shift(cot_sent[k], k) for k in (1, 2, 3)]
+    cot_rows = jnp.stack(cot_got, axis=1).reshape(128, width)
+
+    low_rows = jax.ShapeDtypeStruct((128, width), bf16)
+    datt_shape = jax.ShapeDtypeStruct((2, 128, 160), bf16)
+    smem = pl.BlockSpec(memory_space=pltpu.SMEM)
+    vmem = pl.BlockSpec(memory_space=pltpu.VMEM)
+    out_rows, active, hidden_two, grad_up, dm, grad_mid, *datts, gain_two_grad = pl.pallas_call(
+        feed_kernel,
+        in_specs=[smem] + [vmem] * 10,
+        out_specs=[vmem] * 11,
+        out_shape=[low_rows] * 5
+        + [jax.ShapeDtypeStruct((128, width), f32)]
+        + [datt_shape] * 4
+        + [jax.ShapeDtypeStruct((1, width), f32)],
+        compiler_params=limit,
+        cost_estimate=pl.CostEstimate(flops=2_600_000_000, bytes_accessed=13_000_000, transcendentals=200_000),
+        name="feed",
+    )(info, x_rows, cot_rows, *atts, gain_two, w_out_full, w_up_full, w_down_full)
+
+    back = [datts[0]] + [plane_shift(datts[step], step) for step in (1, 2, 3)]
+    grad_att_near = jnp.stack([item[0] for item in back])
+    grad_att_far = core_swap(jnp.stack([item[1] for item in back]))
+
+    att_all = jnp.stack(atts).reshape(2, 2, 2, 128, 160)
+    att_all = jnp.where(y == 0, att_all, att_all[::-1])
+    att_all = jnp.where(x == 0, att_all, att_all[:, ::-1])
+    att_all = jnp.where(c == 0, att_all, att_all[:, :, ::-1])
+    att_all = att_all.transpose(3, 0, 2, 1, 4).reshape(128, width)
+
+    def weight_grad(left, right):
+        made = lax.dot_general(left, right, (((0,), (0,)), ((), ())), preferred_element_type=bf16)
+        return made.reshape(4, 2, 2, 2, 40, width)
+
+    grads = jnp.stack(
+        [weight_grad(att_all, dm), weight_grad(hidden_two, grad_up), weight_grad(active, cot_rows)], axis=1
+    )
+
+    def added(left, right):
+        return (left.astype(f32) + right.astype(f32)).astype(bf16)
+
+    def halves(array, index, axis):
+        first, second = (lax.index_in_dim(array, i, axis, keepdims=False) for i in (0, 1))
+        return jnp.where(index == 0, first, second), jnp.where(index == 0, second, first)
+
+    kept, away = halves(grads, c, 3)
+    kept = added(kept, core_swap(away))
+    kept_a, away_a = halves(kept[:2], x, 3)
+    kept_b, away_b = halves(kept[2:], y, 2)
+    kept_a = added(kept_a, plane_shift(away_a, 1))
+    kept_b = added(kept_b, plane_shift(away_b, 2))
+    kept_a, away_a = halves(kept_a, y, 2)
+    kept_b, away_b = halves(kept_b, x, 2)
+    kept_a = added(kept_a, plane_shift(away_a, 2))
+    kept_b = added(kept_b, plane_shift(away_b, 1))
+    kept = jnp.concatenate([kept_a, kept_b])
+
+    def ring_sum(array):
+        total = pick(array, z).astype(f32)
+        for k in (1, 2, 3):
+            total += ring_shift(pick(array, (z + k) % 4), k).astype(f32)
+        return total
+
+    big_sums = ring_sum(kept)
+
+    hid_near, hid_far, qkv_grad, gain_one_grad, scale_grad = pl.pallas_call(
+        attend_back_kernel,
+        grid_spec=pltpu.PrefetchScalarGridSpec(
+            num_scalar_prefetch=1,
+            grid=(4,),
+            in_specs=[
+                seq_block(4, width=width), seq_block(4, width=width),
+                whole((1, width)), whole((1, 160)), whole((width, 480)),
+                seq_block(2, 4, width=480), seq_block(4, width=160), seq_block(4, width=160),
+            ],
+            out_specs=[
+                seq_block(4, width=width), seq_block(4, width=width),
+                whole((width, 480)), whole((1, width)), whole((1, 160)),
+            ],
+            scratch_shapes=[
+                pltpu.VMEM((width, 480), f32), pltpu.VMEM((1, width), f32), pltpu.VMEM((1, 160), f32),
+            ],
+        ),
+        out_shape=[
+            jax.ShapeDtypeStruct((4, 128, width), bf16),
+            jax.ShapeDtypeStruct((4, 128, width), bf16),
+            jax.ShapeDtypeStruct((width, 480), bf16),
+            jax.ShapeDtypeStruct((1, width), f32),
+            jax.ShapeDtypeStruct((1, 160), f32),
+        ],
+        compiler_params=limit,
+        cost_estimate=pl.CostEstimate(flops=3_500_000_000, bytes_accessed=12_000_000, transcendentals=600_000),
+        name="attend_back",
+    )(info, near, far, gain_one, query_mult, w_qkv, pre, grad_att_near, grad_att_far)
+
+    hid = added(hid_near, core_swap(hid_far))
+    grad_hid = hid[0].astype(f32)
+    for step in (1, 2, 3):
+        grad_hid += plane_shift(hid[step], step).astype(f32)
+    wide = x_rows.astype(f32)
+    inverse = lax.rsqrt(jnp.mean(wide * wide, axis=1, keepdims=True) + 1e-06)
+    grad_in = (grad_mid + norm_back(grad_hid, wide * inverse, inverse, gain_one)).astype(bf16)
+
+    scale_line = lax.dynamic_update_slice(jnp.zeros((1, width), f32), scale_grad, (0, 160 * plane))
+    lines = jnp.concatenate([gain_one_grad, gain_two_grad, scale_line])
+    lines = lines.reshape(3, 4, 8, 40).transpose(1, 2, 0, 3).reshape(4, 8, 1, 120).astype(bf16)
+    lines = jnp.pad(lines, ((0, 0), (0, 0), (0, 7), (0, 360)))
+    send = jnp.concatenate([qkv_grad.reshape(4, 8, 40, 480), lines], axis=2)
+    sums = ring_sum(send).astype(bf16)
+    sums = lax.all_to_all(sums, ("y", "core", "x"), split_axis=0, concat_axis=0, tiled=True)
+    qkv_sums = sums[:, :40].reshape(8, 40, 3, 160).transpose(2, 1, 0, 3).reshape(3, 40, width).astype(f32)
+    line_sums = jnp.sum(sums[:, 40, :120].astype(f32), axis=0).reshape(3, 40)
+    scale_low = query_scale.astype(bf16).astype(f32)
+    scale_sum = LOG2E / math.sqrt(HD) * jax.nn.sigmoid(scale_low) * line_sums[2]
+
+    def home(rows):
+        rows = rows.reshape(4, 4, 8, width)
+        parts = [rows[:, 0]] + [ring_shift(rows[:, k], -k) for k in (1, 2, 3)]
+        line = jnp.stack(parts + parts[:3])
+        return lax.dynamic_slice_in_dim(line, (4 - z) % 4, 4, 0).reshape(16, 8, width)
+
+    return (
+        home(out_rows), home(grad_in), qkv_sums[0], qkv_sums[1], qkv_sums[2],
+        big_sums[0], big_sums[1], big_sums[2], line_sums[0], line_sums[1], scale_sum,
+    )
+
+
 def solution(mesh):
-    placed = (
-        P(None, ("dp", "ctx"), None),
-        P(None, ("dp", "ctx"), None),
-        P(("dp", "ctx"), None),
-        P(("dp", "ctx"), None),
-        P(("dp", "ctx"), None),
-        P(("dp", "ctx"), None),
-        P(("dp", "ctx"), None),
-        P(("dp", "ctx"), None),
-        P(("dp", "ctx")),
-        P(("dp", "ctx")),
-        P(("dp", "ctx")),
-        P(),
-        P(),
-    )
+    names = ("dp", "ctx")
+    body = per_device
+    if dict(mesh.shape) == {"dp": 16, "ctx": 2}:
+        mesh = Mesh(mesh.devices.reshape(4, 2, 2, 2), ("z", "y", "core", "x"))
+        names = mesh.axis_names
+        body = planes
+    seq, mat, line = P(None, names, None), P(names, None), P(names)
     return jax.shard_map(
-        per_device,
+        body,
         mesh=mesh,
-        in_specs=placed,
-        out_specs=(
-            P(None, ("dp", "ctx"), None),
-            P(None, ("dp", "ctx"), None),
-            P(("dp", "ctx"), None),
-            P(("dp", "ctx"), None),
-            P(("dp", "ctx"), None),
-            P(("dp", "ctx"), None),
-            P(("dp", "ctx"), None),
-            P(("dp", "ctx"), None),
-            P(("dp", "ctx")),
-            P(("dp", "ctx")),
-            P(("dp", "ctx")),
-        ),
+        in_specs=(seq,) * 2 + (mat,) * 6 + (line,) * 3 + (P(), P()),
+        out_specs=(seq,) * 2 + (mat,) * 6 + (line,) * 3,
         check_vma=False,
     )

time: 831 us -> 422 us (0.51)
  waiting for transfers between devices: 565 us -> 214 us
  blocking collectives: 104 us -> 0 us
  matrix products: 63.4 us -> 3.04 us
  starting transfers between devices: 24.6 us -> 64.7 us
  Pallas kernels: 0 us -> 31.4 us
  other arithmetic: 20.9 us -> 43.4 us
  local copies, waits for them, and re-layouts: 37 us -> 45.8 us
    reduce_scatter x1 -> x0, waiting for transfers between devices: 285 us -> none  [per_device(): lax.psum_scatter(matrix_stack, ('dp', 'ctx'), scatter_dimension=1, tiled=...]
    all_gather x6 -> x1, waiting for transfers between devices: 262 us -> 23.2 us  [planes(): big = lax.all_gather(big, 'z', axis=0)]
    ppermute x0 -> x47, waiting for transfers between devices: none -> 185 us  [the longest x21 83.5 us: ring_shift(): return lax.ppermute(value, 'z', [(i, (i + step) % 4) for i in range(4)])]
    unnamed x2 -> x0, blocking collectives: 81.6 us -> none
    dot_general x24 -> x3, matrix products: 63.4 us -> 3.04 us  [weight_grad(): lax.dot_general(left, right, (((0,), (0,)), ((), ())), preferred_element_...]
    ppermute x0 -> x47, starting transfers between devices: none -> 55.8 us  [the longest x21 29.6 us: ring_shift(): return lax.ppermute(value, 'z', [(i, (i + step) % 4) for i in range(4)])]
    pallas_call x0 -> x3, Pallas kernels: none -> 31.4 us  [the longest x1 13.5 us: planes(): pl.pallas_call(attend_back_kernel, grid_spec=pltpu.PrefetchScalarGridSpec...]
    all_gather x2 -> x0, blocking collectives: 22.2 us -> none  [the longest x1 11.5 us: per_device(): value_piece = lax.all_gather(values_three, 'ctx', axis=1, tiled=True)]
  transfers between devices with their start and end apart: 13 -> 50, of which waited for: 8 -> 29; matrix products, arithmetic and copies ran while one was open for 9% -> 13% of each run, Pallas kernels for 0% -> 5%
where the time goes in v1:
time: 422 us; the launch traced here: 417 us
  waiting for transfers between devices  214 us (51%)
  starting transfers between devices  64.7 us (15%)
  local copies, waits for them, and re-layouts  45.8 us (11%)
  other arithmetic  43.4 us (10%)
  Pallas kernels  31.4 us (7%)
  between operations  15.1 us (4%)
    ppermute x21, waiting for transfers between devices, ring_shift(): return lax.ppermute(value, 'z', [(i, (i + step) % 4) for i in range(4)])  83.5 us
    ppermute x8, waiting for transfers between devices, plane_shift(): return lax.ppermute(value, 'x', [(0, 1), (1, 0)])  50.1 us
    ppermute x8, waiting for transfers between devices, plane_shift(): return lax.ppermute(value, 'y', [(0, 1), (1, 0)])  36.5 us
    ppermute x21, starting transfers between devices, ring_shift(): return lax.ppermute(value, 'z', [(i, (i + step) % 4) for i in range(4)])  29.6 us
    all_gather x1, waiting for transfers between devices, planes(): big = lax.all_gather(big, 'z', axis=0)  23.2 us
    pallas_call x1, Pallas kernels, planes(): pl.pallas_call(attend_back_kernel, grid_spec=pltpu.PrefetchScalarGridSpec...  13.5 us
    ppermute x8, starting transfers between devices, plane_shift(): return lax.ppermute(value, 'y', [(0, 1), (1, 0)])  13.2 us
    unnamed x76, local copies, waits for them, and re-layouts  12.9 us
  transfers between devices with their start and end apart: 50, of which 29 were waited for; matrix products, arithmetic and copies ran while one was open for 13% of the time, Pallas kernels for 5%

profile of v1, /device:TPU:0, one launch (start us, length us, event | category | flops | bytes accessed | tf_op | source)
XLA Modules:
  0.0 417.0 jit_solution(8988803498725781171)
XLA Ops:
  13.9 5.2 %all-to-all-start = ((bf16[8,40,480]{2,1,0:T(8,128)(2,1)}), bf16[8,40,480]{2,1,0:T(8,128)(2,1)}, u32[]{:S(2)}, u32[]{:S(2)}) async-start(bf16[8,40,480]{2,1,0:T(8,128)(2,1)} %reshape.478), calls=%async_computation | async-start | bytes 655360 | tf_op jit(solution)/shard_map/all_to_all | solution.py:551
  20.3 2.0 collective-permute-start
  22.3 2.6 collective-permute-start.1
  28.0 4.1 collective-permute-done.1
  32.1 23.2 %all-gather.2.cloned.1.call-done = bf16[4,3,40,1280]{3,2,1,0:T(8,128)(2,1)} async-done(((bf16[1,3,40,1280]{3,2,1,0:T(8,128)(2,1)}), bf16[4,3,40,1280]{3,2,1,0:T(8,128)(2,1)}) %all-gather.2.cloned.1.call-update) | async-done | bytes 1228816 | tf_op jit(solution)/shard_map/all_gather | solution.py:559
  55.3 1.4 fusion.56
  56.8 1.5 collective-permute-start.17
  58.3 1.5 collective-permute-start.19
  59.8 12.0 %collective-permute-done.17 = bf16[2,3,40,1280]{3,2,1,0:T(8,128)(2,1)S(1)} collective-permute-done((bf16[2,3,40,1280]{3,2,1,0:T(8,128)(2,1)S(1)}, bf16[2,3,40,1280]{3,2,1,0:T(8,128)(2,1)S(1)}, u32[]{:S(2)}, u32[]{:S(2)}) %collective-permute-start.17) | collective-permute-done | bytes 614432 | tf_op jit(solution)/shard_map/ppermute | solution.py:346
  76.1 1.5 collective-permute-start.18
  80.1 1.5 collective-permute-start.8
  81.6 1.5 collective-permute-start.7
  83.6 21.0 %collective-permute-done.20 = bf16[2,3,2,40,1280]{4,3,1,0,2:T(8,128)(2,1)} collective-permute-done((bf16[2,3,2,40,1280]{4,3,1,0,2:T(8,128)(2,1)}, bf16[2,3,2,40,1280]{4,3,1,0,2:T(8,128)(2,1)}, u32[]{:S(2)}, u32[]{:S(2)}) %collective-permute-start.20) | collective-permute-done | bytes 1228832 | tf_op jit(solution)/shard_map/ppermute | solution.py:346
  104.7 2.2 collective-permute-start.10
  106.9 1.4 select_bitcast_fusion.6
  108.4 5.5 %collective-permute-done.18 = bf16[2,3,2,40,1280]{4,3,1,0,2:T(8,128)(2,1)} collective-permute-done((bf16[2,3,2,40,1280]{4,3,1,0,2:T(8,128)(2,1)}, bf16[2,3,2,40,1280]{4,3,1,0,2:T(8,128)(2,1)}, u32[]{:S(2)}, u32[]{:S(2)}) %collective-permute-start.18) | collective-permute-done | bytes 1228832 | tf_op jit(solution)/shard_map/ppermute | solution.py:348
  113.8 1.4 select_bitcast_fusion.8
  115.8 2.9 copy.194
  119.5 2.1 collective-permute-start.5
  122.3 2.2 collective-permute-start.11
  124.5 1.4 pad_maximum_fusion.4.near_ref
  127.2 22.3 %collective-permute-done.11 = bf16[320,480]{1,0:T(8,128)(2,1)S(1)} collective-permute-done((bf16[320,480]{1,0:T(8,128)(2,1)}, bf16[320,480]{1,0:T(8,128)(2,1)S(1)}, u32[]{:S(2)}, u32[]{:S(2)}) %collective-permute-start.11) | collective-permute-done | bytes 307232 | tf_op jit(solution)/shard_map/ppermute | solution.py:357
  155.0 8.3 %attend.1 = (f32[2,4,128,480]{3,2,1,0:T(8,128)}, bf16[4,128,160]{2,1,0:T(8,128)(2,1)S(1)}, bf16[4,128,160]{2,1,0:T(8,128)(2,1)S(1)}) custom-call(s32[6]{0:T(128)S(1)} %pad_add_fusion.info_ref, bf16[4,136,1280]{2,1,0:T(8,128)(2,1)S(1)} %pad_maximum_fusion.4.near_ref, bf16[4,136,1280]{2,1,0:T(8,128)(2,1)} %copy-done.25, f32[1,1280]{1,0:T(1,128)S(1)} %slice.247.gain_ref, ...), custom_call_target="tpu_custom_call" | custom-call | flops 1500000000 | bytes 8000000 | tf_op jit(solution)/shard_map/attend/pallas_call | solution.py:585
  165.0 2.4 collective-permute-start.16
  168.9 3.4 collective-permute-done.16.att_3
  172.3 2.2 collective-permute-done.14.att_1
  175.8 4.6 %select_bitcast_fusion.1 = (bf16[4,2,1,2,40,1280]{5,4,0,1,3,2:T(8,128)(2,1)S(1)}, bf16[4,2,1,2,40,1280]{5,4,0,1,3,2:T(8,128)(2,1)S(1)}, bf16[4,2,1,2,40,1280]{5,...) fusion(pred[]{:T(512)S(6)} %eq.86, ...), kind=kLoop, calls=%fused_computation.34 | loop fusion | flops 4096000 | bytes 18022400 | tf_op jit(solution)/shard_map/jit(_where)/select_n | solution.py:372
  180.8 2.0 copy.198
  182.8 2.1 fusion.6
  185.2 1.9 copy.202
  187.4 1.9 copy.196
  189.4 9.6 %feed.1 = (bf16[128,1280]{1,0:T(8,128)(2,1)S(1)}, bf16[128,1280]{1,0:T(8,128)(2,1)S(1)}, bf16[128,1280]{1,0:T(8,128)(2,1)S(1)}, bf16[128,1280]{1,0:T(8,128)(2,1)...) custom-call(s32[6]{0:T(128)S(1)} %pad_add_fusion.info_ref, ...), custom_call_target="tpu_custom_call" | custom-call | flops 2600000000 | bytes 13000000 | tf_op jit(solution)/shard_map/feed/pallas_call | solution.py:617
  201.7 1.5 collective-permute-start.25
  203.2 3.2 collective-permute-start.22
  210.9 3.0 fusion.1
  213.8 2.3 copy-done.6
  216.1 1.5 collective-permute-start.26
  219.7 4.3 %collective-permute-done.26 = bf16[2,128,160]{2,1,0:T(8,128)(2,1)S(1)} collective-permute-done((bf16[2,128,160]{2,1,0:T(8,128)(2,1)S(1)}, bf16[2,128,160]{2,1,0:T(8,128)(2,1)S(1)}, u32[]{:S(2)}, u32[]{:S(2)}) %collective-permute-start.26) | collective-permute-done | bytes 81952 | tf_op jit(solution)/shard_map/ppermute | solution.py:348
  227.9 4.3 %collective-permute-done.28.grad_far = bf16[4,128,160]{2,1,0:T(8,128)(2,1)S(1)} collective-permute-done((bf16[4,128,160]{2,1,0:T(8,128)(2,1)S(1)}, bf16[4,128,160]{2,1,0:T(8,128)(2,1)S(1)}, u32[]{:S(2)}, u32[]{:S(2)}) %collective-permute-start.28) | collective-permute-done | bytes 163872 | tf_op jit(solution)/shard_map/ppermute | solution.py:353
  232.2 13.5 %attend_back.1 = (bf16[4,128,1280]{2,1,0:T(8,128)(2,1)S(1)}, bf16[4,128,1280]{2,1,0:T(8,128)(2,1)}, bf16[1280,480]{1,0:T(8,128)(2,1)}, f32[1,1280]{1,0:T(1,128)S(1)}, f32[1,160]{1,0:T(1,128)S(1)}) custom-call(s32[6]{0:T(128)S(1)} %pad_add_fusion.info_ref, bf16[4,136,1280]{2,1,0:T(8,128)(2,1)} %copy-done, bf16[4,136,1280]{2,1,0:T(8,128)(2,1)} %copy-done.25, ...), custom_call_target="tpu_custom_call" | custom-call | flops 3500000000 | bytes 12000000 | tf_op jit(solution)/shard_map/attend_back/pallas_call | solution.py:675
  246.1 1.6 fusion.8
  247.9 3.8 collective-permute-start.38
  252.3 9.3 %collective-permute-done.36 = bf16[8,48,480]{2,1,0:T(8,128)(2,1)S(1)} collective-permute-done((bf16[8,48,480]{2,1,0:T(8,128)(2,1)S(1)}, bf16[8,48,480]{2,1,0:T(8,128)(2,1)S(1)}, u32[]{:S(2)}, u32[]{:S(2)}) %collective-permute-start.36) | collective-permute-done | bytes 368672 | tf_op jit(solution)/shard_map/ppermute | solution.py:357
  261.6 8.5 %collective-permute-done.38 = bf16[8,48,480]{2,1,0:T(8,128)(2,1)S(1)} collective-permute-done((bf16[8,48,480]{2,1,0:T(8,128)(2,1)S(1)}, bf16[8,48,480]{2,1,0:T(8,128)(2,1)S(1)}, u32[]{:S(2)}, u32[]{:S(2)}) %collective-permute-start.38) | collective-permute-done | bytes 368672 | tf_op jit(solution)/shard_map/ppermute | solution.py:357
  270.1 14.2 %collective-permute-done.37 = bf16[8,48,480]{2,1,0:T(8,128)(2,1)S(1)} collective-permute-done((bf16[8,48,480]{2,1,0:T(8,128)(2,1)S(1)}, bf16[8,48,480]{2,1,0:T(8,128)(2,1)S(1)}, u32[]{:S(2)}, u32[]{:S(2)}) %collective-permute-start.37) | collective-permute-done | bytes 368672 | tf_op jit(solution)/shard_map/ppermute | solution.py:357
  285.2 3.7 all-to-all-start.1
  289.6 1.7 constant_dynamic-slice_fusion.1
  291.3 5.2 %all-to-all-done.1 = bf16[8,48,480]{2,1,0:T(8,128)(2,1)S(1)} async-done(((bf16[8,48,480]{2,1,0:T(8,128)(2,1)}), bf16[8,48,480]{2,1,0:T(8,128)(2,1)S(1)}, u32[]{:S(2)}, u32[]{:S(2)}) %all-to-all-start.1) | async-done | bytes 368672 | tf_op jit(solution)/shard_map/all_to_all | solution.py:719
  296.6 1.8 reshape.501
  298.4 3.9 fusion.55
  306.1 1.6 add_convert_fusion
  309.9 1.5 collective-permute-start.31
  312.0 6.5 %collective-permute-done.30 = bf16[128,1280]{1,0:T(8,128)(2,1)S(1)} collective-permute-done((bf16[128,1280]{1,0:T(8,128)(2,1)S(1)}, bf16[128,1280]{1,0:T(8,128)(2,1)S(1)}, u32[]{:S(2)}, u32[]{:S(2)}) %collective-permute-start.30) | collective-permute-done | bytes 327712 | tf_op jit(solution)/shard_map/ppermute | solution.py:346
  318.5 6.5 %collective-permute-done.32 = bf16[128,1280]{1,0:T(8,128)(2,1)S(1)} collective-permute-done((bf16[128,1280]{1,0:T(8,128)(2,1)S(1)}, bf16[128,1280]{1,0:T(8,128)(2,1)S(1)}, u32[]{:S(2)}, u32[]{:S(2)}) %collective-permute-start.32) | collective-permute-done | bytes 327712 | tf_op jit(solution)/shard_map/ppermute | solution.py:349
  329.1 3.7 collective-permute-done.33
  332.8 3.4 collective-permute-done.34
  336.3 7.4 %fusion = bf16[4,3,2,2,40,1280]{5,4,3,2,0,1:T(8,128)(2,1)S(1)} fusion(bf16[4,3,2,2,40,1280]{5,4,3,2,0,1:T(8,128)(2,1)} %collective-permute-done.39, pred[]{:T(512)S(6)} %eq.86, bf16[4,3,2,2,2,40,1280]{6,5,4,3,2,0,1:T(8,128)(2,1)} %copy-done.6), kind=kLoop, calls=%fused_computation.2 | loop fusion | flops 12288000 | bytes 19660800 | tf_op jit(solution)/shard_map/convert_element_type | solution.py:649
  346.1 24.2 %collective-permute-done.42 = bf16[2,3,2,40,1280]{4,3,2,0,1:T(8,128)(2,1)S(1)} collective-permute-done((bf16[2,3,2,40,1280]{4,3,2,0,1:T(8,128)(2,1)S(1)}, bf16[2,3,2,40,1280]{4,3,2,0,1:T(8,128)(2,1)S(1)}, u32[]{:S(2)}, u32[]{:S(2)}) %collective-permute-start.42) | collective-permute-done | bytes 1228832 | tf_op jit(solution)/shard_map/ppermute | solution.py:348
  371.8 4.0 collective-permute-start.41
  375.8 8.1 %collective-permute-done.43 = bf16[2,3,40,1280]{3,2,0,1:T(8,128)(2,1)S(1)} collective-permute-done((bf16[2,3,40,1280]{3,2,0,1:T(8,128)(2,1)S(1)}, bf16[2,3,40,1280]{3,2,0,1:T(8,128)(2,1)S(1)}, u32[]{:S(2)}, u32[]{:S(2)}) %collective-permute-start.43) | collective-permute-done | bytes 614432 | tf_op jit(solution)/shard_map/ppermute | solution.py:346
  384.7 2.6 collective-permute-start.44
  387.2 3.9 collective-permute-start.45
  391.9 7.0 %collective-permute-done.44 = bf16[3,40,1280]{2,1,0:T(8,128)(2,1)S(1)} collective-permute-done((bf16[3,40,1280]{2,1,0:T(8,128)(2,1)S(1)}, bf16[3,40,1280]{2,1,0:T(8,128)(2,1)S(1)}, u32[]{:S(2)}, u32[]{:S(2)}) %collective-permute-start.44) | collective-permute-done | bytes 307232 | tf_op jit(solution)/shard_map/ppermute | solution.py:357
  398.9 10.2 %collective-permute-done.45 = bf16[3,40,1280]{2,1,0:T(8,128)(2,1)S(1)} collective-permute-done((bf16[3,40,1280]{2,1,0:T(8,128)(2,1)S(1)}, bf16[3,40,1280]{2,1,0:T(8,128)(2,1)S(1)}, u32[]{:S(2)}, u32[]{:S(2)}) %collective-permute-start.45) | collective-permute-done | bytes 307232 | tf_op jit(solution)/shard_map/ppermute | solution.py:357
  (254 shorter events, 65.5 us)
Async XLA Ops:
  11.5 7.7 %copy-start.14 = (f32[40,1280]{1,0:T(8,128)S(1)}, f32[40,1280]{1,0:T(8,128)}, u32[]{:S(2)}) copy-start(f32[40,1280]{1,0:T(8,128)} %param.20) | copy-start | bytes 614404
  11.5 7.7 %copy-start.15 = (f32[40,1280]{1,0:T(8,128)S(1)}, f32[40,1280]{1,0:T(8,128)}, u32[]{:S(2)}) copy-start(f32[40,1280]{1,0:T(8,128)} %param.22) | copy-start | bytes 614404
  11.5 7.7 %copy-start.16 = (f32[40,1280]{1,0:T(8,128)S(1)}, f32[40,1280]{1,0:T(8,128)}, u32[]{:S(2)}) copy-start(f32[40,1280]{1,0:T(8,128)} %param.21) | copy-start | bytes 614404
  12.8 7.3 %copy-start.21 = (f32[40]{0:T(128)S(1)}, f32[40]{0:T(128)}, u32[]{:S(2)}) copy-start(f32[40]{0:T(128)} %param.25) | copy-start | bytes 484
  12.8 7.4 %copy-start.10 = (bf16[16,8,1280]{2,1,0:T(8,128)(2,1)S(1)}, bf16[16,8,1280]{2,1,0:T(8,128)(2,1)}, u32[]{:S(2)}) copy-start(bf16[16,8,1280]{2,1,0:T(8,128)(2,1)} %param.15) | copy-start | bytes 983044
  13.9 69.8 %all-to-all-start = ((bf16[8,40,480]{2,1,0:T(8,128)(2,1)}), bf16[8,40,480]{2,1,0:T(8,128)(2,1)}, u32[]{:S(2)}, u32[]{:S(2)}) async-start(bf16[8,40,480]{2,1,0:T(8,128)(2,1)} %reshape.478), calls=%async_computation | async-start | bytes 655360 | tf_op jit(solution)/shard_map/all_to_all | solution.py:551
  19.1 7.7 %copy-start.11 = (bf16[16,8,1280]{2,1,0:T(8,128)(2,1)S(1)}, bf16[16,8,1280]{2,1,0:T(8,128)(2,1)}, u32[]{:S(2)}) copy-start(bf16[16,8,1280]{2,1,0:T(8,128)(2,1)} %param.16) | copy-start | bytes 983044
  19.1 36.3 %all-gather.2.cloned.1.call-start = ((), (), s32[]{:S(2)}) async-start(), calls=%async_computation.2 | async-start | bytes 1536000 | tf_op jit(solution)/shard_map/all_gather | solution.py:559
  19.2 8.3 %copy-start.27 = (s32[16]{0:T(128)S(1)}, s32[16]{0:T(128)}, u32[]{:S(2)}) copy-start(s32[16]{0:T(128)} %param.27) | copy-start | bytes 196
  19.2 8.3 %copy-start.28 = (s32[16]{0:T(128)S(1)}, s32[16]{0:T(128)}, u32[]{:S(2)}) copy-start(s32[16]{0:T(128)} %param.26) | copy-start | bytes 196
  20.3 7.8 %collective-permute-start = (bf16[5,8,1280]{2,1,0:T(8,128)(2,1)S(1)}, bf16[5,8,1280]{2,1,0:T(8,128)(2,1)S(1)}, u32[]{:S(2)}, u32[]{:S(2)}) collective-permute-start(bf16[5,8,1280]{2,1,0:T(8,128)(2,1)S(1)} %get-tuple-element.126), channel_id=1, source_target_pairs={{0,8},{8,16},{16,24},{24,0},{1,9},{9,17},{17,25},{25,1},{2,10},{10... | collective-permute-start | bytes 307208 | tf_op jit(solution)/shard_map/ppermute | solution.py:357
  22.3 9.9 %collective-permute-start.1 = (bf16[5,8,1280]{2,1,0:T(8,128)(2,1)S(1)}, bf16[5,8,1280]{2,1,0:T(8,128)(2,1)S(1)}, u32[]{:S(2)}, u32[]{:S(2)}) collective-permute-start(bf16[5,8,1280]{2,1,0:T(8,128)(2,1)S(1)} %get-tuple-element.127), channel_id=1, source_target_pairs={{0,16},{8,24},{16,0},{24,8},{1,17},{9,25},{17,1},{25,9},{2,18},{10... | collective-permute-start | bytes 307208 | tf_op jit(solution)/shard_map/ppermute | solution.py:357
  24.9 34.9 %collective-permute-start.2 = (bf16[5,8,1280]{2,1,0:T(8,128)(2,1)S(1)}, bf16[5,8,1280]{2,1,0:T(8,128)(2,1)S(1)}, u32[]{:S(2)}, u32[]{:S(2)}) collective-permute-start(bf16[5,8,1280]{2,1,0:T(8,128)(2,1)S(1)} %get-tuple-element.128), channel_id=1, source_target_pairs={{0,24},{8,0},{16,8},{24,16},{1,25},{9,1},{17,9},{25,17},{2,26},{10... | collective-permute-start | bytes 307208 | tf_op jit(solution)/shard_map/ppermute | solution.py:357
  32.1 39.7 %copy-start.17 = (bf16[5,8,1280]{2,1,0:T(8,128)(2,1)}, bf16[5,8,1280]{2,1,0:T(8,128)(2,1)S(1)}, u32[]{:S(2)}) copy-start(bf16[5,8,1280]{2,1,0:T(8,128)(2,1)S(1)} %collective-permute-done.1) | copy-start | bytes 307204
  55.3 17.7 %copy-start.8 = (bf16[4,3,40,1280]{3,2,1,0:T(8,128)(2,1)S(1)}, bf16[4,3,40,1280]{3,2,1,0:T(8,128)(2,1)}, u32[]{:S(2)}) copy-start(bf16[4,3,40,1280]{3,2,1,0:T(8,128)(2,1)} %all-gather.2.cloned.1.call-done) | copy-start | bytes 3686404
  56.8 15.1 %collective-permute-start.17 = (bf16[2,3,40,1280]{3,2,1,0:T(8,128)(2,1)S(1)}, bf16[2,3,40,1280]{3,2,1,0:T(8,128)(2,1)S(1)}, u32[]{:S(2)}, u32[]{:S(2)}) collective-permute-start(bf16[2,3,40,1280]{3,2,1,0:T(8,128)(2,1)S(1)} %get-tuple-element.92), channel_id=1, source_target_pairs={{0,1},{1,0},{2,3},{3,2},{4,5},{5,4},{6,7},{7,6},{8,9},{9,8},{10,11... | collective-permute-start | bytes 1843208 | tf_op jit(solution)/shard_map/ppermute | solution.py:346
  58.3 14.7 %collective-permute-start.19 = (bf16[2,3,40,1280]{3,2,1,0:T(8,128)(2,1)S(1)}, bf16[2,3,40,1280]{3,2,1,0:T(8,128)(2,1)S(1)}, u32[]{:S(2)}, u32[]{:S(2)}) collective-permute-start(bf16[2,3,40,1280]{3,2,1,0:T(8,128)(2,1)S(1)} %get-tuple-element.93), channel_id=1, source_target_pairs={{0,4},{4,0},{1,5},{5,1},{2,6},{6,2},{3,7},{7,3},{8,12},{12,8},{9,1... | collective-permute-start | bytes 1843208 | tf_op jit(solution)/shard_map/ppermute | solution.py:348
  59.8 12.0 %copy-start.18 = (bf16[5,8,1280]{2,1,0:T(8,128)(2,1)}, bf16[5,8,1280]{2,1,0:T(8,128)(2,1)S(1)}, u32[]{:S(2)}) copy-start(bf16[5,8,1280]{2,1,0:T(8,128)(2,1)S(1)} %collective-permute-done.2) | copy-start | bytes 307204
  74.4 30.3 %collective-permute-start.20 = (bf16[2,3,2,40,1280]{4,3,1,0,2:T(8,128)(2,1)}, bf16[2,3,2,40,1280]{4,3,1,0,2:T(8,128)(2,1)}, u32[]{:S(2)}, u32[]{:S(2)}) collective-permute-start(bf16[2,3,2,40,1280]{4,3,1,0,2:T(8,128)(2,1)} %pad_maximum_fusion.6), channel_id=1, source_target_pairs={{0,1},{1,0},{2,3},{3,2},{4,5},{5,4},{6,7},{7,6},{8,9},{9,8},{10,11... | collective-permute-start | bytes 3686408 | tf_op jit(solution)/shard_map/ppermute | solution.py:346
  76.1 37.7 %collective-permute-start.18 = (bf16[2,3,2,40,1280]{4,3,1,0,2:T(8,128)(2,1)}, bf16[2,3,2,40,1280]{4,3,1,0,2:T(8,128)(2,1)}, u32[]{:S(2)}, u32[]{:S(2)}) collective-permute-start(bf16[2,3,2,40,1280]{4,3,1,0,2:T(8,128)(2,1)} %pad_maximum_fusion.5), channel_id=1, source_target_pairs={{0,4},{4,0},{1,5},{5,1},{2,6},{6,2},{3,7},{7,3},{8,12},{12,8},{9,1... | collective-permute-start | bytes 3686408 | tf_op jit(solution)/shard_map/ppermute | solution.py:348
  80.1 39.4 %collective-permute-start.8 = (bf16[136,1280]{1,0:T(8,128)(2,1)S(1)}, bf16[136,1280]{1,0:T(8,128)(2,1)}, u32[]{:S(2)}, u32[]{:S(2)}) collective-permute-start(bf16[136,1280]{1,0:T(8,128)(2,1)S(1)} %concatenate.64), channel_id=1, source_target_pairs={{0,5},{1,4},{4,1},{5,0},{2,7},{3,6},{6,3},{7,2},{8,13},{9,12},{12,... | collective-permute-start | bytes 1044488 | tf_op jit(solution)/shard_map/ppermute | solution.py:349
  81.6 40.0 %collective-permute-start.7 = (bf16[136,1280]{1,0:T(8,128)(2,1)S(1)}, bf16[136,1280]{1,0:T(8,128)(2,1)}, u32[]{:S(2)}, u32[]{:S(2)}) collective-permute-start(bf16[136,1280]{1,0:T(8,128)(2,1)S(1)} %concatenate.64), channel_id=1, source_target_pairs={{0,4},{4,0},{1,5},{5,1},{2,6},{6,2},{3,7},{7,3},{8,12},{12,8},{9,1... | collective-permute-start | bytes 1044488 | tf_op jit(solution)/shard_map/ppermute | solution.py:348
  83.1 39.2 %collective-permute-start.6 = (bf16[136,1280]{1,0:T(8,128)(2,1)S(1)}, bf16[136,1280]{1,0:T(8,128)(2,1)}, u32[]{:S(2)}, u32[]{:S(2)}) collective-permute-start(bf16[136,1280]{1,0:T(8,128)(2,1)S(1)} %concatenate.64), channel_id=1, source_target_pairs={{0,1},{1,0},{2,3},{3,2},{4,5},{5,4},{6,7},{7,6},{8,9},{9,8},{10,11... | collective-permute-start | bytes 1044488 | tf_op jit(solution)/shard_map/ppermute | solution.py:346
  104.7 21.3 %collective-permute-start.10 = (bf16[320,480]{1,0:T(8,128)(2,1)}, bf16[320,480]{1,0:T(8,128)(2,1)}, u32[]{:S(2)}, u32[]{:S(2)}) collective-permute-start(bf16[320,480]{1,0:T(8,128)(2,1)} %bitcast.35), channel_id=1, source_target_pairs={{0,24},{8,0},{16,8},{24,16},{1,25},{9,1},{17,9},{25,17},{2,26},{10... | collective-permute-start | bytes 921608 | tf_op jit(solution)/shard_map/ppermute | solution.py:357
  118.7 57.1 %collective-permute-start.21 = (bf16[4,3,2,2,40,1280]{5,4,0,2,3,1:T(8,128)(2,1)}, bf16[4,3,2,2,40,1280]{5,4,0,2,3,1:T(8,128)(2,1)}, u32[]{:S(2)}, u32[]{:S(2)}) collective-permute-start(bf16[4,3,2,2,40,1280]{5,4,0,2,3,1:T(8,128)(2,1)} %copy.194), channel_id=1, source_target_pairs={{0,2},{2,0},{1,3},{3,1},{4,6},{6,4},{5,7},{7,5},{8,10},{10,8},{9,1... | collective-permute-start | bytes 14745608 | tf_op jit(solution)/shard_map/ppermute | solution.py:353
  119.5 44.1 %collective-permute-start.5 = (bf16[4,8,1280]{2,1,0:T(8,128)(2,1)}, bf16[4,8,1280]{2,1,0:T(8,128)(2,1)}, u32[]{:S(2)}, u32[]{:S(2)}) collective-permute-start(bf16[4,8,1280]{2,1,0:T(8,128)(2,1)} %get-tuple-element.108), channel_id=1, source_target_pairs={{0,24},{8,0},{16,8},{24,16},{1,25},{9,1},{17,9},{25,17},{2,26},{10... | collective-permute-start | bytes 245768 | tf_op jit(solution)/shard_map/ppermute | solution.py:357
  121.6 42.0 %collective-permute-start.4 = (bf16[4,8,1280]{2,1,0:T(8,128)(2,1)}, bf16[4,8,1280]{2,1,0:T(8,128)(2,1)}, u32[]{:S(2)}, u32[]{:S(2)}) collective-permute-start(bf16[4,8,1280]{2,1,0:T(8,128)(2,1)} %get-tuple-element.109), channel_id=1, source_target_pairs={{0,16},{8,24},{16,0},{24,8},{1,17},{9,25},{17,1},{25,9},{2,18},{10... | collective-permute-start | bytes 245768 | tf_op jit(solution)/shard_map/ppermute | solution.py:357
  122.3 27.2 %collective-permute-start.11 = (bf16[320,480]{1,0:T(8,128)(2,1)}, bf16[320,480]{1,0:T(8,128)(2,1)S(1)}, u32[]{:S(2)}, u32[]{:S(2)}) collective-permute-start(bf16[320,480]{1,0:T(8,128)(2,1)} %bitcast.35), channel_id=1, source_target_pairs={{0,16},{8,24},{16,0},{24,8},{1,17},{9,25},{17,1},{25,9},{2,18},{10... | collective-permute-start | bytes 921608 | tf_op jit(solution)/shard_map/ppermute | solution.py:357
  125.9 29.1 %copy-start = (bf16[4,136,1280]{2,1,0:T(8,128)(2,1)}, bf16[4,136,1280]{2,1,0:T(8,128)(2,1)S(1)}, u32[]{:S(2)}) copy-start(bf16[4,136,1280]{2,1,0:T(8,128)(2,1)S(1)} %pad_maximum_fusion.4.near_ref) | copy-start | bytes 4177924
  125.9 23.6 %collective-permute-start.12 = (bf16[320,480]{1,0:T(8,128)(2,1)}, bf16[320,480]{1,0:T(8,128)(2,1)S(1)}, u32[]{:S(2)}, u32[]{:S(2)}) collective-permute-start(bf16[320,480]{1,0:T(8,128)(2,1)} %bitcast.35), channel_id=1, source_target_pairs={{0,8},{8,16},{16,24},{24,0},{1,9},{9,17},{17,25},{25,1},{2,10},{10... | collective-permute-start | bytes 921608 | tf_op jit(solution)/shard_map/ppermute | solution.py:357
  149.5 3.2 collective-permute-start.9
  149.5 14.1 %collective-permute-start.3 = (bf16[4,8,1280]{2,1,0:T(8,128)(2,1)S(1)}, bf16[4,8,1280]{2,1,0:T(8,128)(2,1)}, u32[]{:S(2)}, u32[]{:S(2)}) collective-permute-start(bf16[4,8,1280]{2,1,0:T(8,128)(2,1)S(1)} %get-tuple-element.110), channel_id=1, source_target_pairs={{0,8},{8,16},{16,24},{24,0},{1,9},{9,17},{17,25},{25,1},{2,10},{10... | collective-permute-start | bytes 245768 | tf_op jit(solution)/shard_map/ppermute | solution.py:357
  152.0 11.3 %copy-start.1 = (bf16[4,320,480]{2,1,0:T(8,128)(2,1)}, bf16[4,320,480]{2,1,0:T(8,128)(2,1)S(1)}, u32[]{:S(2)}) copy-start(bf16[4,320,480]{2,1,0:T(8,128)(2,1)S(1)} %constant_dynamic-slice_fusion.2) | copy-start | bytes 3686404
  163.3 1.6 collective-permute-start.13
  165.0 7.3 %collective-permute-start.16 = (bf16[2,128,160]{2,1,0:T(8,128)(2,1)S(1)}, bf16[2,128,160]{2,1,0:T(8,128)(2,1)S(1)}, u32[]{:S(2)}, u32[]{:S(2)}) collective-permute-start(bf16[2,128,160]{2,1,0:T(8,128)(2,1)S(1)} %get-tuple-element.97), channel_id=1, source_target_pairs={{0,5},{1,4},{4,1},{5,0},{2,7},{3,6},{6,3},{7,2},{8,13},{9,12},{12,... | collective-permute-start | bytes 245768 | tf_op jit(solution)/shard_map/ppermute | solution.py:349
  167.5 7.0 %collective-permute-start.14 = (bf16[2,128,160]{2,1,0:T(8,128)(2,1)S(1)}, bf16[2,128,160]{2,1,0:T(8,128)(2,1)S(1)}, u32[]{:S(2)}, u32[]{:S(2)}) collective-permute-start(bf16[2,128,160]{2,1,0:T(8,128)(2,1)S(1)} %get-tuple-element.99), channel_id=1, source_target_pairs={{0,1},{1,0},{2,3},{3,2},{4,5},{5,4},{6,7},{7,6},{8,9},{9,8},{10,11... | collective-permute-start | bytes 245768 | tf_op jit(solution)/shard_map/ppermute | solution.py:346
  168.0 6.4 %collective-permute-start.15 = (bf16[2,128,160]{2,1,0:T(8,128)(2,1)S(1)}, bf16[2,128,160]{2,1,0:T(8,128)(2,1)S(1)}, u32[]{:S(2)}, u32[]{:S(2)}) collective-permute-start(bf16[2,128,160]{2,1,0:T(8,128)(2,1)S(1)} %get-tuple-element.100), channel_id=1, source_target_pairs={{0,4},{4,0},{1,5},{5,1},{2,6},{6,2},{3,7},{7,3},{8,12},{12,8},{9,1... | collective-permute-start | bytes 245768 | tf_op jit(solution)/shard_map/ppermute | solution.py:348
  201.7 16.5 %collective-permute-start.25 = (bf16[2,128,160]{2,1,0:T(8,128)(2,1)}, bf16[2,128,160]{2,1,0:T(8,128)(2,1)}, u32[]{:S(2)}, u32[]{:S(2)}) collective-permute-start(bf16[2,128,160]{2,1,0:T(8,128)(2,1)} %get-tuple-element.48), channel_id=1, source_target_pairs={{0,1},{1,0},{2,3},{3,2},{4,5},{5,4},{6,7},{7,6},{8,9},{9,8},{10,11... | collective-permute-start | bytes 245768 | tf_op jit(solution)/shard_map/ppermute | solution.py:346
  203.2 21.5 %collective-permute-start.22 = (bf16[4,8,1280]{2,1,0:T(8,128)(2,1)}, bf16[4,8,1280]{2,1,0:T(8,128)(2,1)S(1)}, u32[]{:S(2)}, u32[]{:S(2)}) collective-permute-start(bf16[4,8,1280]{2,1,0:T(8,128)(2,1)} %get-tuple-element.105), channel_id=1, source_target_pairs={{0,24},{8,0},{16,8},{24,16},{1,25},{9,1},{17,9},{25,17},{2,26},{10... | collective-permute-start | bytes 245768 | tf_op jit(solution)/shard_map/ppermute | solution.py:357
  216.1 7.8 %collective-permute-start.26 = (bf16[2,128,160]{2,1,0:T(8,128)(2,1)S(1)}, bf16[2,128,160]{2,1,0:T(8,128)(2,1)S(1)}, u32[]{:S(2)}, u32[]{:S(2)}) collective-permute-start(bf16[2,128,160]{2,1,0:T(8,128)(2,1)S(1)} %copy-done.5), channel_id=1, source_target_pairs={{0,4},{4,0},{1,5},{5,1},{2,6},{6,2},{3,7},{7,3},{8,12},{12,8},{9,1... | collective-permute-start | bytes 245768 | tf_op jit(solution)/shard_map/ppermute | solution.py:348
  217.6 6.3 %collective-permute-start.27 = (bf16[2,128,160]{2,1,0:T(8,128)(2,1)S(1)}, bf16[2,128,160]{2,1,0:T(8,128)(2,1)S(1)}, u32[]{:S(2)}, u32[]{:S(2)}) collective-permute-start(bf16[2,128,160]{2,1,0:T(8,128)(2,1)S(1)} %get-tuple-element.50), channel_id=1, source_target_pairs={{0,5},{1,4},{4,1},{5,0},{2,7},{3,6},{6,3},{7,2},{8,13},{9,12},{12,... | collective-permute-start | bytes 245768 | tf_op jit(solution)/shard_map/ppermute | solution.py:349
  218.2 8.3 %collective-permute-start.24 = (bf16[4,8,1280]{2,1,0:T(8,128)(2,1)}, bf16[4,8,1280]{2,1,0:T(8,128)(2,1)S(1)}, u32[]{:S(2)}, u32[]{:S(2)}) collective-permute-start(bf16[4,8,1280]{2,1,0:T(8,128)(2,1)} %get-tuple-element.104), channel_id=1, source_target_pairs={{0,8},{8,16},{16,24},{24,0},{1,9},{9,17},{17,25},{25,1},{2,10},{10... | collective-permute-start | bytes 245768 | tf_op jit(solution)/shard_map/ppermute | solution.py:357
  218.2 7.7 %collective-permute-start.23 = (bf16[4,8,1280]{2,1,0:T(8,128)(2,1)}, bf16[4,8,1280]{2,1,0:T(8,128)(2,1)S(1)}, u32[]{:S(2)}, u32[]{:S(2)}) collective-permute-start(bf16[4,8,1280]{2,1,0:T(8,128)(2,1)} %get-tuple-element.106), channel_id=1, source_target_pairs={{0,16},{8,24},{16,0},{24,8},{1,17},{9,25},{17,1},{25,9},{2,18},{10... | collective-permute-start | bytes 245768 | tf_op jit(solution)/shard_map/ppermute | solution.py:357
  224.0 112.3 %collective-permute-start.39 = (bf16[4,3,2,2,40,1280]{5,4,3,2,0,1:T(8,128)(2,1)}, bf16[4,3,2,2,40,1280]{5,4,3,2,0,1:T(8,128)(2,1)}, u32[]{:S(2)}, u32[]{:S(2)}) collective-permute-start(bf16[4,3,2,2,40,1280]{5,4,3,2,0,1:T(8,128)(2,1)} %fusion.1), channel_id=1, source_target_pairs={{0,2},{2,0},{1,3},{3,1},{4,6},{6,4},{5,7},{7,5},{8,10},{10,8},{9,1... | collective-permute-start | bytes 14745608 | tf_op jit(solution)/shard_map/ppermute | solution.py:353
  224.1 8.1 %collective-permute-start.28 = (bf16[4,128,160]{2,1,0:T(8,128)(2,1)S(1)}, bf16[4,128,160]{2,1,0:T(8,128)(2,1)S(1)}, u32[]{:S(2)}, u32[]{:S(2)}) collective-permute-start(bf16[4,128,160]{2,1,0:T(8,128)(2,1)S(1)} %pad_maximum_fusion.12), channel_id=1, source_target_pairs={{0,2},{2,0},{1,3},{3,1},{4,6},{6,4},{5,7},{7,5},{8,10},{10,8},{9,1... | collective-permute-start | bytes 491528 | tf_op jit(solution)/shard_map/ppermute | solution.py:353
  224.7 7.5 %copy-start.12 = (bf16[4,8,1280]{2,1,0:T(8,128)(2,1)}, bf16[4,8,1280]{2,1,0:T(8,128)(2,1)S(1)}, u32[]{:S(2)}) copy-start(bf16[4,8,1280]{2,1,0:T(8,128)(2,1)S(1)} %collective-permute-done.22) | copy-start | bytes 245764
  247.8 13.8 %collective-permute-start.36 = (bf16[8,48,480]{2,1,0:T(8,128)(2,1)S(1)}, bf16[8,48,480]{2,1,0:T(8,128)(2,1)S(1)}, u32[]{:S(2)}, u32[]{:S(2)}) collective-permute-start(bf16[8,48,480]{2,1,0:T(8,128)(2,1)S(1)} %get-tuple-element.78), channel_id=1, source_target_pairs={{0,8},{8,16},{16,24},{24,0},{1,9},{9,17},{17,25},{25,1},{2,10},{10... | collective-permute-start | bytes 1105928 | tf_op jit(solution)/shard_map/ppermute | solution.py:357
  247.9 22.2 %collective-permute-start.38 = (bf16[8,48,480]{2,1,0:T(8,128)(2,1)S(1)}, bf16[8,48,480]{2,1,0:T(8,128)(2,1)S(1)}, u32[]{:S(2)}, u32[]{:S(2)}) collective-permute-start(bf16[8,48,480]{2,1,0:T(8,128)(2,1)S(1)} %get-tuple-element.79), channel_id=1, source_target_pairs={{0,24},{8,0},{16,8},{24,16},{1,25},{9,1},{17,9},{25,17},{2,26},{10... | collective-permute-start | bytes 1105928 | tf_op jit(solution)/shard_map/ppermute | solution.py:357
  251.7 32.6 %collective-permute-start.37 = (bf16[8,48,480]{2,1,0:T(8,128)(2,1)S(1)}, bf16[8,48,480]{2,1,0:T(8,128)(2,1)S(1)}, u32[]{:S(2)}, u32[]{:S(2)}) collective-permute-start(bf16[8,48,480]{2,1,0:T(8,128)(2,1)S(1)} %get-tuple-element.80), channel_id=1, source_target_pairs={{0,16},{8,24},{16,0},{24,8},{1,17},{9,25},{17,1},{25,9},{2,18},{10... | collective-permute-start | bytes 1105928 | tf_op jit(solution)/shard_map/ppermute | solution.py:357
  252.3 53.8 %collective-permute-start.29 = (bf16[4,128,1280]{2,1,0:T(8,128)(2,1)}, bf16[4,128,1280]{2,1,0:T(8,128)(2,1)}, u32[]{:S(2)}, u32[]{:S(2)}) collective-permute-start(bf16[4,128,1280]{2,1,0:T(8,128)(2,1)} %get-tuple-element.52), channel_id=1, source_target_pairs={{0,2},{2,0},{1,3},{3,1},{4,6},{6,4},{5,7},{7,5},{8,10},{10,8},{9,1... | collective-permute-start | bytes 3932168 | tf_op jit(solution)/shard_map/ppermute | solution.py:353
  285.2 11.2 %all-to-all-start.1 = ((bf16[8,48,480]{2,1,0:T(8,128)(2,1)}), bf16[8,48,480]{2,1,0:T(8,128)(2,1)S(1)}, u32[]{:S(2)}, u32[]{:S(2)}) async-start(bf16[8,48,480]{2,1,0:T(8,128)(2,1)} %fusion.15), calls=%async_computation.1 | async-start | bytes 786432 | tf_op jit(solution)/shard_map/all_to_all | solution.py:719
  307.8 10.6 %collective-permute-start.30 = (bf16[128,1280]{1,0:T(8,128)(2,1)S(1)}, bf16[128,1280]{1,0:T(8,128)(2,1)S(1)}, u32[]{:S(2)}, u32[]{:S(2)}) collective-permute-start(bf16[128,1280]{1,0:T(8,128)(2,1)S(1)} %get-tuple-element.84), channel_id=1, source_target_pairs={{0,1},{1,0},{2,3},{3,2},{4,5},{5,4},{6,7},{7,6},{8,9},{9,8},{10,11... | collective-permute-start | bytes 983048 | tf_op jit(solution)/shard_map/ppermute | solution.py:346
  308.9 16.0 %collective-permute-start.32 = (bf16[128,1280]{1,0:T(8,128)(2,1)S(1)}, bf16[128,1280]{1,0:T(8,128)(2,1)S(1)}, u32[]{:S(2)}, u32[]{:S(2)}) collective-permute-start(bf16[128,1280]{1,0:T(8,128)(2,1)S(1)} %get-tuple-element.85), channel_id=1, source_target_pairs={{0,5},{1,4},{4,1},{5,0},{2,7},{3,6},{6,3},{7,2},{8,13},{9,12},{12,... | collective-permute-start | bytes 983048 | tf_op jit(solution)/shard_map/ppermute | solution.py:349
  309.9 16.4 %collective-permute-start.31 = (bf16[128,1280]{1,0:T(8,128)(2,1)S(1)}, bf16[128,1280]{1,0:T(8,128)(2,1)S(1)}, u32[]{:S(2)}, u32[]{:S(2)}) collective-permute-start(bf16[128,1280]{1,0:T(8,128)(2,1)S(1)} %get-tuple-element.86), channel_id=1, source_target_pairs={{0,4},{4,0},{1,5},{5,1},{2,6},{6,2},{3,7},{7,3},{8,12},{12,8},{9,1... | collective-permute-start | bytes 983048 | tf_op jit(solution)/shard_map/ppermute | solution.py:348
  327.0 5.8 %collective-permute-start.33 = (bf16[4,8,1280]{2,1,0:T(8,128)(2,1)S(1)}, bf16[4,8,1280]{2,1,0:T(8,128)(2,1)S(1)}, u32[]{:S(2)}, u32[]{:S(2)}) collective-permute-start(bf16[4,8,1280]{2,1,0:T(8,128)(2,1)S(1)} %get-tuple-element.102), channel_id=1, source_target_pairs={{0,24},{8,0},{16,8},{24,16},{1,25},{9,1},{17,9},{25,17},{2,26},{10... | collective-permute-start | bytes 245768 | tf_op jit(solution)/shard_map/ppermute | solution.py:357
  328.2 8.0 %collective-permute-start.35 = (bf16[4,8,1280]{2,1,0:T(8,128)(2,1)S(1)}, bf16[4,8,1280]{2,1,0:T(8,128)(2,1)S(1)}, u32[]{:S(2)}, u32[]{:S(2)}) collective-permute-start(bf16[4,8,1280]{2,1,0:T(8,128)(2,1)S(1)} %get-tuple-element.101), channel_id=1, source_target_pairs={{0,8},{8,16},{16,24},{24,0},{1,9},{9,17},{17,25},{25,1},{2,10},{10... | collective-permute-start | bytes 245768 | tf_op jit(solution)/shard_map/ppermute | solution.py:357
  329.1 7.1 %collective-permute-start.34 = (bf16[4,8,1280]{2,1,0:T(8,128)(2,1)S(1)}, bf16[4,8,1280]{2,1,0:T(8,128)(2,1)S(1)}, u32[]{:S(2)}, u32[]{:S(2)}) collective-permute-start(bf16[4,8,1280]{2,1,0:T(8,128)(2,1)S(1)} %get-tuple-element.103), channel_id=1, source_target_pairs={{0,16},{8,24},{16,0},{24,8},{1,17},{9,25},{17,1},{25,9},{2,18},{10... | collective-permute-start | bytes 245768 | tf_op jit(solution)/shard_map/ppermute | solution.py:357
  343.8 26.5 %collective-permute-start.42 = (bf16[2,3,2,40,1280]{4,3,2,0,1:T(8,128)(2,1)S(1)}, bf16[2,3,2,40,1280]{4,3,2,0,1:T(8,128)(2,1)S(1)}, u32[]{:S(2)}, u32[]{:S(2)}) collective-permute-start(bf16[2,3,2,40,1280]{4,3,2,0,1:T(8,128)(2,1)S(1)} %fusion.9), channel_id=1, source_target_pairs={{0,4},{4,0},{1,5},{5,1},{2,6},{6,2},{3,7},{7,3},{8,12},{12,8},{9,1... | collective-permute-start | bytes 3686408 | tf_op jit(solution)/shard_map/ppermute | solution.py:348
  345.3 26.0 %collective-permute-start.40 = (bf16[2,3,2,40,1280]{4,3,0,1,2:T(8,128)(2,1)S(1)}, bf16[2,3,2,40,1280]{4,3,0,1,2:T(8,128)(2,1)S(1)}, u32[]{:S(2)}, u32[]{:S(2)}) collective-permute-start(bf16[2,3,2,40,1280]{4,3,0,1,2:T(8,128)(2,1)S(1)} %select_bitcast_fusion.4), channel_id=1, source_target_pairs={{0,1},{1,0},{2,3},{3,2},{4,5},{5,4},{6,7},{7,6},{8,9},{9,8},{10,11... | collective-permute-start | bytes 3686408 | tf_op jit(solution)/shard_map/ppermute | solution.py:346
  370.8 13.1 %collective-permute-start.43 = (bf16[2,3,40,1280]{3,2,0,1:T(8,128)(2,1)S(1)}, bf16[2,3,40,1280]{3,2,0,1:T(8,128)(2,1)S(1)}, u32[]{:S(2)}, u32[]{:S(2)}) collective-permute-start(bf16[2,3,40,1280]{3,2,0,1:T(8,128)(2,1)S(1)} %fusion.19), channel_id=1, source_target_pairs={{0,1},{1,0},{2,3},{3,2},{4,5},{5,4},{6,7},{7,6},{8,9},{9,8},{10,11... | collective-permute-start | bytes 1843208 | tf_op jit(solution)/shard_map/ppermute | solution.py:346
  371.8 12.3 %collective-permute-start.41 = (bf16[2,3,40,1280]{3,2,0,1:T(8,128)(2,1)S(1)}, bf16[2,3,40,1280]{3,2,0,1:T(8,128)(2,1)S(1)}, u32[]{:S(2)}, u32[]{:S(2)}) collective-permute-start(bf16[2,3,40,1280]{3,2,0,1:T(8,128)(2,1)S(1)} %select_bitcast_fusion.9), channel_id=1, source_target_pairs={{0,4},{4,0},{1,5},{5,1},{2,6},{6,2},{3,7},{7,3},{8,12},{12,8},{9,1... | collective-permute-start | bytes 1843208 | tf_op jit(solution)/shard_map/ppermute | solution.py:348
  384.7 14.2 %collective-permute-start.44 = (bf16[3,40,1280]{2,1,0:T(8,128)(2,1)S(1)}, bf16[3,40,1280]{2,1,0:T(8,128)(2,1)S(1)}, u32[]{:S(2)}, u32[]{:S(2)}) collective-permute-start(bf16[3,40,1280]{2,1,0:T(8,128)(2,1)S(1)} %get-tuple-element.87), channel_id=1, source_target_pairs={{0,8},{8,16},{16,24},{24,0},{1,9},{9,17},{17,25},{25,1},{2,10},{10... | collective-permute-start | bytes 921608 | tf_op jit(solution)/shard_map/ppermute | solution.py:357
  387.2 21.8 %collective-permute-start.45 = (bf16[3,40,1280]{2,1,0:T(8,128)(2,1)S(1)}, bf16[3,40,1280]{2,1,0:T(8,128)(2,1)S(1)}, u32[]{:S(2)}, u32[]{:S(2)}) collective-permute-start(bf16[3,40,1280]{2,1,0:T(8,128)(2,1)S(1)} %get-tuple-element.88), channel_id=1, source_target_pairs={{0,16},{8,24},{16,0},{24,8},{1,17},{9,25},{17,1},{25,9},{2,18},{10... | collective-permute-start | bytes 921608 | tf_op jit(solution)/shard_map/ppermute | solution.py:357
  391.2 17.9 %collective-permute-start.46 = (bf16[3,40,1280]{2,1,0:T(8,128)(2,1)S(1)}, bf16[3,40,1280]{2,1,0:T(8,128)(2,1)S(1)}, u32[]{:S(2)}, u32[]{:S(2)}) collective-permute-start(bf16[3,40,1280]{2,1,0:T(8,128)(2,1)S(1)} %get-tuple-element.89), channel_id=1, source_target_pairs={{0,24},{8,0},{16,8},{24,16},{1,25},{9,1},{17,9},{25,17},{2,26},{10... | collective-permute-start | bytes 921608 | tf_op jit(solution)/shard_map/ppermute | solution.py:357
  (15 other events, 53.8 us)
Sparse Core Ops, SparseCore 0:
  22.0 33.2 all-gather.1

commit v2 on v1

--- a/solution.py
+++ b/solution.py
@@ -471,39 +471,69 @@
         scale_grad[...] = scale_acc[...]
 
 
+def block_index(z_index, y_index, core):
+    return pl.ds(pl.multiple_of((4 * z_index + 2 * y_index + core) * 80, 80), 80)
+
+
+def source_rows(info_ref, chip, core):
+    source = info_ref[1] ^ (CODES[chip] + 2 * core)
+    return pl.ds(pl.multiple_of(source * 160, 160), 160)
+
+
 def feed_kernel(
-    info_ref, x_ref, g_ref, att_0, att_1, att_2, att_3, gain_ref, wo_ref, up_ref, down_ref,
+    info_ref, x_ref, g_ref, att_0, att_1, att_2, att_3, gain_ref,
+    near_a, across_a, all_b, far_near_a, far_across_a, far_b,
     out_ref, act_ref, hid_ref, dup_ref, dm_ref, dmid_ref, datt_0, datt_1, datt_2, datt_3, gain_grad,
+    weights, sems,
 ):
-    plane_index = info_ref[1]
+    y_index, core_index = info_ref[1] // 4, (info_ref[1] // 2) % 2
+    copies = []
+    for w in range(3):
+        moved = []
+        for core, refs in ((core_index, (near_a, across_a, all_b)), (1 - core_index, (far_near_a, far_across_a, far_b))):
+            for half in range(2):
+                moved.append((refs[0].at[half, w], half, y_index, core))
+                moved.append((refs[1].at[half, w], half, 1 - y_index, core))
+                for row in range(2):
+                    moved.append((refs[2].at[half, w, row], 2 + half, row, core))
+        copies.append([
+            pltpu.make_async_copy(src, weights.at[w, block_index(*place)], sems.at[w, i])
+            for i, (src, *place) in enumerate(moved)
+        ])
+    for group in copies:
+        for copy in group:
+            copy.start()
     atts, datts = (att_0, att_1, att_2, att_3), (datt_0, datt_1, datt_2, datt_3)
 
-    def rows_of(chip, core):
-        source = plane_index ^ (CODES[chip] + 2 * core)
-        return pl.ds(pl.multiple_of(source * 160, 160), 160)
-
+    for copy in copies[0]:
+        copy.wait()
     middle = x_ref[...].astype(jnp.float32)
     for chip in range(4):
         for core in range(2):
             middle += jnp.dot(
-                atts[chip][core], wo_ref[rows_of(chip, core), :], preferred_element_type=jnp.float32
+                atts[chip][core], weights[0, source_rows(info_ref, chip, core), :],
+                preferred_element_type=jnp.float32,
             )
     inverse = lax.rsqrt(jnp.mean(middle * middle, axis=1, keepdims=True) + 1e-06)
     normed = middle * inverse
     gain = gain_ref[...]
     hidden = (normed * gain).astype(jnp.bfloat16)
     hid_ref[...] = hidden
-    up = jnp.dot(hidden, up_ref[...], preferred_element_type=jnp.float32)
+    for copy in copies[1]:
+        copy.wait()
+    up = jnp.dot(hidden, weights[1], preferred_element_type=jnp.float32)
     sigma = jax.nn.sigmoid(up)
     active = (up * sigma).astype(jnp.bfloat16)
     act_ref[...] = active
-    down = jnp.dot(active, down_ref[...], preferred_element_type=jnp.float32)
+    for copy in copies[2]:
+        copy.wait()
+    down = jnp.dot(active, weights[2], preferred_element_type=jnp.float32)
     out_ref[...] = (middle + down).astype(jnp.bfloat16)
     cot = g_ref[...]
-    grad_act = mult_trans(cot, down_ref[...])
+    grad_act = mult_trans(cot, weights[2])
     grad_up = (grad_act * sigma * (1.0 + up * (1.0 - sigma))).astype(jnp.bfloat16)
     dup_ref[...] = grad_up
-    grad_hidden = mult_trans(grad_up, up_ref[...])
+    grad_hidden = mult_trans(grad_up, weights[1])
     gain_grad[...] = jnp.sum(grad_hidden * normed, axis=0, keepdims=True)
     grad_mid = cot.astype(jnp.float32) + norm_back(grad_hidden, normed, inverse, gain)
     dmid_ref[...] = grad_mid
@@ -511,7 +541,39 @@
     dm_ref[...] = low
     for chip in range(4):
         for core in range(2):
-            datts[chip][core] = mult_trans(low, wo_ref[rows_of(chip, core), :]).astype(jnp.bfloat16)
+            datts[chip][core] = mult_trans(low, weights[0, source_rows(info_ref, chip, core), :]).astype(jnp.bfloat16)
+
+
+def grads_kernel(
+    info_ref, att_0, att_1, att_2, att_3, hid_ref, act_ref, dup_ref, dm_ref, g_ref,
+    kept, away, stage, sems,
+):
+    core_index = (info_ref[1] // 2) % 2
+    copies = []
+
+    def leave(w):
+        for z_index in range(4):
+            for row in range(2):
+                for which, (core, target) in enumerate(((core_index, kept), (1 - core_index, away))):
+                    copy = pltpu.make_async_copy(
+                        stage.at[w, block_index(z_index, row, core)],
+                        target.at[z_index, w, row],
+                        sems.at[w, 4 * z_index + 2 * row + which],
+                    )
+                    copy.start()
+                    copies.append(copy)
+
+    for w, left, right in ((2, act_ref, g_ref), (1, hid_ref, dup_ref)):
+        for chunk in range(5):
+            part = slice(256 * chunk, 256 * chunk + 256)
+            stage[w, part, :] = trans_mult(left[:, part], right[...]).astype(jnp.bfloat16)
+        leave(w)
+    for chip, att in enumerate((att_0, att_1, att_2, att_3)):
+        for core in range(2):
+            stage[0, source_rows(info_ref, chip, core), :] = trans_mult(att[core], dm_ref[...]).astype(jnp.bfloat16)
+    leave(0)
+    for copy in copies:
+        copy.wait()
 
 
 def whole(shape):
@@ -553,20 +615,21 @@
     w_qkv = by_source([qkv] + [ring_shift(qkv, k) for k in (1, 2, 3)], z).reshape(width, 480)
 
     near = jnp.stack([own] + [plane_shift(own, step) for step in (1, 2, 3)])
-    far = core_swap(near)
 
     big = jnp.stack([w_output, w_up, w_down]).astype(bf16)
     big = lax.all_gather(big, "z", axis=0)
+    big, near = lax.optimization_barrier((big, near))
+    far = core_swap(near)
     part_a, part_b = big[:2], big[2:]
-    part_a = pair(part_a, plane_shift(part_a, 1), x, 2)
+    near_a = pair(part_a, plane_shift(part_a, 1), x, 2).reshape(2, 3, 80, width)
     part_b = pair(part_b, plane_shift(part_b, 2), y, 2)
-    part_a = pair(part_a, plane_shift(part_a, 2), y, 2)
-    part_b = pair(part_b, plane_shift(part_b, 1), x, 3)
-    big = jnp.concatenate([part_a, part_b])
-    other = core_swap(big)
-    w_out_full, w_up_full, w_down_full = (
-        pair(big[:, i], other[:, i], c, 2).reshape(width, width) for i in range(3)
-    )
+    near_a, part_b, w_qkv, cot_four = lax.optimization_barrier((near_a, part_b, w_qkv, cot_four))
+    cot_sent = [pick(cot_four, (z + k) % 4) for k in range(4)]
+    cot_got = [cot_sent[0]] + [ring_shift(cot_sent[k], k) for k in (1, 2, 3)]
+    cot_rows = jnp.stack(cot_got, axis=1).reshape(128, width)
+
+    across_a = plane_shift(near_a, 2)
+    across_b = plane_shift(part_b, 1)
 
     vecs = jnp.stack([near[:, 128:132, :120], far[:, 128:132, :120]])
     vecs = vecs.astype(f32).reshape(2, 2, 2, 4, 120)
@@ -599,51 +662,61 @@
             jax.ShapeDtypeStruct((4, 128, 160), bf16),
         ],
         compiler_params=limit,
-        cost_estimate=pl.CostEstimate(flops=1_500_000_000, bytes_accessed=8_000_000, transcendentals=600_000),
+        cost_estimate=pl.CostEstimate(flops=9_000_000_000, bytes_accessed=8_000_000, transcendentals=600_000),
         name="attend",
     )(info, near, far, gain_one, query_mult, w_qkv)
 
+    att_near, att_far, cot_rows, near_a = lax.optimization_barrier((att_near, att_far, cot_rows, near_a))
+    far_near_a = core_swap(near_a)
     att_pair = jnp.stack([att_near, core_swap(att_far)], axis=1)
     atts = [att_pair[0]] + [plane_shift(att_pair[step], step) for step in (1, 2, 3)]
-
-    cot_sent = [pick(cot_four, (z + k) % 4) for k in range(4)]
-    cot_got = [cot_sent[0]] + [ring_shift(cot_sent[k], k) for k in (1, 2, 3)]
-    cot_rows = jnp.stack(cot_got, axis=1).reshape(128, width)
+    *atts, far_near_a, across_a, across_b = lax.optimization_barrier((*atts, far_near_a, across_a, across_b))
+    far_across_a = core_swap(across_a)
+    all_b = pair(part_b, across_b, x, 3).reshape(2, 3, 2, 80, width)
+    far_b = core_swap(all_b)
 
     low_rows = jax.ShapeDtypeStruct((128, width), bf16)
     datt_shape = jax.ShapeDtypeStruct((2, 128, 160), bf16)
     smem = pl.BlockSpec(memory_space=pltpu.SMEM)
     vmem = pl.BlockSpec(memory_space=pltpu.VMEM)
+    hbm = pl.BlockSpec(memory_space=pl.ANY)
     out_rows, active, hidden_two, grad_up, dm, grad_mid, *datts, gain_two_grad = pl.pallas_call(
         feed_kernel,
-        in_specs=[smem] + [vmem] * 10,
+        in_specs=[smem] + [vmem] * 7 + [hbm] * 6,
         out_specs=[vmem] * 11,
         out_shape=[low_rows] * 5
         + [jax.ShapeDtypeStruct((128, width), f32)]
         + [datt_shape] * 4
         + [jax.ShapeDtypeStruct((1, width), f32)],
+        scratch_shapes=[pltpu.VMEM((3, width, width), bf16), pltpu.SemaphoreType.DMA((3, 16))],
         compiler_params=limit,
-        cost_estimate=pl.CostEstimate(flops=2_600_000_000, bytes_accessed=13_000_000, transcendentals=200_000),
+        cost_estimate=pl.CostEstimate(flops=12_000_000_000, bytes_accessed=13_000_000, transcendentals=200_000),
         name="feed",
-    )(info, x_rows, cot_rows, *atts, gain_two, w_out_full, w_up_full, w_down_full)
+    )(info, x_rows, cot_rows, *atts, gain_two, near_a, across_a, all_b, far_near_a, far_across_a, far_b)
+
+    def home(rows):
+        rows = rows.reshape(4, 4, 8, width)
+        parts = [rows[:, 0]] + [ring_shift(rows[:, k], -k) for k in (1, 2, 3)]
+        line = jnp.stack(parts + parts[:3])
+        return lax.dynamic_slice_in_dim(line, (4 - z) % 4, 4, 0).reshape(16, 8, width)
 
     back = [datts[0]] + [plane_shift(datts[step], step) for step in (1, 2, 3)]
+    *back, out_rows = lax.optimization_barrier((*back, out_rows))
+    outputs = home(out_rows)
     grad_att_near = jnp.stack([item[0] for item in back])
     grad_att_far = core_swap(jnp.stack([item[1] for item in back]))
 
-    att_all = jnp.stack(atts).reshape(2, 2, 2, 128, 160)
-    att_all = jnp.where(y == 0, att_all, att_all[::-1])
-    att_all = jnp.where(x == 0, att_all, att_all[:, ::-1])
-    att_all = jnp.where(c == 0, att_all, att_all[:, :, ::-1])
-    att_all = att_all.transpose(3, 0, 2, 1, 4).reshape(128, width)
-
-    def weight_grad(left, right):
-        made = lax.dot_general(left, right, (((0,), (0,)), ((), ())), preferred_element_type=bf16)
-        return made.reshape(4, 2, 2, 2, 40, width)
-
-    grads = jnp.stack(
-        [weight_grad(att_all, dm), weight_grad(hidden_two, grad_up), weight_grad(active, cot_rows)], axis=1
-    )
+    block_shape = jax.ShapeDtypeStruct((4, 3, 2, 80, width), bf16)
+    kept, away = pl.pallas_call(
+        grads_kernel,
+        in_specs=[smem] + [vmem] * 9,
+        out_specs=[hbm] * 2,
+        out_shape=[block_shape] * 2,
+        scratch_shapes=[pltpu.VMEM((3, width, width), bf16), pltpu.SemaphoreType.DMA((3, 16))],
+        compiler_params=limit,
+        cost_estimate=pl.CostEstimate(flops=6_000_000_000, bytes_accessed=12_000_000, transcendentals=0),
+        name="grads",
+    )(info, *atts, hidden_two, active, grad_up, dm, cot_rows)
 
     def added(left, right):
         return (left.astype(f32) + right.astype(f32)).astype(bf16)
@@ -652,25 +725,21 @@
         first, second = (lax.index_in_dim(array, i, axis, keepdims=False) for i in (0, 1))
         return jnp.where(index == 0, first, second), jnp.where(index == 0, second, first)
 
-    kept, away = halves(grads, c, 3)
     kept = added(kept, core_swap(away))
+    kept, grad_att_near, grad_att_far, outputs = lax.optimization_barrier(
+        (kept, grad_att_near, grad_att_far, outputs)
+    )
+    kept = kept.reshape(4, 3, 2, 2, 40, width)
     kept_a, away_a = halves(kept[:2], x, 3)
     kept_b, away_b = halves(kept[2:], y, 2)
     kept_a = added(kept_a, plane_shift(away_a, 1))
     kept_b = added(kept_b, plane_shift(away_b, 2))
-    kept_a, away_a = halves(kept_a, y, 2)
-    kept_b, away_b = halves(kept_b, x, 2)
-    kept_a = added(kept_a, plane_shift(away_a, 2))
-    kept_b = added(kept_b, plane_shift(away_b, 1))
-    kept = jnp.concatenate([kept_a, kept_b])
-
     def ring_sum(array):
         total = pick(array, z).astype(f32)
         for k in (1, 2, 3):
             total += ring_shift(pick(array, (z + k) % 4), k).astype(f32)
         return total
 
-    big_sums = ring_sum(kept)
 
     hid_near, hid_far, qkv_grad, gain_one_grad, scale_grad = pl.pallas_call(
         attend_back_kernel,
@@ -698,38 +767,46 @@
             jax.ShapeDtypeStruct((1, 160), f32),
         ],
         compiler_params=limit,
-        cost_estimate=pl.CostEstimate(flops=3_500_000_000, bytes_accessed=12_000_000, transcendentals=600_000),
+        cost_estimate=pl.CostEstimate(flops=15_000_000_000, bytes_accessed=12_000_000, transcendentals=600_000),
         name="attend_back",
     )(info, near, far, gain_one, query_mult, w_qkv, pre, grad_att_near, grad_att_far)
 
-    hid = added(hid_near, core_swap(hid_far))
-    grad_hid = hid[0].astype(f32)
-    for step in (1, 2, 3):
-        grad_hid += plane_shift(hid[step], step).astype(f32)
-    wide = x_rows.astype(f32)
-    inverse = lax.rsqrt(jnp.mean(wide * wide, axis=1, keepdims=True) + 1e-06)
-    grad_in = (grad_mid + norm_back(grad_hid, wide * inverse, inverse, gain_one)).astype(bf16)
-
+    kept_a, kept_b, hid_near, hid_far, qkv_grad = lax.optimization_barrier(
+        (kept_a, kept_b, hid_near, hid_far, qkv_grad)
+    )
+    kept_a, away_a = halves(kept_a, y, 2)
+    kept_b, away_b = halves(kept_b, x, 2)
+    kept_a = added(kept_a, plane_shift(away_a, 2))
+    kept_b = added(kept_b, plane_shift(away_b, 1))
+    kept = jnp.concatenate([kept_a, kept_b])
     scale_line = lax.dynamic_update_slice(jnp.zeros((1, width), f32), scale_grad, (0, 160 * plane))
     lines = jnp.concatenate([gain_one_grad, gain_two_grad, scale_line])
     lines = lines.reshape(3, 4, 8, 40).transpose(1, 2, 0, 3).reshape(4, 8, 1, 120).astype(bf16)
     lines = jnp.pad(lines, ((0, 0), (0, 0), (0, 7), (0, 360)))
     send = jnp.concatenate([qkv_grad.reshape(4, 8, 40, 480), lines], axis=2)
-    sums = ring_sum(send).astype(bf16)
+    one, three = (ring_shift(pick(send, (z + k) % 4), k) for k in (1, 3))
+    hid = added(hid_near, core_swap(hid_far))
+    hid, send = lax.optimization_barrier((hid, send))
+    two = ring_shift(pick(send, (z + 2) % 4), 2)
+    grad_hid = hid[0].astype(f32)
+    moved = [plane_shift(hid[step], step) for step in (1, 2, 3)]
+    *moved, kept = lax.optimization_barrier((*moved, kept))
+    for item in moved:
+        grad_hid += item.astype(f32)
+    wide = x_rows.astype(f32)
+    inverse = lax.rsqrt(jnp.mean(wide * wide, axis=1, keepdims=True) + 1e-06)
+    grad_in = (grad_mid + norm_back(grad_hid, wide * inverse, inverse, gain_one)).astype(bf16)
+
+    sums = sum((item.astype(f32) for item in (one, two, three)), pick(send, z).astype(f32)).astype(bf16)
     sums = lax.all_to_all(sums, ("y", "core", "x"), split_axis=0, concat_axis=0, tiled=True)
+    big_sums = ring_sum(kept)
     qkv_sums = sums[:, :40].reshape(8, 40, 3, 160).transpose(2, 1, 0, 3).reshape(3, 40, width).astype(f32)
     line_sums = jnp.sum(sums[:, 40, :120].astype(f32), axis=0).reshape(3, 40)
     scale_low = query_scale.astype(bf16).astype(f32)
     scale_sum = LOG2E / math.sqrt(HD) * jax.nn.sigmoid(scale_low) * line_sums[2]
 
-    def home(rows):
-        rows = rows.reshape(4, 4, 8, width)
-        parts = [rows[:, 0]] + [ring_shift(rows[:, k], -k) for k in (1, 2, 3)]
-        line = jnp.stack(parts + parts[:3])
-        return lax.dynamic_slice_in_dim(line, (4 - z) % 4, 4, 0).reshape(16, 8, width)
-
     return (
-        home(out_rows), home(grad_in), qkv_sums[0], qkv_sums[1], qkv_sums[2],
+        outputs, home(grad_in), qkv_sums[0], qkv_sums[1], qkv_sums[2],
         big_sums[0], big_sums[1], big_sums[2], line_sums[0], line_sums[1], scale_sum,
     )
 

time: 422 us -> 321 us (0.76); the launches traced: 417 us -> 321 us
  waiting for transfers between devices: 214 us -> 148 us
  other arithmetic: 43.4 us -> 26.7 us
  local copies, waits for them, and re-layouts: 45.8 us -> 33.3 us
  Pallas kernels: 31.4 us -> 36 us
    ppermute x8, waiting for transfers between devices: 50.1 us -> 19.6 us  [plane_shift(): return lax.ppermute(value, 'x', [(0, 1), (1, 0)])]
    all_gather x1, waiting for transfers between devices: 23.2 us -> 0.01 us  [planes(): big = lax.all_gather(big, 'z', axis=0)]
    ppermute x4, waiting for transfers between devices: 9.87 us -> 23.7 us  [plane_shift(): return lax.ppermute(value, ('y', 'x'), [(0, 3), (1, 2), (2, 1), (3, 0)])]
    ppermute x8, waiting for transfers between devices: 36.5 us -> 23.2 us  [plane_shift(): return lax.ppermute(value, 'y', [(0, 1), (1, 0)])]
    ppermute x21, waiting for transfers between devices: 83.5 us -> 73.4 us  [ring_shift(): return lax.ppermute(value, 'z', [(i, (i + step) % 4) for i in range(4)])]
    select_n x5 -> x0, other arithmetic: 7.66 us -> none  [the longest x1 4.63 us: pair(): jnp.where(first, mine, other)]
    all_to_all x1, waiting for transfers between devices: 5.17 us -> 0.01 us  [planes(): lax.all_to_all(sums, ('y', 'core', 'x'), split_axis=0, concat_axis=0, til...]
    pallas_call x1 -> x2, Pallas kernels: 9.59 us -> 14.3 us  [the longest x1 8.49 us: planes(): pl.pallas_call(feed_kernel, in_specs=[smem] + [vmem] * 7 + [hbm] * 6, out...]
  transfers between devices with their start and end apart: 50 -> 52, of which waited for: 29 -> 26; matrix products, arithmetic and copies ran while one was open for 13% -> 11% of each run, Pallas kernels for 5% -> 9%
where the time goes in v2:
time: 321 us
  waiting for transfers between devices  148 us (46%)
  starting transfers between devices  61.3 us (19%)
  Pallas kernels  36 us (11%)
  local copies, waits for them, and re-layouts  33.3 us (10%)
  other arithmetic  26.7 us (8%)
  between operations  15.1 us (5%)
    ppermute x21, waiting for transfers between devices, ring_shift(): return lax.ppermute(value, 'z', [(i, (i + step) % 4) for i in range(4)])  73.4 us
    ppermute x21, starting transfers between devices, ring_shift(): return lax.ppermute(value, 'z', [(i, (i + step) % 4) for i in range(4)])  26 us
    ppermute x4, waiting for transfers between devices, plane_shift(): return lax.ppermute(value, ('y', 'x'), [(0, 3), (1, 2), (2, 1), (3, 0)])  23.7 us
    ppermute x8, waiting for transfers between devices, plane_shift(): return lax.ppermute(value, 'y', [(0, 1), (1, 0)])  23.2 us
    ppermute x8, waiting for transfers between devices, plane_shift(): return lax.ppermute(value, 'x', [(0, 1), (1, 0)])  19.6 us
    pallas_call x1, Pallas kernels, planes(): pl.pallas_call(attend_back_kernel, grid_spec=pltpu.PrefetchScalarGridSpec...  13.4 us
    unnamed x74, local copies, waits for them, and re-layouts  13 us
    convert_element_type x6, other arithmetic, added(): return (left.astype(f32) + right.astype(f32)).astype(bf16)  10.2 us
  transfers between devices with their start and end apart: 52, of which 26 were waited for; matrix products, arithmetic and copies ran while one was open for 11% of the time, Pallas kernels for 9%

profile of v2, /device:TPU:0, one launch (start us, length us, event | category | flops | bytes accessed | tf_op | source)
XLA Modules:
  0.0 320.6 jit_solution(1632526038537309879)
XLA Ops:
  11.5 1.3 maximum_bitcast_fusion
  13.8 5.3 %all-to-all-start = ((bf16[8,40,480]{2,1,0:T(8,128)(2,1)}), bf16[8,40,480]{2,1,0:T(8,128)(2,1)S(1)}, u32[]{:S(2)}, u32[]{:S(2)}) async-start(bf16[8,40,480]{2,1,0:T(8,128)(2,1)} %reshape.339), calls=%async_computation | async-start | bytes 655360 | tf_op jit(solution)/shard_map/all_to_all | solution.py:613
  20.4 1.6 collective-permute-start
  22.0 2.6 collective-permute-start.1
  24.6 1.3 collective-permute-start.2
  25.9 2.0 collective-permute-done
  28.0 4.0 %collective-permute-done.1 = bf16[5,8,1280]{2,1,0:T(8,128)(2,1)S(1)} collective-permute-done((bf16[5,8,1280]{2,1,0:T(8,128)(2,1)S(1)}, bf16[5,8,1280]{2,1,0:T(8,128)(2,1)S(1)}, u32[]{:S(2)}, u32[]{:S(2)}) %collective-permute-start.1) | collective-permute-done | bytes 102432 | tf_op jit(solution)/shard_map/ppermute | solution.py:357
  32.5 2.7 collective-permute-start.5
  36.2 3.7 %collective-permute-start.9 = (bf16[320,480]{1,0:T(8,128)(2,1)S(1)}, bf16[320,480]{1,0:T(8,128)(2,1)S(1)}, u32[]{:S(2)}, u32[]{:S(2)}) collective-permute-start(bf16[320,480]{1,0:T(8,128)(2,1)S(1)} %bitcast.244), channel_id=1, source_target_pairs={{0,24},{8,0},{16,8},{24,16},{1,25},{9,1},{17,9},{25,17},{2,26},{10... | collective-permute-start | bytes 921608 | tf_op jit(solution)/shard_map/ppermute | solution.py:357
  40.1 4.4 %collective-permute-done.5 = bf16[136,1280]{1,0:T(8,128)(2,1)S(1)} collective-permute-done((bf16[136,1280]{1,0:T(8,128)(2,1)S(1)}, bf16[136,1280]{1,0:T(8,128)(2,1)S(1)}, u32[]{:S(2)}, u32[]{:S(2)}) %collective-permute-start.5) | collective-permute-done | bytes 348192 | tf_op jit(solution)/shard_map/ppermute | solution.py:349
  44.6 1.6 collective-permute-start.10
  46.2 4.8 %collective-permute-done.4 = bf16[136,1280]{1,0:T(8,128)(2,1)S(1)} collective-permute-done((bf16[136,1280]{1,0:T(8,128)(2,1)S(1)}, bf16[136,1280]{1,0:T(8,128)(2,1)S(1)}, u32[]{:S(2)}, u32[]{:S(2)}) %collective-permute-start.4) | collective-permute-done | bytes 348192 | tf_op jit(solution)/shard_map/ppermute | solution.py:348
  52.0 1.4 pad_maximum_fusion.1.near_ref
  53.3 13.5 %collective-permute-done.9 = bf16[320,480]{1,0:T(8,128)(2,1)S(1)} collective-permute-done((bf16[320,480]{1,0:T(8,128)(2,1)S(1)}, bf16[320,480]{1,0:T(8,128)(2,1)S(1)}, u32[]{:S(2)}, u32[]{:S(2)}) %collective-permute-start.9) | collective-permute-done | bytes 307232 | tf_op jit(solution)/shard_map/ppermute | solution.py:357
  67.6 15.4 %collective-permute-done.10 = bf16[320,480]{1,0:T(8,128)(2,1)S(1)} collective-permute-done((bf16[320,480]{1,0:T(8,128)(2,1)S(1)}, bf16[320,480]{1,0:T(8,128)(2,1)S(1)}, u32[]{:S(2)}, u32[]{:S(2)}) %collective-permute-start.10) | collective-permute-done | bytes 307232 | tf_op jit(solution)/shard_map/ppermute | solution.py:357
  86.1 1.3 fusion.41
  87.4 1.5 collective-permute-start.8
  88.9 1.5 collective-permute-start.7
  91.9 1.5 constant_dynamic-slice_fusion.2
  93.5 9.4 %collective-permute-done.8 = bf16[2,3,40,1280]{3,2,1,0:T(8,128)(2,1)S(1)} collective-permute-done((bf16[2,3,40,1280]{3,2,1,0:T(8,128)(2,1)S(1)}, bf16[2,3,40,1280]{3,2,1,0:T(8,128)(2,1)S(1)}, u32[]{:S(2)}, u32[]{:S(2)}) %collective-permute-start.8) | collective-permute-done | bytes 614432 | tf_op jit(solution)/shard_map/ppermute | solution.py:348
  102.9 1.2 collective-permute-done.7
  106.6 1.5 collective-permute-start.14
  109.4 3.4 %collective-permute-done.14 = bf16[4,8,1280]{2,1,0:T(8,128)(2,1)S(1)} collective-permute-done((bf16[4,8,1280]{2,1,0:T(8,128)(2,1)S(1)}, bf16[4,8,1280]{2,1,0:T(8,128)(2,1)S(1)}, u32[]{:S(2)}, u32[]{:S(2)}) %collective-permute-start.14) | collective-permute-done | bytes 81952 | tf_op jit(solution)/shard_map/ppermute | solution.py:357
  112.8 1.5 collective-permute-start.21
  117.0 8.3 %attend.1 = (f32[2,4,128,480]{3,2,1,0:T(8,128)}, bf16[4,128,160]{2,1,0:T(8,128)(2,1)S(1)}, bf16[4,128,160]{2,1,0:T(8,128)(2,1)S(1)}) custom-call(s32[6]{0:T(128)S(1)} %pad_add_fusion.info_ref, bf16[4,136,1280]{2,1,0:T(8,128)(2,1)S(1)} %pad_maximum_fusion.1.near_ref, bf16[4,136,1280]{2,1,0:T(8,128)(2,1)} %copy-done.22, f32[1,1280]{1,0:T(1,128)S(1)} %slice.229.gain_ref, ...), custom_call_target="tpu_custom_call" | custom-call | flops 8999999488 | bytes 8000000 | tf_op jit(solution)/shard_map/attend/pallas_call | solution.py:648
  125.8 2.4 collective-permute-done.15
  128.4 1.6 collective-permute-start.18
  130.5 11.3 %collective-permute-done.18.att_3 = bf16[2,128,160]{2,1,0:T(8,128)(2,1)S(1)} collective-permute-done((bf16[2,128,160]{2,1,0:T(8,128)(2,1)S(1)}, bf16[2,128,160]{2,1,0:T(8,128)(2,1)S(1)}, u32[]{:S(2)}, u32[]{:S(2)}) %collective-permute-start.18) | collective-permute-done | bytes 81952 | tf_op jit(solution)/shard_map/ppermute | solution.py:349
  141.8 1.4 collective-permute-start.17
  143.2 3.5 %collective-permute-done.17.att_2 = bf16[2,128,160]{2,1,0:T(8,128)(2,1)S(1)} collective-permute-done((bf16[2,128,160]{2,1,0:T(8,128)(2,1)S(1)}, bf16[2,128,160]{2,1,0:T(8,128)(2,1)S(1)}, u32[]{:S(2)}, u32[]{:S(2)}) %collective-permute-start.17) | collective-permute-done | bytes 81952 | tf_op jit(solution)/shard_map/ppermute | solution.py:348
  147.8 1.8 select_bitcast_fusion.3
  149.9 1.6 copy.112
  152.3 5.4 %collective-permute-done.22.far_across_a = bf16[2,3,80,1280]{3,2,1,0:T(8,128)(2,1)S(1)} collective-permute-done((bf16[2,3,80,1280]{3,2,1,0:T(8,128)(2,1)}, bf16[2,3,80,1280]{3,2,1,0:T(8,128)(2,1)S(1)}, u32[]{:S(2)}, u32[]{:S(2)}) %collective-permute-start.22) | collective-permute-done | bytes 1228832 | tf_op jit(solution)/shard_map/ppermute | solution.py:353
  158.8 8.5 %feed.1 = (bf16[128,1280]{1,0:T(8,128)(2,1)S(1)}, bf16[128,1280]{1,0:T(8,128)(2,1)S(1)}, bf16[128,1280]{1,0:T(8,128)(2,1)S(1)}, bf16[128,1280]{1,0:T(8,128)(2,1)...) custom-call(s32[6]{0:T(128)S(1)} %pad_add_fusion.info_ref, ...), custom_call_target="tpu_custom_call" | custom-call | flops 12000000000 | bytes 13000000 | tf_op jit(solution)/shard_map/feed/pallas_call | solution.py:683
  167.3 1.6 collective-permute-start.25
  168.8 1.4 collective-permute-start.26
  170.9 5.9 %grads.1 = (bf16[4,3,2,80,1280]{4,3,2,1,0:T(8,128)(2,1)}, bf16[4,3,2,80,1280]{4,3,2,1,0:T(8,128)(2,1)}) custom-call(s32[6]{0:T(128)S(1)} %pad_add_fusion.info_ref, bf16[2,128,160]{2,1,0:T(8,128)(2,1)S(1)} %get-tuple-element.92.att_0, bf16[2,128,160]{2,1,0:T(8,128)(2,1)S(1)} %collective-permute-done.16.att_1, ...), custom_call_target="tpu_custom_call" | custom-call | flops 6000000000 | bytes 12000000 | tf_op jit(solution)/shard_map/grads/pallas_call | solution.py:710
  177.2 2.5 collective-permute-start.31
  179.7 1.6 collective-permute-start.29
  181.9 3.7 %collective-permute-done.29 = bf16[4,8,1280]{2,1,0:T(8,128)(2,1)S(1)} collective-permute-done((bf16[4,8,1280]{2,1,0:T(8,128)(2,1)S(1)}, bf16[4,8,1280]{2,1,0:T(8,128)(2,1)S(1)}, u32[]{:S(2)}, u32[]{:S(2)}) %collective-permute-start.29) | collective-permute-done | bytes 81952 | tf_op jit(solution)/shard_map/ppermute | solution.py:357
  185.6 3.5 %collective-permute-done.30 = bf16[4,8,1280]{2,1,0:T(8,128)(2,1)S(1)} collective-permute-done((bf16[4,8,1280]{2,1,0:T(8,128)(2,1)S(1)}, bf16[4,8,1280]{2,1,0:T(8,128)(2,1)S(1)}, u32[]{:S(2)}, u32[]{:S(2)}) %collective-permute-start.30) | collective-permute-done | bytes 81952 | tf_op jit(solution)/shard_map/ppermute | solution.py:357
  189.9 5.2 %add_convert_fusion = bf16[4,3,2,80,1280]{4,3,2,1,0:T(8,128)(2,1)S(1)} fusion(bf16[4,3,2,80,1280]{4,3,2,1,0:T(8,128)(2,1)} %collective-permute-done.24, bf16[4,3,2,80,1280]{4,3,2,1,0:T(8,128)(2,1)} %get-tuple-element.104), kind=kLoop, calls=%fused_computation | loop fusion | flops 9830400 | bytes 14745600 | tf_op jit(solution)/shard_map/convert_element_type | solution.py:722
  195.9 1.5 select_bitcast_fusion.1
  197.5 1.5 collective-permute-start.32
  199.0 1.2 select_bitcast_fusion
  200.1 1.4 collective-permute-start.33
  201.5 13.4 %attend_back.1 = (bf16[4,128,1280]{2,1,0:T(8,128)(2,1)S(1)}, bf16[4,128,1280]{2,1,0:T(8,128)(2,1)S(1)}, bf16[1280,480]{1,0:T(8,128)(2,1)}, f32[1,1280]{1,0:T(1,128)S(1)}, f32[1,160]{1,0:T(1,128)S(1)}) custom-call(s32[6]{0:T(128)S(1)} %pad_add_fusion.info_ref, bf16[4,136,1280]{2,1,0:T(8,128)(2,1)} %copy-done, bf16[4,136,1280]{2,1,0:T(8,128)(2,1)} %copy-done.22, ...), custom_call_target="tpu_custom_call" | custom-call | flops 15000000512 | bytes 12000000 | tf_op jit(solution)/shard_map/attend_back/pallas_call | solution.py:744
  216.4 10.4 %collective-permute-done.32 = bf16[2,3,2,40,1280]{4,3,1,0,2:T(8,128)(2,1)} collective-permute-done((bf16[2,3,2,40,1280]{4,3,1,0,2:T(8,128)(2,1)}, bf16[2,3,2,40,1280]{4,3,1,0,2:T(8,128)(2,1)}, u32[]{:S(2)}, u32[]{:S(2)}) %collective-permute-start.32) | collective-permute-done | bytes 1228832 | tf_op jit(solution)/shard_map/ppermute | solution.py:346
  226.8 2.5 fusion.2
  229.3 1.7 fusion.1
  231.1 1.6 collective-permute-start.39
  232.7 1.4 collective-permute-start.38
  234.6 3.8 %collective-permute-start.45 = (bf16[8,48,480]{2,1,0:T(8,128)(2,1)S(1)}, bf16[8,48,480]{2,1,0:T(8,128)(2,1)S(1)}, u32[]{:S(2)}, u32[]{:S(2)}) collective-permute-start(bf16[8,48,480]{2,1,0:T(8,128)(2,1)S(1)} %get-tuple-element.154), channel_id=1, source_target_pairs={{0,24},{8,0},{16,8},{24,16},{1,25},{9,1},{17,9},{25,17},{2,26},{10... | collective-permute-start | bytes 1105928 | tf_op jit(solution)/shard_map/ppermute | solution.py:357
  238.4 7.8 %collective-permute-done.39 = bf16[2,3,40,1280]{3,2,1,0:T(8,128)(2,1)S(1)} collective-permute-done((bf16[2,3,40,1280]{3,2,1,0:T(8,128)(2,1)S(1)}, bf16[2,3,40,1280]{3,2,1,0:T(8,128)(2,1)S(1)}, u32[]{:S(2)}, u32[]{:S(2)}) %collective-permute-start.39) | collective-permute-done | bytes 614432 | tf_op jit(solution)/shard_map/ppermute | solution.py:346
  246.4 1.1 collective-permute-done.38
  248.2 1.3 collective-permute-start.37
  250.2 1.5 collective-permute-start.35
  251.9 7.9 %collective-permute-done.37 = bf16[128,1280]{1,0:T(8,128)(2,1)S(1)} collective-permute-done((bf16[128,1280]{1,0:T(8,128)(2,1)S(1)}, bf16[128,1280]{1,0:T(8,128)(2,1)S(1)}, u32[]{:S(2)}, u32[]{:S(2)}) %collective-permute-start.37) | collective-permute-done | bytes 327712 | tf_op jit(solution)/shard_map/ppermute | solution.py:349
  259.8 4.0 %collective-permute-done.36 = bf16[128,1280]{1,0:T(8,128)(2,1)S(1)} collective-permute-done((bf16[128,1280]{1,0:T(8,128)(2,1)S(1)}, bf16[128,1280]{1,0:T(8,128)(2,1)S(1)}, u32[]{:S(2)}, u32[]{:S(2)}) %collective-permute-start.36) | collective-permute-done | bytes 327712 | tf_op jit(solution)/shard_map/ppermute | solution.py:348
  264.6 3.8 %collective-permute-start.40 = (bf16[4,8,1280]{2,1,0:T(8,128)(2,1)S(1)}, bf16[4,8,1280]{2,1,0:T(8,128)(2,1)S(1)}, u32[]{:S(2)}, u32[]{:S(2)}) collective-permute-start(bf16[4,8,1280]{2,1,0:T(8,128)(2,1)S(1)} %get-tuple-element.176), channel_id=1, source_target_pairs={{0,24},{8,0},{16,8},{24,16},{1,25},{9,1},{17,9},{25,17},{2,26},{10... | collective-permute-start | bytes 245768 | tf_op jit(solution)/shard_map/ppermute | solution.py:357
  270.7 15.6 %collective-permute-done.44 = bf16[8,48,480]{2,1,0:T(8,128)(2,1)S(1)} collective-permute-done((bf16[8,48,480]{2,1,0:T(8,128)(2,1)S(1)}, bf16[8,48,480]{2,1,0:T(8,128)(2,1)S(1)}, u32[]{:S(2)}, u32[]{:S(2)}) %collective-permute-start.44) | collective-permute-done | bytes 368672 | tf_op jit(solution)/shard_map/ppermute | solution.py:357
  287.3 3.7 %all-to-all-start.1 = ((bf16[8,48,480]{2,1,0:T(8,128)(2,1)}), bf16[8,48,480]{2,1,0:T(8,128)(2,1)S(1)}, u32[]{:S(2)}, u32[]{:S(2)}) async-start(bf16[8,48,480]{2,1,0:T(8,128)(2,1)} %fusion.8), calls=%async_computation.1 | async-start | bytes 786432 | tf_op jit(solution)/shard_map/all_to_all | solution.py:801
  294.9 1.7 constant_dynamic-slice_fusion
  296.7 11.2 %collective-permute-done.47 = bf16[3,40,1280]{2,1,0:T(8,128)(2,1)S(1)} collective-permute-done((bf16[3,40,1280]{2,1,0:T(8,128)(2,1)S(1)}, bf16[3,40,1280]{2,1,0:T(8,128)(2,1)S(1)}, u32[]{:S(2)}, u32[]{:S(2)}) %collective-permute-start.47) | collective-permute-done | bytes 307232 | tf_op jit(solution)/shard_map/ppermute | solution.py:357
  (242 shorter events, 45.7 us)
Async XLA Ops:
  11.5 7.7 %copy-start.17 = (f32[40,1280]{1,0:T(8,128)S(1)}, f32[40,1280]{1,0:T(8,128)}, u32[]{:S(2)}) copy-start(f32[40,1280]{1,0:T(8,128)} %param.20) | copy-start | bytes 614404
  12.7 6.5 %copy-start.18 = (f32[40,1280]{1,0:T(8,128)S(1)}, f32[40,1280]{1,0:T(8,128)}, u32[]{:S(2)}) copy-start(f32[40,1280]{1,0:T(8,128)} %param.22) | copy-start | bytes 614404
  12.8 6.5 %copy-start.19 = (f32[40,1280]{1,0:T(8,128)S(1)}, f32[40,1280]{1,0:T(8,128)}, u32[]{:S(2)}) copy-start(f32[40,1280]{1,0:T(8,128)} %param.21) | copy-start | bytes 614404
  13.8 6.4 %copy-start.15 = (bf16[16,8,1280]{2,1,0:T(8,128)(2,1)S(1)}, bf16[16,8,1280]{2,1,0:T(8,128)(2,1)}, u32[]{:S(2)}) copy-start(bf16[16,8,1280]{2,1,0:T(8,128)(2,1)} %param.15) | copy-start | bytes 983044
  13.8 22.3 %all-to-all-start = ((bf16[8,40,480]{2,1,0:T(8,128)(2,1)}), bf16[8,40,480]{2,1,0:T(8,128)(2,1)S(1)}, u32[]{:S(2)}, u32[]{:S(2)}) async-start(bf16[8,40,480]{2,1,0:T(8,128)(2,1)} %reshape.339), calls=%async_computation | async-start | bytes 655360 | tf_op jit(solution)/shard_map/all_to_all | solution.py:613
  19.2 66.9 %all-gather.2.cloned.1.call-start = ((), (), s32[]{:S(2)}) async-start(), calls=%async_computation.2 | async-start | bytes 1536000 | tf_op jit(solution)/shard_map/all_gather | solution.py:620
  20.3 19.6 %copy-start.26 = (s32[16]{0:T(128)S(1)}, s32[16]{0:T(128)}, u32[]{:S(2)}) copy-start(s32[16]{0:T(128)} %param.27) | copy-start | bytes 196
  20.3 19.6 %copy-start.27 = (s32[16]{0:T(128)S(1)}, s32[16]{0:T(128)}, u32[]{:S(2)}) copy-start(s32[16]{0:T(128)} %param.26) | copy-start | bytes 196
  20.4 7.6 %collective-permute-start = (bf16[5,8,1280]{2,1,0:T(8,128)(2,1)S(1)}, bf16[5,8,1280]{2,1,0:T(8,128)(2,1)S(1)}, u32[]{:S(2)}, u32[]{:S(2)}) collective-permute-start(bf16[5,8,1280]{2,1,0:T(8,128)(2,1)S(1)} %get-tuple-element.200), channel_id=1, source_target_pairs={{0,8},{8,16},{16,24},{24,0},{1,9},{9,17},{17,25},{25,1},{2,10},{10... | collective-permute-start | bytes 307208 | tf_op jit(solution)/shard_map/ppermute | solution.py:357
  22.0 10.0 %collective-permute-start.1 = (bf16[5,8,1280]{2,1,0:T(8,128)(2,1)S(1)}, bf16[5,8,1280]{2,1,0:T(8,128)(2,1)S(1)}, u32[]{:S(2)}, u32[]{:S(2)}) collective-permute-start(bf16[5,8,1280]{2,1,0:T(8,128)(2,1)S(1)} %get-tuple-element.201), channel_id=1, source_target_pairs={{0,16},{8,24},{16,0},{24,8},{1,17},{9,25},{17,1},{25,9},{2,18},{10... | collective-permute-start | bytes 307208 | tf_op jit(solution)/shard_map/ppermute | solution.py:357
  24.6 7.4 %collective-permute-start.2 = (bf16[5,8,1280]{2,1,0:T(8,128)(2,1)S(1)}, bf16[5,8,1280]{2,1,0:T(8,128)(2,1)S(1)}, u32[]{:S(2)}, u32[]{:S(2)}) collective-permute-start(bf16[5,8,1280]{2,1,0:T(8,128)(2,1)S(1)} %get-tuple-element.202), channel_id=1, source_target_pairs={{0,24},{8,0},{16,8},{24,16},{1,25},{9,1},{17,9},{25,17},{2,26},{10... | collective-permute-start | bytes 307208 | tf_op jit(solution)/shard_map/ppermute | solution.py:357
  32.5 12.0 %collective-permute-start.5 = (bf16[136,1280]{1,0:T(8,128)(2,1)S(1)}, bf16[136,1280]{1,0:T(8,128)(2,1)S(1)}, u32[]{:S(2)}, u32[]{:S(2)}) collective-permute-start(bf16[136,1280]{1,0:T(8,128)(2,1)S(1)} %concatenate.61), channel_id=1, source_target_pairs={{0,5},{1,4},{4,1},{5,0},{2,7},{3,6},{6,3},{7,2},{8,13},{9,12},{12,... | collective-permute-start | bytes 1044488 | tf_op jit(solution)/shard_map/ppermute | solution.py:349
  35.2 15.8 %collective-permute-start.4 = (bf16[136,1280]{1,0:T(8,128)(2,1)S(1)}, bf16[136,1280]{1,0:T(8,128)(2,1)S(1)}, u32[]{:S(2)}, u32[]{:S(2)}) collective-permute-start(bf16[136,1280]{1,0:T(8,128)(2,1)S(1)} %concatenate.61), channel_id=1, source_target_pairs={{0,4},{4,0},{1,5},{5,1},{2,6},{6,2},{3,7},{7,3},{8,12},{12,8},{9,1... | collective-permute-start | bytes 1044488 | tf_op jit(solution)/shard_map/ppermute | solution.py:348
  35.8 15.5 %collective-permute-start.3 = (bf16[136,1280]{1,0:T(8,128)(2,1)S(1)}, bf16[136,1280]{1,0:T(8,128)(2,1)S(1)}, u32[]{:S(2)}, u32[]{:S(2)}) collective-permute-start(bf16[136,1280]{1,0:T(8,128)(2,1)S(1)} %concatenate.61), channel_id=1, source_target_pairs={{0,1},{1,0},{2,3},{3,2},{4,5},{5,4},{6,7},{7,6},{8,9},{9,8},{10,11... | collective-permute-start | bytes 1044488 | tf_op jit(solution)/shard_map/ppermute | solution.py:346
  36.2 30.7 %collective-permute-start.9 = (bf16[320,480]{1,0:T(8,128)(2,1)S(1)}, bf16[320,480]{1,0:T(8,128)(2,1)S(1)}, u32[]{:S(2)}, u32[]{:S(2)}) collective-permute-start(bf16[320,480]{1,0:T(8,128)(2,1)S(1)} %bitcast.244), channel_id=1, source_target_pairs={{0,24},{8,0},{16,8},{24,16},{1,25},{9,1},{17,9},{25,17},{2,26},{10... | collective-permute-start | bytes 921608 | tf_op jit(solution)/shard_map/ppermute | solution.py:357
  40.1 43.7 %collective-permute-start.11 = (bf16[320,480]{1,0:T(8,128)(2,1)S(1)}, bf16[320,480]{1,0:T(8,128)(2,1)S(1)}, u32[]{:S(2)}, u32[]{:S(2)}) collective-permute-start(bf16[320,480]{1,0:T(8,128)(2,1)S(1)} %bitcast.245), channel_id=1, source_target_pairs={{0,8},{8,16},{16,24},{24,0},{1,9},{9,17},{17,25},{25,1},{2,10},{10... | collective-permute-start | bytes 921608 | tf_op jit(solution)/shard_map/ppermute | solution.py:357
  44.6 6.7 %copy-start.12 = (bf16[136,1280]{1,0:T(8,128)(2,1)}, bf16[136,1280]{1,0:T(8,128)(2,1)S(1)}, u32[]{:S(2)}) copy-start(bf16[136,1280]{1,0:T(8,128)(2,1)S(1)} %collective-permute-done.5) | copy-start | bytes 1044484
  44.6 38.5 %collective-permute-start.10 = (bf16[320,480]{1,0:T(8,128)(2,1)S(1)}, bf16[320,480]{1,0:T(8,128)(2,1)S(1)}, u32[]{:S(2)}, u32[]{:S(2)}) collective-permute-start(bf16[320,480]{1,0:T(8,128)(2,1)S(1)} %bitcast.246), channel_id=1, source_target_pairs={{0,16},{8,24},{16,0},{24,8},{1,17},{9,25},{17,1},{25,9},{2,18},{10... | collective-permute-start | bytes 921608 | tf_op jit(solution)/shard_map/ppermute | solution.py:357
  53.3 63.7 %copy-start = (bf16[4,136,1280]{2,1,0:T(8,128)(2,1)}, bf16[4,136,1280]{2,1,0:T(8,128)(2,1)S(1)}, u32[]{:S(2)}) copy-start(bf16[4,136,1280]{2,1,0:T(8,128)(2,1)S(1)} %pad_maximum_fusion.1.near_ref) | copy-start | bytes 4177924
  87.4 15.5 %collective-permute-start.8 = (bf16[2,3,40,1280]{3,2,1,0:T(8,128)(2,1)S(1)}, bf16[2,3,40,1280]{3,2,1,0:T(8,128)(2,1)S(1)}, u32[]{:S(2)}, u32[]{:S(2)}) collective-permute-start(bf16[2,3,40,1280]{3,2,1,0:T(8,128)(2,1)S(1)} %get-tuple-element.166), channel_id=1, source_target_pairs={{0,4},{4,0},{1,5},{5,1},{2,6},{6,2},{3,7},{7,3},{8,12},{12,8},{9,1... | collective-permute-start | bytes 1843208 | tf_op jit(solution)/shard_map/ppermute | solution.py:348
  88.9 15.1 %collective-permute-start.7 = (bf16[2,3,40,1280]{3,2,1,0:T(8,128)(2,1)S(1)}, bf16[2,3,40,1280]{3,2,1,0:T(8,128)(2,1)S(1)}, u32[]{:S(2)}, u32[]{:S(2)}) collective-permute-start(bf16[2,3,40,1280]{3,2,1,0:T(8,128)(2,1)S(1)} %get-tuple-element.167), channel_id=1, source_target_pairs={{0,1},{1,0},{2,3},{3,2},{4,5},{5,4},{6,7},{7,6},{8,9},{9,8},{10,11... | collective-permute-start | bytes 1843208 | tf_op jit(solution)/shard_map/ppermute | solution.py:346
  91.9 12.2 %copy-start.10 = (bf16[4,3,40,1280]{3,2,1,0:T(8,128)(2,1)S(1)}, bf16[4,3,40,1280]{3,2,1,0:T(8,128)(2,1)}, u32[]{:S(2)}) copy-start(bf16[4,3,40,1280]{3,2,1,0:T(8,128)(2,1)} %all-gather.2.cloned.1.call-done) | copy-start | bytes 3686404
  93.4 23.6 %copy-start.1 = (bf16[4,320,480]{2,1,0:T(8,128)(2,1)}, bf16[4,320,480]{2,1,0:T(8,128)(2,1)S(1)}, u32[]{:S(2)}) copy-start(bf16[4,320,480]{2,1,0:T(8,128)(2,1)S(1)} %constant_dynamic-slice_fusion.2) | copy-start | bytes 3686404
  93.4 21.9 %collective-permute-start.6 = (bf16[4,136,1280]{2,1,0:T(8,128)(2,1)S(1)}, bf16[4,136,1280]{2,1,0:T(8,128)(2,1)S(1)}, u32[]{:S(2)}, u32[]{:S(2)}) collective-permute-start(bf16[4,136,1280]{2,1,0:T(8,128)(2,1)S(1)} %pad_maximum_fusion.1.near_ref), channel_id=1, source_target_pairs={{0,2},{2,0},{1,3},{3,1},{4,6},{6,4},{5,7},{7,5},{8,10},{10,8},{9,1... | collective-permute-start | bytes 4177928 | tf_op jit(solution)/shard_map/ppermute | solution.py:353
  106.6 6.2 %collective-permute-start.14 = (bf16[4,8,1280]{2,1,0:T(8,128)(2,1)S(1)}, bf16[4,8,1280]{2,1,0:T(8,128)(2,1)S(1)}, u32[]{:S(2)}, u32[]{:S(2)}) collective-permute-start(bf16[4,8,1280]{2,1,0:T(8,128)(2,1)S(1)} %get-tuple-element.182), channel_id=1, source_target_pairs={{0,24},{8,0},{16,8},{24,16},{1,25},{9,1},{17,9},{25,17},{2,26},{10... | collective-permute-start | bytes 245768 | tf_op jit(solution)/shard_map/ppermute | solution.py:357
  108.2 7.1 %collective-permute-start.13 = (bf16[4,8,1280]{2,1,0:T(8,128)(2,1)S(1)}, bf16[4,8,1280]{2,1,0:T(8,128)(2,1)S(1)}, u32[]{:S(2)}, u32[]{:S(2)}) collective-permute-start(bf16[4,8,1280]{2,1,0:T(8,128)(2,1)S(1)} %get-tuple-element.183), channel_id=1, source_target_pairs={{0,16},{8,24},{16,0},{24,8},{1,17},{9,25},{17,1},{25,9},{2,18},{10... | collective-permute-start | bytes 245768 | tf_op jit(solution)/shard_map/ppermute | solution.py:357
  108.2 7.1 %collective-permute-start.12 = (bf16[4,8,1280]{2,1,0:T(8,128)(2,1)S(1)}, bf16[4,8,1280]{2,1,0:T(8,128)(2,1)S(1)}, u32[]{:S(2)}, u32[]{:S(2)}) collective-permute-start(bf16[4,8,1280]{2,1,0:T(8,128)(2,1)S(1)} %get-tuple-element.184), channel_id=1, source_target_pairs={{0,8},{8,16},{16,24},{24,0},{1,9},{9,17},{17,25},{25,1},{2,10},{10... | collective-permute-start | bytes 245768 | tf_op jit(solution)/shard_map/ppermute | solution.py:357
  108.9 37.9 %collective-permute-start.20 = (bf16[2,3,80,1280]{3,2,1,0:T(8,128)(2,1)}, bf16[2,3,80,1280]{3,2,1,0:T(8,128)(2,1)}, u32[]{:S(2)}, u32[]{:S(2)}) collective-permute-start(bf16[2,3,80,1280]{3,2,1,0:T(8,128)(2,1)} %bitcast.30.near_a), channel_id=1, source_target_pairs={{0,4},{4,0},{1,5},{5,1},{2,6},{6,2},{3,7},{7,3},{8,12},{12,8},{9,1... | collective-permute-start | bytes 3686408 | tf_op jit(solution)/shard_map/ppermute | solution.py:348
  112.8 34.0 %collective-permute-start.21 = (bf16[2,3,2,40,1280]{4,3,1,0,2:T(8,128)(2,1)}, bf16[2,3,2,40,1280]{4,3,1,0,2:T(8,128)(2,1)}, u32[]{:S(2)}, u32[]{:S(2)}) collective-permute-start(bf16[2,3,2,40,1280]{4,3,1,0,2:T(8,128)(2,1)} %pad_maximum_fusion.3), channel_id=1, source_target_pairs={{0,1},{1,0},{2,3},{3,2},{4,5},{5,4},{6,7},{7,6},{8,9},{9,8},{10,11... | collective-permute-start | bytes 3686408 | tf_op jit(solution)/shard_map/ppermute | solution.py:346
  125.3 21.4 %collective-permute-start.19 = (bf16[2,3,80,1280]{3,2,1,0:T(8,128)(2,1)}, bf16[2,3,80,1280]{3,2,1,0:T(8,128)(2,1)S(1)}, u32[]{:S(2)}, u32[]{:S(2)}) collective-permute-start(bf16[2,3,80,1280]{3,2,1,0:T(8,128)(2,1)} %bitcast.30.near_a), channel_id=1, source_target_pairs={{0,2},{2,0},{1,3},{3,1},{4,6},{6,4},{5,7},{7,5},{8,10},{10,8},{9,1... | collective-permute-start | bytes 3686408 | tf_op jit(solution)/shard_map/ppermute | solution.py:353
  125.3 2.9 collective-permute-start.15
  128.4 13.4 %collective-permute-start.18 = (bf16[2,128,160]{2,1,0:T(8,128)(2,1)S(1)}, bf16[2,128,160]{2,1,0:T(8,128)(2,1)S(1)}, u32[]{:S(2)}, u32[]{:S(2)}) collective-permute-start(bf16[2,128,160]{2,1,0:T(8,128)(2,1)S(1)} %get-tuple-element.171), channel_id=1, source_target_pairs={{0,5},{1,4},{4,1},{5,0},{2,7},{3,6},{6,3},{7,2},{8,13},{9,12},{12,... | collective-permute-start | bytes 245768 | tf_op jit(solution)/shard_map/ppermute | solution.py:349
  129.9 13.3 %collective-permute-start.16 = (bf16[2,128,160]{2,1,0:T(8,128)(2,1)S(1)}, bf16[2,128,160]{2,1,0:T(8,128)(2,1)S(1)}, u32[]{:S(2)}, u32[]{:S(2)}) collective-permute-start(bf16[2,128,160]{2,1,0:T(8,128)(2,1)S(1)} %get-tuple-element.173), channel_id=1, source_target_pairs={{0,1},{1,0},{2,3},{3,2},{4,5},{5,4},{6,7},{7,6},{8,9},{9,8},{10,11... | collective-permute-start | bytes 245768 | tf_op jit(solution)/shard_map/ppermute | solution.py:346
  141.8 5.0 %collective-permute-start.17 = (bf16[2,128,160]{2,1,0:T(8,128)(2,1)S(1)}, bf16[2,128,160]{2,1,0:T(8,128)(2,1)S(1)}, u32[]{:S(2)}, u32[]{:S(2)}) collective-permute-start(bf16[2,128,160]{2,1,0:T(8,128)(2,1)S(1)} %get-tuple-element.174), channel_id=1, source_target_pairs={{0,4},{4,0},{1,5},{5,1},{2,6},{6,2},{3,7},{7,3},{8,12},{12,8},{9,1... | collective-permute-start | bytes 245768 | tf_op jit(solution)/shard_map/ppermute | solution.py:348
  151.5 6.8 %collective-permute-start.23 = (bf16[2,3,2,80,1280]{4,3,2,1,0:T(8,128)(2,1)}, bf16[2,3,2,80,1280]{4,3,2,1,0:T(8,128)(2,1)}, u32[]{:S(2)}, u32[]{:S(2)}) collective-permute-start(bf16[2,3,2,80,1280]{4,3,2,1,0:T(8,128)(2,1)} %bitcast.57.all_b), channel_id=1, source_target_pairs={{0,2},{2,0},{1,3},{3,1},{4,6},{6,4},{5,7},{7,5},{8,10},{10,8},{9,1... | collective-permute-start | bytes 7372808 | tf_op jit(solution)/shard_map/ppermute | solution.py:353
  151.5 6.3 %collective-permute-start.22 = (bf16[2,3,80,1280]{3,2,1,0:T(8,128)(2,1)}, bf16[2,3,80,1280]{3,2,1,0:T(8,128)(2,1)S(1)}, u32[]{:S(2)}, u32[]{:S(2)}) collective-permute-start(bf16[2,3,80,1280]{3,2,1,0:T(8,128)(2,1)} %collective-permute-done.20.across_a), channel_id=1, source_target_pairs={{0,2},{2,0},{1,3},{3,1},{4,6},{6,4},{5,7},{7,5},{8,10},{10,8},{9,1... | collective-permute-start | bytes 3686408 | tf_op jit(solution)/shard_map/ppermute | solution.py:353
  167.3 9.5 %collective-permute-start.25 = (bf16[2,128,160]{2,1,0:T(8,128)(2,1)S(1)}, bf16[2,128,160]{2,1,0:T(8,128)(2,1)S(1)}, u32[]{:S(2)}, u32[]{:S(2)}) collective-permute-start(bf16[2,128,160]{2,1,0:T(8,128)(2,1)S(1)} %get-tuple-element.107), channel_id=1, source_target_pairs={{0,1},{1,0},{2,3},{3,2},{4,5},{5,4},{6,7},{7,6},{8,9},{9,8},{10,11... | collective-permute-start | bytes 245768 | tf_op jit(solution)/shard_map/ppermute | solution.py:346
  168.8 8.3 %collective-permute-start.26 = (bf16[2,128,160]{2,1,0:T(8,128)(2,1)S(1)}, bf16[2,128,160]{2,1,0:T(8,128)(2,1)S(1)}, u32[]{:S(2)}, u32[]{:S(2)}) collective-permute-start(bf16[2,128,160]{2,1,0:T(8,128)(2,1)S(1)} %get-tuple-element.108), channel_id=1, source_target_pairs={{0,4},{4,0},{1,5},{5,1},{2,6},{6,2},{3,7},{7,3},{8,12},{12,8},{9,1... | collective-permute-start | bytes 245768 | tf_op jit(solution)/shard_map/ppermute | solution.py:348
  170.3 6.9 %collective-permute-start.27 = (bf16[2,128,160]{2,1,0:T(8,128)(2,1)S(1)}, bf16[2,128,160]{2,1,0:T(8,128)(2,1)S(1)}, u32[]{:S(2)}, u32[]{:S(2)}) collective-permute-start(bf16[2,128,160]{2,1,0:T(8,128)(2,1)S(1)} %get-tuple-element.109), channel_id=1, source_target_pairs={{0,5},{1,4},{4,1},{5,0},{2,7},{3,6},{6,3},{7,2},{8,13},{9,12},{12,... | collective-permute-start | bytes 245768 | tf_op jit(solution)/shard_map/ppermute | solution.py:349
  176.7 13.2 %collective-permute-start.24 = (bf16[4,3,2,80,1280]{4,3,2,1,0:T(8,128)(2,1)}, bf16[4,3,2,80,1280]{4,3,2,1,0:T(8,128)(2,1)}, u32[]{:S(2)}, u32[]{:S(2)}) collective-permute-start(bf16[4,3,2,80,1280]{4,3,2,1,0:T(8,128)(2,1)} %get-tuple-element.105), channel_id=1, source_target_pairs={{0,2},{2,0},{1,3},{3,1},{4,6},{6,4},{5,7},{7,5},{8,10},{10,8},{9,1... | collective-permute-start | bytes 14745608 | tf_op jit(solution)/shard_map/ppermute | solution.py:353
  177.2 11.9 %collective-permute-start.31 = (bf16[4,8,1280]{2,1,0:T(8,128)(2,1)S(1)}, bf16[4,8,1280]{2,1,0:T(8,128)(2,1)S(1)}, u32[]{:S(2)}, u32[]{:S(2)}) collective-permute-start(bf16[4,8,1280]{2,1,0:T(8,128)(2,1)S(1)} %get-tuple-element.178), channel_id=1, source_target_pairs={{0,8},{8,16},{16,24},{24,0},{1,9},{9,17},{17,25},{25,1},{2,10},{10... | collective-permute-start | bytes 245768 | tf_op jit(solution)/shard_map/ppermute | solution.py:357
  179.7 5.8 %collective-permute-start.29 = (bf16[4,8,1280]{2,1,0:T(8,128)(2,1)S(1)}, bf16[4,8,1280]{2,1,0:T(8,128)(2,1)S(1)}, u32[]{:S(2)}, u32[]{:S(2)}) collective-permute-start(bf16[4,8,1280]{2,1,0:T(8,128)(2,1)S(1)} %get-tuple-element.179), channel_id=1, source_target_pairs={{0,24},{8,0},{16,8},{24,16},{1,25},{9,1},{17,9},{25,17},{2,26},{10... | collective-permute-start | bytes 245768 | tf_op jit(solution)/shard_map/ppermute | solution.py:357
  181.3 7.8 %collective-permute-start.30 = (bf16[4,8,1280]{2,1,0:T(8,128)(2,1)S(1)}, bf16[4,8,1280]{2,1,0:T(8,128)(2,1)S(1)}, u32[]{:S(2)}, u32[]{:S(2)}) collective-permute-start(bf16[4,8,1280]{2,1,0:T(8,128)(2,1)S(1)} %get-tuple-element.180), channel_id=1, source_target_pairs={{0,16},{8,24},{16,0},{24,8},{1,17},{9,25},{17,1},{25,9},{2,18},{10... | collective-permute-start | bytes 245768 | tf_op jit(solution)/shard_map/ppermute | solution.py:357
  181.7 13.4 %collective-permute-start.28 = (bf16[4,128,160]{2,1,0:T(8,128)(2,1)S(1)}, bf16[4,128,160]{2,1,0:T(8,128)(2,1)S(1)}, u32[]{:S(2)}, u32[]{:S(2)}) collective-permute-start(bf16[4,128,160]{2,1,0:T(8,128)(2,1)S(1)} %pad_maximum_fusion.9), channel_id=1, source_target_pairs={{0,2},{2,0},{1,3},{3,1},{4,6},{6,4},{5,7},{7,5},{8,10},{10,8},{9,1... | collective-permute-start | bytes 491528 | tf_op jit(solution)/shard_map/ppermute | solution.py:353
  197.5 29.3 %collective-permute-start.32 = (bf16[2,3,2,40,1280]{4,3,1,0,2:T(8,128)(2,1)}, bf16[2,3,2,40,1280]{4,3,1,0,2:T(8,128)(2,1)}, u32[]{:S(2)}, u32[]{:S(2)}) collective-permute-start(bf16[2,3,2,40,1280]{4,3,1,0,2:T(8,128)(2,1)} %select_bitcast_fusion.1), channel_id=1, source_target_pairs={{0,1},{1,0},{2,3},{3,2},{4,5},{5,4},{6,7},{7,6},{8,9},{9,8},{10,11... | collective-permute-start | bytes 3686408 | tf_op jit(solution)/shard_map/ppermute | solution.py:346
  200.1 29.1 %collective-permute-start.33 = (bf16[2,3,2,40,1280]{4,3,1,0,2:T(8,128)(2,1)}, bf16[2,3,2,40,1280]{4,3,1,0,2:T(8,128)(2,1)}, u32[]{:S(2)}, u32[]{:S(2)}) collective-permute-start(bf16[2,3,2,40,1280]{4,3,1,0,2:T(8,128)(2,1)} %select_bitcast_fusion), channel_id=1, source_target_pairs={{0,4},{4,0},{1,5},{5,1},{2,6},{6,2},{3,7},{7,3},{8,12},{12,8},{9,1... | collective-permute-start | bytes 3686408 | tf_op jit(solution)/shard_map/ppermute | solution.py:348
  216.4 12.9 %copy-start.5 = (bf16[2,3,1,2,40,1280]{5,4,3,2,1,0:T(8,128)(2,1)S(1)}, bf16[2,3,1,2,40,1280]{5,4,3,2,1,0:T(8,128)(2,1)}, u32[]{:S(2)}) copy-start(bf16[2,3,1,2,40,1280]{5,4,3,2,1,0:T(8,128)(2,1)} %copy-done.4) | copy-start | bytes 3686404
  216.4 12.9 %copy-start.7 = (bf16[2,3,1,2,40,1280]{5,4,3,2,1,0:T(8,128)(2,1)S(1)}, bf16[2,3,1,2,40,1280]{5,4,3,2,1,0:T(8,128)(2,1)}, u32[]{:S(2)}) copy-start(bf16[2,3,1,2,40,1280]{5,4,3,2,1,0:T(8,128)(2,1)} %copy-done.6) | copy-start | bytes 3686404
  231.1 15.0 %collective-permute-start.39 = (bf16[2,3,40,1280]{3,2,1,0:T(8,128)(2,1)S(1)}, bf16[2,3,40,1280]{3,2,1,0:T(8,128)(2,1)S(1)}, u32[]{:S(2)}, u32[]{:S(2)}) collective-permute-start(bf16[2,3,40,1280]{3,2,1,0:T(8,128)(2,1)S(1)} %select_bitcast_fusion.4), channel_id=1, source_target_pairs={{0,1},{1,0},{2,3},{3,2},{4,5},{5,4},{6,7},{7,6},{8,9},{9,8},{10,11... | collective-permute-start | bytes 1843208 | tf_op jit(solution)/shard_map/ppermute | solution.py:346
  232.7 14.8 %collective-permute-start.38 = (bf16[2,3,40,1280]{3,2,1,0:T(8,128)(2,1)S(1)}, bf16[2,3,40,1280]{3,2,1,0:T(8,128)(2,1)S(1)}, u32[]{:S(2)}, u32[]{:S(2)}) collective-permute-start(bf16[2,3,40,1280]{3,2,1,0:T(8,128)(2,1)S(1)} %select_bitcast_fusion.5), channel_id=1, source_target_pairs={{0,4},{4,0},{1,5},{5,1},{2,6},{6,2},{3,7},{7,3},{8,12},{12,8},{9,1... | collective-permute-start | bytes 1843208 | tf_op jit(solution)/shard_map/ppermute | solution.py:348
  234.2 13.6 %collective-permute-start.34 = (bf16[4,128,1280]{2,1,0:T(8,128)(2,1)S(1)}, bf16[4,128,1280]{2,1,0:T(8,128)(2,1)S(1)}, u32[]{:S(2)}, u32[]{:S(2)}) collective-permute-start(bf16[4,128,1280]{2,1,0:T(8,128)(2,1)S(1)} %copy-done.3), channel_id=1, source_target_pairs={{0,2},{2,0},{1,3},{3,1},{4,6},{6,4},{5,7},{7,5},{8,10},{10,8},{9,1... | collective-permute-start | bytes 3932168 | tf_op jit(solution)/shard_map/ppermute | solution.py:353
  234.5 35.5 %collective-permute-start.43 = (bf16[8,48,480]{2,1,0:T(8,128)(2,1)S(1)}, bf16[8,48,480]{2,1,0:T(8,128)(2,1)S(1)}, u32[]{:S(2)}, u32[]{:S(2)}) collective-permute-start(bf16[8,48,480]{2,1,0:T(8,128)(2,1)S(1)} %get-tuple-element.153), channel_id=1, source_target_pairs={{0,8},{8,16},{16,24},{24,0},{1,9},{9,17},{17,25},{25,1},{2,10},{10... | collective-permute-start | bytes 1105928 | tf_op jit(solution)/shard_map/ppermute | solution.py:357
  234.6 35.5 %collective-permute-start.45 = (bf16[8,48,480]{2,1,0:T(8,128)(2,1)S(1)}, bf16[8,48,480]{2,1,0:T(8,128)(2,1)S(1)}, u32[]{:S(2)}, u32[]{:S(2)}) collective-permute-start(bf16[8,48,480]{2,1,0:T(8,128)(2,1)S(1)} %get-tuple-element.154), channel_id=1, source_target_pairs={{0,24},{8,0},{16,8},{24,16},{1,25},{9,1},{17,9},{25,17},{2,26},{10... | collective-permute-start | bytes 1105928 | tf_op jit(solution)/shard_map/ppermute | solution.py:357
  248.2 11.6 %collective-permute-start.37 = (bf16[128,1280]{1,0:T(8,128)(2,1)S(1)}, bf16[128,1280]{1,0:T(8,128)(2,1)S(1)}, u32[]{:S(2)}, u32[]{:S(2)}) collective-permute-start(bf16[128,1280]{1,0:T(8,128)(2,1)S(1)} %get-tuple-element.158), channel_id=1, source_target_pairs={{0,5},{1,4},{4,1},{5,0},{2,7},{3,6},{6,3},{7,2},{8,13},{9,12},{12,... | collective-permute-start | bytes 983048 | tf_op jit(solution)/shard_map/ppermute | solution.py:349
  249.5 14.3 %collective-permute-start.36 = (bf16[128,1280]{1,0:T(8,128)(2,1)S(1)}, bf16[128,1280]{1,0:T(8,128)(2,1)S(1)}, u32[]{:S(2)}, u32[]{:S(2)}) collective-permute-start(bf16[128,1280]{1,0:T(8,128)(2,1)S(1)} %get-tuple-element.159), channel_id=1, source_target_pairs={{0,4},{4,0},{1,5},{5,1},{2,6},{6,2},{3,7},{7,3},{8,12},{12,8},{9,1... | collective-permute-start | bytes 983048 | tf_op jit(solution)/shard_map/ppermute | solution.py:348
  250.2 13.6 %collective-permute-start.35 = (bf16[128,1280]{1,0:T(8,128)(2,1)S(1)}, bf16[128,1280]{1,0:T(8,128)(2,1)S(1)}, u32[]{:S(2)}, u32[]{:S(2)}) collective-permute-start(bf16[128,1280]{1,0:T(8,128)(2,1)S(1)} %get-tuple-element.160), channel_id=1, source_target_pairs={{0,1},{1,0},{2,3},{3,2},{4,5},{5,4},{6,7},{7,6},{8,9},{9,8},{10,11... | collective-permute-start | bytes 983048 | tf_op jit(solution)/shard_map/ppermute | solution.py:346
  259.8 26.5 %collective-permute-start.44 = (bf16[8,48,480]{2,1,0:T(8,128)(2,1)S(1)}, bf16[8,48,480]{2,1,0:T(8,128)(2,1)S(1)}, u32[]{:S(2)}, u32[]{:S(2)}) collective-permute-start(bf16[8,48,480]{2,1,0:T(8,128)(2,1)S(1)} %dynamic-slice_bitcast_fusion.1), channel_id=1, source_target_pairs={{0,16},{8,24},{16,0},{24,8},{1,17},{9,25},{17,1},{25,9},{2,18},{10... | collective-permute-start | bytes 1105928 | tf_op jit(solution)/shard_map/ppermute | solution.py:357
  264.6 27.8 %collective-permute-start.42 = (bf16[4,8,1280]{2,1,0:T(8,128)(2,1)S(1)}, bf16[4,8,1280]{2,1,0:T(8,128)(2,1)S(1)}, u32[]{:S(2)}, u32[]{:S(2)}) collective-permute-start(bf16[4,8,1280]{2,1,0:T(8,128)(2,1)S(1)} %get-tuple-element.175), channel_id=1, source_target_pairs={{0,8},{8,16},{16,24},{24,0},{1,9},{9,17},{17,25},{25,1},{2,10},{10... | collective-permute-start | bytes 245768 | tf_op jit(solution)/shard_map/ppermute | solution.py:357
  264.6 26.4 %collective-permute-start.40 = (bf16[4,8,1280]{2,1,0:T(8,128)(2,1)S(1)}, bf16[4,8,1280]{2,1,0:T(8,128)(2,1)S(1)}, u32[]{:S(2)}, u32[]{:S(2)}) collective-permute-start(bf16[4,8,1280]{2,1,0:T(8,128)(2,1)S(1)} %get-tuple-element.176), channel_id=1, source_target_pairs={{0,24},{8,0},{16,8},{24,16},{1,25},{9,1},{17,9},{25,17},{2,26},{10... | collective-permute-start | bytes 245768 | tf_op jit(solution)/shard_map/ppermute | solution.py:357
  270.0 21.7 %collective-permute-start.41 = (bf16[4,8,1280]{2,1,0:T(8,128)(2,1)S(1)}, bf16[4,8,1280]{2,1,0:T(8,128)(2,1)S(1)}, u32[]{:S(2)}, u32[]{:S(2)}) collective-permute-start(bf16[4,8,1280]{2,1,0:T(8,128)(2,1)S(1)} %get-tuple-element.177), channel_id=1, source_target_pairs={{0,16},{8,24},{16,0},{24,8},{1,17},{9,25},{17,1},{25,9},{2,18},{10... | collective-permute-start | bytes 245768 | tf_op jit(solution)/shard_map/ppermute | solution.py:357
  270.0 26.6 %collective-permute-start.46 = (bf16[3,40,1280]{2,1,0:T(8,128)(2,1)}, bf16[3,40,1280]{2,1,0:T(8,128)(2,1)S(1)}, u32[]{:S(2)}, u32[]{:S(2)}) collective-permute-start(bf16[3,40,1280]{2,1,0:T(8,128)(2,1)} %get-tuple-element.161), channel_id=1, source_target_pairs={{0,8},{8,16},{16,24},{24,0},{1,9},{9,17},{17,25},{25,1},{2,10},{10... | collective-permute-start | bytes 921608 | tf_op jit(solution)/shard_map/ppermute | solution.py:357
  286.3 10.3 %collective-permute-start.48 = (bf16[3,40,1280]{2,1,0:T(8,128)(2,1)}, bf16[3,40,1280]{2,1,0:T(8,128)(2,1)S(1)}, u32[]{:S(2)}, u32[]{:S(2)}) collective-permute-start(bf16[3,40,1280]{2,1,0:T(8,128)(2,1)} %get-tuple-element.162), channel_id=1, source_target_pairs={{0,24},{8,0},{16,8},{24,16},{1,25},{9,1},{17,9},{25,17},{2,26},{10... | collective-permute-start | bytes 921608 | tf_op jit(solution)/shard_map/ppermute | solution.py:357
  287.3 21.5 %all-to-all-start.1 = ((bf16[8,48,480]{2,1,0:T(8,128)(2,1)}), bf16[8,48,480]{2,1,0:T(8,128)(2,1)S(1)}, u32[]{:S(2)}, u32[]{:S(2)}) async-start(bf16[8,48,480]{2,1,0:T(8,128)(2,1)} %fusion.8), calls=%async_computation.1 | async-start | bytes 786432 | tf_op jit(solution)/shard_map/all_to_all | solution.py:801
  291.0 16.8 %collective-permute-start.47 = (bf16[3,40,1280]{2,1,0:T(8,128)(2,1)S(1)}, bf16[3,40,1280]{2,1,0:T(8,128)(2,1)S(1)}, u32[]{:S(2)}, u32[]{:S(2)}) collective-permute-start(bf16[3,40,1280]{2,1,0:T(8,128)(2,1)S(1)} %get-tuple-element.163), channel_id=1, source_target_pairs={{0,16},{8,24},{16,0},{24,8},{1,17},{9,25},{17,1},{25,9},{2,18},{10... | collective-permute-start | bytes 921608 | tf_op jit(solution)/shard_map/ppermute | solution.py:357
  (16 other events, 41.9 us)
Sparse Core Ops, SparseCore 0:
  22.1 49.3 all-gather.1

commit v3 on v2

--- a/solution.py
+++ b/solution.py
@@ -483,7 +483,7 @@
 def feed_kernel(
     info_ref, x_ref, g_ref, att_0, att_1, att_2, att_3, gain_ref,
     near_a, across_a, all_b, far_near_a, far_across_a, far_b,
-    out_ref, act_ref, hid_ref, dup_ref, dm_ref, dmid_ref, datt_0, datt_1, datt_2, datt_3, gain_grad,
+    out_ref, pack_ref, att_pack, dmid_ref, datt_0, datt_1, datt_2, datt_3, gain_grad,
     weights, sems,
 ):
     y_index, core_index = info_ref[1] // 4, (info_ref[1] // 2) % 2
@@ -518,13 +518,13 @@
     normed = middle * inverse
     gain = gain_ref[...]
     hidden = (normed * gain).astype(jnp.bfloat16)
-    hid_ref[...] = hidden
+    pack_ref[1] = hidden
     for copy in copies[1]:
         copy.wait()
     up = jnp.dot(hidden, weights[1], preferred_element_type=jnp.float32)
     sigma = jax.nn.sigmoid(up)
     active = (up * sigma).astype(jnp.bfloat16)
-    act_ref[...] = active
+    pack_ref[0] = active
     for copy in copies[2]:
         copy.wait()
     down = jnp.dot(active, weights[2], preferred_element_type=jnp.float32)
@@ -532,45 +532,50 @@
     cot = g_ref[...]
     grad_act = mult_trans(cot, weights[2])
     grad_up = (grad_act * sigma * (1.0 + up * (1.0 - sigma))).astype(jnp.bfloat16)
-    dup_ref[...] = grad_up
+    pack_ref[2] = grad_up
+    pack_ref[4] = cot
     grad_hidden = mult_trans(grad_up, weights[1])
     gain_grad[...] = jnp.sum(grad_hidden * normed, axis=0, keepdims=True)
     grad_mid = cot.astype(jnp.float32) + norm_back(grad_hidden, normed, inverse, gain)
     dmid_ref[...] = grad_mid
     low = grad_mid.astype(jnp.bfloat16)
-    dm_ref[...] = low
+    pack_ref[3] = low
     for chip in range(4):
         for core in range(2):
+            att_pack[2 * chip + core] = atts[chip][core]
             datts[chip][core] = mult_trans(low, weights[0, source_rows(info_ref, chip, core), :]).astype(jnp.bfloat16)
 
 
-def grads_kernel(
-    info_ref, att_0, att_1, att_2, att_3, hid_ref, act_ref, dup_ref, dm_ref, g_ref,
-    kept, away, stage, sems,
-):
+def grads_kernel(info_ref, pack_ref, att_pack, far_pack, far_att, kept, stage, sems):
     core_index = (info_ref[1] // 2) % 2
     copies = []
 
     def leave(w):
         for z_index in range(4):
             for row in range(2):
-                for which, (core, target) in enumerate(((core_index, kept), (1 - core_index, away))):
-                    copy = pltpu.make_async_copy(
-                        stage.at[w, block_index(z_index, row, core)],
-                        target.at[z_index, w, row],
-                        sems.at[w, 4 * z_index + 2 * row + which],
-                    )
-                    copy.start()
-                    copies.append(copy)
-
-    for w, left, right in ((2, act_ref, g_ref), (1, hid_ref, dup_ref)):
+                copy = pltpu.make_async_copy(
+                    stage.at[w, block_index(z_index, row, core_index)],
+                    kept.at[z_index, w, row],
+                    sems.at[w, 2 * z_index + row],
+                )
+                copy.start()
+                copies.append(copy)
+
+    def both(index, part):
+        return jnp.concatenate([pack_ref[index, :, part], far_pack[index, :, part]], axis=0)
+
+    everything = slice(0, pack_ref.shape[2])
+    for w, left, right in ((2, 0, 4), (1, 1, 2)):
+        grads = both(right, everything)
         for chunk in range(5):
             part = slice(256 * chunk, 256 * chunk + 256)
-            stage[w, part, :] = trans_mult(left[:, part], right[...]).astype(jnp.bfloat16)
+            stage[w, part, :] = trans_mult(both(left, part), grads).astype(jnp.bfloat16)
         leave(w)
-    for chip, att in enumerate((att_0, att_1, att_2, att_3)):
+    grads = both(3, everything)
+    for chip in range(4):
         for core in range(2):
-            stage[0, source_rows(info_ref, chip, core), :] = trans_mult(att[core], dm_ref[...]).astype(jnp.bfloat16)
+            att = jnp.concatenate([att_pack[2 * chip + core], far_att[2 * chip + 1 - core]], axis=0)
+            stage[0, source_rows(info_ref, chip, core), :] = trans_mult(att, grads).astype(jnp.bfloat16)
     leave(0)
     for copy in copies:
         copy.wait()
@@ -601,35 +606,37 @@
     vec = jnp.concatenate([attn_gain, mlp_gain, query_scale]).astype(bf16)
     vec_block = jnp.zeros((1, 8, width), bf16).at[0, 0, :120].set(vec)
     in_four = inputs.reshape(4, 4, 8, width)
-    cot_four = cotangent.reshape(4, 4, 8, width)
     sent = [jnp.concatenate([pick(in_four, (z + k) % 4), vec_block]) for k in range(4)]
     got = [sent[0]] + [ring_shift(sent[k], k) for k in (1, 2, 3)]
     x_rows = jnp.stack([item[:4] for item in got], axis=1).reshape(128, width)
     vec_rows = jnp.concatenate([item[4, :1] for item in got] + [jnp.zeros((4, width), bf16)])
     own = jnp.concatenate([x_rows, vec_rows])
 
+    big = jnp.stack([w_output, w_up, w_down]).astype(bf16)
+    big = lax.all_gather(big, "z", axis=0)
+
     qkv = jnp.stack([w_query, w_key, w_value]).astype(bf16)
+    own, qkv = lax.optimization_barrier((own, qkv))
+    near = jnp.stack([own] + [plane_shift(own, step) for step in (1, 2, 3)])
     qkv = qkv.reshape(3, 40, 8, 160).transpose(2, 1, 0, 3).reshape(8, 40, 480)
     qkv = lax.all_to_all(qkv, ("y", "core", "x"), split_axis=0, concat_axis=0, tiled=True)
     qkv = qkv.reshape(320, 480)
-    w_qkv = by_source([qkv] + [ring_shift(qkv, k) for k in (1, 2, 3)], z).reshape(width, 480)
-
-    near = jnp.stack([own] + [plane_shift(own, step) for step in (1, 2, 3)])
-
-    big = jnp.stack([w_output, w_up, w_down]).astype(bf16)
-    big = lax.all_gather(big, "z", axis=0)
-    big, near = lax.optimization_barrier((big, near))
+
+    late = qkv
+    big, near, qkv = lax.optimization_barrier((big, near, qkv))
+    one, three = ring_shift(qkv, 1), ring_shift(qkv, 3)
     far = core_swap(near)
     part_a, part_b = big[:2], big[2:]
     near_a = pair(part_a, plane_shift(part_a, 1), x, 2).reshape(2, 3, 80, width)
     part_b = pair(part_b, plane_shift(part_b, 2), y, 2)
-    near_a, part_b, w_qkv, cot_four = lax.optimization_barrier((near_a, part_b, w_qkv, cot_four))
-    cot_sent = [pick(cot_four, (z + k) % 4) for k in range(4)]
-    cot_got = [cot_sent[0]] + [ring_shift(cot_sent[k], k) for k in (1, 2, 3)]
-    cot_rows = jnp.stack(cot_got, axis=1).reshape(128, width)
-
+    near_a, part_b, cotangent, late, one, three = lax.optimization_barrier(
+        (near_a, part_b, cotangent, late, one, three)
+    )
+    w_qkv = by_source([qkv, one, ring_shift(late, 2), three], z).reshape(width, 480)
     across_a = plane_shift(near_a, 2)
     across_b = plane_shift(part_b, 1)
+    cot_four = lax.all_to_all(cotangent.reshape(4, 4, 8, width), "z", split_axis=0, concat_axis=0, tiled=True)
+    cot_rows = jnp.stack([pick(cot_four, (z - k) % 4) for k in range(4)], axis=1).reshape(128, width)
 
     vecs = jnp.stack([near[:, 128:132, :120], far[:, 128:132, :120]])
     vecs = vecs.astype(f32).reshape(2, 2, 2, 4, 120)
@@ -680,12 +687,16 @@
     smem = pl.BlockSpec(memory_space=pltpu.SMEM)
     vmem = pl.BlockSpec(memory_space=pltpu.VMEM)
     hbm = pl.BlockSpec(memory_space=pl.ANY)
-    out_rows, active, hidden_two, grad_up, dm, grad_mid, *datts, gain_two_grad = pl.pallas_call(
+    out_rows, pack, att_pack, grad_mid, *datts, gain_two_grad = pl.pallas_call(
         feed_kernel,
         in_specs=[smem] + [vmem] * 7 + [hbm] * 6,
-        out_specs=[vmem] * 11,
-        out_shape=[low_rows] * 5
-        + [jax.ShapeDtypeStruct((128, width), f32)]
+        out_specs=[vmem] * 9,
+        out_shape=[
+            low_rows,
+            jax.ShapeDtypeStruct((5, 128, width), bf16),
+            jax.ShapeDtypeStruct((8, 128, 160), bf16),
+            jax.ShapeDtypeStruct((128, width), f32),
+        ]
         + [datt_shape] * 4
         + [jax.ShapeDtypeStruct((1, width), f32)],
         scratch_shapes=[pltpu.VMEM((3, width, width), bf16), pltpu.SemaphoreType.DMA((3, 16))],
@@ -706,17 +717,16 @@
     grad_att_near = jnp.stack([item[0] for item in back])
     grad_att_far = core_swap(jnp.stack([item[1] for item in back]))
 
-    block_shape = jax.ShapeDtypeStruct((4, 3, 2, 80, width), bf16)
-    kept, away = pl.pallas_call(
+    kept = pl.pallas_call(
         grads_kernel,
-        in_specs=[smem] + [vmem] * 9,
-        out_specs=[hbm] * 2,
-        out_shape=[block_shape] * 2,
-        scratch_shapes=[pltpu.VMEM((3, width, width), bf16), pltpu.SemaphoreType.DMA((3, 16))],
+        in_specs=[smem] + [vmem] * 4,
+        out_specs=hbm,
+        out_shape=jax.ShapeDtypeStruct((4, 3, 2, 80, width), bf16),
+        scratch_shapes=[pltpu.VMEM((3, width, width), bf16), pltpu.SemaphoreType.DMA((3, 8))],
         compiler_params=limit,
-        cost_estimate=pl.CostEstimate(flops=6_000_000_000, bytes_accessed=12_000_000, transcendentals=0),
+        cost_estimate=pl.CostEstimate(flops=6_000_000_000, bytes_accessed=8_000_000, transcendentals=0),
         name="grads",
-    )(info, *atts, hidden_two, active, grad_up, dm, cot_rows)
+    )(info, pack, att_pack, core_swap(pack), core_swap(att_pack))
 
     def added(left, right):
         return (left.astype(f32) + right.astype(f32)).astype(bf16)
@@ -725,7 +735,6 @@
         first, second = (lax.index_in_dim(array, i, axis, keepdims=False) for i in (0, 1))
         return jnp.where(index == 0, first, second), jnp.where(index == 0, second, first)
 
-    kept = added(kept, core_swap(away))
     kept, grad_att_near, grad_att_far, outputs = lax.optimization_barrier(
         (kept, grad_att_near, grad_att_far, outputs)
     )
@@ -771,14 +780,6 @@
         name="attend_back",
     )(info, near, far, gain_one, query_mult, w_qkv, pre, grad_att_near, grad_att_far)
 
-    kept_a, kept_b, hid_near, hid_far, qkv_grad = lax.optimization_barrier(
-        (kept_a, kept_b, hid_near, hid_far, qkv_grad)
-    )
-    kept_a, away_a = halves(kept_a, y, 2)
-    kept_b, away_b = halves(kept_b, x, 2)
-    kept_a = added(kept_a, plane_shift(away_a, 2))
-    kept_b = added(kept_b, plane_shift(away_b, 1))
-    kept = jnp.concatenate([kept_a, kept_b])
     scale_line = lax.dynamic_update_slice(jnp.zeros((1, width), f32), scale_grad, (0, 160 * plane))
     lines = jnp.concatenate([gain_one_grad, gain_two_grad, scale_line])
     lines = lines.reshape(3, 4, 8, 40).transpose(1, 2, 0, 3).reshape(4, 8, 1, 120).astype(bf16)
@@ -786,8 +787,14 @@
     send = jnp.concatenate([qkv_grad.reshape(4, 8, 40, 480), lines], axis=2)
     one, three = (ring_shift(pick(send, (z + k) % 4), k) for k in (1, 3))
     hid = added(hid_near, core_swap(hid_far))
-    hid, send = lax.optimization_barrier((hid, send))
-    two = ring_shift(pick(send, (z + 2) % 4), 2)
+    later = send
+    kept_a, kept_b, hid, one, three, later = lax.optimization_barrier((kept_a, kept_b, hid, one, three, later))
+    kept_a, away_a = halves(kept_a, y, 2)
+    kept_b, away_b = halves(kept_b, x, 2)
+    kept_a = added(kept_a, plane_shift(away_a, 2))
+    kept_b = added(kept_b, plane_shift(away_b, 1))
+    kept = jnp.concatenate([kept_a, kept_b])
+    two = ring_shift(pick(later, (z + 2) % 4), 2)
     grad_hid = hid[0].astype(f32)
     moved = [plane_shift(hid[step], step) for step in (1, 2, 3)]
     *moved, kept = lax.optimization_barrier((*moved, kept))

time: 321 us -> 298 us (0.928)
  waiting for transfers between devices: 148 us -> 113 us
  starting transfers between devices: 61.3 us -> 68.2 us
    ppermute x21 -> x18, waiting for transfers between devices: 73.4 us -> 52.7 us  [ring_shift(): return lax.ppermute(value, 'z', [(i, (i + step) % 4) for i in range(4)])]
    ppermute x4, waiting for transfers between devices: 23.7 us -> 7.04 us  [plane_shift(): return lax.ppermute(value, ('y', 'x'), [(0, 3), (1, 2), (2, 1), (3, 0)])]
    ppermute x8, waiting for transfers between devices: 19.6 us -> 10.9 us  [plane_shift(): return lax.ppermute(value, 'x', [(0, 1), (1, 0)])]
    ppermute x8, waiting for transfers between devices: 23.2 us -> 29.5 us  [plane_shift(): return lax.ppermute(value, 'y', [(0, 1), (1, 0)])]
    all_to_all x0 -> x1, starting transfers between devices: none -> 5.8 us  [planes(): lax.all_to_all(cotangent.reshape(4, 4, 8, width), 'z', split_axis=0, conc...]
    ppermute x21 -> x18, starting transfers between devices: 26 us -> 29.5 us  [ring_shift(): return lax.ppermute(value, 'z', [(i, (i + step) % 4) for i in range(4)])]
    convert_element_type x6 -> x5, other arithmetic: 10.2 us -> 6.83 us  [added(): return (left.astype(f32) + right.astype(f32)).astype(bf16)]
    unnamed x74 -> x96, local copies, waits for them, and re-layouts: 13 us -> 10.7 us
  transfers between devices with their start and end apart: 52 -> 51, of which waited for: 26 -> 26; matrix products, arithmetic and copies ran while one was open for 11% -> 15% of each run, Pallas kernels for 9% -> 9%
where the time goes in v3:
time: 298 us; the launch traced here: 296 us
  waiting for transfers between devices  113 us (38%)
  starting transfers between devices  68.2 us (23%)
  Pallas kernels  36.9 us (12%)
  local copies, waits for them, and re-layouts  34.9 us (12%)
  other arithmetic  28.5 us (10%)
  between operations  15.1 us (5%)
    ppermute x18, waiting for transfers between devices, ring_shift(): return lax.ppermute(value, 'z', [(i, (i + step) % 4) for i in range(4)])  52.7 us
    ppermute x18, starting transfers between devices, ring_shift(): return lax.ppermute(value, 'z', [(i, (i + step) % 4) for i in range(4)])  29.5 us
    ppermute x8, waiting for transfers between devices, plane_shift(): return lax.ppermute(value, 'y', [(0, 1), (1, 0)])  29.5 us
    pallas_call x1, Pallas kernels, planes(): pl.pallas_call(attend_back_kernel, grid_spec=pltpu.PrefetchScalarGridSpec...  13.4 us
    ppermute x8, waiting for transfers between devices, plane_shift(): return lax.ppermute(value, 'x', [(0, 1), (1, 0)])  10.9 us
    unnamed x96, local copies, waits for them, and re-layouts  10.7 us
    pallas_call x1, Pallas kernels, planes(): pl.pallas_call(feed_kernel, in_specs=[smem] + [vmem] * 7 + [hbm] * 6, out...  9.56 us
    ppermute x9, waiting for transfers between devices, core_swap(): return lax.ppermute(value, 'core', [(0, 1), (1, 0)])  8.96 us
  transfers between devices with their start and end apart: 51, of which 26 were waited for; matrix products, arithmetic and copies ran while one was open for 15% of the time, Pallas kernels for 9%

profile of v3, /device:TPU:0, one launch (start us, length us, event | category | flops | bytes accessed | tf_op | source)
XLA Modules:
  0.0 296.4 jit_solution(7480088822263929738)
XLA Ops:
  10.4 3.1 %collective-permute-start = (bf16[5,8,1280]{2,1,0:T(8,128)(2,1)S(1)}, bf16[5,8,1280]{2,1,0:T(8,128)(2,1)S(1)}, u32[]{:S(2)}, u32[]{:S(2)}) collective-permute-start(bf16[5,8,1280]{2,1,0:T(8,128)(2,1)S(1)} %get-tuple-element.200), channel_id=1, source_target_pairs={{0,8},{8,16},{16,24},{24,0},{1,9},{9,17},{17,25},{25,1},{2,10},{10... | collective-permute-start | bytes 307208 | tf_op jit(solution)/shard_map/ppermute | solution.py:357
  13.5 2.6 collective-permute-start.1
  16.1 1.3 collective-permute-start.2
  17.6 1.8 collective-permute-done
  19.3 3.6 %collective-permute-done.1 = bf16[5,8,1280]{2,1,0:T(8,128)(2,1)S(1)} collective-permute-done((bf16[5,8,1280]{2,1,0:T(8,128)(2,1)S(1)}, bf16[5,8,1280]{2,1,0:T(8,128)(2,1)S(1)}, u32[]{:S(2)}, u32[]{:S(2)}) %collective-permute-start.1) | collective-permute-done | bytes 102432 | tf_op jit(solution)/shard_map/ppermute | solution.py:357
  23.5 2.5 collective-permute-start.5
  29.2 3.7 %all-to-all-start = ((bf16[8,40,480]{2,1,0:T(8,128)(2,1)}), bf16[8,40,480]{2,1,0:T(8,128)(2,1)S(1)}, u32[]{:S(2)}, u32[]{:S(2)}) async-start(bf16[8,40,480]{2,1,0:T(8,128)(2,1)} %reshape.334), calls=%async_computation | async-start | bytes 655360 | tf_op jit(solution)/shard_map/all_to_all | solution.py:622
  32.9 2.6 collective-permute-done.5
  35.5 6.7 %collective-permute-done.4 = bf16[136,1280]{1,0:T(8,128)(2,1)S(1)} collective-permute-done((bf16[136,1280]{1,0:T(8,128)(2,1)S(1)}, bf16[136,1280]{1,0:T(8,128)(2,1)S(1)}, u32[]{:S(2)}, u32[]{:S(2)}) %collective-permute-start.4) | collective-permute-done | bytes 348192 | tf_op jit(solution)/shard_map/ppermute | solution.py:348
  43.2 2.1 all-to-all-done
  45.4 2.5 fusion.41
  47.9 1.5 collective-permute-start.8
  49.4 1.2 collective-permute-start.7
  51.0 3.2 %collective-permute-start.10 = (bf16[320,480]{1,0:T(8,128)(2,1)S(1)}, bf16[320,480]{1,0:T(8,128)(2,1)S(1)}, u32[]{:S(2)}, u32[]{:S(2)}) collective-permute-start(bf16[320,480]{1,0:T(8,128)(2,1)S(1)} %bitcast.247), channel_id=1, source_target_pairs={{0,24},{8,0},{16,8},{24,16},{1,25},{9,1},{17,9},{25,17},{2,26},{10... | collective-permute-start | bytes 921608 | tf_op jit(solution)/shard_map/ppermute | solution.py:357
  55.1 9.0 %collective-permute-done.8 = bf16[2,3,40,1280]{3,2,1,0:T(8,128)(2,1)} collective-permute-done((bf16[2,3,40,1280]{3,2,1,0:T(8,128)(2,1)}, bf16[2,3,40,1280]{3,2,1,0:T(8,128)(2,1)}, u32[]{:S(2)}, u32[]{:S(2)}) %collective-permute-start.8) | collective-permute-done | bytes 614432 | tf_op jit(solution)/shard_map/ppermute | solution.py:348
  65.2 1.4 select_bitcast_fusion.7
  69.1 2.1 collective-permute-start.11
  71.4 5.8 %all-to-all-start.1 = ((bf16[4,4,8,1280]{3,2,1,0:T(8,128)(2,1)}), bf16[4,4,8,1280]{3,2,1,0:T(8,128)(2,1)}, u32[]{:S(2)}, u32[]{:S(2)}) async-start(bf16[4,4,8,1280]{3,2,1,0:T(8,128)(2,1)} %bitcast.43), calls=%async_computation.1 | async-start | bytes 655360 | tf_op jit(solution)/shard_map/all_to_all | solution.py:638
  77.8 1.4 collective-permute-start.18
  80.2 10.9 %collective-permute-done.11 = bf16[320,480]{1,0:T(8,128)(2,1)S(1)} collective-permute-done((bf16[320,480]{1,0:T(8,128)(2,1)S(1)}, bf16[320,480]{1,0:T(8,128)(2,1)S(1)}, u32[]{:S(2)}, u32[]{:S(2)}) %collective-permute-start.11) | collective-permute-done | bytes 307232 | tf_op jit(solution)/shard_map/ppermute | solution.py:357
  91.4 1.5 all-to-all-done.1
  95.4 8.3 %attend.1 = (f32[2,4,128,480]{3,2,1,0:T(8,128)}, bf16[4,128,160]{2,1,0:T(8,128)(2,1)S(1)}, bf16[4,128,160]{2,1,0:T(8,128)(2,1)S(1)}) custom-call(s32[6]{0:T(128)S(1)} %pad_add_fusion.info_ref, bf16[4,136,1280]{2,1,0:T(8,128)(2,1)S(1)} %pad_maximum_fusion.1.near_ref, bf16[4,136,1280]{2,1,0:T(8,128)(2,1)} %collective-permute-done.6.far_ref, ...), custom_call_target="tpu_custom_call" | custom-call | flops 8999999488 | bytes 8000000 | tf_op jit(solution)/shard_map/attend/pallas_call | solution.py:655
  104.3 2.8 collective-permute-done.12
  107.2 2.3 collective-permute-start.15
  110.1 4.4 %collective-permute-done.15.att_3 = bf16[2,128,160]{2,1,0:T(8,128)(2,1)S(1)} collective-permute-done((bf16[2,128,160]{2,1,0:T(8,128)(2,1)S(1)}, bf16[2,128,160]{2,1,0:T(8,128)(2,1)S(1)}, u32[]{:S(2)}, u32[]{:S(2)}) %collective-permute-start.15) | collective-permute-done | bytes 81952 | tf_op jit(solution)/shard_map/ppermute | solution.py:349
  114.5 1.4 collective-permute-start.14
  116.4 3.1 %collective-permute-done.14.att_2 = bf16[2,128,160]{2,1,0:T(8,128)(2,1)S(1)} collective-permute-done((bf16[2,128,160]{2,1,0:T(8,128)(2,1)S(1)}, bf16[2,128,160]{2,1,0:T(8,128)(2,1)S(1)}, u32[]{:S(2)}, u32[]{:S(2)}) %collective-permute-start.14) | collective-permute-done | bytes 81952 | tf_op jit(solution)/shard_map/ppermute | solution.py:348
  119.5 2.3 select_bitcast_fusion.3
  122.0 1.6 copy.104
  124.2 6.2 %collective-permute-done.19.far_across_a = bf16[2,3,80,1280]{3,2,1,0:T(8,128)(2,1)} collective-permute-done((bf16[2,3,80,1280]{3,2,1,0:T(8,128)(2,1)}, bf16[2,3,80,1280]{3,2,1,0:T(8,128)(2,1)}, u32[]{:S(2)}, u32[]{:S(2)}) %collective-permute-start.19) | collective-permute-done | bytes 1228832 | tf_op jit(solution)/shard_map/ppermute | solution.py:353
  130.4 9.6 %feed.1 = (bf16[128,1280]{1,0:T(8,128)(2,1)S(1)}, bf16[5,128,1280]{2,1,0:T(8,128)(2,1)}, bf16[8,128,160]{2,1,0:T(8,128)(2,1)S(1)}, f32[128,1280]{1,0:T(8,128)S(1...) custom-call(s32[6]{0:T(128)S(1)} %pad_add_fusion.info_ref, ...), custom_call_target="tpu_custom_call" | custom-call | flops 12000000000 | bytes 13000000 | tf_op jit(solution)/shard_map/feed/pallas_call | solution.py:690
  139.9 1.6 collective-permute-start.23
  141.5 1.3 collective-permute-start.24
  144.3 1.6 collective-permute-done.23
  145.8 3.7 %collective-permute-done.24 = bf16[2,128,160]{2,1,0:T(8,128)(2,1)S(1)} collective-permute-done((bf16[2,128,160]{2,1,0:T(8,128)(2,1)S(1)}, bf16[2,128,160]{2,1,0:T(8,128)(2,1)S(1)}, u32[]{:S(2)}, u32[]{:S(2)}) %collective-permute-start.24) | collective-permute-done | bytes 81952 | tf_op jit(solution)/shard_map/ppermute | solution.py:348
  150.0 3.5 %collective-permute-start.27 = (bf16[4,8,1280]{2,1,0:T(8,128)(2,1)S(1)}, bf16[4,8,1280]{2,1,0:T(8,128)(2,1)S(1)}, u32[]{:S(2)}, u32[]{:S(2)}) collective-permute-start(bf16[4,8,1280]{2,1,0:T(8,128)(2,1)S(1)} %get-tuple-element.179), channel_id=1, source_target_pairs={{0,24},{8,0},{16,8},{24,16},{1,25},{9,1},{17,9},{25,17},{2,26},{10... | collective-permute-start | bytes 245768 | tf_op jit(solution)/shard_map/ppermute | solution.py:357
  153.7 1.9 collective-permute-done.27
  155.6 4.6 %collective-permute-done.28 = bf16[4,8,1280]{2,1,0:T(8,128)(2,1)S(1)} collective-permute-done((bf16[4,8,1280]{2,1,0:T(8,128)(2,1)S(1)}, bf16[4,8,1280]{2,1,0:T(8,128)(2,1)S(1)}, u32[]{:S(2)}, u32[]{:S(2)}) %collective-permute-start.28) | collective-permute-done | bytes 81952 | tf_op jit(solution)/shard_map/ppermute | solution.py:357
  161.1 1.3 copy-done.34
  162.3 5.6 %grads.1 = bf16[4,3,2,80,1280]{4,3,2,1,0:T(8,128)(2,1)} custom-call(s32[6]{0:T(128)S(1)} %pad_add_fusion.info_ref, bf16[5,128,1280]{2,1,0:T(8,128)(2,1)S(1)} %copy-done.2, bf16[8,128,160]{2,1,0:T(8,128)(2,1)S(1)} %get-tuple-element.106.att_pack, bf16[5,128,1280]{2,1,0:T(8,128)(2,1)} %copy-done.34, bf16[8,128,160]{2,1,0:T(8,128)(2,1)S(1)} %collective-permute-done.22.far_att), custom_call_target="tpu_custom_call" | custom-call | flops 6000000000 | bytes 8000000 | tf_op jit(solution)/shard_map/grads/pallas_call | solution.py:720
  167.9 2.8 fusion.37
  176.7 13.4 %attend_back.1 = (bf16[4,128,1280]{2,1,0:T(8,128)(2,1)S(1)}, bf16[4,128,1280]{2,1,0:T(8,128)(2,1)S(1)}, bf16[1280,480]{1,0:T(8,128)(2,1)}, f32[1,1280]{1,0:T(1,128)S(1)}, f32[1,160]{1,0:T(1,128)S(1)}) custom-call(s32[6]{0:T(128)S(1)} %pad_add_fusion.info_ref, bf16[4,136,1280]{2,1,0:T(8,128)(2,1)} %copy-done, ...), custom_call_target="tpu_custom_call" | custom-call | flops 15000000512 | bytes 12000000 | tf_op jit(solution)/shard_map/attend_back/pallas_call | solution.py:753
  191.7 1.7 fusion.3
  193.4 1.4 collective-permute-start.34
  195.5 6.8 %collective-permute-done.30 = bf16[2,3,2,40,1280]{4,3,1,0,2:T(8,128)(2,1)} collective-permute-done((bf16[2,3,2,40,1280]{4,3,1,0,2:T(8,128)(2,1)}, bf16[2,3,2,40,1280]{4,3,1,0,2:T(8,128)(2,1)}, u32[]{:S(2)}, u32[]{:S(2)}) %collective-permute-start.30) | collective-permute-done | bytes 1228832 | tf_op jit(solution)/shard_map/ppermute | solution.py:346
  202.3 1.7 fusion.2
  204.2 2.0 fusion.1
  206.6 6.8 %collective-permute-done.34 = bf16[8,48,480]{2,1,0:T(8,128)(2,1)S(1)} collective-permute-done((bf16[8,48,480]{2,1,0:T(8,128)(2,1)S(1)}, bf16[8,48,480]{2,1,0:T(8,128)(2,1)S(1)}, u32[]{:S(2)}, u32[]{:S(2)}) %collective-permute-start.34) | collective-permute-done | bytes 368672 | tf_op jit(solution)/shard_map/ppermute | solution.py:357
  213.4 1.5 collective-permute-start.43
  220.0 1.3 collective-permute-start.37
  222.3 11.0 %collective-permute-done.43 = bf16[8,48,480]{2,1,0:T(8,128)(2,1)S(1)} collective-permute-done((bf16[8,48,480]{2,1,0:T(8,128)(2,1)S(1)}, bf16[8,48,480]{2,1,0:T(8,128)(2,1)S(1)}, u32[]{:S(2)}, u32[]{:S(2)}) %collective-permute-start.43) | collective-permute-done | bytes 368672 | tf_op jit(solution)/shard_map/ppermute | solution.py:357
  233.4 1.4 collective-permute-start.35
  235.7 3.5 %all-to-all-start.2 = ((bf16[8,48,480]{2,1,0:T(8,128)(2,1)}), bf16[8,48,480]{2,1,0:T(8,128)(2,1)S(1)}, u32[]{:S(2)}, u32[]{:S(2)}) async-start(bf16[8,48,480]{2,1,0:T(8,128)(2,1)} %fusion.8), calls=%async_computation.2 | async-start | bytes 786432 | tf_op jit(solution)/shard_map/all_to_all | solution.py:808
  239.2 1.4 fusion.4
  240.6 1.4 collective-permute-done.38
  242.0 1.3 fusion.5
  243.5 5.5 %collective-permute-done.36 = bf16[128,1280]{1,0:T(8,128)(2,1)S(1)} collective-permute-done((bf16[128,1280]{1,0:T(8,128)(2,1)}, bf16[128,1280]{1,0:T(8,128)(2,1)S(1)}, u32[]{:S(2)}, u32[]{:S(2)}) %collective-permute-start.36) | collective-permute-done | bytes 327712 | tf_op jit(solution)/shard_map/ppermute | solution.py:348
  248.9 1.3 multiply_reduce_fusion
  250.3 1.3 add_convert_fusion.1
  253.5 2.7 collective-permute-start.40
  257.2 1.6 collective-permute-start.44
  258.8 2.2 collective-permute-start.46
  275.4 12.1 %collective-permute-done.45 = bf16[3,40,1280]{2,1,0:T(8,128)(2,1)S(1)} collective-permute-done((bf16[3,40,1280]{2,1,0:T(8,128)(2,1)S(1)}, bf16[3,40,1280]{2,1,0:T(8,128)(2,1)S(1)}, u32[]{:S(2)}, u32[]{:S(2)}) %collective-permute-start.45) | collective-permute-done | bytes 307232 | tf_op jit(solution)/shard_map/ppermute | solution.py:357
  287.5 1.2 fusion.13
  (256 shorter events, 56.2 us)
Async XLA Ops:
  7.2 38.2 %all-gather.2.cloned.1.call-start = ((), (), s32[]{:S(2)}) async-start(), calls=%async_computation.3 | async-start | bytes 1536000 | tf_op jit(solution)/shard_map/all_gather | solution.py:616
  10.4 8.9 %collective-permute-start = (bf16[5,8,1280]{2,1,0:T(8,128)(2,1)S(1)}, bf16[5,8,1280]{2,1,0:T(8,128)(2,1)S(1)}, u32[]{:S(2)}, u32[]{:S(2)}) collective-permute-start(bf16[5,8,1280]{2,1,0:T(8,128)(2,1)S(1)} %get-tuple-element.200), channel_id=1, source_target_pairs={{0,8},{8,16},{16,24},{24,0},{1,9},{9,17},{17,25},{25,1},{2,10},{10... | collective-permute-start | bytes 307208 | tf_op jit(solution)/shard_map/ppermute | solution.py:357
  13.5 9.4 %collective-permute-start.1 = (bf16[5,8,1280]{2,1,0:T(8,128)(2,1)S(1)}, bf16[5,8,1280]{2,1,0:T(8,128)(2,1)S(1)}, u32[]{:S(2)}, u32[]{:S(2)}) collective-permute-start(bf16[5,8,1280]{2,1,0:T(8,128)(2,1)S(1)} %get-tuple-element.201), channel_id=1, source_target_pairs={{0,16},{8,24},{16,0},{24,8},{1,17},{9,25},{17,1},{25,9},{2,18},{10... | collective-permute-start | bytes 307208 | tf_op jit(solution)/shard_map/ppermute | solution.py:357
  16.1 6.9 %collective-permute-start.2 = (bf16[5,8,1280]{2,1,0:T(8,128)(2,1)S(1)}, bf16[5,8,1280]{2,1,0:T(8,128)(2,1)S(1)}, u32[]{:S(2)}, u32[]{:S(2)}) collective-permute-start(bf16[5,8,1280]{2,1,0:T(8,128)(2,1)S(1)} %get-tuple-element.202), channel_id=1, source_target_pairs={{0,24},{8,0},{16,8},{24,16},{1,25},{9,1},{17,9},{25,17},{2,26},{10... | collective-permute-start | bytes 307208 | tf_op jit(solution)/shard_map/ppermute | solution.py:357
  23.5 12.0 %collective-permute-start.5 = (bf16[136,1280]{1,0:T(8,128)(2,1)S(1)}, bf16[136,1280]{1,0:T(8,128)(2,1)S(1)}, u32[]{:S(2)}, u32[]{:S(2)}) collective-permute-start(bf16[136,1280]{1,0:T(8,128)(2,1)S(1)} %concatenate.59), channel_id=1, source_target_pairs={{0,5},{1,4},{4,1},{5,0},{2,7},{3,6},{6,3},{7,2},{8,13},{9,12},{12,... | collective-permute-start | bytes 1044488 | tf_op jit(solution)/shard_map/ppermute | solution.py:349
  26.0 16.2 %collective-permute-start.4 = (bf16[136,1280]{1,0:T(8,128)(2,1)S(1)}, bf16[136,1280]{1,0:T(8,128)(2,1)S(1)}, u32[]{:S(2)}, u32[]{:S(2)}) collective-permute-start(bf16[136,1280]{1,0:T(8,128)(2,1)S(1)} %concatenate.59), channel_id=1, source_target_pairs={{0,4},{4,0},{1,5},{5,1},{2,6},{6,2},{3,7},{7,3},{8,12},{12,8},{9,1... | collective-permute-start | bytes 1044488 | tf_op jit(solution)/shard_map/ppermute | solution.py:348
  26.5 16.5 %collective-permute-start.3 = (bf16[136,1280]{1,0:T(8,128)(2,1)S(1)}, bf16[136,1280]{1,0:T(8,128)(2,1)S(1)}, u32[]{:S(2)}, u32[]{:S(2)}) collective-permute-start(bf16[136,1280]{1,0:T(8,128)(2,1)S(1)} %concatenate.59), channel_id=1, source_target_pairs={{0,1},{1,0},{2,3},{3,2},{4,5},{5,4},{6,7},{7,6},{8,9},{9,8},{10,11... | collective-permute-start | bytes 1044488 | tf_op jit(solution)/shard_map/ppermute | solution.py:346
  29.2 16.2 %all-to-all-start = ((bf16[8,40,480]{2,1,0:T(8,128)(2,1)}), bf16[8,40,480]{2,1,0:T(8,128)(2,1)S(1)}, u32[]{:S(2)}, u32[]{:S(2)}) async-start(bf16[8,40,480]{2,1,0:T(8,128)(2,1)} %reshape.334), calls=%async_computation | async-start | bytes 655360 | tf_op jit(solution)/shard_map/all_to_all | solution.py:622
  43.2 52.2 %copy-start = (bf16[4,136,1280]{2,1,0:T(8,128)(2,1)}, bf16[4,136,1280]{2,1,0:T(8,128)(2,1)S(1)}, u32[]{:S(2)}) copy-start(bf16[4,136,1280]{2,1,0:T(8,128)(2,1)S(1)} %pad_maximum_fusion.1.near_ref) | copy-start | bytes 4177924
  45.4 19.8 %copy-start.18 = (bf16[4,3,40,1280]{3,2,1,0:T(8,128)(2,1)S(1)}, bf16[4,3,40,1280]{3,2,1,0:T(8,128)(2,1)}, u32[]{:S(2)}) copy-start(bf16[4,3,40,1280]{3,2,1,0:T(8,128)(2,1)} %all-gather.2.cloned.1.call-done) | copy-start | bytes 3686404
  47.9 16.2 %collective-permute-start.8 = (bf16[2,3,40,1280]{3,2,1,0:T(8,128)(2,1)}, bf16[2,3,40,1280]{3,2,1,0:T(8,128)(2,1)}, u32[]{:S(2)}, u32[]{:S(2)}) collective-permute-start(bf16[2,3,40,1280]{3,2,1,0:T(8,128)(2,1)} %get-tuple-element.166), channel_id=1, source_target_pairs={{0,4},{4,0},{1,5},{5,1},{2,6},{6,2},{3,7},{7,3},{8,12},{12,8},{9,1... | collective-permute-start | bytes 1843208 | tf_op jit(solution)/shard_map/ppermute | solution.py:348
  49.4 15.8 %collective-permute-start.7 = (bf16[2,3,40,1280]{3,2,1,0:T(8,128)(2,1)}, bf16[2,3,40,1280]{3,2,1,0:T(8,128)(2,1)}, u32[]{:S(2)}, u32[]{:S(2)}) collective-permute-start(bf16[2,3,40,1280]{3,2,1,0:T(8,128)(2,1)} %get-tuple-element.167), channel_id=1, source_target_pairs={{0,1},{1,0},{2,3},{3,2},{4,5},{5,4},{6,7},{7,6},{8,9},{9,8},{10,11... | collective-permute-start | bytes 1843208 | tf_op jit(solution)/shard_map/ppermute | solution.py:346
  51.0 18.2 %collective-permute-start.10 = (bf16[320,480]{1,0:T(8,128)(2,1)S(1)}, bf16[320,480]{1,0:T(8,128)(2,1)S(1)}, u32[]{:S(2)}, u32[]{:S(2)}) collective-permute-start(bf16[320,480]{1,0:T(8,128)(2,1)S(1)} %bitcast.247), channel_id=1, source_target_pairs={{0,24},{8,0},{16,8},{24,16},{1,25},{9,1},{17,9},{25,17},{2,26},{10... | collective-permute-start | bytes 921608 | tf_op jit(solution)/shard_map/ppermute | solution.py:357
  54.2 15.0 %collective-permute-start.9 = (bf16[320,480]{1,0:T(8,128)(2,1)S(1)}, bf16[320,480]{1,0:T(8,128)(2,1)S(1)}, u32[]{:S(2)}, u32[]{:S(2)}) collective-permute-start(bf16[320,480]{1,0:T(8,128)(2,1)S(1)} %bitcast.248), channel_id=1, source_target_pairs={{0,8},{8,16},{16,24},{24,0},{1,9},{9,17},{17,25},{25,1},{2,10},{10... | collective-permute-start | bytes 921608 | tf_op jit(solution)/shard_map/ppermute | solution.py:357
  69.1 22.0 %collective-permute-start.11 = (bf16[320,480]{1,0:T(8,128)(2,1)S(1)}, bf16[320,480]{1,0:T(8,128)(2,1)S(1)}, u32[]{:S(2)}, u32[]{:S(2)}) collective-permute-start(bf16[320,480]{1,0:T(8,128)(2,1)S(1)} %bitcast.249), channel_id=1, source_target_pairs={{0,16},{8,24},{16,0},{24,8},{1,17},{9,25},{17,1},{25,9},{2,18},{10... | collective-permute-start | bytes 921608 | tf_op jit(solution)/shard_map/ppermute | solution.py:357
  71.3 19.8 %copy-start.22 = (bf16[320,480]{1,0:T(8,128)(2,1)S(1)}, bf16[320,480]{1,0:T(8,128)(2,1)}, u32[]{:S(2)}) copy-start(bf16[320,480]{1,0:T(8,128)(2,1)} %copy-done.21) | copy-start | bytes 921604
  71.3 22.7 %collective-permute-start.6 = (bf16[4,136,1280]{2,1,0:T(8,128)(2,1)S(1)}, bf16[4,136,1280]{2,1,0:T(8,128)(2,1)}, u32[]{:S(2)}, u32[]{:S(2)}) collective-permute-start(bf16[4,136,1280]{2,1,0:T(8,128)(2,1)S(1)} %pad_maximum_fusion.1.near_ref), channel_id=1, source_target_pairs={{0,2},{2,0},{1,3},{3,1},{4,6},{6,4},{5,7},{7,5},{8,10},{10,8},{9,1... | collective-permute-start | bytes 4177928 | tf_op jit(solution)/shard_map/ppermute | solution.py:353
  71.4 21.5 %all-to-all-start.1 = ((bf16[4,4,8,1280]{3,2,1,0:T(8,128)(2,1)}), bf16[4,4,8,1280]{3,2,1,0:T(8,128)(2,1)}, u32[]{:S(2)}, u32[]{:S(2)}) async-start(bf16[4,4,8,1280]{3,2,1,0:T(8,128)(2,1)} %bitcast.43), calls=%async_computation.1 | async-start | bytes 655360 | tf_op jit(solution)/shard_map/all_to_all | solution.py:638
  77.2 14.0 %copy-start.24 = (bf16[320,480]{1,0:T(8,128)(2,1)S(1)}, bf16[320,480]{1,0:T(8,128)(2,1)}, u32[]{:S(2)}) copy-start(bf16[320,480]{1,0:T(8,128)(2,1)} %copy-done.23) | copy-start | bytes 921604
  77.2 42.2 %collective-permute-start.17 = (bf16[2,3,80,1280]{3,2,1,0:T(8,128)(2,1)}, bf16[2,3,80,1280]{3,2,1,0:T(8,128)(2,1)}, u32[]{:S(2)}, u32[]{:S(2)}) collective-permute-start(bf16[2,3,80,1280]{3,2,1,0:T(8,128)(2,1)} %bitcast.251), channel_id=1, source_target_pairs={{0,4},{4,0},{1,5},{5,1},{2,6},{6,2},{3,7},{7,3},{8,12},{12,8},{9,1... | collective-permute-start | bytes 3686408 | tf_op jit(solution)/shard_map/ppermute | solution.py:348
  77.8 41.7 %collective-permute-start.18 = (bf16[2,3,2,40,1280]{4,3,1,0,2:T(8,128)(2,1)}, bf16[2,3,2,40,1280]{4,3,1,0,2:T(8,128)(2,1)}, u32[]{:S(2)}, u32[]{:S(2)}) collective-permute-start(bf16[2,3,2,40,1280]{4,3,1,0,2:T(8,128)(2,1)} %pad_maximum_fusion.3), channel_id=1, source_target_pairs={{0,1},{1,0},{2,3},{3,2},{4,5},{5,4},{6,7},{7,6},{8,9},{9,8},{10,11... | collective-permute-start | bytes 3686408 | tf_op jit(solution)/shard_map/ppermute | solution.py:346
  91.4 12.4 %copy-start.1 = (bf16[4,320,480]{2,1,0:T(8,128)(2,1)}, bf16[4,320,480]{2,1,0:T(8,128)(2,1)S(1)}, u32[]{:S(2)}) copy-start(bf16[4,320,480]{2,1,0:T(8,128)(2,1)S(1)} %constant_dynamic-slice_fusion.2) | copy-start | bytes 3686404
  103.8 15.7 %collective-permute-start.16 = (bf16[2,3,80,1280]{3,2,1,0:T(8,128)(2,1)S(1)}, bf16[2,3,80,1280]{3,2,1,0:T(8,128)(2,1)S(1)}, u32[]{:S(2)}, u32[]{:S(2)}) collective-permute-start(bf16[2,3,80,1280]{3,2,1,0:T(8,128)(2,1)S(1)} %bitcast.253), channel_id=1, source_target_pairs={{0,2},{2,0},{1,3},{3,1},{4,6},{6,4},{5,7},{7,5},{8,10},{10,8},{9,1... | collective-permute-start | bytes 3686408 | tf_op jit(solution)/shard_map/ppermute | solution.py:353
  103.8 3.3 %collective-permute-start.12 = (bf16[4,128,160]{2,1,0:T(8,128)(2,1)S(1)}, bf16[4,128,160]{2,1,0:T(8,128)(2,1)S(1)}, u32[]{:S(2)}, u32[]{:S(2)}) collective-permute-start(bf16[4,128,160]{2,1,0:T(8,128)(2,1)S(1)} %get-tuple-element.95), channel_id=1, source_target_pairs={{0,2},{2,0},{1,3},{3,1},{4,6},{6,4},{5,7},{7,5},{8,10},{10,8},{9,1... | collective-permute-start | bytes 491528 | tf_op jit(solution)/shard_map/ppermute | solution.py:353
  107.2 7.3 %collective-permute-start.15 = (bf16[2,128,160]{2,1,0:T(8,128)(2,1)S(1)}, bf16[2,128,160]{2,1,0:T(8,128)(2,1)S(1)}, u32[]{:S(2)}, u32[]{:S(2)}) collective-permute-start(bf16[2,128,160]{2,1,0:T(8,128)(2,1)S(1)} %get-tuple-element.171), channel_id=1, source_target_pairs={{0,5},{1,4},{4,1},{5,0},{2,7},{3,6},{6,3},{7,2},{8,13},{9,12},{12,... | collective-permute-start | bytes 245768 | tf_op jit(solution)/shard_map/ppermute | solution.py:349
  109.5 6.9 %collective-permute-start.13 = (bf16[2,128,160]{2,1,0:T(8,128)(2,1)S(1)}, bf16[2,128,160]{2,1,0:T(8,128)(2,1)S(1)}, u32[]{:S(2)}, u32[]{:S(2)}) collective-permute-start(bf16[2,128,160]{2,1,0:T(8,128)(2,1)S(1)} %get-tuple-element.173), channel_id=1, source_target_pairs={{0,1},{1,0},{2,3},{3,2},{4,5},{5,4},{6,7},{7,6},{8,9},{9,8},{10,11... | collective-permute-start | bytes 245768 | tf_op jit(solution)/shard_map/ppermute | solution.py:346
  114.5 5.0 %collective-permute-start.14 = (bf16[2,128,160]{2,1,0:T(8,128)(2,1)S(1)}, bf16[2,128,160]{2,1,0:T(8,128)(2,1)S(1)}, u32[]{:S(2)}, u32[]{:S(2)}) collective-permute-start(bf16[2,128,160]{2,1,0:T(8,128)(2,1)S(1)} %get-tuple-element.174), channel_id=1, source_target_pairs={{0,4},{4,0},{1,5},{5,1},{2,6},{6,2},{3,7},{7,3},{8,12},{12,8},{9,1... | collective-permute-start | bytes 245768 | tf_op jit(solution)/shard_map/ppermute | solution.py:348
  123.6 6.8 %collective-permute-start.20 = (bf16[2,3,2,80,1280]{4,3,2,1,0:T(8,128)(2,1)}, bf16[2,3,2,80,1280]{4,3,2,1,0:T(8,128)(2,1)}, u32[]{:S(2)}, u32[]{:S(2)}) collective-permute-start(bf16[2,3,2,80,1280]{4,3,2,1,0:T(8,128)(2,1)} %bitcast.57.all_b), channel_id=1, source_target_pairs={{0,2},{2,0},{1,3},{3,1},{4,6},{6,4},{5,7},{7,5},{8,10},{10,8},{9,1... | collective-permute-start | bytes 7372808 | tf_op jit(solution)/shard_map/ppermute | solution.py:353
  123.6 6.8 %collective-permute-start.19 = (bf16[2,3,80,1280]{3,2,1,0:T(8,128)(2,1)}, bf16[2,3,80,1280]{3,2,1,0:T(8,128)(2,1)}, u32[]{:S(2)}, u32[]{:S(2)}) collective-permute-start(bf16[2,3,80,1280]{3,2,1,0:T(8,128)(2,1)} %collective-permute-done.17.across_a), channel_id=1, source_target_pairs={{0,2},{2,0},{1,3},{3,1},{4,6},{6,4},{5,7},{7,5},{8,10},{10,8},{9,1... | collective-permute-start | bytes 3686408 | tf_op jit(solution)/shard_map/ppermute | solution.py:353
  139.9 5.9 %collective-permute-start.23 = (bf16[2,128,160]{2,1,0:T(8,128)(2,1)S(1)}, bf16[2,128,160]{2,1,0:T(8,128)(2,1)S(1)}, u32[]{:S(2)}, u32[]{:S(2)}) collective-permute-start(bf16[2,128,160]{2,1,0:T(8,128)(2,1)S(1)} %get-tuple-element.108), channel_id=1, source_target_pairs={{0,1},{1,0},{2,3},{3,2},{4,5},{5,4},{6,7},{7,6},{8,9},{9,8},{10,11... | collective-permute-start | bytes 245768 | tf_op jit(solution)/shard_map/ppermute | solution.py:346
  141.5 8.1 %collective-permute-start.24 = (bf16[2,128,160]{2,1,0:T(8,128)(2,1)S(1)}, bf16[2,128,160]{2,1,0:T(8,128)(2,1)S(1)}, u32[]{:S(2)}, u32[]{:S(2)}) collective-permute-start(bf16[2,128,160]{2,1,0:T(8,128)(2,1)S(1)} %get-tuple-element.109), channel_id=1, source_target_pairs={{0,4},{4,0},{1,5},{5,1},{2,6},{6,2},{3,7},{7,3},{8,12},{12,8},{9,1... | collective-permute-start | bytes 245768 | tf_op jit(solution)/shard_map/ppermute | solution.py:348
  142.8 6.8 %collective-permute-start.25 = (bf16[2,128,160]{2,1,0:T(8,128)(2,1)S(1)}, bf16[2,128,160]{2,1,0:T(8,128)(2,1)S(1)}, u32[]{:S(2)}, u32[]{:S(2)}) collective-permute-start(bf16[2,128,160]{2,1,0:T(8,128)(2,1)S(1)} %get-tuple-element.110), channel_id=1, source_target_pairs={{0,5},{1,4},{4,1},{5,0},{2,7},{3,6},{6,3},{7,2},{8,13},{9,12},{12,... | collective-permute-start | bytes 245768 | tf_op jit(solution)/shard_map/ppermute | solution.py:349
  143.7 17.3 %collective-permute-start.22 = (bf16[8,128,160]{2,1,0:T(8,128)(2,1)S(1)}, bf16[8,128,160]{2,1,0:T(8,128)(2,1)S(1)}, u32[]{:S(2)}, u32[]{:S(2)}) collective-permute-start(bf16[8,128,160]{2,1,0:T(8,128)(2,1)S(1)} %get-tuple-element.106.att_pack), channel_id=1, source_target_pairs={{0,2},{2,0},{1,3},{3,1},{4,6},{6,4},{5,7},{7,5},{8,10},{10,8},{9,1... | collective-permute-start | bytes 983048 | tf_op jit(solution)/shard_map/ppermute | solution.py:353
  143.8 17.3 %collective-permute-start.21 = (bf16[5,128,1280]{2,1,0:T(8,128)(2,1)}, bf16[5,128,1280]{2,1,0:T(8,128)(2,1)S(1)}, u32[]{:S(2)}, u32[]{:S(2)}) collective-permute-start(bf16[5,128,1280]{2,1,0:T(8,128)(2,1)} %get-tuple-element.105.pack_ref), channel_id=1, source_target_pairs={{0,2},{2,0},{1,3},{3,1},{4,6},{6,4},{5,7},{7,5},{8,10},{10,8},{9,1... | collective-permute-start | bytes 4915208 | tf_op jit(solution)/shard_map/ppermute | solution.py:353
  149.7 10.5 %collective-permute-start.29 = (bf16[4,8,1280]{2,1,0:T(8,128)(2,1)S(1)}, bf16[4,8,1280]{2,1,0:T(8,128)(2,1)S(1)}, u32[]{:S(2)}, u32[]{:S(2)}) collective-permute-start(bf16[4,8,1280]{2,1,0:T(8,128)(2,1)S(1)} %get-tuple-element.178), channel_id=1, source_target_pairs={{0,8},{8,16},{16,24},{24,0},{1,9},{9,17},{17,25},{25,1},{2,10},{10... | collective-permute-start | bytes 245768 | tf_op jit(solution)/shard_map/ppermute | solution.py:357
  150.0 5.6 %collective-permute-start.27 = (bf16[4,8,1280]{2,1,0:T(8,128)(2,1)S(1)}, bf16[4,8,1280]{2,1,0:T(8,128)(2,1)S(1)}, u32[]{:S(2)}, u32[]{:S(2)}) collective-permute-start(bf16[4,8,1280]{2,1,0:T(8,128)(2,1)S(1)} %get-tuple-element.179), channel_id=1, source_target_pairs={{0,24},{8,0},{16,8},{24,16},{1,25},{9,1},{17,9},{25,17},{2,26},{10... | collective-permute-start | bytes 245768 | tf_op jit(solution)/shard_map/ppermute | solution.py:357
  153.6 6.6 %collective-permute-start.28 = (bf16[4,8,1280]{2,1,0:T(8,128)(2,1)S(1)}, bf16[4,8,1280]{2,1,0:T(8,128)(2,1)S(1)}, u32[]{:S(2)}, u32[]{:S(2)}) collective-permute-start(bf16[4,8,1280]{2,1,0:T(8,128)(2,1)S(1)} %get-tuple-element.180), channel_id=1, source_target_pairs={{0,16},{8,24},{16,0},{24,8},{1,17},{9,25},{17,1},{25,9},{2,18},{10... | collective-permute-start | bytes 245768 | tf_op jit(solution)/shard_map/ppermute | solution.py:357
  155.6 12.3 %collective-permute-start.26 = (bf16[4,128,160]{2,1,0:T(8,128)(2,1)S(1)}, bf16[4,128,160]{2,1,0:T(8,128)(2,1)S(1)}, u32[]{:S(2)}, u32[]{:S(2)}) collective-permute-start(bf16[4,128,160]{2,1,0:T(8,128)(2,1)S(1)} %pad_maximum_fusion.10), channel_id=1, source_target_pairs={{0,2},{2,0},{1,3},{3,1},{4,6},{6,4},{5,7},{7,5},{8,10},{10,8},{9,1... | collective-permute-start | bytes 491528 | tf_op jit(solution)/shard_map/ppermute | solution.py:353
  173.5 28.8 %collective-permute-start.30 = (bf16[2,3,2,40,1280]{4,3,1,0,2:T(8,128)(2,1)}, bf16[2,3,2,40,1280]{4,3,1,0,2:T(8,128)(2,1)}, u32[]{:S(2)}, u32[]{:S(2)}) collective-permute-start(bf16[2,3,2,40,1280]{4,3,1,0,2:T(8,128)(2,1)} %select_bitcast_fusion.1), channel_id=1, source_target_pairs={{0,1},{1,0},{2,3},{3,2},{4,5},{5,4},{6,7},{7,6},{8,9},{9,8},{10,11... | collective-permute-start | bytes 3686408 | tf_op jit(solution)/shard_map/ppermute | solution.py:346
  175.7 28.5 %collective-permute-start.31 = (bf16[2,3,2,40,1280]{4,3,1,0,2:T(8,128)(2,1)}, bf16[2,3,2,40,1280]{4,3,1,0,2:T(8,128)(2,1)}, u32[]{:S(2)}, u32[]{:S(2)}) collective-permute-start(bf16[2,3,2,40,1280]{4,3,1,0,2:T(8,128)(2,1)} %select_bitcast_fusion), channel_id=1, source_target_pairs={{0,4},{4,0},{1,5},{5,1},{2,6},{6,2},{3,7},{7,3},{8,12},{12,8},{9,1... | collective-permute-start | bytes 3686408 | tf_op jit(solution)/shard_map/ppermute | solution.py:348
  191.6 14.6 %collective-permute-start.32 = (bf16[4,128,1280]{2,1,0:T(8,128)(2,1)}, bf16[4,128,1280]{2,1,0:T(8,128)(2,1)S(1)}, u32[]{:S(2)}, u32[]{:S(2)}) collective-permute-start(bf16[4,128,1280]{2,1,0:T(8,128)(2,1)} %copy-done.3), channel_id=1, source_target_pairs={{0,2},{2,0},{1,3},{3,1},{4,6},{6,4},{5,7},{7,5},{8,10},{10,8},{9,1... | collective-permute-start | bytes 3932168 | tf_op jit(solution)/shard_map/ppermute | solution.py:353
  191.7 10.7 %copy-start.13 = (bf16[2,3,2,1,40,1280]{5,4,3,2,1,0:T(8,128)(2,1)S(1)}, bf16[2,3,2,1,40,1280]{5,4,3,2,1,0:T(8,128)(2,1)}, u32[]{:S(2)}) copy-start(bf16[2,3,2,1,40,1280]{5,4,3,2,1,0:T(8,128)(2,1)} %copy-done.12) | copy-start | bytes 3686404
  193.3 9.0 %copy-start.11 = (bf16[2,3,2,1,40,1280]{5,4,3,2,1,0:T(8,128)(2,1)S(1)}, bf16[2,3,2,1,40,1280]{5,4,3,2,1,0:T(8,128)(2,1)}, u32[]{:S(2)}) copy-start(bf16[2,3,2,1,40,1280]{5,4,3,2,1,0:T(8,128)(2,1)} %copy-done.10) | copy-start | bytes 3686404
  193.4 20.0 %collective-permute-start.34 = (bf16[8,48,480]{2,1,0:T(8,128)(2,1)S(1)}, bf16[8,48,480]{2,1,0:T(8,128)(2,1)S(1)}, u32[]{:S(2)}, u32[]{:S(2)}) collective-permute-start(bf16[8,48,480]{2,1,0:T(8,128)(2,1)S(1)} %get-tuple-element.153), channel_id=1, source_target_pairs={{0,24},{8,0},{16,8},{24,16},{1,25},{9,1},{17,9},{25,17},{2,26},{10... | collective-permute-start | bytes 1105928 | tf_op jit(solution)/shard_map/ppermute | solution.py:357
  194.8 9.4 %copy-start.7 = (bf16[2,3,1,2,40,1280]{5,4,3,2,1,0:T(8,128)(2,1)S(1)}, bf16[2,3,1,2,40,1280]{5,4,3,2,1,0:T(8,128)(2,1)}, u32[]{:S(2)}) copy-start(bf16[2,3,1,2,40,1280]{5,4,3,2,1,0:T(8,128)(2,1)} %copy-done.6) | copy-start | bytes 3686404
  194.8 9.4 %copy-start.9 = (bf16[2,3,1,2,40,1280]{5,4,3,2,1,0:T(8,128)(2,1)S(1)}, bf16[2,3,1,2,40,1280]{5,4,3,2,1,0:T(8,128)(2,1)}, u32[]{:S(2)}) copy-start(bf16[2,3,1,2,40,1280]{5,4,3,2,1,0:T(8,128)(2,1)} %copy-done.8) | copy-start | bytes 3686404
  194.8 18.6 %collective-permute-start.33 = (bf16[8,48,480]{2,1,0:T(8,128)(2,1)S(1)}, bf16[8,48,480]{2,1,0:T(8,128)(2,1)S(1)}, u32[]{:S(2)}, u32[]{:S(2)}) collective-permute-start(bf16[8,48,480]{2,1,0:T(8,128)(2,1)S(1)} %get-tuple-element.154), channel_id=1, source_target_pairs={{0,8},{8,16},{16,24},{24,0},{1,9},{9,17},{17,25},{25,1},{2,10},{10... | collective-permute-start | bytes 1105928 | tf_op jit(solution)/shard_map/ppermute | solution.py:357
  204.1 10.9 %copy-start.4 = (bf16[2,3,2,40,1280]{4,3,1,0,2:T(8,128)(2,1)}, bf16[2,3,2,40,1280]{4,3,1,0,2:T(8,128)(2,1)S(1)}, u32[]{:S(2)}) copy-start(bf16[2,3,2,40,1280]{4,3,1,0,2:T(8,128)(2,1)S(1)} %fusion.2) | copy-start | bytes 3686404
  206.2 9.6 %copy-start.14 = (bf16[2,3,2,40,1280]{4,3,1,0,2:T(8,128)(2,1)}, bf16[2,3,2,40,1280]{4,3,1,0,2:T(8,128)(2,1)S(1)}, u32[]{:S(2)}) copy-start(bf16[2,3,2,40,1280]{4,3,1,0,2:T(8,128)(2,1)S(1)} %fusion.1) | copy-start | bytes 3686404
  206.6 12.4 %copy-start.16 = (bf16[4,128,1280]{2,1,0:T(8,128)(2,1)}, bf16[4,128,1280]{2,1,0:T(8,128)(2,1)S(1)}, u32[]{:S(2)}) copy-start(bf16[4,128,1280]{2,1,0:T(8,128)(2,1)S(1)} %add_convert_fusion) | copy-start | bytes 3932164
  213.4 19.9 %collective-permute-start.43 = (bf16[8,48,480]{2,1,0:T(8,128)(2,1)S(1)}, bf16[8,48,480]{2,1,0:T(8,128)(2,1)S(1)}, u32[]{:S(2)}, u32[]{:S(2)}) collective-permute-start(bf16[8,48,480]{2,1,0:T(8,128)(2,1)S(1)} %dynamic-slice_bitcast_fusion), channel_id=1, source_target_pairs={{0,16},{8,24},{16,0},{24,8},{1,17},{9,25},{17,1},{25,9},{2,18},{10... | collective-permute-start | bytes 1105928 | tf_op jit(solution)/shard_map/ppermute | solution.py:357
  216.9 22.3 %collective-permute-start.39 = (bf16[2,3,40,1280]{3,2,1,0:T(8,128)(2,1)}, bf16[2,3,40,1280]{3,2,1,0:T(8,128)(2,1)}, u32[]{:S(2)}, u32[]{:S(2)}) collective-permute-start(bf16[2,3,40,1280]{3,2,1,0:T(8,128)(2,1)} %select_bitcast_fusion.4), channel_id=1, source_target_pairs={{0,1},{1,0},{2,3},{3,2},{4,5},{5,4},{6,7},{7,6},{8,9},{9,8},{10,11... | collective-permute-start | bytes 1843208 | tf_op jit(solution)/shard_map/ppermute | solution.py:346
  217.9 24.1 %collective-permute-start.38 = (bf16[2,3,40,1280]{3,2,1,0:T(8,128)(2,1)}, bf16[2,3,40,1280]{3,2,1,0:T(8,128)(2,1)}, u32[]{:S(2)}, u32[]{:S(2)}) collective-permute-start(bf16[2,3,40,1280]{3,2,1,0:T(8,128)(2,1)} %select_bitcast_fusion.5), channel_id=1, source_target_pairs={{0,4},{4,0},{1,5},{5,1},{2,6},{6,2},{3,7},{7,3},{8,12},{12,8},{9,1... | collective-permute-start | bytes 1843208 | tf_op jit(solution)/shard_map/ppermute | solution.py:348
  220.0 23.5 %collective-permute-start.37 = (bf16[128,1280]{1,0:T(8,128)(2,1)}, bf16[128,1280]{1,0:T(8,128)(2,1)S(1)}, u32[]{:S(2)}, u32[]{:S(2)}) collective-permute-start(bf16[128,1280]{1,0:T(8,128)(2,1)} %get-tuple-element.158), channel_id=1, source_target_pairs={{0,5},{1,4},{4,1},{5,0},{2,7},{3,6},{6,3},{7,2},{8,13},{9,12},{12,... | collective-permute-start | bytes 983048 | tf_op jit(solution)/shard_map/ppermute | solution.py:349
  221.3 27.6 %collective-permute-start.36 = (bf16[128,1280]{1,0:T(8,128)(2,1)}, bf16[128,1280]{1,0:T(8,128)(2,1)S(1)}, u32[]{:S(2)}, u32[]{:S(2)}) collective-permute-start(bf16[128,1280]{1,0:T(8,128)(2,1)} %get-tuple-element.159), channel_id=1, source_target_pairs={{0,4},{4,0},{1,5},{5,1},{2,6},{6,2},{3,7},{7,3},{8,12},{12,8},{9,1... | collective-permute-start | bytes 983048 | tf_op jit(solution)/shard_map/ppermute | solution.py:348
  233.4 15.6 %collective-permute-start.35 = (bf16[128,1280]{1,0:T(8,128)(2,1)}, bf16[128,1280]{1,0:T(8,128)(2,1)}, u32[]{:S(2)}, u32[]{:S(2)}) collective-permute-start(bf16[128,1280]{1,0:T(8,128)(2,1)} %get-tuple-element.160), channel_id=1, source_target_pairs={{0,1},{1,0},{2,3},{3,2},{4,5},{5,4},{6,7},{7,6},{8,9},{9,8},{10,11... | collective-permute-start | bytes 983048 | tf_op jit(solution)/shard_map/ppermute | solution.py:346
  235.7 25.9 %all-to-all-start.2 = ((bf16[8,48,480]{2,1,0:T(8,128)(2,1)}), bf16[8,48,480]{2,1,0:T(8,128)(2,1)S(1)}, u32[]{:S(2)}, u32[]{:S(2)}) async-start(bf16[8,48,480]{2,1,0:T(8,128)(2,1)} %fusion.8), calls=%async_computation.2 | async-start | bytes 786432 | tf_op jit(solution)/shard_map/all_to_all | solution.py:808
  251.6 9.4 %copy-start.19 = (bf16[128,1280]{1,0:T(8,128)(2,1)}, bf16[128,1280]{1,0:T(8,128)(2,1)S(1)}, u32[]{:S(2)}) copy-start(bf16[128,1280]{1,0:T(8,128)(2,1)S(1)} %add_convert_fusion.1) | copy-start | bytes 983044
  252.4 18.7 %collective-permute-start.42 = (bf16[4,8,1280]{2,1,0:T(8,128)(2,1)}, bf16[4,8,1280]{2,1,0:T(8,128)(2,1)}, u32[]{:S(2)}, u32[]{:S(2)}) collective-permute-start(bf16[4,8,1280]{2,1,0:T(8,128)(2,1)} %get-tuple-element.175), channel_id=1, source_target_pairs={{0,8},{8,16},{16,24},{24,0},{1,9},{9,17},{17,25},{25,1},{2,10},{10... | collective-permute-start | bytes 245768 | tf_op jit(solution)/shard_map/ppermute | solution.py:357
  253.5 14.7 %collective-permute-start.40 = (bf16[4,8,1280]{2,1,0:T(8,128)(2,1)}, bf16[4,8,1280]{2,1,0:T(8,128)(2,1)}, u32[]{:S(2)}, u32[]{:S(2)}) collective-permute-start(bf16[4,8,1280]{2,1,0:T(8,128)(2,1)} %get-tuple-element.176), channel_id=1, source_target_pairs={{0,24},{8,0},{16,8},{24,16},{1,25},{9,1},{17,9},{25,17},{2,26},{10... | collective-permute-start | bytes 245768 | tf_op jit(solution)/shard_map/ppermute | solution.py:357
  256.2 13.9 %collective-permute-start.41 = (bf16[4,8,1280]{2,1,0:T(8,128)(2,1)}, bf16[4,8,1280]{2,1,0:T(8,128)(2,1)}, u32[]{:S(2)}, u32[]{:S(2)}) collective-permute-start(bf16[4,8,1280]{2,1,0:T(8,128)(2,1)} %get-tuple-element.177), channel_id=1, source_target_pairs={{0,16},{8,24},{16,0},{24,8},{1,17},{9,25},{17,1},{25,9},{2,18},{10... | collective-permute-start | bytes 245768 | tf_op jit(solution)/shard_map/ppermute | solution.py:357
  257.2 18.2 %collective-permute-start.44 = (bf16[3,40,1280]{2,1,0:T(8,128)(2,1)}, bf16[3,40,1280]{2,1,0:T(8,128)(2,1)}, u32[]{:S(2)}, u32[]{:S(2)}) collective-permute-start(bf16[3,40,1280]{2,1,0:T(8,128)(2,1)} %get-tuple-element.161), channel_id=1, source_target_pairs={{0,8},{8,16},{16,24},{24,0},{1,9},{9,17},{17,25},{25,1},{2,10},{10... | collective-permute-start | bytes 921608 | tf_op jit(solution)/shard_map/ppermute | solution.py:357
  258.8 16.6 %collective-permute-start.46 = (bf16[3,40,1280]{2,1,0:T(8,128)(2,1)}, bf16[3,40,1280]{2,1,0:T(8,128)(2,1)}, u32[]{:S(2)}, u32[]{:S(2)}) collective-permute-start(bf16[3,40,1280]{2,1,0:T(8,128)(2,1)} %get-tuple-element.162), channel_id=1, source_target_pairs={{0,24},{8,0},{16,8},{24,16},{1,25},{9,1},{17,9},{25,17},{2,26},{10... | collective-permute-start | bytes 921608 | tf_op jit(solution)/shard_map/ppermute | solution.py:357
  268.2 19.4 %collective-permute-start.45 = (bf16[3,40,1280]{2,1,0:T(8,128)(2,1)S(1)}, bf16[3,40,1280]{2,1,0:T(8,128)(2,1)S(1)}, u32[]{:S(2)}, u32[]{:S(2)}) collective-permute-start(bf16[3,40,1280]{2,1,0:T(8,128)(2,1)S(1)} %copy-done.27), channel_id=1, source_target_pairs={{0,16},{8,24},{16,0},{24,8},{1,17},{9,25},{17,1},{25,9},{2,18},{10... | collective-permute-start | bytes 921608 | tf_op jit(solution)/shard_map/ppermute | solution.py:357
  (26 other events, 106.9 us)
Sparse Core Ops, SparseCore 0:
  10.3 34.8 all-gather.1

commit v4 on v3

--- a/solution.py
+++ b/solution.py
@@ -361,10 +361,15 @@
     return lax.dynamic_index_in_dim(array, index, 0, keepdims=False)
 
 
-def by_source(pieces, z_index):
-    own, one, two, three = pieces
-    line = jnp.stack([three, two, one, own, three, two, one])
-    return lax.dynamic_slice_in_dim(line, 3 - z_index, 4, 0)
+def by_source(pieces, z_index, axis):
+    pieces = [jnp.expand_dims(item, axis) for item in pieces]
+    shape = [1] * pieces[0].ndim
+    shape[axis] = 4
+    hop = ((z_index - jnp.arange(4, dtype=jnp.int32)) % 4).reshape(shape)
+    made = pieces[0]
+    for k in (1, 2, 3):
+        made = jnp.where(hop == k, pieces[k], made)
+    return made
 
 
 def pair(mine, other, index, axis):
@@ -372,19 +377,17 @@
     return jnp.stack([jnp.where(first, mine, other), jnp.where(first, other, mine)], axis=axis)
 
 
-def row_positions(shape, dim, z_index, plane_index):
+def row_positions(shape, dim, plane_index):
     row = lax.broadcasted_iota(jnp.int32, shape, dim)
     chip = (row // 32) % 4
     code = (chip % 2) + 4 * (chip // 2) + 2 * (row // 128)
-    hop = (row % 32) // 8
-    return 64 * ((z_index - hop) & 3) + 8 * (plane_index ^ code) + row % 8
+    return 64 * ((row % 32) // 8) + 8 * (plane_index ^ code) + row % 8
 
 
 def live_pairs(info_ref, seq):
-    z_index, plane_index = info_ref[0], info_ref[1]
     shape = (256, 256)
-    query_pos = row_positions(shape, 0, z_index, plane_index)
-    key_pos = row_positions(shape, 1, z_index, plane_index)
+    query_pos = row_positions(shape, 0, info_ref[1])
+    key_pos = row_positions(shape, 1, info_ref[1])
     return (key_pos <= query_pos) & (key_pos < info_ref[2 + seq])
 
 
@@ -400,7 +403,9 @@
     return weights / jnp.sum(weights, axis=1, keepdims=True)
 
 
-def attend_kernel(info_ref, near_ref, far_ref, gain_ref, mult_ref, w_ref, pre_ref, att_near, att_far):
+def attend_kernel(
+    info_ref, near_ref, far_ref, gain_ref, mult_ref, w_ref, pre_ref, att_near, att_far
+):
     seq = pl.program_id(0)
     live = live_pairs(info_ref, seq)
     wide = block_rows(near_ref, far_ref).astype(jnp.float32)
@@ -608,8 +613,9 @@
     in_four = inputs.reshape(4, 4, 8, width)
     sent = [jnp.concatenate([pick(in_four, (z + k) % 4), vec_block]) for k in range(4)]
     got = [sent[0]] + [ring_shift(sent[k], k) for k in (1, 2, 3)]
-    x_rows = jnp.stack([item[:4] for item in got], axis=1).reshape(128, width)
-    vec_rows = jnp.concatenate([item[4, :1] for item in got] + [jnp.zeros((4, width), bf16)])
+    x_rows = by_source([item[:4] for item in got], z, 1).reshape(128, width)
+    vec_rows = by_source([item[4, 0] for item in got], z, 0)
+    vec_rows = jnp.concatenate([vec_rows, jnp.zeros((4, width), bf16)])
     own = jnp.concatenate([x_rows, vec_rows])
 
     big = jnp.stack([w_output, w_up, w_down]).astype(bf16)
@@ -622,31 +628,22 @@
     qkv = lax.all_to_all(qkv, ("y", "core", "x"), split_axis=0, concat_axis=0, tiled=True)
     qkv = qkv.reshape(320, 480)
 
-    late = qkv
     big, near, qkv = lax.optimization_barrier((big, near, qkv))
-    one, three = ring_shift(qkv, 1), ring_shift(qkv, 3)
+    w_qkv = lax.all_gather(qkv, "z", axis=0, tiled=True)
     far = core_swap(near)
     part_a, part_b = big[:2], big[2:]
     near_a = pair(part_a, plane_shift(part_a, 1), x, 2).reshape(2, 3, 80, width)
     part_b = pair(part_b, plane_shift(part_b, 2), y, 2)
-    near_a, part_b, cotangent, late, one, three = lax.optimization_barrier(
-        (near_a, part_b, cotangent, late, one, three)
-    )
-    w_qkv = by_source([qkv, one, ring_shift(late, 2), three], z).reshape(width, 480)
+    near_a, part_b, far = lax.optimization_barrier((near_a, part_b, far))
     across_a = plane_shift(near_a, 2)
     across_b = plane_shift(part_b, 1)
-    cot_four = lax.all_to_all(cotangent.reshape(4, 4, 8, width), "z", split_axis=0, concat_axis=0, tiled=True)
-    cot_rows = jnp.stack([pick(cot_four, (z - k) % 4) for k in range(4)], axis=1).reshape(128, width)
 
     vecs = jnp.stack([near[:, 128:132, :120], far[:, 128:132, :120]])
     vecs = vecs.astype(f32).reshape(2, 2, 2, 4, 120)
     vecs = jnp.where(c == 0, vecs, vecs[::-1])
     vecs = jnp.where(y == 0, vecs, vecs[:, ::-1])
     vecs = jnp.where(x == 0, vecs, vecs[:, :, ::-1])
-    fours = jnp.arange(4, dtype=jnp.int32)
-    from_hop = (z - fours[:, None]) % 4 == fours[None, :]
-    vecs = jnp.sum(jnp.where(from_hop[:, None, None, None, :, None], vecs[None], 0.0), axis=4)
-    vecs = vecs.reshape(4, 2, 2, 2, 3, 40).transpose(4, 0, 2, 1, 3, 5).reshape(3, width)
+    vecs = vecs.reshape(2, 2, 2, 4, 3, 40).transpose(4, 3, 1, 0, 2, 5).reshape(3, width)
     gain_one, gain_two = vecs[0:1], vecs[1:2]
     my_scale = lax.dynamic_slice_in_dim(vecs[2:3], 160 * plane, 160, 1)
     query_mult = LOG2E / math.sqrt(HD) * jax.nn.softplus(my_scale)
@@ -673,11 +670,16 @@
         name="attend",
     )(info, near, far, gain_one, query_mult, w_qkv)
 
-    att_near, att_far, cot_rows, near_a = lax.optimization_barrier((att_near, att_far, cot_rows, near_a))
+    att_near, att_far, near_a = lax.optimization_barrier((att_near, att_far, near_a))
     far_near_a = core_swap(near_a)
     att_pair = jnp.stack([att_near, core_swap(att_far)], axis=1)
+    att_pair, cotangent = lax.optimization_barrier((att_pair, cotangent))
+    cot_rows = lax.all_to_all(cotangent.reshape(4, 4, 8, width), "z", split_axis=0, concat_axis=0, tiled=True)
+    cot_rows = cot_rows.transpose(1, 0, 2, 3).reshape(128, width)
     atts = [att_pair[0]] + [plane_shift(att_pair[step], step) for step in (1, 2, 3)]
-    *atts, far_near_a, across_a, across_b = lax.optimization_barrier((*atts, far_near_a, across_a, across_b))
+    *atts, far_near_a, across_a, across_b, cot_rows = lax.optimization_barrier(
+        (*atts, far_near_a, across_a, across_b, cot_rows)
+    )
     far_across_a = core_swap(across_a)
     all_b = pair(part_b, across_b, x, 3).reshape(2, 3, 2, 80, width)
     far_b = core_swap(all_b)
@@ -706,13 +708,10 @@
     )(info, x_rows, cot_rows, *atts, gain_two, near_a, across_a, all_b, far_near_a, far_across_a, far_b)
 
     def home(rows):
-        rows = rows.reshape(4, 4, 8, width)
-        parts = [rows[:, 0]] + [ring_shift(rows[:, k], -k) for k in (1, 2, 3)]
-        line = jnp.stack(parts + parts[:3])
-        return lax.dynamic_slice_in_dim(line, (4 - z) % 4, 4, 0).reshape(16, 8, width)
+        rows = rows.reshape(4, 4, 8, width).transpose(1, 0, 2, 3)
+        return lax.all_to_all(rows, "z", split_axis=0, concat_axis=0, tiled=True).reshape(16, 8, width)
 
     back = [datts[0]] + [plane_shift(datts[step], step) for step in (1, 2, 3)]
-    *back, out_rows = lax.optimization_barrier((*back, out_rows))
     outputs = home(out_rows)
     grad_att_near = jnp.stack([item[0] for item in back])
     grad_att_far = core_swap(jnp.stack([item[1] for item in back]))
@@ -743,13 +742,6 @@
     kept_b, away_b = halves(kept[2:], y, 2)
     kept_a = added(kept_a, plane_shift(away_a, 1))
     kept_b = added(kept_b, plane_shift(away_b, 2))
-    def ring_sum(array):
-        total = pick(array, z).astype(f32)
-        for k in (1, 2, 3):
-            total += ring_shift(pick(array, (z + k) % 4), k).astype(f32)
-        return total
-
-
     hid_near, hid_far, qkv_grad, gain_one_grad, scale_grad = pl.pallas_call(
         attend_back_kernel,
         grid_spec=pltpu.PrefetchScalarGridSpec(
@@ -782,38 +774,45 @@
 
     scale_line = lax.dynamic_update_slice(jnp.zeros((1, width), f32), scale_grad, (0, 160 * plane))
     lines = jnp.concatenate([gain_one_grad, gain_two_grad, scale_line])
-    lines = lines.reshape(3, 4, 8, 40).transpose(1, 2, 0, 3).reshape(4, 8, 1, 120).astype(bf16)
-    lines = jnp.pad(lines, ((0, 0), (0, 0), (0, 7), (0, 360)))
-    send = jnp.concatenate([qkv_grad.reshape(4, 8, 40, 480), lines], axis=2)
-    one, three = (ring_shift(pick(send, (z + k) % 4), k) for k in (1, 3))
+    lines = lines.reshape(3, 4, 8, 40).transpose(1, 2, 0, 3).reshape(4, 2, 480).astype(bf16)
+    lines = jnp.pad(lines, ((0, 0), (0, 6), (0, 0)))
+    send = jnp.concatenate([qkv_grad.reshape(4, 320, 480), lines], axis=1)
+    one = ring_shift(pick(send, (z + 1) % 4), 1)
     hid = added(hid_near, core_swap(hid_far))
-    later = send
-    kept_a, kept_b, hid, one, three, later = lax.optimization_barrier((kept_a, kept_b, hid, one, three, later))
+    kept_a, kept_b, hid_sum, one, later = lax.optimization_barrier((kept_a, kept_b, hid, one, send))
+    three = ring_shift(pick(later, (z + 3) % 4), 3)
+    two = ring_shift(pick(later, (z + 2) % 4), 2)
     kept_a, away_a = halves(kept_a, y, 2)
     kept_b, away_b = halves(kept_b, x, 2)
     kept_a = added(kept_a, plane_shift(away_a, 2))
     kept_b = added(kept_b, plane_shift(away_b, 1))
     kept = jnp.concatenate([kept_a, kept_b])
-    two = ring_shift(pick(later, (z + 2) % 4), 2)
+    hid, kept = lax.optimization_barrier((hid, kept))
     grad_hid = hid[0].astype(f32)
     moved = [plane_shift(hid[step], step) for step in (1, 2, 3)]
-    *moved, kept = lax.optimization_barrier((*moved, kept))
+    *moved, three, two = lax.optimization_barrier((*moved, three, two))
+    sums = sum((item.astype(f32) for item in (one, two, three)), pick(send, z).astype(f32)).astype(bf16)
+    lines = jnp.pad(sums[320:322].reshape(8, 1, 120), ((0, 0), (0, 7), (0, 360)))
+    sums = jnp.concatenate([sums[:320].reshape(8, 40, 480), lines], axis=1)
     for item in moved:
         grad_hid += item.astype(f32)
     wide = x_rows.astype(f32)
     inverse = lax.rsqrt(jnp.mean(wide * wide, axis=1, keepdims=True) + 1e-06)
     grad_in = (grad_mid + norm_back(grad_hid, wide * inverse, inverse, gain_one)).astype(bf16)
 
-    sums = sum((item.astype(f32) for item in (one, two, three)), pick(send, z).astype(f32)).astype(bf16)
     sums = lax.all_to_all(sums, ("y", "core", "x"), split_axis=0, concat_axis=0, tiled=True)
-    big_sums = ring_sum(kept)
+    big_sums = lax.psum_scatter(kept, "z", scatter_dimension=0, tiled=True)[0].astype(f32)
     qkv_sums = sums[:, :40].reshape(8, 40, 3, 160).transpose(2, 1, 0, 3).reshape(3, 40, width).astype(f32)
     line_sums = jnp.sum(sums[:, 40, :120].astype(f32), axis=0).reshape(3, 40)
     scale_low = query_scale.astype(bf16).astype(f32)
     scale_sum = LOG2E / math.sqrt(HD) * jax.nn.sigmoid(scale_low) * line_sums[2]
 
+    rows = grad_in.reshape(4, 4, 8, width).transpose(1, 0, 2, 3)
+    grad_home = [pick(rows, z)] + [ring_shift(pick(rows, (z + k) % 4), k) for k in (1, 2, 3)]
+    grad_home = by_source(grad_home, z, 0).reshape(16, 8, width)
+
     return (
-        outputs, home(grad_in), qkv_sums[0], qkv_sums[1], qkv_sums[2],
+        outputs, grad_home, qkv_sums[0], qkv_sums[1], qkv_sums[2],
         big_sums[0], big_sums[1], big_sums[2], line_sums[0], line_sums[1], scale_sum,
     )
 

time: 298 us -> 272 us (0.913)
  waiting for transfers between devices: 113 us -> 97.1 us
  starting transfers between devices: 68.2 us -> 61.3 us
  local copies, waits for them, and re-layouts: 34.9 us -> 31.5 us
    ppermute x18 -> x9, waiting for transfers between devices: 52.7 us -> 18.2 us  [ring_shift(): return lax.ppermute(value, 'z', [(i, (i + step) % 4) for i in range(4)])]
    all_gather x0 -> x1, waiting for transfers between devices: none -> 13.7 us  [planes(): w_qkv = lax.all_gather(qkv, 'z', axis=0, tiled=True)]
    ppermute x18 -> x9, starting transfers between devices: 29.5 us -> 17.5 us  [ring_shift(): return lax.ppermute(value, 'z', [(i, (i + step) % 4) for i in range(4)])]
    ppermute x8, waiting for transfers between devices: 29.5 us -> 23.1 us  [plane_shift(): return lax.ppermute(value, 'y', [(0, 1), (1, 0)])]
    ppermute x4, waiting for transfers between devices: 7.04 us -> 12.8 us  [plane_shift(): return lax.ppermute(value, ('y', 'x'), [(0, 3), (1, 2), (2, 1), (3, 0)])]
    ppermute x8, waiting for transfers between devices: 10.9 us -> 16.6 us  [plane_shift(): return lax.ppermute(value, 'x', [(0, 1), (1, 0)])]
    all_to_all x0 -> x1, starting transfers between devices: none -> 4.58 us  [home(): lax.all_to_all(rows, 'z', split_axis=0, concat_axis=0, tiled=True)]
    unnamed x96 -> x69, local copies, waits for them, and re-layouts: 10.7 us -> 8.2 us
  transfers between devices with their start and end apart: 51 -> 45, of which waited for: 26 -> 25; matrix products, arithmetic and copies ran while one was open for 15% -> 14% of each run, Pallas kernels for 9% -> 10%
where the time goes in v4:
time: 272 us; the launch traced here: 271 us
  waiting for transfers between devices  97.1 us (36%)
  starting transfers between devices  61.3 us (23%)
  Pallas kernels  36.7 us (13%)
  local copies, waits for them, and re-layouts  31.5 us (12%)
  other arithmetic  29.7 us (11%)
  between operations  14.6 us (5%)
    ppermute x8, waiting for transfers between devices, plane_shift(): return lax.ppermute(value, 'y', [(0, 1), (1, 0)])  23.1 us
    ppermute x9, waiting for transfers between devices, ring_shift(): return lax.ppermute(value, 'z', [(i, (i + step) % 4) for i in range(4)])  18.2 us
    ppermute x9, starting transfers between devices, ring_shift(): return lax.ppermute(value, 'z', [(i, (i + step) % 4) for i in range(4)])  17.5 us
    ppermute x8, waiting for transfers between devices, plane_shift(): return lax.ppermute(value, 'x', [(0, 1), (1, 0)])  16.6 us
    all_gather x1, waiting for transfers between devices, planes(): w_qkv = lax.all_gather(qkv, 'z', axis=0, tiled=True)  13.7 us
    pallas_call x1, Pallas kernels, planes(): pl.pallas_call(attend_back_kernel, grid_spec=pltpu.PrefetchScalarGridSpec...  13.4 us
    ppermute x4, waiting for transfers between devices, plane_shift(): return lax.ppermute(value, ('y', 'x'), [(0, 3), (1, 2), (2, 1), (3, 0)])  12.8 us
    ppermute x8, starting transfers between devices, plane_shift(): return lax.ppermute(value, 'x', [(0, 1), (1, 0)])  9.68 us
  transfers between devices with their start and end apart: 45, of which 25 were waited for; matrix products, arithmetic and copies ran while one was open for 14% of the time, Pallas kernels for 10%

profile of v4, /device:TPU:0, one launch (start us, length us, event | category | flops | bytes accessed | tf_op | source)
XLA Modules:
  0.0 271.0 jit_solution(8703994437554132106)
XLA Ops:
  10.4 5.1 %collective-permute-start = (bf16[5,8,1280]{2,1,0:T(8,128)(2,1)S(1)}, bf16[5,8,1280]{2,1,0:T(8,128)(2,1)S(1)}, u32[]{:S(2)}, u32[]{:S(2)}) collective-permute-start(bf16[5,8,1280]{2,1,0:T(8,128)(2,1)S(1)} %get-tuple-element.179), channel_id=1, source_target_pairs={{0,24},{8,0},{16,8},{24,16},{1,25},{9,1},{17,9},{25,17},{2,26},{10... | collective-permute-start | bytes 307208 | tf_op jit(solution)/shard_map/ppermute | solution.py:357
  17.3 1.5 collective-permute-done
  18.8 6.2 %collective-permute-done.1 = bf16[5,8,1280]{2,1,0:T(8,128)(2,1)S(1)} collective-permute-done((bf16[5,8,1280]{2,1,0:T(8,128)(2,1)S(1)}, bf16[5,8,1280]{2,1,0:T(8,128)(2,1)S(1)}, u32[]{:S(2)}, u32[]{:S(2)}) %collective-permute-start.1) | collective-permute-done | bytes 102432 | tf_op jit(solution)/shard_map/ppermute | solution.py:357
  25.5 3.3 %collective-permute-start.5 = (bf16[136,1280]{1,0:T(8,128)(2,1)S(1)}, bf16[136,1280]{1,0:T(8,128)(2,1)S(1)}, u32[]{:S(2)}, u32[]{:S(2)}) collective-permute-start(bf16[136,1280]{1,0:T(8,128)(2,1)S(1)} %maximum_maximum_fusion), channel_id=1, source_target_pairs={{0,5},{1,4},{4,1},{5,0},{2,7},{3,6},{6,3},{7,2},{8,13},{9,12},{12,... | collective-permute-start | bytes 1044488 | tf_op jit(solution)/shard_map/ppermute | solution.py:349
  31.6 4.1 %all-to-all-start = ((bf16[8,40,480]{2,1,0:T(8,128)(2,1)}), bf16[8,40,480]{2,1,0:T(8,128)(2,1)S(1)}, u32[]{:S(2)}, u32[]{:S(2)}) async-start(bf16[8,40,480]{2,1,0:T(8,128)(2,1)} %reshape.404), calls=%async_computation | async-start | bytes 655360 | tf_op jit(solution)/shard_map/all_to_all | solution.py:628
  35.8 2.2 collective-permute-done.5
  38.0 5.8 %collective-permute-done.4 = bf16[136,1280]{1,0:T(8,128)(2,1)S(1)} collective-permute-done((bf16[136,1280]{1,0:T(8,128)(2,1)S(1)}, bf16[136,1280]{1,0:T(8,128)(2,1)S(1)}, u32[]{:S(2)}, u32[]{:S(2)}) %collective-permute-start.4) | collective-permute-done | bytes 348192 | tf_op jit(solution)/shard_map/ppermute | solution.py:348
  43.8 1.2 collective-permute-done.3
  45.0 1.4 pad_maximum_fusion.1.near_ref
  46.6 2.6 fusion.34
  49.2 1.2 collective-permute-start.7
  50.4 1.6 collective-permute-start.6
  52.3 12.6 %collective-permute-done.7 = bf16[2,3,40,1280]{3,2,1,0:T(8,128)(2,1)S(1)} collective-permute-done((bf16[2,3,40,1280]{3,2,1,0:T(8,128)(2,1)}, bf16[2,3,40,1280]{3,2,1,0:T(8,128)(2,1)S(1)}, u32[]{:S(2)}, u32[]{:S(2)}) %collective-permute-start.7) | collective-permute-done | bytes 614432 | tf_op jit(solution)/shard_map/ppermute | solution.py:348
  66.0 1.6 select_bitcast_fusion.7
  67.7 1.2 copy.84
  71.9 1.4 collective-permute-start.15
  73.4 13.7 %all-gather.5.cloned.1.call-done.w_ref = bf16[1280,480]{1,0:T(8,128)(2,1)} async-done(((bf16[320,480]{1,0:T(8,128)(2,1)}), bf16[1280,480]{1,0:T(8,128)(2,1)}) %all-gather.5.cloned.1.call-update) | async-done | bytes 1228816 | tf_op jit(solution)/shard_map/all_gather | solution.py:632
  87.1 1.3 copy-done.2
  88.4 8.2 %attend.1 = (f32[2,4,128,480]{3,2,1,0:T(8,128)}, bf16[4,128,160]{2,1,0:T(8,128)(2,1)S(1)}, bf16[4,128,160]{2,1,0:T(8,128)(2,1)S(1)}) custom-call(s32[6]{0:T(128)S(1)} %pad_add_fusion.info_ref, bf16[4,136,1280]{2,1,0:T(8,128)(2,1)S(1)} %pad_maximum_fusion.1.near_ref, bf16[4,136,1280]{2,1,0:T(8,128)(2,1)} %collective-permute-done.8.far_ref, ...), custom_call_target="tpu_custom_call" | custom-call | flops 8999999488 | bytes 8000000 | tf_op jit(solution)/shard_map/attend/pallas_call | solution.py:652
  97.2 2.4 collective-permute-done.9
  99.7 3.6 %all-to-all-start.1 = ((bf16[4,4,8,1280]{3,2,1,0:T(8,128)(2,1)}), bf16[4,4,8,1280]{3,2,1,0:T(8,128)(2,1)S(1)}, u32[]{:S(2)}, u32[]{:S(2)}) async-start(bf16[4,4,8,1280]{3,2,1,0:T(8,128)(2,1)} %bitcast.40), calls=%async_computation.1 | async-start | bytes 655360 | tf_op jit(solution)/shard_map/all_to_all | solution.py:677
  103.4 2.5 collective-permute-start.12
  106.4 3.8 %collective-permute-done.12.att_3 = bf16[2,128,160]{2,1,0:T(8,128)(2,1)S(1)} collective-permute-done((bf16[2,128,160]{2,1,0:T(8,128)(2,1)S(1)}, bf16[2,128,160]{2,1,0:T(8,128)(2,1)S(1)}, u32[]{:S(2)}, u32[]{:S(2)}) %collective-permute-start.12) | collective-permute-done | bytes 81952 | tf_op jit(solution)/shard_map/ppermute | solution.py:349
  110.2 1.5 collective-permute-start.10
  111.7 2.5 all-to-all-done.1
  115.2 1.8 select_bitcast_fusion.3
  117.2 1.6 copy.89
  119.5 6.2 %collective-permute-done.16.far_across_a = bf16[2,3,80,1280]{3,2,1,0:T(8,128)(2,1)} collective-permute-done((bf16[2,3,80,1280]{3,2,1,0:T(8,128)(2,1)}, bf16[2,3,80,1280]{3,2,1,0:T(8,128)(2,1)}, u32[]{:S(2)}, u32[]{:S(2)}) %collective-permute-start.16) | collective-permute-done | bytes 1228832 | tf_op jit(solution)/shard_map/ppermute | solution.py:353
  125.6 9.5 %feed.1 = (bf16[128,1280]{1,0:T(8,128)(2,1)S(1)}, bf16[5,128,1280]{2,1,0:T(8,128)(2,1)}, bf16[8,128,160]{2,1,0:T(8,128)(2,1)S(1)}, f32[128,1280]{1,0:T(8,128)S(1...) custom-call(s32[6]{0:T(128)S(1)} %pad_add_fusion.info_ref, ...), custom_call_target="tpu_custom_call" | custom-call | flops 12000000000 | bytes 13000000 | tf_op jit(solution)/shard_map/feed/pallas_call | solution.py:692
  135.4 1.5 collective-permute-start.20
  136.9 1.5 collective-permute-start.21
  139.7 4.6 %all-to-all-start.2 = ((bf16[4,4,8,1280]{3,2,1,0:T(8,128)(2,1)}), bf16[4,4,8,1280]{3,2,1,0:T(8,128)(2,1)}, u32[]{:S(2)}, u32[]{:S(2)}) async-start(bf16[4,4,8,1280]{3,2,1,0:T(8,128)(2,1)} %bitcast.165), calls=%async_computation.2 | async-start | bytes 655360 | tf_op jit(solution)/shard_map/all_to_all | solution.py:712
  146.2 1.4 copy-done.1
  147.7 5.6 %grads.1 = bf16[4,3,2,80,1280]{4,3,2,1,0:T(8,128)(2,1)} custom-call(s32[6]{0:T(128)S(1)} %pad_add_fusion.info_ref, bf16[5,128,1280]{2,1,0:T(8,128)(2,1)S(1)} %copy-done.1, bf16[8,128,160]{2,1,0:T(8,128)(2,1)S(1)} %get-tuple-element.100.att_pack, bf16[5,128,1280]{2,1,0:T(8,128)(2,1)} %collective-permute-done.18.far_pack, ...), custom_call_target="tpu_custom_call" | custom-call | flops 6000000000 | bytes 8000000 | tf_op jit(solution)/shard_map/grads/pallas_call | solution.py:719
  154.4 2.8 %fusion.30 = (bf16[2,3,2,80,1280]{4,3,2,1,0:T(8,128)(2,1)S(1)}, bf16[2,3,2,80,1280]{4,3,2,1,0:T(8,128)(2,1)S(1)}) fusion(bf16[4,3,2,80,1280]{4,3,2,1,0:T(8,128)(2,1)} %grads.1), kind=kLoop, calls=%fused_computation.130 | loop fusion | bytes 9830400 | tf_op jit(solution)/shard_map/slice | solution.py:742
  158.8 1.2 select_bitcast_fusion.1
  160.0 1.5 collective-permute-start.25
  161.4 1.2 select_bitcast_fusion
  162.6 1.5 collective-permute-start.26
  164.1 13.4 %attend_back.1 = (bf16[4,128,1280]{2,1,0:T(8,128)(2,1)S(1)}, bf16[4,128,1280]{2,1,0:T(8,128)(2,1)S(1)}, bf16[1280,480]{1,0:T(8,128)(2,1)}, f32[1,1280]{1,0:T(1,128)S(1)}, f32[1,160]{1,0:T(1,128)S(1)}) custom-call(s32[6]{0:T(128)S(1)} %pad_add_fusion.info_ref, bf16[4,136,1280]{2,1,0:T(8,128)(2,1)} %copy-done, ...), custom_call_target="tpu_custom_call" | custom-call | flops 15000000512 | bytes 12000000 | tf_op jit(solution)/shard_map/attend_back/pallas_call | solution.py:745
  179.1 1.7 fusion.3
  181.8 6.4 %collective-permute-done.25 = bf16[2,3,2,40,1280]{4,3,1,0,2:T(8,128)(2,1)} collective-permute-done((bf16[2,3,2,40,1280]{4,3,1,0,2:T(8,128)(2,1)}, bf16[2,3,2,40,1280]{4,3,1,0,2:T(8,128)(2,1)}, u32[]{:S(2)}, u32[]{:S(2)}) %collective-permute-start.25) | collective-permute-done | bytes 1228832 | tf_op jit(solution)/shard_map/ppermute | solution.py:346
  188.2 1.7 fusion.2
  190.6 1.7 fusion.1
  192.3 1.4 add_convert_fusion
  195.5 1.5 collective-permute-start.28
  198.0 2.9 %collective-permute-start.34 = (bf16[328,480]{1,0:T(8,128)(2,1)}, bf16[328,480]{1,0:T(8,128)(2,1)}, u32[]{:S(2)}, u32[]{:S(2)}) collective-permute-start(bf16[328,480]{1,0:T(8,128)(2,1)} %get-tuple-element.141), channel_id=1, source_target_pairs={{0,16},{8,24},{16,0},{24,8},{1,17},{9,25},{17,1},{25,9},{2,18},{10... | collective-permute-start | bytes 944648 | tf_op jit(solution)/shard_map/ppermute | solution.py:357
  200.9 1.5 collective-permute-start.33
  202.3 6.9 %collective-permute-done.29 = bf16[2,3,40,1280]{3,2,1,0:T(8,128)(2,1)S(1)} collective-permute-done((bf16[2,3,40,1280]{3,2,1,0:T(8,128)(2,1)S(1)}, bf16[2,3,40,1280]{3,2,1,0:T(8,128)(2,1)S(1)}, u32[]{:S(2)}, u32[]{:S(2)}) %collective-permute-start.29) | collective-permute-done | bytes 614432 | tf_op jit(solution)/shard_map/ppermute | solution.py:346
  212.8 1.3 collective-permute-start.32
  214.1 1.5 collective-permute-start.31
  216.3 1.2 multiply_reduce_fusion.1
  217.7 6.8 %collective-permute-done.32 = bf16[128,1280]{1,0:T(8,128)(2,1)S(1)} collective-permute-done((bf16[128,1280]{1,0:T(8,128)(2,1)}, bf16[128,1280]{1,0:T(8,128)(2,1)S(1)}, u32[]{:S(2)}, u32[]{:S(2)}) %collective-permute-start.32) | collective-permute-done | bytes 327712 | tf_op jit(solution)/shard_map/ppermute | solution.py:349
  224.5 3.7 %collective-permute-done.31 = bf16[128,1280]{1,0:T(8,128)(2,1)S(1)} collective-permute-done((bf16[128,1280]{1,0:T(8,128)(2,1)}, bf16[128,1280]{1,0:T(8,128)(2,1)S(1)}, u32[]{:S(2)}, u32[]{:S(2)}) %collective-permute-start.31) | collective-permute-done | bytes 327712 | tf_op jit(solution)/shard_map/ppermute | solution.py:348
  228.2 1.6 fusion.9
  230.6 1.8 fusion.13
  232.4 3.7 %all-to-all-start.3 = ((bf16[8,48,480]{2,1,0:T(8,128)(2,1)}), bf16[8,48,480]{2,1,0:T(8,128)(2,1)S(1)}, u32[]{:S(2)}, u32[]{:S(2)}) async-start(bf16[8,48,480]{2,1,0:T(8,128)(2,1)} %fusion.13), calls=%async_computation.3 | async-start | bytes 786432 | tf_op jit(solution)/shard_map/all_to_all | solution.py:803
  236.1 1.4 multiply_reduce_fusion
  238.0 4.9 %collective-permute-start.35 = (bf16[4,8,1280]{2,1,0:T(8,128)(2,1)S(1)}, bf16[4,8,1280]{2,1,0:T(8,128)(2,1)S(1)}, u32[]{:S(2)}, u32[]{:S(2)}) collective-permute-start(bf16[4,8,1280]{2,1,0:T(8,128)(2,1)S(1)} %get-tuple-element.160), channel_id=1, source_target_pairs={{0,24},{8,0},{16,8},{24,16},{1,25},{9,1},{17,9},{25,17},{2,26},{10... | collective-permute-start | bytes 245768 | tf_op jit(solution)/shard_map/ppermute | solution.py:357
  242.9 1.2 collective-permute-start.36
  244.6 3.3 %collective-permute-done.35 = bf16[4,8,1280]{2,1,0:T(8,128)(2,1)S(1)} collective-permute-done((bf16[4,8,1280]{2,1,0:T(8,128)(2,1)S(1)}, bf16[4,8,1280]{2,1,0:T(8,128)(2,1)S(1)}, u32[]{:S(2)}, u32[]{:S(2)}) %collective-permute-start.35) | collective-permute-done | bytes 81952 | tf_op jit(solution)/shard_map/ppermute | solution.py:357
  247.9 4.2 %collective-permute-done.37 = bf16[4,8,1280]{2,1,0:T(8,128)(2,1)S(1)} collective-permute-done((bf16[4,8,1280]{2,1,0:T(8,128)(2,1)S(1)}, bf16[4,8,1280]{2,1,0:T(8,128)(2,1)S(1)}, u32[]{:S(2)}, u32[]{:S(2)}) %collective-permute-start.37) | collective-permute-done | bytes 81952 | tf_op jit(solution)/shard_map/ppermute | solution.py:357
  252.1 3.0 %collective-permute-done.36 = bf16[4,8,1280]{2,1,0:T(8,128)(2,1)S(1)} collective-permute-done((bf16[4,8,1280]{2,1,0:T(8,128)(2,1)S(1)}, bf16[4,8,1280]{2,1,0:T(8,128)(2,1)S(1)}, u32[]{:S(2)}, u32[]{:S(2)}) %collective-permute-start.36) | collective-permute-done | bytes 81952 | tf_op jit(solution)/shard_map/ppermute | solution.py:357
  262.7 1.7 copy.122
  (231 shorter events, 41.3 us)
Async XLA Ops:
  7.2 39.3 %all-gather.3.cloned.1.call-start = ((), (), s32[]{:S(2)}) async-start(), calls=%async_computation.5 | async-start | bytes 1536000 | tf_op jit(solution)/shard_map/all_gather | solution.py:622
  9.3 7.8 %copy-start.23 = (f32[40,1280]{1,0:T(8,128)S(1)}, f32[40,1280]{1,0:T(8,128)}, u32[]{:S(2)}) copy-start(f32[40,1280]{1,0:T(8,128)} %param.17) | copy-start | bytes 614404
  9.3 7.9 %copy-start.24 = (f32[40,1280]{1,0:T(8,128)S(1)}, f32[40,1280]{1,0:T(8,128)}, u32[]{:S(2)}) copy-start(f32[40,1280]{1,0:T(8,128)} %param.19) | copy-start | bytes 614404
  9.3 7.9 %copy-start.25 = (f32[40,1280]{1,0:T(8,128)S(1)}, f32[40,1280]{1,0:T(8,128)}, u32[]{:S(2)}) copy-start(f32[40,1280]{1,0:T(8,128)} %param.18) | copy-start | bytes 614404
  10.4 8.4 %collective-permute-start = (bf16[5,8,1280]{2,1,0:T(8,128)(2,1)S(1)}, bf16[5,8,1280]{2,1,0:T(8,128)(2,1)S(1)}, u32[]{:S(2)}, u32[]{:S(2)}) collective-permute-start(bf16[5,8,1280]{2,1,0:T(8,128)(2,1)S(1)} %get-tuple-element.179), channel_id=1, source_target_pairs={{0,24},{8,0},{16,8},{24,16},{1,25},{9,1},{17,9},{25,17},{2,26},{10... | collective-permute-start | bytes 307208 | tf_op jit(solution)/shard_map/ppermute | solution.py:357
  15.5 9.5 %collective-permute-start.1 = (bf16[5,8,1280]{2,1,0:T(8,128)(2,1)S(1)}, bf16[5,8,1280]{2,1,0:T(8,128)(2,1)S(1)}, u32[]{:S(2)}, u32[]{:S(2)}) collective-permute-start(bf16[5,8,1280]{2,1,0:T(8,128)(2,1)S(1)} %get-tuple-element.180), channel_id=1, source_target_pairs={{0,16},{8,24},{16,0},{24,8},{1,17},{9,25},{17,1},{25,9},{2,18},{10... | collective-permute-start | bytes 307208 | tf_op jit(solution)/shard_map/ppermute | solution.py:357
  15.5 9.5 %collective-permute-start.2 = (bf16[5,8,1280]{2,1,0:T(8,128)(2,1)S(1)}, bf16[5,8,1280]{2,1,0:T(8,128)(2,1)S(1)}, u32[]{:S(2)}, u32[]{:S(2)}) collective-permute-start(bf16[5,8,1280]{2,1,0:T(8,128)(2,1)S(1)} %get-tuple-element.181), channel_id=1, source_target_pairs={{0,8},{8,16},{16,24},{24,0},{1,9},{9,17},{17,25},{25,1},{2,10},{10... | collective-permute-start | bytes 307208 | tf_op jit(solution)/shard_map/ppermute | solution.py:357
  16.5 8.8 %copy-start.26 = (pred[4]{0:T(512)(128)(4,1)}, pred[4]{0:T(512)(128)(4,1)S(1)}, u32[]{:S(2)}) copy-start(pred[4]{0:T(512)(128)(4,1)S(1)} %broadcast_compare_fusion.2) | copy-start | bytes 16
  25.0 4.5 %copy-start.17 = (bf16[4,8,1280]{2,1,0:T(8,128)(2,1)}, bf16[4,8,1280]{2,1,0:T(8,128)(2,1)S(1)}, u32[]{:S(2)}) copy-start(bf16[4,8,1280]{2,1,0:T(8,128)(2,1)S(1)} %slice.263) | copy-start | bytes 245764
  25.1 4.4 %copy-start.18 = (bf16[4,8,1280]{2,1,0:T(8,128)(2,1)}, bf16[4,8,1280]{2,1,0:T(8,128)(2,1)S(1)}, u32[]{:S(2)}) copy-start(bf16[4,8,1280]{2,1,0:T(8,128)(2,1)S(1)} %slice.264) | copy-start | bytes 245764
  25.5 12.4 %collective-permute-start.5 = (bf16[136,1280]{1,0:T(8,128)(2,1)S(1)}, bf16[136,1280]{1,0:T(8,128)(2,1)S(1)}, u32[]{:S(2)}, u32[]{:S(2)}) collective-permute-start(bf16[136,1280]{1,0:T(8,128)(2,1)S(1)} %maximum_maximum_fusion), channel_id=1, source_target_pairs={{0,5},{1,4},{4,1},{5,0},{2,7},{3,6},{6,3},{7,2},{8,13},{9,12},{12,... | collective-permute-start | bytes 1044488 | tf_op jit(solution)/shard_map/ppermute | solution.py:349
  28.9 14.9 %collective-permute-start.4 = (bf16[136,1280]{1,0:T(8,128)(2,1)S(1)}, bf16[136,1280]{1,0:T(8,128)(2,1)S(1)}, u32[]{:S(2)}, u32[]{:S(2)}) collective-permute-start(bf16[136,1280]{1,0:T(8,128)(2,1)S(1)} %maximum_maximum_fusion), channel_id=1, source_target_pairs={{0,4},{4,0},{1,5},{5,1},{2,6},{6,2},{3,7},{7,3},{8,12},{12,8},{9,1... | collective-permute-start | bytes 1044488 | tf_op jit(solution)/shard_map/ppermute | solution.py:348
  28.9 16.1 %collective-permute-start.3 = (bf16[136,1280]{1,0:T(8,128)(2,1)S(1)}, bf16[136,1280]{1,0:T(8,128)(2,1)}, u32[]{:S(2)}, u32[]{:S(2)}) collective-permute-start(bf16[136,1280]{1,0:T(8,128)(2,1)S(1)} %maximum_maximum_fusion), channel_id=1, source_target_pairs={{0,1},{1,0},{2,3},{3,2},{4,5},{5,4},{6,7},{7,6},{8,9},{9,8},{10,11... | collective-permute-start | bytes 1044488 | tf_op jit(solution)/shard_map/ppermute | solution.py:346
  31.6 14.9 %all-to-all-start = ((bf16[8,40,480]{2,1,0:T(8,128)(2,1)}), bf16[8,40,480]{2,1,0:T(8,128)(2,1)S(1)}, u32[]{:S(2)}, u32[]{:S(2)}) async-start(bf16[8,40,480]{2,1,0:T(8,128)(2,1)} %reshape.404), calls=%async_computation | async-start | bytes 655360 | tf_op jit(solution)/shard_map/all_to_all | solution.py:628
  35.7 51.3 %all-gather.5.cloned.1.call-start = ((), (), s32[]{:S(2)}) async-start(), calls=%async_computation.6 | async-start | bytes 1638400 | tf_op jit(solution)/shard_map/all_gather | solution.py:632
  38.0 7.0 %copy-start.19 = (bf16[136,1280]{1,0:T(8,128)(2,1)}, bf16[136,1280]{1,0:T(8,128)(2,1)S(1)}, u32[]{:S(2)}) copy-start(bf16[136,1280]{1,0:T(8,128)(2,1)S(1)} %collective-permute-done.5) | copy-start | bytes 1044484
  46.4 40.7 %copy-start = (bf16[4,136,1280]{2,1,0:T(8,128)(2,1)}, bf16[4,136,1280]{2,1,0:T(8,128)(2,1)S(1)}, u32[]{:S(2)}) copy-start(bf16[4,136,1280]{2,1,0:T(8,128)(2,1)S(1)} %pad_maximum_fusion.1.near_ref) | copy-start | bytes 4177924
  46.5 5.5 %copy-start.32 = (s32[16]{0:T(128)S(1)}, s32[16]{0:T(128)}, u32[]{:S(2)}) copy-start(s32[16]{0:T(128)} %param.27) | copy-start | bytes 196
  46.6 5.5 %copy-start.33 = (s32[16]{0:T(128)S(1)}, s32[16]{0:T(128)}, u32[]{:S(2)}) copy-start(s32[16]{0:T(128)} %param.26) | copy-start | bytes 196
  49.2 15.8 %collective-permute-start.7 = (bf16[2,3,40,1280]{3,2,1,0:T(8,128)(2,1)}, bf16[2,3,40,1280]{3,2,1,0:T(8,128)(2,1)S(1)}, u32[]{:S(2)}, u32[]{:S(2)}) collective-permute-start(bf16[2,3,40,1280]{3,2,1,0:T(8,128)(2,1)} %get-tuple-element.151), channel_id=1, source_target_pairs={{0,4},{4,0},{1,5},{5,1},{2,6},{6,2},{3,7},{7,3},{8,12},{12,8},{9,1... | collective-permute-start | bytes 1843208 | tf_op jit(solution)/shard_map/ppermute | solution.py:348
  50.4 15.6 %collective-permute-start.6 = (bf16[2,3,40,1280]{3,2,1,0:T(8,128)(2,1)S(1)}, bf16[2,3,40,1280]{3,2,1,0:T(8,128)(2,1)}, u32[]{:S(2)}, u32[]{:S(2)}) collective-permute-start(bf16[2,3,40,1280]{3,2,1,0:T(8,128)(2,1)S(1)} %get-tuple-element.152), channel_id=1, source_target_pairs={{0,1},{1,0},{2,3},{3,2},{4,5},{5,4},{6,7},{7,6},{8,9},{9,8},{10,11... | collective-permute-start | bytes 1843208 | tf_op jit(solution)/shard_map/ppermute | solution.py:346
  52.0 18.0 %collective-permute-start.8 = (bf16[4,136,1280]{2,1,0:T(8,128)(2,1)S(1)}, bf16[4,136,1280]{2,1,0:T(8,128)(2,1)}, u32[]{:S(2)}, u32[]{:S(2)}) collective-permute-start(bf16[4,136,1280]{2,1,0:T(8,128)(2,1)S(1)} %pad_maximum_fusion.1.near_ref), channel_id=1, source_target_pairs={{0,2},{2,0},{1,3},{3,1},{4,6},{6,4},{5,7},{7,5},{8,10},{10,8},{9,1... | collective-permute-start | bytes 4177928 | tf_op jit(solution)/shard_map/ppermute | solution.py:353
  71.2 44.0 %collective-permute-start.14 = (bf16[2,3,80,1280]{3,2,1,0:T(8,128)(2,1)}, bf16[2,3,80,1280]{3,2,1,0:T(8,128)(2,1)}, u32[]{:S(2)}, u32[]{:S(2)}) collective-permute-start(bf16[2,3,80,1280]{3,2,1,0:T(8,128)(2,1)} %bitcast.28.near_a), channel_id=1, source_target_pairs={{0,4},{4,0},{1,5},{5,1},{2,6},{6,2},{3,7},{7,3},{8,12},{12,8},{9,1... | collective-permute-start | bytes 3686408 | tf_op jit(solution)/shard_map/ppermute | solution.py:348
  71.9 43.3 %collective-permute-start.15 = (bf16[2,3,2,40,1280]{4,3,1,0,2:T(8,128)(2,1)}, bf16[2,3,2,40,1280]{4,3,1,0,2:T(8,128)(2,1)}, u32[]{:S(2)}, u32[]{:S(2)}) collective-permute-start(bf16[2,3,2,40,1280]{4,3,1,0,2:T(8,128)(2,1)} %pad_maximum_fusion.3), channel_id=1, source_target_pairs={{0,1},{1,0},{2,3},{3,2},{4,5},{5,4},{6,7},{7,6},{8,9},{9,8},{10,11... | collective-permute-start | bytes 3686408 | tf_op jit(solution)/shard_map/ppermute | solution.py:346
  96.6 18.5 %collective-permute-start.13 = (bf16[2,3,80,1280]{3,2,1,0:T(8,128)(2,1)}, bf16[2,3,80,1280]{3,2,1,0:T(8,128)(2,1)}, u32[]{:S(2)}, u32[]{:S(2)}) collective-permute-start(bf16[2,3,80,1280]{3,2,1,0:T(8,128)(2,1)} %bitcast.28.near_a), channel_id=1, source_target_pairs={{0,2},{2,0},{1,3},{3,1},{4,6},{6,4},{5,7},{7,5},{8,10},{10,8},{9,1... | collective-permute-start | bytes 3686408 | tf_op jit(solution)/shard_map/ppermute | solution.py:353
  96.7 2.9 %collective-permute-start.9 = (bf16[4,128,160]{2,1,0:T(8,128)(2,1)S(1)}, bf16[4,128,160]{2,1,0:T(8,128)(2,1)S(1)}, u32[]{:S(2)}, u32[]{:S(2)}) collective-permute-start(bf16[4,128,160]{2,1,0:T(8,128)(2,1)S(1)} %get-tuple-element.86), channel_id=1, source_target_pairs={{0,2},{2,0},{1,3},{3,1},{4,6},{6,4},{5,7},{7,5},{8,10},{10,8},{9,1... | collective-permute-start | bytes 491528 | tf_op jit(solution)/shard_map/ppermute | solution.py:353
  99.7 14.5 %all-to-all-start.1 = ((bf16[4,4,8,1280]{3,2,1,0:T(8,128)(2,1)}), bf16[4,4,8,1280]{3,2,1,0:T(8,128)(2,1)S(1)}, u32[]{:S(2)}, u32[]{:S(2)}) async-start(bf16[4,4,8,1280]{3,2,1,0:T(8,128)(2,1)} %bitcast.40), calls=%async_computation.1 | async-start | bytes 655360 | tf_op jit(solution)/shard_map/all_to_all | solution.py:677
  103.4 6.8 %collective-permute-start.12 = (bf16[2,128,160]{2,1,0:T(8,128)(2,1)S(1)}, bf16[2,128,160]{2,1,0:T(8,128)(2,1)S(1)}, u32[]{:S(2)}, u32[]{:S(2)}) collective-permute-start(bf16[2,128,160]{2,1,0:T(8,128)(2,1)S(1)} %get-tuple-element.156), channel_id=1, source_target_pairs={{0,5},{1,4},{4,1},{5,0},{2,7},{3,6},{6,3},{7,2},{8,13},{9,12},{12,... | collective-permute-start | bytes 245768 | tf_op jit(solution)/shard_map/ppermute | solution.py:349
  105.8 8.4 %collective-permute-start.11 = (bf16[2,128,160]{2,1,0:T(8,128)(2,1)S(1)}, bf16[2,128,160]{2,1,0:T(8,128)(2,1)S(1)}, u32[]{:S(2)}, u32[]{:S(2)}) collective-permute-start(bf16[2,128,160]{2,1,0:T(8,128)(2,1)S(1)} %get-tuple-element.157), channel_id=1, source_target_pairs={{0,4},{4,0},{1,5},{5,1},{2,6},{6,2},{3,7},{7,3},{8,12},{12,8},{9,1... | collective-permute-start | bytes 245768 | tf_op jit(solution)/shard_map/ppermute | solution.py:348
  110.2 5.0 %collective-permute-start.10 = (bf16[2,128,160]{2,1,0:T(8,128)(2,1)S(1)}, bf16[2,128,160]{2,1,0:T(8,128)(2,1)S(1)}, u32[]{:S(2)}, u32[]{:S(2)}) collective-permute-start(bf16[2,128,160]{2,1,0:T(8,128)(2,1)S(1)} %get-tuple-element.158), channel_id=1, source_target_pairs={{0,1},{1,0},{2,3},{3,2},{4,5},{5,4},{6,7},{7,6},{8,9},{9,8},{10,11... | collective-permute-start | bytes 245768 | tf_op jit(solution)/shard_map/ppermute | solution.py:346
  118.9 6.8 %collective-permute-start.17 = (bf16[2,3,2,80,1280]{4,3,2,1,0:T(8,128)(2,1)}, bf16[2,3,2,80,1280]{4,3,2,1,0:T(8,128)(2,1)}, u32[]{:S(2)}, u32[]{:S(2)}) collective-permute-start(bf16[2,3,2,80,1280]{4,3,2,1,0:T(8,128)(2,1)} %bitcast.45.all_b), channel_id=1, source_target_pairs={{0,2},{2,0},{1,3},{3,1},{4,6},{6,4},{5,7},{7,5},{8,10},{10,8},{9,1... | collective-permute-start | bytes 7372808 | tf_op jit(solution)/shard_map/ppermute | solution.py:353
  118.9 6.8 %collective-permute-start.16 = (bf16[2,3,80,1280]{3,2,1,0:T(8,128)(2,1)}, bf16[2,3,80,1280]{3,2,1,0:T(8,128)(2,1)}, u32[]{:S(2)}, u32[]{:S(2)}) collective-permute-start(bf16[2,3,80,1280]{3,2,1,0:T(8,128)(2,1)} %collective-permute-done.14.across_a), channel_id=1, source_target_pairs={{0,2},{2,0},{1,3},{3,1},{4,6},{6,4},{5,7},{7,5},{8,10},{10,8},{9,1... | collective-permute-start | bytes 3686408 | tf_op jit(solution)/shard_map/ppermute | solution.py:353
  135.2 11.1 %collective-permute-start.18 = (bf16[5,128,1280]{2,1,0:T(8,128)(2,1)}, bf16[5,128,1280]{2,1,0:T(8,128)(2,1)}, u32[]{:S(2)}, u32[]{:S(2)}) collective-permute-start(bf16[5,128,1280]{2,1,0:T(8,128)(2,1)} %get-tuple-element.99.pack_ref), channel_id=1, source_target_pairs={{0,2},{2,0},{1,3},{3,1},{4,6},{6,4},{5,7},{7,5},{8,10},{10,8},{9,1... | collective-permute-start | bytes 4915208 | tf_op jit(solution)/shard_map/ppermute | solution.py:353
  135.4 8.9 %collective-permute-start.20 = (bf16[2,128,160]{2,1,0:T(8,128)(2,1)S(1)}, bf16[2,128,160]{2,1,0:T(8,128)(2,1)}, u32[]{:S(2)}, u32[]{:S(2)}) collective-permute-start(bf16[2,128,160]{2,1,0:T(8,128)(2,1)S(1)} %get-tuple-element.102), channel_id=1, source_target_pairs={{0,1},{1,0},{2,3},{3,2},{4,5},{5,4},{6,7},{7,6},{8,9},{9,8},{10,11... | collective-permute-start | bytes 245768 | tf_op jit(solution)/shard_map/ppermute | solution.py:346
  136.9 8.4 %collective-permute-start.21 = (bf16[2,128,160]{2,1,0:T(8,128)(2,1)S(1)}, bf16[2,128,160]{2,1,0:T(8,128)(2,1)S(1)}, u32[]{:S(2)}, u32[]{:S(2)}) collective-permute-start(bf16[2,128,160]{2,1,0:T(8,128)(2,1)S(1)} %get-tuple-element.103), channel_id=1, source_target_pairs={{0,4},{4,0},{1,5},{5,1},{2,6},{6,2},{3,7},{7,3},{8,12},{12,8},{9,1... | collective-permute-start | bytes 245768 | tf_op jit(solution)/shard_map/ppermute | solution.py:348
  138.4 6.8 %collective-permute-start.22 = (bf16[2,128,160]{2,1,0:T(8,128)(2,1)S(1)}, bf16[2,128,160]{2,1,0:T(8,128)(2,1)S(1)}, u32[]{:S(2)}, u32[]{:S(2)}) collective-permute-start(bf16[2,128,160]{2,1,0:T(8,128)(2,1)S(1)} %get-tuple-element.104), channel_id=1, source_target_pairs={{0,5},{1,4},{4,1},{5,0},{2,7},{3,6},{6,3},{7,2},{8,13},{9,12},{12,... | collective-permute-start | bytes 245768 | tf_op jit(solution)/shard_map/ppermute | solution.py:349
  139.7 14.7 %all-to-all-start.2 = ((bf16[4,4,8,1280]{3,2,1,0:T(8,128)(2,1)}), bf16[4,4,8,1280]{3,2,1,0:T(8,128)(2,1)}, u32[]{:S(2)}, u32[]{:S(2)}) async-start(bf16[4,4,8,1280]{3,2,1,0:T(8,128)(2,1)} %bitcast.165), calls=%async_computation.2 | async-start | bytes 655360 | tf_op jit(solution)/shard_map/all_to_all | solution.py:712
  144.3 116.6 %reduce-scatter.2.cloned.1.call-start = ((), (), s32[]{:S(2)}) async-start(), calls=%async_computation.7 | async-start | bytes 1536000 | tf_op jit(solution)/shard_map/reduce_scatter | solution.py:804
  144.3 1.9 collective-permute-start.19
  145.4 7.9 %collective-permute-start.23 = (bf16[4,128,160]{2,1,0:T(8,128)(2,1)S(1)}, bf16[4,128,160]{2,1,0:T(8,128)(2,1)S(1)}, u32[]{:S(2)}, u32[]{:S(2)}) collective-permute-start(bf16[4,128,160]{2,1,0:T(8,128)(2,1)S(1)} %pad_maximum_fusion.9), channel_id=1, source_target_pairs={{0,2},{2,0},{1,3},{3,1},{4,6},{6,4},{5,7},{7,5},{8,10},{10,8},{9,1... | collective-permute-start | bytes 491528 | tf_op jit(solution)/shard_map/ppermute | solution.py:353
  157.5 3.9 %copy-start.4 = (bf16[2,3,1,2,40,1280]{5,4,3,2,1,0:T(8,128)(2,1)}, bf16[2,3,1,2,40,1280]{5,4,3,2,1,0:T(8,128)(2,1)S(1)}, u32[]{:S(2)}) copy-start(bf16[2,3,1,2,40,1280]{5,4,3,2,1,0:T(8,128)(2,1)S(1)} %get-tuple-element.131) | copy-start | bytes 3686404
  157.6 3.9 %copy-start.6 = (bf16[2,3,1,2,40,1280]{5,4,3,2,1,0:T(8,128)(2,1)}, bf16[2,3,1,2,40,1280]{5,4,3,2,1,0:T(8,128)(2,1)S(1)}, u32[]{:S(2)}) copy-start(bf16[2,3,1,2,40,1280]{5,4,3,2,1,0:T(8,128)(2,1)S(1)} %get-tuple-element.132) | copy-start | bytes 3686404
  160.0 28.2 %collective-permute-start.25 = (bf16[2,3,2,40,1280]{4,3,1,0,2:T(8,128)(2,1)}, bf16[2,3,2,40,1280]{4,3,1,0,2:T(8,128)(2,1)}, u32[]{:S(2)}, u32[]{:S(2)}) collective-permute-start(bf16[2,3,2,40,1280]{4,3,1,0,2:T(8,128)(2,1)} %select_bitcast_fusion.1), channel_id=1, source_target_pairs={{0,1},{1,0},{2,3},{3,2},{4,5},{5,4},{6,7},{7,6},{8,9},{9,8},{10,11... | collective-permute-start | bytes 3686408 | tf_op jit(solution)/shard_map/ppermute | solution.py:346
  162.6 27.9 %collective-permute-start.26 = (bf16[2,3,2,40,1280]{4,3,1,0,2:T(8,128)(2,1)}, bf16[2,3,2,40,1280]{4,3,1,0,2:T(8,128)(2,1)}, u32[]{:S(2)}, u32[]{:S(2)}) collective-permute-start(bf16[2,3,2,40,1280]{4,3,1,0,2:T(8,128)(2,1)} %select_bitcast_fusion), channel_id=1, source_target_pairs={{0,4},{4,0},{1,5},{5,1},{2,6},{6,2},{3,7},{7,3},{8,12},{12,8},{9,1... | collective-permute-start | bytes 3686408 | tf_op jit(solution)/shard_map/ppermute | solution.py:348
  179.0 13.3 %collective-permute-start.24 = (bf16[4,128,1280]{2,1,0:T(8,128)(2,1)}, bf16[4,128,1280]{2,1,0:T(8,128)(2,1)S(1)}, u32[]{:S(2)}, u32[]{:S(2)}) collective-permute-start(bf16[4,128,1280]{2,1,0:T(8,128)(2,1)} %copy-done.3), channel_id=1, source_target_pairs={{0,2},{2,0},{1,3},{3,1},{4,6},{6,4},{5,7},{7,5},{8,10},{10,8},{9,1... | collective-permute-start | bytes 3932168 | tf_op jit(solution)/shard_map/ppermute | solution.py:353
  179.1 9.1 %copy-start.9 = (bf16[2,3,2,1,40,1280]{5,4,3,2,1,0:T(8,128)(2,1)S(1)}, bf16[2,3,2,1,40,1280]{5,4,3,2,1,0:T(8,128)(2,1)}, u32[]{:S(2)}) copy-start(bf16[2,3,2,1,40,1280]{5,4,3,2,1,0:T(8,128)(2,1)} %copy-done.8) | copy-start | bytes 3686404
  179.1 9.1 %copy-start.11 = (bf16[2,3,2,1,40,1280]{5,4,3,2,1,0:T(8,128)(2,1)S(1)}, bf16[2,3,2,1,40,1280]{5,4,3,2,1,0:T(8,128)(2,1)}, u32[]{:S(2)}) copy-start(bf16[2,3,2,1,40,1280]{5,4,3,2,1,0:T(8,128)(2,1)} %copy-done.10) | copy-start | bytes 3686404
  180.8 16.3 %copy-start.13 = (bf16[4,328,480]{2,1,0:T(8,128)(2,1)}, bf16[4,328,480]{2,1,0:T(8,128)(2,1)S(1)}, u32[]{:S(2)}) copy-start(bf16[4,328,480]{2,1,0:T(8,128)(2,1)S(1)} %fusion.3) | copy-start | bytes 3778564
  180.8 9.7 %copy-start.5 = (bf16[2,3,1,2,40,1280]{5,4,3,2,1,0:T(8,128)(2,1)S(1)}, bf16[2,3,1,2,40,1280]{5,4,3,2,1,0:T(8,128)(2,1)}, u32[]{:S(2)}) copy-start(bf16[2,3,1,2,40,1280]{5,4,3,2,1,0:T(8,128)(2,1)} %copy-done.4) | copy-start | bytes 3686404
  180.8 9.7 %copy-start.7 = (bf16[2,3,1,2,40,1280]{5,4,3,2,1,0:T(8,128)(2,1)S(1)}, bf16[2,3,1,2,40,1280]{5,4,3,2,1,0:T(8,128)(2,1)}, u32[]{:S(2)}) copy-start(bf16[2,3,1,2,40,1280]{5,4,3,2,1,0:T(8,128)(2,1)} %copy-done.6) | copy-start | bytes 3686404
  180.9 12.9 %collective-permute-start.27 = (bf16[328,480]{1,0:T(8,128)(2,1)S(1)}, bf16[328,480]{1,0:T(8,128)(2,1)S(1)}, u32[]{:S(2)}, u32[]{:S(2)}) collective-permute-start(bf16[328,480]{1,0:T(8,128)(2,1)S(1)} %dynamic-slice_bitcast_fusion.2), channel_id=1, source_target_pairs={{0,8},{8,16},{16,24},{24,0},{1,9},{9,17},{17,25},{25,1},{2,10},{10... | collective-permute-start | bytes 944648 | tf_op jit(solution)/shard_map/ppermute | solution.py:357
  194.5 14.7 %collective-permute-start.29 = (bf16[2,3,40,1280]{3,2,1,0:T(8,128)(2,1)S(1)}, bf16[2,3,40,1280]{3,2,1,0:T(8,128)(2,1)S(1)}, u32[]{:S(2)}, u32[]{:S(2)}) collective-permute-start(bf16[2,3,40,1280]{3,2,1,0:T(8,128)(2,1)S(1)} %select_bitcast_fusion.4), channel_id=1, source_target_pairs={{0,1},{1,0},{2,3},{3,2},{4,5},{5,4},{6,7},{7,6},{8,9},{9,8},{10,11... | collective-permute-start | bytes 1843208 | tf_op jit(solution)/shard_map/ppermute | solution.py:346
  195.5 14.3 %collective-permute-start.28 = (bf16[2,3,40,1280]{3,2,1,0:T(8,128)(2,1)S(1)}, bf16[2,3,40,1280]{3,2,1,0:T(8,128)(2,1)S(1)}, u32[]{:S(2)}, u32[]{:S(2)}) collective-permute-start(bf16[2,3,40,1280]{3,2,1,0:T(8,128)(2,1)S(1)} %select_bitcast_fusion.5), channel_id=1, source_target_pairs={{0,4},{4,0},{1,5},{5,1},{2,6},{6,2},{3,7},{7,3},{8,12},{12,8},{9,1... | collective-permute-start | bytes 1843208 | tf_op jit(solution)/shard_map/ppermute | solution.py:348
  198.0 19.7 %collective-permute-start.34 = (bf16[328,480]{1,0:T(8,128)(2,1)}, bf16[328,480]{1,0:T(8,128)(2,1)}, u32[]{:S(2)}, u32[]{:S(2)}) collective-permute-start(bf16[328,480]{1,0:T(8,128)(2,1)} %get-tuple-element.141), channel_id=1, source_target_pairs={{0,16},{8,24},{16,0},{24,8},{1,17},{9,25},{17,1},{25,9},{2,18},{10... | collective-permute-start | bytes 944648 | tf_op jit(solution)/shard_map/ppermute | solution.py:357
  200.9 16.8 %collective-permute-start.33 = (bf16[328,480]{1,0:T(8,128)(2,1)}, bf16[328,480]{1,0:T(8,128)(2,1)}, u32[]{:S(2)}, u32[]{:S(2)}) collective-permute-start(bf16[328,480]{1,0:T(8,128)(2,1)} %get-tuple-element.142), channel_id=1, source_target_pairs={{0,24},{8,0},{16,8},{24,16},{1,25},{9,1},{17,9},{25,17},{2,26},{10... | collective-permute-start | bytes 944648 | tf_op jit(solution)/shard_map/ppermute | solution.py:357
  211.2 5.1 %copy-start.27 = (pred[4]{0:T(512)(128)(4,1)S(1)}, pred[4]{0:T(512)(128)(4,1)}, u32[]{:S(2)}) copy-start(pred[4]{0:T(512)(128)(4,1)} %copy-done.26) | copy-start | bytes 16
  212.8 11.8 %collective-permute-start.32 = (bf16[128,1280]{1,0:T(8,128)(2,1)}, bf16[128,1280]{1,0:T(8,128)(2,1)S(1)}, u32[]{:S(2)}, u32[]{:S(2)}) collective-permute-start(bf16[128,1280]{1,0:T(8,128)(2,1)} %get-tuple-element.146), channel_id=1, source_target_pairs={{0,5},{1,4},{4,1},{5,0},{2,7},{3,6},{6,3},{7,2},{8,13},{9,12},{12,... | collective-permute-start | bytes 983048 | tf_op jit(solution)/shard_map/ppermute | solution.py:349
  214.1 14.1 %collective-permute-start.31 = (bf16[128,1280]{1,0:T(8,128)(2,1)}, bf16[128,1280]{1,0:T(8,128)(2,1)S(1)}, u32[]{:S(2)}, u32[]{:S(2)}) collective-permute-start(bf16[128,1280]{1,0:T(8,128)(2,1)} %get-tuple-element.147), channel_id=1, source_target_pairs={{0,4},{4,0},{1,5},{5,1},{2,6},{6,2},{3,7},{7,3},{8,12},{12,8},{9,1... | collective-permute-start | bytes 983048 | tf_op jit(solution)/shard_map/ppermute | solution.py:348
  215.6 12.6 %collective-permute-start.30 = (bf16[128,1280]{1,0:T(8,128)(2,1)}, bf16[128,1280]{1,0:T(8,128)(2,1)S(1)}, u32[]{:S(2)}, u32[]{:S(2)}) collective-permute-start(bf16[128,1280]{1,0:T(8,128)(2,1)} %get-tuple-element.148), channel_id=1, source_target_pairs={{0,1},{1,0},{2,3},{3,2},{4,5},{5,4},{6,7},{7,6},{8,9},{9,8},{10,11... | collective-permute-start | bytes 983048 | tf_op jit(solution)/shard_map/ppermute | solution.py:346
  228.2 4.2 %copy-start.15 = (bf16[128,1280]{1,0:T(8,128)(2,1)}, bf16[128,1280]{1,0:T(8,128)(2,1)S(1)}, u32[]{:S(2)}) copy-start(bf16[128,1280]{1,0:T(8,128)(2,1)S(1)} %collective-permute-done.30) | copy-start | bytes 983044
  232.4 23.5 %all-to-all-start.3 = ((bf16[8,48,480]{2,1,0:T(8,128)(2,1)}), bf16[8,48,480]{2,1,0:T(8,128)(2,1)S(1)}, u32[]{:S(2)}, u32[]{:S(2)}) async-start(bf16[8,48,480]{2,1,0:T(8,128)(2,1)} %fusion.13), calls=%async_computation.3 | async-start | bytes 786432 | tf_op jit(solution)/shard_map/all_to_all | solution.py:803
  238.0 9.9 %collective-permute-start.35 = (bf16[4,8,1280]{2,1,0:T(8,128)(2,1)S(1)}, bf16[4,8,1280]{2,1,0:T(8,128)(2,1)S(1)}, u32[]{:S(2)}, u32[]{:S(2)}) collective-permute-start(bf16[4,8,1280]{2,1,0:T(8,128)(2,1)S(1)} %get-tuple-element.160), channel_id=1, source_target_pairs={{0,24},{8,0},{16,8},{24,16},{1,25},{9,1},{17,9},{25,17},{2,26},{10... | collective-permute-start | bytes 245768 | tf_op jit(solution)/shard_map/ppermute | solution.py:357
  242.9 9.2 %collective-permute-start.37 = (bf16[4,8,1280]{2,1,0:T(8,128)(2,1)S(1)}, bf16[4,8,1280]{2,1,0:T(8,128)(2,1)S(1)}, u32[]{:S(2)}, u32[]{:S(2)}) collective-permute-start(bf16[4,8,1280]{2,1,0:T(8,128)(2,1)S(1)} %get-tuple-element.162), channel_id=1, source_target_pairs={{0,8},{8,16},{16,24},{24,0},{1,9},{9,17},{17,25},{25,1},{2,10},{10... | collective-permute-start | bytes 245768 | tf_op jit(solution)/shard_map/ppermute | solution.py:357
  242.9 12.2 %collective-permute-start.36 = (bf16[4,8,1280]{2,1,0:T(8,128)(2,1)S(1)}, bf16[4,8,1280]{2,1,0:T(8,128)(2,1)S(1)}, u32[]{:S(2)}, u32[]{:S(2)}) collective-permute-start(bf16[4,8,1280]{2,1,0:T(8,128)(2,1)S(1)} %get-tuple-element.163), channel_id=1, source_target_pairs={{0,16},{8,24},{16,0},{24,8},{1,17},{9,25},{17,1},{25,9},{2,18},{10... | collective-permute-start | bytes 245768 | tf_op jit(solution)/shard_map/ppermute | solution.py:357
  (15 other events, 28.3 us)
Sparse Core Ops, SparseCore 0:
  10.3 34.4 all-gather.2
  52.5 34.5 all-gather.4
  217.8 35.1 reduce-scatter.1

commit v5 on v4

--- a/solution.py
+++ b/solution.py
@@ -373,8 +373,10 @@
 
 
 def pair(mine, other, index, axis):
-    first = index == 0
-    return jnp.stack([jnp.where(first, mine, other), jnp.where(first, other, mine)], axis=axis)
+    shape = [1] * (mine.ndim + 1)
+    shape[axis] = 2
+    slot = jnp.arange(2, dtype=jnp.int32).reshape(shape)
+    return jnp.where(slot == index, jnp.expand_dims(mine, axis), jnp.expand_dims(other, axis))
 
 
 def row_positions(shape, dim, plane_index):
@@ -403,10 +405,18 @@
     return weights / jnp.sum(weights, axis=1, keepdims=True)
 
 
+def set_weights(info_ref, parts, w_ref):
+    @pl.when(pl.program_id(0) == 0)
+    def _():
+        for hop, part in enumerate(parts):
+            w_ref[pl.ds(pl.multiple_of(((info_ref[0] - hop) & 3) * 320, 320), 320), :] = part[...]
+
+
 def attend_kernel(
-    info_ref, near_ref, far_ref, gain_ref, mult_ref, w_ref, pre_ref, att_near, att_far
+    info_ref, near_ref, far_ref, gain_ref, mult_ref, w_0, w_1, w_2, w_3, pre_ref, att_near, att_far, w_ref
 ):
     seq = pl.program_id(0)
+    set_weights(info_ref, (w_0, w_1, w_2, w_3), w_ref)
     live = live_pairs(info_ref, seq)
     wide = block_rows(near_ref, far_ref).astype(jnp.float32)
     inverse = lax.rsqrt(jnp.mean(wide * wide, axis=1, keepdims=True) + 1e-06)
@@ -427,10 +437,11 @@
 
 
 def attend_back_kernel(
-    info_ref, near_ref, far_ref, gain_ref, mult_ref, w_ref, pre_ref, grad_near, grad_far,
-    hid_near, hid_far, w_grad, gain_grad, scale_grad, w_acc, gain_acc, scale_acc,
+    info_ref, near_ref, far_ref, gain_ref, mult_ref, w_0, w_1, w_2, w_3, pre_ref, grad_near, grad_far, gain_two_ref,
+    hid_near, hid_far, send_0, send_1, send_2, send_3, w_ref, w_acc, gain_acc, scale_acc, lines,
 ):
     seq = pl.program_id(0)
+    set_weights(info_ref, (w_0, w_1, w_2, w_3), w_ref)
 
     @pl.when(seq == 0)
     def _():
@@ -471,9 +482,20 @@
 
     @pl.when(seq == 3)
     def _():
-        w_grad[...] = w_acc[...].astype(jnp.bfloat16)
-        gain_grad[...] = gain_acc[...]
-        scale_grad[...] = scale_acc[...]
+        lines[...] = jnp.zeros_like(lines)
+        for which, source in enumerate((gain_acc, gain_two_ref)):
+            for owner in range(32):
+                lane = 120 * (owner % 4) + 40 * which
+                lines[owner // 4, :, lane : lane + 40] = source[:, 40 * owner : 40 * owner + 40]
+        for part in range(4):
+            lane = 120 * part + 80
+            lines[info_ref[1], :, lane : lane + 40] = scale_acc[:, 40 * part : 40 * part + 40]
+        blank = jnp.zeros((14, 480), jnp.float32)
+        for hop, send in enumerate((send_0, send_1, send_2, send_3)):
+            target = (info_ref[0] + hop) & 3
+            rows = w_acc[pl.ds(pl.multiple_of(target * 320, 320), 320), :]
+            block = jnp.concatenate([rows, lines[2 * target], lines[2 * target + 1], blank], axis=0)
+            send[...] = block.astype(jnp.bfloat16)
 
 
 def block_index(z_index, y_index, core):
@@ -486,9 +508,9 @@
 
 
 def feed_kernel(
-    info_ref, x_ref, g_ref, att_0, att_1, att_2, att_3, gain_ref,
+    info_ref, x_ref, g_ref, atts, gain_ref,
     near_a, across_a, all_b, far_near_a, far_across_a, far_b,
-    out_ref, pack_ref, att_pack, dmid_ref, datt_0, datt_1, datt_2, datt_3, gain_grad,
+    out_ref, pack_ref, dmid_ref, datt_0, datt_1, datt_2, datt_3, gain_grad,
     weights, sems,
 ):
     y_index, core_index = info_ref[1] // 4, (info_ref[1] // 2) % 2
@@ -508,7 +530,7 @@
     for group in copies:
         for copy in group:
             copy.start()
-    atts, datts = (att_0, att_1, att_2, att_3), (datt_0, datt_1, datt_2, datt_3)
+    datts = (datt_0, datt_1, datt_2, datt_3)
 
     for copy in copies[0]:
         copy.wait()
@@ -516,7 +538,7 @@
     for chip in range(4):
         for core in range(2):
             middle += jnp.dot(
-                atts[chip][core], weights[0, source_rows(info_ref, chip, core), :],
+                atts[chip, core], weights[0, source_rows(info_ref, chip, core), :],
                 preferred_element_type=jnp.float32,
             )
     inverse = lax.rsqrt(jnp.mean(middle * middle, axis=1, keepdims=True) + 1e-06)
@@ -533,12 +555,15 @@
     for copy in copies[2]:
         copy.wait()
     down = jnp.dot(active, weights[2], preferred_element_type=jnp.float32)
-    out_ref[...] = (middle + down).astype(jnp.bfloat16)
+    result = middle + down
+    for seq in range(4):
+        for plane_z in range(4):
+            row = 32 * seq + 8 * plane_z
+            out_ref[plane_z, seq] = result[row : row + 8].astype(jnp.bfloat16)
     cot = g_ref[...]
     grad_act = mult_trans(cot, weights[2])
     grad_up = (grad_act * sigma * (1.0 + up * (1.0 - sigma))).astype(jnp.bfloat16)
     pack_ref[2] = grad_up
-    pack_ref[4] = cot
     grad_hidden = mult_trans(grad_up, weights[1])
     gain_grad[...] = jnp.sum(grad_hidden * normed, axis=0, keepdims=True)
     grad_mid = cot.astype(jnp.float32) + norm_back(grad_hidden, normed, inverse, gain)
@@ -547,43 +572,83 @@
     pack_ref[3] = low
     for chip in range(4):
         for core in range(2):
-            att_pack[2 * chip + core] = atts[chip][core]
             datts[chip][core] = mult_trans(low, weights[0, source_rows(info_ref, chip, core), :]).astype(jnp.bfloat16)
 
 
-def grads_kernel(info_ref, pack_ref, att_pack, far_pack, far_att, kept, stage, sems):
-    core_index = (info_ref[1] // 2) % 2
+def grads_kernel(
+    info_ref, pack_ref, far_pack, atts, far_atts, cot_ref, far_cot, half_a, kept_b, away_b, stage, sems
+):
+    y_index, core_index = info_ref[1] // 4, (info_ref[1] // 2) % 2
     copies = []
 
     def leave(w):
-        for z_index in range(4):
-            for row in range(2):
+        for half in range(2):
+            targets = [(half, row, half_a.at[half, w, row]) for row in range(2)]
+            targets += [(2 + half, y_index, kept_b.at[half, w]), (2 + half, 1 - y_index, away_b.at[half, w])]
+            for i, (z_index, row, target) in enumerate(targets):
                 copy = pltpu.make_async_copy(
-                    stage.at[w, block_index(z_index, row, core_index)],
-                    kept.at[z_index, w, row],
-                    sems.at[w, 2 * z_index + row],
+                    stage.at[w, block_index(z_index, row, core_index)], target, sems.at[w, 4 * half + i]
                 )
                 copy.start()
                 copies.append(copy)
 
-    def both(index, part):
-        return jnp.concatenate([pack_ref[index, :, part], far_pack[index, :, part]], axis=0)
-
-    everything = slice(0, pack_ref.shape[2])
-    for w, left, right in ((2, 0, 4), (1, 1, 2)):
-        grads = both(right, everything)
+    def both(near, far):
+        return jnp.concatenate([near, far], axis=0)
+
+    cots = both(cot_ref[...], far_cot[...])
+    for w, left, grads in ((2, 0, cots), (1, 1, both(pack_ref[2], far_pack[2]))):
         for chunk in range(5):
             part = slice(256 * chunk, 256 * chunk + 256)
-            stage[w, part, :] = trans_mult(both(left, part), grads).astype(jnp.bfloat16)
+            acts = both(pack_ref[left, :, part], far_pack[left, :, part])
+            stage[w, part, :] = trans_mult(acts, grads).astype(jnp.bfloat16)
         leave(w)
-    grads = both(3, everything)
+    grads = both(pack_ref[3], far_pack[3])
     for chip in range(4):
         for core in range(2):
-            att = jnp.concatenate([att_pack[2 * chip + core], far_att[2 * chip + 1 - core]], axis=0)
+            att = both(atts[chip, core], far_atts[chip, 1 - core])
             stage[0, source_rows(info_ref, chip, core), :] = trans_mult(att, grads).astype(jnp.bfloat16)
     leave(0)
     for copy in copies:
         copy.wait()
+
+
+def norm_kernel(info_ref, hid_0, hid_1, hid_2, hid_3, x_ref, dmid_ref, gain_ref, out_0, out_1, out_2, out_3, rows):
+    grad = hid_0[...].astype(jnp.float32)
+    for item in (hid_1, hid_2, hid_3):
+        grad += item[...].astype(jnp.float32)
+    wide = x_ref[...].astype(jnp.float32)
+    inverse = lax.rsqrt(jnp.mean(wide * wide, axis=1, keepdims=True) + 1e-06)
+    grad = dmid_ref[...] + norm_back(grad, wide * inverse, inverse, gain_ref[...])
+    for seq in range(4):
+        for plane_z in range(4):
+            row = 32 * seq + 8 * plane_z
+            rows[plane_z, seq] = grad[row : row + 8]
+    for hop, out in enumerate((out_0, out_1, out_2, out_3)):
+        out[...] = rows[(info_ref[0] + hop) & 3].astype(jnp.bfloat16)
+
+
+def fold_kernel(part_0, part_1, part_2, part_3, out_ref, line):
+    total = part_0[...].astype(jnp.float32)
+    for item in (part_1, part_2, part_3):
+        total += item[...].astype(jnp.float32)
+    line[...] = jnp.zeros_like(line)
+    for owner in range(8):
+        lane = 120 * (owner % 4)
+        line[0:1, 0:120] = total[320 + owner // 4 : 321 + owner // 4, lane : lane + 120]
+        block = jnp.concatenate([total[40 * owner : 40 * owner + 40], line[...]], axis=0)
+        out_ref[owner] = block.astype(jnp.bfloat16)
+
+
+def spread_kernel(in_ref, *outs):
+    for which, out in enumerate(outs):
+        for owner in range(8):
+            part = in_ref[owner, 0:40, 160 * which : 160 * which + 160]
+            out[:, 160 * owner : 160 * owner + 160] = part.astype(jnp.float32)
+
+
+def widen_kernel(in_ref, *outs):
+    for which, out in enumerate(outs):
+        out[...] = in_ref[which].astype(jnp.float32)
 
 
 def whole(shape):
@@ -623,13 +688,17 @@
 
     qkv = jnp.stack([w_query, w_key, w_value]).astype(bf16)
     own, qkv = lax.optimization_barrier((own, qkv))
-    near = jnp.stack([own] + [plane_shift(own, step) for step in (1, 2, 3)])
+    near = [own] + [plane_shift(own, step) for step in (1, 2, 3)]
     qkv = qkv.reshape(3, 40, 8, 160).transpose(2, 1, 0, 3).reshape(8, 40, 480)
     qkv = lax.all_to_all(qkv, ("y", "core", "x"), split_axis=0, concat_axis=0, tiled=True)
     qkv = qkv.reshape(320, 480)
 
-    big, near, qkv = lax.optimization_barrier((big, near, qkv))
-    w_qkv = lax.all_gather(qkv, "z", axis=0, tiled=True)
+    late = qkv
+    *near, qkv = lax.optimization_barrier((*near, qkv))
+    near = jnp.stack(near)
+    one, three, late = lax.optimization_barrier((ring_shift(qkv, 1), ring_shift(qkv, 3), late))
+    w_parts = [qkv, one, ring_shift(late, 2), three]
+    big, near = lax.optimization_barrier((big, near))
     far = core_swap(near)
     part_a, part_b = big[:2], big[2:]
     near_a = pair(part_a, plane_shift(part_a, 1), x, 2).reshape(2, 3, 80, width)
@@ -656,9 +725,10 @@
             grid=(4,),
             in_specs=[
                 seq_block(4, width=width), seq_block(4, width=width),
-                whole((1, width)), whole((1, 160)), whole((width, 480)),
+                whole((1, width)), whole((1, 160)), *[whole((320, 480))] * 4,
             ],
             out_specs=[seq_block(2, 4, width=480), seq_block(4, width=160), seq_block(4, width=160)],
+            scratch_shapes=[pltpu.VMEM((width, 480), bf16)],
         ),
         out_shape=[
             jax.ShapeDtypeStruct((2, 4, 128, 480), f32),
@@ -668,7 +738,7 @@
         compiler_params=limit,
         cost_estimate=pl.CostEstimate(flops=9_000_000_000, bytes_accessed=8_000_000, transcendentals=600_000),
         name="attend",
-    )(info, near, far, gain_one, query_mult, w_qkv)
+    )(info, near, far, gain_one, query_mult, *w_parts)
 
     att_near, att_far, near_a = lax.optimization_barrier((att_near, att_far, near_a))
     far_near_a = core_swap(near_a)
@@ -677,26 +747,26 @@
     cot_rows = lax.all_to_all(cotangent.reshape(4, 4, 8, width), "z", split_axis=0, concat_axis=0, tiled=True)
     cot_rows = cot_rows.transpose(1, 0, 2, 3).reshape(128, width)
     atts = [att_pair[0]] + [plane_shift(att_pair[step], step) for step in (1, 2, 3)]
-    *atts, far_near_a, across_a, across_b, cot_rows = lax.optimization_barrier(
-        (*atts, far_near_a, across_a, across_b, cot_rows)
+    atts = jnp.stack(atts)
+    far_atts, far_cot = core_swap(atts), core_swap(cot_rows)
+    atts, far_near_a, across_a, across_b, cot_rows, far_atts, far_cot = lax.optimization_barrier(
+        (atts, far_near_a, across_a, across_b, cot_rows, far_atts, far_cot)
     )
     far_across_a = core_swap(across_a)
     all_b = pair(part_b, across_b, x, 3).reshape(2, 3, 2, 80, width)
     far_b = core_swap(all_b)
 
-    low_rows = jax.ShapeDtypeStruct((128, width), bf16)
     datt_shape = jax.ShapeDtypeStruct((2, 128, 160), bf16)
     smem = pl.BlockSpec(memory_space=pltpu.SMEM)
     vmem = pl.BlockSpec(memory_space=pltpu.VMEM)
     hbm = pl.BlockSpec(memory_space=pl.ANY)
-    out_rows, pack, att_pack, grad_mid, *datts, gain_two_grad = pl.pallas_call(
+    out_rows, pack, grad_mid, *datts, gain_two_grad = pl.pallas_call(
         feed_kernel,
-        in_specs=[smem] + [vmem] * 7 + [hbm] * 6,
-        out_specs=[vmem] * 9,
+        in_specs=[smem] + [vmem] * 4 + [hbm] * 6,
+        out_specs=[vmem] * 8,
         out_shape=[
-            low_rows,
-            jax.ShapeDtypeStruct((5, 128, width), bf16),
-            jax.ShapeDtypeStruct((8, 128, 160), bf16),
+            jax.ShapeDtypeStruct((4, 4, 8, width), bf16),
+            jax.ShapeDtypeStruct((4, 128, width), bf16),
             jax.ShapeDtypeStruct((128, width), f32),
         ]
         + [datt_shape] * 4
@@ -705,27 +775,24 @@
         compiler_params=limit,
         cost_estimate=pl.CostEstimate(flops=12_000_000_000, bytes_accessed=13_000_000, transcendentals=200_000),
         name="feed",
-    )(info, x_rows, cot_rows, *atts, gain_two, near_a, across_a, all_b, far_near_a, far_across_a, far_b)
-
-    def home(rows):
-        rows = rows.reshape(4, 4, 8, width).transpose(1, 0, 2, 3)
-        return lax.all_to_all(rows, "z", split_axis=0, concat_axis=0, tiled=True).reshape(16, 8, width)
+    )(info, x_rows, cot_rows, atts, gain_two, near_a, across_a, all_b, far_near_a, far_across_a, far_b)
 
     back = [datts[0]] + [plane_shift(datts[step], step) for step in (1, 2, 3)]
-    outputs = home(out_rows)
+    outputs = lax.all_to_all(out_rows, "z", split_axis=0, concat_axis=0, tiled=True).reshape(16, 8, width)
     grad_att_near = jnp.stack([item[0] for item in back])
     grad_att_far = core_swap(jnp.stack([item[1] for item in back]))
 
-    kept = pl.pallas_call(
+    part_shape = jax.ShapeDtypeStruct((2, 3, 80, width), bf16)
+    half_a, kept_b, away_b = pl.pallas_call(
         grads_kernel,
-        in_specs=[smem] + [vmem] * 4,
-        out_specs=hbm,
-        out_shape=jax.ShapeDtypeStruct((4, 3, 2, 80, width), bf16),
+        in_specs=[smem] + [vmem] * 6,
+        out_specs=[hbm] * 3,
+        out_shape=[jax.ShapeDtypeStruct((2, 3, 2, 80, width), bf16), part_shape, part_shape],
         scratch_shapes=[pltpu.VMEM((3, width, width), bf16), pltpu.SemaphoreType.DMA((3, 8))],
         compiler_params=limit,
         cost_estimate=pl.CostEstimate(flops=6_000_000_000, bytes_accessed=8_000_000, transcendentals=0),
         name="grads",
-    )(info, pack, att_pack, core_swap(pack), core_swap(att_pack))
+    )(info, pack, core_swap(pack), atts, far_atts, cot_rows, far_cot)
 
     def added(left, right):
         return (left.astype(f32) + right.astype(f32)).astype(bf16)
@@ -734,81 +801,87 @@
         first, second = (lax.index_in_dim(array, i, axis, keepdims=False) for i in (0, 1))
         return jnp.where(index == 0, first, second), jnp.where(index == 0, second, first)
 
-    kept, grad_att_near, grad_att_far, outputs = lax.optimization_barrier(
-        (kept, grad_att_near, grad_att_far, outputs)
-    )
-    kept = kept.reshape(4, 3, 2, 2, 40, width)
-    kept_a, away_a = halves(kept[:2], x, 3)
-    kept_b, away_b = halves(kept[2:], y, 2)
+    half_a, kept_b, away_b, grad_att_near, grad_att_far, outputs = lax.optimization_barrier(
+        (half_a, kept_b, away_b, grad_att_near, grad_att_far, outputs)
+    )
+    kept_a, away_a = halves(half_a.reshape(2, 3, 2, 2, 40, width), x, 3)
     kept_a = added(kept_a, plane_shift(away_a, 1))
-    kept_b = added(kept_b, plane_shift(away_b, 2))
-    hid_near, hid_far, qkv_grad, gain_one_grad, scale_grad = pl.pallas_call(
+    kept_b = added(kept_b, plane_shift(away_b, 2)).reshape(2, 3, 2, 40, width)
+    hid_near, hid_far, *send = pl.pallas_call(
         attend_back_kernel,
         grid_spec=pltpu.PrefetchScalarGridSpec(
             num_scalar_prefetch=1,
             grid=(4,),
             in_specs=[
                 seq_block(4, width=width), seq_block(4, width=width),
-                whole((1, width)), whole((1, 160)), whole((width, 480)),
-                seq_block(2, 4, width=480), seq_block(4, width=160), seq_block(4, width=160),
+                whole((1, width)), whole((1, 160)), *[whole((320, 480))] * 4,
+                seq_block(2, 4, width=480), seq_block(4, width=160), seq_block(4, width=160), whole((1, width)),
             ],
             out_specs=[
                 seq_block(4, width=width), seq_block(4, width=width),
-                whole((width, 480)), whole((1, width)), whole((1, 160)),
+                *[whole((336, 480))] * 4,
             ],
             scratch_shapes=[
-                pltpu.VMEM((width, 480), f32), pltpu.VMEM((1, width), f32), pltpu.VMEM((1, 160), f32),
+                pltpu.VMEM((width, 480), bf16), pltpu.VMEM((width, 480), f32), pltpu.VMEM((1, width), f32),
+                pltpu.VMEM((1, 160), f32), pltpu.VMEM((8, 1, 480), f32),
             ],
         ),
         out_shape=[
             jax.ShapeDtypeStruct((4, 128, width), bf16),
             jax.ShapeDtypeStruct((4, 128, width), bf16),
-            jax.ShapeDtypeStruct((width, 480), bf16),
-            jax.ShapeDtypeStruct((1, width), f32),
-            jax.ShapeDtypeStruct((1, 160), f32),
+            *[jax.ShapeDtypeStruct((336, 480), bf16)] * 4,
         ],
         compiler_params=limit,
         cost_estimate=pl.CostEstimate(flops=15_000_000_000, bytes_accessed=12_000_000, transcendentals=600_000),
         name="attend_back",
-    )(info, near, far, gain_one, query_mult, w_qkv, pre, grad_att_near, grad_att_far)
-
-    scale_line = lax.dynamic_update_slice(jnp.zeros((1, width), f32), scale_grad, (0, 160 * plane))
-    lines = jnp.concatenate([gain_one_grad, gain_two_grad, scale_line])
-    lines = lines.reshape(3, 4, 8, 40).transpose(1, 2, 0, 3).reshape(4, 2, 480).astype(bf16)
-    lines = jnp.pad(lines, ((0, 0), (0, 6), (0, 0)))
-    send = jnp.concatenate([qkv_grad.reshape(4, 320, 480), lines], axis=1)
-    one = ring_shift(pick(send, (z + 1) % 4), 1)
-    hid = added(hid_near, core_swap(hid_far))
-    kept_a, kept_b, hid_sum, one, later = lax.optimization_barrier((kept_a, kept_b, hid, one, send))
-    three = ring_shift(pick(later, (z + 3) % 4), 3)
-    two = ring_shift(pick(later, (z + 2) % 4), 2)
+    )(info, near, far, gain_one, query_mult, *w_parts, pre, grad_att_near, grad_att_far, gain_two_grad)
+
+    one, three = ring_shift(send[1], 1), ring_shift(send[3], 3)
+    swapped = core_swap(hid_far)
+    hid = [added(hid_near[i], swapped[i]) for i in range(4)]
+    kept_a, kept_b, one, three, later = lax.optimization_barrier((kept_a, kept_b, one, three, send[2]))
+    two = ring_shift(later, 2)
     kept_a, away_a = halves(kept_a, y, 2)
     kept_b, away_b = halves(kept_b, x, 2)
     kept_a = added(kept_a, plane_shift(away_a, 2))
     kept_b = added(kept_b, plane_shift(away_b, 1))
     kept = jnp.concatenate([kept_a, kept_b])
-    hid, kept = lax.optimization_barrier((hid, kept))
-    grad_hid = hid[0].astype(f32)
+    *hid, kept, two = lax.optimization_barrier((*hid, kept, two))
     moved = [plane_shift(hid[step], step) for step in (1, 2, 3)]
-    *moved, three, two = lax.optimization_barrier((*moved, three, two))
-    sums = sum((item.astype(f32) for item in (one, two, three)), pick(send, z).astype(f32)).astype(bf16)
-    lines = jnp.pad(sums[320:322].reshape(8, 1, 120), ((0, 0), (0, 7), (0, 360)))
-    sums = jnp.concatenate([sums[:320].reshape(8, 40, 480), lines], axis=1)
-    for item in moved:
-        grad_hid += item.astype(f32)
-    wide = x_rows.astype(f32)
-    inverse = lax.rsqrt(jnp.mean(wide * wide, axis=1, keepdims=True) + 1e-06)
-    grad_in = (grad_mid + norm_back(grad_hid, wide * inverse, inverse, gain_one)).astype(bf16)
-
+    *moved, mine = lax.optimization_barrier((*moved, send[0]))
+    big_sums = lax.psum_scatter(kept, "z", scatter_dimension=0, tiled=True)[0]
+    grad_home = pl.pallas_call(
+        norm_kernel,
+        in_specs=[smem] + [vmem] * 7,
+        out_specs=[vmem] * 4,
+        out_shape=[jax.ShapeDtypeStruct((4, 8, width), bf16)] * 4,
+        scratch_shapes=[pltpu.VMEM((4, 4, 8, width), f32)],
+        compiler_params=limit,
+        cost_estimate=pl.CostEstimate(flops=2_000_000_000, bytes_accessed=2_500_000, transcendentals=128),
+        name="norm",
+    )(info, hid[0], *moved, x_rows, grad_mid, gain_one)
+    sums = pl.pallas_call(
+        fold_kernel,
+        in_specs=[vmem] * 4,
+        out_specs=vmem,
+        out_shape=jax.ShapeDtypeStruct((8, 48, 480), bf16),
+        scratch_shapes=[pltpu.VMEM((8, 480), f32)],
+        compiler_params=limit,
+        cost_estimate=pl.CostEstimate(flops=2_000_000_000, bytes_accessed=1_600_000, transcendentals=0),
+        name="fold",
+    )(mine, one, two, three)
     sums = lax.all_to_all(sums, ("y", "core", "x"), split_axis=0, concat_axis=0, tiled=True)
-    big_sums = lax.psum_scatter(kept, "z", scatter_dimension=0, tiled=True)[0].astype(f32)
-    qkv_sums = sums[:, :40].reshape(8, 40, 3, 160).transpose(2, 1, 0, 3).reshape(3, 40, width).astype(f32)
+    rows_shape = [jax.ShapeDtypeStruct((40, width), f32)] * 3
+    qkv_sums = pl.pallas_call(
+        spread_kernel, in_specs=[vmem], out_specs=[vmem] * 3, out_shape=rows_shape, compiler_params=limit, name="spread"
+    )(sums)
+    big_sums = pl.pallas_call(
+        widen_kernel, in_specs=[vmem], out_specs=[vmem] * 3, out_shape=rows_shape, compiler_params=limit, name="widen"
+    )(big_sums)
     line_sums = jnp.sum(sums[:, 40, :120].astype(f32), axis=0).reshape(3, 40)
     scale_low = query_scale.astype(bf16).astype(f32)
     scale_sum = LOG2E / math.sqrt(HD) * jax.nn.sigmoid(scale_low) * line_sums[2]
-
-    rows = grad_in.reshape(4, 4, 8, width).transpose(1, 0, 2, 3)
-    grad_home = [pick(rows, z)] + [ring_shift(pick(rows, (z + k) % 4), k) for k in (1, 2, 3)]
+    grad_home = [grad_home[0]] + [ring_shift(grad_home[k], k) for k in (1, 2, 3)]
     grad_home = by_source(grad_home, z, 0).reshape(16, 8, width)
 
     return (

time: 272 us -> 267 us (0.982)
  blocking collectives: 0 us -> 15.6 us
  local copies, waits for them, and re-layouts: 31.5 us -> 18.3 us
  other arithmetic: 29.7 us -> 16.8 us
  starting transfers between devices: 61.3 us -> 54.9 us
  waiting for transfers between devices: 97.1 us -> 103 us
  Pallas kernels: 36.7 us -> 42.3 us
    ppermute x9 -> x12, waiting for transfers between devices: 18.2 us -> 42.2 us  [ring_shift(): return lax.ppermute(value, 'z', [(i, (i + step) % 4) for i in range(4)])]
    ppermute x8, waiting for transfers between devices: 16.6 us -> 32.3 us  [plane_shift(): return lax.ppermute(value, 'x', [(0, 1), (1, 0)])]
    all_to_all x0 -> x1, blocking collectives: none -> 15.6 us  [planes(): lax.all_to_all(qkv, ('y', 'core', 'x'), split_axis=0, concat_axis=0, tile...]
    all_gather x1 -> x0, waiting for transfers between devices: 13.7 us -> none  [planes(): w_qkv = lax.all_gather(qkv, 'z', axis=0, tiled=True)]
    ppermute x8, waiting for transfers between devices: 23.1 us -> 13.3 us  [plane_shift(): return lax.ppermute(value, 'y', [(0, 1), (1, 0)])]
    ppermute x4, waiting for transfers between devices: 12.8 us -> 4.53 us  [plane_shift(): return lax.ppermute(value, ('y', 'x'), [(0, 3), (1, 2), (2, 1), (3, 0)])]
    select_n x0 -> x3, other arithmetic: none -> 7.28 us  [pair(): jnp.where(slot == index, jnp.expand_dims(mine, axis), jnp.expand_dims(oth...]
    another operation x8 -> x2, other arithmetic: 6.29 us -> 0.3 us  [the longest x1 0.18 us: planes(): near = jnp.stack(near)]
  transfers between devices with their start and end apart: 45 -> 47, of which waited for: 25 -> 21; matrix products, arithmetic and copies ran while one was open for 14% -> 7% of each run, Pallas kernels for 10% -> 12%
where the time goes in v5:
time: 267 us; the launch traced here: 266 us
  waiting for transfers between devices  103 us (39%)
  starting transfers between devices  54.9 us (21%)
  Pallas kernels  42.3 us (16%)
  local copies, waits for them, and re-layouts  18.3 us (7%)
  other arithmetic  16.8 us (6%)
  blocking collectives  15.6 us (6%)
  between operations  14.8 us (6%)
    ppermute x12, waiting for transfers between devices, ring_shift(): return lax.ppermute(value, 'z', [(i, (i + step) % 4) for i in range(4)])  42.2 us
    ppermute x8, waiting for transfers between devices, plane_shift(): return lax.ppermute(value, 'x', [(0, 1), (1, 0)])  32.3 us
    ppermute x12, starting transfers between devices, ring_shift(): return lax.ppermute(value, 'z', [(i, (i + step) % 4) for i in range(4)])  17.3 us
    all_to_all x1, blocking collectives, planes(): lax.all_to_all(qkv, ('y', 'core', 'x'), split_axis=0, concat_axis=0, tile...  15.6 us
    ppermute x8, waiting for transfers between devices, plane_shift(): return lax.ppermute(value, 'y', [(0, 1), (1, 0)])  13.3 us
    pallas_call x1, Pallas kernels, planes(): pl.pallas_call(attend_back_kernel, grid_spec=pltpu.PrefetchScalarGridSpec...  12.8 us
    ppermute x10, waiting for transfers between devices, core_swap(): return lax.ppermute(value, 'core', [(0, 1), (1, 0)])  10.4 us
    unnamed x67, local copies, waits for them, and re-layouts  9.93 us
  transfers between devices with their start and end apart: 47, of which 21 were waited for; matrix products, arithmetic and copies ran while one was open for 7% of the time, Pallas kernels for 12%

profile of v5, /device:TPU:0, one launch (start us, length us, event | category | flops | bytes accessed | tf_op | source)
XLA Modules:
  0.0 265.7 jit_solution(1300449411153476289)
XLA Ops:
  7.3 1.0 convert_bitcast_fusion.5
  8.3 1.1 convert_bitcast_fusion.3
  10.4 5.1 %collective-permute-start = (bf16[5,8,1280]{2,1,0:T(8,128)(2,1)S(1)}, bf16[5,8,1280]{2,1,0:T(8,128)(2,1)S(1)}, u32[]{:S(2)}, u32[]{:S(2)}) collective-permute-start(bf16[5,8,1280]{2,1,0:T(8,128)(2,1)S(1)} %get-tuple-element.206), channel_id=1, source_target_pairs={{0,24},{8,0},{16,8},{24,16},{1,25},{9,1},{17,9},{25,17},{2,26},{10... | collective-permute-start | bytes 307208 | tf_op jit(solution)/shard_map/ppermute | solution.py:357
  15.5 1.0 collective-permute-start.2
  17.3 1.5 collective-permute-done
  18.8 6.2 %collective-permute-done.1 = bf16[5,8,1280]{2,1,0:T(8,128)(2,1)S(1)} collective-permute-done((bf16[5,8,1280]{2,1,0:T(8,128)(2,1)S(1)}, bf16[5,8,1280]{2,1,0:T(8,128)(2,1)S(1)}, u32[]{:S(2)}, u32[]{:S(2)}) %collective-permute-start.1) | collective-permute-done | bytes 102432 | tf_op jit(solution)/shard_map/ppermute | solution.py:357
  25.5 3.3 %collective-permute-start.5 = (bf16[136,1280]{1,0:T(8,128)(2,1)S(1)}, bf16[136,1280]{1,0:T(8,128)(2,1)S(1)}, u32[]{:S(2)}, u32[]{:S(2)}) collective-permute-start(bf16[136,1280]{1,0:T(8,128)(2,1)S(1)} %maximum_maximum_fusion), channel_id=1, source_target_pairs={{0,5},{1,4},{4,1},{5,0},{2,7},{3,6},{6,3},{7,2},{8,13},{9,12},{12,... | collective-permute-start | bytes 1044488 | tf_op jit(solution)/shard_map/ppermute | solution.py:349
  30.9 15.6 %all_to_all.20 = bf16[8,40,480]{2,1,0:T(8,128)(2,1)S(1)} all-to-all(bf16[8,40,480]{2,1,0:T(8,128)(2,1)S(1)} %reshape.358), channel_id=1, replica_groups=mesh['z'=4,'y'=2,'core'=2,'x'=2] {'y','core','x'}, dimensions={0} | all-to-all | bytes 614400 | tf_op jit(solution)/shard_map/all_to_all | solution.py:693
  47.0 2.5 fusion.24
  49.4 1.6 collective-permute-start.6
  51.0 1.4 collective-permute-start.7
  53.3 1.8 collective-permute-start.9
  55.4 7.1 %collective-permute-done.10.w_3 = bf16[320,480]{1,0:T(8,128)(2,1)S(1)} collective-permute-done((bf16[320,480]{1,0:T(8,128)(2,1)S(1)}, bf16[320,480]{1,0:T(8,128)(2,1)S(1)}, u32[]{:S(2)}, u32[]{:S(2)}) %collective-permute-start.10) | collective-permute-done | bytes 307232 | tf_op jit(solution)/shard_map/ppermute | solution.py:357
  63.2 10.0 %collective-permute-done.9.w_1 = bf16[320,480]{1,0:T(8,128)(2,1)S(1)} collective-permute-done((bf16[320,480]{1,0:T(8,128)(2,1)S(1)}, bf16[320,480]{1,0:T(8,128)(2,1)S(1)}, u32[]{:S(2)}, u32[]{:S(2)}) %collective-permute-start.9) | collective-permute-done | bytes 307232 | tf_op jit(solution)/shard_map/ppermute | solution.py:357
  74.0 1.4 bitcast_select_fusion.1.near_a
  75.4 2.4 broadcast_select_fusion
  79.7 1.3 collective-permute-start.18
  81.1 6.3 %collective-permute-done.11.w_2 = bf16[320,480]{1,0:T(8,128)(2,1)} collective-permute-done((bf16[320,480]{1,0:T(8,128)(2,1)S(1)}, bf16[320,480]{1,0:T(8,128)(2,1)}, u32[]{:S(2)}, u32[]{:S(2)}) %collective-permute-start.11) | collective-permute-done | bytes 307232 | tf_op jit(solution)/shard_map/ppermute | solution.py:357
  87.4 1.0 copy-done.9
  88.4 1.0 copy-done.12
  89.3 8.5 %attend.1 = (f32[2,4,128,480]{3,2,1,0:T(8,128)}, bf16[4,128,160]{2,1,0:T(8,128)(2,1)S(1)}, bf16[4,128,160]{2,1,0:T(8,128)(2,1)S(1)}) custom-call(s32[6]{0:T(128)S(1)} %pad_add_fusion.info_ref, bf16[4,136,1280]{2,1,0:T(8,128)(2,1)S(1)} %pad_maximum_fusion.near_ref, bf16[4,136,1280]{2,1,0:T(8,128)(2,1)} %collective-permute-done.8.far_ref, ...), custom_call_target="tpu_custom_call" | custom-call | flops 8999999488 | bytes 8000000 | tf_op jit(solution)/shard_map/attend/pallas_call | solution.py:721
  98.3 2.4 collective-permute-done.12
  100.9 3.9 %all-to-all-start.1 = ((bf16[4,4,8,1280]{3,2,1,0:T(8,128)(2,1)}), bf16[4,4,8,1280]{3,2,1,0:T(8,128)(2,1)S(1)}, u32[]{:S(2)}, u32[]{:S(2)}) async-start(bf16[4,4,8,1280]{3,2,1,0:T(8,128)(2,1)} %bitcast.133), calls=%async_computation.1 | async-start | bytes 655360 | tf_op jit(solution)/shard_map/all_to_all | solution.py:747
  104.8 1.0 collective-permute-start.15
  105.9 1.0 collective-permute-start.14
  106.9 4.5 %collective-permute-done.15 = bf16[2,128,160]{2,1,0:T(8,128)(2,1)S(1)} collective-permute-done((bf16[2,128,160]{2,1,0:T(8,128)(2,1)S(1)}, bf16[2,128,160]{2,1,0:T(8,128)(2,1)S(1)}, u32[]{:S(2)}, u32[]{:S(2)}) %collective-permute-start.15) | collective-permute-done | bytes 81952 | tf_op jit(solution)/shard_map/ppermute | solution.py:349
  111.9 2.2 collective-permute-done.14
  114.1 2.3 collective-permute-done.13
  117.2 1.3 collective-permute-done.19.far_atts
  119.0 3.4 %bitcast_select_fusion.all_b = bf16[2,3,2,80,1280]{4,3,2,1,0:T(8,128)(2,1)} fusion(pred[80]{0:T(512)(128)(4,1)S(1)} %broadcast_in_dim.341, bf16[2,3,2,40,1280]{4,3,2,1,0:T(8,128)(2,1)} %collective-permute-done.18, bf16[2,3,2,40,1280]{4,3,2,1,0:T(8,128)(2,1)} %broadcast_select_fusion), kind=kLoop, calls=%fused_computation.2 | loop fusion | flops 1228800 | bytes 4915280 | tf_op jit(solution)/shard_map/jit(_where)/select_n | solution.py:379
  123.0 6.2 %collective-permute-done.21.far_across_a = bf16[2,3,80,1280]{3,2,1,0:T(8,128)(2,1)} collective-permute-done((bf16[2,3,80,1280]{3,2,1,0:T(8,128)(2,1)}, bf16[2,3,80,1280]{3,2,1,0:T(8,128)(2,1)}, u32[]{:S(2)}, u32[]{:S(2)}) %collective-permute-start.21) | collective-permute-done | bytes 1228832 | tf_op jit(solution)/shard_map/ppermute | solution.py:353
  129.2 9.6 %feed.1 = (bf16[4,4,8,1280]{3,2,1,0:T(8,128)(2,1)}, bf16[4,128,1280]{2,1,0:T(8,128)(2,1)}, f32[128,1280]{1,0:T(8,128)S(1)}, bf16[2,128,160]{2,1,0:T(8,128)(2,1)S...) custom-call(s32[6]{0:T(128)S(1)} %pad_add_fusion.info_ref, ...), custom_call_target="tpu_custom_call" | custom-call | flops 12000000000 | bytes 13000000 | tf_op jit(solution)/shard_map/feed/pallas_call | solution.py:763
  140.4 4.9 %all-to-all-start.2 = ((bf16[4,4,8,1280]{3,2,1,0:T(8,128)(2,1)}), bf16[4,4,8,1280]{3,2,1,0:T(8,128)(2,1)}, u32[]{:S(2)}, u32[]{:S(2)}) async-start(bf16[4,4,8,1280]{3,2,1,0:T(8,128)(2,1)} %get-tuple-element.138), calls=%async_computation.2 | async-start | bytes 655360 | tf_op jit(solution)/shard_map/all_to_all | solution.py:781
  145.3 1.1 collective-permute-start.25
  146.4 1.9 collective-permute-start.26
  148.3 5.0 %collective-permute-done.25 = bf16[2,128,160]{2,1,0:T(8,128)(2,1)S(1)} collective-permute-done((bf16[2,128,160]{2,1,0:T(8,128)(2,1)S(1)}, bf16[2,128,160]{2,1,0:T(8,128)(2,1)S(1)}, u32[]{:S(2)}, u32[]{:S(2)}) %collective-permute-start.25) | collective-permute-done | bytes 81952 | tf_op jit(solution)/shard_map/ppermute | solution.py:348
  154.6 7.5 %grads.1 = (bf16[2,3,2,80,1280]{4,3,2,1,0:T(8,128)(2,1)}, bf16[2,3,80,1280]{3,2,1,0:T(8,128)(2,1)S(1)}, bf16[2,3,80,1280]{3,2,1,0:T(8,128)(2,1)}) custom-call(s32[6]{0:T(128)S(1)} %pad_add_fusion.info_ref, bf16[4,128,1280]{2,1,0:T(8,128)(2,1)} %get-tuple-element.128.pack_ref, bf16[4,128,1280]{2,1,0:T(8,128)(2,1)} %collective-permute-done.23.far_pack, ...), custom_call_target="tpu_custom_call" | custom-call | flops 6000000000 | bytes 8000000 | tf_op jit(solution)/shard_map/grads/pallas_call | solution.py:786
  162.9 1.2 collective-permute-start.30
  164.0 1.8 fusion.23
  167.1 12.8 %attend_back.1 = (bf16[4,128,1280]{2,1,0:T(8,128)(2,1)}, bf16[4,128,1280]{2,1,0:T(8,128)(2,1)}, bf16[336,480]{1,0:T(8,128)(2,1)S(1)}, bf16[336,480]{1,0:T(8,128)...) custom-call(s32[6]{0:T(128)S(1)} %pad_add_fusion.info_ref, bf16[4,136,1280]{2,1,0:T(8,128)(2,1)} %copy-done, ...), custom_call_target="tpu_custom_call" | custom-call | flops 15000000512 | bytes 12000000 | tf_op jit(solution)/shard_map/attend_back/pallas_call | solution.py:810
  179.9 1.7 collective-permute-start.31
  181.6 2.2 collective-permute-start.32
  183.8 11.5 %collective-permute-done.29 = bf16[2,3,2,40,1280]{4,3,1,0,2:T(8,128)(2,1)S(1)} collective-permute-done((bf16[2,3,2,40,1280]{4,3,1,0,2:T(8,128)(2,1)S(1)}, bf16[2,3,2,40,1280]{4,3,1,0,2:T(8,128)(2,1)S(1)}, u32[]{:S(2)}, u32[]{:S(2)}) %collective-permute-start.29) | collective-permute-done | bytes 1228832 | tf_op jit(solution)/shard_map/ppermute | solution.py:346
  196.0 2.9 %collective-permute-done.32.part_3 = bf16[336,480]{1,0:T(8,128)(2,1)S(1)} collective-permute-done((bf16[336,480]{1,0:T(8,128)(2,1)S(1)}, bf16[336,480]{1,0:T(8,128)(2,1)S(1)}, u32[]{:S(2)}, u32[]{:S(2)}) %collective-permute-start.32) | collective-permute-done | bytes 322592 | tf_op jit(solution)/shard_map/ppermute | solution.py:357
  198.9 1.0 collective-permute-start.35
  201.1 1.5 collective-permute-start.33
  202.6 1.1 fusion.6
  203.7 11.2 %collective-permute-done.34 = bf16[2,3,40,1280]{3,2,1,0:T(8,128)(2,1)S(1)} collective-permute-done((bf16[2,3,40,1280]{3,2,1,0:T(8,128)(2,1)S(1)}, bf16[2,3,40,1280]{3,2,1,0:T(8,128)(2,1)S(1)}, u32[]{:S(2)}, u32[]{:S(2)}) %collective-permute-start.34) | collective-permute-done | bytes 614432 | tf_op jit(solution)/shard_map/ppermute | solution.py:346
  215.7 1.1 pad_maximum_fusion.1
  216.9 1.4 collective-permute-start.36
  218.3 1.0 collective-permute-start.37
  219.3 1.1 collective-permute-start.38
  220.4 7.4 %collective-permute-done.36.hid_1 = bf16[128,1280]{1,0:T(8,128)(2,1)S(1)} collective-permute-done((bf16[128,1280]{1,0:T(8,128)(2,1)}, bf16[128,1280]{1,0:T(8,128)(2,1)S(1)}, u32[]{:S(2)}, u32[]{:S(2)}) %collective-permute-start.36) | collective-permute-done | bytes 327712 | tf_op jit(solution)/shard_map/ppermute | solution.py:346
  227.8 5.8 %collective-permute-done.37.hid_2 = bf16[128,1280]{1,0:T(8,128)(2,1)S(1)} collective-permute-done((bf16[128,1280]{1,0:T(8,128)(2,1)}, bf16[128,1280]{1,0:T(8,128)(2,1)S(1)}, u32[]{:S(2)}, u32[]{:S(2)}) %collective-permute-start.37) | collective-permute-done | bytes 327712 | tf_op jit(solution)/shard_map/ppermute | solution.py:348
  233.6 1.1 fold.1
  234.7 3.5 %all-to-all-start.3 = ((bf16[8,48,480]{2,1,0:T(8,128)(2,1)}), bf16[8,48,480]{2,1,0:T(8,128)(2,1)S(1)}, u32[]{:S(2)}, u32[]{:S(2)}) async-start(bf16[8,48,480]{2,1,0:T(8,128)(2,1)} %fold.1), calls=%async_computation.3 | async-start | bytes 786432 | tf_op jit(solution)/shard_map/all_to_all | solution.py:873
  238.2 1.1 copy-done.19
  239.3 1.0 norm.1
  240.3 2.8 %collective-permute-start.39 = (bf16[4,8,1280]{2,1,0:T(8,128)(2,1)S(1)}, bf16[4,8,1280]{2,1,0:T(8,128)(2,1)S(1)}, u32[]{:S(2)}, u32[]{:S(2)}) collective-permute-start(bf16[4,8,1280]{2,1,0:T(8,128)(2,1)S(1)} %get-tuple-element.164), channel_id=1, source_target_pairs={{0,24},{8,0},{16,8},{24,16},{1,25},{9,1},{17,9},{25,17},{2,26},{10... | collective-permute-start | bytes 245768 | tf_op jit(solution)/shard_map/ppermute | solution.py:357
  243.1 1.0 collective-permute-start.41
  244.6 1.8 collective-permute-done.39
  246.4 6.5 %collective-permute-done.40 = bf16[4,8,1280]{2,1,0:T(8,128)(2,1)S(1)} collective-permute-done((bf16[4,8,1280]{2,1,0:T(8,128)(2,1)S(1)}, bf16[4,8,1280]{2,1,0:T(8,128)(2,1)S(1)}, u32[]{:S(2)}, u32[]{:S(2)}) %collective-permute-start.40) | collective-permute-done | bytes 81952 | tf_op jit(solution)/shard_map/ppermute | solution.py:357
  255.3 1.0 copy-done.5
  257.1 1.7 copy.66
  (198 shorter events, 23.3 us)
Async XLA Ops:
  7.2 3.0 %copy-start.28 = (f32[40]{0:T(128)S(1)}, f32[40]{0:T(128)}, u32[]{:S(2)}) copy-start(f32[40]{0:T(128)} %param.25) | copy-start | bytes 484
  7.2 3.1 %copy-start.24 = (bf16[16,8,1280]{2,1,0:T(8,128)(2,1)S(1)}, bf16[16,8,1280]{2,1,0:T(8,128)(2,1)}, u32[]{:S(2)}) copy-start(bf16[16,8,1280]{2,1,0:T(8,128)(2,1)} %param.15) | copy-start | bytes 983044
  7.2 39.6 %all-gather.2.cloned.1.call-start = ((), (), s32[]{:S(2)}) async-start(), calls=%async_computation.5 | async-start | bytes 1536000 | tf_op jit(solution)/shard_map/all_gather | solution.py:687
  9.3 7.8 %copy-start.25 = (f32[40,1280]{1,0:T(8,128)S(1)}, f32[40,1280]{1,0:T(8,128)}, u32[]{:S(2)}) copy-start(f32[40,1280]{1,0:T(8,128)} %param.17) | copy-start | bytes 614404
  9.3 7.9 %copy-start.26 = (f32[40,1280]{1,0:T(8,128)S(1)}, f32[40,1280]{1,0:T(8,128)}, u32[]{:S(2)}) copy-start(f32[40,1280]{1,0:T(8,128)} %param.19) | copy-start | bytes 614404
  9.3 7.9 %copy-start.27 = (f32[40,1280]{1,0:T(8,128)S(1)}, f32[40,1280]{1,0:T(8,128)}, u32[]{:S(2)}) copy-start(f32[40,1280]{1,0:T(8,128)} %param.18) | copy-start | bytes 614404
  10.4 8.4 %collective-permute-start = (bf16[5,8,1280]{2,1,0:T(8,128)(2,1)S(1)}, bf16[5,8,1280]{2,1,0:T(8,128)(2,1)S(1)}, u32[]{:S(2)}, u32[]{:S(2)}) collective-permute-start(bf16[5,8,1280]{2,1,0:T(8,128)(2,1)S(1)} %get-tuple-element.206), channel_id=1, source_target_pairs={{0,24},{8,0},{16,8},{24,16},{1,25},{9,1},{17,9},{25,17},{2,26},{10... | collective-permute-start | bytes 307208 | tf_op jit(solution)/shard_map/ppermute | solution.py:357
  15.5 9.5 %collective-permute-start.1 = (bf16[5,8,1280]{2,1,0:T(8,128)(2,1)S(1)}, bf16[5,8,1280]{2,1,0:T(8,128)(2,1)S(1)}, u32[]{:S(2)}, u32[]{:S(2)}) collective-permute-start(bf16[5,8,1280]{2,1,0:T(8,128)(2,1)S(1)} %get-tuple-element.207), channel_id=1, source_target_pairs={{0,16},{8,24},{16,0},{24,8},{1,17},{9,25},{17,1},{25,9},{2,18},{10... | collective-permute-start | bytes 307208 | tf_op jit(solution)/shard_map/ppermute | solution.py:357
  15.5 9.5 %collective-permute-start.2 = (bf16[5,8,1280]{2,1,0:T(8,128)(2,1)S(1)}, bf16[5,8,1280]{2,1,0:T(8,128)(2,1)S(1)}, u32[]{:S(2)}, u32[]{:S(2)}) collective-permute-start(bf16[5,8,1280]{2,1,0:T(8,128)(2,1)S(1)} %get-tuple-element.208), channel_id=1, source_target_pairs={{0,8},{8,16},{16,24},{24,0},{1,9},{9,17},{17,25},{25,1},{2,10},{10... | collective-permute-start | bytes 307208 | tf_op jit(solution)/shard_map/ppermute | solution.py:357
  25.5 21.0 %collective-permute-start.5 = (bf16[136,1280]{1,0:T(8,128)(2,1)S(1)}, bf16[136,1280]{1,0:T(8,128)(2,1)S(1)}, u32[]{:S(2)}, u32[]{:S(2)}) collective-permute-start(bf16[136,1280]{1,0:T(8,128)(2,1)S(1)} %maximum_maximum_fusion), channel_id=1, source_target_pairs={{0,5},{1,4},{4,1},{5,0},{2,7},{3,6},{6,3},{7,2},{8,13},{9,12},{12,... | collective-permute-start | bytes 1044488 | tf_op jit(solution)/shard_map/ppermute | solution.py:349
  28.8 17.7 %collective-permute-start.4 = (bf16[136,1280]{1,0:T(8,128)(2,1)S(1)}, bf16[136,1280]{1,0:T(8,128)(2,1)S(1)}, u32[]{:S(2)}, u32[]{:S(2)}) collective-permute-start(bf16[136,1280]{1,0:T(8,128)(2,1)S(1)} %maximum_maximum_fusion), channel_id=1, source_target_pairs={{0,4},{4,0},{1,5},{5,1},{2,6},{6,2},{3,7},{7,3},{8,12},{12,8},{9,1... | collective-permute-start | bytes 1044488 | tf_op jit(solution)/shard_map/ppermute | solution.py:348
  28.8 17.7 %collective-permute-start.3 = (bf16[136,1280]{1,0:T(8,128)(2,1)S(1)}, bf16[136,1280]{1,0:T(8,128)(2,1)S(1)}, u32[]{:S(2)}, u32[]{:S(2)}) collective-permute-start(bf16[136,1280]{1,0:T(8,128)(2,1)S(1)} %maximum_maximum_fusion), channel_id=1, source_target_pairs={{0,1},{1,0},{2,3},{3,2},{4,5},{5,4},{6,7},{7,6},{8,9},{9,8},{10,11... | collective-permute-start | bytes 1044488 | tf_op jit(solution)/shard_map/ppermute | solution.py:346
  46.5 40.9 %copy-start.1 = (bf16[8,40,480]{2,1,0:T(8,128)(2,1)}, bf16[8,40,480]{2,1,0:T(8,128)(2,1)S(1)}, u32[]{:S(2)}) copy-start(bf16[8,40,480]{2,1,0:T(8,128)(2,1)S(1)} %all_to_all.20) | copy-start | bytes 921604
  46.7 40.7 %copy-start = (bf16[4,136,1280]{2,1,0:T(8,128)(2,1)}, bf16[4,136,1280]{2,1,0:T(8,128)(2,1)S(1)}, u32[]{:S(2)}) copy-start(bf16[4,136,1280]{2,1,0:T(8,128)(2,1)S(1)} %pad_maximum_fusion.near_ref) | copy-start | bytes 4177924
  46.7 8.4 %copy-start.31 = (s32[16]{0:T(128)S(1)}, s32[16]{0:T(128)}, u32[]{:S(2)}) copy-start(s32[16]{0:T(128)} %param.27) | copy-start | bytes 196
  46.7 8.4 %copy-start.32 = (s32[16]{0:T(128)S(1)}, s32[16]{0:T(128)}, u32[]{:S(2)}) copy-start(s32[16]{0:T(128)} %param.26) | copy-start | bytes 196
  46.8 31.0 %collective-permute-start.8 = (bf16[4,136,1280]{2,1,0:T(8,128)(2,1)S(1)}, bf16[4,136,1280]{2,1,0:T(8,128)(2,1)}, u32[]{:S(2)}, u32[]{:S(2)}) collective-permute-start(bf16[4,136,1280]{2,1,0:T(8,128)(2,1)S(1)} %pad_maximum_fusion.near_ref), channel_id=1, source_target_pairs={{0,2},{2,0},{1,3},{3,1},{4,6},{6,4},{5,7},{7,5},{8,10},{10,8},{9,1... | collective-permute-start | bytes 4177928 | tf_op jit(solution)/shard_map/ppermute | solution.py:353
  49.4 24.5 %copy-start.22 = (bf16[2,3,40,1280]{3,2,1,0:T(8,128)(2,1)}, bf16[2,3,40,1280]{3,2,1,0:T(8,128)(2,1)S(1)}, u32[]{:S(2)}) copy-start(bf16[2,3,40,1280]{3,2,1,0:T(8,128)(2,1)S(1)} %get-tuple-element.186) | copy-start | bytes 1843204
  49.4 24.5 %collective-permute-start.6 = (bf16[2,3,40,1280]{3,2,1,0:T(8,128)(2,1)S(1)}, bf16[2,3,40,1280]{3,2,1,0:T(8,128)(2,1)}, u32[]{:S(2)}, u32[]{:S(2)}) collective-permute-start(bf16[2,3,40,1280]{3,2,1,0:T(8,128)(2,1)S(1)} %get-tuple-element.186), channel_id=1, source_target_pairs={{0,1},{1,0},{2,3},{3,2},{4,5},{5,4},{6,7},{7,6},{8,9},{9,8},{10,11... | collective-permute-start | bytes 1843208 | tf_op jit(solution)/shard_map/ppermute | solution.py:346
  51.0 24.3 %collective-permute-start.7 = (bf16[2,3,40,1280]{3,2,1,0:T(8,128)(2,1)}, bf16[2,3,40,1280]{3,2,1,0:T(8,128)(2,1)}, u32[]{:S(2)}, u32[]{:S(2)}) collective-permute-start(bf16[2,3,40,1280]{3,2,1,0:T(8,128)(2,1)} %get-tuple-element.185), channel_id=1, source_target_pairs={{0,4},{4,0},{1,5},{5,1},{2,6},{6,2},{3,7},{7,3},{8,12},{12,8},{9,1... | collective-permute-start | bytes 1843208 | tf_op jit(solution)/shard_map/ppermute | solution.py:348
  52.6 9.9 %collective-permute-start.10 = (bf16[320,480]{1,0:T(8,128)(2,1)S(1)}, bf16[320,480]{1,0:T(8,128)(2,1)S(1)}, u32[]{:S(2)}, u32[]{:S(2)}) collective-permute-start(bf16[320,480]{1,0:T(8,128)(2,1)S(1)} %bitcast.113), channel_id=1, source_target_pairs={{0,24},{8,0},{16,8},{24,16},{1,25},{9,1},{17,9},{25,17},{2,26},{10... | collective-permute-start | bytes 921608 | tf_op jit(solution)/shard_map/ppermute | solution.py:357
  53.3 19.9 %collective-permute-start.9 = (bf16[320,480]{1,0:T(8,128)(2,1)S(1)}, bf16[320,480]{1,0:T(8,128)(2,1)S(1)}, u32[]{:S(2)}, u32[]{:S(2)}) collective-permute-start(bf16[320,480]{1,0:T(8,128)(2,1)S(1)} %bitcast.114), channel_id=1, source_target_pairs={{0,8},{8,16},{16,24},{24,0},{1,9},{9,17},{17,25},{25,1},{2,10},{10... | collective-permute-start | bytes 921608 | tf_op jit(solution)/shard_map/ppermute | solution.py:357
  73.9 13.5 %collective-permute-start.11 = (bf16[320,480]{1,0:T(8,128)(2,1)S(1)}, bf16[320,480]{1,0:T(8,128)(2,1)}, u32[]{:S(2)}, u32[]{:S(2)}) collective-permute-start(bf16[320,480]{1,0:T(8,128)(2,1)S(1)} %bitcast.115), channel_id=1, source_target_pairs={{0,16},{8,24},{16,0},{24,8},{1,17},{9,25},{17,1},{25,9},{2,18},{10... | collective-permute-start | bytes 921608 | tf_op jit(solution)/shard_map/ppermute | solution.py:357
  79.0 40.0 %collective-permute-start.17 = (bf16[2,3,80,1280]{3,2,1,0:T(8,128)(2,1)S(1)}, bf16[2,3,80,1280]{3,2,1,0:T(8,128)(2,1)}, u32[]{:S(2)}, u32[]{:S(2)}) collective-permute-start(bf16[2,3,80,1280]{3,2,1,0:T(8,128)(2,1)S(1)} %bitcast_select_fusion.1.near_a), channel_id=1, source_target_pairs={{0,4},{4,0},{1,5},{5,1},{2,6},{6,2},{3,7},{7,3},{8,12},{12,8},{9,1... | collective-permute-start | bytes 3686408 | tf_op jit(solution)/shard_map/ppermute | solution.py:348
  79.7 39.2 %collective-permute-start.18 = (bf16[2,3,2,40,1280]{4,3,2,1,0:T(8,128)(2,1)}, bf16[2,3,2,40,1280]{4,3,2,1,0:T(8,128)(2,1)}, u32[]{:S(2)}, u32[]{:S(2)}) collective-permute-start(bf16[2,3,2,40,1280]{4,3,2,1,0:T(8,128)(2,1)} %broadcast_select_fusion), channel_id=1, source_target_pairs={{0,1},{1,0},{2,3},{3,2},{4,5},{5,4},{6,7},{7,6},{8,9},{9,8},{10,11... | collective-permute-start | bytes 3686408 | tf_op jit(solution)/shard_map/ppermute | solution.py:346
  97.8 21.1 %collective-permute-start.16 = (bf16[2,3,80,1280]{3,2,1,0:T(8,128)(2,1)S(1)}, bf16[2,3,80,1280]{3,2,1,0:T(8,128)(2,1)}, u32[]{:S(2)}, u32[]{:S(2)}) collective-permute-start(bf16[2,3,80,1280]{3,2,1,0:T(8,128)(2,1)S(1)} %bitcast_select_fusion.1.near_a), channel_id=1, source_target_pairs={{0,2},{2,0},{1,3},{3,1},{4,6},{6,4},{5,7},{7,5},{8,10},{10,8},{9,1... | collective-permute-start | bytes 3686408 | tf_op jit(solution)/shard_map/ppermute | solution.py:353
  97.9 2.9 %collective-permute-start.12 = (bf16[4,128,160]{2,1,0:T(8,128)(2,1)S(1)}, bf16[4,128,160]{2,1,0:T(8,128)(2,1)S(1)}, u32[]{:S(2)}, u32[]{:S(2)}) collective-permute-start(bf16[4,128,160]{2,1,0:T(8,128)(2,1)S(1)} %get-tuple-element.118), channel_id=1, source_target_pairs={{0,2},{2,0},{1,3},{3,1},{4,6},{6,4},{5,7},{7,5},{8,10},{10,8},{9,1... | collective-permute-start | bytes 491528 | tf_op jit(solution)/shard_map/ppermute | solution.py:353
  100.9 15.7 %all-to-all-start.1 = ((bf16[4,4,8,1280]{3,2,1,0:T(8,128)(2,1)}), bf16[4,4,8,1280]{3,2,1,0:T(8,128)(2,1)S(1)}, u32[]{:S(2)}, u32[]{:S(2)}) async-start(bf16[4,4,8,1280]{3,2,1,0:T(8,128)(2,1)} %bitcast.133), calls=%async_computation.1 | async-start | bytes 655360 | tf_op jit(solution)/shard_map/all_to_all | solution.py:747
  104.8 6.6 %collective-permute-start.15 = (bf16[2,128,160]{2,1,0:T(8,128)(2,1)S(1)}, bf16[2,128,160]{2,1,0:T(8,128)(2,1)S(1)}, u32[]{:S(2)}, u32[]{:S(2)}) collective-permute-start(bf16[2,128,160]{2,1,0:T(8,128)(2,1)S(1)} %get-tuple-element.188), channel_id=1, source_target_pairs={{0,5},{1,4},{4,1},{5,0},{2,7},{3,6},{6,3},{7,2},{8,13},{9,12},{12,... | collective-permute-start | bytes 245768 | tf_op jit(solution)/shard_map/ppermute | solution.py:349
  105.9 8.3 %collective-permute-start.14 = (bf16[2,128,160]{2,1,0:T(8,128)(2,1)S(1)}, bf16[2,128,160]{2,1,0:T(8,128)(2,1)S(1)}, u32[]{:S(2)}, u32[]{:S(2)}) collective-permute-start(bf16[2,128,160]{2,1,0:T(8,128)(2,1)S(1)} %get-tuple-element.189), channel_id=1, source_target_pairs={{0,4},{4,0},{1,5},{5,1},{2,6},{6,2},{3,7},{7,3},{8,12},{12,8},{9,1... | collective-permute-start | bytes 245768 | tf_op jit(solution)/shard_map/ppermute | solution.py:348
  111.4 5.0 %collective-permute-start.13 = (bf16[2,128,160]{2,1,0:T(8,128)(2,1)S(1)}, bf16[2,128,160]{2,1,0:T(8,128)(2,1)S(1)}, u32[]{:S(2)}, u32[]{:S(2)}) collective-permute-start(bf16[2,128,160]{2,1,0:T(8,128)(2,1)S(1)} %get-tuple-element.190), channel_id=1, source_target_pairs={{0,1},{1,0},{2,3},{3,2},{4,5},{5,4},{6,7},{7,6},{8,9},{9,8},{10,11... | collective-permute-start | bytes 245768 | tf_op jit(solution)/shard_map/ppermute | solution.py:346
  116.5 2.0 collective-permute-start.19
  116.6 12.6 %copy-start.3 = (bf16[4,4,8,1280]{3,2,1,0:T(8,128)(2,1)}, bf16[4,4,8,1280]{3,2,1,0:T(8,128)(2,1)S(1)}, u32[]{:S(2)}) copy-start(bf16[4,4,8,1280]{3,2,1,0:T(8,128)(2,1)S(1)} %copy.47) | copy-start | bytes 983044
  116.6 2.3 collective-permute-start.20
  118.5 3.9 %copy-start.6 = (bf16[4,2,128,160]{3,2,1,0:T(8,128)(2,1)}, bf16[4,2,128,160]{3,2,1,0:T(8,128)(2,1)S(1)}, u32[]{:S(2)}) copy-start(bf16[4,2,128,160]{3,2,1,0:T(8,128)(2,1)S(1)} %collective-permute-done.19.far_atts) | copy-start | bytes 983044
  118.9 3.5 %copy-start.14 = (bf16[128,1280]{1,0:T(8,128)(2,1)}, bf16[128,1280]{1,0:T(8,128)(2,1)S(1)}, u32[]{:S(2)}) copy-start(bf16[128,1280]{1,0:T(8,128)(2,1)S(1)} %collective-permute-done.20.far_cot) | copy-start | bytes 983044
  122.4 6.8 %collective-permute-start.22 = (bf16[2,3,2,80,1280]{4,3,2,1,0:T(8,128)(2,1)}, bf16[2,3,2,80,1280]{4,3,2,1,0:T(8,128)(2,1)}, u32[]{:S(2)}, u32[]{:S(2)}) collective-permute-start(bf16[2,3,2,80,1280]{4,3,2,1,0:T(8,128)(2,1)} %bitcast_select_fusion.all_b), channel_id=1, source_target_pairs={{0,2},{2,0},{1,3},{3,1},{4,6},{6,4},{5,7},{7,5},{8,10},{10,8},{9,1... | collective-permute-start | bytes 7372808 | tf_op jit(solution)/shard_map/ppermute | solution.py:353
  122.5 6.6 %collective-permute-start.21 = (bf16[2,3,80,1280]{3,2,1,0:T(8,128)(2,1)}, bf16[2,3,80,1280]{3,2,1,0:T(8,128)(2,1)}, u32[]{:S(2)}, u32[]{:S(2)}) collective-permute-start(bf16[2,3,80,1280]{3,2,1,0:T(8,128)(2,1)} %collective-permute-done.17.across_a), channel_id=1, source_target_pairs={{0,2},{2,0},{1,3},{3,1},{4,6},{6,4},{5,7},{7,5},{8,10},{10,8},{9,1... | collective-permute-start | bytes 3686408 | tf_op jit(solution)/shard_map/ppermute | solution.py:353
  139.7 13.9 %collective-permute-start.23 = (bf16[4,128,1280]{2,1,0:T(8,128)(2,1)}, bf16[4,128,1280]{2,1,0:T(8,128)(2,1)}, u32[]{:S(2)}, u32[]{:S(2)}) collective-permute-start(bf16[4,128,1280]{2,1,0:T(8,128)(2,1)} %get-tuple-element.128.pack_ref), channel_id=1, source_target_pairs={{0,2},{2,0},{1,3},{3,1},{4,6},{6,4},{5,7},{7,5},{8,10},{10,8},{9,1... | collective-permute-start | bytes 3932168 | tf_op jit(solution)/shard_map/ppermute | solution.py:353
  139.8 8.5 %collective-permute-start.24 = (bf16[2,128,160]{2,1,0:T(8,128)(2,1)S(1)}, bf16[2,128,160]{2,1,0:T(8,128)(2,1)S(1)}, u32[]{:S(2)}, u32[]{:S(2)}) collective-permute-start(bf16[2,128,160]{2,1,0:T(8,128)(2,1)S(1)} %get-tuple-element.135), channel_id=1, source_target_pairs={{0,1},{1,0},{2,3},{3,2},{4,5},{5,4},{6,7},{7,6},{8,9},{9,8},{10,11... | collective-permute-start | bytes 245768 | tf_op jit(solution)/shard_map/ppermute | solution.py:346
  140.4 13.2 %copy-start.4 = (bf16[4,4,8,1280]{3,2,1,0:T(8,128)(2,1)S(1)}, bf16[4,4,8,1280]{3,2,1,0:T(8,128)(2,1)}, u32[]{:S(2)}) copy-start(bf16[4,4,8,1280]{3,2,1,0:T(8,128)(2,1)} %copy-done.3) | copy-start | bytes 983044
  140.4 13.2 %copy-start.7 = (bf16[4,2,128,160]{3,2,1,0:T(8,128)(2,1)S(1)}, bf16[4,2,128,160]{3,2,1,0:T(8,128)(2,1)}, u32[]{:S(2)}) copy-start(bf16[4,2,128,160]{3,2,1,0:T(8,128)(2,1)} %copy-done.6) | copy-start | bytes 983044
  140.4 22.5 %all-to-all-start.2 = ((bf16[4,4,8,1280]{3,2,1,0:T(8,128)(2,1)}), bf16[4,4,8,1280]{3,2,1,0:T(8,128)(2,1)}, u32[]{:S(2)}, u32[]{:S(2)}) async-start(bf16[4,4,8,1280]{3,2,1,0:T(8,128)(2,1)} %get-tuple-element.138), calls=%async_computation.2 | async-start | bytes 655360 | tf_op jit(solution)/shard_map/all_to_all | solution.py:781
  145.3 110.0 %reduce-scatter.2.cloned.1.call-start = ((), (), s32[]{:S(2)}) async-start(), calls=%async_computation.6 | async-start | bytes 1536000 | tf_op jit(solution)/shard_map/reduce_scatter | solution.py:852
  145.3 8.0 %collective-permute-start.25 = (bf16[2,128,160]{2,1,0:T(8,128)(2,1)S(1)}, bf16[2,128,160]{2,1,0:T(8,128)(2,1)S(1)}, u32[]{:S(2)}, u32[]{:S(2)}) collective-permute-start(bf16[2,128,160]{2,1,0:T(8,128)(2,1)S(1)} %get-tuple-element.136), channel_id=1, source_target_pairs={{0,4},{4,0},{1,5},{5,1},{2,6},{6,2},{3,7},{7,3},{8,12},{12,8},{9,1... | collective-permute-start | bytes 245768 | tf_op jit(solution)/shard_map/ppermute | solution.py:348
  146.4 7.0 %collective-permute-start.26 = (bf16[2,128,160]{2,1,0:T(8,128)(2,1)S(1)}, bf16[2,128,160]{2,1,0:T(8,128)(2,1)S(1)}, u32[]{:S(2)}, u32[]{:S(2)}) collective-permute-start(bf16[2,128,160]{2,1,0:T(8,128)(2,1)S(1)} %get-tuple-element.137), channel_id=1, source_target_pairs={{0,5},{1,4},{4,1},{5,0},{2,7},{3,6},{6,3},{7,2},{8,13},{9,12},{12,... | collective-permute-start | bytes 245768 | tf_op jit(solution)/shard_map/ppermute | solution.py:349
  153.5 8.7 %collective-permute-start.27 = (bf16[4,128,160]{2,1,0:T(8,128)(2,1)S(1)}, bf16[4,128,160]{2,1,0:T(8,128)(2,1)S(1)}, u32[]{:S(2)}, u32[]{:S(2)}) collective-permute-start(bf16[4,128,160]{2,1,0:T(8,128)(2,1)S(1)} %pad_maximum_fusion.7), channel_id=1, source_target_pairs={{0,2},{2,0},{1,3},{3,1},{4,6},{6,4},{5,7},{7,5},{8,10},{10,8},{9,1... | collective-permute-start | bytes 491528 | tf_op jit(solution)/shard_map/ppermute | solution.py:353
  162.9 32.8 %collective-permute-start.30 = (bf16[2,3,80,1280]{3,2,1,0:T(8,128)(2,1)}, bf16[2,3,80,1280]{3,2,1,0:T(8,128)(2,1)S(1)}, u32[]{:S(2)}, u32[]{:S(2)}) collective-permute-start(bf16[2,3,80,1280]{3,2,1,0:T(8,128)(2,1)} %get-tuple-element.148), channel_id=1, source_target_pairs={{0,4},{4,0},{1,5},{5,1},{2,6},{6,2},{3,7},{7,3},{8,12},{12,8},{9,1... | collective-permute-start | bytes 3686408 | tf_op jit(solution)/shard_map/ppermute | solution.py:348
  166.0 29.2 %collective-permute-start.29 = (bf16[2,3,2,40,1280]{4,3,1,0,2:T(8,128)(2,1)S(1)}, bf16[2,3,2,40,1280]{4,3,1,0,2:T(8,128)(2,1)S(1)}, u32[]{:S(2)}, u32[]{:S(2)}) collective-permute-start(bf16[2,3,2,40,1280]{4,3,1,0,2:T(8,128)(2,1)S(1)} %select_bitcast_fusion), channel_id=1, source_target_pairs={{0,1},{1,0},{2,3},{3,2},{4,5},{5,4},{6,7},{7,6},{8,9},{9,8},{10,11... | collective-permute-start | bytes 3686408 | tf_op jit(solution)/shard_map/ppermute | solution.py:346
  179.9 15.7 %copy-start.20 = (bf16[336,480]{1,0:T(8,128)(2,1)}, bf16[336,480]{1,0:T(8,128)(2,1)S(1)}, u32[]{:S(2)}) copy-start(bf16[336,480]{1,0:T(8,128)(2,1)S(1)} %get-tuple-element.168.part_0) | copy-start | bytes 967684
  179.9 16.1 %collective-permute-start.31 = (bf16[336,480]{1,0:T(8,128)(2,1)S(1)}, bf16[336,480]{1,0:T(8,128)(2,1)S(1)}, u32[]{:S(2)}, u32[]{:S(2)}) collective-permute-start(bf16[336,480]{1,0:T(8,128)(2,1)S(1)} %get-tuple-element.149), channel_id=1, source_target_pairs={{0,8},{8,16},{16,24},{24,0},{1,9},{9,17},{17,25},{25,1},{2,10},{10... | collective-permute-start | bytes 967688 | tf_op jit(solution)/shard_map/ppermute | solution.py:357
  181.6 17.3 %collective-permute-start.32 = (bf16[336,480]{1,0:T(8,128)(2,1)S(1)}, bf16[336,480]{1,0:T(8,128)(2,1)S(1)}, u32[]{:S(2)}, u32[]{:S(2)}) collective-permute-start(bf16[336,480]{1,0:T(8,128)(2,1)S(1)} %get-tuple-element.150), channel_id=1, source_target_pairs={{0,24},{8,0},{16,8},{24,16},{1,25},{9,1},{17,9},{25,17},{2,26},{10... | collective-permute-start | bytes 967688 | tf_op jit(solution)/shard_map/ppermute | solution.py:357
  183.8 18.8 %collective-permute-start.28 = (bf16[4,128,1280]{2,1,0:T(8,128)(2,1)}, bf16[4,128,1280]{2,1,0:T(8,128)(2,1)S(1)}, u32[]{:S(2)}, u32[]{:S(2)}) collective-permute-start(bf16[4,128,1280]{2,1,0:T(8,128)(2,1)} %get-tuple-element.145), channel_id=1, source_target_pairs={{0,2},{2,0},{1,3},{3,1},{4,6},{6,4},{5,7},{7,5},{8,10},{10,8},{9,1... | collective-permute-start | bytes 3932168 | tf_op jit(solution)/shard_map/ppermute | solution.py:353
  198.9 18.0 %collective-permute-start.35 = (bf16[336,480]{1,0:T(8,128)(2,1)S(1)}, bf16[336,480]{1,0:T(8,128)(2,1)S(1)}, u32[]{:S(2)}, u32[]{:S(2)}) collective-permute-start(bf16[336,480]{1,0:T(8,128)(2,1)S(1)} %get-tuple-element.154), channel_id=1, source_target_pairs={{0,16},{8,24},{16,0},{24,8},{1,17},{9,25},{17,1},{25,9},{2,18},{10... | collective-permute-start | bytes 967688 | tf_op jit(solution)/shard_map/ppermute | solution.py:357
  200.0 14.9 %collective-permute-start.34 = (bf16[2,3,40,1280]{3,2,1,0:T(8,128)(2,1)S(1)}, bf16[2,3,40,1280]{3,2,1,0:T(8,128)(2,1)S(1)}, u32[]{:S(2)}, u32[]{:S(2)}) collective-permute-start(bf16[2,3,40,1280]{3,2,1,0:T(8,128)(2,1)S(1)} %select_bitcast_fusion.1), channel_id=1, source_target_pairs={{0,1},{1,0},{2,3},{3,2},{4,5},{5,4},{6,7},{7,6},{8,9},{9,8},{10,11... | collective-permute-start | bytes 1843208 | tf_op jit(solution)/shard_map/ppermute | solution.py:346
  201.1 14.5 %collective-permute-start.33 = (bf16[2,3,40,1280]{3,2,1,0:T(8,128)(2,1)S(1)}, bf16[2,3,40,1280]{3,2,1,0:T(8,128)(2,1)S(1)}, u32[]{:S(2)}, u32[]{:S(2)}) collective-permute-start(bf16[2,3,40,1280]{3,2,1,0:T(8,128)(2,1)S(1)} %select_bitcast_fusion.2), channel_id=1, source_target_pairs={{0,4},{4,0},{1,5},{5,1},{2,6},{6,2},{3,7},{7,3},{8,12},{12,8},{9,1... | collective-permute-start | bytes 1843208 | tf_op jit(solution)/shard_map/ppermute | solution.py:348
  216.9 16.8 %copy-start.21 = (bf16[336,480]{1,0:T(8,128)(2,1)S(1)}, bf16[336,480]{1,0:T(8,128)(2,1)}, u32[]{:S(2)}) copy-start(bf16[336,480]{1,0:T(8,128)(2,1)} %copy-done.20) | copy-start | bytes 967684
  216.9 10.9 %collective-permute-start.36 = (bf16[128,1280]{1,0:T(8,128)(2,1)}, bf16[128,1280]{1,0:T(8,128)(2,1)S(1)}, u32[]{:S(2)}, u32[]{:S(2)}) collective-permute-start(bf16[128,1280]{1,0:T(8,128)(2,1)} %get-tuple-element.156), channel_id=1, source_target_pairs={{0,1},{1,0},{2,3},{3,2},{4,5},{5,4},{6,7},{7,6},{8,9},{9,8},{10,11... | collective-permute-start | bytes 983048 | tf_op jit(solution)/shard_map/ppermute | solution.py:346
  218.3 15.3 %collective-permute-start.37 = (bf16[128,1280]{1,0:T(8,128)(2,1)}, bf16[128,1280]{1,0:T(8,128)(2,1)S(1)}, u32[]{:S(2)}, u32[]{:S(2)}) collective-permute-start(bf16[128,1280]{1,0:T(8,128)(2,1)} %get-tuple-element.157), channel_id=1, source_target_pairs={{0,4},{4,0},{1,5},{5,1},{2,6},{6,2},{3,7},{7,3},{8,12},{12,8},{9,1... | collective-permute-start | bytes 983048 | tf_op jit(solution)/shard_map/ppermute | solution.py:348
  219.3 14.3 %collective-permute-start.38 = (bf16[128,1280]{1,0:T(8,128)(2,1)S(1)}, bf16[128,1280]{1,0:T(8,128)(2,1)S(1)}, u32[]{:S(2)}, u32[]{:S(2)}) collective-permute-start(bf16[128,1280]{1,0:T(8,128)(2,1)S(1)} %get-tuple-element.158), channel_id=1, source_target_pairs={{0,5},{1,4},{4,1},{5,0},{2,7},{3,6},{6,3},{7,2},{8,13},{9,12},{12,... | collective-permute-start | bytes 983048 | tf_op jit(solution)/shard_map/ppermute | solution.py:349
  234.7 19.0 %all-to-all-start.3 = ((bf16[8,48,480]{2,1,0:T(8,128)(2,1)}), bf16[8,48,480]{2,1,0:T(8,128)(2,1)S(1)}, u32[]{:S(2)}, u32[]{:S(2)}) async-start(bf16[8,48,480]{2,1,0:T(8,128)(2,1)} %fold.1), calls=%async_computation.3 | async-start | bytes 786432 | tf_op jit(solution)/shard_map/all_to_all | solution.py:873
  240.3 6.1 %collective-permute-start.39 = (bf16[4,8,1280]{2,1,0:T(8,128)(2,1)S(1)}, bf16[4,8,1280]{2,1,0:T(8,128)(2,1)S(1)}, u32[]{:S(2)}, u32[]{:S(2)}) collective-permute-start(bf16[4,8,1280]{2,1,0:T(8,128)(2,1)S(1)} %get-tuple-element.164), channel_id=1, source_target_pairs={{0,24},{8,0},{16,8},{24,16},{1,25},{9,1},{17,9},{25,17},{2,26},{10... | collective-permute-start | bytes 245768 | tf_op jit(solution)/shard_map/ppermute | solution.py:357
  243.1 9.8 %collective-permute-start.40 = (bf16[4,8,1280]{2,1,0:T(8,128)(2,1)S(1)}, bf16[4,8,1280]{2,1,0:T(8,128)(2,1)S(1)}, u32[]{:S(2)}, u32[]{:S(2)}) collective-permute-start(bf16[4,8,1280]{2,1,0:T(8,128)(2,1)S(1)} %get-tuple-element.165), channel_id=1, source_target_pairs={{0,16},{8,24},{16,0},{24,8},{1,17},{9,25},{17,1},{25,9},{2,18},{10... | collective-permute-start | bytes 245768 | tf_op jit(solution)/shard_map/ppermute | solution.py:357
  243.1 9.8 %collective-permute-start.41 = (bf16[4,8,1280]{2,1,0:T(8,128)(2,1)S(1)}, bf16[4,8,1280]{2,1,0:T(8,128)(2,1)S(1)}, u32[]{:S(2)}, u32[]{:S(2)}) collective-permute-start(bf16[4,8,1280]{2,1,0:T(8,128)(2,1)S(1)} %get-tuple-element.166), channel_id=1, source_target_pairs={{0,8},{8,16},{16,24},{24,0},{1,9},{9,17},{17,25},{25,1},{2,10},{10... | collective-permute-start | bytes 245768 | tf_op jit(solution)/shard_map/ppermute | solution.py:357
  (16 other events, 21.2 us)
Sparse Core Ops, SparseCore 0:
  10.3 34.4 all-gather.1
  217.0 31.4 reduce-scatter.1

commit v6 on v5

--- a/solution.py
+++ b/solution.py
@@ -509,7 +509,7 @@
 
 def feed_kernel(
     info_ref, x_ref, g_ref, atts, gain_ref,
-    near_a, across_a, all_b, far_near_a, far_across_a, far_b,
+    near_rows, across_a, across_b, far_near_rows, far_across_a, far_across_b,
     out_ref, pack_ref, dmid_ref, datt_0, datt_1, datt_2, datt_3, gain_grad,
     weights, sems,
 ):
@@ -517,12 +517,13 @@
     copies = []
     for w in range(3):
         moved = []
-        for core, refs in ((core_index, (near_a, across_a, all_b)), (1 - core_index, (far_near_a, far_across_a, far_b))):
-            for half in range(2):
-                moved.append((refs[0].at[half, w], half, y_index, core))
-                moved.append((refs[1].at[half, w], half, 1 - y_index, core))
-                for row in range(2):
-                    moved.append((refs[2].at[half, w, row], 2 + half, row, core))
+        for core, own, others in (
+            (core_index, near_rows, (across_a, across_b)),
+            (1 - core_index, far_near_rows, (far_across_a, far_across_b)),
+        ):
+            for z_index in range(4):
+                moved.append((own.at[z_index, w], z_index, y_index, core))
+                moved.append((others[z_index // 2].at[z_index % 2, w], z_index, 1 - y_index, core))
         copies.append([
             pltpu.make_async_copy(src, weights.at[w, block_index(*place)], sems.at[w, i])
             for i, (src, *place) in enumerate(moved)
@@ -700,12 +701,11 @@
     w_parts = [qkv, one, ring_shift(late, 2), three]
     big, near = lax.optimization_barrier((big, near))
     far = core_swap(near)
-    part_a, part_b = big[:2], big[2:]
-    near_a = pair(part_a, plane_shift(part_a, 1), x, 2).reshape(2, 3, 80, width)
-    part_b = pair(part_b, plane_shift(part_b, 2), y, 2)
-    near_a, part_b, far = lax.optimization_barrier((near_a, part_b, far))
-    across_a = plane_shift(near_a, 2)
-    across_b = plane_shift(part_b, 1)
+    beside, across = plane_shift(big, 1), plane_shift(big, 2)
+    beside, across, w_parts[1] = lax.optimization_barrier((beside, across, w_parts[1]))
+    across_a = plane_shift(beside[:2], 2)
+    across_b = plane_shift(across[2:], 1)
+    near_rows = pair(big, beside, x, 2).reshape(4, 3, 80, width)
 
     vecs = jnp.stack([near[:, 128:132, :120], far[:, 128:132, :120]])
     vecs = vecs.astype(f32).reshape(2, 2, 2, 4, 120)
@@ -740,8 +740,13 @@
         name="attend",
     )(info, near, far, gain_one, query_mult, *w_parts)
 
-    att_near, att_far, near_a = lax.optimization_barrier((att_near, att_far, near_a))
-    far_near_a = core_swap(near_a)
+    att_near, att_far, near_rows, across_a, across_b = lax.optimization_barrier(
+        (att_near, att_far, near_rows, across_a, across_b)
+    )
+    far_near_rows = core_swap(near_rows)
+    across_a = pair(across[:2], across_a, x, 2).reshape(2, 3, 80, width)
+    across_b = pair(across[2:], across_b, x, 2).reshape(2, 3, 80, width)
+    far_across_a, far_across_b = core_swap(across_a), core_swap(across_b)
     att_pair = jnp.stack([att_near, core_swap(att_far)], axis=1)
     att_pair, cotangent = lax.optimization_barrier((att_pair, cotangent))
     cot_rows = lax.all_to_all(cotangent.reshape(4, 4, 8, width), "z", split_axis=0, concat_axis=0, tiled=True)
@@ -749,12 +754,7 @@
     atts = [att_pair[0]] + [plane_shift(att_pair[step], step) for step in (1, 2, 3)]
     atts = jnp.stack(atts)
     far_atts, far_cot = core_swap(atts), core_swap(cot_rows)
-    atts, far_near_a, across_a, across_b, cot_rows, far_atts, far_cot = lax.optimization_barrier(
-        (atts, far_near_a, across_a, across_b, cot_rows, far_atts, far_cot)
-    )
-    far_across_a = core_swap(across_a)
-    all_b = pair(part_b, across_b, x, 3).reshape(2, 3, 2, 80, width)
-    far_b = core_swap(all_b)
+    atts, cot_rows, far_atts, far_cot = lax.optimization_barrier((atts, cot_rows, far_atts, far_cot))
 
     datt_shape = jax.ShapeDtypeStruct((2, 128, 160), bf16)
     smem = pl.BlockSpec(memory_space=pltpu.SMEM)
@@ -775,12 +775,9 @@
         compiler_params=limit,
         cost_estimate=pl.CostEstimate(flops=12_000_000_000, bytes_accessed=13_000_000, transcendentals=200_000),
         name="feed",
-    )(info, x_rows, cot_rows, atts, gain_two, near_a, across_a, all_b, far_near_a, far_across_a, far_b)
+    )(info, x_rows, cot_rows, atts, gain_two, near_rows, across_a, across_b, far_near_rows, far_across_a, far_across_b)
 
     back = [datts[0]] + [plane_shift(datts[step], step) for step in (1, 2, 3)]
-    outputs = lax.all_to_all(out_rows, "z", split_axis=0, concat_axis=0, tiled=True).reshape(16, 8, width)
-    grad_att_near = jnp.stack([item[0] for item in back])
-    grad_att_far = core_swap(jnp.stack([item[1] for item in back]))
 
     part_shape = jax.ShapeDtypeStruct((2, 3, 80, width), bf16)
     half_a, kept_b, away_b = pl.pallas_call(
@@ -801,9 +798,10 @@
         first, second = (lax.index_in_dim(array, i, axis, keepdims=False) for i in (0, 1))
         return jnp.where(index == 0, first, second), jnp.where(index == 0, second, first)
 
-    half_a, kept_b, away_b, grad_att_near, grad_att_far, outputs = lax.optimization_barrier(
-        (half_a, kept_b, away_b, grad_att_near, grad_att_far, outputs)
-    )
+    half_a, kept_b, away_b, out_rows, *back = lax.optimization_barrier((half_a, kept_b, away_b, out_rows, *back))
+    outputs = lax.all_to_all(out_rows, "z", split_axis=0, concat_axis=0, tiled=True).reshape(16, 8, width)
+    grad_att_near = jnp.stack([item[0] for item in back])
+    grad_att_far = core_swap(jnp.stack([item[1] for item in back]))
     kept_a, away_a = halves(half_a.reshape(2, 3, 2, 2, 40, width), x, 3)
     kept_a = added(kept_a, plane_shift(away_a, 1))
     kept_b = added(kept_b, plane_shift(away_b, 2)).reshape(2, 3, 2, 40, width)
@@ -836,17 +834,17 @@
         name="attend_back",
     )(info, near, far, gain_one, query_mult, *w_parts, pre, grad_att_near, grad_att_far, gain_two_grad)
 
-    one, three = ring_shift(send[1], 1), ring_shift(send[3], 3)
+    one = ring_shift(send[1], 1)
     swapped = core_swap(hid_far)
     hid = [added(hid_near[i], swapped[i]) for i in range(4)]
-    kept_a, kept_b, one, three, later = lax.optimization_barrier((kept_a, kept_b, one, three, send[2]))
-    two = ring_shift(later, 2)
+    kept_a, kept_b, one, outputs, *later = lax.optimization_barrier((kept_a, kept_b, one, outputs, send[2], send[3]))
+    two, three = ring_shift(later[0], 2), ring_shift(later[1], 3)
     kept_a, away_a = halves(kept_a, y, 2)
     kept_b, away_b = halves(kept_b, x, 2)
     kept_a = added(kept_a, plane_shift(away_a, 2))
     kept_b = added(kept_b, plane_shift(away_b, 1))
     kept = jnp.concatenate([kept_a, kept_b])
-    *hid, kept, two = lax.optimization_barrier((*hid, kept, two))
+    *hid, kept, two, three = lax.optimization_barrier((*hid, kept, two, three))
     moved = [plane_shift(hid[step], step) for step in (1, 2, 3)]
     *moved, mine = lax.optimization_barrier((*moved, send[0]))
     big_sums = lax.psum_scatter(kept, "z", scatter_dimension=0, tiled=True)[0]

time: 267 us -> 272 us (1.019)
  waiting for transfers between devices: 103 us -> 90.6 us
  starting transfers between devices: 54.9 us -> 62.4 us
  other arithmetic: 16.8 us -> 23.9 us
  local copies, waits for them, and re-layouts: 18.3 us -> 21.7 us
    ppermute x12, waiting for transfers between devices: 42.2 us -> 34.2 us  [ring_shift(): return lax.ppermute(value, 'z', [(i, (i + step) % 4) for i in range(4)])]
    ppermute x12, starting transfers between devices: 17.3 us -> 22.7 us  [ring_shift(): return lax.ppermute(value, 'z', [(i, (i + step) % 4) for i in range(4)])]
    ppermute x10, waiting for transfers between devices: 10.4 us -> 5.68 us  [core_swap(): return lax.ppermute(value, 'core', [(0, 1), (1, 0)])]
    select_n x3, other arithmetic: 0.33 us -> 4.32 us  [halves(): jnp.where(index == 0, second, first)]
    convert_element_type x5, other arithmetic: 2.34 us -> 5.89 us  [added(): return (left.astype(f32) + right.astype(f32)).astype(bf16)]
    all_to_all x1, starting transfers between devices: 3.92 us -> 7.02 us  [planes(): lax.all_to_all(cotangent.reshape(4, 4, 8, width), 'z', split_axis=0, conc...]
    select_n x3 -> x2, other arithmetic: 7.28 us -> 5.83 us  [pair(): jnp.where(slot == index, jnp.expand_dims(mine, axis), jnp.expand_dims(oth...]
    unnamed x67 -> x77, local copies, waits for them, and re-layouts: 9.93 us -> 8.99 us
  transfers between devices with their start and end apart: 47 -> 47, of which waited for: 21 -> 21; matrix products, arithmetic and copies ran while one was open for 7% -> 11% of each run, Pallas kernels for 12% -> 12%
where the time goes in v6:
time: 272 us; the launch traced here: 271 us
  waiting for transfers between devices  90.6 us (33%)
  starting transfers between devices  62.4 us (23%)
  Pallas kernels  42.1 us (15%)
  other arithmetic  23.9 us (9%)
  local copies, waits for them, and re-layouts  21.7 us (8%)
  blocking collectives  15.7 us (6%)
  between operations  14.8 us (5%)
    ppermute x12, waiting for transfers between devices, ring_shift(): return lax.ppermute(value, 'z', [(i, (i + step) % 4) for i in range(4)])  34.2 us
    ppermute x8, waiting for transfers between devices, plane_shift(): return lax.ppermute(value, 'x', [(0, 1), (1, 0)])  32.3 us
    ppermute x12, starting transfers between devices, ring_shift(): return lax.ppermute(value, 'z', [(i, (i + step) % 4) for i in range(4)])  22.7 us
    all_to_all x1, blocking collectives, planes(): lax.all_to_all(qkv, ('y', 'core', 'x'), split_axis=0, concat_axis=0, tile...  15.7 us
    ppermute x8, waiting for transfers between devices, plane_shift(): return lax.ppermute(value, 'y', [(0, 1), (1, 0)])  13.8 us
    pallas_call x1, Pallas kernels, planes(): pl.pallas_call(attend_back_kernel, grid_spec=pltpu.PrefetchScalarGridSpec...  12.7 us
    pallas_call x1, Pallas kernels, planes(): pl.pallas_call(feed_kernel, in_specs=[smem] + [vmem] * 4 + [hbm] * 6, out...  9.68 us
    unnamed x77, local copies, waits for them, and re-layouts  8.99 us
  transfers between devices with their start and end apart: 47, of which 21 were waited for; matrix products, arithmetic and copies ran while one was open for 11% of the time, Pallas kernels for 12%

profile of v6, /device:TPU:0, one launch (start us, length us, event | category | flops | bytes accessed | tf_op | source)
XLA Modules:
  0.0 271.1 jit_solution(8294537697589651623)
XLA Ops:
  8.3 1.1 convert_bitcast_fusion.3
  10.4 5.1 %collective-permute-start = (bf16[5,8,1280]{2,1,0:T(8,128)(2,1)S(1)}, bf16[5,8,1280]{2,1,0:T(8,128)(2,1)S(1)}, u32[]{:S(2)}, u32[]{:S(2)}) collective-permute-start(bf16[5,8,1280]{2,1,0:T(8,128)(2,1)S(1)} %get-tuple-element.212), channel_id=1, source_target_pairs={{0,24},{8,0},{16,8},{24,16},{1,25},{9,1},{17,9},{25,17},{2,26},{10... | collective-permute-start | bytes 307208 | tf_op jit(solution)/shard_map/ppermute | solution.py:357
  15.5 1.0 collective-permute-start.2
  17.3 1.5 collective-permute-done
  18.8 6.2 %collective-permute-done.1 = bf16[5,8,1280]{2,1,0:T(8,128)(2,1)S(1)} collective-permute-done((bf16[5,8,1280]{2,1,0:T(8,128)(2,1)S(1)}, bf16[5,8,1280]{2,1,0:T(8,128)(2,1)S(1)}, u32[]{:S(2)}, u32[]{:S(2)}) %collective-permute-start.1) | collective-permute-done | bytes 102432 | tf_op jit(solution)/shard_map/ppermute | solution.py:357
  25.5 3.3 %collective-permute-start.5 = (bf16[136,1280]{1,0:T(8,128)(2,1)S(1)}, bf16[136,1280]{1,0:T(8,128)(2,1)S(1)}, u32[]{:S(2)}, u32[]{:S(2)}) collective-permute-start(bf16[136,1280]{1,0:T(8,128)(2,1)S(1)} %maximum_maximum_fusion), channel_id=1, source_target_pairs={{0,5},{1,4},{4,1},{5,0},{2,7},{3,6},{6,3},{7,2},{8,13},{9,12},{12,... | collective-permute-start | bytes 1044488 | tf_op jit(solution)/shard_map/ppermute | solution.py:349
  30.9 15.7 %all_to_all.20 = bf16[8,40,480]{2,1,0:T(8,128)(2,1)S(1)} all-to-all(bf16[8,40,480]{2,1,0:T(8,128)(2,1)S(1)} %reshape.352), channel_id=1, replica_groups=mesh['z'=4,'y'=2,'core'=2,'x'=2] {'y','core','x'}, dimensions={0} | all-to-all | bytes 614400 | tf_op jit(solution)/shard_map/all_to_all | solution.py:694
  46.6 1.2 pad_maximum_fusion.near_ref
  47.8 1.6 collective-permute-start.8
  49.3 1.4 collective-permute-start.7
  51.4 1.9 collective-permute-start.9
  53.7 7.9 %collective-permute-done.10.w_3 = bf16[320,480]{1,0:T(8,128)(2,1)S(1)} collective-permute-done((bf16[320,480]{1,0:T(8,128)(2,1)S(1)}, bf16[320,480]{1,0:T(8,128)(2,1)S(1)}, u32[]{:S(2)}, u32[]{:S(2)}) %collective-permute-start.10) | collective-permute-done | bytes 307232 | tf_op jit(solution)/shard_map/ppermute | solution.py:357
  61.7 10.7 %collective-permute-done.9.w_1 = bf16[320,480]{1,0:T(8,128)(2,1)S(1)} collective-permute-done((bf16[320,480]{1,0:T(8,128)(2,1)S(1)}, bf16[320,480]{1,0:T(8,128)(2,1)S(1)}, u32[]{:S(2)}, u32[]{:S(2)}) %collective-permute-start.9) | collective-permute-done | bytes 307232 | tf_op jit(solution)/shard_map/ppermute | solution.py:357
  72.4 4.8 %collective-permute-done.8 = bf16[4,3,40,1280]{3,2,1,0:T(8,128)(2,1)} collective-permute-done((bf16[4,3,40,1280]{3,2,1,0:T(8,128)(2,1)}, bf16[4,3,40,1280]{3,2,1,0:T(8,128)(2,1)}, u32[]{:S(2)}, u32[]{:S(2)}) %collective-permute-start.8) | collective-permute-done | bytes 1228832 | tf_op jit(solution)/shard_map/ppermute | solution.py:348
  77.2 1.1 collective-permute-done.7
  78.3 1.9 slice.182
  80.2 3.0 %bitcast_select_fusion.near_rows = bf16[4,3,80,1280]{3,2,1,0:T(8,128)(2,1)} fusion(pred[80]{0:T(512)(128)(4,1)S(1)} %broadcast_in_dim.343, bf16[4,3,40,1280]{3,2,1,0:T(8,128)(2,1)} %collective-permute-done.7, bf16[4,3,40,1280]{3,2,1,0:T(8,128)(2,1)S(1)} %copy-done.20), kind=kLoop, calls=%fused_computation.2 | loop fusion | flops 1228800 | bytes 4915280 | tf_op jit(solution)/shard_map/jit(_where)/select_n | solution.py:379
  83.9 2.4 fusion.24
  86.3 1.4 collective-permute-start.13
  89.0 8.4 %attend.1 = (f32[2,4,128,480]{3,2,1,0:T(8,128)}, bf16[4,128,160]{2,1,0:T(8,128)(2,1)S(1)}, bf16[4,128,160]{2,1,0:T(8,128)(2,1)S(1)}) custom-call(s32[6]{0:T(128)S(1)} %pad_add_fusion.info_ref, bf16[4,136,1280]{2,1,0:T(8,128)(2,1)S(1)} %pad_maximum_fusion.near_ref, bf16[4,136,1280]{2,1,0:T(8,128)(2,1)} %collective-permute-done.6.far_ref, ...), custom_call_target="tpu_custom_call" | custom-call | flops 8999999488 | bytes 8000000 | tf_op jit(solution)/shard_map/attend/pallas_call | solution.py:721
  98.2 2.9 %collective-permute-done.13 = bf16[2,3,40,1280]{3,2,1,0:T(8,128)(2,1)} collective-permute-done((bf16[2,3,40,1280]{3,2,1,0:T(8,128)(2,1)}, bf16[2,3,40,1280]{3,2,1,0:T(8,128)(2,1)}, u32[]{:S(2)}, u32[]{:S(2)}) %collective-permute-start.13) | collective-permute-done | bytes 614432 | tf_op jit(solution)/shard_map/ppermute | solution.py:346
  101.1 2.8 %bitcast_select_fusion.1 = (bf16[2,3,80,1280]{3,2,1,0:T(8,128)(2,1)}, bf16[2,3,80,1280]{3,2,1,0:T(8,128)(2,1)S(1)}) fusion(pred[80]{0:T(512)(128)(4,1)S(1)} %broadcast_in_dim.343, bf16[2,3,40,1280]{3,2,1,0:T(8,128)(2,1)} %collective-permute-done.13, bf16[2,3,40,1280]{3,2,1,0:T(8,128)(2,1)} %get-tuple-element.192, ...), kind=kLoop, calls=%fused_computation.10 | loop fusion | flops 1228800 | bytes 4915280 | tf_op jit(solution)/shard_map/jit(_where)/select_n | solution.py:379
  104.9 4.4 %collective-permute-done.14 = bf16[4,128,160]{2,1,0:T(8,128)(2,1)S(1)} collective-permute-done((bf16[4,128,160]{2,1,0:T(8,128)(2,1)S(1)}, bf16[4,128,160]{2,1,0:T(8,128)(2,1)S(1)}, u32[]{:S(2)}, u32[]{:S(2)}) %collective-permute-start.14) | collective-permute-done | bytes 163872 | tf_op jit(solution)/shard_map/ppermute | solution.py:353
  109.3 7.0 %all-to-all-start.1 = ((bf16[4,4,8,1280]{3,2,1,0:T(8,128)(2,1)}), bf16[4,4,8,1280]{3,2,1,0:T(8,128)(2,1)}, u32[]{:S(2)}, u32[]{:S(2)}) async-start(bf16[4,4,8,1280]{3,2,1,0:T(8,128)(2,1)} %bitcast.39), calls=%async_computation.1 | async-start | bytes 655360 | tf_op jit(solution)/shard_map/all_to_all | solution.py:752
  116.4 1.2 collective-permute-start.17
  118.4 4.6 %collective-permute-done.17 = bf16[2,128,160]{2,1,0:T(8,128)(2,1)S(1)} collective-permute-done((bf16[2,128,160]{2,1,0:T(8,128)(2,1)S(1)}, bf16[2,128,160]{2,1,0:T(8,128)(2,1)S(1)}, u32[]{:S(2)}, u32[]{:S(2)}) %collective-permute-start.17) | collective-permute-done | bytes 81952 | tf_op jit(solution)/shard_map/ppermute | solution.py:349
  123.4 2.2 collective-permute-done.16
  125.6 2.3 collective-permute-done.15
  130.0 1.1 collective-permute-done.19.far_cot
  131.1 9.7 %feed.1 = (bf16[4,4,8,1280]{3,2,1,0:T(8,128)(2,1)}, bf16[4,128,1280]{2,1,0:T(8,128)(2,1)}, f32[128,1280]{1,0:T(8,128)S(1)}, bf16[2,128,160]{2,1,0:T(8,128)(2,1)S...) custom-call(s32[6]{0:T(128)S(1)} %pad_add_fusion.info_ref, ...), custom_call_target="tpu_custom_call" | custom-call | flops 12000000000 | bytes 13000000 | tf_op jit(solution)/shard_map/feed/pallas_call | solution.py:763
  141.7 1.2 collective-permute-start.25
  142.9 1.8 collective-permute-start.26
  144.7 1.1 copy-done.33
  145.8 7.5 %grads.1 = (bf16[2,3,2,80,1280]{4,3,2,1,0:T(8,128)(2,1)}, bf16[2,3,80,1280]{3,2,1,0:T(8,128)(2,1)S(1)}, bf16[2,3,80,1280]{3,2,1,0:T(8,128)(2,1)}) custom-call(s32[6]{0:T(128)S(1)} %pad_add_fusion.info_ref, bf16[4,128,1280]{2,1,0:T(8,128)(2,1)} %get-tuple-element.130.pack_ref, bf16[4,128,1280]{2,1,0:T(8,128)(2,1)} %copy-done.33, ...), custom_call_target="tpu_custom_call" | custom-call | flops 6000000000 | bytes 8000000 | tf_op jit(solution)/shard_map/grads/pallas_call | solution.py:783
  154.7 3.3 %fusion.23 = (bf16[2,3,2,1,40,1280]{5,4,3,2,1,0:T(8,128)(2,1)}, bf16[2,3,2,1,40,1280]{5,4,3,2,1,0:T(8,128)(2,1)}) fusion(bf16[2,3,2,2,40,1280]{5,4,3,2,1,0:T(8,128)(2,1)} %bitcast.130), kind=kLoop, calls=%fused_computation.93 | loop fusion | bytes 4915200 | tf_op jit(solution)/shard_map/slice | solution.py:798
  158.0 4.9 %all-to-all-start.2 = ((bf16[4,4,8,1280]{3,2,1,0:T(8,128)(2,1)}), bf16[4,4,8,1280]{3,2,1,0:T(8,128)(2,1)}, u32[]{:S(2)}, u32[]{:S(2)}) async-start(bf16[4,4,8,1280]{3,2,1,0:T(8,128)(2,1)} %get-tuple-element.151), calls=%async_computation.2 | async-start | bytes 655360 | tf_op jit(solution)/shard_map/all_to_all | solution.py:802
  163.2 1.0 copy-done.14
  164.2 1.6 select_bitcast_fusion
  166.3 1.2 collective-permute-start.28
  167.7 12.7 %attend_back.1 = (bf16[4,128,1280]{2,1,0:T(8,128)(2,1)}, bf16[4,128,1280]{2,1,0:T(8,128)(2,1)}, bf16[336,480]{1,0:T(8,128)(2,1)S(1)}, bf16[336,480]{1,0:T(8,128)...) custom-call(s32[6]{0:T(128)S(1)} %pad_add_fusion.info_ref, bf16[4,136,1280]{2,1,0:T(8,128)(2,1)} %copy-done, ...), custom_call_target="tpu_custom_call" | custom-call | flops 15000000512 | bytes 12000000 | tf_op jit(solution)/shard_map/attend_back/pallas_call | solution.py:808
  181.1 2.0 collective-permute-start.30
  183.2 11.1 %collective-permute-done.27 = bf16[2,3,2,40,1280]{4,3,1,0,2:T(8,128)(2,1)S(1)} collective-permute-done((bf16[2,3,2,40,1280]{4,3,1,0,2:T(8,128)(2,1)S(1)}, bf16[2,3,2,40,1280]{4,3,1,0,2:T(8,128)(2,1)S(1)}, u32[]{:S(2)}, u32[]{:S(2)}) %collective-permute-start.27) | collective-permute-done | bytes 1228832 | tf_op jit(solution)/shard_map/ppermute | solution.py:346
  194.3 1.5 fusion
  195.8 1.3 add_convert_fusion
  197.1 3.2 %collective-permute-start.34 = (bf16[336,480]{1,0:T(8,128)(2,1)S(1)}, bf16[336,480]{1,0:T(8,128)(2,1)S(1)}, u32[]{:S(2)}, u32[]{:S(2)}) collective-permute-start(bf16[336,480]{1,0:T(8,128)(2,1)S(1)} %copy-done.3), channel_id=1, source_target_pairs={{0,16},{8,24},{16,0},{24,8},{1,17},{9,25},{17,1},{25,9},{2,18},{10... | collective-permute-start | bytes 967688 | tf_op jit(solution)/shard_map/ppermute | solution.py:357
  200.3 1.2 collective-permute-start.35
  201.6 1.4 select_bitcast_fusion.1
  203.5 1.3 select_bitcast_fusion.2
  204.8 1.3 collective-permute-start.32
  206.1 2.6 fusion.6
  208.7 8.1 %collective-permute-done.33 = bf16[2,3,40,1280]{3,2,1,0:T(8,128)(2,1)S(1)} collective-permute-done((bf16[2,3,40,1280]{3,2,1,0:T(8,128)(2,1)S(1)}, bf16[2,3,40,1280]{3,2,1,0:T(8,128)(2,1)S(1)}, u32[]{:S(2)}, u32[]{:S(2)}) %collective-permute-start.33) | collective-permute-done | bytes 614432 | tf_op jit(solution)/shard_map/ppermute | solution.py:346
  217.1 1.4 collective-permute-done.32
  218.7 1.1 pad_maximum_fusion.1
  219.9 1.5 collective-permute-start.36
  222.1 1.4 collective-permute-start.38
  223.4 6.8 %collective-permute-done.36.hid_1 = bf16[128,1280]{1,0:T(8,128)(2,1)S(1)} collective-permute-done((bf16[128,1280]{1,0:T(8,128)(2,1)}, bf16[128,1280]{1,0:T(8,128)(2,1)S(1)}, u32[]{:S(2)}, u32[]{:S(2)}) %collective-permute-start.36) | collective-permute-done | bytes 327712 | tf_op jit(solution)/shard_map/ppermute | solution.py:346
  230.2 4.6 %collective-permute-done.37.hid_2 = bf16[128,1280]{1,0:T(8,128)(2,1)S(1)} collective-permute-done((bf16[128,1280]{1,0:T(8,128)(2,1)}, bf16[128,1280]{1,0:T(8,128)(2,1)S(1)}, u32[]{:S(2)}, u32[]{:S(2)}) %collective-permute-start.37) | collective-permute-done | bytes 327712 | tf_op jit(solution)/shard_map/ppermute | solution.py:348
  235.8 1.1 fold.1
  236.8 3.5 %all-to-all-start.3 = ((bf16[8,48,480]{2,1,0:T(8,128)(2,1)}), bf16[8,48,480]{2,1,0:T(8,128)(2,1)S(1)}, u32[]{:S(2)}, u32[]{:S(2)}) async-start(bf16[8,48,480]{2,1,0:T(8,128)(2,1)} %fold.1), calls=%async_computation.3 | async-start | bytes 786432 | tf_op jit(solution)/shard_map/all_to_all | solution.py:871
  240.3 1.1 copy-done.11
  242.4 7.0 %collective-permute-start.39 = (bf16[4,8,1280]{2,1,0:T(8,128)(2,1)S(1)}, bf16[4,8,1280]{2,1,0:T(8,128)(2,1)S(1)}, u32[]{:S(2)}, u32[]{:S(2)}) collective-permute-start(bf16[4,8,1280]{2,1,0:T(8,128)(2,1)S(1)} %get-tuple-element.170), channel_id=1, source_target_pairs={{0,24},{8,0},{16,8},{24,16},{1,25},{9,1},{17,9},{25,17},{2,26},{10... | collective-permute-start | bytes 245768 | tf_op jit(solution)/shard_map/ppermute | solution.py:357
  250.6 1.7 collective-permute-done.39
  252.2 6.1 %collective-permute-done.40 = bf16[4,8,1280]{2,1,0:T(8,128)(2,1)S(1)} collective-permute-done((bf16[4,8,1280]{2,1,0:T(8,128)(2,1)S(1)}, bf16[4,8,1280]{2,1,0:T(8,128)(2,1)S(1)}, u32[]{:S(2)}, u32[]{:S(2)}) %collective-permute-start.40) | collective-permute-done | bytes 81952 | tf_op jit(solution)/shard_map/ppermute | solution.py:357
  262.6 1.7 copy.66
  (207 shorter events, 26.0 us)
Async XLA Ops:
  7.2 40.5 %all-gather.2.cloned.1.call-start = ((), (), s32[]{:S(2)}) async-start(), calls=%async_computation.5 | async-start | bytes 1536000 | tf_op jit(solution)/shard_map/all_gather | solution.py:688
  9.3 7.8 %copy-start.22 = (f32[40,1280]{1,0:T(8,128)S(1)}, f32[40,1280]{1,0:T(8,128)}, u32[]{:S(2)}) copy-start(f32[40,1280]{1,0:T(8,128)} %param.17) | copy-start | bytes 614404
  9.3 7.9 %copy-start.23 = (f32[40,1280]{1,0:T(8,128)S(1)}, f32[40,1280]{1,0:T(8,128)}, u32[]{:S(2)}) copy-start(f32[40,1280]{1,0:T(8,128)} %param.19) | copy-start | bytes 614404
  9.3 7.9 %copy-start.24 = (f32[40,1280]{1,0:T(8,128)S(1)}, f32[40,1280]{1,0:T(8,128)}, u32[]{:S(2)}) copy-start(f32[40,1280]{1,0:T(8,128)} %param.18) | copy-start | bytes 614404
  10.4 8.4 %collective-permute-start = (bf16[5,8,1280]{2,1,0:T(8,128)(2,1)S(1)}, bf16[5,8,1280]{2,1,0:T(8,128)(2,1)S(1)}, u32[]{:S(2)}, u32[]{:S(2)}) collective-permute-start(bf16[5,8,1280]{2,1,0:T(8,128)(2,1)S(1)} %get-tuple-element.212), channel_id=1, source_target_pairs={{0,24},{8,0},{16,8},{24,16},{1,25},{9,1},{17,9},{25,17},{2,26},{10... | collective-permute-start | bytes 307208 | tf_op jit(solution)/shard_map/ppermute | solution.py:357
  15.5 9.5 %collective-permute-start.1 = (bf16[5,8,1280]{2,1,0:T(8,128)(2,1)S(1)}, bf16[5,8,1280]{2,1,0:T(8,128)(2,1)S(1)}, u32[]{:S(2)}, u32[]{:S(2)}) collective-permute-start(bf16[5,8,1280]{2,1,0:T(8,128)(2,1)S(1)} %get-tuple-element.213), channel_id=1, source_target_pairs={{0,16},{8,24},{16,0},{24,8},{1,17},{9,25},{17,1},{25,9},{2,18},{10... | collective-permute-start | bytes 307208 | tf_op jit(solution)/shard_map/ppermute | solution.py:357
  15.5 9.5 %collective-permute-start.2 = (bf16[5,8,1280]{2,1,0:T(8,128)(2,1)S(1)}, bf16[5,8,1280]{2,1,0:T(8,128)(2,1)S(1)}, u32[]{:S(2)}, u32[]{:S(2)}) collective-permute-start(bf16[5,8,1280]{2,1,0:T(8,128)(2,1)S(1)} %get-tuple-element.214), channel_id=1, source_target_pairs={{0,8},{8,16},{16,24},{24,0},{1,9},{9,17},{17,25},{25,1},{2,10},{10... | collective-permute-start | bytes 307208 | tf_op jit(solution)/shard_map/ppermute | solution.py:357
  25.5 21.0 %collective-permute-start.5 = (bf16[136,1280]{1,0:T(8,128)(2,1)S(1)}, bf16[136,1280]{1,0:T(8,128)(2,1)S(1)}, u32[]{:S(2)}, u32[]{:S(2)}) collective-permute-start(bf16[136,1280]{1,0:T(8,128)(2,1)S(1)} %maximum_maximum_fusion), channel_id=1, source_target_pairs={{0,5},{1,4},{4,1},{5,0},{2,7},{3,6},{6,3},{7,2},{8,13},{9,12},{12,... | collective-permute-start | bytes 1044488 | tf_op jit(solution)/shard_map/ppermute | solution.py:349
  28.8 17.7 %collective-permute-start.4 = (bf16[136,1280]{1,0:T(8,128)(2,1)S(1)}, bf16[136,1280]{1,0:T(8,128)(2,1)S(1)}, u32[]{:S(2)}, u32[]{:S(2)}) collective-permute-start(bf16[136,1280]{1,0:T(8,128)(2,1)S(1)} %maximum_maximum_fusion), channel_id=1, source_target_pairs={{0,4},{4,0},{1,5},{5,1},{2,6},{6,2},{3,7},{7,3},{8,12},{12,8},{9,1... | collective-permute-start | bytes 1044488 | tf_op jit(solution)/shard_map/ppermute | solution.py:348
  28.8 17.7 %collective-permute-start.3 = (bf16[136,1280]{1,0:T(8,128)(2,1)S(1)}, bf16[136,1280]{1,0:T(8,128)(2,1)}, u32[]{:S(2)}, u32[]{:S(2)}) collective-permute-start(bf16[136,1280]{1,0:T(8,128)(2,1)S(1)} %maximum_maximum_fusion), channel_id=1, source_target_pairs={{0,1},{1,0},{2,3},{3,2},{4,5},{5,4},{6,7},{7,6},{8,9},{9,8},{10,11... | collective-permute-start | bytes 1044488 | tf_op jit(solution)/shard_map/ppermute | solution.py:346
  46.5 6.9 %copy-start.36 = (s32[16]{0:T(128)S(1)}, s32[16]{0:T(128)}, u32[]{:S(2)}) copy-start(s32[16]{0:T(128)} %param.27) | copy-start | bytes 196
  46.5 6.9 %copy-start.37 = (s32[16]{0:T(128)S(1)}, s32[16]{0:T(128)}, u32[]{:S(2)}) copy-start(s32[16]{0:T(128)} %param.26) | copy-start | bytes 196
  47.7 41.3 %copy-start = (bf16[4,136,1280]{2,1,0:T(8,128)(2,1)}, bf16[4,136,1280]{2,1,0:T(8,128)(2,1)S(1)}, u32[]{:S(2)}) copy-start(bf16[4,136,1280]{2,1,0:T(8,128)(2,1)S(1)} %pad_maximum_fusion.near_ref) | copy-start | bytes 4177924
  47.8 29.4 %collective-permute-start.8 = (bf16[4,3,40,1280]{3,2,1,0:T(8,128)(2,1)}, bf16[4,3,40,1280]{3,2,1,0:T(8,128)(2,1)}, u32[]{:S(2)}, u32[]{:S(2)}) collective-permute-start(bf16[4,3,40,1280]{3,2,1,0:T(8,128)(2,1)} %all-gather.2.cloned.1.call-done), channel_id=1, source_target_pairs={{0,4},{4,0},{1,5},{5,1},{2,6},{6,2},{3,7},{7,3},{8,12},{12,8},{9,1... | collective-permute-start | bytes 3686408 | tf_op jit(solution)/shard_map/ppermute | solution.py:348
  49.3 28.9 %collective-permute-start.7 = (bf16[4,3,40,1280]{3,2,1,0:T(8,128)(2,1)}, bf16[4,3,40,1280]{3,2,1,0:T(8,128)(2,1)}, u32[]{:S(2)}, u32[]{:S(2)}) collective-permute-start(bf16[4,3,40,1280]{3,2,1,0:T(8,128)(2,1)} %all-gather.2.cloned.1.call-done), channel_id=1, source_target_pairs={{0,1},{1,0},{2,3},{3,2},{4,5},{5,4},{6,7},{7,6},{8,9},{9,8},{10,11... | collective-permute-start | bytes 3686408 | tf_op jit(solution)/shard_map/ppermute | solution.py:346
  50.8 36.9 %collective-permute-start.6 = (bf16[4,136,1280]{2,1,0:T(8,128)(2,1)S(1)}, bf16[4,136,1280]{2,1,0:T(8,128)(2,1)}, u32[]{:S(2)}, u32[]{:S(2)}) collective-permute-start(bf16[4,136,1280]{2,1,0:T(8,128)(2,1)S(1)} %pad_maximum_fusion.near_ref), channel_id=1, source_target_pairs={{0,2},{2,0},{1,3},{3,1},{4,6},{6,4},{5,7},{7,5},{8,10},{10,8},{9,1... | collective-permute-start | bytes 4177928 | tf_op jit(solution)/shard_map/ppermute | solution.py:353
  50.8 10.9 %collective-permute-start.10 = (bf16[320,480]{1,0:T(8,128)(2,1)S(1)}, bf16[320,480]{1,0:T(8,128)(2,1)S(1)}, u32[]{:S(2)}, u32[]{:S(2)}) collective-permute-start(bf16[320,480]{1,0:T(8,128)(2,1)S(1)} %bitcast.117), channel_id=1, source_target_pairs={{0,24},{8,0},{16,8},{24,16},{1,25},{9,1},{17,9},{25,17},{2,26},{10... | collective-permute-start | bytes 921608 | tf_op jit(solution)/shard_map/ppermute | solution.py:357
  51.4 21.0 %collective-permute-start.9 = (bf16[320,480]{1,0:T(8,128)(2,1)S(1)}, bf16[320,480]{1,0:T(8,128)(2,1)S(1)}, u32[]{:S(2)}, u32[]{:S(2)}) collective-permute-start(bf16[320,480]{1,0:T(8,128)(2,1)S(1)} %bitcast.118), channel_id=1, source_target_pairs={{0,8},{8,16},{16,24},{24,0},{1,9},{9,17},{17,25},{25,1},{2,10},{10... | collective-permute-start | bytes 921608 | tf_op jit(solution)/shard_map/ppermute | solution.py:357
  53.5 26.8 %copy-start.20 = (bf16[4,3,40,1280]{3,2,1,0:T(8,128)(2,1)S(1)}, bf16[4,3,40,1280]{3,2,1,0:T(8,128)(2,1)}, u32[]{:S(2)}) copy-start(bf16[4,3,40,1280]{3,2,1,0:T(8,128)(2,1)} %all-gather.2.cloned.1.call-done) | copy-start | bytes 3686404
  61.7 27.3 %copy-start.4 = (bf16[320,480]{1,0:T(8,128)(2,1)}, bf16[320,480]{1,0:T(8,128)(2,1)S(1)}, u32[]{:S(2)}) copy-start(bf16[320,480]{1,0:T(8,128)(2,1)S(1)} %collective-permute-done.10.w_3) | copy-start | bytes 921604
  72.4 16.6 %copy-start.6 = (bf16[320,480]{1,0:T(8,128)(2,1)}, bf16[320,480]{1,0:T(8,128)(2,1)S(1)}, u32[]{:S(2)}) copy-start(bf16[320,480]{1,0:T(8,128)(2,1)S(1)} %collective-permute-done.9.w_1) | copy-start | bytes 921604
  72.4 16.6 %collective-permute-start.11 = (bf16[320,480]{1,0:T(8,128)(2,1)S(1)}, bf16[320,480]{1,0:T(8,128)(2,1)S(1)}, u32[]{:S(2)}, u32[]{:S(2)}) collective-permute-start(bf16[320,480]{1,0:T(8,128)(2,1)S(1)} %bitcast.119), channel_id=1, source_target_pairs={{0,16},{8,24},{16,0},{24,8},{1,17},{9,25},{17,1},{25,9},{2,18},{10... | collective-permute-start | bytes 921608 | tf_op jit(solution)/shard_map/ppermute | solution.py:357
  83.3 14.9 %collective-permute-start.12 = (bf16[2,3,40,1280]{3,2,1,0:T(8,128)(2,1)}, bf16[2,3,40,1280]{3,2,1,0:T(8,128)(2,1)}, u32[]{:S(2)}, u32[]{:S(2)}) collective-permute-start(bf16[2,3,40,1280]{3,2,1,0:T(8,128)(2,1)} %slice.182), channel_id=1, source_target_pairs={{0,4},{4,0},{1,5},{5,1},{2,6},{6,2},{3,7},{7,3},{8,12},{12,8},{9,1... | collective-permute-start | bytes 1843208 | tf_op jit(solution)/shard_map/ppermute | solution.py:348
  86.3 14.8 %collective-permute-start.13 = (bf16[2,3,40,1280]{3,2,1,0:T(8,128)(2,1)}, bf16[2,3,40,1280]{3,2,1,0:T(8,128)(2,1)}, u32[]{:S(2)}, u32[]{:S(2)}) collective-permute-start(bf16[2,3,40,1280]{3,2,1,0:T(8,128)(2,1)} %get-tuple-element.192), channel_id=1, source_target_pairs={{0,1},{1,0},{2,3},{3,2},{4,5},{5,4},{6,7},{7,6},{8,9},{9,8},{10,11... | collective-permute-start | bytes 1843208 | tf_op jit(solution)/shard_map/ppermute | solution.py:346
  89.0 12.1 %copy-start.18 = (bf16[2,3,40,1280]{3,2,1,0:T(8,128)(2,1)S(1)}, bf16[2,3,40,1280]{3,2,1,0:T(8,128)(2,1)}, u32[]{:S(2)}) copy-start(bf16[2,3,40,1280]{3,2,1,0:T(8,128)(2,1)} %get-tuple-element.191) | copy-start | bytes 1843204
  89.0 8.4 %copy-start.8 = (bf16[320,480]{1,0:T(8,128)(2,1)}, bf16[320,480]{1,0:T(8,128)(2,1)S(1)}, u32[]{:S(2)}) copy-start(bf16[320,480]{1,0:T(8,128)(2,1)S(1)} %collective-permute-done.11.w_2) | copy-start | bytes 921604
  101.1 30.0 %collective-permute-start.20 = (bf16[4,3,80,1280]{3,2,1,0:T(8,128)(2,1)}, bf16[4,3,80,1280]{3,2,1,0:T(8,128)(2,1)}, u32[]{:S(2)}, u32[]{:S(2)}) collective-permute-start(bf16[4,3,80,1280]{3,2,1,0:T(8,128)(2,1)} %bitcast_select_fusion.near_rows), channel_id=1, source_target_pairs={{0,2},{2,0},{1,3},{3,1},{4,6},{6,4},{5,7},{7,5},{8,10},{10,8},{9,1... | collective-permute-start | bytes 7372808 | tf_op jit(solution)/shard_map/ppermute | solution.py:353
  103.9 27.2 %collective-permute-start.22 = (bf16[2,3,80,1280]{3,2,1,0:T(8,128)(2,1)}, bf16[2,3,80,1280]{3,2,1,0:T(8,128)(2,1)}, u32[]{:S(2)}, u32[]{:S(2)}) collective-permute-start(bf16[2,3,80,1280]{3,2,1,0:T(8,128)(2,1)} %get-tuple-element.218.across_b), channel_id=1, source_target_pairs={{0,2},{2,0},{1,3},{3,1},{4,6},{6,4},{5,7},{7,5},{8,10},{10,8},{9,1... | collective-permute-start | bytes 3686408 | tf_op jit(solution)/shard_map/ppermute | solution.py:353
  104.4 26.7 %collective-permute-start.21 = (bf16[2,3,80,1280]{3,2,1,0:T(8,128)(2,1)S(1)}, bf16[2,3,80,1280]{3,2,1,0:T(8,128)(2,1)}, u32[]{:S(2)}, u32[]{:S(2)}) collective-permute-start(bf16[2,3,80,1280]{3,2,1,0:T(8,128)(2,1)S(1)} %get-tuple-element.219.across_a), channel_id=1, source_target_pairs={{0,2},{2,0},{1,3},{3,1},{4,6},{6,4},{5,7},{7,5},{8,10},{10,8},{9,1... | collective-permute-start | bytes 3686408 | tf_op jit(solution)/shard_map/ppermute | solution.py:353
  104.4 4.9 %collective-permute-start.14 = (bf16[4,128,160]{2,1,0:T(8,128)(2,1)S(1)}, bf16[4,128,160]{2,1,0:T(8,128)(2,1)S(1)}, u32[]{:S(2)}, u32[]{:S(2)}) collective-permute-start(bf16[4,128,160]{2,1,0:T(8,128)(2,1)S(1)} %get-tuple-element.122), channel_id=1, source_target_pairs={{0,2},{2,0},{1,3},{3,1},{4,6},{6,4},{5,7},{7,5},{8,10},{10,8},{9,1... | collective-permute-start | bytes 491528 | tf_op jit(solution)/shard_map/ppermute | solution.py:353
  109.3 18.8 %all-to-all-start.1 = ((bf16[4,4,8,1280]{3,2,1,0:T(8,128)(2,1)}), bf16[4,4,8,1280]{3,2,1,0:T(8,128)(2,1)}, u32[]{:S(2)}, u32[]{:S(2)}) async-start(bf16[4,4,8,1280]{3,2,1,0:T(8,128)(2,1)} %bitcast.39), calls=%async_computation.1 | async-start | bytes 655360 | tf_op jit(solution)/shard_map/all_to_all | solution.py:752
  116.4 6.6 %collective-permute-start.17 = (bf16[2,128,160]{2,1,0:T(8,128)(2,1)S(1)}, bf16[2,128,160]{2,1,0:T(8,128)(2,1)S(1)}, u32[]{:S(2)}, u32[]{:S(2)}) collective-permute-start(bf16[2,128,160]{2,1,0:T(8,128)(2,1)S(1)} %get-tuple-element.194), channel_id=1, source_target_pairs={{0,5},{1,4},{4,1},{5,0},{2,7},{3,6},{6,3},{7,2},{8,13},{9,12},{12,... | collective-permute-start | bytes 245768 | tf_op jit(solution)/shard_map/ppermute | solution.py:349
  117.6 8.0 %collective-permute-start.16 = (bf16[2,128,160]{2,1,0:T(8,128)(2,1)S(1)}, bf16[2,128,160]{2,1,0:T(8,128)(2,1)S(1)}, u32[]{:S(2)}, u32[]{:S(2)}) collective-permute-start(bf16[2,128,160]{2,1,0:T(8,128)(2,1)S(1)} %get-tuple-element.195), channel_id=1, source_target_pairs={{0,4},{4,0},{1,5},{5,1},{2,6},{6,2},{3,7},{7,3},{8,12},{12,8},{9,1... | collective-permute-start | bytes 245768 | tf_op jit(solution)/shard_map/ppermute | solution.py:348
  123.0 5.0 %collective-permute-start.15 = (bf16[2,128,160]{2,1,0:T(8,128)(2,1)S(1)}, bf16[2,128,160]{2,1,0:T(8,128)(2,1)S(1)}, u32[]{:S(2)}, u32[]{:S(2)}) collective-permute-start(bf16[2,128,160]{2,1,0:T(8,128)(2,1)S(1)} %get-tuple-element.196), channel_id=1, source_target_pairs={{0,1},{1,0},{2,3},{3,2},{4,5},{5,4},{6,7},{7,6},{8,9},{9,8},{10,11... | collective-permute-start | bytes 245768 | tf_op jit(solution)/shard_map/ppermute | solution.py:346
  128.1 2.0 collective-permute-start.18
  129.1 1.9 collective-permute-start.19
  140.8 12.6 %copy-start.10 = (f32[128,1280]{1,0:T(8,128)}, f32[128,1280]{1,0:T(8,128)S(1)}, u32[]{:S(2)}) copy-start(f32[128,1280]{1,0:T(8,128)S(1)} %get-tuple-element.169.dmid_ref) | copy-start | bytes 1966084
  140.8 3.9 %collective-permute-start.23 = (bf16[4,128,1280]{2,1,0:T(8,128)(2,1)}, bf16[4,128,1280]{2,1,0:T(8,128)(2,1)S(1)}, u32[]{:S(2)}, u32[]{:S(2)}) collective-permute-start(bf16[4,128,1280]{2,1,0:T(8,128)(2,1)} %get-tuple-element.130.pack_ref), channel_id=1, source_target_pairs={{0,2},{2,0},{1,3},{3,1},{4,6},{6,4},{5,7},{7,5},{8,10},{10,8},{9,1... | collective-permute-start | bytes 3932168 | tf_op jit(solution)/shard_map/ppermute | solution.py:353
  141.2 12.1 %collective-permute-start.24 = (bf16[2,128,160]{2,1,0:T(8,128)(2,1)S(1)}, bf16[2,128,160]{2,1,0:T(8,128)(2,1)S(1)}, u32[]{:S(2)}, u32[]{:S(2)}) collective-permute-start(bf16[2,128,160]{2,1,0:T(8,128)(2,1)S(1)} %get-tuple-element.138), channel_id=1, source_target_pairs={{0,1},{1,0},{2,3},{3,2},{4,5},{5,4},{6,7},{7,6},{8,9},{9,8},{10,11... | collective-permute-start | bytes 245768 | tf_op jit(solution)/shard_map/ppermute | solution.py:346
  141.7 11.7 %collective-permute-start.25 = (bf16[2,128,160]{2,1,0:T(8,128)(2,1)S(1)}, bf16[2,128,160]{2,1,0:T(8,128)(2,1)S(1)}, u32[]{:S(2)}, u32[]{:S(2)}) collective-permute-start(bf16[2,128,160]{2,1,0:T(8,128)(2,1)S(1)} %get-tuple-element.139), channel_id=1, source_target_pairs={{0,4},{4,0},{1,5},{5,1},{2,6},{6,2},{3,7},{7,3},{8,12},{12,8},{9,1... | collective-permute-start | bytes 245768 | tf_op jit(solution)/shard_map/ppermute | solution.py:348
  142.9 10.5 %collective-permute-start.26 = (bf16[2,128,160]{2,1,0:T(8,128)(2,1)S(1)}, bf16[2,128,160]{2,1,0:T(8,128)(2,1)S(1)}, u32[]{:S(2)}, u32[]{:S(2)}) collective-permute-start(bf16[2,128,160]{2,1,0:T(8,128)(2,1)S(1)} %get-tuple-element.140), channel_id=1, source_target_pairs={{0,5},{1,4},{4,1},{5,0},{2,7},{3,6},{6,3},{7,2},{8,13},{9,12},{12,... | collective-permute-start | bytes 245768 | tf_op jit(solution)/shard_map/ppermute | solution.py:349
  154.7 8.2 %copy-start.26 = (bf16[2,128,160]{2,1,0:T(8,128)(2,1)S(1)}, bf16[2,128,160]{2,1,0:T(8,128)(2,1)}, u32[]{:S(2)}) copy-start(bf16[2,128,160]{2,1,0:T(8,128)(2,1)} %copy-done.25) | copy-start | bytes 245764
  158.0 39.2 %all-to-all-start.2 = ((bf16[4,4,8,1280]{3,2,1,0:T(8,128)(2,1)}), bf16[4,4,8,1280]{3,2,1,0:T(8,128)(2,1)}, u32[]{:S(2)}, u32[]{:S(2)}) async-start(bf16[4,4,8,1280]{3,2,1,0:T(8,128)(2,1)} %get-tuple-element.151), calls=%async_computation.2 | async-start | bytes 655360 | tf_op jit(solution)/shard_map/all_to_all | solution.py:802
  162.9 97.8 %reduce-scatter.2.cloned.1.call-start = ((), (), s32[]{:S(2)}) async-start(), calls=%async_computation.6 | async-start | bytes 1536000 | tf_op jit(solution)/shard_map/reduce_scatter | solution.py:850
  163.1 4.5 %collective-permute-start.29 = (bf16[4,128,160]{2,1,0:T(8,128)(2,1)S(1)}, bf16[4,128,160]{2,1,0:T(8,128)(2,1)S(1)}, u32[]{:S(2)}, u32[]{:S(2)}) collective-permute-start(bf16[4,128,160]{2,1,0:T(8,128)(2,1)S(1)} %pad_maximum_fusion.7), channel_id=1, source_target_pairs={{0,2},{2,0},{1,3},{3,1},{4,6},{6,4},{5,7},{7,5},{8,10},{10,8},{9,1... | collective-permute-start | bytes 491528 | tf_op jit(solution)/shard_map/ppermute | solution.py:353
  165.8 28.5 %collective-permute-start.27 = (bf16[2,3,2,40,1280]{4,3,1,0,2:T(8,128)(2,1)S(1)}, bf16[2,3,2,40,1280]{4,3,1,0,2:T(8,128)(2,1)S(1)}, u32[]{:S(2)}, u32[]{:S(2)}) collective-permute-start(bf16[2,3,2,40,1280]{4,3,1,0,2:T(8,128)(2,1)S(1)} %select_bitcast_fusion), channel_id=1, source_target_pairs={{0,1},{1,0},{2,3},{3,2},{4,5},{5,4},{6,7},{7,6},{8,9},{9,8},{10,11... | collective-permute-start | bytes 3686408 | tf_op jit(solution)/shard_map/ppermute | solution.py:346
  166.3 29.5 %collective-permute-start.28 = (bf16[2,3,80,1280]{3,2,1,0:T(8,128)(2,1)S(1)}, bf16[2,3,80,1280]{3,2,1,0:T(8,128)(2,1)S(1)}, u32[]{:S(2)}, u32[]{:S(2)}) collective-permute-start(bf16[2,3,80,1280]{3,2,1,0:T(8,128)(2,1)S(1)} %copy-done.34), channel_id=1, source_target_pairs={{0,4},{4,0},{1,5},{5,1},{2,6},{6,2},{3,7},{7,3},{8,12},{12,8},{9,1... | collective-permute-start | bytes 3686408 | tf_op jit(solution)/shard_map/ppermute | solution.py:348
  167.7 26.6 %copy-start.15 = (bf16[2,3,2,1,40,1280]{5,4,3,2,1,0:T(8,128)(2,1)S(1)}, bf16[2,3,2,1,40,1280]{5,4,3,2,1,0:T(8,128)(2,1)}, u32[]{:S(2)}) copy-start(bf16[2,3,2,1,40,1280]{5,4,3,2,1,0:T(8,128)(2,1)} %get-tuple-element.190) | copy-start | bytes 3686404
  181.1 14.7 %copy-start.2 = (bf16[336,480]{1,0:T(8,128)(2,1)}, bf16[336,480]{1,0:T(8,128)(2,1)S(1)}, u32[]{:S(2)}) copy-start(bf16[336,480]{1,0:T(8,128)(2,1)S(1)} %get-tuple-element.159) | copy-start | bytes 967684
  181.1 16.0 %collective-permute-start.30 = (bf16[336,480]{1,0:T(8,128)(2,1)S(1)}, bf16[336,480]{1,0:T(8,128)(2,1)S(1)}, u32[]{:S(2)}, u32[]{:S(2)}) collective-permute-start(bf16[336,480]{1,0:T(8,128)(2,1)S(1)} %get-tuple-element.150), channel_id=1, source_target_pairs={{0,8},{8,16},{16,24},{24,0},{1,9},{9,17},{17,25},{25,1},{2,10},{10... | collective-permute-start | bytes 967688 | tf_op jit(solution)/shard_map/ppermute | solution.py:357
  183.1 23.0 %collective-permute-start.31 = (bf16[4,128,1280]{2,1,0:T(8,128)(2,1)}, bf16[4,128,1280]{2,1,0:T(8,128)(2,1)}, u32[]{:S(2)}, u32[]{:S(2)}) collective-permute-start(bf16[4,128,1280]{2,1,0:T(8,128)(2,1)} %get-tuple-element.156), channel_id=1, source_target_pairs={{0,2},{2,0},{1,3},{3,1},{4,6},{6,4},{5,7},{7,5},{8,10},{10,8},{9,1... | collective-permute-start | bytes 3932168 | tf_op jit(solution)/shard_map/ppermute | solution.py:353
  197.1 22.7 %collective-permute-start.34 = (bf16[336,480]{1,0:T(8,128)(2,1)S(1)}, bf16[336,480]{1,0:T(8,128)(2,1)S(1)}, u32[]{:S(2)}, u32[]{:S(2)}) collective-permute-start(bf16[336,480]{1,0:T(8,128)(2,1)S(1)} %copy-done.3), channel_id=1, source_target_pairs={{0,16},{8,24},{16,0},{24,8},{1,17},{9,25},{17,1},{25,9},{2,18},{10... | collective-permute-start | bytes 967688 | tf_op jit(solution)/shard_map/ppermute | solution.py:357
  200.3 19.5 %collective-permute-start.35 = (bf16[336,480]{1,0:T(8,128)(2,1)S(1)}, bf16[336,480]{1,0:T(8,128)(2,1)S(1)}, u32[]{:S(2)}, u32[]{:S(2)}) collective-permute-start(bf16[336,480]{1,0:T(8,128)(2,1)S(1)} %get-tuple-element.160), channel_id=1, source_target_pairs={{0,24},{8,0},{16,8},{24,16},{1,25},{9,1},{17,9},{25,17},{2,26},{10... | collective-permute-start | bytes 967688 | tf_op jit(solution)/shard_map/ppermute | solution.py:357
  203.0 13.8 %collective-permute-start.33 = (bf16[2,3,40,1280]{3,2,1,0:T(8,128)(2,1)S(1)}, bf16[2,3,40,1280]{3,2,1,0:T(8,128)(2,1)S(1)}, u32[]{:S(2)}, u32[]{:S(2)}) collective-permute-start(bf16[2,3,40,1280]{3,2,1,0:T(8,128)(2,1)S(1)} %select_bitcast_fusion.1), channel_id=1, source_target_pairs={{0,1},{1,0},{2,3},{3,2},{4,5},{5,4},{6,7},{7,6},{8,9},{9,8},{10,11... | collective-permute-start | bytes 1843208 | tf_op jit(solution)/shard_map/ppermute | solution.py:346
  204.8 13.7 %collective-permute-start.32 = (bf16[2,3,40,1280]{3,2,1,0:T(8,128)(2,1)S(1)}, bf16[2,3,40,1280]{3,2,1,0:T(8,128)(2,1)S(1)}, u32[]{:S(2)}, u32[]{:S(2)}) collective-permute-start(bf16[2,3,40,1280]{3,2,1,0:T(8,128)(2,1)S(1)} %select_bitcast_fusion.2), channel_id=1, source_target_pairs={{0,4},{4,0},{1,5},{5,1},{2,6},{6,2},{3,7},{7,3},{8,12},{12,8},{9,1... | collective-permute-start | bytes 1843208 | tf_op jit(solution)/shard_map/ppermute | solution.py:348
  206.1 10.7 %copy-start.17 = (bf16[2,3,80,1280]{3,2,1,0:T(8,128)(2,1)S(1)}, bf16[2,3,80,1280]{3,2,1,0:T(8,128)(2,1)}, u32[]{:S(2)}) copy-start(bf16[2,3,80,1280]{3,2,1,0:T(8,128)(2,1)} %add_convert_fusion) | copy-start | bytes 3686404
  208.7 9.8 %copy-start.16 = (bf16[2,3,2,40,1280]{4,3,1,0,2:T(8,128)(2,1)S(1)}, bf16[2,3,2,40,1280]{4,3,1,0,2:T(8,128)(2,1)}, u32[]{:S(2)}) copy-start(bf16[2,3,2,40,1280]{4,3,1,0,2:T(8,128)(2,1)} %fusion) | copy-start | bytes 3686404
  219.9 10.3 %collective-permute-start.36 = (bf16[128,1280]{1,0:T(8,128)(2,1)}, bf16[128,1280]{1,0:T(8,128)(2,1)S(1)}, u32[]{:S(2)}, u32[]{:S(2)}) collective-permute-start(bf16[128,1280]{1,0:T(8,128)(2,1)} %get-tuple-element.162), channel_id=1, source_target_pairs={{0,1},{1,0},{2,3},{3,2},{4,5},{5,4},{6,7},{7,6},{8,9},{9,8},{10,11... | collective-permute-start | bytes 983048 | tf_op jit(solution)/shard_map/ppermute | solution.py:346
  221.4 13.4 %collective-permute-start.37 = (bf16[128,1280]{1,0:T(8,128)(2,1)}, bf16[128,1280]{1,0:T(8,128)(2,1)S(1)}, u32[]{:S(2)}, u32[]{:S(2)}) collective-permute-start(bf16[128,1280]{1,0:T(8,128)(2,1)} %get-tuple-element.163), channel_id=1, source_target_pairs={{0,4},{4,0},{1,5},{5,1},{2,6},{6,2},{3,7},{7,3},{8,12},{12,8},{9,1... | collective-permute-start | bytes 983048 | tf_op jit(solution)/shard_map/ppermute | solution.py:348
  222.1 12.7 %collective-permute-start.38 = (bf16[128,1280]{1,0:T(8,128)(2,1)}, bf16[128,1280]{1,0:T(8,128)(2,1)S(1)}, u32[]{:S(2)}, u32[]{:S(2)}) collective-permute-start(bf16[128,1280]{1,0:T(8,128)(2,1)} %get-tuple-element.164), channel_id=1, source_target_pairs={{0,5},{1,4},{4,1},{5,0},{2,7},{3,6},{6,3},{7,2},{8,13},{9,12},{12,... | collective-permute-start | bytes 983048 | tf_op jit(solution)/shard_map/ppermute | solution.py:349
  236.8 22.4 %all-to-all-start.3 = ((bf16[8,48,480]{2,1,0:T(8,128)(2,1)}), bf16[8,48,480]{2,1,0:T(8,128)(2,1)S(1)}, u32[]{:S(2)}, u32[]{:S(2)}) async-start(bf16[8,48,480]{2,1,0:T(8,128)(2,1)} %fold.1), calls=%async_computation.3 | async-start | bytes 786432 | tf_op jit(solution)/shard_map/all_to_all | solution.py:871
  242.4 9.8 %collective-permute-start.39 = (bf16[4,8,1280]{2,1,0:T(8,128)(2,1)S(1)}, bf16[4,8,1280]{2,1,0:T(8,128)(2,1)S(1)}, u32[]{:S(2)}, u32[]{:S(2)}) collective-permute-start(bf16[4,8,1280]{2,1,0:T(8,128)(2,1)S(1)} %get-tuple-element.170), channel_id=1, source_target_pairs={{0,24},{8,0},{16,8},{24,16},{1,25},{9,1},{17,9},{25,17},{2,26},{10... | collective-permute-start | bytes 245768 | tf_op jit(solution)/shard_map/ppermute | solution.py:357
  249.4 8.9 %collective-permute-start.40 = (bf16[4,8,1280]{2,1,0:T(8,128)(2,1)S(1)}, bf16[4,8,1280]{2,1,0:T(8,128)(2,1)S(1)}, u32[]{:S(2)}, u32[]{:S(2)}) collective-permute-start(bf16[4,8,1280]{2,1,0:T(8,128)(2,1)S(1)} %get-tuple-element.171), channel_id=1, source_target_pairs={{0,16},{8,24},{16,0},{24,8},{1,17},{9,25},{17,1},{25,9},{2,18},{10... | collective-permute-start | bytes 245768 | tf_op jit(solution)/shard_map/ppermute | solution.py:357
  249.4 8.9 %collective-permute-start.41 = (bf16[4,8,1280]{2,1,0:T(8,128)(2,1)S(1)}, bf16[4,8,1280]{2,1,0:T(8,128)(2,1)S(1)}, u32[]{:S(2)}, u32[]{:S(2)}) collective-permute-start(bf16[4,8,1280]{2,1,0:T(8,128)(2,1)S(1)} %get-tuple-element.172), channel_id=1, source_target_pairs={{0,8},{8,16},{16,24},{24,0},{1,9},{9,17},{17,25},{25,1},{2,10},{10... | collective-permute-start | bytes 245768 | tf_op jit(solution)/shard_map/ppermute | solution.py:357
  (21 other events, 47.3 us)
Sparse Core Ops, SparseCore 0:
  10.3 34.4 all-gather.1
  220.0 31.7 reduce-scatter.1

commit v7 on v6

--- a/solution.py
+++ b/solution.py
@@ -405,18 +405,10 @@
     return weights / jnp.sum(weights, axis=1, keepdims=True)
 
 
-def set_weights(info_ref, parts, w_ref):
-    @pl.when(pl.program_id(0) == 0)
-    def _():
-        for hop, part in enumerate(parts):
-            w_ref[pl.ds(pl.multiple_of(((info_ref[0] - hop) & 3) * 320, 320), 320), :] = part[...]
-
-
 def attend_kernel(
-    info_ref, near_ref, far_ref, gain_ref, mult_ref, w_0, w_1, w_2, w_3, pre_ref, att_near, att_far, w_ref
+    info_ref, near_ref, far_ref, gain_ref, mult_ref, w_ref, pre_ref, att_ref
 ):
     seq = pl.program_id(0)
-    set_weights(info_ref, (w_0, w_1, w_2, w_3), w_ref)
     live = live_pairs(info_ref, seq)
     wide = block_rows(near_ref, far_ref).astype(jnp.float32)
     inverse = lax.rsqrt(jnp.mean(wide * wide, axis=1, keepdims=True) + 1e-06)
@@ -432,16 +424,16 @@
         probs = soft_probs(query[:, part], key[:, part], live).astype(jnp.bfloat16)
         heads.append(jnp.dot(probs, value[:, part], preferred_element_type=jnp.float32))
     att = jnp.concatenate(heads, axis=1).astype(jnp.bfloat16).reshape(2, 4, 32, 160)
-    att_near[...] = att[0]
-    att_far[...] = att[1]
+    for chip in range(4):
+        for core in range(2):
+            att_ref[chip, core] = att[core, chip]
 
 
 def attend_back_kernel(
-    info_ref, near_ref, far_ref, gain_ref, mult_ref, w_0, w_1, w_2, w_3, pre_ref, grad_near, grad_far, gain_two_ref,
-    hid_near, hid_far, send_0, send_1, send_2, send_3, w_ref, w_acc, gain_acc, scale_acc, lines,
+    info_ref, near_ref, far_ref, gain_ref, mult_ref, w_ref, pre_ref, grad_near, grad_far, gain_two_ref,
+    hid_near, hid_far, send_0, send_1, send_2, send_3, w_acc, gain_acc, scale_acc, lines,
 ):
     seq = pl.program_id(0)
-    set_weights(info_ref, (w_0, w_1, w_2, w_3), w_ref)
 
     @pl.when(seq == 0)
     def _():
@@ -459,7 +451,7 @@
     query = (pre[:, 0:160] * mult).astype(jnp.bfloat16)
     key = pre[:, 160:320].astype(jnp.bfloat16)
     value = pre[:, 320:480].astype(jnp.bfloat16)
-    grad_att = block_rows(grad_near, grad_far)
+    grad_att = jnp.concatenate([grad_near[:, 0], grad_far[:, 0]], axis=0).reshape(256, 160)
     grad_q, grad_k, grad_v = [], [], []
     for head in range(2):
         part = slice(80 * head, 80 * head + 80)
@@ -508,7 +500,7 @@
 
 
 def feed_kernel(
-    info_ref, x_ref, g_ref, atts, gain_ref,
+    info_ref, x_ref, g_ref, atts, far_atts, gain_ref,
     near_rows, across_a, across_b, far_near_rows, far_across_a, far_across_b,
     out_ref, pack_ref, dmid_ref, datt_0, datt_1, datt_2, datt_3, gain_grad,
     weights, sems,
@@ -539,7 +531,7 @@
     for chip in range(4):
         for core in range(2):
             middle += jnp.dot(
-                atts[chip, core], weights[0, source_rows(info_ref, chip, core), :],
+                (far_atts if core else atts)[chip, core], weights[0, source_rows(info_ref, chip, core), :],
                 preferred_element_type=jnp.float32,
             )
     inverse = lax.rsqrt(jnp.mean(middle * middle, axis=1, keepdims=True) + 1e-06)
@@ -606,11 +598,33 @@
     grads = both(pack_ref[3], far_pack[3])
     for chip in range(4):
         for core in range(2):
-            att = both(atts[chip, core], far_atts[chip, 1 - core])
+            near, far = (far_atts, far_atts) if core else (atts, atts)
+            att = both(near[chip, core], far[chip, 1 - core])
             stage[0, source_rows(info_ref, chip, core), :] = trans_mult(att, grads).astype(jnp.bfloat16)
     leave(0)
     for copy in copies:
         copy.wait()
+
+
+def meet_kernel(info_ref, half_a, from_a, half_b, from_b, keep_a, away_a, keep_b, away_b):
+    y_index, x_index = info_ref[1] // 4, info_ref[1] % 2
+    for half in range(2):
+        for w in range(3):
+            for row, out in ((y_index, keep_a), (1 - y_index, away_a)):
+                out[half, w] = sum_low(half_a[half, w, row, x_index], from_a[half, w, row])
+            for row, out in ((x_index, keep_b), (1 - x_index, away_b)):
+                out[half, w] = sum_low(half_b[half, w, row], from_b[half, w, row])
+
+
+def join_kernel(keep_a, from_a, keep_b, from_b, out_ref):
+    for half in range(2):
+        for w in range(3):
+            out_ref[half, w] = sum_low(keep_a[half, w], from_a[half, w])
+            out_ref[2 + half, w] = sum_low(keep_b[half, w], from_b[half, w])
+
+
+def sum_low(left, right):
+    return (left.astype(jnp.float32) + right.astype(jnp.float32)).astype(jnp.bfloat16)
 
 
 def norm_kernel(info_ref, hid_0, hid_1, hid_2, hid_3, x_ref, dmid_ref, gain_ref, out_0, out_1, out_2, out_3, rows):
@@ -678,6 +692,8 @@
     vec_block = jnp.zeros((1, 8, width), bf16).at[0, 0, :120].set(vec)
     in_four = inputs.reshape(4, 4, 8, width)
     sent = [jnp.concatenate([pick(in_four, (z + k) % 4), vec_block]) for k in range(4)]
+    qkv = jnp.stack([w_query, w_key, w_value]).astype(bf16)
+    *sent, qkv = lax.optimization_barrier((*sent, qkv))
     got = [sent[0]] + [ring_shift(sent[k], k) for k in (1, 2, 3)]
     x_rows = by_source([item[:4] for item in got], z, 1).reshape(128, width)
     vec_rows = by_source([item[4, 0] for item in got], z, 0)
@@ -687,25 +703,17 @@
     big = jnp.stack([w_output, w_up, w_down]).astype(bf16)
     big = lax.all_gather(big, "z", axis=0)
 
-    qkv = jnp.stack([w_query, w_key, w_value]).astype(bf16)
-    own, qkv = lax.optimization_barrier((own, qkv))
-    near = [own] + [plane_shift(own, step) for step in (1, 2, 3)]
     qkv = qkv.reshape(3, 40, 8, 160).transpose(2, 1, 0, 3).reshape(8, 40, 480)
     qkv = lax.all_to_all(qkv, ("y", "core", "x"), split_axis=0, concat_axis=0, tiled=True)
-    qkv = qkv.reshape(320, 480)
-
-    late = qkv
-    *near, qkv = lax.optimization_barrier((*near, qkv))
-    near = jnp.stack(near)
-    one, three, late = lax.optimization_barrier((ring_shift(qkv, 1), ring_shift(qkv, 3), late))
-    w_parts = [qkv, one, ring_shift(late, 2), three]
+    own, qkv = lax.optimization_barrier((own, qkv.reshape(320, 480)))
+    w_qkv = lax.all_gather(qkv, "z", axis=0, tiled=True)
+    near = jnp.stack([own] + [plane_shift(own, step) for step in (1, 2, 3)])
     big, near = lax.optimization_barrier((big, near))
     far = core_swap(near)
     beside, across = plane_shift(big, 1), plane_shift(big, 2)
-    beside, across, w_parts[1] = lax.optimization_barrier((beside, across, w_parts[1]))
-    across_a = plane_shift(beside[:2], 2)
-    across_b = plane_shift(across[2:], 1)
-    near_rows = pair(big, beside, x, 2).reshape(4, 3, 80, width)
+    relay_a, relay_b = beside[:2], across[2:]
+    relay_a, relay_b, cotangent = lax.optimization_barrier((relay_a, relay_b, cotangent))
+    across_a, across_b = plane_shift(relay_a, 2), plane_shift(relay_b, 1)
 
     vecs = jnp.stack([near[:, 128:132, :120], far[:, 128:132, :120]])
     vecs = vecs.astype(f32).reshape(2, 2, 2, 4, 120)
@@ -718,51 +726,48 @@
     query_mult = LOG2E / math.sqrt(HD) * jax.nn.softplus(my_scale)
 
     limit = pltpu.CompilerParams(vmem_limit_bytes=50 * 1024 * 1024)
-    pre, att_near, att_far = pl.pallas_call(
+    pre, att_made = pl.pallas_call(
         attend_kernel,
         grid_spec=pltpu.PrefetchScalarGridSpec(
             num_scalar_prefetch=1,
             grid=(4,),
             in_specs=[
                 seq_block(4, width=width), seq_block(4, width=width),
-                whole((1, width)), whole((1, 160)), *[whole((320, 480))] * 4,
+                whole((1, width)), whole((1, 160)), whole((width, 480)),
             ],
-            out_specs=[seq_block(2, 4, width=480), seq_block(4, width=160), seq_block(4, width=160)],
-            scratch_shapes=[pltpu.VMEM((width, 480), bf16)],
+            out_specs=[seq_block(2, 4, width=480), seq_block(4, 2, width=160)],
         ),
         out_shape=[
             jax.ShapeDtypeStruct((2, 4, 128, 480), f32),
-            jax.ShapeDtypeStruct((4, 128, 160), bf16),
-            jax.ShapeDtypeStruct((4, 128, 160), bf16),
+            jax.ShapeDtypeStruct((4, 2, 128, 160), bf16),
         ],
         compiler_params=limit,
         cost_estimate=pl.CostEstimate(flops=9_000_000_000, bytes_accessed=8_000_000, transcendentals=600_000),
         name="attend",
-    )(info, near, far, gain_one, query_mult, *w_parts)
-
-    att_near, att_far, near_rows, across_a, across_b = lax.optimization_barrier(
-        (att_near, att_far, near_rows, across_a, across_b)
+    )(info, near, far, gain_one, query_mult, w_qkv)
+
+    cot_rows = lax.all_to_all(cotangent.reshape(4, 4, 8, width), "z", split_axis=0, concat_axis=0, tiled=True)
+    near_rows = pair(big, beside, x, 2).reshape(4, 3, 80, width)
+    att_made, near_rows, across_a, across_b, cot_rows = lax.optimization_barrier(
+        (att_made, near_rows, across_a, across_b, cot_rows)
     )
     far_near_rows = core_swap(near_rows)
+    atts = [att_made[0]] + [plane_shift(att_made[step], step) for step in (1, 2, 3)]
+    atts = jnp.stack(atts)
+    far_atts = core_swap(atts)
     across_a = pair(across[:2], across_a, x, 2).reshape(2, 3, 80, width)
     across_b = pair(across[2:], across_b, x, 2).reshape(2, 3, 80, width)
     far_across_a, far_across_b = core_swap(across_a), core_swap(across_b)
-    att_pair = jnp.stack([att_near, core_swap(att_far)], axis=1)
-    att_pair, cotangent = lax.optimization_barrier((att_pair, cotangent))
-    cot_rows = lax.all_to_all(cotangent.reshape(4, 4, 8, width), "z", split_axis=0, concat_axis=0, tiled=True)
     cot_rows = cot_rows.transpose(1, 0, 2, 3).reshape(128, width)
-    atts = [att_pair[0]] + [plane_shift(att_pair[step], step) for step in (1, 2, 3)]
-    atts = jnp.stack(atts)
-    far_atts, far_cot = core_swap(atts), core_swap(cot_rows)
-    atts, cot_rows, far_atts, far_cot = lax.optimization_barrier((atts, cot_rows, far_atts, far_cot))
-
+    far_cot = core_swap(cot_rows)
+    far_cot, far_atts, cot_rows = lax.optimization_barrier((far_cot, far_atts, cot_rows))
     datt_shape = jax.ShapeDtypeStruct((2, 128, 160), bf16)
     smem = pl.BlockSpec(memory_space=pltpu.SMEM)
     vmem = pl.BlockSpec(memory_space=pltpu.VMEM)
     hbm = pl.BlockSpec(memory_space=pl.ANY)
     out_rows, pack, grad_mid, *datts, gain_two_grad = pl.pallas_call(
         feed_kernel,
-        in_specs=[smem] + [vmem] * 4 + [hbm] * 6,
+        in_specs=[smem] + [vmem] * 5 + [hbm] * 6,
         out_specs=[vmem] * 8,
         out_shape=[
             jax.ShapeDtypeStruct((4, 4, 8, width), bf16),
@@ -775,7 +780,7 @@
         compiler_params=limit,
         cost_estimate=pl.CostEstimate(flops=12_000_000_000, bytes_accessed=13_000_000, transcendentals=200_000),
         name="feed",
-    )(info, x_rows, cot_rows, atts, gain_two, near_rows, across_a, across_b, far_near_rows, far_across_a, far_across_b)
+    )(info, x_rows, cot_rows, atts, far_atts, gain_two, near_rows, across_a, across_b, far_near_rows, far_across_a, far_across_b)
 
     back = [datts[0]] + [plane_shift(datts[step], step) for step in (1, 2, 3)]
 
@@ -791,20 +796,11 @@
         name="grads",
     )(info, pack, core_swap(pack), atts, far_atts, cot_rows, far_cot)
 
-    def added(left, right):
-        return (left.astype(f32) + right.astype(f32)).astype(bf16)
-
-    def halves(array, index, axis):
-        first, second = (lax.index_in_dim(array, i, axis, keepdims=False) for i in (0, 1))
-        return jnp.where(index == 0, first, second), jnp.where(index == 0, second, first)
-
-    half_a, kept_b, away_b, out_rows, *back = lax.optimization_barrier((half_a, kept_b, away_b, out_rows, *back))
-    outputs = lax.all_to_all(out_rows, "z", split_axis=0, concat_axis=0, tiled=True).reshape(16, 8, width)
-    grad_att_near = jnp.stack([item[0] for item in back])
-    grad_att_far = core_swap(jnp.stack([item[1] for item in back]))
-    kept_a, away_a = halves(half_a.reshape(2, 3, 2, 2, 40, width), x, 3)
-    kept_a = added(kept_a, plane_shift(away_a, 1))
-    kept_b = added(kept_b, plane_shift(away_b, 2)).reshape(2, 3, 2, 40, width)
+    half_a, kept_b, away_b, *back = lax.optimization_barrier((half_a, kept_b, away_b, *back))
+    half_a = half_a.reshape(2, 3, 2, 2, 40, width)
+    away_a = lax.dynamic_index_in_dim(half_a, 1 - x, 3, keepdims=False)
+    away_a, away_b, grad_atts = lax.optimization_barrier((away_a, away_b, jnp.stack(back)))
+    from_a, from_b = plane_shift(away_a, 1), plane_shift(away_b, 2)
     hid_near, hid_far, *send = pl.pallas_call(
         attend_back_kernel,
         grid_spec=pltpu.PrefetchScalarGridSpec(
@@ -812,15 +808,17 @@
             grid=(4,),
             in_specs=[
                 seq_block(4, width=width), seq_block(4, width=width),
-                whole((1, width)), whole((1, 160)), *[whole((320, 480))] * 4,
-                seq_block(2, 4, width=480), seq_block(4, width=160), seq_block(4, width=160), whole((1, width)),
+                whole((1, width)), whole((1, 160)), whole((width, 480)),
+                seq_block(2, 4, width=480),
+                *[pl.BlockSpec((4, 1, 32, 160), lambda s, info, core=core: (0, core, s, 0)) for core in range(2)],
+                whole((1, width)),
             ],
             out_specs=[
                 seq_block(4, width=width), seq_block(4, width=width),
                 *[whole((336, 480))] * 4,
             ],
             scratch_shapes=[
-                pltpu.VMEM((width, 480), bf16), pltpu.VMEM((width, 480), f32), pltpu.VMEM((1, width), f32),
+                pltpu.VMEM((width, 480), f32), pltpu.VMEM((1, width), f32),
                 pltpu.VMEM((1, 160), f32), pltpu.VMEM((8, 1, 480), f32),
             ],
         ),
@@ -832,18 +830,36 @@
         compiler_params=limit,
         cost_estimate=pl.CostEstimate(flops=15_000_000_000, bytes_accessed=12_000_000, transcendentals=600_000),
         name="attend_back",
-    )(info, near, far, gain_one, query_mult, *w_parts, pre, grad_att_near, grad_att_far, gain_two_grad)
-
+    )(info, near, far, gain_one, query_mult, w_qkv, pre, grad_atts, core_swap(grad_atts), gain_two_grad)
+
+    *send, out_rows = lax.optimization_barrier((*send, out_rows))
+    outputs = lax.all_to_all(out_rows, "z", split_axis=0, concat_axis=0, tiled=True).reshape(16, 8, width)
     one = ring_shift(send[1], 1)
     swapped = core_swap(hid_far)
-    hid = [added(hid_near[i], swapped[i]) for i in range(4)]
-    kept_a, kept_b, one, outputs, *later = lax.optimization_barrier((kept_a, kept_b, one, outputs, send[2], send[3]))
+    hid = [sum_low(hid_near[i], swapped[i]) for i in range(4)]
+    from_a, from_b, one, outputs, *later = lax.optimization_barrier(
+        (from_a, from_b, one, outputs, send[2], send[3])
+    )
     two, three = ring_shift(later[0], 2), ring_shift(later[1], 3)
-    kept_a, away_a = halves(kept_a, y, 2)
-    kept_b, away_b = halves(kept_b, x, 2)
-    kept_a = added(kept_a, plane_shift(away_a, 2))
-    kept_b = added(kept_b, plane_shift(away_b, 1))
-    kept = jnp.concatenate([kept_a, kept_b])
+    split = (2, 3, 2, 40, width)
+    keep_a, away_a, keep_b, away_b = pl.pallas_call(
+        meet_kernel,
+        in_specs=[smem] + [vmem] * 4,
+        out_specs=[vmem] * 4,
+        out_shape=[jax.ShapeDtypeStruct((2, 3, 40, width), bf16)] * 4,
+        compiler_params=limit,
+        cost_estimate=pl.CostEstimate(flops=3_000_000_000, bytes_accessed=8_000_000, transcendentals=0),
+        name="meet",
+    )(info, half_a, from_a, kept_b.reshape(split), from_b.reshape(split))
+    kept = pl.pallas_call(
+        join_kernel,
+        in_specs=[vmem] * 4,
+        out_specs=vmem,
+        out_shape=jax.ShapeDtypeStruct((4, 3, 40, width), bf16),
+        compiler_params=limit,
+        cost_estimate=pl.CostEstimate(flops=2_000_000_000, bytes_accessed=4_000_000, transcendentals=0),
+        name="join",
+    )(keep_a, plane_shift(away_a, 2), keep_b, plane_shift(away_b, 1))
     *hid, kept, two, three = lax.optimization_barrier((*hid, kept, two, three))
     moved = [plane_shift(hid[step], step) for step in (1, 2, 3)]
     *moved, mine = lax.optimization_barrier((*moved, send[0]))

time: 272 us -> 262 us (0.963)
  blocking collectives: 15.7 us -> 0 us
  waiting for transfers between devices: 90.6 us -> 106 us
  other arithmetic: 23.9 us -> 14 us
  Pallas kernels: 42.1 us -> 46.8 us
  starting transfers between devices: 62.4 us -> 58.5 us
    all_to_all x1 -> x0, blocking collectives: 15.7 us -> none  [planes(): lax.all_to_all(qkv, ('y', 'core', 'x'), split_axis=0, concat_axis=0, tile...]
    ppermute x4, waiting for transfers between devices: 4.59 us -> 12.8 us  [plane_shift(): return lax.ppermute(value, ('y', 'x'), [(0, 3), (1, 2), (2, 1), (3, 0)])]
    ppermute x8, waiting for transfers between devices: 13.8 us -> 21.7 us  [plane_shift(): return lax.ppermute(value, 'y', [(0, 1), (1, 0)])]
    ppermute x12 -> x9, waiting for transfers between devices: 34.2 us -> 28.4 us  [ring_shift(): return lax.ppermute(value, 'z', [(i, (i + step) % 4) for i in range(4)])]
    ppermute x8, waiting for transfers between devices: 32.3 us -> 37.4 us  [plane_shift(): return lax.ppermute(value, 'x', [(0, 1), (1, 0)])]
    slice x7 -> x2, local copies, waits for them, and re-layouts: 5.29 us -> 0.91 us  [the longest x1 0.87 us: planes(): relay_a, relay_b = (beside[:2], across[2:])]
    select_n x3 -> x0, other arithmetic: 4.32 us -> none  [halves(): jnp.where(index == 0, second, first)]
    pallas_call x1 -> x3, Pallas kernels: 9.68 us -> 13.7 us  [the longest x1 9.43 us: planes(): pl.pallas_call(feed_kernel, in_specs=[smem] + [vmem] * 5 + [hbm] * 6, out...]
  transfers between devices with their start and end apart: 47 -> 45, of which waited for: 21 -> 22; matrix products, arithmetic and copies ran while one was open for 11% -> 8% of each run, Pallas kernels for 12% -> 14%
where the time goes in v7:
time: 262 us; the launch traced here: 261 us
  waiting for transfers between devices  106 us (40%)
  starting transfers between devices  58.5 us (22%)
  Pallas kernels  46.8 us (18%)
  local copies, waits for them, and re-layouts  21.4 us (8%)
  between operations  14.4 us (5%)
  other arithmetic  14 us (5%)
    ppermute x8, waiting for transfers between devices, plane_shift(): return lax.ppermute(value, 'x', [(0, 1), (1, 0)])  37.4 us
    ppermute x9, waiting for transfers between devices, ring_shift(): return lax.ppermute(value, 'z', [(i, (i + step) % 4) for i in range(4)])  28.4 us
    ppermute x8, waiting for transfers between devices, plane_shift(): return lax.ppermute(value, 'y', [(0, 1), (1, 0)])  21.7 us
    ppermute x9, starting transfers between devices, ring_shift(): return lax.ppermute(value, 'z', [(i, (i + step) % 4) for i in range(4)])  19.1 us
    pallas_call x1, Pallas kernels, planes(): pl.pallas_call(attend_back_kernel, grid_spec=pltpu.PrefetchScalarGridSpec...  13.5 us
    ppermute x4, waiting for transfers between devices, plane_shift(): return lax.ppermute(value, ('y', 'x'), [(0, 3), (1, 2), (2, 1), (3, 0)])  12.8 us
    unnamed x49, local copies, waits for them, and re-layouts  9.48 us
    pallas_call x1, Pallas kernels, planes(): pl.pallas_call(feed_kernel, in_specs=[smem] + [vmem] * 5 + [hbm] * 6, out...  9.43 us
  transfers between devices with their start and end apart: 45, of which 22 were waited for; matrix products, arithmetic and copies ran while one was open for 8% of the time, Pallas kernels for 14%

profile of v7, /device:TPU:0, one launch (start us, length us, event | category | flops | bytes accessed | tf_op | source)
XLA Modules:
  0.0 261.1 jit_solution(11583557684157847181)
XLA Ops:
  7.3 1.1 convert_bitcast_fusion.2
  8.4 1.1 convert_bitcast_fusion
  10.7 5.1 %collective-permute-start = (bf16[5,8,1280]{2,1,0:T(8,128)(2,1)S(1)}, bf16[5,8,1280]{2,1,0:T(8,128)(2,1)S(1)}, u32[]{:S(2)}, u32[]{:S(2)}) collective-permute-start(bf16[5,8,1280]{2,1,0:T(8,128)(2,1)S(1)} %get-tuple-element.108), channel_id=1, source_target_pairs={{0,24},{8,0},{16,8},{24,16},{1,25},{9,1},{17,9},{25,17},{2,26},{10... | collective-permute-start | bytes 307208 | tf_op jit(solution)/shard_map/ppermute | solution.py:357
  15.8 1.0 collective-permute-start.2
  17.9 1.1 reshape.336
  18.9 3.7 %all-to-all-start = ((bf16[8,40,480]{2,1,0:T(8,128)(2,1)}), bf16[8,40,480]{2,1,0:T(8,128)(2,1)S(1)}, u32[]{:S(2)}, u32[]{:S(2)}) async-start(bf16[8,40,480]{2,1,0:T(8,128)(2,1)} %reshape.336), calls=%async_computation | async-start | bytes 655360 | tf_op jit(solution)/shard_map/all_to_all | solution.py:707
  23.4 3.1 %collective-permute-done.1 = bf16[5,8,1280]{2,1,0:T(8,128)(2,1)S(1)} collective-permute-done((bf16[5,8,1280]{2,1,0:T(8,128)(2,1)S(1)}, bf16[5,8,1280]{2,1,0:T(8,128)(2,1)S(1)}, u32[]{:S(2)}, u32[]{:S(2)}) %collective-permute-start.1) | collective-permute-done | bytes 102432 | tf_op jit(solution)/shard_map/ppermute | solution.py:357
  27.0 2.8 %all-to-all-done = bf16[8,40,480]{2,1,0:T(8,128)(2,1)S(1)} async-done(((bf16[8,40,480]{2,1,0:T(8,128)(2,1)}), bf16[8,40,480]{2,1,0:T(8,128)(2,1)S(1)}, u32[]{:S(2)}, u32[]{:S(2)}) %all-to-all-start) | async-done | bytes 307232 | tf_op jit(solution)/shard_map/all_to_all | solution.py:707
  29.8 1.0 collective-permute-start.5
  30.8 1.5 collective-permute-start.4
  32.3 1.0 collective-permute-start.3
  33.3 8.4 %collective-permute-done.5 = bf16[136,1280]{1,0:T(8,128)(2,1)S(1)} collective-permute-done((bf16[136,1280]{1,0:T(8,128)(2,1)S(1)}, bf16[136,1280]{1,0:T(8,128)(2,1)S(1)}, u32[]{:S(2)}, u32[]{:S(2)}) %collective-permute-start.5) | collective-permute-done | bytes 348192 | tf_op jit(solution)/shard_map/ppermute | solution.py:349
  41.7 6.3 %collective-permute-done.4 = bf16[136,1280]{1,0:T(8,128)(2,1)S(1)} collective-permute-done((bf16[136,1280]{1,0:T(8,128)(2,1)S(1)}, bf16[136,1280]{1,0:T(8,128)(2,1)S(1)}, u32[]{:S(2)}, u32[]{:S(2)}) %collective-permute-start.4) | collective-permute-done | bytes 348192 | tf_op jit(solution)/shard_map/ppermute | solution.py:348
  48.3 1.0 collective-permute-start.7
  50.6 26.8 %collective-permute-done.7 = bf16[4,3,40,1280]{3,2,1,0:T(8,128)(2,1)S(1)} collective-permute-done((bf16[4,3,40,1280]{3,2,1,0:T(8,128)(2,1)}, bf16[4,3,40,1280]{3,2,1,0:T(8,128)(2,1)S(1)}, u32[]{:S(2)}, u32[]{:S(2)}) %collective-permute-start.7) | collective-permute-done | bytes 1228832 | tf_op jit(solution)/shard_map/ppermute | solution.py:346
  78.3 2.4 fusion.20
  80.8 4.3 %all-to-all-start.1 = ((bf16[4,4,8,1280]{3,2,1,0:T(8,128)(2,1)}), bf16[4,4,8,1280]{3,2,1,0:T(8,128)(2,1)}, u32[]{:S(2)}, u32[]{:S(2)}) async-start(bf16[4,4,8,1280]{3,2,1,0:T(8,128)(2,1)} %bitcast.31), calls=%async_computation.1 | async-start | bytes 655360 | tf_op jit(solution)/shard_map/all_to_all | solution.py:749
  85.1 1.2 collective-permute-start.9
  87.2 2.9 %bitcast_select_fusion.near_rows = bf16[4,3,80,1280]{3,2,1,0:T(8,128)(2,1)} fusion(pred[80]{0:T(512)(128)(4,1)S(1)} %broadcast_in_dim.340, bf16[4,3,40,1280]{3,2,1,0:T(8,128)(2,1)S(1)} %collective-permute-done.7, bf16[4,3,40,1280]{3,2,1,0:T(8,128)(2,1)} %all-gather.3.cloned.1.call-done), kind=kLoop, calls=%fused_computation | loop fusion | flops 1228800 | bytes 4915280 | tf_op jit(solution)/shard_map/jit(_where)/select_n | solution.py:379
  91.4 1.3 copy-done.2
  92.8 8.2 %attend.1 = (f32[2,4,128,480]{3,2,1,0:T(8,128)}, bf16[4,2,128,160]{3,2,1,0:T(8,128)(2,1)S(1)}) custom-call(s32[6]{0:T(128)S(1)} %pad_add_fusion.info_ref, bf16[4,136,1280]{2,1,0:T(8,128)(2,1)S(1)} %pad_maximum_fusion.near_ref, bf16[4,136,1280]{2,1,0:T(8,128)(2,1)} %collective-permute-done.6.far_ref, f32[1,1280]{1,0:T(1,128)S(1)} %slice.141.gain_ref, ...), custom_call_target="tpu_custom_call" | custom-call | flops 8999999488 | bytes 8000000 | tf_op jit(solution)/shard_map/attend/pallas_call | solution.py:729
  101.1 3.0 %bitcast_select_fusion.1 = (bf16[2,3,80,1280]{3,2,1,0:T(8,128)(2,1)}, bf16[2,3,80,1280]{3,2,1,0:T(8,128)(2,1)}) fusion(pred[80]{0:T(512)(128)(4,1)S(1)} %broadcast_in_dim.340, bf16[2,3,40,1280]{3,2,1,0:T(8,128)(2,1)} %collective-permute-done.10, bf16[2,3,40,1280]{3,2,1,0:T(8,128)(2,1)S(1)} %copy-done.12, bf16[2,3,40,1280]{3,2,1,0:T(8,128)(2,1)} %collective-permute-done.9, ...), kind=kLoop, calls=%fused_computation.2 | loop fusion | flops 1228800 | bytes 4915280 | tf_op jit(solution)/shard_map/jit(_where)/select_n | solution.py:379
  104.6 1.8 collective-permute-start.14
  107.2 4.4 %collective-permute-done.14 = bf16[2,128,160]{2,1,0:T(8,128)(2,1)S(1)} collective-permute-done((bf16[2,128,160]{2,1,0:T(8,128)(2,1)S(1)}, bf16[2,128,160]{2,1,0:T(8,128)(2,1)S(1)}, u32[]{:S(2)}, u32[]{:S(2)}) %collective-permute-start.14) | collective-permute-done | bytes 81952 | tf_op jit(solution)/shard_map/ppermute | solution.py:349
  111.6 1.0 collective-permute-start.12
  112.6 1.0 copy.39
  114.3 2.3 collective-permute-done.12
  117.0 1.8 collective-permute-done.15.far_atts
  118.8 1.0 copy-done.20
  119.8 9.4 %feed.1 = (bf16[4,4,8,1280]{3,2,1,0:T(8,128)(2,1)}, bf16[4,128,1280]{2,1,0:T(8,128)(2,1)}, f32[128,1280]{1,0:T(8,128)S(1)}, bf16[2,128,160]{2,1,0:T(8,128)(2,1)S...) custom-call(s32[6]{0:T(128)S(1)} %pad_add_fusion.info_ref, ...), custom_call_target="tpu_custom_call" | custom-call | flops 12000000000 | bytes 13000000 | tf_op jit(solution)/shard_map/feed/pallas_call | solution.py:768
  130.2 1.0 collective-permute-start.20
  131.2 1.3 collective-permute-start.21
  132.5 1.2 collective-permute-start.22
  133.7 7.4 %grads.1 = (bf16[2,3,2,80,1280]{4,3,2,1,0:T(8,128)(2,1)}, bf16[2,3,80,1280]{3,2,1,0:T(8,128)(2,1)S(1)}, bf16[2,3,80,1280]{3,2,1,0:T(8,128)(2,1)}) custom-call(s32[6]{0:T(128)S(1)} %pad_add_fusion.info_ref, bf16[4,128,1280]{2,1,0:T(8,128)(2,1)} %get-tuple-element.128.pack_ref, bf16[4,128,1280]{2,1,0:T(8,128)(2,1)} %collective-permute-done.19.far_pack, ...), custom_call_target="tpu_custom_call" | custom-call | flops 6000000000 | bytes 8000000 | tf_op jit(solution)/shard_map/grads/pallas_call | solution.py:788
  141.2 2.8 %dynamic-slice_bitcast_fusion = bf16[2,3,2,40,1280]{4,3,2,1,0:T(8,128)(2,1)} fusion(bf16[2,3,2,2,40,1280]{5,4,3,2,1,0:T(8,128)(2,1)} %bitcast.116, s32[]{:T(128)S(6)} %select_n.191), kind=kLoop, calls=%fused_computation.4 | loop fusion | bytes 2457604 | tf_op jit(solution)/shard_map/jit(dynamic_index_in_dim)/squeeze | solution.py:801
  144.3 1.1 collective-permute-start.23
  145.3 1.3 collective-permute-start.24
  146.6 13.5 %attend_back.1 = (bf16[4,128,1280]{2,1,0:T(8,128)(2,1)S(1)}, bf16[4,128,1280]{2,1,0:T(8,128)(2,1)}, bf16[336,480]{1,0:T(8,128)(2,1)S(1)}, bf16[336,480]{1,0:T(8,...) custom-call(s32[6]{0:T(128)S(1)} %pad_add_fusion.info_ref, bf16[4,136,1280]{2,1,0:T(8,128)(2,1)} %copy-done, ...), custom_call_target="tpu_custom_call" | custom-call | flops 15000000512 | bytes 12000000 | tf_op jit(solution)/shard_map/attend_back/pallas_call | solution.py:804
  161.6 4.5 %all-to-all-start.2 = ((bf16[4,4,8,1280]{3,2,1,0:T(8,128)(2,1)}), bf16[4,4,8,1280]{3,2,1,0:T(8,128)(2,1)}, u32[]{:S(2)}, u32[]{:S(2)}) async-start(bf16[4,4,8,1280]{3,2,1,0:T(8,128)(2,1)} %get-tuple-element.154), calls=%async_computation.2 | async-start | bytes 655360 | tf_op jit(solution)/shard_map/all_to_all | solution.py:836
  166.1 2.0 collective-permute-start.26
  168.2 15.5 %collective-permute-done.26.part_1 = bf16[336,480]{1,0:T(8,128)(2,1)S(1)} collective-permute-done((bf16[336,480]{1,0:T(8,128)(2,1)}, bf16[336,480]{1,0:T(8,128)(2,1)S(1)}, u32[]{:S(2)}, u32[]{:S(2)}) %collective-permute-start.26) | collective-permute-done | bytes 322592 | tf_op jit(solution)/shard_map/ppermute | solution.py:357
  184.6 3.0 %meet.1 = (bf16[2,3,40,1280]{3,2,1,0:T(8,128)(2,1)S(1)}, bf16[2,3,40,1280]{3,2,1,0:T(8,128)(2,1)S(1)}, bf16[2,3,40,1280]{3,2,1,0:T(8,128)(2,1)S(1)}, bf16[2,3,40,1280]{3,2,1,0:T(8,128)(2,1)S(1)}) custom-call(s32[6]{0:T(128)S(1)} %pad_add_fusion.info_ref, bf16[2,3,2,2,40,1280]{5,4,3,2,1,0:T(8,128)(2,1)} %bitcast.117, ...), custom_call_target="tpu_custom_call" | custom-call | flops 3000000000 | bytes 8000000 | tf_op jit(solution)/shard_map/meet/pallas_call | solution.py:845
  187.5 1.1 collective-permute-start.28
  188.7 1.0 collective-permute-start.29
  189.7 1.0 collective-permute-start.30
  191.2 2.4 fusion.3
  193.6 9.2 %collective-permute-done.28.from_a = bf16[2,3,40,1280]{3,2,1,0:T(8,128)(2,1)S(1)} collective-permute-done((bf16[2,3,40,1280]{3,2,1,0:T(8,128)(2,1)S(1)}, bf16[2,3,40,1280]{3,2,1,0:T(8,128)(2,1)S(1)}, u32[]{:S(2)}, u32[]{:S(2)}) %collective-permute-start.28) | collective-permute-done | bytes 614432 | tf_op jit(solution)/shard_map/ppermute | solution.py:348
  203.6 1.3 join.1
  204.9 1.2 collective-permute-done.30.part_2
  206.1 1.0 collective-permute-done.31.part_3
  208.1 1.2 collective-permute-start.33
  209.3 1.4 collective-permute-start.34
  210.7 7.4 %collective-permute-done.32.hid_1 = bf16[128,1280]{1,0:T(8,128)(2,1)S(1)} collective-permute-done((bf16[128,1280]{1,0:T(8,128)(2,1)}, bf16[128,1280]{1,0:T(8,128)(2,1)S(1)}, u32[]{:S(2)}, u32[]{:S(2)}) %collective-permute-start.32) | collective-permute-done | bytes 327712 | tf_op jit(solution)/shard_map/ppermute | solution.py:346
  218.1 5.5 %collective-permute-done.33.hid_2 = bf16[128,1280]{1,0:T(8,128)(2,1)S(1)} collective-permute-done((bf16[128,1280]{1,0:T(8,128)(2,1)}, bf16[128,1280]{1,0:T(8,128)(2,1)S(1)}, u32[]{:S(2)}, u32[]{:S(2)}) %collective-permute-start.33) | collective-permute-done | bytes 327712 | tf_op jit(solution)/shard_map/ppermute | solution.py:348
  223.6 1.0 copy-done.10
  224.6 1.1 fold.1
  225.6 3.5 %all-to-all-start.3 = ((bf16[8,48,480]{2,1,0:T(8,128)(2,1)}), bf16[8,48,480]{2,1,0:T(8,128)(2,1)S(1)}, u32[]{:S(2)}, u32[]{:S(2)}) async-start(bf16[8,48,480]{2,1,0:T(8,128)(2,1)} %fold.1), calls=%async_computation.3 | async-start | bytes 786432 | tf_op jit(solution)/shard_map/all_to_all | solution.py:887
  229.1 1.1 copy-done.8
  230.2 1.0 norm.1
  231.2 6.3 %collective-permute-start.35 = (bf16[4,8,1280]{2,1,0:T(8,128)(2,1)S(1)}, bf16[4,8,1280]{2,1,0:T(8,128)(2,1)S(1)}, u32[]{:S(2)}, u32[]{:S(2)}) collective-permute-start(bf16[4,8,1280]{2,1,0:T(8,128)(2,1)S(1)} %get-tuple-element.178), channel_id=1, source_target_pairs={{0,24},{8,0},{16,8},{24,16},{1,25},{9,1},{17,9},{25,17},{2,26},{10... | collective-permute-start | bytes 245768 | tf_op jit(solution)/shard_map/ppermute | solution.py:357
  237.5 3.1 %collective-permute-start.36 = (bf16[4,8,1280]{2,1,0:T(8,128)(2,1)S(1)}, bf16[4,8,1280]{2,1,0:T(8,128)(2,1)S(1)}, u32[]{:S(2)}, u32[]{:S(2)}) collective-permute-start(bf16[4,8,1280]{2,1,0:T(8,128)(2,1)S(1)} %get-tuple-element.179), channel_id=1, source_target_pairs={{0,16},{8,24},{16,0},{24,8},{1,17},{9,25},{17,1},{25,9},{2,18},{10... | collective-permute-start | bytes 245768 | tf_op jit(solution)/shard_map/ppermute | solution.py:357
  241.1 1.1 collective-permute-done.35
  242.2 6.5 %collective-permute-done.36 = bf16[4,8,1280]{2,1,0:T(8,128)(2,1)S(1)} collective-permute-done((bf16[4,8,1280]{2,1,0:T(8,128)(2,1)S(1)}, bf16[4,8,1280]{2,1,0:T(8,128)(2,1)S(1)}, u32[]{:S(2)}, u32[]{:S(2)}) %collective-permute-start.36) | collective-permute-done | bytes 81952 | tf_op jit(solution)/shard_map/ppermute | solution.py:357
  252.9 1.7 copy.44
  (164 shorter events, 21.0 us)
Async XLA Ops:
  7.2 3.1 %copy-start.21 = (f32[40]{0:T(128)S(1)}, f32[40]{0:T(128)}, u32[]{:S(2)}) copy-start(f32[40]{0:T(128)} %param.23) | copy-start | bytes 484
  7.2 3.1 %copy-start.15 = (f32[40,1280]{1,0:T(8,128)S(1)}, f32[40,1280]{1,0:T(8,128)}, u32[]{:S(2)}) copy-start(f32[40,1280]{1,0:T(8,128)} %param.17) | copy-start | bytes 614404
  7.2 3.2 %copy-start.18 = (f32[40]{0:T(128)S(1)}, f32[40]{0:T(128)}, u32[]{:S(2)}) copy-start(f32[40]{0:T(128)} %param.25) | copy-start | bytes 484
  7.2 3.2 %copy-start.19 = (f32[40]{0:T(128)S(1)}, f32[40]{0:T(128)}, u32[]{:S(2)}) copy-start(f32[40]{0:T(128)} %param.24) | copy-start | bytes 484
  7.2 3.2 %copy-start.16 = (f32[40,1280]{1,0:T(8,128)S(1)}, f32[40,1280]{1,0:T(8,128)}, u32[]{:S(2)}) copy-start(f32[40,1280]{1,0:T(8,128)} %param.19) | copy-start | bytes 614404
  7.2 3.2 %copy-start.17 = (f32[40,1280]{1,0:T(8,128)S(1)}, f32[40,1280]{1,0:T(8,128)}, u32[]{:S(2)}) copy-start(f32[40,1280]{1,0:T(8,128)} %param.18) | copy-start | bytes 614404
  7.2 41.0 %all-gather.3.cloned.1.call-start = ((), (), s32[]{:S(2)}) async-start(), calls=%async_computation.5 | async-start | bytes 1536000 | tf_op jit(solution)/shard_map/all_gather | solution.py:704
  9.5 1.1 copy-start.14
  10.7 12.7 %collective-permute-start = (bf16[5,8,1280]{2,1,0:T(8,128)(2,1)S(1)}, bf16[5,8,1280]{2,1,0:T(8,128)(2,1)S(1)}, u32[]{:S(2)}, u32[]{:S(2)}) collective-permute-start(bf16[5,8,1280]{2,1,0:T(8,128)(2,1)S(1)} %get-tuple-element.108), channel_id=1, source_target_pairs={{0,24},{8,0},{16,8},{24,16},{1,25},{9,1},{17,9},{25,17},{2,26},{10... | collective-permute-start | bytes 307208 | tf_op jit(solution)/shard_map/ppermute | solution.py:357
  15.8 10.7 %collective-permute-start.1 = (bf16[5,8,1280]{2,1,0:T(8,128)(2,1)S(1)}, bf16[5,8,1280]{2,1,0:T(8,128)(2,1)S(1)}, u32[]{:S(2)}, u32[]{:S(2)}) collective-permute-start(bf16[5,8,1280]{2,1,0:T(8,128)(2,1)S(1)} %get-tuple-element.109), channel_id=1, source_target_pairs={{0,16},{8,24},{16,0},{24,8},{1,17},{9,25},{17,1},{25,9},{2,18},{10... | collective-permute-start | bytes 307208 | tf_op jit(solution)/shard_map/ppermute | solution.py:357
  15.8 10.7 %collective-permute-start.2 = (bf16[5,8,1280]{2,1,0:T(8,128)(2,1)S(1)}, bf16[5,8,1280]{2,1,0:T(8,128)(2,1)S(1)}, u32[]{:S(2)}, u32[]{:S(2)}) collective-permute-start(bf16[5,8,1280]{2,1,0:T(8,128)(2,1)S(1)} %get-tuple-element.110), channel_id=1, source_target_pairs={{0,8},{8,16},{16,24},{24,0},{1,9},{9,17},{17,25},{25,1},{2,10},{10... | collective-permute-start | bytes 307208 | tf_op jit(solution)/shard_map/ppermute | solution.py:357
  18.9 10.9 %all-to-all-start = ((bf16[8,40,480]{2,1,0:T(8,128)(2,1)}), bf16[8,40,480]{2,1,0:T(8,128)(2,1)S(1)}, u32[]{:S(2)}, u32[]{:S(2)}) async-start(bf16[8,40,480]{2,1,0:T(8,128)(2,1)} %reshape.336), calls=%async_computation | async-start | bytes 655360 | tf_op jit(solution)/shard_map/all_to_all | solution.py:707
  22.6 68.8 %all-gather.5.cloned.1.call-start = ((), (), s32[]{:S(2)}) async-start(), calls=%async_computation.6 | async-start | bytes 1638400 | tf_op jit(solution)/shard_map/all_gather | solution.py:709
  29.8 18.3 %copy-start.13 = (bf16[8,40,480]{2,1,0:T(8,128)(2,1)}, bf16[8,40,480]{2,1,0:T(8,128)(2,1)S(1)}, u32[]{:S(2)}) copy-start(bf16[8,40,480]{2,1,0:T(8,128)(2,1)S(1)} %all-to-all-done) | copy-start | bytes 921604
  29.8 11.9 %collective-permute-start.5 = (bf16[136,1280]{1,0:T(8,128)(2,1)S(1)}, bf16[136,1280]{1,0:T(8,128)(2,1)S(1)}, u32[]{:S(2)}, u32[]{:S(2)}) collective-permute-start(bf16[136,1280]{1,0:T(8,128)(2,1)S(1)} %maximum_maximum_fusion), channel_id=1, source_target_pairs={{0,5},{1,4},{4,1},{5,0},{2,7},{3,6},{6,3},{7,2},{8,13},{9,12},{12,... | collective-permute-start | bytes 1044488 | tf_op jit(solution)/shard_map/ppermute | solution.py:349
  30.8 17.2 %collective-permute-start.4 = (bf16[136,1280]{1,0:T(8,128)(2,1)S(1)}, bf16[136,1280]{1,0:T(8,128)(2,1)S(1)}, u32[]{:S(2)}, u32[]{:S(2)}) collective-permute-start(bf16[136,1280]{1,0:T(8,128)(2,1)S(1)} %maximum_maximum_fusion), channel_id=1, source_target_pairs={{0,4},{4,0},{1,5},{5,1},{2,6},{6,2},{3,7},{7,3},{8,12},{12,8},{9,1... | collective-permute-start | bytes 1044488 | tf_op jit(solution)/shard_map/ppermute | solution.py:348
  32.3 15.8 %collective-permute-start.3 = (bf16[136,1280]{1,0:T(8,128)(2,1)S(1)}, bf16[136,1280]{1,0:T(8,128)(2,1)S(1)}, u32[]{:S(2)}, u32[]{:S(2)}) collective-permute-start(bf16[136,1280]{1,0:T(8,128)(2,1)S(1)} %maximum_maximum_fusion), channel_id=1, source_target_pairs={{0,1},{1,0},{2,3},{3,2},{4,5},{5,4},{6,7},{7,6},{8,9},{9,8},{10,11... | collective-permute-start | bytes 1044488 | tf_op jit(solution)/shard_map/ppermute | solution.py:346
  48.1 2.2 copy-start.22
  48.1 2.2 copy-start.23
  48.3 43.2 %copy-start = (bf16[4,136,1280]{2,1,0:T(8,128)(2,1)}, bf16[4,136,1280]{2,1,0:T(8,128)(2,1)S(1)}, u32[]{:S(2)}) copy-start(bf16[4,136,1280]{2,1,0:T(8,128)(2,1)S(1)} %pad_maximum_fusion.near_ref) | copy-start | bytes 4177924
  48.3 29.0 %collective-permute-start.7 = (bf16[4,3,40,1280]{3,2,1,0:T(8,128)(2,1)}, bf16[4,3,40,1280]{3,2,1,0:T(8,128)(2,1)S(1)}, u32[]{:S(2)}, u32[]{:S(2)}) collective-permute-start(bf16[4,3,40,1280]{3,2,1,0:T(8,128)(2,1)} %all-gather.3.cloned.1.call-done), channel_id=1, source_target_pairs={{0,1},{1,0},{2,3},{3,2},{4,5},{5,4},{6,7},{7,6},{8,9},{9,8},{10,11... | collective-permute-start | bytes 3686408 | tf_op jit(solution)/shard_map/ppermute | solution.py:346
  49.3 29.0 %collective-permute-start.8 = (bf16[4,3,40,1280]{3,2,1,0:T(8,128)(2,1)}, bf16[4,3,40,1280]{3,2,1,0:T(8,128)(2,1)}, u32[]{:S(2)}, u32[]{:S(2)}) collective-permute-start(bf16[4,3,40,1280]{3,2,1,0:T(8,128)(2,1)} %all-gather.3.cloned.1.call-done), channel_id=1, source_target_pairs={{0,4},{4,0},{1,5},{5,1},{2,6},{6,2},{3,7},{7,3},{8,12},{12,8},{9,1... | collective-permute-start | bytes 3686408 | tf_op jit(solution)/shard_map/ppermute | solution.py:348
  50.1 40.1 %collective-permute-start.6 = (bf16[4,136,1280]{2,1,0:T(8,128)(2,1)S(1)}, bf16[4,136,1280]{2,1,0:T(8,128)(2,1)}, u32[]{:S(2)}, u32[]{:S(2)}) collective-permute-start(bf16[4,136,1280]{2,1,0:T(8,128)(2,1)S(1)} %pad_maximum_fusion.near_ref), channel_id=1, source_target_pairs={{0,2},{2,0},{1,3},{3,1},{4,6},{6,4},{5,7},{7,5},{8,10},{10,8},{9,1... | collective-permute-start | bytes 4177928 | tf_op jit(solution)/shard_map/ppermute | solution.py:353
  80.8 20.2 %all-to-all-start.1 = ((bf16[4,4,8,1280]{3,2,1,0:T(8,128)(2,1)}), bf16[4,4,8,1280]{3,2,1,0:T(8,128)(2,1)}, u32[]{:S(2)}, u32[]{:S(2)}) async-start(bf16[4,4,8,1280]{3,2,1,0:T(8,128)(2,1)} %bitcast.31), calls=%async_computation.1 | async-start | bytes 655360 | tf_op jit(solution)/shard_map/all_to_all | solution.py:749
  85.1 15.9 %collective-permute-start.9 = (bf16[2,3,40,1280]{3,2,1,0:T(8,128)(2,1)}, bf16[2,3,40,1280]{3,2,1,0:T(8,128)(2,1)}, u32[]{:S(2)}, u32[]{:S(2)}) collective-permute-start(bf16[2,3,40,1280]{3,2,1,0:T(8,128)(2,1)} %slice.174), channel_id=1, source_target_pairs={{0,4},{4,0},{1,5},{5,1},{2,6},{6,2},{3,7},{7,3},{8,12},{12,8},{9,1... | collective-permute-start | bytes 1843208 | tf_op jit(solution)/shard_map/ppermute | solution.py:348
  86.2 14.8 %collective-permute-start.10 = (bf16[2,3,40,1280]{3,2,1,0:T(8,128)(2,1)}, bf16[2,3,40,1280]{3,2,1,0:T(8,128)(2,1)}, u32[]{:S(2)}, u32[]{:S(2)}) collective-permute-start(bf16[2,3,40,1280]{3,2,1,0:T(8,128)(2,1)} %get-tuple-element.119), channel_id=1, source_target_pairs={{0,1},{1,0},{2,3},{3,2},{4,5},{5,4},{6,7},{7,6},{8,9},{9,8},{10,11... | collective-permute-start | bytes 1843208 | tf_op jit(solution)/shard_map/ppermute | solution.py:346
  91.4 1.3 copy-start.2
  92.8 8.3 %copy-start.11 = (bf16[2,3,40,1280]{3,2,1,0:T(8,128)(2,1)S(1)}, bf16[2,3,40,1280]{3,2,1,0:T(8,128)(2,1)}, u32[]{:S(2)}) copy-start(bf16[2,3,40,1280]{3,2,1,0:T(8,128)(2,1)} %get-tuple-element.197) | copy-start | bytes 1843204
  92.8 8.3 %copy-start.12 = (bf16[2,3,40,1280]{3,2,1,0:T(8,128)(2,1)S(1)}, bf16[2,3,40,1280]{3,2,1,0:T(8,128)(2,1)}, u32[]{:S(2)}) copy-start(bf16[2,3,40,1280]{3,2,1,0:T(8,128)(2,1)} %get-tuple-element.119) | copy-start | bytes 1843204
  101.1 18.7 %collective-permute-start.16 = (bf16[4,3,80,1280]{3,2,1,0:T(8,128)(2,1)}, bf16[4,3,80,1280]{3,2,1,0:T(8,128)(2,1)}, u32[]{:S(2)}, u32[]{:S(2)}) collective-permute-start(bf16[4,3,80,1280]{3,2,1,0:T(8,128)(2,1)} %bitcast_select_fusion.near_rows), channel_id=1, source_target_pairs={{0,2},{2,0},{1,3},{3,1},{4,6},{6,4},{5,7},{7,5},{8,10},{10,8},{9,1... | collective-permute-start | bytes 7372808 | tf_op jit(solution)/shard_map/ppermute | solution.py:353
  104.1 14.7 %collective-permute-start.18 = (bf16[2,3,80,1280]{3,2,1,0:T(8,128)(2,1)}, bf16[2,3,80,1280]{3,2,1,0:T(8,128)(2,1)S(1)}, u32[]{:S(2)}, u32[]{:S(2)}) collective-permute-start(bf16[2,3,80,1280]{3,2,1,0:T(8,128)(2,1)} %get-tuple-element.217.across_b), channel_id=1, source_target_pairs={{0,2},{2,0},{1,3},{3,1},{4,6},{6,4},{5,7},{7,5},{8,10},{10,8},{9,1... | collective-permute-start | bytes 3686408 | tf_op jit(solution)/shard_map/ppermute | solution.py:353
  104.6 14.2 %collective-permute-start.17 = (bf16[2,3,80,1280]{3,2,1,0:T(8,128)(2,1)}, bf16[2,3,80,1280]{3,2,1,0:T(8,128)(2,1)}, u32[]{:S(2)}, u32[]{:S(2)}) collective-permute-start(bf16[2,3,80,1280]{3,2,1,0:T(8,128)(2,1)} %get-tuple-element.218.across_a), channel_id=1, source_target_pairs={{0,2},{2,0},{1,3},{3,1},{4,6},{6,4},{5,7},{7,5},{8,10},{10,8},{9,1... | collective-permute-start | bytes 3686408 | tf_op jit(solution)/shard_map/ppermute | solution.py:353
  104.6 7.0 %collective-permute-start.14 = (bf16[2,128,160]{2,1,0:T(8,128)(2,1)S(1)}, bf16[2,128,160]{2,1,0:T(8,128)(2,1)S(1)}, u32[]{:S(2)}, u32[]{:S(2)}) collective-permute-start(bf16[2,128,160]{2,1,0:T(8,128)(2,1)S(1)} %get-tuple-element.200), channel_id=1, source_target_pairs={{0,5},{1,4},{4,1},{5,0},{2,7},{3,6},{6,3},{7,2},{8,13},{9,12},{12,... | collective-permute-start | bytes 245768 | tf_op jit(solution)/shard_map/ppermute | solution.py:349
  106.4 7.9 %collective-permute-start.13 = (bf16[2,128,160]{2,1,0:T(8,128)(2,1)S(1)}, bf16[2,128,160]{2,1,0:T(8,128)(2,1)S(1)}, u32[]{:S(2)}, u32[]{:S(2)}) collective-permute-start(bf16[2,128,160]{2,1,0:T(8,128)(2,1)S(1)} %get-tuple-element.201), channel_id=1, source_target_pairs={{0,4},{4,0},{1,5},{5,1},{2,6},{6,2},{3,7},{7,3},{8,12},{12,8},{9,1... | collective-permute-start | bytes 245768 | tf_op jit(solution)/shard_map/ppermute | solution.py:348
  111.6 5.1 %collective-permute-start.12 = (bf16[2,128,160]{2,1,0:T(8,128)(2,1)S(1)}, bf16[2,128,160]{2,1,0:T(8,128)(2,1)S(1)}, u32[]{:S(2)}, u32[]{:S(2)}) collective-permute-start(bf16[2,128,160]{2,1,0:T(8,128)(2,1)S(1)} %get-tuple-element.202), channel_id=1, source_target_pairs={{0,1},{1,0},{2,3},{3,2},{4,5},{5,4},{6,7},{7,6},{8,9},{9,8},{10,11... | collective-permute-start | bytes 245768 | tf_op jit(solution)/shard_map/ppermute | solution.py:346
  114.3 2.7 %collective-permute-start.11 = (bf16[128,1280]{1,0:T(8,128)(2,1)S(1)}, bf16[128,1280]{1,0:T(8,128)(2,1)S(1)}, u32[]{:S(2)}, u32[]{:S(2)}) collective-permute-start(bf16[128,1280]{1,0:T(8,128)(2,1)S(1)} %bitcast.107), channel_id=1, source_target_pairs={{0,2},{2,0},{1,3},{3,1},{4,6},{6,4},{5,7},{7,5},{8,10},{10,8},{9,1... | collective-permute-start | bytes 983048 | tf_op jit(solution)/shard_map/ppermute | solution.py:353
  116.8 2.0 collective-permute-start.15
  118.7 1.1 copy-start.20
  130.1 3.6 %collective-permute-start.19 = (bf16[4,128,1280]{2,1,0:T(8,128)(2,1)}, bf16[4,128,1280]{2,1,0:T(8,128)(2,1)}, u32[]{:S(2)}, u32[]{:S(2)}) collective-permute-start(bf16[4,128,1280]{2,1,0:T(8,128)(2,1)} %get-tuple-element.128.pack_ref), channel_id=1, source_target_pairs={{0,2},{2,0},{1,3},{3,1},{4,6},{6,4},{5,7},{7,5},{8,10},{10,8},{9,1... | collective-permute-start | bytes 3932168 | tf_op jit(solution)/shard_map/ppermute | solution.py:353
  130.2 11.0 %collective-permute-start.20 = (bf16[2,128,160]{2,1,0:T(8,128)(2,1)S(1)}, bf16[2,128,160]{2,1,0:T(8,128)(2,1)S(1)}, u32[]{:S(2)}, u32[]{:S(2)}) collective-permute-start(bf16[2,128,160]{2,1,0:T(8,128)(2,1)S(1)} %get-tuple-element.134), channel_id=1, source_target_pairs={{0,1},{1,0},{2,3},{3,2},{4,5},{5,4},{6,7},{7,6},{8,9},{9,8},{10,11... | collective-permute-start | bytes 245768 | tf_op jit(solution)/shard_map/ppermute | solution.py:346
  131.2 10.0 %collective-permute-start.21 = (bf16[2,128,160]{2,1,0:T(8,128)(2,1)S(1)}, bf16[2,128,160]{2,1,0:T(8,128)(2,1)S(1)}, u32[]{:S(2)}, u32[]{:S(2)}) collective-permute-start(bf16[2,128,160]{2,1,0:T(8,128)(2,1)S(1)} %get-tuple-element.135), channel_id=1, source_target_pairs={{0,4},{4,0},{1,5},{5,1},{2,6},{6,2},{3,7},{7,3},{8,12},{12,8},{9,1... | collective-permute-start | bytes 245768 | tf_op jit(solution)/shard_map/ppermute | solution.py:348
  132.5 8.7 %collective-permute-start.22 = (bf16[2,128,160]{2,1,0:T(8,128)(2,1)S(1)}, bf16[2,128,160]{2,1,0:T(8,128)(2,1)S(1)}, u32[]{:S(2)}, u32[]{:S(2)}) collective-permute-start(bf16[2,128,160]{2,1,0:T(8,128)(2,1)S(1)} %get-tuple-element.136), channel_id=1, source_target_pairs={{0,5},{1,4},{4,1},{5,0},{2,7},{3,6},{6,3},{7,2},{8,13},{9,12},{12,... | collective-permute-start | bytes 245768 | tf_op jit(solution)/shard_map/ppermute | solution.py:349
  141.2 2.9 %copy-start.6 = (bf16[2,3,80,1280]{3,2,1,0:T(8,128)(2,1)}, bf16[2,3,80,1280]{3,2,1,0:T(8,128)(2,1)S(1)}, u32[]{:S(2)}) copy-start(bf16[2,3,80,1280]{3,2,1,0:T(8,128)(2,1)S(1)} %get-tuple-element.161) | copy-start | bytes 3686404
  144.2 2.4 collective-permute-start.25
  144.3 40.3 %collective-permute-start.23 = (bf16[2,3,2,40,1280]{4,3,2,1,0:T(8,128)(2,1)}, bf16[2,3,2,40,1280]{4,3,2,1,0:T(8,128)(2,1)S(1)}, u32[]{:S(2)}, u32[]{:S(2)}) collective-permute-start(bf16[2,3,2,40,1280]{4,3,2,1,0:T(8,128)(2,1)} %dynamic-slice_bitcast_fusion), channel_id=1, source_target_pairs={{0,1},{1,0},{2,3},{3,2},{4,5},{5,4},{6,7},{7,6},{8,9},{9,8},{10,11... | collective-permute-start | bytes 3686408 | tf_op jit(solution)/shard_map/ppermute | solution.py:346
  145.3 39.2 %collective-permute-start.24 = (bf16[2,3,80,1280]{3,2,1,0:T(8,128)(2,1)}, bf16[2,3,80,1280]{3,2,1,0:T(8,128)(2,1)}, u32[]{:S(2)}, u32[]{:S(2)}) collective-permute-start(bf16[2,3,80,1280]{3,2,1,0:T(8,128)(2,1)} %get-tuple-element.144), channel_id=1, source_target_pairs={{0,4},{4,0},{1,5},{5,1},{2,6},{6,2},{3,7},{7,3},{8,12},{12,8},{9,1... | collective-permute-start | bytes 3686408 | tf_op jit(solution)/shard_map/ppermute | solution.py:348
  161.6 29.6 %collective-permute-start.27 = (bf16[4,128,1280]{2,1,0:T(8,128)(2,1)}, bf16[4,128,1280]{2,1,0:T(8,128)(2,1)}, u32[]{:S(2)}, u32[]{:S(2)}) collective-permute-start(bf16[4,128,1280]{2,1,0:T(8,128)(2,1)} %get-tuple-element.159), channel_id=1, source_target_pairs={{0,2},{2,0},{1,3},{3,1},{4,6},{6,4},{5,7},{7,5},{8,10},{10,8},{9,1... | collective-permute-start | bytes 3932168 | tf_op jit(solution)/shard_map/ppermute | solution.py:353
  161.6 22.9 %all-to-all-start.2 = ((bf16[4,4,8,1280]{3,2,1,0:T(8,128)(2,1)}), bf16[4,4,8,1280]{3,2,1,0:T(8,128)(2,1)}, u32[]{:S(2)}, u32[]{:S(2)}) async-start(bf16[4,4,8,1280]{3,2,1,0:T(8,128)(2,1)} %get-tuple-element.154), calls=%async_computation.2 | async-start | bytes 655360 | tf_op jit(solution)/shard_map/all_to_all | solution.py:836
  166.1 85.0 %reduce-scatter.2.cloned.1.call-start = ((), (), s32[]{:S(2)}) async-start(), calls=%async_computation.7 | async-start | bytes 1536000 | tf_op jit(solution)/shard_map/reduce_scatter | solution.py:866
  166.1 17.5 %collective-permute-start.26 = (bf16[336,480]{1,0:T(8,128)(2,1)}, bf16[336,480]{1,0:T(8,128)(2,1)S(1)}, u32[]{:S(2)}, u32[]{:S(2)}) collective-permute-start(bf16[336,480]{1,0:T(8,128)(2,1)} %copy-done.5), channel_id=1, source_target_pairs={{0,8},{8,16},{16,24},{24,0},{1,9},{9,17},{17,25},{25,1},{2,10},{10... | collective-permute-start | bytes 967688 | tf_op jit(solution)/shard_map/ppermute | solution.py:357
  183.6 3.9 %copy-start.3 = (bf16[336,480]{1,0:T(8,128)(2,1)}, bf16[336,480]{1,0:T(8,128)(2,1)S(1)}, u32[]{:S(2)}) copy-start(bf16[336,480]{1,0:T(8,128)(2,1)S(1)} %collective-permute-done.26.part_1) | copy-start | bytes 967684
  187.5 15.2 %collective-permute-start.28 = (bf16[2,3,40,1280]{3,2,1,0:T(8,128)(2,1)S(1)}, bf16[2,3,40,1280]{3,2,1,0:T(8,128)(2,1)S(1)}, u32[]{:S(2)}, u32[]{:S(2)}) collective-permute-start(bf16[2,3,40,1280]{3,2,1,0:T(8,128)(2,1)S(1)} %get-tuple-element.164), channel_id=1, source_target_pairs={{0,4},{4,0},{1,5},{5,1},{2,6},{6,2},{3,7},{7,3},{8,12},{12,8},{9,1... | collective-permute-start | bytes 1843208 | tf_op jit(solution)/shard_map/ppermute | solution.py:348
  188.7 14.9 %collective-permute-start.29 = (bf16[2,3,40,1280]{3,2,1,0:T(8,128)(2,1)S(1)}, bf16[2,3,40,1280]{3,2,1,0:T(8,128)(2,1)S(1)}, u32[]{:S(2)}, u32[]{:S(2)}) collective-permute-start(bf16[2,3,40,1280]{3,2,1,0:T(8,128)(2,1)S(1)} %get-tuple-element.166), channel_id=1, source_target_pairs={{0,1},{1,0},{2,3},{3,2},{4,5},{5,4},{6,7},{7,6},{8,9},{9,8},{10,11... | collective-permute-start | bytes 1843208 | tf_op jit(solution)/shard_map/ppermute | solution.py:346
  189.7 16.5 %collective-permute-start.30 = (bf16[336,480]{1,0:T(8,128)(2,1)}, bf16[336,480]{1,0:T(8,128)(2,1)S(1)}, u32[]{:S(2)}, u32[]{:S(2)}) collective-permute-start(bf16[336,480]{1,0:T(8,128)(2,1)} %get-tuple-element.167), channel_id=1, source_target_pairs={{0,16},{8,24},{16,0},{24,8},{1,17},{9,25},{17,1},{25,9},{2,18},{10... | collective-permute-start | bytes 967688 | tf_op jit(solution)/shard_map/ppermute | solution.py:357
  190.7 16.5 %collective-permute-start.31 = (bf16[336,480]{1,0:T(8,128)(2,1)}, bf16[336,480]{1,0:T(8,128)(2,1)S(1)}, u32[]{:S(2)}, u32[]{:S(2)}) collective-permute-start(bf16[336,480]{1,0:T(8,128)(2,1)} %get-tuple-element.168), channel_id=1, source_target_pairs={{0,24},{8,0},{16,8},{24,16},{1,25},{9,1},{17,9},{25,17},{2,26},{10... | collective-permute-start | bytes 967688 | tf_op jit(solution)/shard_map/ppermute | solution.py:357
  203.6 20.0 %copy-start.4 = (bf16[336,480]{1,0:T(8,128)(2,1)S(1)}, bf16[336,480]{1,0:T(8,128)(2,1)}, u32[]{:S(2)}) copy-start(bf16[336,480]{1,0:T(8,128)(2,1)} %copy-done.3) | copy-start | bytes 967684
  207.2 10.9 %collective-permute-start.32 = (bf16[128,1280]{1,0:T(8,128)(2,1)}, bf16[128,1280]{1,0:T(8,128)(2,1)S(1)}, u32[]{:S(2)}, u32[]{:S(2)}) collective-permute-start(bf16[128,1280]{1,0:T(8,128)(2,1)} %get-tuple-element.170), channel_id=1, source_target_pairs={{0,1},{1,0},{2,3},{3,2},{4,5},{5,4},{6,7},{7,6},{8,9},{9,8},{10,11... | collective-permute-start | bytes 983048 | tf_op jit(solution)/shard_map/ppermute | solution.py:346
  208.1 15.4 %collective-permute-start.33 = (bf16[128,1280]{1,0:T(8,128)(2,1)}, bf16[128,1280]{1,0:T(8,128)(2,1)S(1)}, u32[]{:S(2)}, u32[]{:S(2)}) collective-permute-start(bf16[128,1280]{1,0:T(8,128)(2,1)} %get-tuple-element.171), channel_id=1, source_target_pairs={{0,4},{4,0},{1,5},{5,1},{2,6},{6,2},{3,7},{7,3},{8,12},{12,8},{9,1... | collective-permute-start | bytes 983048 | tf_op jit(solution)/shard_map/ppermute | solution.py:348
  209.3 14.3 %collective-permute-start.34 = (bf16[128,1280]{1,0:T(8,128)(2,1)}, bf16[128,1280]{1,0:T(8,128)(2,1)S(1)}, u32[]{:S(2)}, u32[]{:S(2)}) collective-permute-start(bf16[128,1280]{1,0:T(8,128)(2,1)} %get-tuple-element.172), channel_id=1, source_target_pairs={{0,5},{1,4},{4,1},{5,0},{2,7},{3,6},{6,3},{7,2},{8,13},{9,12},{12,... | collective-permute-start | bytes 983048 | tf_op jit(solution)/shard_map/ppermute | solution.py:349
  225.6 23.9 %all-to-all-start.3 = ((bf16[8,48,480]{2,1,0:T(8,128)(2,1)}), bf16[8,48,480]{2,1,0:T(8,128)(2,1)S(1)}, u32[]{:S(2)}, u32[]{:S(2)}) async-start(bf16[8,48,480]{2,1,0:T(8,128)(2,1)} %fold.1), calls=%async_computation.3 | async-start | bytes 786432 | tf_op jit(solution)/shard_map/all_to_all | solution.py:887
  229.1 1.1 copy-start.8
  231.2 11.0 %collective-permute-start.35 = (bf16[4,8,1280]{2,1,0:T(8,128)(2,1)S(1)}, bf16[4,8,1280]{2,1,0:T(8,128)(2,1)S(1)}, u32[]{:S(2)}, u32[]{:S(2)}) collective-permute-start(bf16[4,8,1280]{2,1,0:T(8,128)(2,1)S(1)} %get-tuple-element.178), channel_id=1, source_target_pairs={{0,24},{8,0},{16,8},{24,16},{1,25},{9,1},{17,9},{25,17},{2,26},{10... | collective-permute-start | bytes 245768 | tf_op jit(solution)/shard_map/ppermute | solution.py:357
  237.5 11.1 %collective-permute-start.36 = (bf16[4,8,1280]{2,1,0:T(8,128)(2,1)S(1)}, bf16[4,8,1280]{2,1,0:T(8,128)(2,1)S(1)}, u32[]{:S(2)}, u32[]{:S(2)}) collective-permute-start(bf16[4,8,1280]{2,1,0:T(8,128)(2,1)S(1)} %get-tuple-element.179), channel_id=1, source_target_pairs={{0,16},{8,24},{16,0},{24,8},{1,17},{9,25},{17,1},{25,9},{2,18},{10... | collective-permute-start | bytes 245768 | tf_op jit(solution)/shard_map/ppermute | solution.py:357
  240.7 8.0 %collective-permute-start.37 = (bf16[4,8,1280]{2,1,0:T(8,128)(2,1)S(1)}, bf16[4,8,1280]{2,1,0:T(8,128)(2,1)S(1)}, u32[]{:S(2)}, u32[]{:S(2)}) collective-permute-start(bf16[4,8,1280]{2,1,0:T(8,128)(2,1)S(1)} %get-tuple-element.180), channel_id=1, source_target_pairs={{0,8},{8,16},{16,24},{24,0},{1,9},{9,17},{17,25},{25,1},{2,10},{10... | collective-permute-start | bytes 245768 | tf_op jit(solution)/shard_map/ppermute | solution.py:357
  (5 other events, 4.3 us)
Sparse Core Ops, SparseCore 0:
  10.4 34.5 all-gather.2
  50.4 32.6 all-gather.4
  207.3 33.7 reduce-scatter.1

commit v8 on v7

--- a/solution.py
+++ b/solution.py
@@ -572,38 +572,52 @@
     info_ref, pack_ref, far_pack, atts, far_atts, cot_ref, far_cot, half_a, kept_b, away_b, stage, sems
 ):
     y_index, core_index = info_ref[1] // 4, (info_ref[1] // 2) % 2
-    copies = []
 
     def leave(w):
+        copies = []
         for half in range(2):
             targets = [(half, row, half_a.at[half, w, row]) for row in range(2)]
             targets += [(2 + half, y_index, kept_b.at[half, w]), (2 + half, 1 - y_index, away_b.at[half, w])]
             for i, (z_index, row, target) in enumerate(targets):
-                copy = pltpu.make_async_copy(
-                    stage.at[w, block_index(z_index, row, core_index)], target, sems.at[w, 4 * half + i]
-                )
-                copy.start()
-                copies.append(copy)
+                block = pl.ds(pl.multiple_of(160 * z_index + 80 * row, 80), 80)
+                copies.append(pltpu.make_async_copy(stage.at[w, block], target, sems.at[w, 4 * half + i]))
+        return copies
 
     def both(near, far):
         return jnp.concatenate([near, far], axis=0)
 
     cots = both(cot_ref[...], far_cot[...])
-    for w, left, grads in ((2, 0, cots), (1, 1, both(pack_ref[2], far_pack[2]))):
-        for chunk in range(5):
-            part = slice(256 * chunk, 256 * chunk + 256)
-            acts = both(pack_ref[left, :, part], far_pack[left, :, part])
-            stage[w, part, :] = trans_mult(acts, grads).astype(jnp.bfloat16)
-        leave(w)
-    grads = both(pack_ref[3], far_pack[3])
-    for chip in range(4):
-        for core in range(2):
-            near, far = (far_atts, far_atts) if core else (atts, atts)
-            att = both(near[chip, core], far[chip, 1 - core])
-            stage[0, source_rows(info_ref, chip, core), :] = trans_mult(att, grads).astype(jnp.bfloat16)
-    leave(0)
-    for copy in copies:
-        copy.wait()
+    for core in range(2):
+
+        @pl.when(core_index == core)
+        def _():
+            def own_columns(near, far):
+                return both(*(
+                    jnp.concatenate([ref[:, 160 * i + 80 * core : 160 * i + 80 * core + 80] for i in range(8)], axis=1)
+                    for ref in (near, far)
+                ))
+
+            acts = own_columns(pack_ref.at[0], far_pack.at[0])
+            stage[2] = trans_mult(acts, cots).astype(jnp.bfloat16)
+            for copy in leave(2):
+                copy.start()
+            acts = own_columns(pack_ref.at[1], far_pack.at[1])
+            stage[1] = trans_mult(acts, both(pack_ref[2], far_pack[2])).astype(jnp.bfloat16)
+            for copy in leave(1):
+                copy.start()
+            grads = both(pack_ref[3], far_pack[3])
+            for chip in range(4):
+                for source in range(2):
+                    near, far = (far_atts, far_atts) if source else (atts, atts)
+                    att = both(near[chip, source], far[chip, 1 - source])[:, 80 * core : 80 * core + 80]
+                    place = (info_ref[1] ^ (CODES[chip] + 2 * source)) * 80
+                    stage[0, pl.ds(pl.multiple_of(place, 80), 80), :] = trans_mult(att, grads).astype(jnp.bfloat16)
+            for copy in leave(0):
+                copy.start()
+
+    for w in range(3):
+        for copy in leave(w):
+            copy.wait()
 
 
 def meet_kernel(info_ref, half_a, from_a, half_b, from_b, keep_a, away_a, keep_b, away_b):
@@ -708,11 +722,12 @@
     own, qkv = lax.optimization_barrier((own, qkv.reshape(320, 480)))
     w_qkv = lax.all_gather(qkv, "z", axis=0, tiled=True)
     near = jnp.stack([own] + [plane_shift(own, step) for step in (1, 2, 3)])
-    big, near = lax.optimization_barrier((big, near))
+    big, near, cotangent = lax.optimization_barrier((big, near, cotangent))
     far = core_swap(near)
     beside, across = plane_shift(big, 1), plane_shift(big, 2)
     relay_a, relay_b = beside[:2], across[2:]
-    relay_a, relay_b, cotangent = lax.optimization_barrier((relay_a, relay_b, cotangent))
+    cot_rows = lax.all_to_all(cotangent.reshape(4, 4, 8, width), "z", split_axis=0, concat_axis=0, tiled=True)
+    relay_a, relay_b, cot_rows = lax.optimization_barrier((relay_a, relay_b, cot_rows))
     across_a, across_b = plane_shift(relay_a, 2), plane_shift(relay_b, 1)
 
     vecs = jnp.stack([near[:, 128:132, :120], far[:, 128:132, :120]])
@@ -746,11 +761,8 @@
         name="attend",
     )(info, near, far, gain_one, query_mult, w_qkv)
 
-    cot_rows = lax.all_to_all(cotangent.reshape(4, 4, 8, width), "z", split_axis=0, concat_axis=0, tiled=True)
     near_rows = pair(big, beside, x, 2).reshape(4, 3, 80, width)
-    att_made, near_rows, across_a, across_b, cot_rows = lax.optimization_barrier(
-        (att_made, near_rows, across_a, across_b, cot_rows)
-    )
+    att_made, near_rows, across_a, across_b = lax.optimization_barrier((att_made, near_rows, across_a, across_b))
     far_near_rows = core_swap(near_rows)
     atts = [att_made[0]] + [plane_shift(att_made[step], step) for step in (1, 2, 3)]
     atts = jnp.stack(atts)
@@ -790,7 +802,7 @@
         in_specs=[smem] + [vmem] * 6,
         out_specs=[hbm] * 3,
         out_shape=[jax.ShapeDtypeStruct((2, 3, 2, 80, width), bf16), part_shape, part_shape],
-        scratch_shapes=[pltpu.VMEM((3, width, width), bf16), pltpu.SemaphoreType.DMA((3, 8))],
+        scratch_shapes=[pltpu.VMEM((3, 640, width), bf16), pltpu.SemaphoreType.DMA((3, 8))],
         compiler_params=limit,
         cost_estimate=pl.CostEstimate(flops=6_000_000_000, bytes_accessed=8_000_000, transcendentals=0),
         name="grads",
@@ -832,15 +844,14 @@
         name="attend_back",
     )(info, near, far, gain_one, query_mult, w_qkv, pre, grad_atts, core_swap(grad_atts), gain_two_grad)
 
-    *send, out_rows = lax.optimization_barrier((*send, out_rows))
+    send[0], out_rows = lax.optimization_barrier((send[0], out_rows))
     outputs = lax.all_to_all(out_rows, "z", split_axis=0, concat_axis=0, tiled=True).reshape(16, 8, width)
-    one = ring_shift(send[1], 1)
     swapped = core_swap(hid_far)
+    from_a, from_b, outputs, hid_near, *early = lax.optimization_barrier(
+        (from_a, from_b, outputs, hid_near, send[1], send[3])
+    )
+    one, three = ring_shift(early[0], 1), ring_shift(early[1], 3)
     hid = [sum_low(hid_near[i], swapped[i]) for i in range(4)]
-    from_a, from_b, one, outputs, *later = lax.optimization_barrier(
-        (from_a, from_b, one, outputs, send[2], send[3])
-    )
-    two, three = ring_shift(later[0], 2), ring_shift(later[1], 3)
     split = (2, 3, 2, 40, width)
     keep_a, away_a, keep_b, away_b = pl.pallas_call(
         meet_kernel,
@@ -860,7 +871,8 @@
         cost_estimate=pl.CostEstimate(flops=2_000_000_000, bytes_accessed=4_000_000, transcendentals=0),
         name="join",
     )(keep_a, plane_shift(away_a, 2), keep_b, plane_shift(away_b, 1))
-    *hid, kept, two, three = lax.optimization_barrier((*hid, kept, two, three))
+    *hid, kept, one, three, late = lax.optimization_barrier((*hid, kept, one, three, send[2]))
+    two = ring_shift(late, 2)
     moved = [plane_shift(hid[step], step) for step in (1, 2, 3)]
     *moved, mine = lax.optimization_barrier((*moved, send[0]))
     big_sums = lax.psum_scatter(kept, "z", scatter_dimension=0, tiled=True)[0]

time: 262 us -> 258 us (0.985)
  blocking collectives: 0 us -> 14.8 us
  starting transfers between devices: 58.5 us -> 48 us
  local copies, waits for them, and re-layouts: 21.4 us -> 15.9 us
    all_to_all x0 -> x1, blocking collectives: none -> 14.8 us  [planes(): lax.all_to_all(out_rows, 'z', split_axis=0, concat_axis=0, tiled=True)]
    ppermute x9, starting transfers between devices: 19.1 us -> 12.6 us  [ring_shift(): return lax.ppermute(value, 'z', [(i, (i + step) % 4) for i in range(4)])]
    ppermute x8, waiting for transfers between devices: 37.4 us -> 32.4 us  [plane_shift(): return lax.ppermute(value, 'x', [(0, 1), (1, 0)])]
    ppermute x9, waiting for transfers between devices: 28.4 us -> 33 us  [ring_shift(): return lax.ppermute(value, 'z', [(i, (i + step) % 4) for i in range(4)])]
    all_to_all x1 -> x0, starting transfers between devices: 4.52 us -> none  [planes(): lax.all_to_all(out_rows, 'z', split_axis=0, concat_axis=0, tiled=True)]
    unnamed x49 -> x41, local copies, waits for them, and re-layouts: 9.48 us -> 6.03 us
  transfers between devices with their start and end apart: 45 -> 44, of which waited for: 22 -> 21; matrix products, arithmetic and copies ran while one was open for 8% -> 7% of each run, Pallas kernels for 14% -> 14%
where the time goes in v8:
time: 258 us
  waiting for transfers between devices  106 us (41%)
  starting transfers between devices  48 us (19%)
  Pallas kernels  46.2 us (18%)
  local copies, waits for them, and re-layouts  15.9 us (6%)
  blocking collectives  14.8 us (6%)
  between operations  14.4 us (6%)
  other arithmetic  12.7 us (5%)
    ppermute x9, waiting for transfers between devices, ring_shift(): return lax.ppermute(value, 'z', [(i, (i + step) % 4) for i in range(4)])  33 us
    ppermute x8, waiting for transfers between devices, plane_shift(): return lax.ppermute(value, 'x', [(0, 1), (1, 0)])  32.4 us
    ppermute x8, waiting for transfers between devices, plane_shift(): return lax.ppermute(value, 'y', [(0, 1), (1, 0)])  23.2 us
    all_to_all x1, blocking collectives, planes(): lax.all_to_all(out_rows, 'z', split_axis=0, concat_axis=0, tiled=True)  14.8 us
    pallas_call x1, Pallas kernels, planes(): pl.pallas_call(attend_back_kernel, grid_spec=pltpu.PrefetchScalarGridSpec...  13 us
    ppermute x9, starting transfers between devices, ring_shift(): return lax.ppermute(value, 'z', [(i, (i + step) % 4) for i in range(4)])  12.6 us
    ppermute x4, waiting for transfers between devices, plane_shift(): return lax.ppermute(value, ('y', 'x'), [(0, 3), (1, 2), (2, 1), (3, 0)])  12.3 us
    ppermute x8, starting transfers between devices, plane_shift(): return lax.ppermute(value, 'x', [(0, 1), (1, 0)])  9.66 us
  transfers between devices with their start and end apart: 44, of which 21 were waited for; matrix products, arithmetic and copies ran while one was open for 7% of the time, Pallas kernels for 14%

profile of v8, /device:TPU:0, one launch (start us, length us, event | category | flops | bytes accessed | tf_op | source)
XLA Modules:
  0.0 257.7 jit_solution(15594869199214259942)
XLA Ops:
  7.3 1.1 convert_bitcast_fusion.2
  8.4 1.1 convert_bitcast_fusion
  10.7 5.1 %collective-permute-start = (bf16[5,8,1280]{2,1,0:T(8,128)(2,1)S(1)}, bf16[5,8,1280]{2,1,0:T(8,128)(2,1)S(1)}, u32[]{:S(2)}, u32[]{:S(2)}) collective-permute-start(bf16[5,8,1280]{2,1,0:T(8,128)(2,1)S(1)} %get-tuple-element.106), channel_id=1, source_target_pairs={{0,24},{8,0},{16,8},{24,16},{1,25},{9,1},{17,9},{25,17},{2,26},{10... | collective-permute-start | bytes 307208 | tf_op jit(solution)/shard_map/ppermute | solution.py:357
  15.8 1.0 collective-permute-start.2
  17.9 1.1 reshape.336
  18.9 3.7 %all-to-all-start = ((bf16[8,40,480]{2,1,0:T(8,128)(2,1)}), bf16[8,40,480]{2,1,0:T(8,128)(2,1)S(1)}, u32[]{:S(2)}, u32[]{:S(2)}) async-start(bf16[8,40,480]{2,1,0:T(8,128)(2,1)} %reshape.336), calls=%async_computation | async-start | bytes 655360 | tf_op jit(solution)/shard_map/all_to_all | solution.py:721
  23.4 3.1 %collective-permute-done.1 = bf16[5,8,1280]{2,1,0:T(8,128)(2,1)S(1)} collective-permute-done((bf16[5,8,1280]{2,1,0:T(8,128)(2,1)S(1)}, bf16[5,8,1280]{2,1,0:T(8,128)(2,1)S(1)}, u32[]{:S(2)}, u32[]{:S(2)}) %collective-permute-start.1) | collective-permute-done | bytes 102432 | tf_op jit(solution)/shard_map/ppermute | solution.py:357
  27.0 2.8 %all-to-all-done = bf16[8,40,480]{2,1,0:T(8,128)(2,1)S(1)} async-done(((bf16[8,40,480]{2,1,0:T(8,128)(2,1)}), bf16[8,40,480]{2,1,0:T(8,128)(2,1)S(1)}, u32[]{:S(2)}, u32[]{:S(2)}) %all-to-all-start) | async-done | bytes 307232 | tf_op jit(solution)/shard_map/all_to_all | solution.py:721
  29.8 1.0 collective-permute-start.5
  30.8 1.5 collective-permute-start.4
  32.3 1.0 collective-permute-start.3
  33.3 8.4 %collective-permute-done.5 = bf16[136,1280]{1,0:T(8,128)(2,1)S(1)} collective-permute-done((bf16[136,1280]{1,0:T(8,128)(2,1)S(1)}, bf16[136,1280]{1,0:T(8,128)(2,1)S(1)}, u32[]{:S(2)}, u32[]{:S(2)}) %collective-permute-start.5) | collective-permute-done | bytes 348192 | tf_op jit(solution)/shard_map/ppermute | solution.py:349
  41.7 6.3 %collective-permute-done.4 = bf16[136,1280]{1,0:T(8,128)(2,1)S(1)} collective-permute-done((bf16[136,1280]{1,0:T(8,128)(2,1)S(1)}, bf16[136,1280]{1,0:T(8,128)(2,1)S(1)}, u32[]{:S(2)}, u32[]{:S(2)}) %collective-permute-start.4) | collective-permute-done | bytes 348192 | tf_op jit(solution)/shard_map/ppermute | solution.py:348
  48.3 1.0 collective-permute-start.6
  50.5 4.1 %all-to-all-start.1 = ((bf16[4,4,8,1280]{3,2,1,0:T(8,128)(2,1)}), bf16[4,4,8,1280]{3,2,1,0:T(8,128)(2,1)S(1)}, u32[]{:S(2)}, u32[]{:S(2)}) async-start(bf16[4,4,8,1280]{3,2,1,0:T(8,128)(2,1)} %bitcast.124), calls=%async_computation.1 | async-start | bytes 655360 | tf_op jit(solution)/shard_map/all_to_all | solution.py:729
  54.6 22.7 %collective-permute-done.6 = bf16[4,3,40,1280]{3,2,1,0:T(8,128)(2,1)S(1)} collective-permute-done((bf16[4,3,40,1280]{3,2,1,0:T(8,128)(2,1)}, bf16[4,3,40,1280]{3,2,1,0:T(8,128)(2,1)S(1)}, u32[]{:S(2)}, u32[]{:S(2)}) %collective-permute-start.6) | collective-permute-done | bytes 1228832 | tf_op jit(solution)/shard_map/ppermute | solution.py:346
  77.3 0.9 slice.171
  78.3 2.4 fusion.20
  80.7 1.1 collective-permute-start.10
  81.8 1.0 collective-permute-start.11
  82.8 2.9 %bitcast_select_fusion.near_rows = bf16[4,3,80,1280]{3,2,1,0:T(8,128)(2,1)} fusion(pred[80]{0:T(512)(128)(4,1)S(1)} %broadcast_in_dim.340, bf16[4,3,40,1280]{3,2,1,0:T(8,128)(2,1)S(1)} %collective-permute-done.6, bf16[4,3,40,1280]{3,2,1,0:T(8,128)(2,1)} %all-gather.3.cloned.1.call-done), kind=kLoop, calls=%fused_computation | loop fusion | flops 1228800 | bytes 4915280 | tf_op jit(solution)/shard_map/jit(_where)/select_n | solution.py:379
  87.0 1.3 copy-done.2
  88.4 8.2 %attend.1 = (f32[2,4,128,480]{3,2,1,0:T(8,128)}, bf16[4,2,128,160]{3,2,1,0:T(8,128)(2,1)S(1)}) custom-call(s32[6]{0:T(128)S(1)} %pad_add_fusion.info_ref, bf16[4,136,1280]{2,1,0:T(8,128)(2,1)S(1)} %pad_maximum_fusion.near_ref, bf16[4,136,1280]{2,1,0:T(8,128)(2,1)} %collective-permute-done.9.far_ref, f32[1,1280]{1,0:T(1,128)S(1)} %slice.143.gain_ref, ...), custom_call_target="tpu_custom_call" | custom-call | flops 8999999488 | bytes 8000000 | tf_op jit(solution)/shard_map/attend/pallas_call | solution.py:744
  96.7 2.9 %bitcast_select_fusion.1 = (bf16[2,3,80,1280]{3,2,1,0:T(8,128)(2,1)}, bf16[2,3,80,1280]{3,2,1,0:T(8,128)(2,1)}) fusion(pred[80]{0:T(512)(128)(4,1)S(1)} %broadcast_in_dim.340, bf16[2,3,40,1280]{3,2,1,0:T(8,128)(2,1)} %collective-permute-done.11, bf16[2,3,40,1280]{3,2,1,0:T(8,128)(2,1)S(1)} %copy-done.7, bf16[2,3,40,1280]{3,2,1,0:T(8,128)(2,1)} %collective-permute-done.10, ...), kind=kLoop, calls=%fused_computation.2 | loop fusion | flops 1228800 | bytes 4915280 | tf_op jit(solution)/shard_map/jit(_where)/select_n | solution.py:379
  100.2 1.9 collective-permute-start.14
  102.0 1.2 collective-permute-start.13
  103.3 3.9 %collective-permute-done.14 = bf16[2,128,160]{2,1,0:T(8,128)(2,1)S(1)} collective-permute-done((bf16[2,128,160]{2,1,0:T(8,128)(2,1)S(1)}, bf16[2,128,160]{2,1,0:T(8,128)(2,1)S(1)}, u32[]{:S(2)}, u32[]{:S(2)}) %collective-permute-start.14) | collective-permute-done | bytes 81952 | tf_op jit(solution)/shard_map/ppermute | solution.py:349
  107.1 1.6 collective-permute-start.12
  108.7 1.1 collective-permute-done.13
  109.9 2.3 collective-permute-done.12
  112.5 1.8 collective-permute-done.15.far_atts
  114.3 9.5 %feed.1 = (bf16[4,4,8,1280]{3,2,1,0:T(8,128)(2,1)S(1)}, bf16[4,128,1280]{2,1,0:T(8,128)(2,1)}, f32[128,1280]{1,0:T(8,128)S(1)}, bf16[2,128,160]{2,1,0:T(8,128)(2...) custom-call(s32[6]{0:T(128)S(1)} %pad_add_fusion.info_ref, ...), custom_call_target="tpu_custom_call" | custom-call | flops 12000000000 | bytes 13000000 | tf_op jit(solution)/shard_map/feed/pallas_call | solution.py:780
  124.8 1.6 collective-permute-start.20
  127.1 1.2 collective-permute-start.22
  128.3 7.3 %grads.1 = (bf16[2,3,2,80,1280]{4,3,2,1,0:T(8,128)(2,1)}, bf16[2,3,80,1280]{3,2,1,0:T(8,128)(2,1)S(1)}, bf16[2,3,80,1280]{3,2,1,0:T(8,128)(2,1)}) custom-call(s32[6]{0:T(128)S(1)} %pad_add_fusion.info_ref, bf16[4,128,1280]{2,1,0:T(8,128)(2,1)} %get-tuple-element.126.pack_ref, bf16[4,128,1280]{2,1,0:T(8,128)(2,1)} %collective-permute-done.19.far_pack, ...), custom_call_target="tpu_custom_call" | custom-call | flops 6000000000 | bytes 8000000 | tf_op jit(solution)/shard_map/grads/pallas_call | solution.py:800
  135.7 1.8 dynamic-slice_bitcast_fusion
  137.8 1.5 collective-permute-start.23
  140.1 13.0 %attend_back.1 = (bf16[4,128,1280]{2,1,0:T(8,128)(2,1)S(1)}, bf16[4,128,1280]{2,1,0:T(8,128)(2,1)}, bf16[336,480]{1,0:T(8,128)(2,1)S(1)}, bf16[336,480]{1,0:T(8,...) custom-call(s32[6]{0:T(128)S(1)} %pad_add_fusion.info_ref, bf16[4,136,1280]{2,1,0:T(8,128)(2,1)} %copy-done, ...), custom_call_target="tpu_custom_call" | custom-call | flops 15000000512 | bytes 12000000 | tf_op jit(solution)/shard_map/attend_back/pallas_call | solution.py:816
  153.1 14.8 %all_to_all.20 = bf16[4,4,8,1280]{3,2,1,0:T(8,128)(2,1)S(1)} all-to-all(bf16[4,4,8,1280]{3,2,1,0:T(8,128)(2,1)S(1)} %get-tuple-element.148), channel_id=1, replica_groups=mesh['z'=4,'y'=2,'core'=2,'x'=2] {'z'}, dimensions={0} | all-to-all | bytes 655360 | tf_op jit(solution)/shard_map/all_to_all | solution.py:848
  168.4 1.0 copy-done.16
  169.5 3.0 %meet.1 = (bf16[2,3,40,1280]{3,2,1,0:T(8,128)(2,1)S(1)}, bf16[2,3,40,1280]{3,2,1,0:T(8,128)(2,1)S(1)}, bf16[2,3,40,1280]{3,2,1,0:T(8,128)(2,1)S(1)}, bf16[2,3,40,1280]{3,2,1,0:T(8,128)(2,1)S(1)}) custom-call(s32[6]{0:T(128)S(1)} %pad_add_fusion.info_ref, bf16[2,3,2,2,40,1280]{5,4,3,2,1,0:T(8,128)(2,1)} %bitcast.119, ...), custom_call_target="tpu_custom_call" | custom-call | flops 3000000000 | bytes 8000000 | tf_op jit(solution)/shard_map/meet/pallas_call | solution.py:856
  173.3 0.9 collective-permute-start.28
  174.2 2.2 collective-permute-start.29
  176.5 1.6 collective-permute-start.30
  178.1 1.1 fusion.3
  179.2 8.4 %collective-permute-done.27.from_a = bf16[2,3,40,1280]{3,2,1,0:T(8,128)(2,1)S(1)} collective-permute-done((bf16[2,3,40,1280]{3,2,1,0:T(8,128)(2,1)S(1)}, bf16[2,3,40,1280]{3,2,1,0:T(8,128)(2,1)S(1)}, u32[]{:S(2)}, u32[]{:S(2)}) %collective-permute-start.27) | collective-permute-done | bytes 614432 | tf_op jit(solution)/shard_map/ppermute | solution.py:348
  188.1 1.3 join.1
  189.5 2.8 %collective-permute-done.30.part_3 = bf16[336,480]{1,0:T(8,128)(2,1)S(1)} collective-permute-done((bf16[336,480]{1,0:T(8,128)(2,1)S(1)}, bf16[336,480]{1,0:T(8,128)(2,1)S(1)}, u32[]{:S(2)}, u32[]{:S(2)}) %collective-permute-start.30) | collective-permute-done | bytes 322592 | tf_op jit(solution)/shard_map/ppermute | solution.py:357
  192.3 1.1 collective-permute-start.31
  193.3 1.1 collective-permute-start.32
  194.5 1.3 collective-permute-start.33
  196.4 6.7 %collective-permute-done.31.hid_1 = bf16[128,1280]{1,0:T(8,128)(2,1)S(1)} collective-permute-done((bf16[128,1280]{1,0:T(8,128)(2,1)}, bf16[128,1280]{1,0:T(8,128)(2,1)S(1)}, u32[]{:S(2)}, u32[]{:S(2)}) %collective-permute-start.31) | collective-permute-done | bytes 327712 | tf_op jit(solution)/shard_map/ppermute | solution.py:346
  203.1 6.8 %collective-permute-done.32.hid_2 = bf16[128,1280]{1,0:T(8,128)(2,1)S(1)} collective-permute-done((bf16[128,1280]{1,0:T(8,128)(2,1)}, bf16[128,1280]{1,0:T(8,128)(2,1)S(1)}, u32[]{:S(2)}, u32[]{:S(2)}) %collective-permute-start.32) | collective-permute-done | bytes 327712 | tf_op jit(solution)/shard_map/ppermute | solution.py:348
  209.9 20.2 %collective-permute-done.37.part_2 = bf16[336,480]{1,0:T(8,128)(2,1)S(1)} collective-permute-done((bf16[336,480]{1,0:T(8,128)(2,1)S(1)}, bf16[336,480]{1,0:T(8,128)(2,1)S(1)}, u32[]{:S(2)}, u32[]{:S(2)}) %collective-permute-start.37) | collective-permute-done | bytes 322592 | tf_op jit(solution)/shard_map/ppermute | solution.py:357
  230.2 1.1 fold.1
  231.2 3.5 %all-to-all-start.3 = ((bf16[8,48,480]{2,1,0:T(8,128)(2,1)}), bf16[8,48,480]{2,1,0:T(8,128)(2,1)S(1)}, u32[]{:S(2)}, u32[]{:S(2)}) async-start(bf16[8,48,480]{2,1,0:T(8,128)(2,1)} %fold.1), calls=%async_computation.3 | async-start | bytes 786432 | tf_op jit(solution)/shard_map/all_to_all | solution.py:899
  234.7 1.1 copy-done.5
  235.8 1.0 norm.1
  237.2 1.6 collective-permute-start.36
  239.4 3.4 %collective-permute-done.34 = bf16[4,8,1280]{2,1,0:T(8,128)(2,1)S(1)} collective-permute-done((bf16[4,8,1280]{2,1,0:T(8,128)(2,1)S(1)}, bf16[4,8,1280]{2,1,0:T(8,128)(2,1)S(1)}, u32[]{:S(2)}, u32[]{:S(2)}) %collective-permute-start.34) | collective-permute-done | bytes 81952 | tf_op jit(solution)/shard_map/ppermute | solution.py:357
  242.7 3.4 %collective-permute-done.35 = bf16[4,8,1280]{2,1,0:T(8,128)(2,1)S(1)} collective-permute-done((bf16[4,8,1280]{2,1,0:T(8,128)(2,1)S(1)}, bf16[4,8,1280]{2,1,0:T(8,128)(2,1)S(1)}, u32[]{:S(2)}, u32[]{:S(2)}) %collective-permute-start.35) | collective-permute-done | bytes 81952 | tf_op jit(solution)/shard_map/ppermute | solution.py:357
  246.2 0.9 fusion.5
  247.1 0.9 spread.1
  248.6 1.0 copy-done.1
  (155 shorter events, 15.6 us)
Async XLA Ops:
  7.2 3.1 %copy-start.17 = (f32[40]{0:T(128)S(1)}, f32[40]{0:T(128)}, u32[]{:S(2)}) copy-start(f32[40]{0:T(128)} %param.23) | copy-start | bytes 484
  7.2 3.1 %copy-start.10 = (f32[40,1280]{1,0:T(8,128)S(1)}, f32[40,1280]{1,0:T(8,128)}, u32[]{:S(2)}) copy-start(f32[40,1280]{1,0:T(8,128)} %param.17) | copy-start | bytes 614404
  7.2 3.2 %copy-start.13 = (f32[40]{0:T(128)S(1)}, f32[40]{0:T(128)}, u32[]{:S(2)}) copy-start(f32[40]{0:T(128)} %param.25) | copy-start | bytes 484
  7.2 3.2 %copy-start.14 = (f32[40]{0:T(128)S(1)}, f32[40]{0:T(128)}, u32[]{:S(2)}) copy-start(f32[40]{0:T(128)} %param.24) | copy-start | bytes 484
  7.2 3.2 %copy-start.11 = (f32[40,1280]{1,0:T(8,128)S(1)}, f32[40,1280]{1,0:T(8,128)}, u32[]{:S(2)}) copy-start(f32[40,1280]{1,0:T(8,128)} %param.19) | copy-start | bytes 614404
  7.2 3.2 %copy-start.12 = (f32[40,1280]{1,0:T(8,128)S(1)}, f32[40,1280]{1,0:T(8,128)}, u32[]{:S(2)}) copy-start(f32[40,1280]{1,0:T(8,128)} %param.18) | copy-start | bytes 614404
  7.2 41.1 %all-gather.3.cloned.1.call-start = ((), (), s32[]{:S(2)}) async-start(), calls=%async_computation.5 | async-start | bytes 1536000 | tf_op jit(solution)/shard_map/all_gather | solution.py:718
  9.5 1.1 copy-start.9
  10.7 12.7 %collective-permute-start = (bf16[5,8,1280]{2,1,0:T(8,128)(2,1)S(1)}, bf16[5,8,1280]{2,1,0:T(8,128)(2,1)S(1)}, u32[]{:S(2)}, u32[]{:S(2)}) collective-permute-start(bf16[5,8,1280]{2,1,0:T(8,128)(2,1)S(1)} %get-tuple-element.106), channel_id=1, source_target_pairs={{0,24},{8,0},{16,8},{24,16},{1,25},{9,1},{17,9},{25,17},{2,26},{10... | collective-permute-start | bytes 307208 | tf_op jit(solution)/shard_map/ppermute | solution.py:357
  15.8 10.7 %collective-permute-start.1 = (bf16[5,8,1280]{2,1,0:T(8,128)(2,1)S(1)}, bf16[5,8,1280]{2,1,0:T(8,128)(2,1)S(1)}, u32[]{:S(2)}, u32[]{:S(2)}) collective-permute-start(bf16[5,8,1280]{2,1,0:T(8,128)(2,1)S(1)} %get-tuple-element.107), channel_id=1, source_target_pairs={{0,16},{8,24},{16,0},{24,8},{1,17},{9,25},{17,1},{25,9},{2,18},{10... | collective-permute-start | bytes 307208 | tf_op jit(solution)/shard_map/ppermute | solution.py:357
  15.8 10.7 %collective-permute-start.2 = (bf16[5,8,1280]{2,1,0:T(8,128)(2,1)S(1)}, bf16[5,8,1280]{2,1,0:T(8,128)(2,1)S(1)}, u32[]{:S(2)}, u32[]{:S(2)}) collective-permute-start(bf16[5,8,1280]{2,1,0:T(8,128)(2,1)S(1)} %get-tuple-element.108), channel_id=1, source_target_pairs={{0,8},{8,16},{16,24},{24,0},{1,9},{9,17},{17,25},{25,1},{2,10},{10... | collective-permute-start | bytes 307208 | tf_op jit(solution)/shard_map/ppermute | solution.py:357
  18.9 10.9 %all-to-all-start = ((bf16[8,40,480]{2,1,0:T(8,128)(2,1)}), bf16[8,40,480]{2,1,0:T(8,128)(2,1)S(1)}, u32[]{:S(2)}, u32[]{:S(2)}) async-start(bf16[8,40,480]{2,1,0:T(8,128)(2,1)} %reshape.336), calls=%async_computation | async-start | bytes 655360 | tf_op jit(solution)/shard_map/all_to_all | solution.py:721
  22.6 64.4 %all-gather.5.cloned.1.call-start = ((), (), s32[]{:S(2)}) async-start(), calls=%async_computation.6 | async-start | bytes 1638400 | tf_op jit(solution)/shard_map/all_gather | solution.py:723
  29.8 18.5 %copy-start.8 = (bf16[8,40,480]{2,1,0:T(8,128)(2,1)}, bf16[8,40,480]{2,1,0:T(8,128)(2,1)S(1)}, u32[]{:S(2)}) copy-start(bf16[8,40,480]{2,1,0:T(8,128)(2,1)S(1)} %all-to-all-done) | copy-start | bytes 921604
  29.8 11.9 %collective-permute-start.5 = (bf16[136,1280]{1,0:T(8,128)(2,1)S(1)}, bf16[136,1280]{1,0:T(8,128)(2,1)S(1)}, u32[]{:S(2)}, u32[]{:S(2)}) collective-permute-start(bf16[136,1280]{1,0:T(8,128)(2,1)S(1)} %maximum_maximum_fusion), channel_id=1, source_target_pairs={{0,5},{1,4},{4,1},{5,0},{2,7},{3,6},{6,3},{7,2},{8,13},{9,12},{12,... | collective-permute-start | bytes 1044488 | tf_op jit(solution)/shard_map/ppermute | solution.py:349
  30.8 17.2 %collective-permute-start.4 = (bf16[136,1280]{1,0:T(8,128)(2,1)S(1)}, bf16[136,1280]{1,0:T(8,128)(2,1)S(1)}, u32[]{:S(2)}, u32[]{:S(2)}) collective-permute-start(bf16[136,1280]{1,0:T(8,128)(2,1)S(1)} %maximum_maximum_fusion), channel_id=1, source_target_pairs={{0,4},{4,0},{1,5},{5,1},{2,6},{6,2},{3,7},{7,3},{8,12},{12,8},{9,1... | collective-permute-start | bytes 1044488 | tf_op jit(solution)/shard_map/ppermute | solution.py:348
  32.3 15.8 %collective-permute-start.3 = (bf16[136,1280]{1,0:T(8,128)(2,1)S(1)}, bf16[136,1280]{1,0:T(8,128)(2,1)S(1)}, u32[]{:S(2)}, u32[]{:S(2)}) collective-permute-start(bf16[136,1280]{1,0:T(8,128)(2,1)S(1)} %maximum_maximum_fusion), channel_id=1, source_target_pairs={{0,1},{1,0},{2,3},{3,2},{4,5},{5,4},{6,7},{7,6},{8,9},{9,8},{10,11... | collective-permute-start | bytes 1044488 | tf_op jit(solution)/shard_map/ppermute | solution.py:346
  48.1 2.2 copy-start.18
  48.1 2.2 copy-start.19
  48.3 38.8 %copy-start = (bf16[4,136,1280]{2,1,0:T(8,128)(2,1)}, bf16[4,136,1280]{2,1,0:T(8,128)(2,1)S(1)}, u32[]{:S(2)}) copy-start(bf16[4,136,1280]{2,1,0:T(8,128)(2,1)S(1)} %pad_maximum_fusion.near_ref) | copy-start | bytes 4177924
  48.3 29.0 %collective-permute-start.6 = (bf16[4,3,40,1280]{3,2,1,0:T(8,128)(2,1)}, bf16[4,3,40,1280]{3,2,1,0:T(8,128)(2,1)S(1)}, u32[]{:S(2)}, u32[]{:S(2)}) collective-permute-start(bf16[4,3,40,1280]{3,2,1,0:T(8,128)(2,1)} %all-gather.3.cloned.1.call-done), channel_id=1, source_target_pairs={{0,1},{1,0},{2,3},{3,2},{4,5},{5,4},{6,7},{7,6},{8,9},{9,8},{10,11... | collective-permute-start | bytes 3686408 | tf_op jit(solution)/shard_map/ppermute | solution.py:346
  49.3 29.0 %collective-permute-start.7 = (bf16[4,3,40,1280]{3,2,1,0:T(8,128)(2,1)}, bf16[4,3,40,1280]{3,2,1,0:T(8,128)(2,1)}, u32[]{:S(2)}, u32[]{:S(2)}) collective-permute-start(bf16[4,3,40,1280]{3,2,1,0:T(8,128)(2,1)} %all-gather.3.cloned.1.call-done), channel_id=1, source_target_pairs={{0,4},{4,0},{1,5},{5,1},{2,6},{6,2},{3,7},{7,3},{8,12},{12,8},{9,1... | collective-permute-start | bytes 3686408 | tf_op jit(solution)/shard_map/ppermute | solution.py:348
  50.0 35.7 %collective-permute-start.9 = (bf16[4,136,1280]{2,1,0:T(8,128)(2,1)S(1)}, bf16[4,136,1280]{2,1,0:T(8,128)(2,1)}, u32[]{:S(2)}, u32[]{:S(2)}) collective-permute-start(bf16[4,136,1280]{2,1,0:T(8,128)(2,1)S(1)} %pad_maximum_fusion.near_ref), channel_id=1, source_target_pairs={{0,2},{2,0},{1,3},{3,1},{4,6},{6,4},{5,7},{7,5},{8,10},{10,8},{9,1... | collective-permute-start | bytes 4177928 | tf_op jit(solution)/shard_map/ppermute | solution.py:353
  50.5 30.2 %all-to-all-start.1 = ((bf16[4,4,8,1280]{3,2,1,0:T(8,128)(2,1)}), bf16[4,4,8,1280]{3,2,1,0:T(8,128)(2,1)S(1)}, u32[]{:S(2)}, u32[]{:S(2)}) async-start(bf16[4,4,8,1280]{3,2,1,0:T(8,128)(2,1)} %bitcast.124), calls=%async_computation.1 | async-start | bytes 655360 | tf_op jit(solution)/shard_map/all_to_all | solution.py:729
  54.6 194.0 %reduce-scatter.2.cloned.1.call-start = ((), (), s32[]{:S(2)}) async-start(), calls=%async_computation.7 | async-start | bytes 1536000 | tf_op jit(solution)/shard_map/reduce_scatter | solution.py:878
  80.7 15.9 %collective-permute-start.10 = (bf16[2,3,40,1280]{3,2,1,0:T(8,128)(2,1)}, bf16[2,3,40,1280]{3,2,1,0:T(8,128)(2,1)}, u32[]{:S(2)}, u32[]{:S(2)}) collective-permute-start(bf16[2,3,40,1280]{3,2,1,0:T(8,128)(2,1)} %slice.171), channel_id=1, source_target_pairs={{0,4},{4,0},{1,5},{5,1},{2,6},{6,2},{3,7},{7,3},{8,12},{12,8},{9,1... | collective-permute-start | bytes 1843208 | tf_op jit(solution)/shard_map/ppermute | solution.py:348
  81.8 14.9 %collective-permute-start.11 = (bf16[2,3,40,1280]{3,2,1,0:T(8,128)(2,1)}, bf16[2,3,40,1280]{3,2,1,0:T(8,128)(2,1)}, u32[]{:S(2)}, u32[]{:S(2)}) collective-permute-start(bf16[2,3,40,1280]{3,2,1,0:T(8,128)(2,1)} %get-tuple-element.119), channel_id=1, source_target_pairs={{0,1},{1,0},{2,3},{3,2},{4,5},{5,4},{6,7},{7,6},{8,9},{9,8},{10,11... | collective-permute-start | bytes 1843208 | tf_op jit(solution)/shard_map/ppermute | solution.py:346
  87.0 1.3 copy-start.2
  88.4 8.3 %copy-start.6 = (bf16[2,3,40,1280]{3,2,1,0:T(8,128)(2,1)S(1)}, bf16[2,3,40,1280]{3,2,1,0:T(8,128)(2,1)}, u32[]{:S(2)}) copy-start(bf16[2,3,40,1280]{3,2,1,0:T(8,128)(2,1)} %get-tuple-element.193) | copy-start | bytes 1843204
  88.4 8.3 %copy-start.7 = (bf16[2,3,40,1280]{3,2,1,0:T(8,128)(2,1)S(1)}, bf16[2,3,40,1280]{3,2,1,0:T(8,128)(2,1)}, u32[]{:S(2)}) copy-start(bf16[2,3,40,1280]{3,2,1,0:T(8,128)(2,1)} %get-tuple-element.119) | copy-start | bytes 1843204
  96.7 17.6 %collective-permute-start.16 = (bf16[4,3,80,1280]{3,2,1,0:T(8,128)(2,1)}, bf16[4,3,80,1280]{3,2,1,0:T(8,128)(2,1)}, u32[]{:S(2)}, u32[]{:S(2)}) collective-permute-start(bf16[4,3,80,1280]{3,2,1,0:T(8,128)(2,1)} %bitcast_select_fusion.near_rows), channel_id=1, source_target_pairs={{0,2},{2,0},{1,3},{3,1},{4,6},{6,4},{5,7},{7,5},{8,10},{10,8},{9,1... | collective-permute-start | bytes 7372808 | tf_op jit(solution)/shard_map/ppermute | solution.py:353
  99.6 14.6 %collective-permute-start.18 = (bf16[2,3,80,1280]{3,2,1,0:T(8,128)(2,1)}, bf16[2,3,80,1280]{3,2,1,0:T(8,128)(2,1)}, u32[]{:S(2)}, u32[]{:S(2)}) collective-permute-start(bf16[2,3,80,1280]{3,2,1,0:T(8,128)(2,1)} %get-tuple-element.213.across_b), channel_id=1, source_target_pairs={{0,2},{2,0},{1,3},{3,1},{4,6},{6,4},{5,7},{7,5},{8,10},{10,8},{9,1... | collective-permute-start | bytes 3686408 | tf_op jit(solution)/shard_map/ppermute | solution.py:353
  100.1 14.2 %collective-permute-start.17 = (bf16[2,3,80,1280]{3,2,1,0:T(8,128)(2,1)}, bf16[2,3,80,1280]{3,2,1,0:T(8,128)(2,1)}, u32[]{:S(2)}, u32[]{:S(2)}) collective-permute-start(bf16[2,3,80,1280]{3,2,1,0:T(8,128)(2,1)} %get-tuple-element.214.across_a), channel_id=1, source_target_pairs={{0,2},{2,0},{1,3},{3,1},{4,6},{6,4},{5,7},{7,5},{8,10},{10,8},{9,1... | collective-permute-start | bytes 3686408 | tf_op jit(solution)/shard_map/ppermute | solution.py:353
  100.2 7.0 %collective-permute-start.14 = (bf16[2,128,160]{2,1,0:T(8,128)(2,1)S(1)}, bf16[2,128,160]{2,1,0:T(8,128)(2,1)S(1)}, u32[]{:S(2)}, u32[]{:S(2)}) collective-permute-start(bf16[2,128,160]{2,1,0:T(8,128)(2,1)S(1)} %get-tuple-element.196), channel_id=1, source_target_pairs={{0,5},{1,4},{4,1},{5,0},{2,7},{3,6},{6,3},{7,2},{8,13},{9,12},{12,... | collective-permute-start | bytes 245768 | tf_op jit(solution)/shard_map/ppermute | solution.py:349
  102.0 7.8 %collective-permute-start.13 = (bf16[2,128,160]{2,1,0:T(8,128)(2,1)S(1)}, bf16[2,128,160]{2,1,0:T(8,128)(2,1)S(1)}, u32[]{:S(2)}, u32[]{:S(2)}) collective-permute-start(bf16[2,128,160]{2,1,0:T(8,128)(2,1)S(1)} %get-tuple-element.197), channel_id=1, source_target_pairs={{0,4},{4,0},{1,5},{5,1},{2,6},{6,2},{3,7},{7,3},{8,12},{12,8},{9,1... | collective-permute-start | bytes 245768 | tf_op jit(solution)/shard_map/ppermute | solution.py:348
  107.1 5.0 %collective-permute-start.12 = (bf16[2,128,160]{2,1,0:T(8,128)(2,1)S(1)}, bf16[2,128,160]{2,1,0:T(8,128)(2,1)S(1)}, u32[]{:S(2)}, u32[]{:S(2)}) collective-permute-start(bf16[2,128,160]{2,1,0:T(8,128)(2,1)S(1)} %get-tuple-element.198), channel_id=1, source_target_pairs={{0,1},{1,0},{2,3},{3,2},{4,5},{5,4},{6,7},{7,6},{8,9},{9,8},{10,11... | collective-permute-start | bytes 245768 | tf_op jit(solution)/shard_map/ppermute | solution.py:346
  109.8 2.7 %collective-permute-start.8 = (bf16[128,1280]{1,0:T(8,128)(2,1)S(1)}, bf16[128,1280]{1,0:T(8,128)(2,1)S(1)}, u32[]{:S(2)}, u32[]{:S(2)}) collective-permute-start(bf16[128,1280]{1,0:T(8,128)(2,1)S(1)} %bitcast.107), channel_id=1, source_target_pairs={{0,2},{2,0},{1,3},{3,1},{4,6},{6,4},{5,7},{7,5},{8,10},{10,8},{9,1... | collective-permute-start | bytes 983048 | tf_op jit(solution)/shard_map/ppermute | solution.py:353
  112.3 2.0 collective-permute-start.15
  123.8 0.8 copy-start.4
  124.6 3.6 %collective-permute-start.19 = (bf16[4,128,1280]{2,1,0:T(8,128)(2,1)}, bf16[4,128,1280]{2,1,0:T(8,128)(2,1)}, u32[]{:S(2)}, u32[]{:S(2)}) collective-permute-start(bf16[4,128,1280]{2,1,0:T(8,128)(2,1)} %get-tuple-element.126.pack_ref), channel_id=1, source_target_pairs={{0,2},{2,0},{1,3},{3,1},{4,6},{6,4},{5,7},{7,5},{8,10},{10,8},{9,1... | collective-permute-start | bytes 3932168 | tf_op jit(solution)/shard_map/ppermute | solution.py:353
  124.8 10.9 %collective-permute-start.20 = (bf16[2,128,160]{2,1,0:T(8,128)(2,1)S(1)}, bf16[2,128,160]{2,1,0:T(8,128)(2,1)S(1)}, u32[]{:S(2)}, u32[]{:S(2)}) collective-permute-start(bf16[2,128,160]{2,1,0:T(8,128)(2,1)S(1)} %get-tuple-element.132), channel_id=1, source_target_pairs={{0,1},{1,0},{2,3},{3,2},{4,5},{5,4},{6,7},{7,6},{8,9},{9,8},{10,11... | collective-permute-start | bytes 245768 | tf_op jit(solution)/shard_map/ppermute | solution.py:346
  126.3 9.3 %collective-permute-start.21 = (bf16[2,128,160]{2,1,0:T(8,128)(2,1)S(1)}, bf16[2,128,160]{2,1,0:T(8,128)(2,1)S(1)}, u32[]{:S(2)}, u32[]{:S(2)}) collective-permute-start(bf16[2,128,160]{2,1,0:T(8,128)(2,1)S(1)} %get-tuple-element.133), channel_id=1, source_target_pairs={{0,4},{4,0},{1,5},{5,1},{2,6},{6,2},{3,7},{7,3},{8,12},{12,8},{9,1... | collective-permute-start | bytes 245768 | tf_op jit(solution)/shard_map/ppermute | solution.py:348
  127.1 8.5 %collective-permute-start.22 = (bf16[2,128,160]{2,1,0:T(8,128)(2,1)S(1)}, bf16[2,128,160]{2,1,0:T(8,128)(2,1)S(1)}, u32[]{:S(2)}, u32[]{:S(2)}) collective-permute-start(bf16[2,128,160]{2,1,0:T(8,128)(2,1)S(1)} %get-tuple-element.134), channel_id=1, source_target_pairs={{0,5},{1,4},{4,1},{5,0},{2,7},{3,6},{6,3},{7,2},{8,13},{9,12},{12,... | collective-permute-start | bytes 245768 | tf_op jit(solution)/shard_map/ppermute | solution.py:349
  135.6 1.9 copy-start.3
  135.7 3.7 %copy-start.15 = (bf16[2,3,80,1280]{3,2,1,0:T(8,128)(2,1)S(1)}, bf16[2,3,80,1280]{3,2,1,0:T(8,128)(2,1)}, u32[]{:S(2)}) copy-start(bf16[2,3,80,1280]{3,2,1,0:T(8,128)(2,1)} %get-tuple-element.142) | copy-start | bytes 3686404
  137.6 2.5 collective-permute-start.25
  137.8 30.1 %collective-permute-start.23 = (bf16[2,3,2,40,1280]{4,3,2,1,0:T(8,128)(2,1)S(1)}, bf16[2,3,2,40,1280]{4,3,2,1,0:T(8,128)(2,1)S(1)}, u32[]{:S(2)}, u32[]{:S(2)}) collective-permute-start(bf16[2,3,2,40,1280]{4,3,2,1,0:T(8,128)(2,1)S(1)} %dynamic-slice_bitcast_fusion), channel_id=1, source_target_pairs={{0,1},{1,0},{2,3},{3,2},{4,5},{5,4},{6,7},{7,6},{8,9},{9,8},{10,11... | collective-permute-start | bytes 3686408 | tf_op jit(solution)/shard_map/ppermute | solution.py:346
  139.3 29.1 %collective-permute-start.24 = (bf16[2,3,80,1280]{3,2,1,0:T(8,128)(2,1)S(1)}, bf16[2,3,80,1280]{3,2,1,0:T(8,128)(2,1)S(1)}, u32[]{:S(2)}, u32[]{:S(2)}) collective-permute-start(bf16[2,3,80,1280]{3,2,1,0:T(8,128)(2,1)S(1)} %copy-done.15), channel_id=1, source_target_pairs={{0,4},{4,0},{1,5},{5,1},{2,6},{6,2},{3,7},{7,3},{8,12},{12,8},{9,1... | collective-permute-start | bytes 3686408 | tf_op jit(solution)/shard_map/ppermute | solution.py:348
  153.1 24.9 %collective-permute-start.26 = (bf16[4,128,1280]{2,1,0:T(8,128)(2,1)}, bf16[4,128,1280]{2,1,0:T(8,128)(2,1)S(1)}, u32[]{:S(2)}, u32[]{:S(2)}) collective-permute-start(bf16[4,128,1280]{2,1,0:T(8,128)(2,1)} %get-tuple-element.154), channel_id=1, source_target_pairs={{0,2},{2,0},{1,3},{3,1},{4,6},{6,4},{5,7},{7,5},{8,10},{10,8},{9,1... | collective-permute-start | bytes 3932168 | tf_op jit(solution)/shard_map/ppermute | solution.py:353
  168.4 1.0 copy-start.16
  172.4 15.2 %collective-permute-start.27 = (bf16[2,3,40,1280]{3,2,1,0:T(8,128)(2,1)S(1)}, bf16[2,3,40,1280]{3,2,1,0:T(8,128)(2,1)S(1)}, u32[]{:S(2)}, u32[]{:S(2)}) collective-permute-start(bf16[2,3,40,1280]{3,2,1,0:T(8,128)(2,1)S(1)} %get-tuple-element.159), channel_id=1, source_target_pairs={{0,4},{4,0},{1,5},{5,1},{2,6},{6,2},{3,7},{7,3},{8,12},{12,8},{9,1... | collective-permute-start | bytes 1843208 | tf_op jit(solution)/shard_map/ppermute | solution.py:348
  173.3 14.8 %collective-permute-start.28 = (bf16[2,3,40,1280]{3,2,1,0:T(8,128)(2,1)S(1)}, bf16[2,3,40,1280]{3,2,1,0:T(8,128)(2,1)S(1)}, u32[]{:S(2)}, u32[]{:S(2)}) collective-permute-start(bf16[2,3,40,1280]{3,2,1,0:T(8,128)(2,1)S(1)} %get-tuple-element.161), channel_id=1, source_target_pairs={{0,1},{1,0},{2,3},{3,2},{4,5},{5,4},{6,7},{7,6},{8,9},{9,8},{10,11... | collective-permute-start | bytes 1843208 | tf_op jit(solution)/shard_map/ppermute | solution.py:346
  174.2 15.2 %collective-permute-start.29 = (bf16[336,480]{1,0:T(8,128)(2,1)S(1)}, bf16[336,480]{1,0:T(8,128)(2,1)S(1)}, u32[]{:S(2)}, u32[]{:S(2)}) collective-permute-start(bf16[336,480]{1,0:T(8,128)(2,1)S(1)} %get-tuple-element.162), channel_id=1, source_target_pairs={{0,8},{8,16},{16,24},{24,0},{1,9},{9,17},{17,25},{25,1},{2,10},{10... | collective-permute-start | bytes 967688 | tf_op jit(solution)/shard_map/ppermute | solution.py:357
  176.5 15.8 %collective-permute-start.30 = (bf16[336,480]{1,0:T(8,128)(2,1)S(1)}, bf16[336,480]{1,0:T(8,128)(2,1)S(1)}, u32[]{:S(2)}, u32[]{:S(2)}) collective-permute-start(bf16[336,480]{1,0:T(8,128)(2,1)S(1)} %get-tuple-element.163), channel_id=1, source_target_pairs={{0,24},{8,0},{16,8},{24,16},{1,25},{9,1},{17,9},{25,17},{2,26},{10... | collective-permute-start | bytes 967688 | tf_op jit(solution)/shard_map/ppermute | solution.py:357
  192.3 10.8 %collective-permute-start.31 = (bf16[128,1280]{1,0:T(8,128)(2,1)}, bf16[128,1280]{1,0:T(8,128)(2,1)S(1)}, u32[]{:S(2)}, u32[]{:S(2)}) collective-permute-start(bf16[128,1280]{1,0:T(8,128)(2,1)} %get-tuple-element.166), channel_id=1, source_target_pairs={{0,1},{1,0},{2,3},{3,2},{4,5},{5,4},{6,7},{7,6},{8,9},{9,8},{10,11... | collective-permute-start | bytes 983048 | tf_op jit(solution)/shard_map/ppermute | solution.py:346
  193.3 16.6 %collective-permute-start.32 = (bf16[128,1280]{1,0:T(8,128)(2,1)}, bf16[128,1280]{1,0:T(8,128)(2,1)S(1)}, u32[]{:S(2)}, u32[]{:S(2)}) collective-permute-start(bf16[128,1280]{1,0:T(8,128)(2,1)} %get-tuple-element.167), channel_id=1, source_target_pairs={{0,4},{4,0},{1,5},{5,1},{2,6},{6,2},{3,7},{7,3},{8,12},{12,8},{9,1... | collective-permute-start | bytes 983048 | tf_op jit(solution)/shard_map/ppermute | solution.py:348
  194.5 15.4 %collective-permute-start.33 = (bf16[128,1280]{1,0:T(8,128)(2,1)}, bf16[128,1280]{1,0:T(8,128)(2,1)S(1)}, u32[]{:S(2)}, u32[]{:S(2)}) collective-permute-start(bf16[128,1280]{1,0:T(8,128)(2,1)} %get-tuple-element.168), channel_id=1, source_target_pairs={{0,5},{1,4},{4,1},{5,0},{2,7},{3,6},{6,3},{7,2},{8,13},{9,12},{12,... | collective-permute-start | bytes 983048 | tf_op jit(solution)/shard_map/ppermute | solution.py:349
  195.8 34.3 %collective-permute-start.37 = (bf16[336,480]{1,0:T(8,128)(2,1)S(1)}, bf16[336,480]{1,0:T(8,128)(2,1)S(1)}, u32[]{:S(2)}, u32[]{:S(2)}) collective-permute-start(bf16[336,480]{1,0:T(8,128)(2,1)S(1)} %get-tuple-element.180), channel_id=1, source_target_pairs={{0,16},{8,24},{16,0},{24,8},{1,17},{9,25},{17,1},{25,9},{2,18},{10... | collective-permute-start | bytes 967688 | tf_op jit(solution)/shard_map/ppermute | solution.py:357
  231.2 15.8 %all-to-all-start.3 = ((bf16[8,48,480]{2,1,0:T(8,128)(2,1)}), bf16[8,48,480]{2,1,0:T(8,128)(2,1)S(1)}, u32[]{:S(2)}, u32[]{:S(2)}) async-start(bf16[8,48,480]{2,1,0:T(8,128)(2,1)} %fold.1), calls=%async_computation.3 | async-start | bytes 786432 | tf_op jit(solution)/shard_map/all_to_all | solution.py:899
  234.7 1.1 copy-start.5
  236.8 6.0 %collective-permute-start.34 = (bf16[4,8,1280]{2,1,0:T(8,128)(2,1)S(1)}, bf16[4,8,1280]{2,1,0:T(8,128)(2,1)S(1)}, u32[]{:S(2)}, u32[]{:S(2)}) collective-permute-start(bf16[4,8,1280]{2,1,0:T(8,128)(2,1)S(1)} %get-tuple-element.174), channel_id=1, source_target_pairs={{0,24},{8,0},{16,8},{24,16},{1,25},{9,1},{17,9},{25,17},{2,26},{10... | collective-permute-start | bytes 245768 | tf_op jit(solution)/shard_map/ppermute | solution.py:357
  237.2 9.0 %collective-permute-start.35 = (bf16[4,8,1280]{2,1,0:T(8,128)(2,1)S(1)}, bf16[4,8,1280]{2,1,0:T(8,128)(2,1)S(1)}, u32[]{:S(2)}, u32[]{:S(2)}) collective-permute-start(bf16[4,8,1280]{2,1,0:T(8,128)(2,1)S(1)} %get-tuple-element.175), channel_id=1, source_target_pairs={{0,16},{8,24},{16,0},{24,8},{1,17},{9,25},{17,1},{25,9},{2,18},{10... | collective-permute-start | bytes 245768 | tf_op jit(solution)/shard_map/ppermute | solution.py:357
  237.2 9.0 %collective-permute-start.36 = (bf16[4,8,1280]{2,1,0:T(8,128)(2,1)S(1)}, bf16[4,8,1280]{2,1,0:T(8,128)(2,1)S(1)}, u32[]{:S(2)}, u32[]{:S(2)}) collective-permute-start(bf16[4,8,1280]{2,1,0:T(8,128)(2,1)S(1)} %get-tuple-element.176), channel_id=1, source_target_pairs={{0,8},{8,16},{16,24},{24,0},{1,9},{9,17},{17,25},{25,1},{2,10},{10... | collective-permute-start | bytes 245768 | tf_op jit(solution)/shard_map/ppermute | solution.py:357
  248.6 1.0 copy-start.1
Sparse Core Ops, SparseCore 0:
  10.4 34.5 all-gather.2
  50.4 36.6 all-gather.4
  192.4 39.9 reduce-scatter.1

commit v9 on v8

--- a/solution.py
+++ b/solution.py
@@ -430,7 +430,7 @@
 
 
 def attend_back_kernel(
-    info_ref, near_ref, far_ref, gain_ref, mult_ref, w_ref, pre_ref, grad_near, grad_far, gain_two_ref,
+    info_ref, near_ref, far_ref, gain_ref, mult_ref, w_ref, pre_ref, grad_near, grad_far, gain_two_ref, result_ref,
     hid_near, hid_far, send_0, send_1, send_2, send_3, w_acc, gain_acc, scale_acc, lines,
 ):
     seq = pl.program_id(0)
@@ -487,16 +487,25 @@
             target = (info_ref[0] + hop) & 3
             rows = w_acc[pl.ds(pl.multiple_of(target * 320, 320), 320), :]
             block = jnp.concatenate([rows, lines[2 * target], lines[2 * target + 1], blank], axis=0)
-            send[...] = block.astype(jnp.bfloat16)
+            send[0:336, :] = block.astype(jnp.bfloat16)
+            result = result_ref[target].reshape(32, 1280).astype(jnp.bfloat16)
+            send[336:368, :] = result[:, 0:480]
+            send[368:400, :] = result[:, 480:960]
+            send[400:432, 0:320] = result[:, 960:1280]
+            send[400:432, 320:480] = jnp.zeros((32, 160), jnp.bfloat16)
 
 
 def block_index(z_index, y_index, core):
     return pl.ds(pl.multiple_of((4 * z_index + 2 * y_index + core) * 80, 80), 80)
 
 
-def source_rows(info_ref, chip, core):
-    source = info_ref[1] ^ (CODES[chip] + 2 * core)
-    return pl.ds(pl.multiple_of(source * 160, 160), 160)
+def arrival_rows(info_ref, w, z_index, y_index, core):
+    if w > 0:
+        return block_index(z_index, y_index, core)
+    block = 4 * z_index + 2 * y_index + core
+    code = info_ref[1] ^ (block // 2)
+    arrival = 2 * ((code & 1) + 2 * (code // 4)) + ((code // 2) & 1)
+    return pl.ds(pl.multiple_of(160 * arrival + 80 * (block & 1), 80), 80)
 
 
 def feed_kernel(
@@ -517,7 +526,7 @@
                 moved.append((own.at[z_index, w], z_index, y_index, core))
                 moved.append((others[z_index // 2].at[z_index % 2, w], z_index, 1 - y_index, core))
         copies.append([
-            pltpu.make_async_copy(src, weights.at[w, block_index(*place)], sems.at[w, i])
+            pltpu.make_async_copy(src, weights.at[w, arrival_rows(info_ref, w, *place)], sems.at[w, i])
             for i, (src, *place) in enumerate(moved)
         ])
     for group in copies:
@@ -527,13 +536,11 @@
 
     for copy in copies[0]:
         copy.wait()
+    att = jnp.concatenate(
+        [(far_atts if core else atts)[chip, core] for chip in range(4) for core in range(2)], axis=1
+    )
     middle = x_ref[...].astype(jnp.float32)
-    for chip in range(4):
-        for core in range(2):
-            middle += jnp.dot(
-                (far_atts if core else atts)[chip, core], weights[0, source_rows(info_ref, chip, core), :],
-                preferred_element_type=jnp.float32,
-            )
+    middle += jnp.dot(att, weights[0], preferred_element_type=jnp.float32)
     inverse = lax.rsqrt(jnp.mean(middle * middle, axis=1, keepdims=True) + 1e-06)
     normed = middle * inverse
     gain = gain_ref[...]
@@ -552,7 +559,7 @@
     for seq in range(4):
         for plane_z in range(4):
             row = 32 * seq + 8 * plane_z
-            out_ref[plane_z, seq] = result[row : row + 8].astype(jnp.bfloat16)
+            out_ref[plane_z, seq] = result[row : row + 8]
     cot = g_ref[...]
     grad_act = mult_trans(cot, weights[2])
     grad_up = (grad_act * sigma * (1.0 + up * (1.0 - sigma))).astype(jnp.bfloat16)
@@ -563,9 +570,11 @@
     dmid_ref[...] = grad_mid
     low = grad_mid.astype(jnp.bfloat16)
     pack_ref[3] = low
+    grad_att = mult_trans(low, weights[0]).astype(jnp.bfloat16)
     for chip in range(4):
         for core in range(2):
-            datts[chip][core] = mult_trans(low, weights[0, source_rows(info_ref, chip, core), :]).astype(jnp.bfloat16)
+            lane = 160 * (2 * chip + core)
+            datts[chip][core] = grad_att[:, lane : lane + 160]
 
 
 def grads_kernel(
@@ -606,12 +615,15 @@
             for copy in leave(1):
                 copy.start()
             grads = both(pack_ref[3], far_pack[3])
+            pieces = []
             for chip in range(4):
                 for source in range(2):
                     near, far = (far_atts, far_atts) if source else (atts, atts)
-                    att = both(near[chip, source], far[chip, 1 - source])[:, 80 * core : 80 * core + 80]
-                    place = (info_ref[1] ^ (CODES[chip] + 2 * source)) * 80
-                    stage[0, pl.ds(pl.multiple_of(place, 80), 80), :] = trans_mult(att, grads).astype(jnp.bfloat16)
+                    pieces.append(both(near[chip, source], far[chip, 1 - source])[:, 80 * core : 80 * core + 80])
+            made = trans_mult(jnp.concatenate(pieces, axis=1), grads).astype(jnp.bfloat16)
+            for i in range(8):
+                place = (info_ref[1] ^ (CODES[i // 2] + 2 * (i % 2))) * 80
+                stage[0, pl.ds(pl.multiple_of(place, 80), 80), :] = made[80 * i : 80 * i + 80]
             for copy in leave(0):
                 copy.start()
 
@@ -656,16 +668,21 @@
         out[...] = rows[(info_ref[0] + hop) & 3].astype(jnp.bfloat16)
 
 
-def fold_kernel(part_0, part_1, part_2, part_3, out_ref, line):
-    total = part_0[...].astype(jnp.float32)
-    for item in (part_1, part_2, part_3):
-        total += item[...].astype(jnp.float32)
+def fold_kernel(info_ref, part_0, part_1, part_2, part_3, out_ref, home_ref, line):
+    parts = (part_0, part_1, part_2, part_3)
+    total = sum(item[0:336, :].astype(jnp.float32) for item in parts)
     line[...] = jnp.zeros_like(line)
     for owner in range(8):
         lane = 120 * (owner % 4)
         line[0:1, 0:120] = total[320 + owner // 4 : 321 + owner // 4, lane : lane + 120]
         block = jnp.concatenate([total[40 * owner : 40 * owner + 40], line[...]], axis=0)
         out_ref[owner] = block.astype(jnp.bfloat16)
+    for hop, item in enumerate(parts):
+        source = (info_ref[0] - hop) & 3
+        rows = item[336:432, :].astype(jnp.float32)
+        for i, lanes in enumerate((480, 480, 320)):
+            part = rows[32 * i : 32 * i + 32, 0:lanes].reshape(4, 8, lanes).astype(jnp.bfloat16)
+            home_ref[source, :, :, 480 * i : 480 * i + lanes] = part
 
 
 def spread_kernel(in_ref, *outs):
@@ -782,7 +799,7 @@
         in_specs=[smem] + [vmem] * 5 + [hbm] * 6,
         out_specs=[vmem] * 8,
         out_shape=[
-            jax.ShapeDtypeStruct((4, 4, 8, width), bf16),
+            jax.ShapeDtypeStruct((4, 4, 8, width), f32),
             jax.ShapeDtypeStruct((4, 128, width), bf16),
             jax.ShapeDtypeStruct((128, width), f32),
         ]
@@ -823,11 +840,11 @@
                 whole((1, width)), whole((1, 160)), whole((width, 480)),
                 seq_block(2, 4, width=480),
                 *[pl.BlockSpec((4, 1, 32, 160), lambda s, info, core=core: (0, core, s, 0)) for core in range(2)],
-                whole((1, width)),
+                whole((1, width)), whole((4, 4, 8, width)),
             ],
             out_specs=[
                 seq_block(4, width=width), seq_block(4, width=width),
-                *[whole((336, 480))] * 4,
+                *[whole((432, 480))] * 4,
             ],
             scratch_shapes=[
                 pltpu.VMEM((width, 480), f32), pltpu.VMEM((1, width), f32),
@@ -837,20 +854,17 @@
         out_shape=[
             jax.ShapeDtypeStruct((4, 128, width), bf16),
             jax.ShapeDtypeStruct((4, 128, width), bf16),
-            *[jax.ShapeDtypeStruct((336, 480), bf16)] * 4,
+            *[jax.ShapeDtypeStruct((432, 480), bf16)] * 4,
         ],
         compiler_params=limit,
         cost_estimate=pl.CostEstimate(flops=15_000_000_000, bytes_accessed=12_000_000, transcendentals=600_000),
         name="attend_back",
-    )(info, near, far, gain_one, query_mult, w_qkv, pre, grad_atts, core_swap(grad_atts), gain_two_grad)
-
-    send[0], out_rows = lax.optimization_barrier((send[0], out_rows))
-    outputs = lax.all_to_all(out_rows, "z", split_axis=0, concat_axis=0, tiled=True).reshape(16, 8, width)
+    )(info, near, far, gain_one, query_mult, w_qkv, pre, grad_atts, core_swap(grad_atts), gain_two_grad, out_rows)
+
+    one, three = ring_shift(send[1], 1), ring_shift(send[3], 3)
     swapped = core_swap(hid_far)
-    from_a, from_b, outputs, hid_near, *early = lax.optimization_barrier(
-        (from_a, from_b, outputs, hid_near, send[1], send[3])
-    )
-    one, three = ring_shift(early[0], 1), ring_shift(early[1], 3)
+    from_a, from_b, one, three, late = lax.optimization_barrier((from_a, from_b, one, three, send[2]))
+    two = ring_shift(late, 2)
     hid = [sum_low(hid_near[i], swapped[i]) for i in range(4)]
     split = (2, 3, 2, 40, width)
     keep_a, away_a, keep_b, away_b = pl.pallas_call(
@@ -871,10 +885,9 @@
         cost_estimate=pl.CostEstimate(flops=2_000_000_000, bytes_accessed=4_000_000, transcendentals=0),
         name="join",
     )(keep_a, plane_shift(away_a, 2), keep_b, plane_shift(away_b, 1))
-    *hid, kept, one, three, late = lax.optimization_barrier((*hid, kept, one, three, send[2]))
-    two = ring_shift(late, 2)
+    *hid, kept, two = lax.optimization_barrier((*hid, kept, two))
     moved = [plane_shift(hid[step], step) for step in (1, 2, 3)]
-    *moved, mine = lax.optimization_barrier((*moved, send[0]))
+    moved[0], mine = lax.optimization_barrier((moved[0], send[0]))
     big_sums = lax.psum_scatter(kept, "z", scatter_dimension=0, tiled=True)[0]
     grad_home = pl.pallas_call(
         norm_kernel,
@@ -886,16 +899,16 @@
         cost_estimate=pl.CostEstimate(flops=2_000_000_000, bytes_accessed=2_500_000, transcendentals=128),
         name="norm",
     )(info, hid[0], *moved, x_rows, grad_mid, gain_one)
-    sums = pl.pallas_call(
+    sums, outputs = pl.pallas_call(
         fold_kernel,
-        in_specs=[vmem] * 4,
-        out_specs=vmem,
-        out_shape=jax.ShapeDtypeStruct((8, 48, 480), bf16),
+        in_specs=[smem] + [vmem] * 4,
+        out_specs=[vmem] * 2,
+        out_shape=[jax.ShapeDtypeStruct((8, 48, 480), bf16), jax.ShapeDtypeStruct((4, 4, 8, width), bf16)],
         scratch_shapes=[pltpu.VMEM((8, 480), f32)],
         compiler_params=limit,
         cost_estimate=pl.CostEstimate(flops=2_000_000_000, bytes_accessed=1_600_000, transcendentals=0),
         name="fold",
-    )(mine, one, two, three)
+    )(info, mine, one, two, three)
     sums = lax.all_to_all(sums, ("y", "core", "x"), split_axis=0, concat_axis=0, tiled=True)
     rows_shape = [jax.ShapeDtypeStruct((40, width), f32)] * 3
     qkv_sums = pl.pallas_call(
@@ -911,7 +924,7 @@
     grad_home = by_source(grad_home, z, 0).reshape(16, 8, width)
 
     return (
-        outputs, grad_home, qkv_sums[0], qkv_sums[1], qkv_sums[2],
+        outputs.reshape(16, 8, width), grad_home, qkv_sums[0], qkv_sums[1], qkv_sums[2],
         big_sums[0], big_sums[1], big_sums[2], line_sums[0], line_sums[1], scale_sum,
     )
 

time: 258 us -> 253 us (0.981)
  blocking collectives: 14.8 us -> 0 us
  waiting for transfers between devices: 106 us -> 110 us
    all_to_all x1 -> x0, blocking collectives: 14.8 us -> none  [planes(): lax.all_to_all(out_rows, 'z', split_axis=0, concat_axis=0, tiled=True)]
    ppermute x9, waiting for transfers between devices: 33 us -> 40.3 us  [ring_shift(): return lax.ppermute(value, 'z', [(i, (i + step) % 4) for i in range(4)])]
    ppermute x8, waiting for transfers between devices: 23.2 us -> 20.2 us  [plane_shift(): return lax.ppermute(value, 'y', [(0, 1), (1, 0)])]
    unnamed x41 -> x50, local copies, waits for them, and re-layouts: 6.03 us -> 7.98 us
  transfers between devices with their start and end apart: 44 -> 44, of which waited for: 21 -> 22; matrix products, arithmetic and copies ran while one was open for 7% -> 7% of each run, Pallas kernels for 14% -> 15%
where the time goes in v9:
time: 253 us; the launch traced here: 252 us
  waiting for transfers between devices  110 us (43%)
  starting transfers between devices  48.6 us (19%)
  Pallas kernels  47.5 us (19%)
  local copies, waits for them, and re-layouts  17.9 us (7%)
  between operations  14.4 us (6%)
  other arithmetic  12.8 us (5%)
    ppermute x9, waiting for transfers between devices, ring_shift(): return lax.ppermute(value, 'z', [(i, (i + step) % 4) for i in range(4)])  40.3 us
    ppermute x8, waiting for transfers between devices, plane_shift(): return lax.ppermute(value, 'x', [(0, 1), (1, 0)])  33 us
    ppermute x8, waiting for transfers between devices, plane_shift(): return lax.ppermute(value, 'y', [(0, 1), (1, 0)])  20.2 us
    pallas_call x1, Pallas kernels, planes(): pl.pallas_call(attend_back_kernel, grid_spec=pltpu.PrefetchScalarGridSpec...  13.1 us
    ppermute x9, starting transfers between devices, ring_shift(): return lax.ppermute(value, 'z', [(i, (i + step) % 4) for i in range(4)])  13.1 us
    ppermute x4, waiting for transfers between devices, plane_shift(): return lax.ppermute(value, ('y', 'x'), [(0, 3), (1, 2), (2, 1), (3, 0)])  12.3 us
    pallas_call x1, Pallas kernels, planes(): pl.pallas_call(feed_kernel, in_specs=[smem] + [vmem] * 5 + [hbm] * 6, out...  9.64 us
    ppermute x8, starting transfers between devices, plane_shift(): return lax.ppermute(value, 'x', [(0, 1), (1, 0)])  9.28 us
  transfers between devices with their start and end apart: 44, of which 22 were waited for; matrix products, arithmetic and copies ran while one was open for 7% of the time, Pallas kernels for 15%

profile of v9, /device:TPU:0, one launch (start us, length us, event | category | flops | bytes accessed | tf_op | source)
XLA Modules:
  0.0 251.7 jit_solution(6979591644842378897)
XLA Ops:
  7.3 1.1 convert_bitcast_fusion.5
  8.4 1.1 convert_bitcast_fusion.3
  10.7 5.1 %collective-permute-start = (bf16[5,8,1280]{2,1,0:T(8,128)(2,1)S(1)}, bf16[5,8,1280]{2,1,0:T(8,128)(2,1)S(1)}, u32[]{:S(2)}, u32[]{:S(2)}) collective-permute-start(bf16[5,8,1280]{2,1,0:T(8,128)(2,1)S(1)} %get-tuple-element.101), channel_id=1, source_target_pairs={{0,24},{8,0},{16,8},{24,16},{1,25},{9,1},{17,9},{25,17},{2,26},{10... | collective-permute-start | bytes 307208 | tf_op jit(solution)/shard_map/ppermute | solution.py:357
  15.8 1.0 collective-permute-start.2
  17.9 1.1 reshape.336
  18.9 3.7 %all-to-all-start = ((bf16[8,40,480]{2,1,0:T(8,128)(2,1)}), bf16[8,40,480]{2,1,0:T(8,128)(2,1)S(1)}, u32[]{:S(2)}, u32[]{:S(2)}) async-start(bf16[8,40,480]{2,1,0:T(8,128)(2,1)} %reshape.336), calls=%async_computation | async-start | bytes 655360 | tf_op jit(solution)/shard_map/all_to_all | solution.py:738
  23.4 3.1 %collective-permute-done.1 = bf16[5,8,1280]{2,1,0:T(8,128)(2,1)S(1)} collective-permute-done((bf16[5,8,1280]{2,1,0:T(8,128)(2,1)S(1)}, bf16[5,8,1280]{2,1,0:T(8,128)(2,1)S(1)}, u32[]{:S(2)}, u32[]{:S(2)}) %collective-permute-start.1) | collective-permute-done | bytes 102432 | tf_op jit(solution)/shard_map/ppermute | solution.py:357
  27.0 2.8 %all-to-all-done = bf16[8,40,480]{2,1,0:T(8,128)(2,1)S(1)} async-done(((bf16[8,40,480]{2,1,0:T(8,128)(2,1)}), bf16[8,40,480]{2,1,0:T(8,128)(2,1)S(1)}, u32[]{:S(2)}, u32[]{:S(2)}) %all-to-all-start) | async-done | bytes 307232 | tf_op jit(solution)/shard_map/all_to_all | solution.py:738
  29.8 1.0 collective-permute-start.5
  30.8 1.5 collective-permute-start.4
  32.3 1.0 collective-permute-start.3
  33.3 8.4 %collective-permute-done.5 = bf16[136,1280]{1,0:T(8,128)(2,1)S(1)} collective-permute-done((bf16[136,1280]{1,0:T(8,128)(2,1)S(1)}, bf16[136,1280]{1,0:T(8,128)(2,1)S(1)}, u32[]{:S(2)}, u32[]{:S(2)}) %collective-permute-start.5) | collective-permute-done | bytes 348192 | tf_op jit(solution)/shard_map/ppermute | solution.py:349
  41.7 6.3 %collective-permute-done.4 = bf16[136,1280]{1,0:T(8,128)(2,1)S(1)} collective-permute-done((bf16[136,1280]{1,0:T(8,128)(2,1)S(1)}, bf16[136,1280]{1,0:T(8,128)(2,1)S(1)}, u32[]{:S(2)}, u32[]{:S(2)}) %collective-permute-start.4) | collective-permute-done | bytes 348192 | tf_op jit(solution)/shard_map/ppermute | solution.py:348
  48.3 1.0 collective-permute-start.7
  50.5 4.1 %all-to-all-start.1 = ((bf16[4,4,8,1280]{3,2,1,0:T(8,128)(2,1)}), bf16[4,4,8,1280]{3,2,1,0:T(8,128)(2,1)S(1)}, u32[]{:S(2)}, u32[]{:S(2)}) async-start(bf16[4,4,8,1280]{3,2,1,0:T(8,128)(2,1)} %bitcast.123), calls=%async_computation.1 | async-start | bytes 655360 | tf_op jit(solution)/shard_map/all_to_all | solution.py:746
  54.6 22.7 %collective-permute-done.7 = bf16[4,3,40,1280]{3,2,1,0:T(8,128)(2,1)S(1)} collective-permute-done((bf16[4,3,40,1280]{3,2,1,0:T(8,128)(2,1)}, bf16[4,3,40,1280]{3,2,1,0:T(8,128)(2,1)S(1)}, u32[]{:S(2)}, u32[]{:S(2)}) %collective-permute-start.7) | collective-permute-done | bytes 1228832 | tf_op jit(solution)/shard_map/ppermute | solution.py:346
  77.3 0.9 slice.174
  78.3 2.4 fusion.20
  80.7 1.1 collective-permute-start.10
  81.8 1.0 collective-permute-start.11
  82.8 2.9 %bitcast_select_fusion.near_rows = bf16[4,3,80,1280]{3,2,1,0:T(8,128)(2,1)} fusion(pred[80]{0:T(512)(128)(4,1)S(1)} %broadcast_in_dim.340, bf16[4,3,40,1280]{3,2,1,0:T(8,128)(2,1)S(1)} %collective-permute-done.7, bf16[4,3,40,1280]{3,2,1,0:T(8,128)(2,1)} %all-gather.3.cloned.1.call-done), kind=kLoop, calls=%fused_computation | loop fusion | flops 1228800 | bytes 4915280 | tf_op jit(solution)/shard_map/jit(_where)/select_n | solution.py:379
  87.0 1.3 copy-done.2
  88.4 8.2 %attend.1 = (f32[2,4,128,480]{3,2,1,0:T(8,128)}, bf16[4,2,128,160]{3,2,1,0:T(8,128)(2,1)S(1)}) custom-call(s32[6]{0:T(128)S(1)} %pad_add_fusion.info_ref, bf16[4,136,1280]{2,1,0:T(8,128)(2,1)S(1)} %pad_maximum_fusion.near_ref, bf16[4,136,1280]{2,1,0:T(8,128)(2,1)} %collective-permute-done.6.far_ref, f32[1,1280]{1,0:T(1,128)S(1)} %slice.141.gain_ref, ...), custom_call_target="tpu_custom_call" | custom-call | flops 8999999488 | bytes 8000000 | tf_op jit(solution)/shard_map/attend/pallas_call | solution.py:761
  96.7 3.0 %bitcast_select_fusion.1 = (bf16[2,3,80,1280]{3,2,1,0:T(8,128)(2,1)}, bf16[2,3,80,1280]{3,2,1,0:T(8,128)(2,1)}) fusion(pred[80]{0:T(512)(128)(4,1)S(1)} %broadcast_in_dim.340, bf16[2,3,40,1280]{3,2,1,0:T(8,128)(2,1)} %collective-permute-done.11, bf16[2,3,40,1280]{3,2,1,0:T(8,128)(2,1)S(1)} %copy-done.11, bf16[2,3,40,1280]{3,2,1,0:T(8,128)(2,1)} %collective-permute-done.10, ...), kind=kLoop, calls=%fused_computation.2 | loop fusion | flops 1228800 | bytes 4915280 | tf_op jit(solution)/shard_map/jit(_where)/select_n | solution.py:379
  100.2 1.9 collective-permute-start.14
  102.1 1.2 collective-permute-start.13
  103.3 3.8 %collective-permute-done.14 = bf16[2,128,160]{2,1,0:T(8,128)(2,1)S(1)} collective-permute-done((bf16[2,128,160]{2,1,0:T(8,128)(2,1)S(1)}, bf16[2,128,160]{2,1,0:T(8,128)(2,1)S(1)}, u32[]{:S(2)}, u32[]{:S(2)}) %collective-permute-start.14) | collective-permute-done | bytes 81952 | tf_op jit(solution)/shard_map/ppermute | solution.py:349
  107.1 1.6 collective-permute-start.12
  108.7 1.1 collective-permute-done.13
  109.9 2.3 collective-permute-done.12
  112.5 1.8 collective-permute-done.15.far_atts
  114.3 9.6 %feed.1 = (f32[4,4,8,1280]{3,2,1,0:T(8,128)S(1)}, bf16[4,128,1280]{2,1,0:T(8,128)(2,1)}, f32[128,1280]{1,0:T(8,128)S(1)}, bf16[2,128,160]{2,1,0:T(8,128)(2,1)S(1...) custom-call(s32[6]{0:T(128)S(1)} %pad_add_fusion.info_ref, ...), custom_call_target="tpu_custom_call" | custom-call | flops 12000000000 | bytes 13000000 | tf_op jit(solution)/shard_map/feed/pallas_call | solution.py:797
  123.9 0.8 copy-done.4
  125.8 1.6 collective-permute-start.20
  128.2 1.1 collective-permute-start.22
  129.3 7.2 %grads.1 = (bf16[2,3,2,80,1280]{4,3,2,1,0:T(8,128)(2,1)}, bf16[2,3,80,1280]{3,2,1,0:T(8,128)(2,1)S(1)}, bf16[2,3,80,1280]{3,2,1,0:T(8,128)(2,1)}) custom-call(s32[6]{0:T(128)S(1)} %pad_add_fusion.info_ref, bf16[4,128,1280]{2,1,0:T(8,128)(2,1)} %get-tuple-element.122.pack_ref, bf16[4,128,1280]{2,1,0:T(8,128)(2,1)} %collective-permute-done.19.far_pack, ...), custom_call_target="tpu_custom_call" | custom-call | flops 6000000000 | bytes 8000000 | tf_op jit(solution)/shard_map/grads/pallas_call | solution.py:817
  136.5 1.8 dynamic-slice_bitcast_fusion
  138.6 1.6 collective-permute-start.25
  141.0 13.1 %attend_back.1 = (bf16[4,128,1280]{2,1,0:T(8,128)(2,1)}, bf16[4,128,1280]{2,1,0:T(8,128)(2,1)}, bf16[432,480]{1,0:T(8,128)(2,1)S(1)}, bf16[432,480]{1,0:T(8,128)...) custom-call(s32[6]{0:T(128)S(1)} %pad_add_fusion.info_ref, bf16[4,136,1280]{2,1,0:T(8,128)(2,1)} %copy-done, ...), custom_call_target="tpu_custom_call" | custom-call | flops 15000000512 | bytes 12000000 | tf_op jit(solution)/shard_map/attend_back/pallas_call | solution.py:833
  154.9 2.3 collective-permute-start.27
  157.2 1.5 collective-permute-start.28
  158.7 11.0 %collective-permute-done.27.part_1 = bf16[432,480]{1,0:T(8,128)(2,1)S(1)} collective-permute-done((bf16[432,480]{1,0:T(8,128)(2,1)S(1)}, bf16[432,480]{1,0:T(8,128)(2,1)S(1)}, u32[]{:S(2)}, u32[]{:S(2)}) %collective-permute-start.27) | collective-permute-done | bytes 414752 | tf_op jit(solution)/shard_map/ppermute | solution.py:357
  169.8 9.1 %collective-permute-done.28.part_3 = bf16[432,480]{1,0:T(8,128)(2,1)S(1)} collective-permute-done((bf16[432,480]{1,0:T(8,128)(2,1)S(1)}, bf16[432,480]{1,0:T(8,128)(2,1)S(1)}, u32[]{:S(2)}, u32[]{:S(2)}) %collective-permute-start.28) | collective-permute-done | bytes 414752 | tf_op jit(solution)/shard_map/ppermute | solution.py:357
  178.9 1.1 copy-done.21
  179.9 3.1 %meet.1 = (bf16[2,3,40,1280]{3,2,1,0:T(8,128)(2,1)S(1)}, bf16[2,3,40,1280]{3,2,1,0:T(8,128)(2,1)S(1)}, bf16[2,3,40,1280]{3,2,1,0:T(8,128)(2,1)S(1)}, bf16[2,3,40,1280]{3,2,1,0:T(8,128)(2,1)S(1)}) custom-call(s32[6]{0:T(128)S(1)} %pad_add_fusion.info_ref, bf16[2,3,2,2,40,1280]{5,4,3,2,1,0:T(8,128)(2,1)} %bitcast.118, ...), custom_call_target="tpu_custom_call" | custom-call | flops 3000000000 | bytes 8000000 | tf_op jit(solution)/shard_map/meet/pallas_call | solution.py:870
  183.0 1.1 collective-permute-start.29
  185.5 1.1 fusion.3
  186.6 12.3 %collective-permute-done.29.from_a = bf16[2,3,40,1280]{3,2,1,0:T(8,128)(2,1)S(1)} collective-permute-done((bf16[2,3,40,1280]{3,2,1,0:T(8,128)(2,1)S(1)}, bf16[2,3,40,1280]{3,2,1,0:T(8,128)(2,1)S(1)}, u32[]{:S(2)}, u32[]{:S(2)}) %collective-permute-start.29) | collective-permute-done | bytes 614432 | tf_op jit(solution)/shard_map/ppermute | solution.py:348
  199.5 1.3 join.1
  200.8 6.0 %collective-permute-done.31.part_2 = bf16[432,480]{1,0:T(8,128)(2,1)S(1)} collective-permute-done((bf16[432,480]{1,0:T(8,128)(2,1)S(1)}, bf16[432,480]{1,0:T(8,128)(2,1)S(1)}, u32[]{:S(2)}, u32[]{:S(2)}) %collective-permute-start.31) | collective-permute-done | bytes 414752 | tf_op jit(solution)/shard_map/ppermute | solution.py:357
  207.6 1.4 collective-permute-start.33
  209.0 1.3 collective-permute-start.34
  210.3 7.3 %collective-permute-done.32.hid_1 = bf16[128,1280]{1,0:T(8,128)(2,1)S(1)} collective-permute-done((bf16[128,1280]{1,0:T(8,128)(2,1)}, bf16[128,1280]{1,0:T(8,128)(2,1)S(1)}, u32[]{:S(2)}, u32[]{:S(2)}) %collective-permute-start.32) | collective-permute-done | bytes 327712 | tf_op jit(solution)/shard_map/ppermute | solution.py:346
  217.6 1.0 copy-done.7
  218.6 1.7 fold.1
  220.4 3.5 %all-to-all-start.2 = ((bf16[8,48,480]{2,1,0:T(8,128)(2,1)}), bf16[8,48,480]{2,1,0:T(8,128)(2,1)S(1)}, u32[]{:S(2)}, u32[]{:S(2)}) async-start(bf16[8,48,480]{2,1,0:T(8,128)(2,1)} %get-tuple-element.171), calls=%async_computation.2 | async-start | bytes 786432 | tf_op jit(solution)/shard_map/all_to_all | solution.py:912
  224.2 1.1 copy-done.5
  225.3 1.5 norm.1
  226.7 1.9 collective-permute-start.35
  229.8 3.4 %collective-permute-done.35 = bf16[4,8,1280]{2,1,0:T(8,128)(2,1)S(1)} collective-permute-done((bf16[4,8,1280]{2,1,0:T(8,128)(2,1)S(1)}, bf16[4,8,1280]{2,1,0:T(8,128)(2,1)S(1)}, u32[]{:S(2)}, u32[]{:S(2)}) %collective-permute-start.35) | collective-permute-done | bytes 81952 | tf_op jit(solution)/shard_map/ppermute | solution.py:357
  233.2 7.7 %collective-permute-done.36 = bf16[4,8,1280]{2,1,0:T(8,128)(2,1)S(1)} collective-permute-done((bf16[4,8,1280]{2,1,0:T(8,128)(2,1)S(1)}, bf16[4,8,1280]{2,1,0:T(8,128)(2,1)S(1)}, u32[]{:S(2)}, u32[]{:S(2)}) %collective-permute-start.36) | collective-permute-done | bytes 81952 | tf_op jit(solution)/shard_map/ppermute | solution.py:357
  240.9 0.9 fusion.5
  241.8 0.9 spread.1
  243.3 1.0 copy-done.1
  (163 shorter events, 16.5 us)
Async XLA Ops:
  7.2 3.1 %copy-start.22 = (f32[40]{0:T(128)S(1)}, f32[40]{0:T(128)}, u32[]{:S(2)}) copy-start(f32[40]{0:T(128)} %param.23) | copy-start | bytes 484
  7.2 3.1 %copy-start.15 = (f32[40,1280]{1,0:T(8,128)S(1)}, f32[40,1280]{1,0:T(8,128)}, u32[]{:S(2)}) copy-start(f32[40,1280]{1,0:T(8,128)} %param.17) | copy-start | bytes 614404
  7.2 3.2 %copy-start.18 = (f32[40]{0:T(128)S(1)}, f32[40]{0:T(128)}, u32[]{:S(2)}) copy-start(f32[40]{0:T(128)} %param.25) | copy-start | bytes 484
  7.2 3.2 %copy-start.19 = (f32[40]{0:T(128)S(1)}, f32[40]{0:T(128)}, u32[]{:S(2)}) copy-start(f32[40]{0:T(128)} %param.24) | copy-start | bytes 484
  7.2 3.2 %copy-start.16 = (f32[40,1280]{1,0:T(8,128)S(1)}, f32[40,1280]{1,0:T(8,128)}, u32[]{:S(2)}) copy-start(f32[40,1280]{1,0:T(8,128)} %param.19) | copy-start | bytes 614404
  7.2 3.2 %copy-start.17 = (f32[40,1280]{1,0:T(8,128)S(1)}, f32[40,1280]{1,0:T(8,128)}, u32[]{:S(2)}) copy-start(f32[40,1280]{1,0:T(8,128)} %param.18) | copy-start | bytes 614404
  7.2 41.1 %all-gather.3.cloned.1.call-start = ((), (), s32[]{:S(2)}) async-start(), calls=%async_computation.4 | async-start | bytes 1536000 | tf_op jit(solution)/shard_map/all_gather | solution.py:735
  9.5 1.1 copy-start.14
  10.7 12.7 %collective-permute-start = (bf16[5,8,1280]{2,1,0:T(8,128)(2,1)S(1)}, bf16[5,8,1280]{2,1,0:T(8,128)(2,1)S(1)}, u32[]{:S(2)}, u32[]{:S(2)}) collective-permute-start(bf16[5,8,1280]{2,1,0:T(8,128)(2,1)S(1)} %get-tuple-element.101), channel_id=1, source_target_pairs={{0,24},{8,0},{16,8},{24,16},{1,25},{9,1},{17,9},{25,17},{2,26},{10... | collective-permute-start | bytes 307208 | tf_op jit(solution)/shard_map/ppermute | solution.py:357
  15.8 10.7 %collective-permute-start.1 = (bf16[5,8,1280]{2,1,0:T(8,128)(2,1)S(1)}, bf16[5,8,1280]{2,1,0:T(8,128)(2,1)S(1)}, u32[]{:S(2)}, u32[]{:S(2)}) collective-permute-start(bf16[5,8,1280]{2,1,0:T(8,128)(2,1)S(1)} %get-tuple-element.102), channel_id=1, source_target_pairs={{0,16},{8,24},{16,0},{24,8},{1,17},{9,25},{17,1},{25,9},{2,18},{10... | collective-permute-start | bytes 307208 | tf_op jit(solution)/shard_map/ppermute | solution.py:357
  15.8 10.7 %collective-permute-start.2 = (bf16[5,8,1280]{2,1,0:T(8,128)(2,1)S(1)}, bf16[5,8,1280]{2,1,0:T(8,128)(2,1)S(1)}, u32[]{:S(2)}, u32[]{:S(2)}) collective-permute-start(bf16[5,8,1280]{2,1,0:T(8,128)(2,1)S(1)} %get-tuple-element.103), channel_id=1, source_target_pairs={{0,8},{8,16},{16,24},{24,0},{1,9},{9,17},{17,25},{25,1},{2,10},{10... | collective-permute-start | bytes 307208 | tf_op jit(solution)/shard_map/ppermute | solution.py:357
  18.9 10.9 %all-to-all-start = ((bf16[8,40,480]{2,1,0:T(8,128)(2,1)}), bf16[8,40,480]{2,1,0:T(8,128)(2,1)S(1)}, u32[]{:S(2)}, u32[]{:S(2)}) async-start(bf16[8,40,480]{2,1,0:T(8,128)(2,1)} %reshape.336), calls=%async_computation | async-start | bytes 655360 | tf_op jit(solution)/shard_map/all_to_all | solution.py:738
  22.6 64.4 %all-gather.5.cloned.1.call-start = ((), (), s32[]{:S(2)}) async-start(), calls=%async_computation.5 | async-start | bytes 1638400 | tf_op jit(solution)/shard_map/all_gather | solution.py:740
  29.8 18.5 %copy-start.12 = (bf16[8,40,480]{2,1,0:T(8,128)(2,1)}, bf16[8,40,480]{2,1,0:T(8,128)(2,1)S(1)}, u32[]{:S(2)}) copy-start(bf16[8,40,480]{2,1,0:T(8,128)(2,1)S(1)} %all-to-all-done) | copy-start | bytes 921604
  29.8 11.9 %collective-permute-start.5 = (bf16[136,1280]{1,0:T(8,128)(2,1)S(1)}, bf16[136,1280]{1,0:T(8,128)(2,1)S(1)}, u32[]{:S(2)}, u32[]{:S(2)}) collective-permute-start(bf16[136,1280]{1,0:T(8,128)(2,1)S(1)} %maximum_maximum_fusion), channel_id=1, source_target_pairs={{0,5},{1,4},{4,1},{5,0},{2,7},{3,6},{6,3},{7,2},{8,13},{9,12},{12,... | collective-permute-start | bytes 1044488 | tf_op jit(solution)/shard_map/ppermute | solution.py:349
  30.8 17.2 %collective-permute-start.4 = (bf16[136,1280]{1,0:T(8,128)(2,1)S(1)}, bf16[136,1280]{1,0:T(8,128)(2,1)S(1)}, u32[]{:S(2)}, u32[]{:S(2)}) collective-permute-start(bf16[136,1280]{1,0:T(8,128)(2,1)S(1)} %maximum_maximum_fusion), channel_id=1, source_target_pairs={{0,4},{4,0},{1,5},{5,1},{2,6},{6,2},{3,7},{7,3},{8,12},{12,8},{9,1... | collective-permute-start | bytes 1044488 | tf_op jit(solution)/shard_map/ppermute | solution.py:348
  32.3 15.8 %collective-permute-start.3 = (bf16[136,1280]{1,0:T(8,128)(2,1)S(1)}, bf16[136,1280]{1,0:T(8,128)(2,1)S(1)}, u32[]{:S(2)}, u32[]{:S(2)}) collective-permute-start(bf16[136,1280]{1,0:T(8,128)(2,1)S(1)} %maximum_maximum_fusion), channel_id=1, source_target_pairs={{0,1},{1,0},{2,3},{3,2},{4,5},{5,4},{6,7},{7,6},{8,9},{9,8},{10,11... | collective-permute-start | bytes 1044488 | tf_op jit(solution)/shard_map/ppermute | solution.py:346
  48.1 2.2 copy-start.23
  48.1 2.2 copy-start.24
  48.3 38.8 %copy-start = (bf16[4,136,1280]{2,1,0:T(8,128)(2,1)}, bf16[4,136,1280]{2,1,0:T(8,128)(2,1)S(1)}, u32[]{:S(2)}) copy-start(bf16[4,136,1280]{2,1,0:T(8,128)(2,1)S(1)} %pad_maximum_fusion.near_ref) | copy-start | bytes 4177924
  48.3 29.0 %collective-permute-start.7 = (bf16[4,3,40,1280]{3,2,1,0:T(8,128)(2,1)}, bf16[4,3,40,1280]{3,2,1,0:T(8,128)(2,1)S(1)}, u32[]{:S(2)}, u32[]{:S(2)}) collective-permute-start(bf16[4,3,40,1280]{3,2,1,0:T(8,128)(2,1)} %all-gather.3.cloned.1.call-done), channel_id=1, source_target_pairs={{0,1},{1,0},{2,3},{3,2},{4,5},{5,4},{6,7},{7,6},{8,9},{9,8},{10,11... | collective-permute-start | bytes 3686408 | tf_op jit(solution)/shard_map/ppermute | solution.py:346
  49.3 29.0 %collective-permute-start.8 = (bf16[4,3,40,1280]{3,2,1,0:T(8,128)(2,1)}, bf16[4,3,40,1280]{3,2,1,0:T(8,128)(2,1)}, u32[]{:S(2)}, u32[]{:S(2)}) collective-permute-start(bf16[4,3,40,1280]{3,2,1,0:T(8,128)(2,1)} %all-gather.3.cloned.1.call-done), channel_id=1, source_target_pairs={{0,4},{4,0},{1,5},{5,1},{2,6},{6,2},{3,7},{7,3},{8,12},{12,8},{9,1... | collective-permute-start | bytes 3686408 | tf_op jit(solution)/shard_map/ppermute | solution.py:348
  50.0 35.7 %collective-permute-start.6 = (bf16[4,136,1280]{2,1,0:T(8,128)(2,1)S(1)}, bf16[4,136,1280]{2,1,0:T(8,128)(2,1)}, u32[]{:S(2)}, u32[]{:S(2)}) collective-permute-start(bf16[4,136,1280]{2,1,0:T(8,128)(2,1)S(1)} %pad_maximum_fusion.near_ref), channel_id=1, source_target_pairs={{0,2},{2,0},{1,3},{3,1},{4,6},{6,4},{5,7},{7,5},{8,10},{10,8},{9,1... | collective-permute-start | bytes 4177928 | tf_op jit(solution)/shard_map/ppermute | solution.py:353
  50.5 30.2 %all-to-all-start.1 = ((bf16[4,4,8,1280]{3,2,1,0:T(8,128)(2,1)}), bf16[4,4,8,1280]{3,2,1,0:T(8,128)(2,1)S(1)}, u32[]{:S(2)}, u32[]{:S(2)}) async-start(bf16[4,4,8,1280]{3,2,1,0:T(8,128)(2,1)} %bitcast.123), calls=%async_computation.1 | async-start | bytes 655360 | tf_op jit(solution)/shard_map/all_to_all | solution.py:746
  54.6 188.7 %reduce-scatter.2.cloned.1.call-start = ((), (), s32[]{:S(2)}) async-start(), calls=%async_computation.6 | async-start | bytes 1536000 | tf_op jit(solution)/shard_map/reduce_scatter | solution.py:891
  80.7 15.9 %collective-permute-start.10 = (bf16[2,3,40,1280]{3,2,1,0:T(8,128)(2,1)}, bf16[2,3,40,1280]{3,2,1,0:T(8,128)(2,1)}, u32[]{:S(2)}, u32[]{:S(2)}) collective-permute-start(bf16[2,3,40,1280]{3,2,1,0:T(8,128)(2,1)} %slice.174), channel_id=1, source_target_pairs={{0,4},{4,0},{1,5},{5,1},{2,6},{6,2},{3,7},{7,3},{8,12},{12,8},{9,1... | collective-permute-start | bytes 1843208 | tf_op jit(solution)/shard_map/ppermute | solution.py:348
  81.8 14.9 %collective-permute-start.11 = (bf16[2,3,40,1280]{3,2,1,0:T(8,128)(2,1)}, bf16[2,3,40,1280]{3,2,1,0:T(8,128)(2,1)}, u32[]{:S(2)}, u32[]{:S(2)}) collective-permute-start(bf16[2,3,40,1280]{3,2,1,0:T(8,128)(2,1)} %get-tuple-element.115), channel_id=1, source_target_pairs={{0,1},{1,0},{2,3},{3,2},{4,5},{5,4},{6,7},{7,6},{8,9},{9,8},{10,11... | collective-permute-start | bytes 1843208 | tf_op jit(solution)/shard_map/ppermute | solution.py:346
  87.0 1.3 copy-start.2
  88.3 8.4 %copy-start.10 = (bf16[2,3,40,1280]{3,2,1,0:T(8,128)(2,1)S(1)}, bf16[2,3,40,1280]{3,2,1,0:T(8,128)(2,1)}, u32[]{:S(2)}) copy-start(bf16[2,3,40,1280]{3,2,1,0:T(8,128)(2,1)} %get-tuple-element.183) | copy-start | bytes 1843204
  88.4 8.4 %copy-start.11 = (bf16[2,3,40,1280]{3,2,1,0:T(8,128)(2,1)S(1)}, bf16[2,3,40,1280]{3,2,1,0:T(8,128)(2,1)}, u32[]{:S(2)}) copy-start(bf16[2,3,40,1280]{3,2,1,0:T(8,128)(2,1)} %get-tuple-element.115) | copy-start | bytes 1843204
  96.7 17.6 %collective-permute-start.16 = (bf16[4,3,80,1280]{3,2,1,0:T(8,128)(2,1)}, bf16[4,3,80,1280]{3,2,1,0:T(8,128)(2,1)}, u32[]{:S(2)}, u32[]{:S(2)}) collective-permute-start(bf16[4,3,80,1280]{3,2,1,0:T(8,128)(2,1)} %bitcast_select_fusion.near_rows), channel_id=1, source_target_pairs={{0,2},{2,0},{1,3},{3,1},{4,6},{6,4},{5,7},{7,5},{8,10},{10,8},{9,1... | collective-permute-start | bytes 7372808 | tf_op jit(solution)/shard_map/ppermute | solution.py:353
  99.7 14.6 %collective-permute-start.18 = (bf16[2,3,80,1280]{3,2,1,0:T(8,128)(2,1)}, bf16[2,3,80,1280]{3,2,1,0:T(8,128)(2,1)}, u32[]{:S(2)}, u32[]{:S(2)}) collective-permute-start(bf16[2,3,80,1280]{3,2,1,0:T(8,128)(2,1)} %get-tuple-element.203.across_b), channel_id=1, source_target_pairs={{0,2},{2,0},{1,3},{3,1},{4,6},{6,4},{5,7},{7,5},{8,10},{10,8},{9,1... | collective-permute-start | bytes 3686408 | tf_op jit(solution)/shard_map/ppermute | solution.py:353
  100.1 14.1 %collective-permute-start.17 = (bf16[2,3,80,1280]{3,2,1,0:T(8,128)(2,1)}, bf16[2,3,80,1280]{3,2,1,0:T(8,128)(2,1)}, u32[]{:S(2)}, u32[]{:S(2)}) collective-permute-start(bf16[2,3,80,1280]{3,2,1,0:T(8,128)(2,1)} %get-tuple-element.204.across_a), channel_id=1, source_target_pairs={{0,2},{2,0},{1,3},{3,1},{4,6},{6,4},{5,7},{7,5},{8,10},{10,8},{9,1... | collective-permute-start | bytes 3686408 | tf_op jit(solution)/shard_map/ppermute | solution.py:353
  100.2 6.9 %collective-permute-start.14 = (bf16[2,128,160]{2,1,0:T(8,128)(2,1)S(1)}, bf16[2,128,160]{2,1,0:T(8,128)(2,1)S(1)}, u32[]{:S(2)}, u32[]{:S(2)}) collective-permute-start(bf16[2,128,160]{2,1,0:T(8,128)(2,1)S(1)} %get-tuple-element.186), channel_id=1, source_target_pairs={{0,5},{1,4},{4,1},{5,0},{2,7},{3,6},{6,3},{7,2},{8,13},{9,12},{12,... | collective-permute-start | bytes 245768 | tf_op jit(solution)/shard_map/ppermute | solution.py:349
  102.1 7.8 %collective-permute-start.13 = (bf16[2,128,160]{2,1,0:T(8,128)(2,1)S(1)}, bf16[2,128,160]{2,1,0:T(8,128)(2,1)S(1)}, u32[]{:S(2)}, u32[]{:S(2)}) collective-permute-start(bf16[2,128,160]{2,1,0:T(8,128)(2,1)S(1)} %get-tuple-element.187), channel_id=1, source_target_pairs={{0,4},{4,0},{1,5},{5,1},{2,6},{6,2},{3,7},{7,3},{8,12},{12,8},{9,1... | collective-permute-start | bytes 245768 | tf_op jit(solution)/shard_map/ppermute | solution.py:348
  107.1 5.0 %collective-permute-start.12 = (bf16[2,128,160]{2,1,0:T(8,128)(2,1)S(1)}, bf16[2,128,160]{2,1,0:T(8,128)(2,1)S(1)}, u32[]{:S(2)}, u32[]{:S(2)}) collective-permute-start(bf16[2,128,160]{2,1,0:T(8,128)(2,1)S(1)} %get-tuple-element.188), channel_id=1, source_target_pairs={{0,1},{1,0},{2,3},{3,2},{4,5},{5,4},{6,7},{7,6},{8,9},{9,8},{10,11... | collective-permute-start | bytes 245768 | tf_op jit(solution)/shard_map/ppermute | solution.py:346
  109.8 2.6 %collective-permute-start.9 = (bf16[128,1280]{1,0:T(8,128)(2,1)S(1)}, bf16[128,1280]{1,0:T(8,128)(2,1)S(1)}, u32[]{:S(2)}, u32[]{:S(2)}) collective-permute-start(bf16[128,1280]{1,0:T(8,128)(2,1)S(1)} %bitcast.107), channel_id=1, source_target_pairs={{0,2},{2,0},{1,3},{3,1},{4,6},{6,4},{5,7},{7,5},{8,10},{10,8},{9,1... | collective-permute-start | bytes 983048 | tf_op jit(solution)/shard_map/ppermute | solution.py:353
  112.3 2.0 collective-permute-start.15
  125.6 3.6 %collective-permute-start.19 = (bf16[4,128,1280]{2,1,0:T(8,128)(2,1)}, bf16[4,128,1280]{2,1,0:T(8,128)(2,1)}, u32[]{:S(2)}, u32[]{:S(2)}) collective-permute-start(bf16[4,128,1280]{2,1,0:T(8,128)(2,1)} %get-tuple-element.122.pack_ref), channel_id=1, source_target_pairs={{0,2},{2,0},{1,3},{3,1},{4,6},{6,4},{5,7},{7,5},{8,10},{10,8},{9,1... | collective-permute-start | bytes 3932168 | tf_op jit(solution)/shard_map/ppermute | solution.py:353
  125.8 10.7 %collective-permute-start.20 = (bf16[2,128,160]{2,1,0:T(8,128)(2,1)S(1)}, bf16[2,128,160]{2,1,0:T(8,128)(2,1)S(1)}, u32[]{:S(2)}, u32[]{:S(2)}) collective-permute-start(bf16[2,128,160]{2,1,0:T(8,128)(2,1)S(1)} %get-tuple-element.128), channel_id=1, source_target_pairs={{0,1},{1,0},{2,3},{3,2},{4,5},{5,4},{6,7},{7,6},{8,9},{9,8},{10,11... | collective-permute-start | bytes 245768 | tf_op jit(solution)/shard_map/ppermute | solution.py:346
  127.4 9.1 %collective-permute-start.21 = (bf16[2,128,160]{2,1,0:T(8,128)(2,1)S(1)}, bf16[2,128,160]{2,1,0:T(8,128)(2,1)S(1)}, u32[]{:S(2)}, u32[]{:S(2)}) collective-permute-start(bf16[2,128,160]{2,1,0:T(8,128)(2,1)S(1)} %get-tuple-element.129), channel_id=1, source_target_pairs={{0,4},{4,0},{1,5},{5,1},{2,6},{6,2},{3,7},{7,3},{8,12},{12,8},{9,1... | collective-permute-start | bytes 245768 | tf_op jit(solution)/shard_map/ppermute | solution.py:348
  128.2 8.3 %collective-permute-start.22 = (bf16[2,128,160]{2,1,0:T(8,128)(2,1)S(1)}, bf16[2,128,160]{2,1,0:T(8,128)(2,1)S(1)}, u32[]{:S(2)}, u32[]{:S(2)}) collective-permute-start(bf16[2,128,160]{2,1,0:T(8,128)(2,1)S(1)} %get-tuple-element.130), channel_id=1, source_target_pairs={{0,5},{1,4},{4,1},{5,0},{2,7},{3,6},{6,3},{7,2},{8,13},{9,12},{12,... | collective-permute-start | bytes 245768 | tf_op jit(solution)/shard_map/ppermute | solution.py:349
  136.4 1.9 copy-start.3
  136.5 3.7 %copy-start.20 = (bf16[2,3,80,1280]{3,2,1,0:T(8,128)(2,1)S(1)}, bf16[2,3,80,1280]{3,2,1,0:T(8,128)(2,1)}, u32[]{:S(2)}) copy-start(bf16[2,3,80,1280]{3,2,1,0:T(8,128)(2,1)} %get-tuple-element.143) | copy-start | bytes 3686404
  136.5 4.5 %copy-start.9 = (f32[4,4,8,1280]{3,2,1,0:T(8,128)S(1)}, f32[4,4,8,1280]{3,2,1,0:T(8,128)}, u32[]{:S(2)}) copy-start(f32[4,4,8,1280]{3,2,1,0:T(8,128)} %copy-done.8) | copy-start | bytes 1966084
  138.5 2.5 %collective-permute-start.23 = (bf16[4,2,128,160]{3,2,1,0:T(8,128)(2,1)S(1)}, bf16[4,2,128,160]{3,2,1,0:T(8,128)(2,1)S(1)}, u32[]{:S(2)}, u32[]{:S(2)}) collective-permute-start(bf16[4,2,128,160]{3,2,1,0:T(8,128)(2,1)S(1)} %pad_maximum_fusion.2.grad_near), channel_id=1, source_target_pairs={{0,2},{2,0},{1,3},{3,1},{4,6},{6,4},{5,7},{7,5},{8,10},{10,8},{9,1... | collective-permute-start | bytes 983048 | tf_op jit(solution)/shard_map/ppermute | solution.py:353
  138.6 40.3 %collective-permute-start.25 = (bf16[2,3,2,40,1280]{4,3,2,1,0:T(8,128)(2,1)S(1)}, bf16[2,3,2,40,1280]{4,3,2,1,0:T(8,128)(2,1)S(1)}, u32[]{:S(2)}, u32[]{:S(2)}) collective-permute-start(bf16[2,3,2,40,1280]{4,3,2,1,0:T(8,128)(2,1)S(1)} %dynamic-slice_bitcast_fusion), channel_id=1, source_target_pairs={{0,1},{1,0},{2,3},{3,2},{4,5},{5,4},{6,7},{7,6},{8,9},{9,8},{10,11... | collective-permute-start | bytes 3686408 | tf_op jit(solution)/shard_map/ppermute | solution.py:346
  140.2 38.7 %collective-permute-start.26 = (bf16[2,3,80,1280]{3,2,1,0:T(8,128)(2,1)S(1)}, bf16[2,3,80,1280]{3,2,1,0:T(8,128)(2,1)S(1)}, u32[]{:S(2)}, u32[]{:S(2)}) collective-permute-start(bf16[2,3,80,1280]{3,2,1,0:T(8,128)(2,1)S(1)} %copy-done.20), channel_id=1, source_target_pairs={{0,4},{4,0},{1,5},{5,1},{2,6},{6,2},{3,7},{7,3},{8,12},{12,8},{9,1... | collective-permute-start | bytes 3686408 | tf_op jit(solution)/shard_map/ppermute | solution.py:348
  154.9 30.6 %collective-permute-start.24 = (bf16[4,128,1280]{2,1,0:T(8,128)(2,1)}, bf16[4,128,1280]{2,1,0:T(8,128)(2,1)S(1)}, u32[]{:S(2)}, u32[]{:S(2)}) collective-permute-start(bf16[4,128,1280]{2,1,0:T(8,128)(2,1)} %get-tuple-element.141), channel_id=1, source_target_pairs={{0,2},{2,0},{1,3},{3,1},{4,6},{6,4},{5,7},{7,5},{8,10},{10,8},{9,1... | collective-permute-start | bytes 3932168 | tf_op jit(solution)/shard_map/ppermute | solution.py:353
  154.9 14.9 %collective-permute-start.27 = (bf16[432,480]{1,0:T(8,128)(2,1)S(1)}, bf16[432,480]{1,0:T(8,128)(2,1)S(1)}, u32[]{:S(2)}, u32[]{:S(2)}) collective-permute-start(bf16[432,480]{1,0:T(8,128)(2,1)S(1)} %get-tuple-element.144), channel_id=1, source_target_pairs={{0,8},{8,16},{16,24},{24,0},{1,9},{9,17},{17,25},{25,1},{2,10},{10... | collective-permute-start | bytes 1244168 | tf_op jit(solution)/shard_map/ppermute | solution.py:357
  157.2 21.6 %collective-permute-start.28 = (bf16[432,480]{1,0:T(8,128)(2,1)S(1)}, bf16[432,480]{1,0:T(8,128)(2,1)S(1)}, u32[]{:S(2)}, u32[]{:S(2)}) collective-permute-start(bf16[432,480]{1,0:T(8,128)(2,1)S(1)} %get-tuple-element.145), channel_id=1, source_target_pairs={{0,24},{8,0},{16,8},{24,16},{1,25},{9,1},{17,9},{25,17},{2,26},{10... | collective-permute-start | bytes 1244168 | tf_op jit(solution)/shard_map/ppermute | solution.py:357
  178.9 1.1 copy-start.21
  179.9 5.5 %copy-start.13 = (bf16[4,128,1280]{2,1,0:T(8,128)(2,1)S(1)}, bf16[4,128,1280]{2,1,0:T(8,128)(2,1)}, u32[]{:S(2)}) copy-start(bf16[4,128,1280]{2,1,0:T(8,128)(2,1)} %get-tuple-element.140) | copy-start | bytes 3932164
  183.0 15.9 %collective-permute-start.29 = (bf16[2,3,40,1280]{3,2,1,0:T(8,128)(2,1)S(1)}, bf16[2,3,40,1280]{3,2,1,0:T(8,128)(2,1)S(1)}, u32[]{:S(2)}, u32[]{:S(2)}) collective-permute-start(bf16[2,3,40,1280]{3,2,1,0:T(8,128)(2,1)S(1)} %get-tuple-element.151), channel_id=1, source_target_pairs={{0,4},{4,0},{1,5},{5,1},{2,6},{6,2},{3,7},{7,3},{8,12},{12,8},{9,1... | collective-permute-start | bytes 1843208 | tf_op jit(solution)/shard_map/ppermute | solution.py:348
  184.1 15.3 %collective-permute-start.30 = (bf16[2,3,40,1280]{3,2,1,0:T(8,128)(2,1)S(1)}, bf16[2,3,40,1280]{3,2,1,0:T(8,128)(2,1)S(1)}, u32[]{:S(2)}, u32[]{:S(2)}) collective-permute-start(bf16[2,3,40,1280]{3,2,1,0:T(8,128)(2,1)S(1)} %get-tuple-element.153), channel_id=1, source_target_pairs={{0,1},{1,0},{2,3},{3,2},{4,5},{5,4},{6,7},{7,6},{8,9},{9,8},{10,11... | collective-permute-start | bytes 1843208 | tf_op jit(solution)/shard_map/ppermute | solution.py:346
  184.9 21.9 %collective-permute-start.31 = (bf16[432,480]{1,0:T(8,128)(2,1)S(1)}, bf16[432,480]{1,0:T(8,128)(2,1)S(1)}, u32[]{:S(2)}, u32[]{:S(2)}) collective-permute-start(bf16[432,480]{1,0:T(8,128)(2,1)S(1)} %get-tuple-element.154), channel_id=1, source_target_pairs={{0,16},{8,24},{16,0},{24,8},{1,17},{9,25},{17,1},{25,9},{2,18},{10... | collective-permute-start | bytes 1244168 | tf_op jit(solution)/shard_map/ppermute | solution.py:357
  206.8 10.9 %collective-permute-start.32 = (bf16[128,1280]{1,0:T(8,128)(2,1)}, bf16[128,1280]{1,0:T(8,128)(2,1)S(1)}, u32[]{:S(2)}, u32[]{:S(2)}) collective-permute-start(bf16[128,1280]{1,0:T(8,128)(2,1)} %get-tuple-element.155), channel_id=1, source_target_pairs={{0,1},{1,0},{2,3},{3,2},{4,5},{5,4},{6,7},{7,6},{8,9},{9,8},{10,11... | collective-permute-start | bytes 983048 | tf_op jit(solution)/shard_map/ppermute | solution.py:346
  207.6 16.6 %collective-permute-start.33 = (bf16[128,1280]{1,0:T(8,128)(2,1)}, bf16[128,1280]{1,0:T(8,128)(2,1)S(1)}, u32[]{:S(2)}, u32[]{:S(2)}) collective-permute-start(bf16[128,1280]{1,0:T(8,128)(2,1)} %get-tuple-element.164), channel_id=1, source_target_pairs={{0,4},{4,0},{1,5},{5,1},{2,6},{6,2},{3,7},{7,3},{8,12},{12,8},{9,1... | collective-permute-start | bytes 983048 | tf_op jit(solution)/shard_map/ppermute | solution.py:348
  209.0 15.2 %collective-permute-start.34 = (bf16[128,1280]{1,0:T(8,128)(2,1)S(1)}, bf16[128,1280]{1,0:T(8,128)(2,1)}, u32[]{:S(2)}, u32[]{:S(2)}) collective-permute-start(bf16[128,1280]{1,0:T(8,128)(2,1)S(1)} %get-tuple-element.165), channel_id=1, source_target_pairs={{0,5},{1,4},{4,1},{5,0},{2,7},{3,6},{6,3},{7,2},{8,13},{9,12},{12,... | collective-permute-start | bytes 983048 | tf_op jit(solution)/shard_map/ppermute | solution.py:349
  220.4 21.4 %all-to-all-start.2 = ((bf16[8,48,480]{2,1,0:T(8,128)(2,1)}), bf16[8,48,480]{2,1,0:T(8,128)(2,1)S(1)}, u32[]{:S(2)}, u32[]{:S(2)}) async-start(bf16[8,48,480]{2,1,0:T(8,128)(2,1)} %get-tuple-element.171), calls=%async_computation.2 | async-start | bytes 786432 | tf_op jit(solution)/shard_map/all_to_all | solution.py:912
  224.2 1.1 copy-start.5
  226.7 6.4 %collective-permute-start.35 = (bf16[4,8,1280]{2,1,0:T(8,128)(2,1)S(1)}, bf16[4,8,1280]{2,1,0:T(8,128)(2,1)S(1)}, u32[]{:S(2)}, u32[]{:S(2)}) collective-permute-start(bf16[4,8,1280]{2,1,0:T(8,128)(2,1)S(1)} %get-tuple-element.167), channel_id=1, source_target_pairs={{0,24},{8,0},{16,8},{24,16},{1,25},{9,1},{17,9},{25,17},{2,26},{10... | collective-permute-start | bytes 245768 | tf_op jit(solution)/shard_map/ppermute | solution.py:357
  228.7 12.2 %collective-permute-start.36 = (bf16[4,8,1280]{2,1,0:T(8,128)(2,1)S(1)}, bf16[4,8,1280]{2,1,0:T(8,128)(2,1)S(1)}, u32[]{:S(2)}, u32[]{:S(2)}) collective-permute-start(bf16[4,8,1280]{2,1,0:T(8,128)(2,1)S(1)} %get-tuple-element.168), channel_id=1, source_target_pairs={{0,16},{8,24},{16,0},{24,8},{1,17},{9,25},{17,1},{25,9},{2,18},{10... | collective-permute-start | bytes 245768 | tf_op jit(solution)/shard_map/ppermute | solution.py:357
  228.7 12.2 %collective-permute-start.37 = (bf16[4,8,1280]{2,1,0:T(8,128)(2,1)S(1)}, bf16[4,8,1280]{2,1,0:T(8,128)(2,1)S(1)}, u32[]{:S(2)}, u32[]{:S(2)}) collective-permute-start(bf16[4,8,1280]{2,1,0:T(8,128)(2,1)S(1)} %get-tuple-element.169), channel_id=1, source_target_pairs={{0,8},{8,16},{16,24},{24,0},{1,9},{9,17},{17,25},{25,1},{2,10},{10... | collective-permute-start | bytes 245768 | tf_op jit(solution)/shard_map/ppermute | solution.py:357
  (5 other events, 4.4 us)
Sparse Core Ops, SparseCore 0:
  10.4 34.5 all-gather.2
  50.4 36.6 all-gather.4
  206.9 32.9 reduce-scatter.1

commit v10 on v9

--- a/solution.py
+++ b/solution.py
@@ -430,8 +430,8 @@
 
 
 def attend_back_kernel(
-    info_ref, near_ref, far_ref, gain_ref, mult_ref, w_ref, pre_ref, grad_near, grad_far, gain_two_ref, result_ref,
-    hid_near, hid_far, send_0, send_1, send_2, send_3, w_acc, gain_acc, scale_acc, lines,
+    info_ref, near_ref, far_ref, gain_ref, mult_ref, w_ref, pre_ref, grad_near, grad_far, gain_two_ref,
+    hid_near, hid_far, send_ref, w_acc, gain_acc, scale_acc, lines,
 ):
     seq = pl.program_id(0)
 
@@ -483,16 +483,10 @@
             lane = 120 * part + 80
             lines[info_ref[1], :, lane : lane + 40] = scale_acc[:, 40 * part : 40 * part + 40]
         blank = jnp.zeros((14, 480), jnp.float32)
-        for hop, send in enumerate((send_0, send_1, send_2, send_3)):
-            target = (info_ref[0] + hop) & 3
-            rows = w_acc[pl.ds(pl.multiple_of(target * 320, 320), 320), :]
+        for target in range(4):
+            rows = w_acc[320 * target : 320 * target + 320, :]
             block = jnp.concatenate([rows, lines[2 * target], lines[2 * target + 1], blank], axis=0)
-            send[0:336, :] = block.astype(jnp.bfloat16)
-            result = result_ref[target].reshape(32, 1280).astype(jnp.bfloat16)
-            send[336:368, :] = result[:, 0:480]
-            send[368:400, :] = result[:, 480:960]
-            send[400:432, 0:320] = result[:, 960:1280]
-            send[400:432, 320:480] = jnp.zeros((32, 160), jnp.bfloat16)
+            send_ref[target] = block.astype(jnp.bfloat16)
 
 
 def block_index(z_index, y_index, core):
@@ -559,7 +553,7 @@
     for seq in range(4):
         for plane_z in range(4):
             row = 32 * seq + 8 * plane_z
-            out_ref[plane_z, seq] = result[row : row + 8]
+            out_ref[plane_z, seq] = result[row : row + 8].astype(jnp.bfloat16)
     cot = g_ref[...]
     grad_act = mult_trans(cot, weights[2])
     grad_up = (grad_act * sigma * (1.0 + up * (1.0 - sigma))).astype(jnp.bfloat16)
@@ -668,21 +662,14 @@
         out[...] = rows[(info_ref[0] + hop) & 3].astype(jnp.bfloat16)
 
 
-def fold_kernel(info_ref, part_0, part_1, part_2, part_3, out_ref, home_ref, line):
-    parts = (part_0, part_1, part_2, part_3)
-    total = sum(item[0:336, :].astype(jnp.float32) for item in parts)
+def fold_kernel(in_ref, out_ref, line):
+    total = in_ref[0].astype(jnp.float32)
     line[...] = jnp.zeros_like(line)
     for owner in range(8):
         lane = 120 * (owner % 4)
         line[0:1, 0:120] = total[320 + owner // 4 : 321 + owner // 4, lane : lane + 120]
         block = jnp.concatenate([total[40 * owner : 40 * owner + 40], line[...]], axis=0)
         out_ref[owner] = block.astype(jnp.bfloat16)
-    for hop, item in enumerate(parts):
-        source = (info_ref[0] - hop) & 3
-        rows = item[336:432, :].astype(jnp.float32)
-        for i, lanes in enumerate((480, 480, 320)):
-            part = rows[32 * i : 32 * i + 32, 0:lanes].reshape(4, 8, lanes).astype(jnp.bfloat16)
-            home_ref[source, :, :, 480 * i : 480 * i + lanes] = part
 
 
 def spread_kernel(in_ref, *outs):
@@ -736,10 +723,9 @@
 
     qkv = qkv.reshape(3, 40, 8, 160).transpose(2, 1, 0, 3).reshape(8, 40, 480)
     qkv = lax.all_to_all(qkv, ("y", "core", "x"), split_axis=0, concat_axis=0, tiled=True)
-    own, qkv = lax.optimization_barrier((own, qkv.reshape(320, 480)))
+    near = jnp.stack([own] + [plane_shift(own, step) for step in (1, 2, 3)])
+    big, near, cotangent, qkv = lax.optimization_barrier((big, near, cotangent, qkv.reshape(320, 480)))
     w_qkv = lax.all_gather(qkv, "z", axis=0, tiled=True)
-    near = jnp.stack([own] + [plane_shift(own, step) for step in (1, 2, 3)])
-    big, near, cotangent = lax.optimization_barrier((big, near, cotangent))
     far = core_swap(near)
     beside, across = plane_shift(big, 1), plane_shift(big, 2)
     relay_a, relay_b = beside[:2], across[2:]
@@ -799,7 +785,7 @@
         in_specs=[smem] + [vmem] * 5 + [hbm] * 6,
         out_specs=[vmem] * 8,
         out_shape=[
-            jax.ShapeDtypeStruct((4, 4, 8, width), f32),
+            jax.ShapeDtypeStruct((4, 4, 8, width), bf16),
             jax.ShapeDtypeStruct((4, 128, width), bf16),
             jax.ShapeDtypeStruct((128, width), f32),
         ]
@@ -830,7 +816,7 @@
     away_a = lax.dynamic_index_in_dim(half_a, 1 - x, 3, keepdims=False)
     away_a, away_b, grad_atts = lax.optimization_barrier((away_a, away_b, jnp.stack(back)))
     from_a, from_b = plane_shift(away_a, 1), plane_shift(away_b, 2)
-    hid_near, hid_far, *send = pl.pallas_call(
+    hid_near, hid_far, send = pl.pallas_call(
         attend_back_kernel,
         grid_spec=pltpu.PrefetchScalarGridSpec(
             num_scalar_prefetch=1,
@@ -840,11 +826,11 @@
                 whole((1, width)), whole((1, 160)), whole((width, 480)),
                 seq_block(2, 4, width=480),
                 *[pl.BlockSpec((4, 1, 32, 160), lambda s, info, core=core: (0, core, s, 0)) for core in range(2)],
-                whole((1, width)), whole((4, 4, 8, width)),
+                whole((1, width)),
             ],
             out_specs=[
                 seq_block(4, width=width), seq_block(4, width=width),
-                *[whole((432, 480))] * 4,
+                whole((4, 336, 480)),
             ],
             scratch_shapes=[
                 pltpu.VMEM((width, 480), f32), pltpu.VMEM((1, width), f32),
@@ -854,17 +840,22 @@
         out_shape=[
             jax.ShapeDtypeStruct((4, 128, width), bf16),
             jax.ShapeDtypeStruct((4, 128, width), bf16),
-            *[jax.ShapeDtypeStruct((432, 480), bf16)] * 4,
+            jax.ShapeDtypeStruct((4, 336, 480), bf16),
         ],
         compiler_params=limit,
         cost_estimate=pl.CostEstimate(flops=15_000_000_000, bytes_accessed=12_000_000, transcendentals=600_000),
         name="attend_back",
-    )(info, near, far, gain_one, query_mult, w_qkv, pre, grad_atts, core_swap(grad_atts), gain_two_grad, out_rows)
-
-    one, three = ring_shift(send[1], 1), ring_shift(send[3], 3)
+    )(info, near, far, gain_one, query_mult, w_qkv, pre, grad_atts, core_swap(grad_atts), gain_two_grad)
+
+    send, out_rows = lax.optimization_barrier((send, out_rows))
+    sums = lax.psum_scatter(send, "z", scatter_dimension=0, tiled=True)
+    out_sent = [pick(out_rows, (z + k) % 4) for k in range(4)]
+    out_one, out_three = ring_shift(out_sent[1], 1), ring_shift(out_sent[3], 3)
+    from_a, from_b, hid_far, out_one, out_three = lax.optimization_barrier(
+        (from_a, from_b, hid_far, out_one, out_three)
+    )
     swapped = core_swap(hid_far)
-    from_a, from_b, one, three, late = lax.optimization_barrier((from_a, from_b, one, three, send[2]))
-    two = ring_shift(late, 2)
+    outputs = by_source([out_sent[0], out_one, ring_shift(out_sent[2], 2), out_three], z, 0).reshape(16, 8, width)
     hid = [sum_low(hid_near[i], swapped[i]) for i in range(4)]
     split = (2, 3, 2, 40, width)
     keep_a, away_a, keep_b, away_b = pl.pallas_call(
@@ -885,9 +876,9 @@
         cost_estimate=pl.CostEstimate(flops=2_000_000_000, bytes_accessed=4_000_000, transcendentals=0),
         name="join",
     )(keep_a, plane_shift(away_a, 2), keep_b, plane_shift(away_b, 1))
-    *hid, kept, two = lax.optimization_barrier((*hid, kept, two))
+    *hid, kept, outputs = lax.optimization_barrier((*hid, kept, outputs))
     moved = [plane_shift(hid[step], step) for step in (1, 2, 3)]
-    moved[0], mine = lax.optimization_barrier((moved[0], send[0]))
+    moved[0], sums = lax.optimization_barrier((moved[0], sums))
     big_sums = lax.psum_scatter(kept, "z", scatter_dimension=0, tiled=True)[0]
     grad_home = pl.pallas_call(
         norm_kernel,
@@ -899,16 +890,16 @@
         cost_estimate=pl.CostEstimate(flops=2_000_000_000, bytes_accessed=2_500_000, transcendentals=128),
         name="norm",
     )(info, hid[0], *moved, x_rows, grad_mid, gain_one)
-    sums, outputs = pl.pallas_call(
+    sums = pl.pallas_call(
         fold_kernel,
-        in_specs=[smem] + [vmem] * 4,
-        out_specs=[vmem] * 2,
-        out_shape=[jax.ShapeDtypeStruct((8, 48, 480), bf16), jax.ShapeDtypeStruct((4, 4, 8, width), bf16)],
+        in_specs=[vmem],
+        out_specs=vmem,
+        out_shape=jax.ShapeDtypeStruct((8, 48, 480), bf16),
         scratch_shapes=[pltpu.VMEM((8, 480), f32)],
         compiler_params=limit,
         cost_estimate=pl.CostEstimate(flops=2_000_000_000, bytes_accessed=1_600_000, transcendentals=0),
         name="fold",
-    )(info, mine, one, two, three)
+    )(sums)
     sums = lax.all_to_all(sums, ("y", "core", "x"), split_axis=0, concat_axis=0, tiled=True)
     rows_shape = [jax.ShapeDtypeStruct((40, width), f32)] * 3
     qkv_sums = pl.pallas_call(
@@ -924,7 +915,7 @@
     grad_home = by_source(grad_home, z, 0).reshape(16, 8, width)
 
     return (
-        outputs.reshape(16, 8, width), grad_home, qkv_sums[0], qkv_sums[1], qkv_sums[2],
+        outputs, grad_home, qkv_sums[0], qkv_sums[1], qkv_sums[2],
         big_sums[0], big_sums[1], big_sums[2], line_sums[0], line_sums[1], scale_sum,
     )
 

time: 253 us -> 249 us (0.984)
  waiting for transfers between devices: 110 us -> 98.6 us
  other arithmetic: 12.8 us -> 16 us
  starting transfers between devices: 48.6 us -> 51.5 us
    ppermute x8, waiting for transfers between devices: 20.2 us -> 6.23 us  [plane_shift(): return lax.ppermute(value, 'y', [(0, 1), (1, 0)])]
    ppermute x8, waiting for transfers between devices: 33 us -> 38 us  [plane_shift(): return lax.ppermute(value, 'x', [(0, 1), (1, 0)])]
    all_gather x1, waiting for transfers between devices: 0.06 us -> 4.62 us  [planes(): w_qkv = lax.all_gather(qkv, 'z', axis=0, tiled=True)]
    ppermute x9, waiting for transfers between devices: 40.3 us -> 36.2 us  [ring_shift(): return lax.ppermute(value, 'z', [(i, (i + step) % 4) for i in range(4)])]
    all_to_all x1, starting transfers between devices: 4.09 us -> 7.36 us  [planes(): lax.all_to_all(cotangent.reshape(4, 4, 8, width), 'z', split_axis=0, conc...]
    all_to_all x1, waiting for transfers between devices: 2.84 us -> 0.29 us  [planes(): lax.all_to_all(qkv, ('y', 'core', 'x'), split_axis=0, concat_axis=0, tile...]
    unnamed x50 -> x46, local copies, waits for them, and re-layouts: 7.98 us -> 7.97 us
  transfers between devices with their start and end apart: 44 -> 45, of which waited for: 22 -> 25; matrix products, arithmetic and copies ran while one was open for 7% -> 8% of each run, Pallas kernels for 15% -> 16%
where the time goes in v10:
time: 249 us; the launch traced here: 248 us
  waiting for transfers between devices  98.6 us (40%)
  starting transfers between devices  51.5 us (21%)
  Pallas kernels  49 us (20%)
  local copies, waits for them, and re-layouts  18.9 us (8%)
  other arithmetic  16 us (6%)
  between operations  14.4 us (6%)
    ppermute x8, waiting for transfers between devices, plane_shift(): return lax.ppermute(value, 'x', [(0, 1), (1, 0)])  38 us
    ppermute x9, waiting for transfers between devices, ring_shift(): return lax.ppermute(value, 'z', [(i, (i + step) % 4) for i in range(4)])  36.2 us
    ppermute x9, starting transfers between devices, ring_shift(): return lax.ppermute(value, 'z', [(i, (i + step) % 4) for i in range(4)])  15 us
    pallas_call x1, Pallas kernels, planes(): pl.pallas_call(attend_back_kernel, grid_spec=pltpu.PrefetchScalarGridSpec...  13.5 us
    ppermute x4, waiting for transfers between devices, plane_shift(): return lax.ppermute(value, ('y', 'x'), [(0, 3), (1, 2), (2, 1), (3, 0)])  10.6 us
    pallas_call x1, Pallas kernels, planes(): pl.pallas_call(feed_kernel, in_specs=[smem] + [vmem] * 5 + [hbm] * 6, out...  9.64 us
    ppermute x8, starting transfers between devices, plane_shift(): return lax.ppermute(value, 'x', [(0, 1), (1, 0)])  8.63 us
    pallas_call x1, Pallas kernels, planes(): pl.pallas_call(attend_kernel, grid_spec=pltpu.PrefetchScalarGridSpec(num_...  8.24 us
  transfers between devices with their start and end apart: 45, of which 25 were waited for; matrix products, arithmetic and copies ran while one was open for 8% of the time, Pallas kernels for 16%

profile of v10, /device:TPU:0, one launch (start us, length us, event | category | flops | bytes accessed | tf_op | source)
XLA Modules:
  0.0 248.5 jit_solution(528517202735686893)
XLA Ops:
  7.3 1.1 convert_bitcast_fusion.5
  8.4 1.1 convert_bitcast_fusion.3
  10.7 5.1 %collective-permute-start = (bf16[5,8,1280]{2,1,0:T(8,128)(2,1)S(1)}, bf16[5,8,1280]{2,1,0:T(8,128)(2,1)S(1)}, u32[]{:S(2)}, u32[]{:S(2)}) collective-permute-start(bf16[5,8,1280]{2,1,0:T(8,128)(2,1)S(1)} %get-tuple-element.97), channel_id=1, source_target_pairs={{0,24},{8,0},{16,8},{24,16},{1,25},{9,1},{17,9},{25,17},{2,26},{10... | collective-permute-start | bytes 307208 | tf_op jit(solution)/shard_map/ppermute | solution.py:357
  15.8 1.0 collective-permute-start.2
  17.5 1.6 collective-permute-done
  19.1 7.4 %collective-permute-done.1 = bf16[5,8,1280]{2,1,0:T(8,128)(2,1)S(1)} collective-permute-done((bf16[5,8,1280]{2,1,0:T(8,128)(2,1)S(1)}, bf16[5,8,1280]{2,1,0:T(8,128)(2,1)S(1)}, u32[]{:S(2)}, u32[]{:S(2)}) %collective-permute-start.1) | collective-permute-done | bytes 102432 | tf_op jit(solution)/shard_map/ppermute | solution.py:357
  27.0 1.7 collective-permute-start.4
  28.6 1.5 collective-permute-start.3
  31.6 1.1 reshape.345
  32.6 3.9 %all-to-all-start = ((bf16[8,40,480]{2,1,0:T(8,128)(2,1)}), bf16[8,40,480]{2,1,0:T(8,128)(2,1)S(1)}, u32[]{:S(2)}, u32[]{:S(2)}) async-start(bf16[8,40,480]{2,1,0:T(8,128)(2,1)} %reshape.345), calls=%async_computation | async-start | bytes 655360 | tf_op jit(solution)/shard_map/all_to_all | solution.py:725
  37.2 2.6 %collective-permute-done.3 = bf16[136,1280]{1,0:T(8,128)(2,1)} collective-permute-done((bf16[136,1280]{1,0:T(8,128)(2,1)S(1)}, bf16[136,1280]{1,0:T(8,128)(2,1)}, u32[]{:S(2)}, u32[]{:S(2)}) %collective-permute-start.3) | collective-permute-done | bytes 348192 | tf_op jit(solution)/shard_map/ppermute | solution.py:346
  39.8 5.7 %collective-permute-done.5 = bf16[136,1280]{1,0:T(8,128)(2,1)} collective-permute-done((bf16[136,1280]{1,0:T(8,128)(2,1)S(1)}, bf16[136,1280]{1,0:T(8,128)(2,1)}, u32[]{:S(2)}, u32[]{:S(2)}) %collective-permute-start.5) | collective-permute-done | bytes 348192 | tf_op jit(solution)/shard_map/ppermute | solution.py:349
  45.5 1.3 pad_maximum_fusion.near_ref
  47.1 1.5 collective-permute-start.7
  48.6 1.3 collective-permute-start.8
  50.4 7.4 %all-to-all-start.1 = ((bf16[4,4,8,1280]{3,2,1,0:T(8,128)(2,1)}), bf16[4,4,8,1280]{3,2,1,0:T(8,128)(2,1)S(1)}, u32[]{:S(2)}, u32[]{:S(2)}) async-start(bf16[4,4,8,1280]{3,2,1,0:T(8,128)(2,1)} %bitcast.140), calls=%async_computation.1 | async-start | bytes 655360 | tf_op jit(solution)/shard_map/all_to_all | solution.py:732
  57.8 18.6 %collective-permute-done.7 = bf16[4,3,40,1280]{3,2,1,0:T(8,128)(2,1)S(1)} collective-permute-done((bf16[4,3,40,1280]{3,2,1,0:T(8,128)(2,1)}, bf16[4,3,40,1280]{3,2,1,0:T(8,128)(2,1)S(1)}, u32[]{:S(2)}, u32[]{:S(2)}) %collective-permute-start.7) | collective-permute-done | bytes 1228832 | tf_op jit(solution)/shard_map/ppermute | solution.py:346
  76.3 0.9 slice.174
  77.5 2.4 fusion.23
  80.4 1.0 collective-permute-start.11
  81.4 2.9 %bitcast_select_fusion.near_rows = bf16[4,3,80,1280]{3,2,1,0:T(8,128)(2,1)} fusion(pred[80]{0:T(512)(128)(4,1)S(1)} %broadcast_in_dim.383, bf16[4,3,40,1280]{3,2,1,0:T(8,128)(2,1)S(1)} %collective-permute-done.7, bf16[4,3,40,1280]{3,2,1,0:T(8,128)(2,1)} %all-gather.3.cloned.1.call-done), kind=kLoop, calls=%fused_computation | loop fusion | flops 1228800 | bytes 4915280 | tf_op jit(solution)/shard_map/jit(_where)/select_n | solution.py:379
  85.6 4.6 %all-gather.5.cloned.1.call-done.w_ref = bf16[1280,480]{1,0:T(8,128)(2,1)} async-done(((bf16[320,480]{1,0:T(8,128)(2,1)}), bf16[1280,480]{1,0:T(8,128)(2,1)}) %all-gather.5.cloned.1.call-update) | async-done | bytes 1228816 | tf_op jit(solution)/shard_map/all_gather | solution.py:728
  90.2 1.3 copy-done.2
  91.5 8.2 %attend.1 = (f32[2,4,128,480]{3,2,1,0:T(8,128)}, bf16[4,2,128,160]{3,2,1,0:T(8,128)(2,1)S(1)}) custom-call(s32[6]{0:T(128)S(1)} %pad_add_fusion.info_ref, bf16[4,136,1280]{2,1,0:T(8,128)(2,1)S(1)} %pad_maximum_fusion.near_ref, bf16[4,136,1280]{2,1,0:T(8,128)(2,1)} %collective-permute-done.6.far_ref, f32[1,1280]{1,0:T(1,128)S(1)} %slice.141.gain_ref, ...), custom_call_target="tpu_custom_call" | custom-call | flops 8999999488 | bytes 8000000 | tf_op jit(solution)/shard_map/attend/pallas_call | solution.py:747
  99.9 2.9 %bitcast_select_fusion.1 = (bf16[2,3,80,1280]{3,2,1,0:T(8,128)(2,1)}, bf16[2,3,80,1280]{3,2,1,0:T(8,128)(2,1)}) fusion(pred[80]{0:T(512)(128)(4,1)S(1)} %broadcast_in_dim.383, bf16[2,3,40,1280]{3,2,1,0:T(8,128)(2,1)} %collective-permute-done.11, bf16[2,3,40,1280]{3,2,1,0:T(8,128)(2,1)S(1)} %copy-done.12, bf16[2,3,40,1280]{3,2,1,0:T(8,128)(2,1)} %collective-permute-done.10, ...), kind=kLoop, calls=%fused_computation.2 | loop fusion | flops 1228800 | bytes 4915280 | tf_op jit(solution)/shard_map/jit(_where)/select_n | solution.py:379
  103.9 1.5 collective-permute-start.13
  105.3 5.0 %collective-permute-done.14 = bf16[2,128,160]{2,1,0:T(8,128)(2,1)S(1)} collective-permute-done((bf16[2,128,160]{2,1,0:T(8,128)(2,1)S(1)}, bf16[2,128,160]{2,1,0:T(8,128)(2,1)S(1)}, u32[]{:S(2)}, u32[]{:S(2)}) %collective-permute-start.14) | collective-permute-done | bytes 81952 | tf_op jit(solution)/shard_map/ppermute | solution.py:349
  110.8 1.5 collective-permute-done.13
  112.3 3.0 %collective-permute-done.12 = bf16[2,128,160]{2,1,0:T(8,128)(2,1)S(1)} collective-permute-done((bf16[2,128,160]{2,1,0:T(8,128)(2,1)S(1)}, bf16[2,128,160]{2,1,0:T(8,128)(2,1)S(1)}, u32[]{:S(2)}, u32[]{:S(2)}) %collective-permute-start.12) | collective-permute-done | bytes 81952 | tf_op jit(solution)/shard_map/ppermute | solution.py:346
  115.6 1.8 collective-permute-done.15.far_atts
  117.4 9.6 %feed.1 = (bf16[4,4,8,1280]{3,2,1,0:T(8,128)(2,1)S(1)}, bf16[4,128,1280]{2,1,0:T(8,128)(2,1)}, f32[128,1280]{1,0:T(8,128)S(1)}, bf16[2,128,160]{2,1,0:T(8,128)(2...) custom-call(s32[6]{0:T(128)S(1)} %pad_add_fusion.info_ref, ...), custom_call_target="tpu_custom_call" | custom-call | flops 12000000000 | bytes 13000000 | tf_op jit(solution)/shard_map/feed/pallas_call | solution.py:783
  129.0 2.5 %collective-permute-start.22 = (bf16[2,128,160]{2,1,0:T(8,128)(2,1)S(1)}, bf16[2,128,160]{2,1,0:T(8,128)(2,1)S(1)}, u32[]{:S(2)}, u32[]{:S(2)}) collective-permute-start(bf16[2,128,160]{2,1,0:T(8,128)(2,1)S(1)} %get-tuple-element.125), channel_id=1, source_target_pairs={{0,5},{1,4},{4,1},{5,0},{2,7},{3,6},{6,3},{7,2},{8,13},{9,12},{12,... | collective-permute-start | bytes 245768 | tf_op jit(solution)/shard_map/ppermute | solution.py:349
  131.5 7.2 %grads.1 = (bf16[2,3,2,80,1280]{4,3,2,1,0:T(8,128)(2,1)}, bf16[2,3,80,1280]{3,2,1,0:T(8,128)(2,1)S(1)}, bf16[2,3,80,1280]{3,2,1,0:T(8,128)(2,1)}) custom-call(s32[6]{0:T(128)S(1)} %pad_add_fusion.info_ref, bf16[4,128,1280]{2,1,0:T(8,128)(2,1)} %get-tuple-element.117.pack_ref, bf16[4,128,1280]{2,1,0:T(8,128)(2,1)} %collective-permute-done.19.far_pack, ...), custom_call_target="tpu_custom_call" | custom-call | flops 6000000000 | bytes 8000000 | tf_op jit(solution)/shard_map/grads/pallas_call | solution.py:803
  138.8 2.8 %dynamic-slice_bitcast_fusion = bf16[2,3,2,40,1280]{4,3,2,1,0:T(8,128)(2,1)} fusion(bf16[2,3,2,2,40,1280]{5,4,3,2,1,0:T(8,128)(2,1)} %bitcast.136, s32[]{:T(128)S(6)} %select_n.217), kind=kLoop, calls=%fused_computation.4 | loop fusion | bytes 2457604 | tf_op jit(solution)/shard_map/jit(dynamic_index_in_dim)/squeeze | solution.py:816
  143.7 13.5 %attend_back.1 = (bf16[4,128,1280]{2,1,0:T(8,128)(2,1)S(1)}, bf16[4,128,1280]{2,1,0:T(8,128)(2,1)S(1)}, bf16[4,336,480]{2,1,0:T(8,128)(2,1)}) custom-call(s32[6]{0:T(128)S(1)} %pad_add_fusion.info_ref, bf16[4,136,1280]{2,1,0:T(8,128)(2,1)} %copy-done, bf16[4,136,1280]{2,1,0:T(8,128)(2,1)} %collective-permute-done.6.far_ref, f32[1,1280]{1,0:T(1,128)S(1)} %slice.141.gain_ref, ...), custom_call_target="tpu_custom_call" | custom-call | flops 15000000512 | bytes 12000000 | tf_op jit(solution)/shard_map/attend_back/pallas_call | solution.py:819
  157.3 1.5 collective-permute-start.27
  159.4 2.5 collective-permute-done.27
  161.8 3.6 %collective-permute-done.26 = bf16[4,8,1280]{2,1,0:T(8,128)(2,1)S(1)} collective-permute-done((bf16[4,8,1280]{2,1,0:T(8,128)(2,1)S(1)}, bf16[4,8,1280]{2,1,0:T(8,128)(2,1)S(1)}, u32[]{:S(2)}, u32[]{:S(2)}) %collective-permute-start.26) | collective-permute-done | bytes 81952 | tf_op jit(solution)/shard_map/ppermute | solution.py:357
  165.4 6.1 %collective-permute-done.24.from_a = bf16[2,3,2,40,1280]{4,3,2,1,0:T(8,128)(2,1)} collective-permute-done((bf16[2,3,2,40,1280]{4,3,2,1,0:T(8,128)(2,1)}, bf16[2,3,2,40,1280]{4,3,2,1,0:T(8,128)(2,1)}, u32[]{:S(2)}, u32[]{:S(2)}) %collective-permute-start.24) | collective-permute-done | bytes 1228832 | tf_op jit(solution)/shard_map/ppermute | solution.py:346
  171.7 4.2 %meet.1 = (bf16[2,3,40,1280]{3,2,1,0:T(8,128)(2,1)S(1)}, bf16[2,3,40,1280]{3,2,1,0:T(8,128)(2,1)}, bf16[2,3,40,1280]{3,2,1,0:T(8,128)(2,1)S(1)}, bf16[2,3,40,1280]{3,2,1,0:T(8,128)(2,1)}) custom-call(s32[6]{0:T(128)S(1)} %pad_add_fusion.info_ref, bf16[2,3,2,2,40,1280]{5,4,3,2,1,0:T(8,128)(2,1)} %bitcast.137, ...), custom_call_target="tpu_custom_call" | custom-call | flops 3000000000 | bytes 8000000 | tf_op jit(solution)/shard_map/meet/pallas_call | solution.py:861
  178.1 1.6 collective-permute-start.30
  179.7 2.4 collective-permute-start.31
  182.5 8.4 %collective-permute-done.31 = bf16[4,8,1280]{2,1,0:T(8,128)(2,1)S(1)} collective-permute-done((bf16[4,8,1280]{2,1,0:T(8,128)(2,1)S(1)}, bf16[4,8,1280]{2,1,0:T(8,128)(2,1)S(1)}, u32[]{:S(2)}, u32[]{:S(2)}) %collective-permute-start.31) | collective-permute-done | bytes 81952 | tf_op jit(solution)/shard_map/ppermute | solution.py:357
  191.8 2.4 collective-permute-done.29.from_a
  194.4 1.1 copy-done.6
  195.5 1.1 copy-done.8
  196.6 2.7 %join.1 = bf16[4,3,40,1280]{3,2,1,0:T(8,128)(2,1)} custom-call(bf16[2,3,40,1280]{3,2,1,0:T(8,128)(2,1)S(1)} %copy-done.6, bf16[2,3,40,1280]{3,2,1,0:T(8,128)(2,1)} %collective-permute-done.29.from_a, bf16[2,3,40,1280]{3,2,1,0:T(8,128)(2,1)S(1)} %copy-done.8, bf16[2,3,40,1280]{3,2,1,0:T(8,128)(2,1)} %collective-permute-done.30.from_b), custom_call_target="tpu_custom_call" | custom-call | flops 2000000000 | bytes 4000000 | tf_op jit(solution)/shard_map/join/pallas_call | solution.py:870
  199.2 2.4 fusion.3
  201.7 1.6 collective-permute-start.32
  203.3 1.5 collective-permute-start.33
  205.2 7.4 %collective-permute-done.32.hid_1 = bf16[128,1280]{1,0:T(8,128)(2,1)S(1)} collective-permute-done((bf16[128,1280]{1,0:T(8,128)(2,1)}, bf16[128,1280]{1,0:T(8,128)(2,1)S(1)}, u32[]{:S(2)}, u32[]{:S(2)}) %collective-permute-start.32) | collective-permute-done | bytes 327712 | tf_op jit(solution)/shard_map/ppermute | solution.py:346
  212.6 1.0 copy-done.3
  213.6 0.9 fold.1
  214.5 3.8 %all-to-all-start.2 = ((bf16[8,48,480]{2,1,0:T(8,128)(2,1)}), bf16[8,48,480]{2,1,0:T(8,128)(2,1)S(1)}, u32[]{:S(2)}, u32[]{:S(2)}) async-start(bf16[8,48,480]{2,1,0:T(8,128)(2,1)} %fold.1), calls=%async_computation.3 | async-start | bytes 786432 | tf_op jit(solution)/shard_map/all_to_all | solution.py:903
  218.3 1.1 collective-permute-done.33.hid_2
  219.4 1.0 norm.1
  220.5 1.5 collective-permute-start.35
  222.0 1.0 collective-permute-start.36
  223.0 1.9 collective-permute-start.37
  224.9 3.6 %collective-permute-done.35 = bf16[4,8,1280]{2,1,0:T(8,128)(2,1)S(1)} collective-permute-done((bf16[4,8,1280]{2,1,0:T(8,128)(2,1)S(1)}, bf16[4,8,1280]{2,1,0:T(8,128)(2,1)S(1)}, u32[]{:S(2)}, u32[]{:S(2)}) %collective-permute-start.35) | collective-permute-done | bytes 81952 | tf_op jit(solution)/shard_map/ppermute | solution.py:357
  228.5 9.2 %collective-permute-done.36 = bf16[4,8,1280]{2,1,0:T(8,128)(2,1)S(1)} collective-permute-done((bf16[4,8,1280]{2,1,0:T(8,128)(2,1)S(1)}, bf16[4,8,1280]{2,1,0:T(8,128)(2,1)S(1)}, u32[]{:S(2)}, u32[]{:S(2)}) %collective-permute-start.36) | collective-permute-done | bytes 81952 | tf_op jit(solution)/shard_map/ppermute | solution.py:357
  237.7 0.9 fusion.5
  238.6 0.9 spread.1
  240.1 1.0 copy-done.1
  (164 shorter events, 19.6 us)
Async XLA Ops:
  7.2 3.1 %copy-start.20 = (f32[40]{0:T(128)S(1)}, f32[40]{0:T(128)}, u32[]{:S(2)}) copy-start(f32[40]{0:T(128)} %param.23) | copy-start | bytes 484
  7.2 3.1 %copy-start.15 = (f32[40,1280]{1,0:T(8,128)S(1)}, f32[40,1280]{1,0:T(8,128)}, u32[]{:S(2)}) copy-start(f32[40,1280]{1,0:T(8,128)} %param.17) | copy-start | bytes 614404
  7.2 3.2 %copy-start.18 = (f32[40]{0:T(128)S(1)}, f32[40]{0:T(128)}, u32[]{:S(2)}) copy-start(f32[40]{0:T(128)} %param.25) | copy-start | bytes 484
  7.2 3.2 %copy-start.19 = (f32[40]{0:T(128)S(1)}, f32[40]{0:T(128)}, u32[]{:S(2)}) copy-start(f32[40]{0:T(128)} %param.24) | copy-start | bytes 484
  7.2 3.2 %copy-start.16 = (f32[40,1280]{1,0:T(8,128)S(1)}, f32[40,1280]{1,0:T(8,128)}, u32[]{:S(2)}) copy-start(f32[40,1280]{1,0:T(8,128)} %param.19) | copy-start | bytes 614404
  7.2 3.2 %copy-start.17 = (f32[40,1280]{1,0:T(8,128)S(1)}, f32[40,1280]{1,0:T(8,128)}, u32[]{:S(2)}) copy-start(f32[40,1280]{1,0:T(8,128)} %param.18) | copy-start | bytes 614404
  7.2 39.8 %all-gather.3.cloned.1.call-start = ((), (), s32[]{:S(2)}) async-start(), calls=%async_computation.5 | async-start | bytes 1536000 | tf_op jit(solution)/shard_map/all_gather | solution.py:722
  9.5 1.1 copy-start.14
  10.7 8.4 %collective-permute-start = (bf16[5,8,1280]{2,1,0:T(8,128)(2,1)S(1)}, bf16[5,8,1280]{2,1,0:T(8,128)(2,1)S(1)}, u32[]{:S(2)}, u32[]{:S(2)}) collective-permute-start(bf16[5,8,1280]{2,1,0:T(8,128)(2,1)S(1)} %get-tuple-element.97), channel_id=1, source_target_pairs={{0,24},{8,0},{16,8},{24,16},{1,25},{9,1},{17,9},{25,17},{2,26},{10... | collective-permute-start | bytes 307208 | tf_op jit(solution)/shard_map/ppermute | solution.py:357
  15.8 10.7 %collective-permute-start.1 = (bf16[5,8,1280]{2,1,0:T(8,128)(2,1)S(1)}, bf16[5,8,1280]{2,1,0:T(8,128)(2,1)S(1)}, u32[]{:S(2)}, u32[]{:S(2)}) collective-permute-start(bf16[5,8,1280]{2,1,0:T(8,128)(2,1)S(1)} %get-tuple-element.98), channel_id=1, source_target_pairs={{0,16},{8,24},{16,0},{24,8},{1,17},{9,25},{17,1},{25,9},{2,18},{10... | collective-permute-start | bytes 307208 | tf_op jit(solution)/shard_map/ppermute | solution.py:357
  15.8 10.7 %collective-permute-start.2 = (bf16[5,8,1280]{2,1,0:T(8,128)(2,1)S(1)}, bf16[5,8,1280]{2,1,0:T(8,128)(2,1)S(1)}, u32[]{:S(2)}, u32[]{:S(2)}) collective-permute-start(bf16[5,8,1280]{2,1,0:T(8,128)(2,1)S(1)} %get-tuple-element.99), channel_id=1, source_target_pairs={{0,8},{8,16},{16,24},{24,0},{1,9},{9,17},{17,25},{25,1},{2,10},{10... | collective-permute-start | bytes 307208 | tf_op jit(solution)/shard_map/ppermute | solution.py:357
  27.0 10.2 %collective-permute-start.4 = (bf16[136,1280]{1,0:T(8,128)(2,1)S(1)}, bf16[136,1280]{1,0:T(8,128)(2,1)S(1)}, u32[]{:S(2)}, u32[]{:S(2)}) collective-permute-start(bf16[136,1280]{1,0:T(8,128)(2,1)S(1)} %get-tuple-element.182), channel_id=1, source_target_pairs={{0,4},{4,0},{1,5},{5,1},{2,6},{6,2},{3,7},{7,3},{8,12},{12,8},{9,1... | collective-permute-start | bytes 1044488 | tf_op jit(solution)/shard_map/ppermute | solution.py:348
  28.6 11.2 %collective-permute-start.3 = (bf16[136,1280]{1,0:T(8,128)(2,1)S(1)}, bf16[136,1280]{1,0:T(8,128)(2,1)}, u32[]{:S(2)}, u32[]{:S(2)}) collective-permute-start(bf16[136,1280]{1,0:T(8,128)(2,1)S(1)} %get-tuple-element.182), channel_id=1, source_target_pairs={{0,1},{1,0},{2,3},{3,2},{4,5},{5,4},{6,7},{7,6},{8,9},{9,8},{10,11... | collective-permute-start | bytes 1044488 | tf_op jit(solution)/shard_map/ppermute | solution.py:346
  30.2 15.3 %collective-permute-start.5 = (bf16[136,1280]{1,0:T(8,128)(2,1)S(1)}, bf16[136,1280]{1,0:T(8,128)(2,1)}, u32[]{:S(2)}, u32[]{:S(2)}) collective-permute-start(bf16[136,1280]{1,0:T(8,128)(2,1)S(1)} %get-tuple-element.182), channel_id=1, source_target_pairs={{0,5},{1,4},{4,1},{5,0},{2,7},{3,6},{6,3},{7,2},{8,13},{9,12},{12,... | collective-permute-start | bytes 1044488 | tf_op jit(solution)/shard_map/ppermute | solution.py:349
  32.6 14.4 %all-to-all-start = ((bf16[8,40,480]{2,1,0:T(8,128)(2,1)}), bf16[8,40,480]{2,1,0:T(8,128)(2,1)S(1)}, u32[]{:S(2)}, u32[]{:S(2)}) async-start(bf16[8,40,480]{2,1,0:T(8,128)(2,1)} %reshape.345), calls=%async_computation | async-start | bytes 655360 | tf_op jit(solution)/shard_map/all_to_all | solution.py:725
  36.5 53.7 %all-gather.5.cloned.1.call-start = ((), (), s32[]{:S(2)}) async-start(), calls=%async_computation.6 | async-start | bytes 1638400 | tf_op jit(solution)/shard_map/all_gather | solution.py:728
  45.5 4.6 %copy-start.21 = (s32[16]{0:T(128)S(1)}, s32[16]{0:T(128)}, u32[]{:S(2)}) copy-start(s32[16]{0:T(128)} %param.27) | copy-start | bytes 196
  45.5 4.6 %copy-start.22 = (s32[16]{0:T(128)S(1)}, s32[16]{0:T(128)}, u32[]{:S(2)}) copy-start(s32[16]{0:T(128)} %param.26) | copy-start | bytes 196
  46.8 43.4 %copy-start = (bf16[4,136,1280]{2,1,0:T(8,128)(2,1)}, bf16[4,136,1280]{2,1,0:T(8,128)(2,1)S(1)}, u32[]{:S(2)}) copy-start(bf16[4,136,1280]{2,1,0:T(8,128)(2,1)S(1)} %pad_maximum_fusion.near_ref) | copy-start | bytes 4177924
  47.1 3.0 %copy-start.13 = (bf16[8,40,480]{2,1,0:T(8,128)(2,1)}, bf16[8,40,480]{2,1,0:T(8,128)(2,1)S(1)}, u32[]{:S(2)}) copy-start(bf16[8,40,480]{2,1,0:T(8,128)(2,1)S(1)} %all-to-all-done) | copy-start | bytes 921604
  47.1 29.3 %collective-permute-start.7 = (bf16[4,3,40,1280]{3,2,1,0:T(8,128)(2,1)}, bf16[4,3,40,1280]{3,2,1,0:T(8,128)(2,1)S(1)}, u32[]{:S(2)}, u32[]{:S(2)}) collective-permute-start(bf16[4,3,40,1280]{3,2,1,0:T(8,128)(2,1)} %all-gather.3.cloned.1.call-done), channel_id=1, source_target_pairs={{0,1},{1,0},{2,3},{3,2},{4,5},{5,4},{6,7},{7,6},{8,9},{9,8},{10,11... | collective-permute-start | bytes 3686408 | tf_op jit(solution)/shard_map/ppermute | solution.py:346
  48.6 28.9 %collective-permute-start.8 = (bf16[4,3,40,1280]{3,2,1,0:T(8,128)(2,1)}, bf16[4,3,40,1280]{3,2,1,0:T(8,128)(2,1)}, u32[]{:S(2)}, u32[]{:S(2)}) collective-permute-start(bf16[4,3,40,1280]{3,2,1,0:T(8,128)(2,1)} %all-gather.3.cloned.1.call-done), channel_id=1, source_target_pairs={{0,4},{4,0},{1,5},{5,1},{2,6},{6,2},{3,7},{7,3},{8,12},{12,8},{9,1... | collective-permute-start | bytes 3686408 | tf_op jit(solution)/shard_map/ppermute | solution.py:348
  49.9 34.4 %collective-permute-start.6 = (bf16[4,136,1280]{2,1,0:T(8,128)(2,1)S(1)}, bf16[4,136,1280]{2,1,0:T(8,128)(2,1)}, u32[]{:S(2)}, u32[]{:S(2)}) collective-permute-start(bf16[4,136,1280]{2,1,0:T(8,128)(2,1)S(1)} %pad_maximum_fusion.near_ref), channel_id=1, source_target_pairs={{0,2},{2,0},{1,3},{3,1},{4,6},{6,4},{5,7},{7,5},{8,10},{10,8},{9,1... | collective-permute-start | bytes 4177928 | tf_op jit(solution)/shard_map/ppermute | solution.py:353
  50.4 29.5 %all-to-all-start.1 = ((bf16[4,4,8,1280]{3,2,1,0:T(8,128)(2,1)}), bf16[4,4,8,1280]{3,2,1,0:T(8,128)(2,1)S(1)}, u32[]{:S(2)}, u32[]{:S(2)}) async-start(bf16[4,4,8,1280]{3,2,1,0:T(8,128)(2,1)} %bitcast.140), calls=%async_computation.1 | async-start | bytes 655360 | tf_op jit(solution)/shard_map/all_to_all | solution.py:732
  57.8 154.9 %reduce-scatter.3.cloned.1.call-start = ((), (), s32[]{:S(2)}) async-start(), calls=%async_computation.7 | async-start | bytes 1720320 | tf_op jit(solution)/shard_map/reduce_scatter | solution.py:851
  79.9 19.8 %collective-permute-start.10 = (bf16[2,3,40,1280]{3,2,1,0:T(8,128)(2,1)}, bf16[2,3,40,1280]{3,2,1,0:T(8,128)(2,1)}, u32[]{:S(2)}, u32[]{:S(2)}) collective-permute-start(bf16[2,3,40,1280]{3,2,1,0:T(8,128)(2,1)} %slice.174), channel_id=1, source_target_pairs={{0,4},{4,0},{1,5},{5,1},{2,6},{6,2},{3,7},{7,3},{8,12},{12,8},{9,1... | collective-permute-start | bytes 1843208 | tf_op jit(solution)/shard_map/ppermute | solution.py:348
  80.4 19.4 %collective-permute-start.11 = (bf16[2,3,40,1280]{3,2,1,0:T(8,128)(2,1)}, bf16[2,3,40,1280]{3,2,1,0:T(8,128)(2,1)}, u32[]{:S(2)}, u32[]{:S(2)}) collective-permute-start(bf16[2,3,40,1280]{3,2,1,0:T(8,128)(2,1)} %get-tuple-element.110), channel_id=1, source_target_pairs={{0,1},{1,0},{2,3},{3,2},{4,5},{5,4},{6,7},{7,6},{8,9},{9,8},{10,11... | collective-permute-start | bytes 1843208 | tf_op jit(solution)/shard_map/ppermute | solution.py:346
  90.2 1.3 copy-start.2
  91.5 8.4 %copy-start.11 = (bf16[2,3,40,1280]{3,2,1,0:T(8,128)(2,1)S(1)}, bf16[2,3,40,1280]{3,2,1,0:T(8,128)(2,1)}, u32[]{:S(2)}) copy-start(bf16[2,3,40,1280]{3,2,1,0:T(8,128)(2,1)} %get-tuple-element.175) | copy-start | bytes 1843204
  91.5 8.4 %copy-start.12 = (bf16[2,3,40,1280]{3,2,1,0:T(8,128)(2,1)S(1)}, bf16[2,3,40,1280]{3,2,1,0:T(8,128)(2,1)}, u32[]{:S(2)}) copy-start(bf16[2,3,40,1280]{3,2,1,0:T(8,128)(2,1)} %get-tuple-element.110) | copy-start | bytes 1843204
  99.7 17.7 %collective-permute-start.16 = (bf16[4,3,80,1280]{3,2,1,0:T(8,128)(2,1)}, bf16[4,3,80,1280]{3,2,1,0:T(8,128)(2,1)}, u32[]{:S(2)}, u32[]{:S(2)}) collective-permute-start(bf16[4,3,80,1280]{3,2,1,0:T(8,128)(2,1)} %bitcast_select_fusion.near_rows), channel_id=1, source_target_pairs={{0,2},{2,0},{1,3},{3,1},{4,6},{6,4},{5,7},{7,5},{8,10},{10,8},{9,1... | collective-permute-start | bytes 7372808 | tf_op jit(solution)/shard_map/ppermute | solution.py:353
  102.8 14.6 %collective-permute-start.18 = (bf16[2,3,80,1280]{3,2,1,0:T(8,128)(2,1)}, bf16[2,3,80,1280]{3,2,1,0:T(8,128)(2,1)}, u32[]{:S(2)}, u32[]{:S(2)}) collective-permute-start(bf16[2,3,80,1280]{3,2,1,0:T(8,128)(2,1)} %get-tuple-element.201.across_b), channel_id=1, source_target_pairs={{0,2},{2,0},{1,3},{3,1},{4,6},{6,4},{5,7},{7,5},{8,10},{10,8},{9,1... | collective-permute-start | bytes 3686408 | tf_op jit(solution)/shard_map/ppermute | solution.py:353
  103.3 14.1 %collective-permute-start.17 = (bf16[2,3,80,1280]{3,2,1,0:T(8,128)(2,1)}, bf16[2,3,80,1280]{3,2,1,0:T(8,128)(2,1)}, u32[]{:S(2)}, u32[]{:S(2)}) collective-permute-start(bf16[2,3,80,1280]{3,2,1,0:T(8,128)(2,1)} %get-tuple-element.202.across_a), channel_id=1, source_target_pairs={{0,2},{2,0},{1,3},{3,1},{4,6},{6,4},{5,7},{7,5},{8,10},{10,8},{9,1... | collective-permute-start | bytes 3686408 | tf_op jit(solution)/shard_map/ppermute | solution.py:353
  103.4 6.9 %collective-permute-start.14 = (bf16[2,128,160]{2,1,0:T(8,128)(2,1)S(1)}, bf16[2,128,160]{2,1,0:T(8,128)(2,1)S(1)}, u32[]{:S(2)}, u32[]{:S(2)}) collective-permute-start(bf16[2,128,160]{2,1,0:T(8,128)(2,1)S(1)} %get-tuple-element.178), channel_id=1, source_target_pairs={{0,5},{1,4},{4,1},{5,0},{2,7},{3,6},{6,3},{7,2},{8,13},{9,12},{12,... | collective-permute-start | bytes 245768 | tf_op jit(solution)/shard_map/ppermute | solution.py:349
  103.9 8.4 %collective-permute-start.13 = (bf16[2,128,160]{2,1,0:T(8,128)(2,1)S(1)}, bf16[2,128,160]{2,1,0:T(8,128)(2,1)S(1)}, u32[]{:S(2)}, u32[]{:S(2)}) collective-permute-start(bf16[2,128,160]{2,1,0:T(8,128)(2,1)S(1)} %get-tuple-element.179), channel_id=1, source_target_pairs={{0,4},{4,0},{1,5},{5,1},{2,6},{6,2},{3,7},{7,3},{8,12},{12,8},{9,1... | collective-permute-start | bytes 245768 | tf_op jit(solution)/shard_map/ppermute | solution.py:348
  110.3 5.0 %collective-permute-start.12 = (bf16[2,128,160]{2,1,0:T(8,128)(2,1)S(1)}, bf16[2,128,160]{2,1,0:T(8,128)(2,1)S(1)}, u32[]{:S(2)}, u32[]{:S(2)}) collective-permute-start(bf16[2,128,160]{2,1,0:T(8,128)(2,1)S(1)} %get-tuple-element.180), channel_id=1, source_target_pairs={{0,1},{1,0},{2,3},{3,2},{4,5},{5,4},{6,7},{7,6},{8,9},{9,8},{10,11... | collective-permute-start | bytes 245768 | tf_op jit(solution)/shard_map/ppermute | solution.py:346
  112.3 3.4 %collective-permute-start.9 = (bf16[128,1280]{1,0:T(8,128)(2,1)S(1)}, bf16[128,1280]{1,0:T(8,128)(2,1)S(1)}, u32[]{:S(2)}, u32[]{:S(2)}) collective-permute-start(bf16[128,1280]{1,0:T(8,128)(2,1)S(1)} %bitcast.127), channel_id=1, source_target_pairs={{0,2},{2,0},{1,3},{3,1},{4,6},{6,4},{5,7},{7,5},{8,10},{10,8},{9,1... | collective-permute-start | bytes 983048 | tf_op jit(solution)/shard_map/ppermute | solution.py:353
  115.4 2.0 collective-permute-start.15
  127.9 3.6 %collective-permute-start.19 = (bf16[4,128,1280]{2,1,0:T(8,128)(2,1)}, bf16[4,128,1280]{2,1,0:T(8,128)(2,1)}, u32[]{:S(2)}, u32[]{:S(2)}) collective-permute-start(bf16[4,128,1280]{2,1,0:T(8,128)(2,1)} %get-tuple-element.117.pack_ref), channel_id=1, source_target_pairs={{0,2},{2,0},{1,3},{3,1},{4,6},{6,4},{5,7},{7,5},{8,10},{10,8},{9,1... | collective-permute-start | bytes 3932168 | tf_op jit(solution)/shard_map/ppermute | solution.py:353
  128.0 10.7 %collective-permute-start.20 = (bf16[2,128,160]{2,1,0:T(8,128)(2,1)S(1)}, bf16[2,128,160]{2,1,0:T(8,128)(2,1)S(1)}, u32[]{:S(2)}, u32[]{:S(2)}) collective-permute-start(bf16[2,128,160]{2,1,0:T(8,128)(2,1)S(1)} %get-tuple-element.123), channel_id=1, source_target_pairs={{0,1},{1,0},{2,3},{3,2},{4,5},{5,4},{6,7},{7,6},{8,9},{9,8},{10,11... | collective-permute-start | bytes 245768 | tf_op jit(solution)/shard_map/ppermute | solution.py:346
  128.5 10.2 %collective-permute-start.21 = (bf16[2,128,160]{2,1,0:T(8,128)(2,1)S(1)}, bf16[2,128,160]{2,1,0:T(8,128)(2,1)S(1)}, u32[]{:S(2)}, u32[]{:S(2)}) collective-permute-start(bf16[2,128,160]{2,1,0:T(8,128)(2,1)S(1)} %get-tuple-element.124), channel_id=1, source_target_pairs={{0,4},{4,0},{1,5},{5,1},{2,6},{6,2},{3,7},{7,3},{8,12},{12,8},{9,1... | collective-permute-start | bytes 245768 | tf_op jit(solution)/shard_map/ppermute | solution.py:348
  129.0 9.7 %collective-permute-start.22 = (bf16[2,128,160]{2,1,0:T(8,128)(2,1)S(1)}, bf16[2,128,160]{2,1,0:T(8,128)(2,1)S(1)}, u32[]{:S(2)}, u32[]{:S(2)}) collective-permute-start(bf16[2,128,160]{2,1,0:T(8,128)(2,1)S(1)} %get-tuple-element.125), channel_id=1, source_target_pairs={{0,5},{1,4},{4,1},{5,0},{2,7},{3,6},{6,3},{7,2},{8,13},{9,12},{12,... | collective-permute-start | bytes 245768 | tf_op jit(solution)/shard_map/ppermute | solution.py:349
  138.7 2.9 %copy-start.4 = (bf16[2,3,80,1280]{3,2,1,0:T(8,128)(2,1)}, bf16[2,3,80,1280]{3,2,1,0:T(8,128)(2,1)S(1)}, u32[]{:S(2)}) copy-start(bf16[2,3,80,1280]{3,2,1,0:T(8,128)(2,1)S(1)} %get-tuple-element.143) | copy-start | bytes 3686404
  141.7 2.0 collective-permute-start.23
  141.9 29.7 %collective-permute-start.24 = (bf16[2,3,2,40,1280]{4,3,2,1,0:T(8,128)(2,1)}, bf16[2,3,2,40,1280]{4,3,2,1,0:T(8,128)(2,1)}, u32[]{:S(2)}, u32[]{:S(2)}) collective-permute-start(bf16[2,3,2,40,1280]{4,3,2,1,0:T(8,128)(2,1)} %dynamic-slice_bitcast_fusion), channel_id=1, source_target_pairs={{0,1},{1,0},{2,3},{3,2},{4,5},{5,4},{6,7},{7,6},{8,9},{9,8},{10,11... | collective-permute-start | bytes 3686408 | tf_op jit(solution)/shard_map/ppermute | solution.py:346
  142.3 29.4 %collective-permute-start.25 = (bf16[2,3,80,1280]{3,2,1,0:T(8,128)(2,1)}, bf16[2,3,80,1280]{3,2,1,0:T(8,128)(2,1)}, u32[]{:S(2)}, u32[]{:S(2)}) collective-permute-start(bf16[2,3,80,1280]{3,2,1,0:T(8,128)(2,1)} %get-tuple-element.136), channel_id=1, source_target_pairs={{0,4},{4,0},{1,5},{5,1},{2,6},{6,2},{3,7},{7,3},{8,12},{12,8},{9,1... | collective-permute-start | bytes 3686408 | tf_op jit(solution)/shard_map/ppermute | solution.py:348
  157.2 82.9 %reduce-scatter.5.cloned.1.call-start = ((), (), s32[]{:S(2)}) async-start(), calls=%async_computation.8 | async-start | bytes 1536000 | tf_op jit(solution)/shard_map/reduce_scatter | solution.py:882
  157.3 4.5 %collective-permute-start.27 = (bf16[4,8,1280]{2,1,0:T(8,128)(2,1)S(1)}, bf16[4,8,1280]{2,1,0:T(8,128)(2,1)S(1)}, u32[]{:S(2)}, u32[]{:S(2)}) collective-permute-start(bf16[4,8,1280]{2,1,0:T(8,128)(2,1)S(1)} %get-tuple-element.185), channel_id=1, source_target_pairs={{0,24},{8,0},{16,8},{24,16},{1,25},{9,1},{17,9},{25,17},{2,26},{10... | collective-permute-start | bytes 245768 | tf_op jit(solution)/shard_map/ppermute | solution.py:357
  158.8 6.6 %collective-permute-start.26 = (bf16[4,8,1280]{2,1,0:T(8,128)(2,1)S(1)}, bf16[4,8,1280]{2,1,0:T(8,128)(2,1)S(1)}, u32[]{:S(2)}, u32[]{:S(2)}) collective-permute-start(bf16[4,8,1280]{2,1,0:T(8,128)(2,1)S(1)} %get-tuple-element.186), channel_id=1, source_target_pairs={{0,8},{8,16},{16,24},{24,0},{1,9},{9,17},{17,25},{25,1},{2,10},{10... | collective-permute-start | bytes 245768 | tf_op jit(solution)/shard_map/ppermute | solution.py:357
  171.7 27.5 %collective-permute-start.28 = (bf16[4,128,1280]{2,1,0:T(8,128)(2,1)S(1)}, bf16[4,128,1280]{2,1,0:T(8,128)(2,1)}, u32[]{:S(2)}, u32[]{:S(2)}) collective-permute-start(bf16[4,128,1280]{2,1,0:T(8,128)(2,1)S(1)} %get-tuple-element.141), channel_id=1, source_target_pairs={{0,2},{2,0},{1,3},{3,1},{4,6},{6,4},{5,7},{7,5},{8,10},{10,8},{9,1... | collective-permute-start | bytes 3932168 | tf_op jit(solution)/shard_map/ppermute | solution.py:353
  177.6 16.6 %collective-permute-start.29 = (bf16[2,3,40,1280]{3,2,1,0:T(8,128)(2,1)}, bf16[2,3,40,1280]{3,2,1,0:T(8,128)(2,1)}, u32[]{:S(2)}, u32[]{:S(2)}) collective-permute-start(bf16[2,3,40,1280]{3,2,1,0:T(8,128)(2,1)} %get-tuple-element.146), channel_id=1, source_target_pairs={{0,4},{4,0},{1,5},{5,1},{2,6},{6,2},{3,7},{7,3},{8,12},{12,8},{9,1... | collective-permute-start | bytes 1843208 | tf_op jit(solution)/shard_map/ppermute | solution.py:348
  178.1 16.3 %collective-permute-start.30 = (bf16[2,3,40,1280]{3,2,1,0:T(8,128)(2,1)}, bf16[2,3,40,1280]{3,2,1,0:T(8,128)(2,1)}, u32[]{:S(2)}, u32[]{:S(2)}) collective-permute-start(bf16[2,3,40,1280]{3,2,1,0:T(8,128)(2,1)} %get-tuple-element.148), channel_id=1, source_target_pairs={{0,1},{1,0},{2,3},{3,2},{4,5},{5,4},{6,7},{7,6},{8,9},{9,8},{10,11... | collective-permute-start | bytes 1843208 | tf_op jit(solution)/shard_map/ppermute | solution.py:346
  179.7 11.2 %collective-permute-start.31 = (bf16[4,8,1280]{2,1,0:T(8,128)(2,1)S(1)}, bf16[4,8,1280]{2,1,0:T(8,128)(2,1)S(1)}, u32[]{:S(2)}, u32[]{:S(2)}) collective-permute-start(bf16[4,8,1280]{2,1,0:T(8,128)(2,1)S(1)} %get-tuple-element.183), channel_id=1, source_target_pairs={{0,16},{8,24},{16,0},{24,8},{1,17},{9,25},{17,1},{25,9},{2,18},{10... | collective-permute-start | bytes 245768 | tf_op jit(solution)/shard_map/ppermute | solution.py:357
  194.4 1.1 copy-start.6
  195.5 1.1 copy-start.8
  201.7 17.8 %copy-start.10 = (f32[128,1280]{1,0:T(8,128)S(1)}, f32[128,1280]{1,0:T(8,128)}, u32[]{:S(2)}) copy-start(f32[128,1280]{1,0:T(8,128)} %copy-done.9) | copy-start | bytes 1966084
  201.7 10.9 %collective-permute-start.32 = (bf16[128,1280]{1,0:T(8,128)(2,1)}, bf16[128,1280]{1,0:T(8,128)(2,1)S(1)}, u32[]{:S(2)}, u32[]{:S(2)}) collective-permute-start(bf16[128,1280]{1,0:T(8,128)(2,1)} %get-tuple-element.153), channel_id=1, source_target_pairs={{0,1},{1,0},{2,3},{3,2},{4,5},{5,4},{6,7},{7,6},{8,9},{9,8},{10,11... | collective-permute-start | bytes 983048 | tf_op jit(solution)/shard_map/ppermute | solution.py:346
  203.3 16.1 %collective-permute-start.33 = (bf16[128,1280]{1,0:T(8,128)(2,1)}, bf16[128,1280]{1,0:T(8,128)(2,1)S(1)}, u32[]{:S(2)}, u32[]{:S(2)}) collective-permute-start(bf16[128,1280]{1,0:T(8,128)(2,1)} %get-tuple-element.156), channel_id=1, source_target_pairs={{0,4},{4,0},{1,5},{5,1},{2,6},{6,2},{3,7},{7,3},{8,12},{12,8},{9,1... | collective-permute-start | bytes 983048 | tf_op jit(solution)/shard_map/ppermute | solution.py:348
  204.9 14.6 %collective-permute-start.34 = (bf16[128,1280]{1,0:T(8,128)(2,1)S(1)}, bf16[128,1280]{1,0:T(8,128)(2,1)S(1)}, u32[]{:S(2)}, u32[]{:S(2)}) collective-permute-start(bf16[128,1280]{1,0:T(8,128)(2,1)S(1)} %get-tuple-element.157), channel_id=1, source_target_pairs={{0,5},{1,4},{4,1},{5,0},{2,7},{3,6},{6,3},{7,2},{8,13},{9,12},{12,... | collective-permute-start | bytes 983048 | tf_op jit(solution)/shard_map/ppermute | solution.py:349
  212.6 1.0 copy-start.3
  214.5 24.1 %all-to-all-start.2 = ((bf16[8,48,480]{2,1,0:T(8,128)(2,1)}), bf16[8,48,480]{2,1,0:T(8,128)(2,1)S(1)}, u32[]{:S(2)}, u32[]{:S(2)}) async-start(bf16[8,48,480]{2,1,0:T(8,128)(2,1)} %fold.1), calls=%async_computation.3 | async-start | bytes 786432 | tf_op jit(solution)/shard_map/all_to_all | solution.py:903
  220.5 8.1 %collective-permute-start.35 = (bf16[4,8,1280]{2,1,0:T(8,128)(2,1)S(1)}, bf16[4,8,1280]{2,1,0:T(8,128)(2,1)S(1)}, u32[]{:S(2)}, u32[]{:S(2)}) collective-permute-start(bf16[4,8,1280]{2,1,0:T(8,128)(2,1)S(1)} %get-tuple-element.159), channel_id=1, source_target_pairs={{0,24},{8,0},{16,8},{24,16},{1,25},{9,1},{17,9},{25,17},{2,26},{10... | collective-permute-start | bytes 245768 | tf_op jit(solution)/shard_map/ppermute | solution.py:357
  222.0 15.8 %collective-permute-start.36 = (bf16[4,8,1280]{2,1,0:T(8,128)(2,1)S(1)}, bf16[4,8,1280]{2,1,0:T(8,128)(2,1)S(1)}, u32[]{:S(2)}, u32[]{:S(2)}) collective-permute-start(bf16[4,8,1280]{2,1,0:T(8,128)(2,1)S(1)} %get-tuple-element.160), channel_id=1, source_target_pairs={{0,16},{8,24},{16,0},{24,8},{1,17},{9,25},{17,1},{25,9},{2,18},{10... | collective-permute-start | bytes 245768 | tf_op jit(solution)/shard_map/ppermute | solution.py:357
  223.0 14.7 %collective-permute-start.37 = (bf16[4,8,1280]{2,1,0:T(8,128)(2,1)S(1)}, bf16[4,8,1280]{2,1,0:T(8,128)(2,1)S(1)}, u32[]{:S(2)}, u32[]{:S(2)}) collective-permute-start(bf16[4,8,1280]{2,1,0:T(8,128)(2,1)S(1)} %get-tuple-element.161), channel_id=1, source_target_pairs={{0,8},{8,16},{16,24},{24,0},{1,9},{9,17},{17,25},{25,1},{2,10},{10... | collective-permute-start | bytes 245768 | tf_op jit(solution)/shard_map/ppermute | solution.py:357
  (4 other events, 3.5 us)
Sparse Core Ops, SparseCore 0:
  10.4 34.5 all-gather.2
  50.2 39.8 all-gather.4
  157.3 33.1 reduce-scatter.2
  201.8 35.4 reduce-scatter.4

commit v11 on v10

--- a/solution.py
+++ b/solution.py
@@ -572,19 +572,28 @@
 
 
 def grads_kernel(
-    info_ref, pack_ref, far_pack, atts, far_atts, cot_ref, far_cot, half_a, kept_b, away_b, stage, sems
+    info_ref, pack_ref, far_pack, atts, far_atts, cot_ref, far_cot, keep_a, away_a, keep_b, away_b, stage, sems
 ):
-    y_index, core_index = info_ref[1] // 4, (info_ref[1] // 2) % 2
+    y_index, core_index, x_index = info_ref[1] // 4, (info_ref[1] // 2) % 2, info_ref[1] % 2
 
     def leave(w):
         copies = []
         for half in range(2):
-            targets = [(half, row, half_a.at[half, w, row]) for row in range(2)]
-            targets += [(2 + half, y_index, kept_b.at[half, w]), (2 + half, 1 - y_index, away_b.at[half, w])]
-            for i, (z_index, row, target) in enumerate(targets):
-                block = pl.ds(pl.multiple_of(160 * z_index + 80 * row, 80), 80)
-                copies.append(pltpu.make_async_copy(stage.at[w, block], target, sems.at[w, 4 * half + i]))
+            for i in range(2):
+                moves = (
+                    (stage.at[w, half, i, x_index], keep_a),
+                    (stage.at[w, half, i, 1 - x_index], away_a),
+                    (stage.at[w, 2 + half, y_index, i], keep_b),
+                    (stage.at[w, 2 + half, 1 - y_index, i], away_b),
+                )
+                for j, (block, target) in enumerate(moves):
+                    sem = sems.at[w, 8 * half + 4 * i + j]
+                    copies.append(pltpu.make_async_copy(block, target.at[half, w, i], sem))
         return copies
+
+    def store(w, made):
+        for i in range(16):
+            stage[w, i // 4, (i // 2) % 2, i % 2] = made[40 * i : 40 * i + 40].astype(jnp.bfloat16)
 
     def both(near, far):
         return jnp.concatenate([near, far], axis=0)
@@ -601,11 +610,11 @@
                 ))
 
             acts = own_columns(pack_ref.at[0], far_pack.at[0])
-            stage[2] = trans_mult(acts, cots).astype(jnp.bfloat16)
+            store(2, trans_mult(acts, cots))
             for copy in leave(2):
                 copy.start()
             acts = own_columns(pack_ref.at[1], far_pack.at[1])
-            stage[1] = trans_mult(acts, both(pack_ref[2], far_pack[2])).astype(jnp.bfloat16)
+            store(1, trans_mult(acts, both(pack_ref[2], far_pack[2])))
             for copy in leave(1):
                 copy.start()
             grads = both(pack_ref[3], far_pack[3])
@@ -614,10 +623,12 @@
                 for source in range(2):
                     near, far = (far_atts, far_atts) if source else (atts, atts)
                     pieces.append(both(near[chip, source], far[chip, 1 - source])[:, 80 * core : 80 * core + 80])
-            made = trans_mult(jnp.concatenate(pieces, axis=1), grads).astype(jnp.bfloat16)
+            made = trans_mult(jnp.concatenate(pieces, axis=1), grads)
             for i in range(8):
-                place = (info_ref[1] ^ (CODES[i // 2] + 2 * (i % 2))) * 80
-                stage[0, pl.ds(pl.multiple_of(place, 80), 80), :] = made[80 * i : 80 * i + 80]
+                source = info_ref[1] ^ (CODES[i // 2] + 2 * (i % 2))
+                for part in range(2):
+                    row = 80 * i + 40 * part
+                    stage[0, source // 2, source & 1, part] = made[row : row + 40].astype(jnp.bfloat16)
             for copy in leave(0):
                 copy.start()
 
@@ -626,14 +637,14 @@
             copy.wait()
 
 
-def meet_kernel(info_ref, half_a, from_a, half_b, from_b, keep_a, away_a, keep_b, away_b):
+def meet_kernel(info_ref, mine_a, from_a, mine_b, from_b, keep_a, away_a, keep_b, away_b):
     y_index, x_index = info_ref[1] // 4, info_ref[1] % 2
     for half in range(2):
         for w in range(3):
             for row, out in ((y_index, keep_a), (1 - y_index, away_a)):
-                out[half, w] = sum_low(half_a[half, w, row, x_index], from_a[half, w, row])
+                out[half, w] = sum_low(mine_a[half, w, row], from_a[half, w, row])
             for row, out in ((x_index, keep_b), (1 - x_index, away_b)):
-                out[half, w] = sum_low(half_b[half, w, row], from_b[half, w, row])
+                out[half, w] = sum_low(mine_b[half, w, row], from_b[half, w, row])
 
 
 def join_kernel(keep_a, from_a, keep_b, from_b, out_ref):
@@ -743,7 +754,10 @@
     my_scale = lax.dynamic_slice_in_dim(vecs[2:3], 160 * plane, 160, 1)
     query_mult = LOG2E / math.sqrt(HD) * jax.nn.softplus(my_scale)
 
-    limit = pltpu.CompilerParams(vmem_limit_bytes=50 * 1024 * 1024)
+
+    def limit(megabytes):
+        return pltpu.CompilerParams(vmem_limit_bytes=megabytes * 1024 * 1024)
+
     pre, att_made = pl.pallas_call(
         attend_kernel,
         grid_spec=pltpu.PrefetchScalarGridSpec(
@@ -759,7 +773,7 @@
             jax.ShapeDtypeStruct((2, 4, 128, 480), f32),
             jax.ShapeDtypeStruct((4, 2, 128, 160), bf16),
         ],
-        compiler_params=limit,
+        compiler_params=limit(14),
         cost_estimate=pl.CostEstimate(flops=9_000_000_000, bytes_accessed=8_000_000, transcendentals=600_000),
         name="attend",
     )(info, near, far, gain_one, query_mult, w_qkv)
@@ -792,28 +806,25 @@
         + [datt_shape] * 4
         + [jax.ShapeDtypeStruct((1, width), f32)],
         scratch_shapes=[pltpu.VMEM((3, width, width), bf16), pltpu.SemaphoreType.DMA((3, 16))],
-        compiler_params=limit,
+        compiler_params=limit(28),
         cost_estimate=pl.CostEstimate(flops=12_000_000_000, bytes_accessed=13_000_000, transcendentals=200_000),
         name="feed",
     )(info, x_rows, cot_rows, atts, far_atts, gain_two, near_rows, across_a, across_b, far_near_rows, far_across_a, far_across_b)
 
     back = [datts[0]] + [plane_shift(datts[step], step) for step in (1, 2, 3)]
 
-    part_shape = jax.ShapeDtypeStruct((2, 3, 80, width), bf16)
-    half_a, kept_b, away_b = pl.pallas_call(
+    mine_a, away_a, mine_b, away_b = pl.pallas_call(
         grads_kernel,
         in_specs=[smem] + [vmem] * 6,
-        out_specs=[hbm] * 3,
-        out_shape=[jax.ShapeDtypeStruct((2, 3, 2, 80, width), bf16), part_shape, part_shape],
-        scratch_shapes=[pltpu.VMEM((3, 640, width), bf16), pltpu.SemaphoreType.DMA((3, 8))],
-        compiler_params=limit,
+        out_specs=[hbm] * 4,
+        out_shape=[jax.ShapeDtypeStruct((2, 3, 2, 40, width), bf16)] * 4,
+        scratch_shapes=[pltpu.VMEM((3, 4, 2, 2, 40, width), bf16), pltpu.SemaphoreType.DMA((3, 16))],
+        compiler_params=limit(22),
         cost_estimate=pl.CostEstimate(flops=6_000_000_000, bytes_accessed=8_000_000, transcendentals=0),
         name="grads",
     )(info, pack, core_swap(pack), atts, far_atts, cot_rows, far_cot)
 
-    half_a, kept_b, away_b, *back = lax.optimization_barrier((half_a, kept_b, away_b, *back))
-    half_a = half_a.reshape(2, 3, 2, 2, 40, width)
-    away_a = lax.dynamic_index_in_dim(half_a, 1 - x, 3, keepdims=False)
+    mine_a, away_a, mine_b, away_b, *back = lax.optimization_barrier((mine_a, away_a, mine_b, away_b, *back))
     away_a, away_b, grad_atts = lax.optimization_barrier((away_a, away_b, jnp.stack(back)))
     from_a, from_b = plane_shift(away_a, 1), plane_shift(away_b, 2)
     hid_near, hid_far, send = pl.pallas_call(
@@ -842,7 +853,7 @@
             jax.ShapeDtypeStruct((4, 128, width), bf16),
             jax.ShapeDtypeStruct((4, 336, 480), bf16),
         ],
-        compiler_params=limit,
+        compiler_params=limit(22),
         cost_estimate=pl.CostEstimate(flops=15_000_000_000, bytes_accessed=12_000_000, transcendentals=600_000),
         name="attend_back",
     )(info, near, far, gain_one, query_mult, w_qkv, pre, grad_atts, core_swap(grad_atts), gain_two_grad)
@@ -855,28 +866,28 @@
         (from_a, from_b, hid_far, out_one, out_three)
     )
     swapped = core_swap(hid_far)
+    hid = [sum_low(hid_near[i], swapped[i]) for i in range(4)]
     outputs = by_source([out_sent[0], out_one, ring_shift(out_sent[2], 2), out_three], z, 0).reshape(16, 8, width)
-    hid = [sum_low(hid_near[i], swapped[i]) for i in range(4)]
-    split = (2, 3, 2, 40, width)
     keep_a, away_a, keep_b, away_b = pl.pallas_call(
         meet_kernel,
         in_specs=[smem] + [vmem] * 4,
         out_specs=[vmem] * 4,
         out_shape=[jax.ShapeDtypeStruct((2, 3, 40, width), bf16)] * 4,
-        compiler_params=limit,
+        compiler_params=limit(18),
         cost_estimate=pl.CostEstimate(flops=3_000_000_000, bytes_accessed=8_000_000, transcendentals=0),
         name="meet",
-    )(info, half_a, from_a, kept_b.reshape(split), from_b.reshape(split))
+    )(info, mine_a, from_a, mine_b, from_b)
+    from_a, from_b = plane_shift(away_a, 2), plane_shift(away_b, 1)
+    *hid, from_a, from_b, outputs = lax.optimization_barrier((*hid, from_a, from_b, outputs))
     kept = pl.pallas_call(
         join_kernel,
         in_specs=[vmem] * 4,
         out_specs=vmem,
         out_shape=jax.ShapeDtypeStruct((4, 3, 40, width), bf16),
-        compiler_params=limit,
+        compiler_params=limit(12),
         cost_estimate=pl.CostEstimate(flops=2_000_000_000, bytes_accessed=4_000_000, transcendentals=0),
         name="join",
-    )(keep_a, plane_shift(away_a, 2), keep_b, plane_shift(away_b, 1))
-    *hid, kept, outputs = lax.optimization_barrier((*hid, kept, outputs))
+    )(keep_a, from_a, keep_b, from_b)
     moved = [plane_shift(hid[step], step) for step in (1, 2, 3)]
     moved[0], sums = lax.optimization_barrier((moved[0], sums))
     big_sums = lax.psum_scatter(kept, "z", scatter_dimension=0, tiled=True)[0]
@@ -886,7 +897,7 @@
         out_specs=[vmem] * 4,
         out_shape=[jax.ShapeDtypeStruct((4, 8, width), bf16)] * 4,
         scratch_shapes=[pltpu.VMEM((4, 4, 8, width), f32)],
-        compiler_params=limit,
+        compiler_params=limit(10),
         cost_estimate=pl.CostEstimate(flops=2_000_000_000, bytes_accessed=2_500_000, transcendentals=128),
         name="norm",
     )(info, hid[0], *moved, x_rows, grad_mid, gain_one)
@@ -896,17 +907,17 @@
         out_specs=vmem,
         out_shape=jax.ShapeDtypeStruct((8, 48, 480), bf16),
         scratch_shapes=[pltpu.VMEM((8, 480), f32)],
-        compiler_params=limit,
+        compiler_params=limit(8),
         cost_estimate=pl.CostEstimate(flops=2_000_000_000, bytes_accessed=1_600_000, transcendentals=0),
         name="fold",
     )(sums)
     sums = lax.all_to_all(sums, ("y", "core", "x"), split_axis=0, concat_axis=0, tiled=True)
     rows_shape = [jax.ShapeDtypeStruct((40, width), f32)] * 3
     qkv_sums = pl.pallas_call(
-        spread_kernel, in_specs=[vmem], out_specs=[vmem] * 3, out_shape=rows_shape, compiler_params=limit, name="spread"
+        spread_kernel, in_specs=[vmem], out_specs=[vmem] * 3, out_shape=rows_shape, compiler_params=limit(6), name="spread"
     )(sums)
     big_sums = pl.pallas_call(
-        widen_kernel, in_specs=[vmem], out_specs=[vmem] * 3, out_shape=rows_shape, compiler_params=limit, name="widen"
+        widen_kernel, in_specs=[vmem], out_specs=[vmem] * 3, out_shape=rows_shape, compiler_params=limit(6), name="widen"
     )(big_sums)
     line_sums = jnp.sum(sums[:, 40, :120].astype(f32), axis=0).reshape(3, 40)
     scale_low = query_scale.astype(bf16).astype(f32)

time: 249 us -> 249 us (level)
  local copies, waits for them, and re-layouts: 18.9 us -> 23.3 us
    unnamed x46 -> x62, local copies, waits for them, and re-layouts: 7.97 us -> 13.8 us
    squeeze x1 -> x0, local copies, waits for them, and re-layouts: 2.85 us -> none  [planes(): away_a = lax.dynamic_index_in_dim(half_a, 1 - x, 3, keepdims=False)]
  transfers between devices with their start and end apart: 45 -> 45, of which waited for: 25 -> 25; matrix products, arithmetic and copies ran while one was open for 8% -> 8% of each run, Pallas kernels for 16% -> 15%
where the time goes in v11:
time: 249 us; the launch traced here: 248 us
  waiting for transfers between devices  96.6 us (39%)
  starting transfers between devices  50 us (20%)
  Pallas kernels  49.7 us (20%)
  local copies, waits for them, and re-layouts  23.3 us (9%)
  other arithmetic  14.5 us (6%)
  between operations  14.4 us (6%)
    ppermute x8, waiting for transfers between devices, plane_shift(): return lax.ppermute(value, 'x', [(0, 1), (1, 0)])  36.1 us
    ppermute x9, waiting for transfers between devices, ring_shift(): return lax.ppermute(value, 'z', [(i, (i + step) % 4) for i in range(4)])  35.1 us
    unnamed x62, local copies, waits for them, and re-layouts  13.8 us
    ppermute x9, starting transfers between devices, ring_shift(): return lax.ppermute(value, 'z', [(i, (i + step) % 4) for i in range(4)])  13.2 us
    pallas_call x1, Pallas kernels, planes(): pl.pallas_call(attend_back_kernel, grid_spec=pltpu.PrefetchScalarGridSpec...  12.9 us
    pallas_call x1, Pallas kernels, planes(): pl.pallas_call(feed_kernel, in_specs=[smem] + [vmem] * 5 + [hbm] * 6, out...  11.3 us
    ppermute x4, waiting for transfers between devices, plane_shift(): return lax.ppermute(value, ('y', 'x'), [(0, 3), (1, 2), (2, 1), (3, 0)])  10.6 us
    ppermute x8, starting transfers between devices, plane_shift(): return lax.ppermute(value, 'x', [(0, 1), (1, 0)])  8.49 us
  transfers between devices with their start and end apart: 45, of which 25 were waited for; matrix products, arithmetic and copies ran while one was open for 8% of the time, Pallas kernels for 15%

profile of v11, /device:TPU:0, one launch (start us, length us, event | category | flops | bytes accessed | tf_op | source)
XLA Modules:
  0.0 248.3 jit_solution(16038998405090479183)
XLA Ops:
  7.3 1.1 convert_bitcast_fusion.5
  8.4 1.1 convert_bitcast_fusion.3
  10.7 5.1 %collective-permute-start = (bf16[5,8,1280]{2,1,0:T(8,128)(2,1)S(1)}, bf16[5,8,1280]{2,1,0:T(8,128)(2,1)S(1)}, u32[]{:S(2)}, u32[]{:S(2)}) collective-permute-start(bf16[5,8,1280]{2,1,0:T(8,128)(2,1)S(1)} %get-tuple-element.100), channel_id=1, source_target_pairs={{0,24},{8,0},{16,8},{24,16},{1,25},{9,1},{17,9},{25,17},{2,26},{10... | collective-permute-start | bytes 307208 | tf_op jit(solution)/shard_map/ppermute | solution.py:357
  15.8 1.0 collective-permute-start.2
  17.5 1.6 collective-permute-done
  19.1 7.4 %collective-permute-done.1 = bf16[5,8,1280]{2,1,0:T(8,128)(2,1)S(1)} collective-permute-done((bf16[5,8,1280]{2,1,0:T(8,128)(2,1)S(1)}, bf16[5,8,1280]{2,1,0:T(8,128)(2,1)S(1)}, u32[]{:S(2)}, u32[]{:S(2)}) %collective-permute-start.1) | collective-permute-done | bytes 102432 | tf_op jit(solution)/shard_map/ppermute | solution.py:357
  27.0 1.7 collective-permute-start.4
  28.7 1.5 collective-permute-start.3
  31.6 1.1 reshape.336
  32.7 3.9 %all-to-all-start = ((bf16[8,40,480]{2,1,0:T(8,128)(2,1)}), bf16[8,40,480]{2,1,0:T(8,128)(2,1)S(1)}, u32[]{:S(2)}, u32[]{:S(2)}) async-start(bf16[8,40,480]{2,1,0:T(8,128)(2,1)} %reshape.336), calls=%async_computation | async-start | bytes 655360 | tf_op jit(solution)/shard_map/all_to_all | solution.py:736
  37.2 2.5 %collective-permute-done.3 = bf16[136,1280]{1,0:T(8,128)(2,1)S(1)} collective-permute-done((bf16[136,1280]{1,0:T(8,128)(2,1)S(1)}, bf16[136,1280]{1,0:T(8,128)(2,1)S(1)}, u32[]{:S(2)}, u32[]{:S(2)}) %collective-permute-start.3) | collective-permute-done | bytes 348192 | tf_op jit(solution)/shard_map/ppermute | solution.py:346
  39.7 5.7 %collective-permute-done.5 = bf16[136,1280]{1,0:T(8,128)(2,1)S(1)} collective-permute-done((bf16[136,1280]{1,0:T(8,128)(2,1)S(1)}, bf16[136,1280]{1,0:T(8,128)(2,1)S(1)}, u32[]{:S(2)}, u32[]{:S(2)}) %collective-permute-start.5) | collective-permute-done | bytes 348192 | tf_op jit(solution)/shard_map/ppermute | solution.py:349
  45.4 1.3 pad_maximum_fusion.near_ref
  47.1 1.5 collective-permute-start.7
  48.6 1.0 collective-permute-start.8
  50.9 7.6 %all-to-all-start.1 = ((bf16[4,4,8,1280]{3,2,1,0:T(8,128)(2,1)}), bf16[4,4,8,1280]{3,2,1,0:T(8,128)(2,1)S(1)}, u32[]{:S(2)}, u32[]{:S(2)}) async-start(bf16[4,4,8,1280]{3,2,1,0:T(8,128)(2,1)} %bitcast.29), calls=%async_computation.1 | async-start | bytes 655360 | tf_op jit(solution)/shard_map/all_to_all | solution.py:743
  58.5 17.9 %collective-permute-done.7 = bf16[4,3,40,1280]{3,2,1,0:T(8,128)(2,1)S(1)} collective-permute-done((bf16[4,3,40,1280]{3,2,1,0:T(8,128)(2,1)}, bf16[4,3,40,1280]{3,2,1,0:T(8,128)(2,1)S(1)}, u32[]{:S(2)}, u32[]{:S(2)}) %collective-permute-start.7) | collective-permute-done | bytes 1228832 | tf_op jit(solution)/shard_map/ppermute | solution.py:346
  76.3 1.0 slice.174
  77.6 2.2 fusion.23
  80.5 1.2 collective-permute-start.11
  81.6 1.9 bitcast_select_fusion.near_rows
  84.8 6.1 %all-gather.5.cloned.1.call-done.w_ref = bf16[1280,480]{1,0:T(8,128)(2,1)} async-done(((bf16[320,480]{1,0:T(8,128)(2,1)}), bf16[1280,480]{1,0:T(8,128)(2,1)}) %all-gather.5.cloned.1.call-update) | async-done | bytes 1228816 | tf_op jit(solution)/shard_map/all_gather | solution.py:739
  90.9 1.3 copy-done.3
  92.2 7.5 %attend.1 = (f32[2,4,128,480]{3,2,1,0:T(8,128)S(1)}, bf16[4,2,128,160]{3,2,1,0:T(8,128)(2,1)S(1)}) custom-call(s32[6]{0:T(128)S(1)} %pad_add_fusion.info_ref, bf16[4,136,1280]{2,1,0:T(8,128)(2,1)} %pad_maximum_fusion.near_ref, bf16[4,136,1280]{2,1,0:T(8,128)(2,1)} %collective-permute-done.6.far_ref, f32[1,1280]{1,0:T(1,128)S(1)} %slice.141.gain_ref, ...), custom_call_target="tpu_custom_call" | custom-call | flops 8999999488 | bytes 8000000 | tf_op jit(solution)/shard_map/attend/pallas_call | solution.py:761
  99.7 1.3 copy-done.16
  101.1 3.2 %bitcast_select_fusion.1 = (bf16[2,3,80,1280]{3,2,1,0:T(8,128)(2,1)}, bf16[2,3,80,1280]{3,2,1,0:T(8,128)(2,1)}) fusion(pred[80]{0:T(512)(128)(4,1)S(1)} %broadcast_in_dim.383, bf16[2,3,40,1280]{3,2,1,0:T(8,128)(2,1)} %collective-permute-done.11, bf16[2,3,40,1280]{3,2,1,0:T(8,128)(2,1)} %get-tuple-element.113, ...), kind=kLoop, calls=%fused_computation.2 | loop fusion | flops 1228800 | bytes 4915280 | tf_op jit(solution)/shard_map/jit(_where)/select_n | solution.py:379
  105.4 1.5 collective-permute-start.13
  106.9 4.9 %collective-permute-done.14 = bf16[2,128,160]{2,1,0:T(8,128)(2,1)S(1)} collective-permute-done((bf16[2,128,160]{2,1,0:T(8,128)(2,1)S(1)}, bf16[2,128,160]{2,1,0:T(8,128)(2,1)S(1)}, u32[]{:S(2)}, u32[]{:S(2)}) %collective-permute-start.14) | collective-permute-done | bytes 81952 | tf_op jit(solution)/shard_map/ppermute | solution.py:349
  113.8 3.0 %collective-permute-done.12 = bf16[2,128,160]{2,1,0:T(8,128)(2,1)S(1)} collective-permute-done((bf16[2,128,160]{2,1,0:T(8,128)(2,1)S(1)}, bf16[2,128,160]{2,1,0:T(8,128)(2,1)S(1)}, u32[]{:S(2)}, u32[]{:S(2)}) %collective-permute-start.12) | collective-permute-done | bytes 81952 | tf_op jit(solution)/shard_map/ppermute | solution.py:346
  117.1 1.9 collective-permute-done.15.far_atts
  119.0 11.3 %feed.1 = (bf16[4,4,8,1280]{3,2,1,0:T(8,128)(2,1)S(1)}, bf16[4,128,1280]{2,1,0:T(8,128)(2,1)S(1)}, f32[128,1280]{1,0:T(8,128)S(1)}, bf16[2,128,160]{2,1,0:T(8,12...) custom-call(s32[6]{0:T(128)S(1)} %pad_add_fusion.info_ref, ...), custom_call_target="tpu_custom_call" | custom-call | flops 12000000000 | bytes 13000000 | tf_op jit(solution)/shard_map/feed/pallas_call | solution.py:797
  132.2 2.5 collective-permute-start.22
  134.7 8.5 %grads.1 = (bf16[2,3,2,40,1280]{4,3,2,1,0:T(8,128)(2,1)S(1)}, bf16[2,3,2,40,1280]{4,3,2,1,0:T(8,128)(2,1)}, bf16[2,3,2,40,1280]{4,3,2,1,0:T(8,128)(2,1)S(1)}, bf16[2,3,2,40,1280]{4,3,2,1,0:T(8,128)(2,1)}) custom-call(s32[6]{0:T(128)S(1)} %pad_add_fusion.info_ref, bf16[4,128,1280]{2,1,0:T(8,128)(2,1)S(1)} %get-tuple-element.120.pack_ref, ...), custom_call_target="tpu_custom_call" | custom-call | flops 6000000000 | bytes 8000000 | tf_op jit(solution)/shard_map/grads/pallas_call | solution.py:816
  143.2 1.0 copy-done.10
  144.2 1.0 copy-done.12
  147.4 12.9 %attend_back.1 = (bf16[4,128,1280]{2,1,0:T(8,128)(2,1)S(1)}, bf16[4,128,1280]{2,1,0:T(8,128)(2,1)S(1)}, bf16[4,336,480]{2,1,0:T(8,128)(2,1)}) custom-call(s32[6]{0:T(128)S(1)} %pad_add_fusion.info_ref, bf16[4,136,1280]{2,1,0:T(8,128)(2,1)} %pad_maximum_fusion.near_ref, bf16[4,136,1280]{2,1,0:T(8,128)(2,1)} %collective-permute-done.6.far_ref, ...), custom_call_target="tpu_custom_call" | custom-call | flops 15000000512 | bytes 12000000 | tf_op jit(solution)/shard_map/attend_back/pallas_call | solution.py:830
  160.4 0.9 copy-done.1
  161.3 1.5 collective-permute-start.27
  163.4 3.4 %collective-permute-done.27 = bf16[4,8,1280]{2,1,0:T(8,128)(2,1)S(1)} collective-permute-done((bf16[4,8,1280]{2,1,0:T(8,128)(2,1)S(1)}, bf16[4,8,1280]{2,1,0:T(8,128)(2,1)S(1)}, u32[]{:S(2)}, u32[]{:S(2)}) %collective-permute-start.27) | collective-permute-done | bytes 81952 | tf_op jit(solution)/shard_map/ppermute | solution.py:357
  166.8 3.3 %collective-permute-done.26 = bf16[4,8,1280]{2,1,0:T(8,128)(2,1)S(1)} collective-permute-done((bf16[4,8,1280]{2,1,0:T(8,128)(2,1)S(1)}, bf16[4,8,1280]{2,1,0:T(8,128)(2,1)S(1)}, u32[]{:S(2)}, u32[]{:S(2)}) %collective-permute-start.26) | collective-permute-done | bytes 81952 | tf_op jit(solution)/shard_map/ppermute | solution.py:357
  170.1 5.1 %collective-permute-done.24.from_a = bf16[2,3,2,40,1280]{4,3,2,1,0:T(8,128)(2,1)} collective-permute-done((bf16[2,3,2,40,1280]{4,3,2,1,0:T(8,128)(2,1)}, bf16[2,3,2,40,1280]{4,3,2,1,0:T(8,128)(2,1)}, u32[]{:S(2)}, u32[]{:S(2)}) %collective-permute-start.24) | collective-permute-done | bytes 1228832 | tf_op jit(solution)/shard_map/ppermute | solution.py:346
  175.5 1.3 copy-done.11
  176.8 1.3 copy-done.13
  178.1 3.2 %meet.1 = (bf16[2,3,40,1280]{3,2,1,0:T(8,128)(2,1)S(1)}, bf16[2,3,40,1280]{3,2,1,0:T(8,128)(2,1)}, bf16[2,3,40,1280]{3,2,1,0:T(8,128)(2,1)S(1)}, bf16[2,3,40,1280]{3,2,1,0:T(8,128)(2,1)}) custom-call(s32[6]{0:T(128)S(1)} %pad_add_fusion.info_ref, bf16[2,3,2,40,1280]{4,3,2,1,0:T(8,128)(2,1)S(1)} %copy-done.11, ...), custom_call_target="tpu_custom_call" | custom-call | flops 3000000000 | bytes 8000000 | tf_op jit(solution)/shard_map/meet/pallas_call | solution.py:871
  183.8 1.3 collective-permute-start.30
  185.1 1.5 collective-permute-start.31
  187.1 7.4 %collective-permute-done.31 = bf16[4,8,1280]{2,1,0:T(8,128)(2,1)S(1)} collective-permute-done((bf16[4,8,1280]{2,1,0:T(8,128)(2,1)S(1)}, bf16[4,8,1280]{2,1,0:T(8,128)(2,1)S(1)}, u32[]{:S(2)}, u32[]{:S(2)}) %collective-permute-start.31) | collective-permute-done | bytes 81952 | tf_op jit(solution)/shard_map/ppermute | solution.py:357
  195.3 1.7 fusion.3
  197.0 2.5 %collective-permute-done.29.from_a = bf16[2,3,40,1280]{3,2,1,0:T(8,128)(2,1)} collective-permute-done((bf16[2,3,40,1280]{3,2,1,0:T(8,128)(2,1)}, bf16[2,3,40,1280]{3,2,1,0:T(8,128)(2,1)}, u32[]{:S(2)}, u32[]{:S(2)}) %collective-permute-start.29) | collective-permute-done | bytes 614432 | tf_op jit(solution)/shard_map/ppermute | solution.py:348
  200.0 2.6 %join.1 = bf16[4,3,40,1280]{3,2,1,0:T(8,128)(2,1)} custom-call(bf16[2,3,40,1280]{3,2,1,0:T(8,128)(2,1)S(1)} %copy-done.7, bf16[2,3,40,1280]{3,2,1,0:T(8,128)(2,1)} %collective-permute-done.29.from_a, bf16[2,3,40,1280]{3,2,1,0:T(8,128)(2,1)S(1)} %copy-done.9, bf16[2,3,40,1280]{3,2,1,0:T(8,128)(2,1)} %collective-permute-done.30.from_b), custom_call_target="tpu_custom_call" | custom-call | flops 2000000000 | bytes 4000000 | tf_op jit(solution)/shard_map/join/pallas_call | solution.py:882
  202.6 1.4 collective-permute-start.32
  204.0 1.5 collective-permute-start.33
  206.2 7.2 %collective-permute-done.32.hid_1 = bf16[128,1280]{1,0:T(8,128)(2,1)S(1)} collective-permute-done((bf16[128,1280]{1,0:T(8,128)(2,1)S(1)}, bf16[128,1280]{1,0:T(8,128)(2,1)S(1)}, u32[]{:S(2)}, u32[]{:S(2)}) %collective-permute-start.32) | collective-permute-done | bytes 327712 | tf_op jit(solution)/shard_map/ppermute | solution.py:346
  213.4 1.0 copy-done.5
  215.2 3.6 %all-to-all-start.2 = ((bf16[8,48,480]{2,1,0:T(8,128)(2,1)}), bf16[8,48,480]{2,1,0:T(8,128)(2,1)S(1)}, u32[]{:S(2)}, u32[]{:S(2)}) async-start(bf16[8,48,480]{2,1,0:T(8,128)(2,1)} %fold.1), calls=%async_computation.3 | async-start | bytes 786432 | tf_op jit(solution)/shard_map/all_to_all | solution.py:914
  218.8 1.2 collective-permute-done.33.hid_2
  220.0 1.1 copy-done.15
  221.0 1.0 norm.1
  222.1 1.5 collective-permute-start.35
  223.6 1.9 collective-permute-start.37
  225.5 4.2 %collective-permute-done.35 = bf16[4,8,1280]{2,1,0:T(8,128)(2,1)S(1)} collective-permute-done((bf16[4,8,1280]{2,1,0:T(8,128)(2,1)S(1)}, bf16[4,8,1280]{2,1,0:T(8,128)(2,1)S(1)}, u32[]{:S(2)}, u32[]{:S(2)}) %collective-permute-start.35) | collective-permute-done | bytes 81952 | tf_op jit(solution)/shard_map/ppermute | solution.py:357
  229.8 7.8 %collective-permute-done.36 = bf16[4,8,1280]{2,1,0:T(8,128)(2,1)S(1)} collective-permute-done((bf16[4,8,1280]{2,1,0:T(8,128)(2,1)S(1)}, bf16[4,8,1280]{2,1,0:T(8,128)(2,1)S(1)}, u32[]{:S(2)}, u32[]{:S(2)}) %collective-permute-start.36) | collective-permute-done | bytes 81952 | tf_op jit(solution)/shard_map/ppermute | solution.py:357
  238.4 0.9 spread.1
  240.0 1.0 copy-done.2
  (179 shorter events, 24.6 us)
Async XLA Ops:
  7.2 3.1 %copy-start.28 = (f32[40]{0:T(128)S(1)}, f32[40]{0:T(128)}, u32[]{:S(2)}) copy-start(f32[40]{0:T(128)} %param.23) | copy-start | bytes 484
  7.2 3.1 %copy-start.23 = (f32[40,1280]{1,0:T(8,128)S(1)}, f32[40,1280]{1,0:T(8,128)}, u32[]{:S(2)}) copy-start(f32[40,1280]{1,0:T(8,128)} %param.17) | copy-start | bytes 614404
  7.2 3.2 %copy-start.26 = (f32[40]{0:T(128)S(1)}, f32[40]{0:T(128)}, u32[]{:S(2)}) copy-start(f32[40]{0:T(128)} %param.25) | copy-start | bytes 484
  7.2 3.2 %copy-start.27 = (f32[40]{0:T(128)S(1)}, f32[40]{0:T(128)}, u32[]{:S(2)}) copy-start(f32[40]{0:T(128)} %param.24) | copy-start | bytes 484
  7.2 3.2 %copy-start.24 = (f32[40,1280]{1,0:T(8,128)S(1)}, f32[40,1280]{1,0:T(8,128)}, u32[]{:S(2)}) copy-start(f32[40,1280]{1,0:T(8,128)} %param.19) | copy-start | bytes 614404
  7.2 3.2 %copy-start.25 = (f32[40,1280]{1,0:T(8,128)S(1)}, f32[40,1280]{1,0:T(8,128)}, u32[]{:S(2)}) copy-start(f32[40,1280]{1,0:T(8,128)} %param.18) | copy-start | bytes 614404
  7.2 39.9 %all-gather.3.cloned.1.call-start = ((), (), s32[]{:S(2)}) async-start(), calls=%async_computation.5 | async-start | bytes 1536000 | tf_op jit(solution)/shard_map/all_gather | solution.py:733
  10.7 8.4 %collective-permute-start = (bf16[5,8,1280]{2,1,0:T(8,128)(2,1)S(1)}, bf16[5,8,1280]{2,1,0:T(8,128)(2,1)S(1)}, u32[]{:S(2)}, u32[]{:S(2)}) collective-permute-start(bf16[5,8,1280]{2,1,0:T(8,128)(2,1)S(1)} %get-tuple-element.100), channel_id=1, source_target_pairs={{0,24},{8,0},{16,8},{24,16},{1,25},{9,1},{17,9},{25,17},{2,26},{10... | collective-permute-start | bytes 307208 | tf_op jit(solution)/shard_map/ppermute | solution.py:357
  15.8 10.7 %collective-permute-start.1 = (bf16[5,8,1280]{2,1,0:T(8,128)(2,1)S(1)}, bf16[5,8,1280]{2,1,0:T(8,128)(2,1)S(1)}, u32[]{:S(2)}, u32[]{:S(2)}) collective-permute-start(bf16[5,8,1280]{2,1,0:T(8,128)(2,1)S(1)} %get-tuple-element.101), channel_id=1, source_target_pairs={{0,16},{8,24},{16,0},{24,8},{1,17},{9,25},{17,1},{25,9},{2,18},{10... | collective-permute-start | bytes 307208 | tf_op jit(solution)/shard_map/ppermute | solution.py:357
  15.8 10.7 %collective-permute-start.2 = (bf16[5,8,1280]{2,1,0:T(8,128)(2,1)S(1)}, bf16[5,8,1280]{2,1,0:T(8,128)(2,1)S(1)}, u32[]{:S(2)}, u32[]{:S(2)}) collective-permute-start(bf16[5,8,1280]{2,1,0:T(8,128)(2,1)S(1)} %get-tuple-element.102), channel_id=1, source_target_pairs={{0,8},{8,16},{16,24},{24,0},{1,9},{9,17},{17,25},{25,1},{2,10},{10... | collective-permute-start | bytes 307208 | tf_op jit(solution)/shard_map/ppermute | solution.py:357
  27.0 10.2 %collective-permute-start.4 = (bf16[136,1280]{1,0:T(8,128)(2,1)S(1)}, bf16[136,1280]{1,0:T(8,128)(2,1)S(1)}, u32[]{:S(2)}, u32[]{:S(2)}) collective-permute-start(bf16[136,1280]{1,0:T(8,128)(2,1)S(1)} %get-tuple-element.188), channel_id=1, source_target_pairs={{0,4},{4,0},{1,5},{5,1},{2,6},{6,2},{3,7},{7,3},{8,12},{12,8},{9,1... | collective-permute-start | bytes 1044488 | tf_op jit(solution)/shard_map/ppermute | solution.py:348
  28.7 11.1 %collective-permute-start.3 = (bf16[136,1280]{1,0:T(8,128)(2,1)S(1)}, bf16[136,1280]{1,0:T(8,128)(2,1)S(1)}, u32[]{:S(2)}, u32[]{:S(2)}) collective-permute-start(bf16[136,1280]{1,0:T(8,128)(2,1)S(1)} %get-tuple-element.188), channel_id=1, source_target_pairs={{0,1},{1,0},{2,3},{3,2},{4,5},{5,4},{6,7},{7,6},{8,9},{9,8},{10,11... | collective-permute-start | bytes 1044488 | tf_op jit(solution)/shard_map/ppermute | solution.py:346
  30.2 15.2 %collective-permute-start.5 = (bf16[136,1280]{1,0:T(8,128)(2,1)S(1)}, bf16[136,1280]{1,0:T(8,128)(2,1)S(1)}, u32[]{:S(2)}, u32[]{:S(2)}) collective-permute-start(bf16[136,1280]{1,0:T(8,128)(2,1)S(1)} %get-tuple-element.188), channel_id=1, source_target_pairs={{0,5},{1,4},{4,1},{5,0},{2,7},{3,6},{6,3},{7,2},{8,13},{9,12},{12,... | collective-permute-start | bytes 1044488 | tf_op jit(solution)/shard_map/ppermute | solution.py:349
  32.7 14.4 %all-to-all-start = ((bf16[8,40,480]{2,1,0:T(8,128)(2,1)}), bf16[8,40,480]{2,1,0:T(8,128)(2,1)S(1)}, u32[]{:S(2)}, u32[]{:S(2)}) async-start(bf16[8,40,480]{2,1,0:T(8,128)(2,1)} %reshape.336), calls=%async_computation | async-start | bytes 655360 | tf_op jit(solution)/shard_map/all_to_all | solution.py:736
  36.5 54.4 %all-gather.5.cloned.1.call-start = ((), (), s32[]{:S(2)}) async-start(), calls=%async_computation.6 | async-start | bytes 1638400 | tf_op jit(solution)/shard_map/all_gather | solution.py:739
  45.4 4.5 %copy-start.29 = (s32[16]{0:T(128)S(1)}, s32[16]{0:T(128)}, u32[]{:S(2)}) copy-start(s32[16]{0:T(128)} %param.27) | copy-start | bytes 196
  45.4 4.5 %copy-start.30 = (s32[16]{0:T(128)S(1)}, s32[16]{0:T(128)}, u32[]{:S(2)}) copy-start(s32[16]{0:T(128)} %param.26) | copy-start | bytes 196
  47.1 2.8 %copy-start.19 = (bf16[8,40,480]{2,1,0:T(8,128)(2,1)}, bf16[8,40,480]{2,1,0:T(8,128)(2,1)S(1)}, u32[]{:S(2)}) copy-start(bf16[8,40,480]{2,1,0:T(8,128)(2,1)S(1)} %all-to-all-done) | copy-start | bytes 921604
  47.1 29.3 %collective-permute-start.7 = (bf16[4,3,40,1280]{3,2,1,0:T(8,128)(2,1)}, bf16[4,3,40,1280]{3,2,1,0:T(8,128)(2,1)S(1)}, u32[]{:S(2)}, u32[]{:S(2)}) collective-permute-start(bf16[4,3,40,1280]{3,2,1,0:T(8,128)(2,1)} %all-gather.3.cloned.1.call-done), channel_id=1, source_target_pairs={{0,1},{1,0},{2,3},{3,2},{4,5},{5,4},{6,7},{7,6},{8,9},{9,8},{10,11... | collective-permute-start | bytes 3686408 | tf_op jit(solution)/shard_map/ppermute | solution.py:346
  48.6 28.9 %collective-permute-start.8 = (bf16[4,3,40,1280]{3,2,1,0:T(8,128)(2,1)}, bf16[4,3,40,1280]{3,2,1,0:T(8,128)(2,1)}, u32[]{:S(2)}, u32[]{:S(2)}) collective-permute-start(bf16[4,3,40,1280]{3,2,1,0:T(8,128)(2,1)} %all-gather.3.cloned.1.call-done), channel_id=1, source_target_pairs={{0,4},{4,0},{1,5},{5,1},{2,6},{6,2},{3,7},{7,3},{8,12},{12,8},{9,1... | collective-permute-start | bytes 3686408 | tf_op jit(solution)/shard_map/ppermute | solution.py:348
  49.7 33.8 %collective-permute-start.6 = (bf16[4,136,1280]{2,1,0:T(8,128)(2,1)}, bf16[4,136,1280]{2,1,0:T(8,128)(2,1)}, u32[]{:S(2)}, u32[]{:S(2)}) collective-permute-start(bf16[4,136,1280]{2,1,0:T(8,128)(2,1)} %pad_maximum_fusion.near_ref), channel_id=1, source_target_pairs={{0,2},{2,0},{1,3},{3,1},{4,6},{6,4},{5,7},{7,5},{8,10},{10,8},{9,1... | collective-permute-start | bytes 4177928 | tf_op jit(solution)/shard_map/ppermute | solution.py:353
  50.9 28.8 %all-to-all-start.1 = ((bf16[4,4,8,1280]{3,2,1,0:T(8,128)(2,1)}), bf16[4,4,8,1280]{3,2,1,0:T(8,128)(2,1)S(1)}, u32[]{:S(2)}, u32[]{:S(2)}) async-start(bf16[4,4,8,1280]{3,2,1,0:T(8,128)(2,1)} %bitcast.29), calls=%async_computation.1 | async-start | bytes 655360 | tf_op jit(solution)/shard_map/all_to_all | solution.py:743
  58.5 154.9 %reduce-scatter.3.cloned.1.call-start = ((), (), s32[]{:S(2)}) async-start(), calls=%async_computation.7 | async-start | bytes 1720320 | tf_op jit(solution)/shard_map/reduce_scatter | solution.py:862
  76.3 3.4 %copy-start.18 = (bf16[4,3,40,1280]{3,2,1,0:T(8,128)(2,1)}, bf16[4,3,40,1280]{3,2,1,0:T(8,128)(2,1)S(1)}, u32[]{:S(2)}) copy-start(bf16[4,3,40,1280]{3,2,1,0:T(8,128)(2,1)S(1)} %collective-permute-done.7) | copy-start | bytes 3686404
  79.8 21.3 %collective-permute-start.10 = (bf16[2,3,40,1280]{3,2,1,0:T(8,128)(2,1)}, bf16[2,3,40,1280]{3,2,1,0:T(8,128)(2,1)}, u32[]{:S(2)}, u32[]{:S(2)}) collective-permute-start(bf16[2,3,40,1280]{3,2,1,0:T(8,128)(2,1)} %slice.174), channel_id=1, source_target_pairs={{0,4},{4,0},{1,5},{5,1},{2,6},{6,2},{3,7},{7,3},{8,12},{12,8},{9,1... | collective-permute-start | bytes 1843208 | tf_op jit(solution)/shard_map/ppermute | solution.py:348
  80.5 20.5 %collective-permute-start.11 = (bf16[2,3,40,1280]{3,2,1,0:T(8,128)(2,1)}, bf16[2,3,40,1280]{3,2,1,0:T(8,128)(2,1)}, u32[]{:S(2)}, u32[]{:S(2)}) collective-permute-start(bf16[2,3,40,1280]{3,2,1,0:T(8,128)(2,1)} %get-tuple-element.113), channel_id=1, source_target_pairs={{0,1},{1,0},{2,3},{3,2},{4,5},{5,4},{6,7},{7,6},{8,9},{9,8},{10,11... | collective-permute-start | bytes 1843208 | tf_op jit(solution)/shard_map/ppermute | solution.py:346
  90.9 1.3 copy-start.3
  99.7 1.3 copy-start.16
  101.0 18.0 %collective-permute-start.16 = (bf16[4,3,80,1280]{3,2,1,0:T(8,128)(2,1)S(1)}, bf16[4,3,80,1280]{3,2,1,0:T(8,128)(2,1)}, u32[]{:S(2)}, u32[]{:S(2)}) collective-permute-start(bf16[4,3,80,1280]{3,2,1,0:T(8,128)(2,1)S(1)} %bitcast_select_fusion.near_rows), channel_id=1, source_target_pairs={{0,2},{2,0},{1,3},{3,1},{4,6},{6,4},{5,7},{7,5},{8,10},{10,8},{9,1... | collective-permute-start | bytes 7372808 | tf_op jit(solution)/shard_map/ppermute | solution.py:353
  101.1 11.2 %copy-start.21 = (bf16[4,4,8,1280]{3,2,1,0:T(8,128)(2,1)S(1)}, bf16[4,4,8,1280]{3,2,1,0:T(8,128)(2,1)}, u32[]{:S(2)}) copy-start(bf16[4,4,8,1280]{3,2,1,0:T(8,128)(2,1)} %copy-done.20) | copy-start | bytes 983044
  104.3 14.7 %collective-permute-start.18 = (bf16[2,3,80,1280]{3,2,1,0:T(8,128)(2,1)}, bf16[2,3,80,1280]{3,2,1,0:T(8,128)(2,1)}, u32[]{:S(2)}, u32[]{:S(2)}) collective-permute-start(bf16[2,3,80,1280]{3,2,1,0:T(8,128)(2,1)} %get-tuple-element.207.across_b), channel_id=1, source_target_pairs={{0,2},{2,0},{1,3},{3,1},{4,6},{6,4},{5,7},{7,5},{8,10},{10,8},{9,1... | collective-permute-start | bytes 3686408 | tf_op jit(solution)/shard_map/ppermute | solution.py:353
  104.8 14.3 %collective-permute-start.17 = (bf16[2,3,80,1280]{3,2,1,0:T(8,128)(2,1)}, bf16[2,3,80,1280]{3,2,1,0:T(8,128)(2,1)}, u32[]{:S(2)}, u32[]{:S(2)}) collective-permute-start(bf16[2,3,80,1280]{3,2,1,0:T(8,128)(2,1)} %get-tuple-element.208.across_a), channel_id=1, source_target_pairs={{0,2},{2,0},{1,3},{3,1},{4,6},{6,4},{5,7},{7,5},{8,10},{10,8},{9,1... | collective-permute-start | bytes 3686408 | tf_op jit(solution)/shard_map/ppermute | solution.py:353
  104.9 6.9 %collective-permute-start.14 = (bf16[2,128,160]{2,1,0:T(8,128)(2,1)S(1)}, bf16[2,128,160]{2,1,0:T(8,128)(2,1)S(1)}, u32[]{:S(2)}, u32[]{:S(2)}) collective-permute-start(bf16[2,128,160]{2,1,0:T(8,128)(2,1)S(1)} %get-tuple-element.184), channel_id=1, source_target_pairs={{0,5},{1,4},{4,1},{5,0},{2,7},{3,6},{6,3},{7,2},{8,13},{9,12},{12,... | collective-permute-start | bytes 245768 | tf_op jit(solution)/shard_map/ppermute | solution.py:349
  105.4 8.4 %collective-permute-start.13 = (bf16[2,128,160]{2,1,0:T(8,128)(2,1)S(1)}, bf16[2,128,160]{2,1,0:T(8,128)(2,1)S(1)}, u32[]{:S(2)}, u32[]{:S(2)}) collective-permute-start(bf16[2,128,160]{2,1,0:T(8,128)(2,1)S(1)} %get-tuple-element.185), channel_id=1, source_target_pairs={{0,4},{4,0},{1,5},{5,1},{2,6},{6,2},{3,7},{7,3},{8,12},{12,8},{9,1... | collective-permute-start | bytes 245768 | tf_op jit(solution)/shard_map/ppermute | solution.py:348
  111.8 5.0 %collective-permute-start.12 = (bf16[2,128,160]{2,1,0:T(8,128)(2,1)S(1)}, bf16[2,128,160]{2,1,0:T(8,128)(2,1)S(1)}, u32[]{:S(2)}, u32[]{:S(2)}) collective-permute-start(bf16[2,128,160]{2,1,0:T(8,128)(2,1)S(1)} %get-tuple-element.186), channel_id=1, source_target_pairs={{0,1},{1,0},{2,3},{3,2},{4,5},{5,4},{6,7},{7,6},{8,9},{9,8},{10,11... | collective-permute-start | bytes 245768 | tf_op jit(solution)/shard_map/ppermute | solution.py:346
  113.8 3.3 %collective-permute-start.9 = (bf16[128,1280]{1,0:T(8,128)(2,1)}, bf16[128,1280]{1,0:T(8,128)(2,1)}, u32[]{:S(2)}, u32[]{:S(2)}) collective-permute-start(bf16[128,1280]{1,0:T(8,128)(2,1)} %bitcast.31.g_ref.cot_ref), channel_id=1, source_target_pairs={{0,2},{2,0},{1,3},{3,1},{4,6},{6,4},{5,7},{7,5},{8,10},{10,8},{9,1... | collective-permute-start | bytes 983048 | tf_op jit(solution)/shard_map/ppermute | solution.py:353
  116.9 2.1 collective-permute-start.15
  131.0 12.2 %copy-start.14 = (f32[128,1280]{1,0:T(8,128)}, f32[128,1280]{1,0:T(8,128)S(1)}, u32[]{:S(2)}) copy-start(f32[128,1280]{1,0:T(8,128)S(1)} %get-tuple-element.161.dmid_ref) | copy-start | bytes 1966084
  131.0 3.7 %collective-permute-start.19 = (bf16[4,128,1280]{2,1,0:T(8,128)(2,1)S(1)}, bf16[4,128,1280]{2,1,0:T(8,128)(2,1)S(1)}, u32[]{:S(2)}, u32[]{:S(2)}) collective-permute-start(bf16[4,128,1280]{2,1,0:T(8,128)(2,1)S(1)} %get-tuple-element.120.pack_ref), channel_id=1, source_target_pairs={{0,2},{2,0},{1,3},{3,1},{4,6},{6,4},{5,7},{7,5},{8,10},{10,8},{9,1... | collective-permute-start | bytes 3932168 | tf_op jit(solution)/shard_map/ppermute | solution.py:353
  131.2 14.1 %collective-permute-start.20 = (bf16[2,128,160]{2,1,0:T(8,128)(2,1)S(1)}, bf16[2,128,160]{2,1,0:T(8,128)(2,1)S(1)}, u32[]{:S(2)}, u32[]{:S(2)}) collective-permute-start(bf16[2,128,160]{2,1,0:T(8,128)(2,1)S(1)} %get-tuple-element.127), channel_id=1, source_target_pairs={{0,1},{1,0},{2,3},{3,2},{4,5},{5,4},{6,7},{7,6},{8,9},{9,8},{10,11... | collective-permute-start | bytes 245768 | tf_op jit(solution)/shard_map/ppermute | solution.py:346
  131.7 13.6 %collective-permute-start.21 = (bf16[2,128,160]{2,1,0:T(8,128)(2,1)S(1)}, bf16[2,128,160]{2,1,0:T(8,128)(2,1)S(1)}, u32[]{:S(2)}, u32[]{:S(2)}) collective-permute-start(bf16[2,128,160]{2,1,0:T(8,128)(2,1)S(1)} %get-tuple-element.128), channel_id=1, source_target_pairs={{0,4},{4,0},{1,5},{5,1},{2,6},{6,2},{3,7},{7,3},{8,12},{12,8},{9,1... | collective-permute-start | bytes 245768 | tf_op jit(solution)/shard_map/ppermute | solution.py:348
  132.2 15.2 %copy-start.4 = (bf16[1280,480]{1,0:T(8,128)(2,1)S(1)}, bf16[1280,480]{1,0:T(8,128)(2,1)}, u32[]{:S(2)}) copy-start(bf16[1280,480]{1,0:T(8,128)(2,1)} %all-gather.5.cloned.1.call-done.w_ref) | copy-start | bytes 3686404
  132.2 15.2 %copy-start.17 = (f32[2,4,128,480]{3,2,1,0:T(8,128)S(1)}, f32[2,4,128,480]{3,2,1,0:T(8,128)}, u32[]{:S(2)}) copy-start(f32[2,4,128,480]{3,2,1,0:T(8,128)} %copy-done.16) | copy-start | bytes 5898244
  132.2 13.0 %collective-permute-start.22 = (bf16[2,128,160]{2,1,0:T(8,128)(2,1)S(1)}, bf16[2,128,160]{2,1,0:T(8,128)(2,1)S(1)}, u32[]{:S(2)}, u32[]{:S(2)}) collective-permute-start(bf16[2,128,160]{2,1,0:T(8,128)(2,1)S(1)} %get-tuple-element.129), channel_id=1, source_target_pairs={{0,5},{1,4},{4,1},{5,0},{2,7},{3,6},{6,3},{7,2},{8,13},{9,12},{12,... | collective-permute-start | bytes 245768 | tf_op jit(solution)/shard_map/ppermute | solution.py:349
  145.4 2.0 collective-permute-start.23
  145.5 29.8 %collective-permute-start.24 = (bf16[2,3,2,40,1280]{4,3,2,1,0:T(8,128)(2,1)}, bf16[2,3,2,40,1280]{4,3,2,1,0:T(8,128)(2,1)}, u32[]{:S(2)}, u32[]{:S(2)}) collective-permute-start(bf16[2,3,2,40,1280]{4,3,2,1,0:T(8,128)(2,1)} %get-tuple-element.139), channel_id=1, source_target_pairs={{0,1},{1,0},{2,3},{3,2},{4,5},{5,4},{6,7},{7,6},{8,9},{9,8},{10,11... | collective-permute-start | bytes 3686408 | tf_op jit(solution)/shard_map/ppermute | solution.py:346
  146.0 29.4 %collective-permute-start.25 = (bf16[2,3,2,40,1280]{4,3,2,1,0:T(8,128)(2,1)}, bf16[2,3,2,40,1280]{4,3,2,1,0:T(8,128)(2,1)}, u32[]{:S(2)}, u32[]{:S(2)}) collective-permute-start(bf16[2,3,2,40,1280]{4,3,2,1,0:T(8,128)(2,1)} %get-tuple-element.140), channel_id=1, source_target_pairs={{0,4},{4,0},{1,5},{5,1},{2,6},{6,2},{3,7},{7,3},{8,12},{12,8},{9,1... | collective-permute-start | bytes 3686408 | tf_op jit(solution)/shard_map/ppermute | solution.py:348
  160.3 79.6 %reduce-scatter.5.cloned.1.call-start = ((), (), s32[]{:S(2)}) async-start(), calls=%async_computation.8 | async-start | bytes 1536000 | tf_op jit(solution)/shard_map/reduce_scatter | solution.py:893
  161.3 5.5 %collective-permute-start.27 = (bf16[4,8,1280]{2,1,0:T(8,128)(2,1)S(1)}, bf16[4,8,1280]{2,1,0:T(8,128)(2,1)S(1)}, u32[]{:S(2)}, u32[]{:S(2)}) collective-permute-start(bf16[4,8,1280]{2,1,0:T(8,128)(2,1)S(1)} %get-tuple-element.191), channel_id=1, source_target_pairs={{0,24},{8,0},{16,8},{24,16},{1,25},{9,1},{17,9},{25,17},{2,26},{10... | collective-permute-start | bytes 245768 | tf_op jit(solution)/shard_map/ppermute | solution.py:357
  162.8 7.3 %collective-permute-start.26 = (bf16[4,8,1280]{2,1,0:T(8,128)(2,1)S(1)}, bf16[4,8,1280]{2,1,0:T(8,128)(2,1)S(1)}, u32[]{:S(2)}, u32[]{:S(2)}) collective-permute-start(bf16[4,8,1280]{2,1,0:T(8,128)(2,1)S(1)} %get-tuple-element.192), channel_id=1, source_target_pairs={{0,8},{8,16},{16,24},{24,0},{1,9},{9,17},{17,25},{25,1},{2,10},{10... | collective-permute-start | bytes 245768 | tf_op jit(solution)/shard_map/ppermute | solution.py:357
  175.5 19.9 %collective-permute-start.28 = (bf16[4,128,1280]{2,1,0:T(8,128)(2,1)S(1)}, bf16[4,128,1280]{2,1,0:T(8,128)(2,1)}, u32[]{:S(2)}, u32[]{:S(2)}) collective-permute-start(bf16[4,128,1280]{2,1,0:T(8,128)(2,1)S(1)} %get-tuple-element.145), channel_id=1, source_target_pairs={{0,2},{2,0},{1,3},{3,1},{4,6},{6,4},{5,7},{7,5},{8,10},{10,8},{9,1... | collective-permute-start | bytes 3932168 | tf_op jit(solution)/shard_map/ppermute | solution.py:353
  176.7 1.3 copy-start.13
  183.0 16.5 %collective-permute-start.29 = (bf16[2,3,40,1280]{3,2,1,0:T(8,128)(2,1)}, bf16[2,3,40,1280]{3,2,1,0:T(8,128)(2,1)}, u32[]{:S(2)}, u32[]{:S(2)}) collective-permute-start(bf16[2,3,40,1280]{3,2,1,0:T(8,128)(2,1)} %get-tuple-element.150), channel_id=1, source_target_pairs={{0,4},{4,0},{1,5},{5,1},{2,6},{6,2},{3,7},{7,3},{8,12},{12,8},{9,1... | collective-permute-start | bytes 1843208 | tf_op jit(solution)/shard_map/ppermute | solution.py:348
  183.8 16.3 %collective-permute-start.30 = (bf16[2,3,40,1280]{3,2,1,0:T(8,128)(2,1)}, bf16[2,3,40,1280]{3,2,1,0:T(8,128)(2,1)}, u32[]{:S(2)}, u32[]{:S(2)}) collective-permute-start(bf16[2,3,40,1280]{3,2,1,0:T(8,128)(2,1)} %get-tuple-element.151), channel_id=1, source_target_pairs={{0,1},{1,0},{2,3},{3,2},{4,5},{5,4},{6,7},{7,6},{8,9},{9,8},{10,11... | collective-permute-start | bytes 1843208 | tf_op jit(solution)/shard_map/ppermute | solution.py:346
  185.1 9.4 %collective-permute-start.31 = (bf16[4,8,1280]{2,1,0:T(8,128)(2,1)S(1)}, bf16[4,8,1280]{2,1,0:T(8,128)(2,1)S(1)}, u32[]{:S(2)}, u32[]{:S(2)}) collective-permute-start(bf16[4,8,1280]{2,1,0:T(8,128)(2,1)S(1)} %get-tuple-element.189), channel_id=1, source_target_pairs={{0,16},{8,24},{16,0},{24,8},{1,17},{9,25},{17,1},{25,9},{2,18},{10... | collective-permute-start | bytes 245768 | tf_op jit(solution)/shard_map/ppermute | solution.py:357
  195.3 4.7 %copy-start.7 = (bf16[2,3,40,1280]{3,2,1,0:T(8,128)(2,1)S(1)}, bf16[2,3,40,1280]{3,2,1,0:T(8,128)(2,1)}, u32[]{:S(2)}) copy-start(bf16[2,3,40,1280]{3,2,1,0:T(8,128)(2,1)} %copy-done.6) | copy-start | bytes 1843204
  195.3 4.7 %copy-start.9 = (bf16[2,3,40,1280]{3,2,1,0:T(8,128)(2,1)S(1)}, bf16[2,3,40,1280]{3,2,1,0:T(8,128)(2,1)}, u32[]{:S(2)}) copy-start(bf16[2,3,40,1280]{3,2,1,0:T(8,128)(2,1)} %copy-done.8) | copy-start | bytes 1843204
  202.6 10.7 %collective-permute-start.32 = (bf16[128,1280]{1,0:T(8,128)(2,1)S(1)}, bf16[128,1280]{1,0:T(8,128)(2,1)S(1)}, u32[]{:S(2)}, u32[]{:S(2)}) collective-permute-start(bf16[128,1280]{1,0:T(8,128)(2,1)S(1)} %get-tuple-element.156), channel_id=1, source_target_pairs={{0,1},{1,0},{2,3},{3,2},{4,5},{5,4},{6,7},{7,6},{8,9},{9,8},{10,11... | collective-permute-start | bytes 983048 | tf_op jit(solution)/shard_map/ppermute | solution.py:346
  204.0 15.9 %collective-permute-start.33 = (bf16[128,1280]{1,0:T(8,128)(2,1)S(1)}, bf16[128,1280]{1,0:T(8,128)(2,1)S(1)}, u32[]{:S(2)}, u32[]{:S(2)}) collective-permute-start(bf16[128,1280]{1,0:T(8,128)(2,1)S(1)} %get-tuple-element.159), channel_id=1, source_target_pairs={{0,4},{4,0},{1,5},{5,1},{2,6},{6,2},{3,7},{7,3},{8,12},{12,8},{9,1... | collective-permute-start | bytes 983048 | tf_op jit(solution)/shard_map/ppermute | solution.py:348
  205.6 14.4 %collective-permute-start.34 = (bf16[128,1280]{1,0:T(8,128)(2,1)S(1)}, bf16[128,1280]{1,0:T(8,128)(2,1)S(1)}, u32[]{:S(2)}, u32[]{:S(2)}) collective-permute-start(bf16[128,1280]{1,0:T(8,128)(2,1)S(1)} %get-tuple-element.160), channel_id=1, source_target_pairs={{0,5},{1,4},{4,1},{5,0},{2,7},{3,6},{6,3},{7,2},{8,13},{9,12},{12,... | collective-permute-start | bytes 983048 | tf_op jit(solution)/shard_map/ppermute | solution.py:349
  215.2 23.2 %all-to-all-start.2 = ((bf16[8,48,480]{2,1,0:T(8,128)(2,1)}), bf16[8,48,480]{2,1,0:T(8,128)(2,1)S(1)}, u32[]{:S(2)}, u32[]{:S(2)}) async-start(bf16[8,48,480]{2,1,0:T(8,128)(2,1)} %fold.1), calls=%async_computation.3 | async-start | bytes 786432 | tf_op jit(solution)/shard_map/all_to_all | solution.py:914
  222.1 7.7 %collective-permute-start.35 = (bf16[4,8,1280]{2,1,0:T(8,128)(2,1)S(1)}, bf16[4,8,1280]{2,1,0:T(8,128)(2,1)S(1)}, u32[]{:S(2)}, u32[]{:S(2)}) collective-permute-start(bf16[4,8,1280]{2,1,0:T(8,128)(2,1)S(1)} %get-tuple-element.162), channel_id=1, source_target_pairs={{0,24},{8,0},{16,8},{24,16},{1,25},{9,1},{17,9},{25,17},{2,26},{10... | collective-permute-start | bytes 245768 | tf_op jit(solution)/shard_map/ppermute | solution.py:357
  223.5 14.0 %collective-permute-start.36 = (bf16[4,8,1280]{2,1,0:T(8,128)(2,1)S(1)}, bf16[4,8,1280]{2,1,0:T(8,128)(2,1)S(1)}, u32[]{:S(2)}, u32[]{:S(2)}) collective-permute-start(bf16[4,8,1280]{2,1,0:T(8,128)(2,1)S(1)} %get-tuple-element.163), channel_id=1, source_target_pairs={{0,16},{8,24},{16,0},{24,8},{1,17},{9,25},{17,1},{25,9},{2,18},{10... | collective-permute-start | bytes 245768 | tf_op jit(solution)/shard_map/ppermute | solution.py:357
  223.6 14.0 %collective-permute-start.37 = (bf16[4,8,1280]{2,1,0:T(8,128)(2,1)S(1)}, bf16[4,8,1280]{2,1,0:T(8,128)(2,1)S(1)}, u32[]{:S(2)}, u32[]{:S(2)}) collective-permute-start(bf16[4,8,1280]{2,1,0:T(8,128)(2,1)S(1)} %get-tuple-element.164), channel_id=1, source_target_pairs={{0,8},{8,16},{16,24},{24,0},{1,9},{9,17},{17,25},{25,1},{2,10},{10... | collective-permute-start | bytes 245768 | tf_op jit(solution)/shard_map/ppermute | solution.py:357
  (12 other events, 11.7 us)
Sparse Core Ops, SparseCore 0:
  10.4 34.5 all-gather.2
  50.0 40.8 all-gather.4
  160.5 32.6 reduce-scatter.2
  202.8 33.9 reduce-scatter.4

commit v12 on v11

--- a/solution.py
+++ b/solution.py
@@ -580,16 +580,18 @@
         copies = []
         for half in range(2):
             for i in range(2):
-                moves = (
-                    (stage.at[w, half, i, x_index], keep_a),
-                    (stage.at[w, half, i, 1 - x_index], away_a),
-                    (stage.at[w, 2 + half, y_index, i], keep_b),
-                    (stage.at[w, 2 + half, 1 - y_index, i], away_b),
-                )
+                moves = ((stage.at[w, half, i, 1 - x_index], away_a), (stage.at[w, 2 + half, 1 - y_index, i], away_b))
                 for j, (block, target) in enumerate(moves):
-                    sem = sems.at[w, 8 * half + 4 * i + j]
+                    sem = sems.at[w, 4 * half + 2 * i + j]
                     copies.append(pltpu.make_async_copy(block, target.at[half, w, i], sem))
         return copies
+
+    def keep():
+        for half in range(2):
+            for w in range(3):
+                for i in range(2):
+                    keep_a[half, w, i] = stage[w, half, i, x_index]
+                    keep_b[half, w, i] = stage[w, 2 + half, y_index, i]
 
     def store(w, made):
         for i in range(16):
@@ -632,6 +634,7 @@
             for copy in leave(0):
                 copy.start()
 
+    keep()
     for w in range(3):
         for copy in leave(w):
             copy.wait()
@@ -735,13 +738,12 @@
     qkv = qkv.reshape(3, 40, 8, 160).transpose(2, 1, 0, 3).reshape(8, 40, 480)
     qkv = lax.all_to_all(qkv, ("y", "core", "x"), split_axis=0, concat_axis=0, tiled=True)
     near = jnp.stack([own] + [plane_shift(own, step) for step in (1, 2, 3)])
-    big, near, cotangent, qkv = lax.optimization_barrier((big, near, cotangent, qkv.reshape(320, 480)))
+    big, near, qkv = lax.optimization_barrier((big, near, qkv.reshape(320, 480)))
     w_qkv = lax.all_gather(qkv, "z", axis=0, tiled=True)
     far = core_swap(near)
     beside, across = plane_shift(big, 1), plane_shift(big, 2)
     relay_a, relay_b = beside[:2], across[2:]
-    cot_rows = lax.all_to_all(cotangent.reshape(4, 4, 8, width), "z", split_axis=0, concat_axis=0, tiled=True)
-    relay_a, relay_b, cot_rows = lax.optimization_barrier((relay_a, relay_b, cot_rows))
+    relay_a, relay_b = lax.optimization_barrier((relay_a, relay_b))
     across_a, across_b = plane_shift(relay_a, 2), plane_shift(relay_b, 1)
 
     vecs = jnp.stack([near[:, 128:132, :120], far[:, 128:132, :120]])
@@ -753,6 +755,8 @@
     gain_one, gain_two = vecs[0:1], vecs[1:2]
     my_scale = lax.dynamic_slice_in_dim(vecs[2:3], 160 * plane, 160, 1)
     query_mult = LOG2E / math.sqrt(HD) * jax.nn.softplus(my_scale)
+    query_mult, cotangent = lax.optimization_barrier((query_mult, cotangent))
+    cot_rows = lax.all_to_all(cotangent.reshape(4, 4, 8, width), "z", split_axis=0, concat_axis=0, tiled=True)
 
 
     def limit(megabytes):
@@ -779,7 +783,9 @@
     )(info, near, far, gain_one, query_mult, w_qkv)
 
     near_rows = pair(big, beside, x, 2).reshape(4, 3, 80, width)
-    att_made, near_rows, across_a, across_b = lax.optimization_barrier((att_made, near_rows, across_a, across_b))
+    att_made, near_rows, across_a, across_b, cot_rows = lax.optimization_barrier(
+        (att_made, near_rows, across_a, across_b, cot_rows)
+    )
     far_near_rows = core_swap(near_rows)
     atts = [att_made[0]] + [plane_shift(att_made[step], step) for step in (1, 2, 3)]
     atts = jnp.stack(atts)
@@ -793,7 +799,7 @@
     datt_shape = jax.ShapeDtypeStruct((2, 128, 160), bf16)
     smem = pl.BlockSpec(memory_space=pltpu.SMEM)
     vmem = pl.BlockSpec(memory_space=pltpu.VMEM)
-    hbm = pl.BlockSpec(memory_space=pl.ANY)
+    hbm = pl.BlockSpec(memory_space=pltpu.HBM)
     out_rows, pack, grad_mid, *datts, gain_two_grad = pl.pallas_call(
         feed_kernel,
         in_specs=[smem] + [vmem] * 5 + [hbm] * 6,
@@ -816,9 +822,9 @@
     mine_a, away_a, mine_b, away_b = pl.pallas_call(
         grads_kernel,
         in_specs=[smem] + [vmem] * 6,
-        out_specs=[hbm] * 4,
+        out_specs=[vmem, hbm, vmem, hbm],
         out_shape=[jax.ShapeDtypeStruct((2, 3, 2, 40, width), bf16)] * 4,
-        scratch_shapes=[pltpu.VMEM((3, 4, 2, 2, 40, width), bf16), pltpu.SemaphoreType.DMA((3, 16))],
+        scratch_shapes=[pltpu.VMEM((3, 4, 2, 2, 40, width), bf16), pltpu.SemaphoreType.DMA((3, 8))],
         compiler_params=limit(22),
         cost_estimate=pl.CostEstimate(flops=6_000_000_000, bytes_accessed=8_000_000, transcendentals=0),
         name="grads",

time: 249 us -> 248 us (level)
  starting transfers between devices: 50 us -> 56.1 us
  Pallas kernels: 49.7 us -> 45.5 us
  waiting for transfers between devices: 96.6 us -> 92.8 us
    all_gather x1, waiting for transfers between devices: 6.08 us -> 0.02 us  [planes(): w_qkv = lax.all_gather(qkv, 'z', axis=0, tiled=True)]
    ppermute x9, starting transfers between devices: 13.2 us -> 18 us  [ring_shift(): return lax.ppermute(value, 'z', [(i, (i + step) % 4) for i in range(4)])]
    pallas_call x1, Pallas kernels: 8.49 us -> 4.37 us  [planes(): pl.pallas_call(grads_kernel, in_specs=[smem] + [vmem] * 6, out_specs=[vme...]
    ppermute x8, waiting for transfers between devices: 36.1 us -> 39.9 us  [plane_shift(): return lax.ppermute(value, 'x', [(0, 1), (1, 0)])]
    ppermute x8, waiting for transfers between devices: 5.62 us -> 2.88 us  [plane_shift(): return lax.ppermute(value, 'y', [(0, 1), (1, 0)])]
    unnamed x62 -> x60, local copies, waits for them, and re-layouts: 13.8 us -> 13.7 us
  transfers between devices with their start and end apart: 45 -> 45, of which waited for: 25 -> 22; matrix products, arithmetic and copies ran while one was open for 8% -> 9% of each run, Pallas kernels for 15% -> 14%
where the time goes in v12:
time: 248 us; the launch traced here: 247 us
  waiting for transfers between devices  92.8 us (37%)
  starting transfers between devices  56.1 us (23%)
  Pallas kernels  45.5 us (18%)
  local copies, waits for them, and re-layouts  23.1 us (9%)
  other arithmetic  15.3 us (6%)
  between operations  14.4 us (6%)
    ppermute x8, waiting for transfers between devices, plane_shift(): return lax.ppermute(value, 'x', [(0, 1), (1, 0)])  39.9 us
    ppermute x9, waiting for transfers between devices, ring_shift(): return lax.ppermute(value, 'z', [(i, (i + step) % 4) for i in range(4)])  37.3 us
    ppermute x9, starting transfers between devices, ring_shift(): return lax.ppermute(value, 'z', [(i, (i + step) % 4) for i in range(4)])  18 us
    unnamed x60, local copies, waits for them, and re-layouts  13.7 us
    pallas_call x1, Pallas kernels, planes(): pl.pallas_call(attend_back_kernel, grid_spec=pltpu.PrefetchScalarGridSpec...  12.9 us
    pallas_call x1, Pallas kernels, planes(): pl.pallas_call(feed_kernel, in_specs=[smem] + [vmem] * 5 + [hbm] * 6, out...  11.3 us
    ppermute x4, waiting for transfers between devices, plane_shift(): return lax.ppermute(value, ('y', 'x'), [(0, 3), (1, 2), (2, 1), (3, 0)])  10.4 us
    ppermute x8, starting transfers between devices, plane_shift(): return lax.ppermute(value, 'y', [(0, 1), (1, 0)])  9.06 us
  transfers between devices with their start and end apart: 45, of which 22 were waited for; matrix products, arithmetic and copies ran while one was open for 9% of the time, Pallas kernels for 14%

profile of v12, /device:TPU:0, one launch (start us, length us, event | category | flops | bytes accessed | tf_op | source)
XLA Modules:
  0.0 247.3 jit_solution(11318488641511194806)
XLA Ops:
  7.3 1.1 convert_bitcast_fusion.5
  8.4 1.1 convert_bitcast_fusion.3
  10.7 5.1 %collective-permute-start = (bf16[5,8,1280]{2,1,0:T(8,128)(2,1)S(1)}, bf16[5,8,1280]{2,1,0:T(8,128)(2,1)S(1)}, u32[]{:S(2)}, u32[]{:S(2)}) collective-permute-start(bf16[5,8,1280]{2,1,0:T(8,128)(2,1)S(1)} %get-tuple-element.101), channel_id=1, source_target_pairs={{0,24},{8,0},{16,8},{24,16},{1,25},{9,1},{17,9},{25,17},{2,26},{10... | collective-permute-start | bytes 307208 | tf_op jit(solution)/shard_map/ppermute | solution.py:357
  15.8 1.0 collective-permute-start.2
  17.5 1.6 collective-permute-done
  19.1 7.4 %collective-permute-done.1 = bf16[5,8,1280]{2,1,0:T(8,128)(2,1)S(1)} collective-permute-done((bf16[5,8,1280]{2,1,0:T(8,128)(2,1)S(1)}, bf16[5,8,1280]{2,1,0:T(8,128)(2,1)S(1)}, u32[]{:S(2)}, u32[]{:S(2)}) %collective-permute-start.1) | collective-permute-done | bytes 102432 | tf_op jit(solution)/shard_map/ppermute | solution.py:357
  27.0 1.7 collective-permute-start.4
  28.6 1.5 collective-permute-start.3
  31.6 1.1 reshape.336
  32.6 3.9 %all-to-all-start = ((bf16[8,40,480]{2,1,0:T(8,128)(2,1)}), bf16[8,40,480]{2,1,0:T(8,128)(2,1)S(1)}, u32[]{:S(2)}, u32[]{:S(2)}) async-start(bf16[8,40,480]{2,1,0:T(8,128)(2,1)} %reshape.336), calls=%async_computation | async-start | bytes 655360 | tf_op jit(solution)/shard_map/all_to_all | solution.py:739
  37.2 2.5 %collective-permute-done.3 = bf16[136,1280]{1,0:T(8,128)(2,1)S(1)} collective-permute-done((bf16[136,1280]{1,0:T(8,128)(2,1)S(1)}, bf16[136,1280]{1,0:T(8,128)(2,1)S(1)}, u32[]{:S(2)}, u32[]{:S(2)}) %collective-permute-start.3) | collective-permute-done | bytes 348192 | tf_op jit(solution)/shard_map/ppermute | solution.py:346
  39.7 5.8 %collective-permute-done.5 = bf16[136,1280]{1,0:T(8,128)(2,1)} collective-permute-done((bf16[136,1280]{1,0:T(8,128)(2,1)S(1)}, bf16[136,1280]{1,0:T(8,128)(2,1)}, u32[]{:S(2)}, u32[]{:S(2)}) %collective-permute-start.5) | collective-permute-done | bytes 348192 | tf_op jit(solution)/shard_map/ppermute | solution.py:349
  45.5 2.3 pad_maximum_fusion.near_ref
  47.8 1.5 collective-permute-start.7
  49.3 1.5 collective-permute-start.8
  52.0 24.3 %collective-permute-done.7 = bf16[4,3,40,1280]{3,2,1,0:T(8,128)(2,1)S(1)} collective-permute-done((bf16[4,3,40,1280]{3,2,1,0:T(8,128)(2,1)}, bf16[4,3,40,1280]{3,2,1,0:T(8,128)(2,1)S(1)}, u32[]{:S(2)}, u32[]{:S(2)}) %collective-permute-start.7) | collective-permute-done | bytes 1228832 | tf_op jit(solution)/shard_map/ppermute | solution.py:346
  76.3 1.0 slice.174
  77.4 1.1 fusion.23
  79.3 1.0 collective-permute-start.10
  80.3 1.6 bitcast_select_fusion.near_rows
  83.1 8.1 %all-to-all-start.1 = ((bf16[4,4,8,1280]{3,2,1,0:T(8,128)(2,1)}), bf16[4,4,8,1280]{3,2,1,0:T(8,128)(2,1)}, u32[]{:S(2)}, u32[]{:S(2)}) async-start(bf16[4,4,8,1280]{3,2,1,0:T(8,128)(2,1)} %bitcast.31), calls=%async_computation.1 | async-start | bytes 655360 | tf_op jit(solution)/shard_map/all_to_all | solution.py:759
  91.3 1.3 copy-done.3
  92.6 7.5 %attend.1 = (f32[2,4,128,480]{3,2,1,0:T(8,128)S(1)}, bf16[4,2,128,160]{3,2,1,0:T(8,128)(2,1)S(1)}) custom-call(s32[6]{0:T(128)S(1)} %pad_add_fusion.info_ref, bf16[4,136,1280]{2,1,0:T(8,128)(2,1)} %pad_maximum_fusion.near_ref, bf16[4,136,1280]{2,1,0:T(8,128)(2,1)} %collective-permute-done.6.far_ref, f32[1,1280]{1,0:T(1,128)S(1)} %slice.141.gain_ref, ...), custom_call_target="tpu_custom_call" | custom-call | flops 8999999488 | bytes 8000000 | tf_op jit(solution)/shard_map/attend/pallas_call | solution.py:765
  100.2 1.3 copy-done.16
  101.6 3.3 %bitcast_select_fusion.1 = (bf16[2,3,80,1280]{3,2,1,0:T(8,128)(2,1)}, bf16[2,3,80,1280]{3,2,1,0:T(8,128)(2,1)}) fusion(pred[80]{0:T(512)(128)(4,1)S(1)} %broadcast_in_dim.383, bf16[2,3,40,1280]{3,2,1,0:T(8,128)(2,1)} %collective-permute-done.10, bf16[2,3,40,1280]{3,2,1,0:T(8,128)(2,1)} %get-tuple-element.113, ...), kind=kLoop, calls=%fused_computation.2 | loop fusion | flops 1228800 | bytes 4915280 | tf_op jit(solution)/shard_map/jit(_where)/select_n | solution.py:379
  106.3 1.5 collective-permute-start.13
  107.7 4.7 %collective-permute-done.14 = bf16[2,128,160]{2,1,0:T(8,128)(2,1)S(1)} collective-permute-done((bf16[2,128,160]{2,1,0:T(8,128)(2,1)S(1)}, bf16[2,128,160]{2,1,0:T(8,128)(2,1)S(1)}, u32[]{:S(2)}, u32[]{:S(2)}) %collective-permute-start.14) | collective-permute-done | bytes 81952 | tf_op jit(solution)/shard_map/ppermute | solution.py:349
  113.2 1.7 copy.39
  114.9 2.6 %collective-permute-done.12 = bf16[2,128,160]{2,1,0:T(8,128)(2,1)S(1)} collective-permute-done((bf16[2,128,160]{2,1,0:T(8,128)(2,1)S(1)}, bf16[2,128,160]{2,1,0:T(8,128)(2,1)S(1)}, u32[]{:S(2)}, u32[]{:S(2)}) %collective-permute-start.12) | collective-permute-done | bytes 81952 | tf_op jit(solution)/shard_map/ppermute | solution.py:346
  117.8 1.9 collective-permute-done.15.far_atts
  119.7 11.3 %feed.1 = (bf16[4,4,8,1280]{3,2,1,0:T(8,128)(2,1)S(1)}, bf16[4,128,1280]{2,1,0:T(8,128)(2,1)S(1)}, f32[128,1280]{1,0:T(8,128)S(1)}, bf16[2,128,160]{2,1,0:T(8,12...) custom-call(s32[6]{0:T(128)S(1)} %pad_add_fusion.info_ref, ...), custom_call_target="tpu_custom_call" | custom-call | flops 12000000000 | bytes 13000000 | tf_op jit(solution)/shard_map/feed/pallas_call | solution.py:803
  133.2 2.2 collective-permute-start.22
  135.4 4.4 %grads.1 = (bf16[2,3,2,40,1280]{4,3,2,1,0:T(8,128)(2,1)S(1)}, bf16[2,3,2,40,1280]{4,3,2,1,0:T(8,128)(2,1)}, bf16[2,3,2,40,1280]{4,3,2,1,0:T(8,128)(2,1)S(1)}, bf16[2,3,2,40,1280]{4,3,2,1,0:T(8,128)(2,1)}) custom-call(s32[6]{0:T(128)S(1)} %pad_add_fusion.info_ref, bf16[4,128,1280]{2,1,0:T(8,128)(2,1)S(1)} %get-tuple-element.122.pack_ref, ...), custom_call_target="tpu_custom_call" | custom-call | flops 6000000000 | bytes 8000000 | tf_op jit(solution)/shard_map/grads/pallas_call | solution.py:822
  139.8 1.0 copy-done.10
  140.8 1.0 copy-done.12
  144.0 12.9 %attend_back.1 = (bf16[4,128,1280]{2,1,0:T(8,128)(2,1)S(1)}, bf16[4,128,1280]{2,1,0:T(8,128)(2,1)S(1)}, bf16[4,336,480]{2,1,0:T(8,128)(2,1)}) custom-call(s32[6]{0:T(128)S(1)} %pad_add_fusion.info_ref, bf16[4,136,1280]{2,1,0:T(8,128)(2,1)} %pad_maximum_fusion.near_ref, bf16[4,136,1280]{2,1,0:T(8,128)(2,1)} %collective-permute-done.6.far_ref, ...), custom_call_target="tpu_custom_call" | custom-call | flops 15000000512 | bytes 12000000 | tf_op jit(solution)/shard_map/attend_back/pallas_call | solution.py:836
  157.0 0.9 copy-done.1
  157.9 3.9 %collective-permute-start.27 = (bf16[4,8,1280]{2,1,0:T(8,128)(2,1)S(1)}, bf16[4,8,1280]{2,1,0:T(8,128)(2,1)S(1)}, u32[]{:S(2)}, u32[]{:S(2)}) collective-permute-start(bf16[4,8,1280]{2,1,0:T(8,128)(2,1)S(1)} %get-tuple-element.193), channel_id=1, source_target_pairs={{0,24},{8,0},{16,8},{24,16},{1,25},{9,1},{17,9},{25,17},{2,26},{10... | collective-permute-start | bytes 245768 | tf_op jit(solution)/shard_map/ppermute | solution.py:357
  161.8 4.0 %collective-permute-done.27 = bf16[4,8,1280]{2,1,0:T(8,128)(2,1)S(1)} collective-permute-done((bf16[4,8,1280]{2,1,0:T(8,128)(2,1)S(1)}, bf16[4,8,1280]{2,1,0:T(8,128)(2,1)S(1)}, u32[]{:S(2)}, u32[]{:S(2)}) %collective-permute-start.27) | collective-permute-done | bytes 81952 | tf_op jit(solution)/shard_map/ppermute | solution.py:357
  165.7 3.3 %collective-permute-done.26 = bf16[4,8,1280]{2,1,0:T(8,128)(2,1)S(1)} collective-permute-done((bf16[4,8,1280]{2,1,0:T(8,128)(2,1)S(1)}, bf16[4,8,1280]{2,1,0:T(8,128)(2,1)S(1)}, u32[]{:S(2)}, u32[]{:S(2)}) %collective-permute-start.26) | collective-permute-done | bytes 81952 | tf_op jit(solution)/shard_map/ppermute | solution.py:357
  169.0 2.8 %collective-permute-done.24.from_a = bf16[2,3,2,40,1280]{4,3,2,1,0:T(8,128)(2,1)} collective-permute-done((bf16[2,3,2,40,1280]{4,3,2,1,0:T(8,128)(2,1)}, bf16[2,3,2,40,1280]{4,3,2,1,0:T(8,128)(2,1)}, u32[]{:S(2)}, u32[]{:S(2)}) %collective-permute-start.24) | collective-permute-done | bytes 1228832 | tf_op jit(solution)/shard_map/ppermute | solution.py:346
  172.3 1.3 copy-done.11
  173.6 1.3 copy-done.13
  174.9 3.2 %meet.1 = (bf16[2,3,40,1280]{3,2,1,0:T(8,128)(2,1)S(1)}, bf16[2,3,40,1280]{3,2,1,0:T(8,128)(2,1)}, bf16[2,3,40,1280]{3,2,1,0:T(8,128)(2,1)S(1)}, bf16[2,3,40,1280]{3,2,1,0:T(8,128)(2,1)}) custom-call(s32[6]{0:T(128)S(1)} %pad_add_fusion.info_ref, bf16[2,3,2,40,1280]{4,3,2,1,0:T(8,128)(2,1)S(1)} %copy-done.11, ...), custom_call_target="tpu_custom_call" | custom-call | flops 3000000000 | bytes 8000000 | tf_op jit(solution)/shard_map/meet/pallas_call | solution.py:877
  178.1 0.9 copy-done.6
  180.7 0.9 collective-permute-start.30
  181.5 2.9 %collective-permute-start.31 = (bf16[4,8,1280]{2,1,0:T(8,128)(2,1)S(1)}, bf16[4,8,1280]{2,1,0:T(8,128)(2,1)S(1)}, u32[]{:S(2)}, u32[]{:S(2)}) collective-permute-start(bf16[4,8,1280]{2,1,0:T(8,128)(2,1)S(1)} %get-tuple-element.191), channel_id=1, source_target_pairs={{0,16},{8,24},{16,0},{24,8},{1,17},{9,25},{17,1},{25,9},{2,18},{10... | collective-permute-start | bytes 245768 | tf_op jit(solution)/shard_map/ppermute | solution.py:357
  185.0 8.1 %collective-permute-done.31 = bf16[4,8,1280]{2,1,0:T(8,128)(2,1)S(1)} collective-permute-done((bf16[4,8,1280]{2,1,0:T(8,128)(2,1)S(1)}, bf16[4,8,1280]{2,1,0:T(8,128)(2,1)S(1)}, u32[]{:S(2)}, u32[]{:S(2)}) %collective-permute-start.31) | collective-permute-done | bytes 81952 | tf_op jit(solution)/shard_map/ppermute | solution.py:357
  193.9 1.7 fusion.3
  197.0 2.6 %join.1 = bf16[4,3,40,1280]{3,2,1,0:T(8,128)(2,1)} custom-call(bf16[2,3,40,1280]{3,2,1,0:T(8,128)(2,1)S(1)} %copy-done.7, bf16[2,3,40,1280]{3,2,1,0:T(8,128)(2,1)} %collective-permute-done.29.from_a, bf16[2,3,40,1280]{3,2,1,0:T(8,128)(2,1)S(1)} %copy-done.9, bf16[2,3,40,1280]{3,2,1,0:T(8,128)(2,1)} %collective-permute-done.30.from_b), custom_call_target="tpu_custom_call" | custom-call | flops 2000000000 | bytes 4000000 | tf_op jit(solution)/shard_map/join/pallas_call | solution.py:888
  199.6 1.0 collective-permute-start.32
  200.6 1.5 collective-permute-start.33
  202.1 1.0 collective-permute-start.34
  203.2 7.2 %collective-permute-done.32.hid_1 = bf16[128,1280]{1,0:T(8,128)(2,1)S(1)} collective-permute-done((bf16[128,1280]{1,0:T(8,128)(2,1)S(1)}, bf16[128,1280]{1,0:T(8,128)(2,1)S(1)}, u32[]{:S(2)}, u32[]{:S(2)}) %collective-permute-start.32) | collective-permute-done | bytes 327712 | tf_op jit(solution)/shard_map/ppermute | solution.py:346
  210.3 1.0 copy-done.5
  212.2 3.5 %all-to-all-start.2 = ((bf16[8,48,480]{2,1,0:T(8,128)(2,1)}), bf16[8,48,480]{2,1,0:T(8,128)(2,1)S(1)}, u32[]{:S(2)}, u32[]{:S(2)}) async-start(bf16[8,48,480]{2,1,0:T(8,128)(2,1)} %fold.1), calls=%async_computation.3 | async-start | bytes 786432 | tf_op jit(solution)/shard_map/all_to_all | solution.py:920
  216.4 1.1 copy-done.15
  217.5 1.0 norm.1
  218.5 3.9 %collective-permute-start.35 = (bf16[4,8,1280]{2,1,0:T(8,128)(2,1)S(1)}, bf16[4,8,1280]{2,1,0:T(8,128)(2,1)S(1)}, u32[]{:S(2)}, u32[]{:S(2)}) collective-permute-start(bf16[4,8,1280]{2,1,0:T(8,128)(2,1)S(1)} %get-tuple-element.164), channel_id=1, source_target_pairs={{0,24},{8,0},{16,8},{24,16},{1,25},{9,1},{17,9},{25,17},{2,26},{10... | collective-permute-start | bytes 245768 | tf_op jit(solution)/shard_map/ppermute | solution.py:357
  222.4 1.1 collective-permute-start.37
  223.6 3.6 %collective-permute-done.35 = bf16[4,8,1280]{2,1,0:T(8,128)(2,1)S(1)} collective-permute-done((bf16[4,8,1280]{2,1,0:T(8,128)(2,1)S(1)}, bf16[4,8,1280]{2,1,0:T(8,128)(2,1)S(1)}, u32[]{:S(2)}, u32[]{:S(2)}) %collective-permute-start.35) | collective-permute-done | bytes 81952 | tf_op jit(solution)/shard_map/ppermute | solution.py:357
  227.2 9.4 %collective-permute-done.36 = bf16[4,8,1280]{2,1,0:T(8,128)(2,1)S(1)} collective-permute-done((bf16[4,8,1280]{2,1,0:T(8,128)(2,1)S(1)}, bf16[4,8,1280]{2,1,0:T(8,128)(2,1)S(1)}, u32[]{:S(2)}, u32[]{:S(2)}) %collective-permute-start.36) | collective-permute-done | bytes 81952 | tf_op jit(solution)/shard_map/ppermute | solution.py:357
  237.4 0.9 spread.1
  238.9 1.0 copy-done.2
  (177 shorter events, 23.2 us)
Async XLA Ops:
  7.2 3.1 %copy-start.27 = (f32[40]{0:T(128)S(1)}, f32[40]{0:T(128)}, u32[]{:S(2)}) copy-start(f32[40]{0:T(128)} %param.23) | copy-start | bytes 484
  7.2 3.1 %copy-start.22 = (f32[40,1280]{1,0:T(8,128)S(1)}, f32[40,1280]{1,0:T(8,128)}, u32[]{:S(2)}) copy-start(f32[40,1280]{1,0:T(8,128)} %param.17) | copy-start | bytes 614404
  7.2 3.2 %copy-start.25 = (f32[40]{0:T(128)S(1)}, f32[40]{0:T(128)}, u32[]{:S(2)}) copy-start(f32[40]{0:T(128)} %param.25) | copy-start | bytes 484
  7.2 3.2 %copy-start.26 = (f32[40]{0:T(128)S(1)}, f32[40]{0:T(128)}, u32[]{:S(2)}) copy-start(f32[40]{0:T(128)} %param.24) | copy-start | bytes 484
  7.2 3.2 %copy-start.23 = (f32[40,1280]{1,0:T(8,128)S(1)}, f32[40,1280]{1,0:T(8,128)}, u32[]{:S(2)}) copy-start(f32[40,1280]{1,0:T(8,128)} %param.19) | copy-start | bytes 614404
  7.2 3.2 %copy-start.24 = (f32[40,1280]{1,0:T(8,128)S(1)}, f32[40,1280]{1,0:T(8,128)}, u32[]{:S(2)}) copy-start(f32[40,1280]{1,0:T(8,128)} %param.18) | copy-start | bytes 614404
  7.2 40.5 %all-gather.3.cloned.1.call-start = ((), (), s32[]{:S(2)}) async-start(), calls=%async_computation.5 | async-start | bytes 1536000 | tf_op jit(solution)/shard_map/all_gather | solution.py:736
  10.7 8.4 %collective-permute-start = (bf16[5,8,1280]{2,1,0:T(8,128)(2,1)S(1)}, bf16[5,8,1280]{2,1,0:T(8,128)(2,1)S(1)}, u32[]{:S(2)}, u32[]{:S(2)}) collective-permute-start(bf16[5,8,1280]{2,1,0:T(8,128)(2,1)S(1)} %get-tuple-element.101), channel_id=1, source_target_pairs={{0,24},{8,0},{16,8},{24,16},{1,25},{9,1},{17,9},{25,17},{2,26},{10... | collective-permute-start | bytes 307208 | tf_op jit(solution)/shard_map/ppermute | solution.py:357
  15.8 10.7 %collective-permute-start.1 = (bf16[5,8,1280]{2,1,0:T(8,128)(2,1)S(1)}, bf16[5,8,1280]{2,1,0:T(8,128)(2,1)S(1)}, u32[]{:S(2)}, u32[]{:S(2)}) collective-permute-start(bf16[5,8,1280]{2,1,0:T(8,128)(2,1)S(1)} %get-tuple-element.102), channel_id=1, source_target_pairs={{0,16},{8,24},{16,0},{24,8},{1,17},{9,25},{17,1},{25,9},{2,18},{10... | collective-permute-start | bytes 307208 | tf_op jit(solution)/shard_map/ppermute | solution.py:357
  15.8 10.7 %collective-permute-start.2 = (bf16[5,8,1280]{2,1,0:T(8,128)(2,1)S(1)}, bf16[5,8,1280]{2,1,0:T(8,128)(2,1)S(1)}, u32[]{:S(2)}, u32[]{:S(2)}) collective-permute-start(bf16[5,8,1280]{2,1,0:T(8,128)(2,1)S(1)} %get-tuple-element.103), channel_id=1, source_target_pairs={{0,8},{8,16},{16,24},{24,0},{1,9},{9,17},{17,25},{25,1},{2,10},{10... | collective-permute-start | bytes 307208 | tf_op jit(solution)/shard_map/ppermute | solution.py:357
  27.0 10.2 %collective-permute-start.4 = (bf16[136,1280]{1,0:T(8,128)(2,1)S(1)}, bf16[136,1280]{1,0:T(8,128)(2,1)S(1)}, u32[]{:S(2)}, u32[]{:S(2)}) collective-permute-start(bf16[136,1280]{1,0:T(8,128)(2,1)S(1)} %get-tuple-element.190), channel_id=1, source_target_pairs={{0,4},{4,0},{1,5},{5,1},{2,6},{6,2},{3,7},{7,3},{8,12},{12,8},{9,1... | collective-permute-start | bytes 1044488 | tf_op jit(solution)/shard_map/ppermute | solution.py:348
  28.6 11.1 %collective-permute-start.3 = (bf16[136,1280]{1,0:T(8,128)(2,1)S(1)}, bf16[136,1280]{1,0:T(8,128)(2,1)S(1)}, u32[]{:S(2)}, u32[]{:S(2)}) collective-permute-start(bf16[136,1280]{1,0:T(8,128)(2,1)S(1)} %get-tuple-element.190), channel_id=1, source_target_pairs={{0,1},{1,0},{2,3},{3,2},{4,5},{5,4},{6,7},{7,6},{8,9},{9,8},{10,11... | collective-permute-start | bytes 1044488 | tf_op jit(solution)/shard_map/ppermute | solution.py:346
  30.2 15.3 %collective-permute-start.5 = (bf16[136,1280]{1,0:T(8,128)(2,1)S(1)}, bf16[136,1280]{1,0:T(8,128)(2,1)}, u32[]{:S(2)}, u32[]{:S(2)}) collective-permute-start(bf16[136,1280]{1,0:T(8,128)(2,1)S(1)} %get-tuple-element.190), channel_id=1, source_target_pairs={{0,5},{1,4},{4,1},{5,0},{2,7},{3,6},{6,3},{7,2},{8,13},{9,12},{12,... | collective-permute-start | bytes 1044488 | tf_op jit(solution)/shard_map/ppermute | solution.py:349
  32.6 15.1 %all-to-all-start = ((bf16[8,40,480]{2,1,0:T(8,128)(2,1)}), bf16[8,40,480]{2,1,0:T(8,128)(2,1)S(1)}, u32[]{:S(2)}, u32[]{:S(2)}) async-start(bf16[8,40,480]{2,1,0:T(8,128)(2,1)} %reshape.336), calls=%async_computation | async-start | bytes 655360 | tf_op jit(solution)/shard_map/all_to_all | solution.py:739
  36.5 54.8 %all-gather.5.cloned.1.call-start = ((), (), s32[]{:S(2)}) async-start(), calls=%async_computation.6 | async-start | bytes 1638400 | tf_op jit(solution)/shard_map/all_gather | solution.py:742
  45.5 5.5 %copy-start.28 = (s32[16]{0:T(128)S(1)}, s32[16]{0:T(128)}, u32[]{:S(2)}) copy-start(s32[16]{0:T(128)} %param.27) | copy-start | bytes 196
  45.5 5.6 %copy-start.29 = (s32[16]{0:T(128)S(1)}, s32[16]{0:T(128)}, u32[]{:S(2)}) copy-start(s32[16]{0:T(128)} %param.26) | copy-start | bytes 196
  47.8 3.2 %copy-start.19 = (bf16[8,40,480]{2,1,0:T(8,128)(2,1)}, bf16[8,40,480]{2,1,0:T(8,128)(2,1)S(1)}, u32[]{:S(2)}) copy-start(bf16[8,40,480]{2,1,0:T(8,128)(2,1)S(1)} %all-to-all-done) | copy-start | bytes 921604
  47.8 28.6 %collective-permute-start.7 = (bf16[4,3,40,1280]{3,2,1,0:T(8,128)(2,1)}, bf16[4,3,40,1280]{3,2,1,0:T(8,128)(2,1)S(1)}, u32[]{:S(2)}, u32[]{:S(2)}) collective-permute-start(bf16[4,3,40,1280]{3,2,1,0:T(8,128)(2,1)} %all-gather.3.cloned.1.call-done), channel_id=1, source_target_pairs={{0,1},{1,0},{2,3},{3,2},{4,5},{5,4},{6,7},{7,6},{8,9},{9,8},{10,11... | collective-permute-start | bytes 3686408 | tf_op jit(solution)/shard_map/ppermute | solution.py:346
  49.3 28.1 %collective-permute-start.8 = (bf16[4,3,40,1280]{3,2,1,0:T(8,128)(2,1)}, bf16[4,3,40,1280]{3,2,1,0:T(8,128)(2,1)S(1)}, u32[]{:S(2)}, u32[]{:S(2)}) collective-permute-start(bf16[4,3,40,1280]{3,2,1,0:T(8,128)(2,1)} %all-gather.3.cloned.1.call-done), channel_id=1, source_target_pairs={{0,4},{4,0},{1,5},{5,1},{2,6},{6,2},{3,7},{7,3},{8,12},{12,8},{9,1... | collective-permute-start | bytes 3686408 | tf_op jit(solution)/shard_map/ppermute | solution.py:348
  50.8 31.1 %collective-permute-start.6 = (bf16[4,136,1280]{2,1,0:T(8,128)(2,1)}, bf16[4,136,1280]{2,1,0:T(8,128)(2,1)}, u32[]{:S(2)}, u32[]{:S(2)}) collective-permute-start(bf16[4,136,1280]{2,1,0:T(8,128)(2,1)} %pad_maximum_fusion.near_ref), channel_id=1, source_target_pairs={{0,2},{2,0},{1,3},{3,1},{4,6},{6,4},{5,7},{7,5},{8,10},{10,8},{9,1... | collective-permute-start | bytes 4177928 | tf_op jit(solution)/shard_map/ppermute | solution.py:353
  76.3 2.2 copy-start.18
  77.3 3.0 %copy-start.20 = (bf16[4,3,40,1280]{3,2,1,0:T(8,128)(2,1)S(1)}, bf16[4,3,40,1280]{3,2,1,0:T(8,128)(2,1)}, u32[]{:S(2)}) copy-start(bf16[4,3,40,1280]{3,2,1,0:T(8,128)(2,1)} %all-gather.3.cloned.1.call-done) | copy-start | bytes 3686404
  78.6 22.9 %collective-permute-start.9 = (bf16[2,3,40,1280]{3,2,1,0:T(8,128)(2,1)}, bf16[2,3,40,1280]{3,2,1,0:T(8,128)(2,1)}, u32[]{:S(2)}, u32[]{:S(2)}) collective-permute-start(bf16[2,3,40,1280]{3,2,1,0:T(8,128)(2,1)} %slice.174), channel_id=1, source_target_pairs={{0,4},{4,0},{1,5},{5,1},{2,6},{6,2},{3,7},{7,3},{8,12},{12,8},{9,1... | collective-permute-start | bytes 1843208 | tf_op jit(solution)/shard_map/ppermute | solution.py:348
  79.3 22.2 %collective-permute-start.10 = (bf16[2,3,40,1280]{3,2,1,0:T(8,128)(2,1)}, bf16[2,3,40,1280]{3,2,1,0:T(8,128)(2,1)}, u32[]{:S(2)}, u32[]{:S(2)}) collective-permute-start(bf16[2,3,40,1280]{3,2,1,0:T(8,128)(2,1)} %get-tuple-element.113), channel_id=1, source_target_pairs={{0,1},{1,0},{2,3},{3,2},{4,5},{5,4},{6,7},{7,6},{8,9},{9,8},{10,11... | collective-permute-start | bytes 1843208 | tf_op jit(solution)/shard_map/ppermute | solution.py:346
  83.1 18.4 %all-to-all-start.1 = ((bf16[4,4,8,1280]{3,2,1,0:T(8,128)(2,1)}), bf16[4,4,8,1280]{3,2,1,0:T(8,128)(2,1)}, u32[]{:S(2)}, u32[]{:S(2)}) async-start(bf16[4,4,8,1280]{3,2,1,0:T(8,128)(2,1)} %bitcast.31), calls=%async_computation.1 | async-start | bytes 655360 | tf_op jit(solution)/shard_map/all_to_all | solution.py:759
  91.2 119.1 %reduce-scatter.3.cloned.1.call-start = ((), (), s32[]{:S(2)}) async-start(), calls=%async_computation.7 | async-start | bytes 1720320 | tf_op jit(solution)/shard_map/reduce_scatter | solution.py:868
  91.3 1.3 copy-start.3
  100.2 1.3 copy-start.16
  101.5 18.2 %collective-permute-start.16 = (bf16[4,3,80,1280]{3,2,1,0:T(8,128)(2,1)S(1)}, bf16[4,3,80,1280]{3,2,1,0:T(8,128)(2,1)}, u32[]{:S(2)}, u32[]{:S(2)}) collective-permute-start(bf16[4,3,80,1280]{3,2,1,0:T(8,128)(2,1)S(1)} %bitcast_select_fusion.near_rows), channel_id=1, source_target_pairs={{0,2},{2,0},{1,3},{3,1},{4,6},{6,4},{5,7},{7,5},{8,10},{10,8},{9,1... | collective-permute-start | bytes 7372808 | tf_op jit(solution)/shard_map/ppermute | solution.py:353
  104.9 14.8 %collective-permute-start.18 = (bf16[2,3,80,1280]{3,2,1,0:T(8,128)(2,1)}, bf16[2,3,80,1280]{3,2,1,0:T(8,128)(2,1)}, u32[]{:S(2)}, u32[]{:S(2)}) collective-permute-start(bf16[2,3,80,1280]{3,2,1,0:T(8,128)(2,1)} %get-tuple-element.209.across_b), channel_id=1, source_target_pairs={{0,2},{2,0},{1,3},{3,1},{4,6},{6,4},{5,7},{7,5},{8,10},{10,8},{9,1... | collective-permute-start | bytes 3686408 | tf_op jit(solution)/shard_map/ppermute | solution.py:353
  105.4 14.3 %collective-permute-start.17 = (bf16[2,3,80,1280]{3,2,1,0:T(8,128)(2,1)}, bf16[2,3,80,1280]{3,2,1,0:T(8,128)(2,1)}, u32[]{:S(2)}, u32[]{:S(2)}) collective-permute-start(bf16[2,3,80,1280]{3,2,1,0:T(8,128)(2,1)} %get-tuple-element.210.across_a), channel_id=1, source_target_pairs={{0,2},{2,0},{1,3},{3,1},{4,6},{6,4},{5,7},{7,5},{8,10},{10,8},{9,1... | collective-permute-start | bytes 3686408 | tf_op jit(solution)/shard_map/ppermute | solution.py:353
  105.5 7.0 %collective-permute-start.14 = (bf16[2,128,160]{2,1,0:T(8,128)(2,1)S(1)}, bf16[2,128,160]{2,1,0:T(8,128)(2,1)S(1)}, u32[]{:S(2)}, u32[]{:S(2)}) collective-permute-start(bf16[2,128,160]{2,1,0:T(8,128)(2,1)S(1)} %get-tuple-element.186), channel_id=1, source_target_pairs={{0,5},{1,4},{4,1},{5,0},{2,7},{3,6},{6,3},{7,2},{8,13},{9,12},{12,... | collective-permute-start | bytes 245768 | tf_op jit(solution)/shard_map/ppermute | solution.py:349
  106.3 8.6 %collective-permute-start.13 = (bf16[2,128,160]{2,1,0:T(8,128)(2,1)S(1)}, bf16[2,128,160]{2,1,0:T(8,128)(2,1)S(1)}, u32[]{:S(2)}, u32[]{:S(2)}) collective-permute-start(bf16[2,128,160]{2,1,0:T(8,128)(2,1)S(1)} %get-tuple-element.187), channel_id=1, source_target_pairs={{0,4},{4,0},{1,5},{5,1},{2,6},{6,2},{3,7},{7,3},{8,12},{12,8},{9,1... | collective-permute-start | bytes 245768 | tf_op jit(solution)/shard_map/ppermute | solution.py:348
  112.4 5.0 %collective-permute-start.12 = (bf16[2,128,160]{2,1,0:T(8,128)(2,1)S(1)}, bf16[2,128,160]{2,1,0:T(8,128)(2,1)S(1)}, u32[]{:S(2)}, u32[]{:S(2)}) collective-permute-start(bf16[2,128,160]{2,1,0:T(8,128)(2,1)S(1)} %get-tuple-element.188), channel_id=1, source_target_pairs={{0,1},{1,0},{2,3},{3,2},{4,5},{5,4},{6,7},{7,6},{8,9},{9,8},{10,11... | collective-permute-start | bytes 245768 | tf_op jit(solution)/shard_map/ppermute | solution.py:346
  114.9 2.9 %collective-permute-start.11 = (bf16[128,1280]{1,0:T(8,128)(2,1)}, bf16[128,1280]{1,0:T(8,128)(2,1)}, u32[]{:S(2)}, u32[]{:S(2)}) collective-permute-start(bf16[128,1280]{1,0:T(8,128)(2,1)} %bitcast.33.g_ref.cot_ref), channel_id=1, source_target_pairs={{0,2},{2,0},{1,3},{3,1},{4,6},{6,4},{5,7},{7,5},{8,10},{10,8},{9,1... | collective-permute-start | bytes 983048 | tf_op jit(solution)/shard_map/ppermute | solution.py:353
  117.6 2.1 collective-permute-start.15
  131.8 8.0 %copy-start.14 = (f32[128,1280]{1,0:T(8,128)}, f32[128,1280]{1,0:T(8,128)S(1)}, u32[]{:S(2)}) copy-start(f32[128,1280]{1,0:T(8,128)S(1)} %get-tuple-element.163.dmid_ref) | copy-start | bytes 1966084
  131.8 3.6 %collective-permute-start.19 = (bf16[4,128,1280]{2,1,0:T(8,128)(2,1)S(1)}, bf16[4,128,1280]{2,1,0:T(8,128)(2,1)S(1)}, u32[]{:S(2)}, u32[]{:S(2)}) collective-permute-start(bf16[4,128,1280]{2,1,0:T(8,128)(2,1)S(1)} %get-tuple-element.122.pack_ref), channel_id=1, source_target_pairs={{0,2},{2,0},{1,3},{3,1},{4,6},{6,4},{5,7},{7,5},{8,10},{10,8},{9,1... | collective-permute-start | bytes 3932168 | tf_op jit(solution)/shard_map/ppermute | solution.py:353
  131.9 10.0 %collective-permute-start.20 = (bf16[2,128,160]{2,1,0:T(8,128)(2,1)S(1)}, bf16[2,128,160]{2,1,0:T(8,128)(2,1)S(1)}, u32[]{:S(2)}, u32[]{:S(2)}) collective-permute-start(bf16[2,128,160]{2,1,0:T(8,128)(2,1)S(1)} %get-tuple-element.129), channel_id=1, source_target_pairs={{0,1},{1,0},{2,3},{3,2},{4,5},{5,4},{6,7},{7,6},{8,9},{9,8},{10,11... | collective-permute-start | bytes 245768 | tf_op jit(solution)/shard_map/ppermute | solution.py:346
  132.7 9.2 %collective-permute-start.21 = (bf16[2,128,160]{2,1,0:T(8,128)(2,1)S(1)}, bf16[2,128,160]{2,1,0:T(8,128)(2,1)S(1)}, u32[]{:S(2)}, u32[]{:S(2)}) collective-permute-start(bf16[2,128,160]{2,1,0:T(8,128)(2,1)S(1)} %get-tuple-element.130), channel_id=1, source_target_pairs={{0,4},{4,0},{1,5},{5,1},{2,6},{6,2},{3,7},{7,3},{8,12},{12,8},{9,1... | collective-permute-start | bytes 245768 | tf_op jit(solution)/shard_map/ppermute | solution.py:348
  133.2 10.8 %copy-start.4 = (bf16[1280,480]{1,0:T(8,128)(2,1)S(1)}, bf16[1280,480]{1,0:T(8,128)(2,1)}, u32[]{:S(2)}) copy-start(bf16[1280,480]{1,0:T(8,128)(2,1)} %all-gather.5.cloned.1.call-done.w_ref) | copy-start | bytes 3686404
  133.2 10.8 %copy-start.17 = (f32[2,4,128,480]{3,2,1,0:T(8,128)S(1)}, f32[2,4,128,480]{3,2,1,0:T(8,128)}, u32[]{:S(2)}) copy-start(f32[2,4,128,480]{3,2,1,0:T(8,128)} %copy-done.16) | copy-start | bytes 5898244
  133.2 8.7 %collective-permute-start.22 = (bf16[2,128,160]{2,1,0:T(8,128)(2,1)S(1)}, bf16[2,128,160]{2,1,0:T(8,128)(2,1)S(1)}, u32[]{:S(2)}, u32[]{:S(2)}) collective-permute-start(bf16[2,128,160]{2,1,0:T(8,128)(2,1)S(1)} %get-tuple-element.131), channel_id=1, source_target_pairs={{0,5},{1,4},{4,1},{5,0},{2,7},{3,6},{6,3},{7,2},{8,13},{9,12},{12,... | collective-permute-start | bytes 245768 | tf_op jit(solution)/shard_map/ppermute | solution.py:349
  142.0 2.0 collective-permute-start.23
  142.1 29.8 %collective-permute-start.24 = (bf16[2,3,2,40,1280]{4,3,2,1,0:T(8,128)(2,1)}, bf16[2,3,2,40,1280]{4,3,2,1,0:T(8,128)(2,1)}, u32[]{:S(2)}, u32[]{:S(2)}) collective-permute-start(bf16[2,3,2,40,1280]{4,3,2,1,0:T(8,128)(2,1)} %get-tuple-element.141), channel_id=1, source_target_pairs={{0,1},{1,0},{2,3},{3,2},{4,5},{5,4},{6,7},{7,6},{8,9},{9,8},{10,11... | collective-permute-start | bytes 3686408 | tf_op jit(solution)/shard_map/ppermute | solution.py:346
  142.9 29.4 %collective-permute-start.25 = (bf16[2,3,2,40,1280]{4,3,2,1,0:T(8,128)(2,1)}, bf16[2,3,2,40,1280]{4,3,2,1,0:T(8,128)(2,1)}, u32[]{:S(2)}, u32[]{:S(2)}) collective-permute-start(bf16[2,3,2,40,1280]{4,3,2,1,0:T(8,128)(2,1)} %get-tuple-element.142), channel_id=1, source_target_pairs={{0,4},{4,0},{1,5},{5,1},{2,6},{6,2},{3,7},{7,3},{8,12},{12,8},{9,1... | collective-permute-start | bytes 3686408 | tf_op jit(solution)/shard_map/ppermute | solution.py:348
  156.9 82.0 %reduce-scatter.5.cloned.1.call-start = ((), (), s32[]{:S(2)}) async-start(), calls=%async_computation.8 | async-start | bytes 1536000 | tf_op jit(solution)/shard_map/reduce_scatter | solution.py:899
  157.9 7.8 %collective-permute-start.27 = (bf16[4,8,1280]{2,1,0:T(8,128)(2,1)S(1)}, bf16[4,8,1280]{2,1,0:T(8,128)(2,1)S(1)}, u32[]{:S(2)}, u32[]{:S(2)}) collective-permute-start(bf16[4,8,1280]{2,1,0:T(8,128)(2,1)S(1)} %get-tuple-element.193), channel_id=1, source_target_pairs={{0,24},{8,0},{16,8},{24,16},{1,25},{9,1},{17,9},{25,17},{2,26},{10... | collective-permute-start | bytes 245768 | tf_op jit(solution)/shard_map/ppermute | solution.py:357
  161.8 7.3 %collective-permute-start.26 = (bf16[4,8,1280]{2,1,0:T(8,128)(2,1)S(1)}, bf16[4,8,1280]{2,1,0:T(8,128)(2,1)S(1)}, u32[]{:S(2)}, u32[]{:S(2)}) collective-permute-start(bf16[4,8,1280]{2,1,0:T(8,128)(2,1)S(1)} %get-tuple-element.194), channel_id=1, source_target_pairs={{0,8},{8,16},{16,24},{24,0},{1,9},{9,17},{17,25},{25,1},{2,10},{10... | collective-permute-start | bytes 245768 | tf_op jit(solution)/shard_map/ppermute | solution.py:357
  172.3 21.6 %collective-permute-start.28 = (bf16[4,128,1280]{2,1,0:T(8,128)(2,1)S(1)}, bf16[4,128,1280]{2,1,0:T(8,128)(2,1)}, u32[]{:S(2)}, u32[]{:S(2)}) collective-permute-start(bf16[4,128,1280]{2,1,0:T(8,128)(2,1)S(1)} %get-tuple-element.147), channel_id=1, source_target_pairs={{0,2},{2,0},{1,3},{3,1},{4,6},{6,4},{5,7},{7,5},{8,10},{10,8},{9,1... | collective-permute-start | bytes 3932168 | tf_op jit(solution)/shard_map/ppermute | solution.py:353
  173.6 1.3 copy-start.13
  179.8 16.6 %collective-permute-start.29 = (bf16[2,3,40,1280]{3,2,1,0:T(8,128)(2,1)}, bf16[2,3,40,1280]{3,2,1,0:T(8,128)(2,1)}, u32[]{:S(2)}, u32[]{:S(2)}) collective-permute-start(bf16[2,3,40,1280]{3,2,1,0:T(8,128)(2,1)} %get-tuple-element.152), channel_id=1, source_target_pairs={{0,4},{4,0},{1,5},{5,1},{2,6},{6,2},{3,7},{7,3},{8,12},{12,8},{9,1... | collective-permute-start | bytes 1843208 | tf_op jit(solution)/shard_map/ppermute | solution.py:348
  180.7 16.3 %collective-permute-start.30 = (bf16[2,3,40,1280]{3,2,1,0:T(8,128)(2,1)}, bf16[2,3,40,1280]{3,2,1,0:T(8,128)(2,1)}, u32[]{:S(2)}, u32[]{:S(2)}) collective-permute-start(bf16[2,3,40,1280]{3,2,1,0:T(8,128)(2,1)} %get-tuple-element.153), channel_id=1, source_target_pairs={{0,1},{1,0},{2,3},{3,2},{4,5},{5,4},{6,7},{7,6},{8,9},{9,8},{10,11... | collective-permute-start | bytes 1843208 | tf_op jit(solution)/shard_map/ppermute | solution.py:346
  181.5 11.5 %collective-permute-start.31 = (bf16[4,8,1280]{2,1,0:T(8,128)(2,1)S(1)}, bf16[4,8,1280]{2,1,0:T(8,128)(2,1)S(1)}, u32[]{:S(2)}, u32[]{:S(2)}) collective-permute-start(bf16[4,8,1280]{2,1,0:T(8,128)(2,1)S(1)} %get-tuple-element.191), channel_id=1, source_target_pairs={{0,16},{8,24},{16,0},{24,8},{1,17},{9,25},{17,1},{25,9},{2,18},{10... | collective-permute-start | bytes 245768 | tf_op jit(solution)/shard_map/ppermute | solution.py:357
  193.9 3.1 %copy-start.7 = (bf16[2,3,40,1280]{3,2,1,0:T(8,128)(2,1)S(1)}, bf16[2,3,40,1280]{3,2,1,0:T(8,128)(2,1)}, u32[]{:S(2)}) copy-start(bf16[2,3,40,1280]{3,2,1,0:T(8,128)(2,1)} %copy-done.6) | copy-start | bytes 1843204
  193.9 3.1 %copy-start.9 = (bf16[2,3,40,1280]{3,2,1,0:T(8,128)(2,1)S(1)}, bf16[2,3,40,1280]{3,2,1,0:T(8,128)(2,1)}, u32[]{:S(2)}) copy-start(bf16[2,3,40,1280]{3,2,1,0:T(8,128)(2,1)} %copy-done.8) | copy-start | bytes 1843204
  199.6 10.7 %collective-permute-start.32 = (bf16[128,1280]{1,0:T(8,128)(2,1)S(1)}, bf16[128,1280]{1,0:T(8,128)(2,1)S(1)}, u32[]{:S(2)}, u32[]{:S(2)}) collective-permute-start(bf16[128,1280]{1,0:T(8,128)(2,1)S(1)} %get-tuple-element.158), channel_id=1, source_target_pairs={{0,1},{1,0},{2,3},{3,2},{4,5},{5,4},{6,7},{7,6},{8,9},{9,8},{10,11... | collective-permute-start | bytes 983048 | tf_op jit(solution)/shard_map/ppermute | solution.py:346
  200.6 15.8 %collective-permute-start.33 = (bf16[128,1280]{1,0:T(8,128)(2,1)S(1)}, bf16[128,1280]{1,0:T(8,128)(2,1)S(1)}, u32[]{:S(2)}, u32[]{:S(2)}) collective-permute-start(bf16[128,1280]{1,0:T(8,128)(2,1)S(1)} %get-tuple-element.161), channel_id=1, source_target_pairs={{0,4},{4,0},{1,5},{5,1},{2,6},{6,2},{3,7},{7,3},{8,12},{12,8},{9,1... | collective-permute-start | bytes 983048 | tf_op jit(solution)/shard_map/ppermute | solution.py:348
  202.1 14.3 %collective-permute-start.34 = (bf16[128,1280]{1,0:T(8,128)(2,1)S(1)}, bf16[128,1280]{1,0:T(8,128)(2,1)S(1)}, u32[]{:S(2)}, u32[]{:S(2)}) collective-permute-start(bf16[128,1280]{1,0:T(8,128)(2,1)S(1)} %get-tuple-element.162), channel_id=1, source_target_pairs={{0,5},{1,4},{4,1},{5,0},{2,7},{3,6},{6,3},{7,2},{8,13},{9,12},{12,... | collective-permute-start | bytes 983048 | tf_op jit(solution)/shard_map/ppermute | solution.py:349
  212.2 25.2 %all-to-all-start.2 = ((bf16[8,48,480]{2,1,0:T(8,128)(2,1)}), bf16[8,48,480]{2,1,0:T(8,128)(2,1)S(1)}, u32[]{:S(2)}, u32[]{:S(2)}) async-start(bf16[8,48,480]{2,1,0:T(8,128)(2,1)} %fold.1), calls=%async_computation.3 | async-start | bytes 786432 | tf_op jit(solution)/shard_map/all_to_all | solution.py:920
  218.5 8.6 %collective-permute-start.35 = (bf16[4,8,1280]{2,1,0:T(8,128)(2,1)S(1)}, bf16[4,8,1280]{2,1,0:T(8,128)(2,1)S(1)}, u32[]{:S(2)}, u32[]{:S(2)}) collective-permute-start(bf16[4,8,1280]{2,1,0:T(8,128)(2,1)S(1)} %get-tuple-element.164), channel_id=1, source_target_pairs={{0,24},{8,0},{16,8},{24,16},{1,25},{9,1},{17,9},{25,17},{2,26},{10... | collective-permute-start | bytes 245768 | tf_op jit(solution)/shard_map/ppermute | solution.py:357
  222.4 14.1 %collective-permute-start.36 = (bf16[4,8,1280]{2,1,0:T(8,128)(2,1)S(1)}, bf16[4,8,1280]{2,1,0:T(8,128)(2,1)S(1)}, u32[]{:S(2)}, u32[]{:S(2)}) collective-permute-start(bf16[4,8,1280]{2,1,0:T(8,128)(2,1)S(1)} %get-tuple-element.165), channel_id=1, source_target_pairs={{0,16},{8,24},{16,0},{24,8},{1,17},{9,25},{17,1},{25,9},{2,18},{10... | collective-permute-start | bytes 245768 | tf_op jit(solution)/shard_map/ppermute | solution.py:357
  222.4 14.1 %collective-permute-start.37 = (bf16[4,8,1280]{2,1,0:T(8,128)(2,1)S(1)}, bf16[4,8,1280]{2,1,0:T(8,128)(2,1)S(1)}, u32[]{:S(2)}, u32[]{:S(2)}) collective-permute-start(bf16[4,8,1280]{2,1,0:T(8,128)(2,1)S(1)} %get-tuple-element.166), channel_id=1, source_target_pairs={{0,8},{8,16},{16,24},{24,0},{1,9},{9,17},{17,25},{25,1},{2,10},{10... | collective-permute-start | bytes 245768 | tf_op jit(solution)/shard_map/ppermute | solution.py:357
  (11 other events, 10.9 us)
Sparse Core Ops, SparseCore 0:
  10.4 34.5 all-gather.2
  51.2 34.4 all-gather.4
  157.0 34.9 reduce-scatter.2
  199.7 36.2 reduce-scatter.4

commit v13 on v12

--- a/solution.py
+++ b/solution.py
@@ -1,3 +1,4 @@
+import functools
 import math
 
 import jax
@@ -489,19 +490,6 @@
             send_ref[target] = block.astype(jnp.bfloat16)
 
 
-def block_index(z_index, y_index, core):
-    return pl.ds(pl.multiple_of((4 * z_index + 2 * y_index + core) * 80, 80), 80)
-
-
-def arrival_rows(info_ref, w, z_index, y_index, core):
-    if w > 0:
-        return block_index(z_index, y_index, core)
-    block = 4 * z_index + 2 * y_index + core
-    code = info_ref[1] ^ (block // 2)
-    arrival = 2 * ((code & 1) + 2 * (code // 4)) + ((code // 2) & 1)
-    return pl.ds(pl.multiple_of(160 * arrival + 80 * (block & 1), 80), 80)
-
-
 def feed_kernel(
     info_ref, x_ref, g_ref, atts, far_atts, gain_ref,
     near_rows, across_a, across_b, far_near_rows, far_across_a, far_across_b,
@@ -516,13 +504,11 @@
             (core_index, near_rows, (across_a, across_b)),
             (1 - core_index, far_near_rows, (far_across_a, far_across_b)),
         ):
-            for z_index in range(4):
-                moved.append((own.at[z_index, w], z_index, y_index, core))
-                moved.append((others[z_index // 2].at[z_index % 2, w], z_index, 1 - y_index, core))
-        copies.append([
-            pltpu.make_async_copy(src, weights.at[w, arrival_rows(info_ref, w, *place)], sems.at[w, i])
-            for i, (src, *place) in enumerate(moved)
-        ])
+            moved.append((own.at[:, w], weights.at[w, :, y_index, core]))
+            for half in range(2):
+                moved.append((others[half].at[:, w], weights.at[w, pl.ds(2 * half, 2), 1 - y_index, core]))
+        copies.append([pltpu.make_async_copy(*refs, sems.at[w, i]) for i, refs in enumerate(moved)])
+    size = x_ref.shape[1]
     for group in copies:
         for copy in group:
             copy.start()
@@ -530,11 +516,11 @@
 
     for copy in copies[0]:
         copy.wait()
-    att = jnp.concatenate(
-        [(far_atts if core else atts)[chip, core] for chip in range(4) for core in range(2)], axis=1
-    )
+    heads = [(chip, core, info_ref[1] ^ (CODES[chip] + 2 * core)) for chip in range(4) for core in range(2)]
     middle = x_ref[...].astype(jnp.float32)
-    middle += jnp.dot(att, weights[0], preferred_element_type=jnp.float32)
+    for chip, core, source in heads:
+        rows = weights[0, source // 2, source & 1].reshape(160, size)
+        middle += jnp.dot((far_atts if core else atts)[chip, core], rows, preferred_element_type=jnp.float32)
     inverse = lax.rsqrt(jnp.mean(middle * middle, axis=1, keepdims=True) + 1e-06)
     normed = middle * inverse
     gain = gain_ref[...]
@@ -542,33 +528,31 @@
     pack_ref[1] = hidden
     for copy in copies[1]:
         copy.wait()
-    up = jnp.dot(hidden, weights[1], preferred_element_type=jnp.float32)
+    up = jnp.dot(hidden, weights[1].reshape(size, size), preferred_element_type=jnp.float32)
     sigma = jax.nn.sigmoid(up)
     active = (up * sigma).astype(jnp.bfloat16)
     pack_ref[0] = active
     for copy in copies[2]:
         copy.wait()
-    down = jnp.dot(active, weights[2], preferred_element_type=jnp.float32)
+    down = jnp.dot(active, weights[2].reshape(size, size), preferred_element_type=jnp.float32)
     result = middle + down
     for seq in range(4):
         for plane_z in range(4):
             row = 32 * seq + 8 * plane_z
             out_ref[plane_z, seq] = result[row : row + 8].astype(jnp.bfloat16)
     cot = g_ref[...]
-    grad_act = mult_trans(cot, weights[2])
+    grad_act = mult_trans(cot, weights[2].reshape(size, size))
     grad_up = (grad_act * sigma * (1.0 + up * (1.0 - sigma))).astype(jnp.bfloat16)
     pack_ref[2] = grad_up
-    grad_hidden = mult_trans(grad_up, weights[1])
+    grad_hidden = mult_trans(grad_up, weights[1].reshape(size, size))
     gain_grad[...] = jnp.sum(grad_hidden * normed, axis=0, keepdims=True)
     grad_mid = cot.astype(jnp.float32) + norm_back(grad_hidden, normed, inverse, gain)
     dmid_ref[...] = grad_mid
     low = grad_mid.astype(jnp.bfloat16)
     pack_ref[3] = low
-    grad_att = mult_trans(low, weights[0]).astype(jnp.bfloat16)
-    for chip in range(4):
-        for core in range(2):
-            lane = 160 * (2 * chip + core)
-            datts[chip][core] = grad_att[:, lane : lane + 160]
+    for chip, core, source in heads:
+        rows = weights[0, source // 2, source & 1].reshape(160, size)
+        datts[chip][core] = mult_trans(low, rows).astype(jnp.bfloat16)
 
 
 def grads_kernel(
@@ -640,14 +624,14 @@
             copy.wait()
 
 
-def meet_kernel(info_ref, mine_a, from_a, mine_b, from_b, keep_a, away_a, keep_b, away_b):
+def meet_kernel(far_side, info_ref, mine_a, from_a, mine_b, from_b, out_a, out_b):
     y_index, x_index = info_ref[1] // 4, info_ref[1] % 2
+    if far_side:
+        y_index, x_index = 1 - y_index, 1 - x_index
     for half in range(2):
         for w in range(3):
-            for row, out in ((y_index, keep_a), (1 - y_index, away_a)):
-                out[half, w] = sum_low(mine_a[half, w, row], from_a[half, w, row])
-            for row, out in ((x_index, keep_b), (1 - x_index, away_b)):
-                out[half, w] = sum_low(mine_b[half, w, row], from_b[half, w, row])
+            out_a[half, w] = sum_low(mine_a[half, w, y_index], from_a[half, w, y_index])
+            out_b[half, w] = sum_low(mine_b[half, w, x_index], from_b[half, w, x_index])
 
 
 def join_kernel(keep_a, from_a, keep_b, from_b, out_ref):
@@ -738,12 +722,13 @@
     qkv = qkv.reshape(3, 40, 8, 160).transpose(2, 1, 0, 3).reshape(8, 40, 480)
     qkv = lax.all_to_all(qkv, ("y", "core", "x"), split_axis=0, concat_axis=0, tiled=True)
     near = jnp.stack([own] + [plane_shift(own, step) for step in (1, 2, 3)])
-    big, near, qkv = lax.optimization_barrier((big, near, qkv.reshape(320, 480)))
+    big, near, cotangent, qkv = lax.optimization_barrier((big, near, cotangent, qkv.reshape(320, 480)))
     w_qkv = lax.all_gather(qkv, "z", axis=0, tiled=True)
     far = core_swap(near)
     beside, across = plane_shift(big, 1), plane_shift(big, 2)
     relay_a, relay_b = beside[:2], across[2:]
-    relay_a, relay_b = lax.optimization_barrier((relay_a, relay_b))
+    cot_rows = lax.all_to_all(cotangent.reshape(4, 4, 8, width), "z", split_axis=0, concat_axis=0, tiled=True)
+    relay_a, relay_b, cot_rows = lax.optimization_barrier((relay_a, relay_b, cot_rows))
     across_a, across_b = plane_shift(relay_a, 2), plane_shift(relay_b, 1)
 
     vecs = jnp.stack([near[:, 128:132, :120], far[:, 128:132, :120]])
@@ -755,8 +740,6 @@
     gain_one, gain_two = vecs[0:1], vecs[1:2]
     my_scale = lax.dynamic_slice_in_dim(vecs[2:3], 160 * plane, 160, 1)
     query_mult = LOG2E / math.sqrt(HD) * jax.nn.softplus(my_scale)
-    query_mult, cotangent = lax.optimization_barrier((query_mult, cotangent))
-    cot_rows = lax.all_to_all(cotangent.reshape(4, 4, 8, width), "z", split_axis=0, concat_axis=0, tiled=True)
 
 
     def limit(megabytes):
@@ -783,9 +766,7 @@
     )(info, near, far, gain_one, query_mult, w_qkv)
 
     near_rows = pair(big, beside, x, 2).reshape(4, 3, 80, width)
-    att_made, near_rows, across_a, across_b, cot_rows = lax.optimization_barrier(
-        (att_made, near_rows, across_a, across_b, cot_rows)
-    )
+    att_made, near_rows, across_a, across_b = lax.optimization_barrier((att_made, near_rows, across_a, across_b))
     far_near_rows = core_swap(near_rows)
     atts = [att_made[0]] + [plane_shift(att_made[step], step) for step in (1, 2, 3)]
     atts = jnp.stack(atts)
@@ -811,8 +792,8 @@
         ]
         + [datt_shape] * 4
         + [jax.ShapeDtypeStruct((1, width), f32)],
-        scratch_shapes=[pltpu.VMEM((3, width, width), bf16), pltpu.SemaphoreType.DMA((3, 16))],
-        compiler_params=limit(28),
+        scratch_shapes=[pltpu.VMEM((3, 4, 2, 2, 80, width), bf16), pltpu.SemaphoreType.DMA((3, 6))],
+        compiler_params=limit(36),
         cost_estimate=pl.CostEstimate(flops=12_000_000_000, bytes_accessed=13_000_000, transcendentals=200_000),
         name="feed",
     )(info, x_rows, cot_rows, atts, far_atts, gain_two, near_rows, across_a, across_b, far_near_rows, far_across_a, far_across_b)
@@ -874,15 +855,20 @@
     swapped = core_swap(hid_far)
     hid = [sum_low(hid_near[i], swapped[i]) for i in range(4)]
     outputs = by_source([out_sent[0], out_one, ring_shift(out_sent[2], 2), out_three], z, 0).reshape(16, 8, width)
-    keep_a, away_a, keep_b, away_b = pl.pallas_call(
-        meet_kernel,
-        in_specs=[smem] + [vmem] * 4,
-        out_specs=[vmem] * 4,
-        out_shape=[jax.ShapeDtypeStruct((2, 3, 40, width), bf16)] * 4,
-        compiler_params=limit(18),
-        cost_estimate=pl.CostEstimate(flops=3_000_000_000, bytes_accessed=8_000_000, transcendentals=0),
-        name="meet",
-    )(info, mine_a, from_a, mine_b, from_b)
+    def meet(far_side, *parts):
+        return pl.pallas_call(
+            functools.partial(meet_kernel, far_side),
+            in_specs=[smem] + [vmem] * 4,
+            out_specs=[vmem] * 2,
+            out_shape=[jax.ShapeDtypeStruct((2, 3, 40, width), bf16)] * 2,
+            compiler_params=limit(50),
+            cost_estimate=pl.CostEstimate(flops=2_000_000_000, bytes_accessed=4_000_000, transcendentals=0),
+            name="meet",
+        )(info, *parts)
+
+    parts = mine_a, from_a, mine_b, from_b
+    away_a, away_b = meet(True, *parts)
+    keep_a, keep_b = meet(False, *parts)
     from_a, from_b = plane_shift(away_a, 2), plane_shift(away_b, 1)
     *hid, from_a, from_b, outputs = lax.optimization_barrier((*hid, from_a, from_b, outputs))
     kept = pl.pallas_call(
@@ -890,7 +876,7 @@
         in_specs=[vmem] * 4,
         out_specs=vmem,
         out_shape=jax.ShapeDtypeStruct((4, 3, 40, width), bf16),
-        compiler_params=limit(12),
+        compiler_params=limit(50),
         cost_estimate=pl.CostEstimate(flops=2_000_000_000, bytes_accessed=4_000_000, transcendentals=0),
         name="join",
     )(keep_a, from_a, keep_b, from_b)

time: 248 us -> 237 us (0.956)
  starting transfers between devices: 56.1 us -> 50.3 us
  local copies, waits for them, and re-layouts: 23.1 us -> 18.5 us
  waiting for transfers between devices: 92.8 us -> 95.5 us
  Pallas kernels: 45.5 us -> 43 us
    ppermute x9, waiting for transfers between devices: 37.3 us -> 31 us  [ring_shift(): return lax.ppermute(value, 'z', [(i, (i + step) % 4) for i in range(4)])]
    ppermute x8, waiting for transfers between devices: 2.88 us -> 9.14 us  [plane_shift(): return lax.ppermute(value, 'y', [(0, 1), (1, 0)])]
    all_gather x1, waiting for transfers between devices: 0.02 us -> 6.01 us  [planes(): w_qkv = lax.all_gather(qkv, 'z', axis=0, tiled=True)]
    ppermute x9, starting transfers between devices: 18 us -> 13 us  [ring_shift(): return lax.ppermute(value, 'z', [(i, (i + step) % 4) for i in range(4)])]
    unnamed x60 -> x52, local copies, waits for them, and re-layouts: 13.7 us -> 9.02 us
    ppermute x8, waiting for transfers between devices: 39.9 us -> 36.3 us  [plane_shift(): return lax.ppermute(value, 'x', [(0, 1), (1, 0)])]
    pallas_call x1, Pallas kernels: 11.3 us -> 8.51 us  [planes(): pl.pallas_call(feed_kernel, in_specs=[smem] + [vmem] * 5 + [hbm] * 6, out...]
  transfers between devices with their start and end apart: 45 -> 45, of which waited for: 22 -> 24; matrix products, arithmetic and copies ran while one was open for 9% -> 9% of each run, Pallas kernels for 14% -> 14%
where the time goes in v13:
time: 237 us; the launch traced here: 236 us
  waiting for transfers between devices  95.5 us (40%)
  starting transfers between devices  50.3 us (21%)
  Pallas kernels  43 us (18%)
  local copies, waits for them, and re-layouts  18.5 us (8%)
  other arithmetic  14.4 us (6%)
  between operations  14.4 us (6%)
    ppermute x8, waiting for transfers between devices, plane_shift(): return lax.ppermute(value, 'x', [(0, 1), (1, 0)])  36.3 us
    ppermute x9, waiting for transfers between devices, ring_shift(): return lax.ppermute(value, 'z', [(i, (i + step) % 4) for i in range(4)])  31 us
    ppermute x9, starting transfers between devices, ring_shift(): return lax.ppermute(value, 'z', [(i, (i + step) % 4) for i in range(4)])  13 us
    pallas_call x1, Pallas kernels, planes(): pl.pallas_call(attend_back_kernel, grid_spec=pltpu.PrefetchScalarGridSpec...  12.9 us
    ppermute x4, waiting for transfers between devices, plane_shift(): return lax.ppermute(value, ('y', 'x'), [(0, 3), (1, 2), (2, 1), (3, 0)])  10.6 us
    ppermute x8, waiting for transfers between devices, plane_shift(): return lax.ppermute(value, 'y', [(0, 1), (1, 0)])  9.14 us
    unnamed x52, local copies, waits for them, and re-layouts  9.02 us
    ppermute x8, starting transfers between devices, plane_shift(): return lax.ppermute(value, 'x', [(0, 1), (1, 0)])  8.69 us
  transfers between devices with their start and end apart: 45, of which 24 were waited for; matrix products, arithmetic and copies ran while one was open for 9% of the time, Pallas kernels for 14%

profile of v13, /device:TPU:0, one launch (start us, length us, event | category | flops | bytes accessed | tf_op | source)
XLA Modules:
  0.0 236.1 jit_solution(15924524239188173158)
XLA Ops:
  7.3 1.1 convert_bitcast_fusion.5
  8.4 1.1 convert_bitcast_fusion.3
  10.7 5.1 %collective-permute-start = (bf16[5,8,1280]{2,1,0:T(8,128)(2,1)S(1)}, bf16[5,8,1280]{2,1,0:T(8,128)(2,1)S(1)}, u32[]{:S(2)}, u32[]{:S(2)}) collective-permute-start(bf16[5,8,1280]{2,1,0:T(8,128)(2,1)S(1)} %get-tuple-element.100), channel_id=1, source_target_pairs={{0,24},{8,0},{16,8},{24,16},{1,25},{9,1},{17,9},{25,17},{2,26},{10... | collective-permute-start | bytes 307208 | tf_op jit(solution)/shard_map/ppermute | solution.py:358
  15.8 1.0 collective-permute-start.2
  17.5 1.6 collective-permute-done
  19.1 7.4 %collective-permute-done.1 = bf16[5,8,1280]{2,1,0:T(8,128)(2,1)S(1)} collective-permute-done((bf16[5,8,1280]{2,1,0:T(8,128)(2,1)S(1)}, bf16[5,8,1280]{2,1,0:T(8,128)(2,1)S(1)}, u32[]{:S(2)}, u32[]{:S(2)}) %collective-permute-start.1) | collective-permute-done | bytes 102432 | tf_op jit(solution)/shard_map/ppermute | solution.py:358
  27.0 1.7 collective-permute-start.4
  28.7 1.5 collective-permute-start.3
  31.6 1.1 reshape.336
  32.7 3.9 %all-to-all-start = ((bf16[8,40,480]{2,1,0:T(8,128)(2,1)}), bf16[8,40,480]{2,1,0:T(8,128)(2,1)S(1)}, u32[]{:S(2)}, u32[]{:S(2)}) async-start(bf16[8,40,480]{2,1,0:T(8,128)(2,1)} %reshape.336), calls=%async_computation | async-start | bytes 655360 | tf_op jit(solution)/shard_map/all_to_all | solution.py:723
  37.2 2.5 %collective-permute-done.3 = bf16[136,1280]{1,0:T(8,128)(2,1)S(1)} collective-permute-done((bf16[136,1280]{1,0:T(8,128)(2,1)S(1)}, bf16[136,1280]{1,0:T(8,128)(2,1)S(1)}, u32[]{:S(2)}, u32[]{:S(2)}) %collective-permute-start.3) | collective-permute-done | bytes 348192 | tf_op jit(solution)/shard_map/ppermute | solution.py:347
  39.7 5.7 %collective-permute-done.5 = bf16[136,1280]{1,0:T(8,128)(2,1)S(1)} collective-permute-done((bf16[136,1280]{1,0:T(8,128)(2,1)S(1)}, bf16[136,1280]{1,0:T(8,128)(2,1)S(1)}, u32[]{:S(2)}, u32[]{:S(2)}) %collective-permute-start.5) | collective-permute-done | bytes 348192 | tf_op jit(solution)/shard_map/ppermute | solution.py:350
  45.4 1.3 pad_maximum_fusion.near_ref
  47.1 1.5 collective-permute-start.7
  48.6 1.1 collective-permute-start.8
  50.9 7.6 %all-to-all-start.1 = ((bf16[4,4,8,1280]{3,2,1,0:T(8,128)(2,1)}), bf16[4,4,8,1280]{3,2,1,0:T(8,128)(2,1)S(1)}, u32[]{:S(2)}, u32[]{:S(2)}) async-start(bf16[4,4,8,1280]{3,2,1,0:T(8,128)(2,1)} %bitcast.29), calls=%async_computation.1 | async-start | bytes 655360 | tf_op jit(solution)/shard_map/all_to_all | solution.py:730
  58.5 17.9 %collective-permute-done.7 = bf16[4,3,40,1280]{3,2,1,0:T(8,128)(2,1)S(1)} collective-permute-done((bf16[4,3,40,1280]{3,2,1,0:T(8,128)(2,1)}, bf16[4,3,40,1280]{3,2,1,0:T(8,128)(2,1)S(1)}, u32[]{:S(2)}, u32[]{:S(2)}) %collective-permute-start.7) | collective-permute-done | bytes 1228832 | tf_op jit(solution)/shard_map/ppermute | solution.py:347
  76.3 1.0 slice.174
  77.6 2.2 fusion.23
  80.5 1.2 collective-permute-start.11
  81.7 1.9 bitcast_select_fusion.near_rows
  84.8 6.0 %all-gather.5.cloned.1.call-done.w_ref = bf16[1280,480]{1,0:T(8,128)(2,1)} async-done(((bf16[320,480]{1,0:T(8,128)(2,1)}), bf16[1280,480]{1,0:T(8,128)(2,1)}) %all-gather.5.cloned.1.call-update) | async-done | bytes 1228816 | tf_op jit(solution)/shard_map/all_gather | solution.py:726
  90.9 1.3 copy-done.3
  92.2 7.5 %attend.1 = (f32[2,4,128,480]{3,2,1,0:T(8,128)S(1)}, bf16[4,2,128,160]{3,2,1,0:T(8,128)(2,1)S(1)}) custom-call(s32[6]{0:T(128)S(1)} %pad_add_fusion.info_ref, bf16[4,136,1280]{2,1,0:T(8,128)(2,1)} %pad_maximum_fusion.near_ref, bf16[4,136,1280]{2,1,0:T(8,128)(2,1)} %collective-permute-done.6.far_ref, f32[1,1280]{1,0:T(1,128)S(1)} %slice.141.gain_ref, ...), custom_call_target="tpu_custom_call" | custom-call | flops 8999999488 | bytes 8000000 | tf_op jit(solution)/shard_map/attend/pallas_call | solution.py:748
  99.7 1.3 copy-done.11
  101.1 3.3 %bitcast_select_fusion.1 = (bf16[2,3,80,1280]{3,2,1,0:T(8,128)(2,1)}, bf16[2,3,80,1280]{3,2,1,0:T(8,128)(2,1)}) fusion(pred[80]{0:T(512)(128)(4,1)S(1)} %broadcast_in_dim.383, bf16[2,3,40,1280]{3,2,1,0:T(8,128)(2,1)} %collective-permute-done.11, bf16[2,3,40,1280]{3,2,1,0:T(8,128)(2,1)} %get-tuple-element.113, ...), kind=kLoop, calls=%fused_computation.2 | loop fusion | flops 1228800 | bytes 4915280 | tf_op jit(solution)/shard_map/jit(_where)/select_n | solution.py:380
  105.4 1.4 collective-permute-start.13
  106.9 4.9 %collective-permute-done.14 = bf16[2,128,160]{2,1,0:T(8,128)(2,1)S(1)} collective-permute-done((bf16[2,128,160]{2,1,0:T(8,128)(2,1)S(1)}, bf16[2,128,160]{2,1,0:T(8,128)(2,1)S(1)}, u32[]{:S(2)}, u32[]{:S(2)}) %collective-permute-start.14) | collective-permute-done | bytes 81952 | tf_op jit(solution)/shard_map/ppermute | solution.py:350
  113.8 3.0 %collective-permute-done.12 = bf16[2,128,160]{2,1,0:T(8,128)(2,1)S(1)} collective-permute-done((bf16[2,128,160]{2,1,0:T(8,128)(2,1)S(1)}, bf16[2,128,160]{2,1,0:T(8,128)(2,1)S(1)}, u32[]{:S(2)}, u32[]{:S(2)}) %collective-permute-start.12) | collective-permute-done | bytes 81952 | tf_op jit(solution)/shard_map/ppermute | solution.py:347
  117.1 1.9 collective-permute-done.15.far_atts
  119.0 8.5 %feed.1 = (bf16[4,4,8,1280]{3,2,1,0:T(8,128)(2,1)S(1)}, bf16[4,128,1280]{2,1,0:T(8,128)(2,1)S(1)}, f32[128,1280]{1,0:T(8,128)S(1)}, bf16[2,128,160]{2,1,0:T(8,12...) custom-call(s32[6]{0:T(128)S(1)} %pad_add_fusion.info_ref, ...), custom_call_target="tpu_custom_call" | custom-call | flops 12000000000 | bytes 13000000 | tf_op jit(solution)/shard_map/feed/pallas_call | solution.py:784
  128.8 2.5 %collective-permute-start.22 = (bf16[2,128,160]{2,1,0:T(8,128)(2,1)S(1)}, bf16[2,128,160]{2,1,0:T(8,128)(2,1)S(1)}, u32[]{:S(2)}, u32[]{:S(2)}) collective-permute-start(bf16[2,128,160]{2,1,0:T(8,128)(2,1)S(1)} %get-tuple-element.129), channel_id=1, source_target_pairs={{0,5},{1,4},{4,1},{5,0},{2,7},{3,6},{6,3},{7,2},{8,13},{9,12},{12,... | collective-permute-start | bytes 245768 | tf_op jit(solution)/shard_map/ppermute | solution.py:350
  131.3 4.4 %grads.1 = (bf16[2,3,2,40,1280]{4,3,2,1,0:T(8,128)(2,1)S(1)}, bf16[2,3,2,40,1280]{4,3,2,1,0:T(8,128)(2,1)}, bf16[2,3,2,40,1280]{4,3,2,1,0:T(8,128)(2,1)S(1)}, bf16[2,3,2,40,1280]{4,3,2,1,0:T(8,128)(2,1)}) custom-call(s32[6]{0:T(128)S(1)} %pad_add_fusion.info_ref, bf16[4,128,1280]{2,1,0:T(8,128)(2,1)S(1)} %get-tuple-element.120.pack_ref, ...), custom_call_target="tpu_custom_call" | custom-call | flops 6000000000 | bytes 8000000 | tf_op jit(solution)/shard_map/grads/pallas_call | solution.py:803
  135.8 1.0 copy-done.8
  137.0 1.4 collective-permute-start.24
  138.9 12.9 %attend_back.1 = (bf16[4,128,1280]{2,1,0:T(8,128)(2,1)S(1)}, bf16[4,128,1280]{2,1,0:T(8,128)(2,1)S(1)}, bf16[4,336,480]{2,1,0:T(8,128)(2,1)}) custom-call(s32[6]{0:T(128)S(1)} %pad_add_fusion.info_ref, bf16[4,136,1280]{2,1,0:T(8,128)(2,1)} %pad_maximum_fusion.near_ref, bf16[4,136,1280]{2,1,0:T(8,128)(2,1)} %collective-permute-done.6.far_ref, ...), custom_call_target="tpu_custom_call" | custom-call | flops 15000000512 | bytes 12000000 | tf_op jit(solution)/shard_map/attend_back/pallas_call | solution.py:817
  152.9 1.5 collective-permute-start.27
  154.9 3.3 %collective-permute-done.27 = bf16[4,8,1280]{2,1,0:T(8,128)(2,1)S(1)} collective-permute-done((bf16[4,8,1280]{2,1,0:T(8,128)(2,1)S(1)}, bf16[4,8,1280]{2,1,0:T(8,128)(2,1)S(1)}, u32[]{:S(2)}, u32[]{:S(2)}) %collective-permute-start.27) | collective-permute-done | bytes 81952 | tf_op jit(solution)/shard_map/ppermute | solution.py:358
  158.3 3.4 %collective-permute-done.26 = bf16[4,8,1280]{2,1,0:T(8,128)(2,1)S(1)} collective-permute-done((bf16[4,8,1280]{2,1,0:T(8,128)(2,1)S(1)}, bf16[4,8,1280]{2,1,0:T(8,128)(2,1)S(1)}, u32[]{:S(2)}, u32[]{:S(2)}) %collective-permute-start.26) | collective-permute-done | bytes 81952 | tf_op jit(solution)/shard_map/ppermute | solution.py:358
  161.6 5.2 %collective-permute-done.24.from_a = bf16[2,3,2,40,1280]{4,3,2,1,0:T(8,128)(2,1)} collective-permute-done((bf16[2,3,2,40,1280]{4,3,2,1,0:T(8,128)(2,1)}, bf16[2,3,2,40,1280]{4,3,2,1,0:T(8,128)(2,1)}, u32[]{:S(2)}, u32[]{:S(2)}) %collective-permute-start.24) | collective-permute-done | bytes 1228832 | tf_op jit(solution)/shard_map/ppermute | solution.py:347
  166.8 1.0 collective-permute-done.25.from_b
  168.3 1.2 collective-permute-start.31
  169.5 1.3 copy-done.7
  170.8 2.3 meet.2
  173.2 1.0 collective-permute-start.29
  174.1 1.0 collective-permute-start.30
  175.1 2.3 meet.3
  177.5 3.4 %collective-permute-done.31 = bf16[4,8,1280]{2,1,0:T(8,128)(2,1)S(1)} collective-permute-done((bf16[4,8,1280]{2,1,0:T(8,128)(2,1)S(1)}, bf16[4,8,1280]{2,1,0:T(8,128)(2,1)S(1)}, u32[]{:S(2)}, u32[]{:S(2)}) %collective-permute-start.31) | collective-permute-done | bytes 81952 | tf_op jit(solution)/shard_map/ppermute | solution.py:358
  181.7 1.6 fusion.3
  183.3 5.9 %collective-permute-done.29.from_a = bf16[2,3,40,1280]{3,2,1,0:T(8,128)(2,1)S(1)} collective-permute-done((bf16[2,3,40,1280]{3,2,1,0:T(8,128)(2,1)S(1)}, bf16[2,3,40,1280]{3,2,1,0:T(8,128)(2,1)S(1)}, u32[]{:S(2)}, u32[]{:S(2)}) %collective-permute-start.29) | collective-permute-done | bytes 614432 | tf_op jit(solution)/shard_map/ppermute | solution.py:349
  189.8 1.3 join.1
  191.2 1.1 collective-permute-start.32
  192.3 1.1 collective-permute-start.33
  193.4 1.4 collective-permute-start.34
  194.8 7.2 %collective-permute-done.32.hid_1 = bf16[128,1280]{1,0:T(8,128)(2,1)S(1)} collective-permute-done((bf16[128,1280]{1,0:T(8,128)(2,1)S(1)}, bf16[128,1280]{1,0:T(8,128)(2,1)S(1)}, u32[]{:S(2)}, u32[]{:S(2)}) %collective-permute-start.32) | collective-permute-done | bytes 327712 | tf_op jit(solution)/shard_map/ppermute | solution.py:347
  201.9 1.0 copy-done.5
  203.8 3.5 %all-to-all-start.2 = ((bf16[8,48,480]{2,1,0:T(8,128)(2,1)}), bf16[8,48,480]{2,1,0:T(8,128)(2,1)S(1)}, u32[]{:S(2)}, u32[]{:S(2)}) async-start(bf16[8,48,480]{2,1,0:T(8,128)(2,1)} %fold.1), calls=%async_computation.3 | async-start | bytes 786432 | tf_op jit(solution)/shard_map/all_to_all | solution.py:906
  207.8 1.1 copy-done.10
  208.9 1.0 norm.1
  210.3 1.7 collective-permute-start.36
  212.0 1.4 collective-permute-start.37
  213.4 4.1 %collective-permute-done.35 = bf16[4,8,1280]{2,1,0:T(8,128)(2,1)S(1)} collective-permute-done((bf16[4,8,1280]{2,1,0:T(8,128)(2,1)S(1)}, bf16[4,8,1280]{2,1,0:T(8,128)(2,1)S(1)}, u32[]{:S(2)}, u32[]{:S(2)}) %collective-permute-start.35) | collective-permute-done | bytes 81952 | tf_op jit(solution)/shard_map/ppermute | solution.py:358
  217.5 7.9 %collective-permute-done.36 = bf16[4,8,1280]{2,1,0:T(8,128)(2,1)S(1)} collective-permute-done((bf16[4,8,1280]{2,1,0:T(8,128)(2,1)S(1)}, bf16[4,8,1280]{2,1,0:T(8,128)(2,1)S(1)}, u32[]{:S(2)}, u32[]{:S(2)}) %collective-permute-start.36) | collective-permute-done | bytes 81952 | tf_op jit(solution)/shard_map/ppermute | solution.py:358
  227.8 1.0 copy-done.2
  (170 shorter events, 22.1 us)
Async XLA Ops:
  7.2 3.1 %copy-start.23 = (f32[40]{0:T(128)S(1)}, f32[40]{0:T(128)}, u32[]{:S(2)}) copy-start(f32[40]{0:T(128)} %param.23) | copy-start | bytes 484
  7.2 3.1 %copy-start.18 = (f32[40,1280]{1,0:T(8,128)S(1)}, f32[40,1280]{1,0:T(8,128)}, u32[]{:S(2)}) copy-start(f32[40,1280]{1,0:T(8,128)} %param.17) | copy-start | bytes 614404
  7.2 3.2 %copy-start.21 = (f32[40]{0:T(128)S(1)}, f32[40]{0:T(128)}, u32[]{:S(2)}) copy-start(f32[40]{0:T(128)} %param.25) | copy-start | bytes 484
  7.2 3.2 %copy-start.22 = (f32[40]{0:T(128)S(1)}, f32[40]{0:T(128)}, u32[]{:S(2)}) copy-start(f32[40]{0:T(128)} %param.24) | copy-start | bytes 484
  7.2 3.2 %copy-start.19 = (f32[40,1280]{1,0:T(8,128)S(1)}, f32[40,1280]{1,0:T(8,128)}, u32[]{:S(2)}) copy-start(f32[40,1280]{1,0:T(8,128)} %param.19) | copy-start | bytes 614404
  7.2 3.2 %copy-start.20 = (f32[40,1280]{1,0:T(8,128)S(1)}, f32[40,1280]{1,0:T(8,128)}, u32[]{:S(2)}) copy-start(f32[40,1280]{1,0:T(8,128)} %param.18) | copy-start | bytes 614404
  7.2 39.9 %all-gather.3.cloned.1.call-start = ((), (), s32[]{:S(2)}) async-start(), calls=%async_computation.5 | async-start | bytes 1536000 | tf_op jit(solution)/shard_map/all_gather | solution.py:720
  10.7 8.4 %collective-permute-start = (bf16[5,8,1280]{2,1,0:T(8,128)(2,1)S(1)}, bf16[5,8,1280]{2,1,0:T(8,128)(2,1)S(1)}, u32[]{:S(2)}, u32[]{:S(2)}) collective-permute-start(bf16[5,8,1280]{2,1,0:T(8,128)(2,1)S(1)} %get-tuple-element.100), channel_id=1, source_target_pairs={{0,24},{8,0},{16,8},{24,16},{1,25},{9,1},{17,9},{25,17},{2,26},{10... | collective-permute-start | bytes 307208 | tf_op jit(solution)/shard_map/ppermute | solution.py:358
  15.8 10.7 %collective-permute-start.1 = (bf16[5,8,1280]{2,1,0:T(8,128)(2,1)S(1)}, bf16[5,8,1280]{2,1,0:T(8,128)(2,1)S(1)}, u32[]{:S(2)}, u32[]{:S(2)}) collective-permute-start(bf16[5,8,1280]{2,1,0:T(8,128)(2,1)S(1)} %get-tuple-element.101), channel_id=1, source_target_pairs={{0,16},{8,24},{16,0},{24,8},{1,17},{9,25},{17,1},{25,9},{2,18},{10... | collective-permute-start | bytes 307208 | tf_op jit(solution)/shard_map/ppermute | solution.py:358
  15.8 10.7 %collective-permute-start.2 = (bf16[5,8,1280]{2,1,0:T(8,128)(2,1)S(1)}, bf16[5,8,1280]{2,1,0:T(8,128)(2,1)S(1)}, u32[]{:S(2)}, u32[]{:S(2)}) collective-permute-start(bf16[5,8,1280]{2,1,0:T(8,128)(2,1)S(1)} %get-tuple-element.102), channel_id=1, source_target_pairs={{0,8},{8,16},{16,24},{24,0},{1,9},{9,17},{17,25},{25,1},{2,10},{10... | collective-permute-start | bytes 307208 | tf_op jit(solution)/shard_map/ppermute | solution.py:358
  27.0 10.2 %collective-permute-start.4 = (bf16[136,1280]{1,0:T(8,128)(2,1)S(1)}, bf16[136,1280]{1,0:T(8,128)(2,1)S(1)}, u32[]{:S(2)}, u32[]{:S(2)}) collective-permute-start(bf16[136,1280]{1,0:T(8,128)(2,1)S(1)} %get-tuple-element.188), channel_id=1, source_target_pairs={{0,4},{4,0},{1,5},{5,1},{2,6},{6,2},{3,7},{7,3},{8,12},{12,8},{9,1... | collective-permute-start | bytes 1044488 | tf_op jit(solution)/shard_map/ppermute | solution.py:349
  28.7 11.1 %collective-permute-start.3 = (bf16[136,1280]{1,0:T(8,128)(2,1)S(1)}, bf16[136,1280]{1,0:T(8,128)(2,1)S(1)}, u32[]{:S(2)}, u32[]{:S(2)}) collective-permute-start(bf16[136,1280]{1,0:T(8,128)(2,1)S(1)} %get-tuple-element.188), channel_id=1, source_target_pairs={{0,1},{1,0},{2,3},{3,2},{4,5},{5,4},{6,7},{7,6},{8,9},{9,8},{10,11... | collective-permute-start | bytes 1044488 | tf_op jit(solution)/shard_map/ppermute | solution.py:347
  30.2 15.2 %collective-permute-start.5 = (bf16[136,1280]{1,0:T(8,128)(2,1)S(1)}, bf16[136,1280]{1,0:T(8,128)(2,1)S(1)}, u32[]{:S(2)}, u32[]{:S(2)}) collective-permute-start(bf16[136,1280]{1,0:T(8,128)(2,1)S(1)} %get-tuple-element.188), channel_id=1, source_target_pairs={{0,5},{1,4},{4,1},{5,0},{2,7},{3,6},{6,3},{7,2},{8,13},{9,12},{12,... | collective-permute-start | bytes 1044488 | tf_op jit(solution)/shard_map/ppermute | solution.py:350
  32.7 14.4 %all-to-all-start = ((bf16[8,40,480]{2,1,0:T(8,128)(2,1)}), bf16[8,40,480]{2,1,0:T(8,128)(2,1)S(1)}, u32[]{:S(2)}, u32[]{:S(2)}) async-start(bf16[8,40,480]{2,1,0:T(8,128)(2,1)} %reshape.336), calls=%async_computation | async-start | bytes 655360 | tf_op jit(solution)/shard_map/all_to_all | solution.py:723
  36.5 54.3 %all-gather.5.cloned.1.call-start = ((), (), s32[]{:S(2)}) async-start(), calls=%async_computation.6 | async-start | bytes 1638400 | tf_op jit(solution)/shard_map/all_gather | solution.py:726
  45.4 4.5 %copy-start.24 = (s32[16]{0:T(128)S(1)}, s32[16]{0:T(128)}, u32[]{:S(2)}) copy-start(s32[16]{0:T(128)} %param.27) | copy-start | bytes 196
  45.4 4.5 %copy-start.25 = (s32[16]{0:T(128)S(1)}, s32[16]{0:T(128)}, u32[]{:S(2)}) copy-start(s32[16]{0:T(128)} %param.26) | copy-start | bytes 196
  47.1 2.8 %copy-start.14 = (bf16[8,40,480]{2,1,0:T(8,128)(2,1)}, bf16[8,40,480]{2,1,0:T(8,128)(2,1)S(1)}, u32[]{:S(2)}) copy-start(bf16[8,40,480]{2,1,0:T(8,128)(2,1)S(1)} %all-to-all-done) | copy-start | bytes 921604
  47.1 29.3 %collective-permute-start.7 = (bf16[4,3,40,1280]{3,2,1,0:T(8,128)(2,1)}, bf16[4,3,40,1280]{3,2,1,0:T(8,128)(2,1)S(1)}, u32[]{:S(2)}, u32[]{:S(2)}) collective-permute-start(bf16[4,3,40,1280]{3,2,1,0:T(8,128)(2,1)} %all-gather.3.cloned.1.call-done), channel_id=1, source_target_pairs={{0,1},{1,0},{2,3},{3,2},{4,5},{5,4},{6,7},{7,6},{8,9},{9,8},{10,11... | collective-permute-start | bytes 3686408 | tf_op jit(solution)/shard_map/ppermute | solution.py:347
  48.6 28.9 %collective-permute-start.8 = (bf16[4,3,40,1280]{3,2,1,0:T(8,128)(2,1)}, bf16[4,3,40,1280]{3,2,1,0:T(8,128)(2,1)}, u32[]{:S(2)}, u32[]{:S(2)}) collective-permute-start(bf16[4,3,40,1280]{3,2,1,0:T(8,128)(2,1)} %all-gather.3.cloned.1.call-done), channel_id=1, source_target_pairs={{0,4},{4,0},{1,5},{5,1},{2,6},{6,2},{3,7},{7,3},{8,12},{12,8},{9,1... | collective-permute-start | bytes 3686408 | tf_op jit(solution)/shard_map/ppermute | solution.py:349
  49.7 33.9 %collective-permute-start.6 = (bf16[4,136,1280]{2,1,0:T(8,128)(2,1)}, bf16[4,136,1280]{2,1,0:T(8,128)(2,1)}, u32[]{:S(2)}, u32[]{:S(2)}) collective-permute-start(bf16[4,136,1280]{2,1,0:T(8,128)(2,1)} %pad_maximum_fusion.near_ref), channel_id=1, source_target_pairs={{0,2},{2,0},{1,3},{3,1},{4,6},{6,4},{5,7},{7,5},{8,10},{10,8},{9,1... | collective-permute-start | bytes 4177928 | tf_op jit(solution)/shard_map/ppermute | solution.py:354
  50.9 28.9 %all-to-all-start.1 = ((bf16[4,4,8,1280]{3,2,1,0:T(8,128)(2,1)}), bf16[4,4,8,1280]{3,2,1,0:T(8,128)(2,1)S(1)}, u32[]{:S(2)}, u32[]{:S(2)}) async-start(bf16[4,4,8,1280]{3,2,1,0:T(8,128)(2,1)} %bitcast.29), calls=%async_computation.1 | async-start | bytes 655360 | tf_op jit(solution)/shard_map/all_to_all | solution.py:730
  58.5 143.5 %reduce-scatter.3.cloned.1.call-start = ((), (), s32[]{:S(2)}) async-start(), calls=%async_computation.7 | async-start | bytes 1720320 | tf_op jit(solution)/shard_map/reduce_scatter | solution.py:849
  76.3 3.4 %copy-start.13 = (bf16[4,3,40,1280]{3,2,1,0:T(8,128)(2,1)}, bf16[4,3,40,1280]{3,2,1,0:T(8,128)(2,1)S(1)}, u32[]{:S(2)}) copy-start(bf16[4,3,40,1280]{3,2,1,0:T(8,128)(2,1)S(1)} %collective-permute-done.7) | copy-start | bytes 3686404
  79.8 21.2 %collective-permute-start.10 = (bf16[2,3,40,1280]{3,2,1,0:T(8,128)(2,1)}, bf16[2,3,40,1280]{3,2,1,0:T(8,128)(2,1)}, u32[]{:S(2)}, u32[]{:S(2)}) collective-permute-start(bf16[2,3,40,1280]{3,2,1,0:T(8,128)(2,1)} %slice.174), channel_id=1, source_target_pairs={{0,4},{4,0},{1,5},{5,1},{2,6},{6,2},{3,7},{7,3},{8,12},{12,8},{9,1... | collective-permute-start | bytes 1843208 | tf_op jit(solution)/shard_map/ppermute | solution.py:349
  80.5 20.5 %collective-permute-start.11 = (bf16[2,3,40,1280]{3,2,1,0:T(8,128)(2,1)}, bf16[2,3,40,1280]{3,2,1,0:T(8,128)(2,1)}, u32[]{:S(2)}, u32[]{:S(2)}) collective-permute-start(bf16[2,3,40,1280]{3,2,1,0:T(8,128)(2,1)} %get-tuple-element.113), channel_id=1, source_target_pairs={{0,1},{1,0},{2,3},{3,2},{4,5},{5,4},{6,7},{7,6},{8,9},{9,8},{10,11... | collective-permute-start | bytes 1843208 | tf_op jit(solution)/shard_map/ppermute | solution.py:347
  90.9 1.3 copy-start.3
  99.7 1.3 copy-start.11
  101.0 18.0 %collective-permute-start.16 = (bf16[4,3,80,1280]{3,2,1,0:T(8,128)(2,1)S(1)}, bf16[4,3,80,1280]{3,2,1,0:T(8,128)(2,1)}, u32[]{:S(2)}, u32[]{:S(2)}) collective-permute-start(bf16[4,3,80,1280]{3,2,1,0:T(8,128)(2,1)S(1)} %bitcast_select_fusion.near_rows), channel_id=1, source_target_pairs={{0,2},{2,0},{1,3},{3,1},{4,6},{6,4},{5,7},{7,5},{8,10},{10,8},{9,1... | collective-permute-start | bytes 7372808 | tf_op jit(solution)/shard_map/ppermute | solution.py:354
  101.1 11.2 %copy-start.16 = (bf16[4,4,8,1280]{3,2,1,0:T(8,128)(2,1)S(1)}, bf16[4,4,8,1280]{3,2,1,0:T(8,128)(2,1)}, u32[]{:S(2)}) copy-start(bf16[4,4,8,1280]{3,2,1,0:T(8,128)(2,1)} %copy-done.15) | copy-start | bytes 983044
  104.3 14.7 %collective-permute-start.18 = (bf16[2,3,80,1280]{3,2,1,0:T(8,128)(2,1)}, bf16[2,3,80,1280]{3,2,1,0:T(8,128)(2,1)}, u32[]{:S(2)}, u32[]{:S(2)}) collective-permute-start(bf16[2,3,80,1280]{3,2,1,0:T(8,128)(2,1)} %get-tuple-element.207.across_b), channel_id=1, source_target_pairs={{0,2},{2,0},{1,3},{3,1},{4,6},{6,4},{5,7},{7,5},{8,10},{10,8},{9,1... | collective-permute-start | bytes 3686408 | tf_op jit(solution)/shard_map/ppermute | solution.py:354
  104.8 14.3 %collective-permute-start.17 = (bf16[2,3,80,1280]{3,2,1,0:T(8,128)(2,1)}, bf16[2,3,80,1280]{3,2,1,0:T(8,128)(2,1)}, u32[]{:S(2)}, u32[]{:S(2)}) collective-permute-start(bf16[2,3,80,1280]{3,2,1,0:T(8,128)(2,1)} %get-tuple-element.208.across_a), channel_id=1, source_target_pairs={{0,2},{2,0},{1,3},{3,1},{4,6},{6,4},{5,7},{7,5},{8,10},{10,8},{9,1... | collective-permute-start | bytes 3686408 | tf_op jit(solution)/shard_map/ppermute | solution.py:354
  104.9 6.9 %collective-permute-start.14 = (bf16[2,128,160]{2,1,0:T(8,128)(2,1)S(1)}, bf16[2,128,160]{2,1,0:T(8,128)(2,1)S(1)}, u32[]{:S(2)}, u32[]{:S(2)}) collective-permute-start(bf16[2,128,160]{2,1,0:T(8,128)(2,1)S(1)} %get-tuple-element.184), channel_id=1, source_target_pairs={{0,5},{1,4},{4,1},{5,0},{2,7},{3,6},{6,3},{7,2},{8,13},{9,12},{12,... | collective-permute-start | bytes 245768 | tf_op jit(solution)/shard_map/ppermute | solution.py:350
  105.4 8.4 %collective-permute-start.13 = (bf16[2,128,160]{2,1,0:T(8,128)(2,1)S(1)}, bf16[2,128,160]{2,1,0:T(8,128)(2,1)S(1)}, u32[]{:S(2)}, u32[]{:S(2)}) collective-permute-start(bf16[2,128,160]{2,1,0:T(8,128)(2,1)S(1)} %get-tuple-element.185), channel_id=1, source_target_pairs={{0,4},{4,0},{1,5},{5,1},{2,6},{6,2},{3,7},{7,3},{8,12},{12,8},{9,1... | collective-permute-start | bytes 245768 | tf_op jit(solution)/shard_map/ppermute | solution.py:349
  111.8 5.0 %collective-permute-start.12 = (bf16[2,128,160]{2,1,0:T(8,128)(2,1)S(1)}, bf16[2,128,160]{2,1,0:T(8,128)(2,1)S(1)}, u32[]{:S(2)}, u32[]{:S(2)}) collective-permute-start(bf16[2,128,160]{2,1,0:T(8,128)(2,1)S(1)} %get-tuple-element.186), channel_id=1, source_target_pairs={{0,1},{1,0},{2,3},{3,2},{4,5},{5,4},{6,7},{7,6},{8,9},{9,8},{10,11... | collective-permute-start | bytes 245768 | tf_op jit(solution)/shard_map/ppermute | solution.py:347
  113.8 3.3 %collective-permute-start.9 = (bf16[128,1280]{1,0:T(8,128)(2,1)}, bf16[128,1280]{1,0:T(8,128)(2,1)}, u32[]{:S(2)}, u32[]{:S(2)}) collective-permute-start(bf16[128,1280]{1,0:T(8,128)(2,1)} %bitcast.31.g_ref.cot_ref), channel_id=1, source_target_pairs={{0,2},{2,0},{1,3},{3,1},{4,6},{6,4},{5,7},{7,5},{8,10},{10,8},{9,1... | collective-permute-start | bytes 983048 | tf_op jit(solution)/shard_map/ppermute | solution.py:354
  116.9 2.1 collective-permute-start.15
  127.6 8.2 %copy-start = (bf16[4,4,8,1280]{3,2,1,0:T(8,128)(2,1)}, bf16[4,4,8,1280]{3,2,1,0:T(8,128)(2,1)S(1)}, u32[]{:S(2)}) copy-start(bf16[4,4,8,1280]{3,2,1,0:T(8,128)(2,1)S(1)} %get-tuple-element.144) | copy-start | bytes 983044
  127.6 8.2 %copy-start.9 = (f32[128,1280]{1,0:T(8,128)}, f32[128,1280]{1,0:T(8,128)S(1)}, u32[]{:S(2)}) copy-start(f32[128,1280]{1,0:T(8,128)S(1)} %get-tuple-element.161.dmid_ref) | copy-start | bytes 1966084
  127.6 3.7 %collective-permute-start.19 = (bf16[4,128,1280]{2,1,0:T(8,128)(2,1)S(1)}, bf16[4,128,1280]{2,1,0:T(8,128)(2,1)S(1)}, u32[]{:S(2)}, u32[]{:S(2)}) collective-permute-start(bf16[4,128,1280]{2,1,0:T(8,128)(2,1)S(1)} %get-tuple-element.120.pack_ref), channel_id=1, source_target_pairs={{0,2},{2,0},{1,3},{3,1},{4,6},{6,4},{5,7},{7,5},{8,10},{10,8},{9,1... | collective-permute-start | bytes 3932168 | tf_op jit(solution)/shard_map/ppermute | solution.py:354
  127.8 9.0 %collective-permute-start.20 = (bf16[2,128,160]{2,1,0:T(8,128)(2,1)S(1)}, bf16[2,128,160]{2,1,0:T(8,128)(2,1)S(1)}, u32[]{:S(2)}, u32[]{:S(2)}) collective-permute-start(bf16[2,128,160]{2,1,0:T(8,128)(2,1)S(1)} %get-tuple-element.127), channel_id=1, source_target_pairs={{0,1},{1,0},{2,3},{3,2},{4,5},{5,4},{6,7},{7,6},{8,9},{9,8},{10,11... | collective-permute-start | bytes 245768 | tf_op jit(solution)/shard_map/ppermute | solution.py:347
  128.3 8.5 %collective-permute-start.21 = (bf16[2,128,160]{2,1,0:T(8,128)(2,1)S(1)}, bf16[2,128,160]{2,1,0:T(8,128)(2,1)S(1)}, u32[]{:S(2)}, u32[]{:S(2)}) collective-permute-start(bf16[2,128,160]{2,1,0:T(8,128)(2,1)S(1)} %get-tuple-element.128), channel_id=1, source_target_pairs={{0,4},{4,0},{1,5},{5,1},{2,6},{6,2},{3,7},{7,3},{8,12},{12,8},{9,1... | collective-permute-start | bytes 245768 | tf_op jit(solution)/shard_map/ppermute | solution.py:349
  128.8 10.1 %copy-start.4 = (bf16[1280,480]{1,0:T(8,128)(2,1)S(1)}, bf16[1280,480]{1,0:T(8,128)(2,1)}, u32[]{:S(2)}) copy-start(bf16[1280,480]{1,0:T(8,128)(2,1)} %all-gather.5.cloned.1.call-done.w_ref) | copy-start | bytes 3686404
  128.8 10.1 %copy-start.12 = (f32[2,4,128,480]{3,2,1,0:T(8,128)S(1)}, f32[2,4,128,480]{3,2,1,0:T(8,128)}, u32[]{:S(2)}) copy-start(f32[2,4,128,480]{3,2,1,0:T(8,128)} %copy-done.11) | copy-start | bytes 5898244
  128.8 8.0 %collective-permute-start.22 = (bf16[2,128,160]{2,1,0:T(8,128)(2,1)S(1)}, bf16[2,128,160]{2,1,0:T(8,128)(2,1)S(1)}, u32[]{:S(2)}, u32[]{:S(2)}) collective-permute-start(bf16[2,128,160]{2,1,0:T(8,128)(2,1)S(1)} %get-tuple-element.129), channel_id=1, source_target_pairs={{0,5},{1,4},{4,1},{5,0},{2,7},{3,6},{6,3},{7,2},{8,13},{9,12},{12,... | collective-permute-start | bytes 245768 | tf_op jit(solution)/shard_map/ppermute | solution.py:350
  136.8 15.1 %copy-start.6 = (bf16[2,3,2,40,1280]{4,3,2,1,0:T(8,128)(2,1)}, bf16[2,3,2,40,1280]{4,3,2,1,0:T(8,128)(2,1)S(1)}, u32[]{:S(2)}) copy-start(bf16[2,3,2,40,1280]{4,3,2,1,0:T(8,128)(2,1)S(1)} %get-tuple-element.146.mine_a) | copy-start | bytes 3686404
  136.9 2.0 collective-permute-start.23
  137.0 29.8 %collective-permute-start.24 = (bf16[2,3,2,40,1280]{4,3,2,1,0:T(8,128)(2,1)}, bf16[2,3,2,40,1280]{4,3,2,1,0:T(8,128)(2,1)}, u32[]{:S(2)}, u32[]{:S(2)}) collective-permute-start(bf16[2,3,2,40,1280]{4,3,2,1,0:T(8,128)(2,1)} %get-tuple-element.139), channel_id=1, source_target_pairs={{0,1},{1,0},{2,3},{3,2},{4,5},{5,4},{6,7},{7,6},{8,9},{9,8},{10,11... | collective-permute-start | bytes 3686408 | tf_op jit(solution)/shard_map/ppermute | solution.py:347
  138.4 29.4 %collective-permute-start.25 = (bf16[2,3,2,40,1280]{4,3,2,1,0:T(8,128)(2,1)}, bf16[2,3,2,40,1280]{4,3,2,1,0:T(8,128)(2,1)}, u32[]{:S(2)}, u32[]{:S(2)}) collective-permute-start(bf16[2,3,2,40,1280]{4,3,2,1,0:T(8,128)(2,1)} %get-tuple-element.140), channel_id=1, source_target_pairs={{0,4},{4,0},{1,5},{5,1},{2,6},{6,2},{3,7},{7,3},{8,12},{12,8},{9,1... | collective-permute-start | bytes 3686408 | tf_op jit(solution)/shard_map/ppermute | solution.py:349
  151.9 75.9 %reduce-scatter.5.cloned.1.call-start = ((), (), s32[]{:S(2)}) async-start(), calls=%async_computation.8 | async-start | bytes 1536000 | tf_op jit(solution)/shard_map/reduce_scatter | solution.py:885
  152.9 5.4 %collective-permute-start.27 = (bf16[4,8,1280]{2,1,0:T(8,128)(2,1)S(1)}, bf16[4,8,1280]{2,1,0:T(8,128)(2,1)S(1)}, u32[]{:S(2)}, u32[]{:S(2)}) collective-permute-start(bf16[4,8,1280]{2,1,0:T(8,128)(2,1)S(1)} %get-tuple-element.191), channel_id=1, source_target_pairs={{0,24},{8,0},{16,8},{24,16},{1,25},{9,1},{17,9},{25,17},{2,26},{10... | collective-permute-start | bytes 245768 | tf_op jit(solution)/shard_map/ppermute | solution.py:358
  154.4 7.2 %collective-permute-start.26 = (bf16[4,8,1280]{2,1,0:T(8,128)(2,1)S(1)}, bf16[4,8,1280]{2,1,0:T(8,128)(2,1)S(1)}, u32[]{:S(2)}, u32[]{:S(2)}) collective-permute-start(bf16[4,8,1280]{2,1,0:T(8,128)(2,1)S(1)} %get-tuple-element.192), channel_id=1, source_target_pairs={{0,8},{8,16},{16,24},{24,0},{1,9},{9,17},{17,25},{25,1},{2,10},{10... | collective-permute-start | bytes 245768 | tf_op jit(solution)/shard_map/ppermute | solution.py:358
  167.8 13.9 %collective-permute-start.28 = (bf16[4,128,1280]{2,1,0:T(8,128)(2,1)S(1)}, bf16[4,128,1280]{2,1,0:T(8,128)(2,1)}, u32[]{:S(2)}, u32[]{:S(2)}) collective-permute-start(bf16[4,128,1280]{2,1,0:T(8,128)(2,1)S(1)} %get-tuple-element.145), channel_id=1, source_target_pairs={{0,2},{2,0},{1,3},{3,1},{4,6},{6,4},{5,7},{7,5},{8,10},{10,8},{9,1... | collective-permute-start | bytes 3932168 | tf_op jit(solution)/shard_map/ppermute | solution.py:354
  168.3 12.6 %collective-permute-start.31 = (bf16[4,8,1280]{2,1,0:T(8,128)(2,1)S(1)}, bf16[4,8,1280]{2,1,0:T(8,128)(2,1)S(1)}, u32[]{:S(2)}, u32[]{:S(2)}) collective-permute-start(bf16[4,8,1280]{2,1,0:T(8,128)(2,1)S(1)} %get-tuple-element.189), channel_id=1, source_target_pairs={{0,16},{8,24},{16,0},{24,8},{1,17},{9,25},{17,1},{25,9},{2,18},{10... | collective-permute-start | bytes 245768 | tf_op jit(solution)/shard_map/ppermute | solution.py:358
  169.5 1.3 copy-start.7
  173.2 16.1 %collective-permute-start.29 = (bf16[2,3,40,1280]{3,2,1,0:T(8,128)(2,1)S(1)}, bf16[2,3,40,1280]{3,2,1,0:T(8,128)(2,1)S(1)}, u32[]{:S(2)}, u32[]{:S(2)}) collective-permute-start(bf16[2,3,40,1280]{3,2,1,0:T(8,128)(2,1)S(1)} %get-tuple-element.150), channel_id=1, source_target_pairs={{0,4},{4,0},{1,5},{5,1},{2,6},{6,2},{3,7},{7,3},{8,12},{12,8},{9,1... | collective-permute-start | bytes 1843208 | tf_op jit(solution)/shard_map/ppermute | solution.py:349
  174.1 15.7 %collective-permute-start.30 = (bf16[2,3,40,1280]{3,2,1,0:T(8,128)(2,1)S(1)}, bf16[2,3,40,1280]{3,2,1,0:T(8,128)(2,1)S(1)}, u32[]{:S(2)}, u32[]{:S(2)}) collective-permute-start(bf16[2,3,40,1280]{3,2,1,0:T(8,128)(2,1)S(1)} %get-tuple-element.151), channel_id=1, source_target_pairs={{0,1},{1,0},{2,3},{3,2},{4,5},{5,4},{6,7},{7,6},{8,9},{9,8},{10,11... | collective-permute-start | bytes 1843208 | tf_op jit(solution)/shard_map/ppermute | solution.py:347
  191.2 10.7 %collective-permute-start.32 = (bf16[128,1280]{1,0:T(8,128)(2,1)S(1)}, bf16[128,1280]{1,0:T(8,128)(2,1)S(1)}, u32[]{:S(2)}, u32[]{:S(2)}) collective-permute-start(bf16[128,1280]{1,0:T(8,128)(2,1)S(1)} %get-tuple-element.156), channel_id=1, source_target_pairs={{0,1},{1,0},{2,3},{3,2},{4,5},{5,4},{6,7},{7,6},{8,9},{9,8},{10,11... | collective-permute-start | bytes 983048 | tf_op jit(solution)/shard_map/ppermute | solution.py:347
  192.3 15.5 %collective-permute-start.33 = (bf16[128,1280]{1,0:T(8,128)(2,1)S(1)}, bf16[128,1280]{1,0:T(8,128)(2,1)S(1)}, u32[]{:S(2)}, u32[]{:S(2)}) collective-permute-start(bf16[128,1280]{1,0:T(8,128)(2,1)S(1)} %get-tuple-element.159), channel_id=1, source_target_pairs={{0,4},{4,0},{1,5},{5,1},{2,6},{6,2},{3,7},{7,3},{8,12},{12,8},{9,1... | collective-permute-start | bytes 983048 | tf_op jit(solution)/shard_map/ppermute | solution.py:349
  193.4 14.4 %collective-permute-start.34 = (bf16[128,1280]{1,0:T(8,128)(2,1)S(1)}, bf16[128,1280]{1,0:T(8,128)(2,1)S(1)}, u32[]{:S(2)}, u32[]{:S(2)}) collective-permute-start(bf16[128,1280]{1,0:T(8,128)(2,1)S(1)} %get-tuple-element.160), channel_id=1, source_target_pairs={{0,5},{1,4},{4,1},{5,0},{2,7},{3,6},{6,3},{7,2},{8,13},{9,12},{12,... | collective-permute-start | bytes 983048 | tf_op jit(solution)/shard_map/ppermute | solution.py:350
  203.8 22.5 %all-to-all-start.2 = ((bf16[8,48,480]{2,1,0:T(8,128)(2,1)}), bf16[8,48,480]{2,1,0:T(8,128)(2,1)S(1)}, u32[]{:S(2)}, u32[]{:S(2)}) async-start(bf16[8,48,480]{2,1,0:T(8,128)(2,1)} %fold.1), calls=%async_computation.3 | async-start | bytes 786432 | tf_op jit(solution)/shard_map/all_to_all | solution.py:906
  209.9 7.6 %collective-permute-start.35 = (bf16[4,8,1280]{2,1,0:T(8,128)(2,1)S(1)}, bf16[4,8,1280]{2,1,0:T(8,128)(2,1)S(1)}, u32[]{:S(2)}, u32[]{:S(2)}) collective-permute-start(bf16[4,8,1280]{2,1,0:T(8,128)(2,1)S(1)} %get-tuple-element.162), channel_id=1, source_target_pairs={{0,24},{8,0},{16,8},{24,16},{1,25},{9,1},{17,9},{25,17},{2,26},{10... | collective-permute-start | bytes 245768 | tf_op jit(solution)/shard_map/ppermute | solution.py:358
  210.3 15.0 %collective-permute-start.36 = (bf16[4,8,1280]{2,1,0:T(8,128)(2,1)S(1)}, bf16[4,8,1280]{2,1,0:T(8,128)(2,1)S(1)}, u32[]{:S(2)}, u32[]{:S(2)}) collective-permute-start(bf16[4,8,1280]{2,1,0:T(8,128)(2,1)S(1)} %get-tuple-element.163), channel_id=1, source_target_pairs={{0,16},{8,24},{16,0},{24,8},{1,17},{9,25},{17,1},{25,9},{2,18},{10... | collective-permute-start | bytes 245768 | tf_op jit(solution)/shard_map/ppermute | solution.py:358
  212.0 13.3 %collective-permute-start.37 = (bf16[4,8,1280]{2,1,0:T(8,128)(2,1)S(1)}, bf16[4,8,1280]{2,1,0:T(8,128)(2,1)S(1)}, u32[]{:S(2)}, u32[]{:S(2)}) collective-permute-start(bf16[4,8,1280]{2,1,0:T(8,128)(2,1)S(1)} %get-tuple-element.164), channel_id=1, source_target_pairs={{0,8},{8,16},{16,24},{24,0},{1,9},{9,17},{17,25},{25,1},{2,10},{10... | collective-permute-start | bytes 245768 | tf_op jit(solution)/shard_map/ppermute | solution.py:358
  (7 other events, 6.9 us)
Sparse Core Ops, SparseCore 0:
  10.4 34.5 all-gather.2
  50.0 40.7 all-gather.4
  152.0 32.9 reduce-scatter.2
  191.3 33.1 reduce-scatter.4

commit v14 on v13

--- a/solution.py
+++ b/solution.py
@@ -766,8 +766,9 @@
     )(info, near, far, gain_one, query_mult, w_qkv)
 
     near_rows = pair(big, beside, x, 2).reshape(4, 3, 80, width)
-    att_made, near_rows, across_a, across_b = lax.optimization_barrier((att_made, near_rows, across_a, across_b))
-    far_near_rows = core_swap(near_rows)
+    att_made, far_near_rows, across_a, across_b = lax.optimization_barrier(
+        (att_made, core_swap(near_rows), across_a, across_b)
+    )
     atts = [att_made[0]] + [plane_shift(att_made[step], step) for step in (1, 2, 3)]
     atts = jnp.stack(atts)
     far_atts = core_swap(atts)
@@ -854,7 +855,6 @@
     )
     swapped = core_swap(hid_far)
     hid = [sum_low(hid_near[i], swapped[i]) for i in range(4)]
-    outputs = by_source([out_sent[0], out_one, ring_shift(out_sent[2], 2), out_three], z, 0).reshape(16, 8, width)
     def meet(far_side, *parts):
         return pl.pallas_call(
             functools.partial(meet_kernel, far_side),
@@ -870,7 +870,8 @@
     away_a, away_b = meet(True, *parts)
     keep_a, keep_b = meet(False, *parts)
     from_a, from_b = plane_shift(away_a, 2), plane_shift(away_b, 1)
-    *hid, from_a, from_b, outputs = lax.optimization_barrier((*hid, from_a, from_b, outputs))
+    *hid, from_a, from_b, out_sent[2] = lax.optimization_barrier((*hid, from_a, from_b, out_sent[2]))
+    out_two = ring_shift(out_sent[2], 2)
     kept = pl.pallas_call(
         join_kernel,
         in_specs=[vmem] * 4,
@@ -881,7 +882,8 @@
         name="join",
     )(keep_a, from_a, keep_b, from_b)
     moved = [plane_shift(hid[step], step) for step in (1, 2, 3)]
-    moved[0], sums = lax.optimization_barrier((moved[0], sums))
+    moved[0], sums, out_two = lax.optimization_barrier((moved[0], sums, out_two))
+    outputs = by_source([out_sent[0], out_one, out_two, out_three], z, 0).reshape(16, 8, width)
     big_sums = lax.psum_scatter(kept, "z", scatter_dimension=0, tiled=True)[0]
     grad_home = pl.pallas_call(
         norm_kernel,
@@ -915,6 +917,7 @@
     scale_low = query_scale.astype(bf16).astype(f32)
     scale_sum = LOG2E / math.sqrt(HD) * jax.nn.sigmoid(scale_low) * line_sums[2]
     grad_home = [grad_home[0]] + [ring_shift(grad_home[k], k) for k in (1, 2, 3)]
+    grad_home[2], *qkv_sums, scale_sum = lax.optimization_barrier((grad_home[2], *qkv_sums, scale_sum))
     grad_home = by_source(grad_home, z, 0).reshape(16, 8, width)
 
     return (

time: 237 us -> 235 us (level)
  waiting for transfers between devices: 95.5 us -> 89.8 us
  starting transfers between devices: 50.3 us -> 53.6 us
    ppermute x8, waiting for transfers between devices: 9.14 us -> 22.7 us  [plane_shift(): return lax.ppermute(value, 'y', [(0, 1), (1, 0)])]
    ppermute x8, waiting for transfers between devices: 36.3 us -> 24.2 us  [plane_shift(): return lax.ppermute(value, 'x', [(0, 1), (1, 0)])]
    ppermute x9, waiting for transfers between devices: 31 us -> 27.1 us  [ring_shift(): return lax.ppermute(value, 'z', [(i, (i + step) % 4) for i in range(4)])]
    ppermute x4, waiting for transfers between devices: 10.6 us -> 7.75 us  [plane_shift(): return lax.ppermute(value, ('y', 'x'), [(0, 3), (1, 2), (2, 1), (3, 0)])]
    ppermute x9, starting transfers between devices: 13 us -> 15.4 us  [ring_shift(): return lax.ppermute(value, 'z', [(i, (i + step) % 4) for i in range(4)])]
  transfers between devices with their start and end apart: 45 -> 45, of which waited for: 24 -> 23; matrix products, arithmetic and copies ran while one was open for 9% -> 8% of each run, Pallas kernels for 14% -> 14%
where the time goes in v14:
time: 235 us; the launch traced here: 234 us
  waiting for transfers between devices  89.8 us (38%)
  starting transfers between devices  53.6 us (23%)
  Pallas kernels  43 us (18%)
  local copies, waits for them, and re-layouts  19.9 us (8%)
  between operations  14.4 us (6%)
  other arithmetic  13.1 us (6%)
    ppermute x9, waiting for transfers between devices, ring_shift(): return lax.ppermute(value, 'z', [(i, (i + step) % 4) for i in range(4)])  27.1 us
    ppermute x8, waiting for transfers between devices, plane_shift(): return lax.ppermute(value, 'x', [(0, 1), (1, 0)])  24.2 us
    ppermute x8, waiting for transfers between devices, plane_shift(): return lax.ppermute(value, 'y', [(0, 1), (1, 0)])  22.7 us
    ppermute x9, starting transfers between devices, ring_shift(): return lax.ppermute(value, 'z', [(i, (i + step) % 4) for i in range(4)])  15.4 us
    pallas_call x1, Pallas kernels, planes(): pl.pallas_call(attend_back_kernel, grid_spec=pltpu.PrefetchScalarGridSpec...  12.9 us
    ppermute x8, starting transfers between devices, plane_shift(): return lax.ppermute(value, 'x', [(0, 1), (1, 0)])  9.25 us
    ppermute x8, starting transfers between devices, plane_shift(): return lax.ppermute(value, 'y', [(0, 1), (1, 0)])  9.22 us
    pallas_call x1, Pallas kernels, planes(): pl.pallas_call(feed_kernel, in_specs=[smem] + [vmem] * 5 + [hbm] * 6, out...  8.48 us
  transfers between devices with their start and end apart: 45, of which 23 were waited for; matrix products, arithmetic and copies ran while one was open for 8% of the time, Pallas kernels for 14%

profile of v14, /device:TPU:0, one launch (start us, length us, event | category | flops | bytes accessed | tf_op | source)
XLA Modules:
  0.0 233.9 jit_solution(14971669272917712969)
XLA Ops:
  7.3 1.1 convert_bitcast_fusion.2
  8.4 1.1 convert_bitcast_fusion
  10.7 5.1 %collective-permute-start = (bf16[5,8,1280]{2,1,0:T(8,128)(2,1)S(1)}, bf16[5,8,1280]{2,1,0:T(8,128)(2,1)S(1)}, u32[]{:S(2)}, u32[]{:S(2)}) collective-permute-start(bf16[5,8,1280]{2,1,0:T(8,128)(2,1)S(1)} %get-tuple-element.106), channel_id=1, source_target_pairs={{0,24},{8,0},{16,8},{24,16},{1,25},{9,1},{17,9},{25,17},{2,26},{10... | collective-permute-start | bytes 307208 | tf_op jit(solution)/shard_map/ppermute | solution.py:358
  15.8 1.0 collective-permute-start.2
  17.5 1.6 collective-permute-done
  19.1 7.4 %collective-permute-done.1 = bf16[5,8,1280]{2,1,0:T(8,128)(2,1)S(1)} collective-permute-done((bf16[5,8,1280]{2,1,0:T(8,128)(2,1)S(1)}, bf16[5,8,1280]{2,1,0:T(8,128)(2,1)S(1)}, u32[]{:S(2)}, u32[]{:S(2)}) %collective-permute-start.1) | collective-permute-done | bytes 102432 | tf_op jit(solution)/shard_map/ppermute | solution.py:358
  27.0 1.7 collective-permute-start.4
  28.6 1.5 collective-permute-start.3
  31.6 1.1 reshape.336
  32.7 3.9 %all-to-all-start = ((bf16[8,40,480]{2,1,0:T(8,128)(2,1)}), bf16[8,40,480]{2,1,0:T(8,128)(2,1)S(1)}, u32[]{:S(2)}, u32[]{:S(2)}) async-start(bf16[8,40,480]{2,1,0:T(8,128)(2,1)} %reshape.336), calls=%async_computation | async-start | bytes 655360 | tf_op jit(solution)/shard_map/all_to_all | solution.py:723
  37.2 2.5 %collective-permute-done.3 = bf16[136,1280]{1,0:T(8,128)(2,1)S(1)} collective-permute-done((bf16[136,1280]{1,0:T(8,128)(2,1)S(1)}, bf16[136,1280]{1,0:T(8,128)(2,1)S(1)}, u32[]{:S(2)}, u32[]{:S(2)}) %collective-permute-start.3) | collective-permute-done | bytes 348192 | tf_op jit(solution)/shard_map/ppermute | solution.py:347
  39.7 5.7 %collective-permute-done.5 = bf16[136,1280]{1,0:T(8,128)(2,1)S(1)} collective-permute-done((bf16[136,1280]{1,0:T(8,128)(2,1)S(1)}, bf16[136,1280]{1,0:T(8,128)(2,1)S(1)}, u32[]{:S(2)}, u32[]{:S(2)}) %collective-permute-start.5) | collective-permute-done | bytes 348192 | tf_op jit(solution)/shard_map/ppermute | solution.py:350
  45.4 1.3 pad_maximum_fusion.near_ref
  47.1 1.5 collective-permute-start.6
  48.6 1.1 collective-permute-start.7
  50.9 7.6 %all-to-all-start.1 = ((bf16[4,4,8,1280]{3,2,1,0:T(8,128)(2,1)}), bf16[4,4,8,1280]{3,2,1,0:T(8,128)(2,1)}, u32[]{:S(2)}, u32[]{:S(2)}) async-start(bf16[4,4,8,1280]{3,2,1,0:T(8,128)(2,1)} %bitcast.26), calls=%async_computation.1 | async-start | bytes 655360 | tf_op jit(solution)/shard_map/all_to_all | solution.py:730
  58.5 18.0 %collective-permute-done.6 = bf16[4,3,40,1280]{3,2,1,0:T(8,128)(2,1)} collective-permute-done((bf16[4,3,40,1280]{3,2,1,0:T(8,128)(2,1)}, bf16[4,3,40,1280]{3,2,1,0:T(8,128)(2,1)}, u32[]{:S(2)}, u32[]{:S(2)}) %collective-permute-start.6) | collective-permute-done | bytes 1228832 | tf_op jit(solution)/shard_map/ppermute | solution.py:347
  76.4 1.9 bitcast_select_fusion.near_rows
  78.4 1.9 slice.171
  80.3 2.2 fusion.23
  83.3 1.1 collective-permute-start.12
  85.6 5.7 %all-gather.5.cloned.1.call-done.w_ref = bf16[1280,480]{1,0:T(8,128)(2,1)} async-done(((bf16[320,480]{1,0:T(8,128)(2,1)}), bf16[1280,480]{1,0:T(8,128)(2,1)}) %all-gather.5.cloned.1.call-update) | async-done | bytes 1228816 | tf_op jit(solution)/shard_map/all_gather | solution.py:726
  91.3 1.3 copy-done.3
  92.6 7.5 %attend.1 = (f32[2,4,128,480]{3,2,1,0:T(8,128)S(1)}, bf16[4,2,128,160]{3,2,1,0:T(8,128)(2,1)S(1)}) custom-call(s32[6]{0:T(128)S(1)} %pad_add_fusion.info_ref, bf16[4,136,1280]{2,1,0:T(8,128)(2,1)} %pad_maximum_fusion.near_ref, bf16[4,136,1280]{2,1,0:T(8,128)(2,1)} %collective-permute-done.9.far_ref, f32[1,1280]{1,0:T(1,128)S(1)} %slice.143.gain_ref, ...), custom_call_target="tpu_custom_call" | custom-call | flops 8999999488 | bytes 8000000 | tf_op jit(solution)/shard_map/attend/pallas_call | solution.py:748
  100.1 1.4 copy-done.11
  101.5 2.9 %bitcast_select_fusion.1 = (bf16[2,3,80,1280]{3,2,1,0:T(8,128)(2,1)}, bf16[2,3,80,1280]{3,2,1,0:T(8,128)(2,1)}) fusion(pred[80]{0:T(512)(128)(4,1)S(1)} %broadcast_in_dim.386, bf16[2,3,40,1280]{3,2,1,0:T(8,128)(2,1)} %collective-permute-done.12, bf16[2,3,40,1280]{3,2,1,0:T(8,128)(2,1)S(1)} %copy-done.13, bf16[2,3,40,1280]{3,2,1,0:T(8,128)(2,1)} %collective-permute-done.11, ...), kind=kLoop, calls=%fused_computation.2 | loop fusion | flops 1228800 | bytes 4915280 | tf_op jit(solution)/shard_map/jit(_where)/select_n | solution.py:380
  105.6 1.4 collective-permute-start.14
  107.0 1.6 collective-permute-start.13
  108.6 1.7 copy.37
  110.3 2.1 collective-permute-done.15
  112.4 1.2 collective-permute-done.14
  114.3 1.4 collective-permute-done.16.far_atts
  115.8 8.5 %feed.1 = (bf16[4,4,8,1280]{3,2,1,0:T(8,128)(2,1)S(1)}, bf16[4,128,1280]{2,1,0:T(8,128)(2,1)S(1)}, f32[128,1280]{1,0:T(8,128)S(1)}, bf16[2,128,160]{2,1,0:T(8,12...) custom-call(s32[6]{0:T(128)S(1)} %pad_add_fusion.info_ref, ...), custom_call_target="tpu_custom_call" | custom-call | flops 12000000000 | bytes 13000000 | tf_op jit(solution)/shard_map/feed/pallas_call | solution.py:785
  124.5 1.2 collective-permute-start.20
  126.3 1.7 collective-permute-start.22
  128.0 4.4 %grads.1 = (bf16[2,3,2,40,1280]{4,3,2,1,0:T(8,128)(2,1)S(1)}, bf16[2,3,2,40,1280]{4,3,2,1,0:T(8,128)(2,1)}, bf16[2,3,2,40,1280]{4,3,2,1,0:T(8,128)(2,1)S(1)}, bf16[2,3,2,40,1280]{4,3,2,1,0:T(8,128)(2,1)}) custom-call(s32[6]{0:T(128)S(1)} %pad_add_fusion.info_ref, bf16[4,128,1280]{2,1,0:T(8,128)(2,1)S(1)} %get-tuple-element.125.pack_ref, ...), custom_call_target="tpu_custom_call" | custom-call | flops 6000000000 | bytes 8000000 | tf_op jit(solution)/shard_map/grads/pallas_call | solution.py:804
  132.5 1.0 copy-done.8
  135.1 1.3 collective-permute-start.24
  136.4 12.9 %attend_back.1 = (bf16[4,128,1280]{2,1,0:T(8,128)(2,1)S(1)}, bf16[4,128,1280]{2,1,0:T(8,128)(2,1)S(1)}, bf16[4,336,480]{2,1,0:T(8,128)(2,1)}) custom-call(s32[6]{0:T(128)S(1)} %pad_add_fusion.info_ref, bf16[4,136,1280]{2,1,0:T(8,128)(2,1)} %pad_maximum_fusion.near_ref, bf16[4,136,1280]{2,1,0:T(8,128)(2,1)} %collective-permute-done.9.far_ref, ...), custom_call_target="tpu_custom_call" | custom-call | flops 15000000512 | bytes 12000000 | tf_op jit(solution)/shard_map/attend_back/pallas_call | solution.py:818
  151.0 1.0 collective-permute-start.27
  151.9 1.0 collective-permute-start.26
  153.0 2.4 %collective-permute-done.27 = bf16[4,8,1280]{2,1,0:T(8,128)(2,1)S(1)} collective-permute-done((bf16[4,8,1280]{2,1,0:T(8,128)(2,1)S(1)}, bf16[4,8,1280]{2,1,0:T(8,128)(2,1)S(1)}, u32[]{:S(2)}, u32[]{:S(2)}) %collective-permute-start.27) | collective-permute-done | bytes 81952 | tf_op jit(solution)/shard_map/ppermute | solution.py:358
  155.4 6.8 %collective-permute-done.26 = bf16[4,8,1280]{2,1,0:T(8,128)(2,1)S(1)} collective-permute-done((bf16[4,8,1280]{2,1,0:T(8,128)(2,1)S(1)}, bf16[4,8,1280]{2,1,0:T(8,128)(2,1)S(1)}, u32[]{:S(2)}, u32[]{:S(2)}) %collective-permute-start.26) | collective-permute-done | bytes 81952 | tf_op jit(solution)/shard_map/ppermute | solution.py:358
  162.2 1.8 collective-permute-done.23.from_a
  164.5 1.3 copy-done.7
  165.8 2.3 %meet.2 = (bf16[2,3,40,1280]{3,2,1,0:T(8,128)(2,1)S(1)}, bf16[2,3,40,1280]{3,2,1,0:T(8,128)(2,1)S(1)}) custom-call(s32[6]{0:T(128)S(1)} %pad_add_fusion.info_ref, bf16[2,3,2,40,1280]{4,3,2,1,0:T(8,128)(2,1)S(1)} %copy-done.7, bf16[2,3,2,40,1280]{4,3,2,1,0:T(8,128)(2,1)} %collective-permute-done.23.from_a, bf16[2,3,2,40,1280]{4,3,2,1,0:T(8,128)(2,1)} %copy-done.8, ...), custom_call_target="tpu_custom_call" | custom-call | flops 2000000000 | bytes 4000000 | tf_op jit(solution)/shard_map/meet/pallas_call | solution.py:859
  168.2 1.4 collective-permute-start.29
  170.3 2.4 %meet.3 = (bf16[2,3,40,1280]{3,2,1,0:T(8,128)(2,1)S(1)}, bf16[2,3,40,1280]{3,2,1,0:T(8,128)(2,1)S(1)}) custom-call(s32[6]{0:T(128)S(1)} %pad_add_fusion.info_ref, bf16[2,3,2,40,1280]{4,3,2,1,0:T(8,128)(2,1)S(1)} %copy-done.7, bf16[2,3,2,40,1280]{4,3,2,1,0:T(8,128)(2,1)} %collective-permute-done.23.from_a, bf16[2,3,2,40,1280]{4,3,2,1,0:T(8,128)(2,1)} %copy-done.8, ...), custom_call_target="tpu_custom_call" | custom-call | flops 2000000000 | bytes 4000000 | tf_op jit(solution)/shard_map/meet/pallas_call | solution.py:859
  172.6 1.2 fusion.3
  173.8 10.7 %collective-permute-done.29.from_a = bf16[2,3,40,1280]{3,2,1,0:T(8,128)(2,1)S(1)} collective-permute-done((bf16[2,3,40,1280]{3,2,1,0:T(8,128)(2,1)S(1)}, bf16[2,3,40,1280]{3,2,1,0:T(8,128)(2,1)S(1)}, u32[]{:S(2)}, u32[]{:S(2)}) %collective-permute-start.29) | collective-permute-done | bytes 614432 | tf_op jit(solution)/shard_map/ppermute | solution.py:349
  184.5 1.0 collective-permute-done.30.from_b
  185.6 1.3 join.1
  187.7 5.2 %collective-permute-start.32 = (bf16[4,8,1280]{2,1,0:T(8,128)(2,1)S(1)}, bf16[4,8,1280]{2,1,0:T(8,128)(2,1)S(1)}, u32[]{:S(2)}, u32[]{:S(2)}) collective-permute-start(bf16[4,8,1280]{2,1,0:T(8,128)(2,1)S(1)} %copy-done.19), channel_id=1, source_target_pairs={{0,16},{8,24},{16,0},{24,8},{1,17},{9,25},{17,1},{25,9},{2,18},{10... | collective-permute-start | bytes 245768 | tf_op jit(solution)/shard_map/ppermute | solution.py:358
  192.9 1.0 collective-permute-start.33
  193.8 1.2 collective-permute-start.34
  195.0 0.9 collective-permute-done.32
  196.8 1.0 copy-done.5
  198.7 3.5 %all-to-all-start.2 = ((bf16[8,48,480]{2,1,0:T(8,128)(2,1)}), bf16[8,48,480]{2,1,0:T(8,128)(2,1)S(1)}, u32[]{:S(2)}, u32[]{:S(2)}) async-start(bf16[8,48,480]{2,1,0:T(8,128)(2,1)} %fold.1), calls=%async_computation.3 | async-start | bytes 786432 | tf_op jit(solution)/shard_map/all_to_all | solution.py:908
  202.7 9.1 %collective-permute-done.33.hid_2 = bf16[128,1280]{1,0:T(8,128)(2,1)S(1)} collective-permute-done((bf16[128,1280]{1,0:T(8,128)(2,1)}, bf16[128,1280]{1,0:T(8,128)(2,1)S(1)}, u32[]{:S(2)}, u32[]{:S(2)}) %collective-permute-start.33) | collective-permute-done | bytes 327712 | tf_op jit(solution)/shard_map/ppermute | solution.py:349
  211.8 1.0 norm.1
  213.0 1.9 collective-permute-start.37
  216.4 8.0 %collective-permute-done.36 = bf16[4,8,1280]{2,1,0:T(8,128)(2,1)S(1)} collective-permute-done((bf16[4,8,1280]{2,1,0:T(8,128)(2,1)S(1)}, bf16[4,8,1280]{2,1,0:T(8,128)(2,1)S(1)}, u32[]{:S(2)}, u32[]{:S(2)}) %collective-permute-start.36) | collective-permute-done | bytes 81952 | tf_op jit(solution)/shard_map/ppermute | solution.py:358
  224.4 1.1 fusion.5
  225.5 1.0 copy-done.2
  (169 shorter events, 20.7 us)
Async XLA Ops:
  7.2 3.1 %copy-start.23 = (f32[40]{0:T(128)S(1)}, f32[40]{0:T(128)}, u32[]{:S(2)}) copy-start(f32[40]{0:T(128)} %param.23) | copy-start | bytes 484
  7.2 3.1 %copy-start.16 = (f32[40,1280]{1,0:T(8,128)S(1)}, f32[40,1280]{1,0:T(8,128)}, u32[]{:S(2)}) copy-start(f32[40,1280]{1,0:T(8,128)} %param.17) | copy-start | bytes 614404
  7.2 3.2 %copy-start.20 = (f32[40]{0:T(128)S(1)}, f32[40]{0:T(128)}, u32[]{:S(2)}) copy-start(f32[40]{0:T(128)} %param.25) | copy-start | bytes 484
  7.2 3.2 %copy-start.22 = (f32[40]{0:T(128)S(1)}, f32[40]{0:T(128)}, u32[]{:S(2)}) copy-start(f32[40]{0:T(128)} %param.24) | copy-start | bytes 484
  7.2 3.2 %copy-start.17 = (f32[40,1280]{1,0:T(8,128)S(1)}, f32[40,1280]{1,0:T(8,128)}, u32[]{:S(2)}) copy-start(f32[40,1280]{1,0:T(8,128)} %param.19) | copy-start | bytes 614404
  7.2 3.2 %copy-start.18 = (f32[40,1280]{1,0:T(8,128)S(1)}, f32[40,1280]{1,0:T(8,128)}, u32[]{:S(2)}) copy-start(f32[40,1280]{1,0:T(8,128)} %param.18) | copy-start | bytes 614404
  7.2 39.8 %all-gather.3.cloned.1.call-start = ((), (), s32[]{:S(2)}) async-start(), calls=%async_computation.5 | async-start | bytes 1536000 | tf_op jit(solution)/shard_map/all_gather | solution.py:720
  10.7 8.4 %collective-permute-start = (bf16[5,8,1280]{2,1,0:T(8,128)(2,1)S(1)}, bf16[5,8,1280]{2,1,0:T(8,128)(2,1)S(1)}, u32[]{:S(2)}, u32[]{:S(2)}) collective-permute-start(bf16[5,8,1280]{2,1,0:T(8,128)(2,1)S(1)} %get-tuple-element.106), channel_id=1, source_target_pairs={{0,24},{8,0},{16,8},{24,16},{1,25},{9,1},{17,9},{25,17},{2,26},{10... | collective-permute-start | bytes 307208 | tf_op jit(solution)/shard_map/ppermute | solution.py:358
  15.8 10.7 %collective-permute-start.1 = (bf16[5,8,1280]{2,1,0:T(8,128)(2,1)S(1)}, bf16[5,8,1280]{2,1,0:T(8,128)(2,1)S(1)}, u32[]{:S(2)}, u32[]{:S(2)}) collective-permute-start(bf16[5,8,1280]{2,1,0:T(8,128)(2,1)S(1)} %get-tuple-element.107), channel_id=1, source_target_pairs={{0,16},{8,24},{16,0},{24,8},{1,17},{9,25},{17,1},{25,9},{2,18},{10... | collective-permute-start | bytes 307208 | tf_op jit(solution)/shard_map/ppermute | solution.py:358
  15.8 10.7 %collective-permute-start.2 = (bf16[5,8,1280]{2,1,0:T(8,128)(2,1)S(1)}, bf16[5,8,1280]{2,1,0:T(8,128)(2,1)S(1)}, u32[]{:S(2)}, u32[]{:S(2)}) collective-permute-start(bf16[5,8,1280]{2,1,0:T(8,128)(2,1)S(1)} %get-tuple-element.108), channel_id=1, source_target_pairs={{0,8},{8,16},{16,24},{24,0},{1,9},{9,17},{17,25},{25,1},{2,10},{10... | collective-permute-start | bytes 307208 | tf_op jit(solution)/shard_map/ppermute | solution.py:358
  27.0 10.2 %collective-permute-start.4 = (bf16[136,1280]{1,0:T(8,128)(2,1)S(1)}, bf16[136,1280]{1,0:T(8,128)(2,1)S(1)}, u32[]{:S(2)}, u32[]{:S(2)}) collective-permute-start(bf16[136,1280]{1,0:T(8,128)(2,1)S(1)} %get-tuple-element.200), channel_id=1, source_target_pairs={{0,4},{4,0},{1,5},{5,1},{2,6},{6,2},{3,7},{7,3},{8,12},{12,8},{9,1... | collective-permute-start | bytes 1044488 | tf_op jit(solution)/shard_map/ppermute | solution.py:349
  28.6 11.1 %collective-permute-start.3 = (bf16[136,1280]{1,0:T(8,128)(2,1)S(1)}, bf16[136,1280]{1,0:T(8,128)(2,1)S(1)}, u32[]{:S(2)}, u32[]{:S(2)}) collective-permute-start(bf16[136,1280]{1,0:T(8,128)(2,1)S(1)} %get-tuple-element.200), channel_id=1, source_target_pairs={{0,1},{1,0},{2,3},{3,2},{4,5},{5,4},{6,7},{7,6},{8,9},{9,8},{10,11... | collective-permute-start | bytes 1044488 | tf_op jit(solution)/shard_map/ppermute | solution.py:347
  30.2 15.2 %collective-permute-start.5 = (bf16[136,1280]{1,0:T(8,128)(2,1)S(1)}, bf16[136,1280]{1,0:T(8,128)(2,1)S(1)}, u32[]{:S(2)}, u32[]{:S(2)}) collective-permute-start(bf16[136,1280]{1,0:T(8,128)(2,1)S(1)} %get-tuple-element.200), channel_id=1, source_target_pairs={{0,5},{1,4},{4,1},{5,0},{2,7},{3,6},{6,3},{7,2},{8,13},{9,12},{12,... | collective-permute-start | bytes 1044488 | tf_op jit(solution)/shard_map/ppermute | solution.py:350
  32.7 14.4 %all-to-all-start = ((bf16[8,40,480]{2,1,0:T(8,128)(2,1)}), bf16[8,40,480]{2,1,0:T(8,128)(2,1)S(1)}, u32[]{:S(2)}, u32[]{:S(2)}) async-start(bf16[8,40,480]{2,1,0:T(8,128)(2,1)} %reshape.336), calls=%async_computation | async-start | bytes 655360 | tf_op jit(solution)/shard_map/all_to_all | solution.py:723
  36.5 54.8 %all-gather.5.cloned.1.call-start = ((), (), s32[]{:S(2)}) async-start(), calls=%async_computation.6 | async-start | bytes 1638400 | tf_op jit(solution)/shard_map/all_gather | solution.py:726
  45.4 4.5 %copy-start.24 = (s32[16]{0:T(128)S(1)}, s32[16]{0:T(128)}, u32[]{:S(2)}) copy-start(s32[16]{0:T(128)} %param.27) | copy-start | bytes 196
  45.4 4.5 %copy-start.25 = (s32[16]{0:T(128)S(1)}, s32[16]{0:T(128)}, u32[]{:S(2)}) copy-start(s32[16]{0:T(128)} %param.26) | copy-start | bytes 196
  47.1 2.8 %copy-start.14 = (bf16[8,40,480]{2,1,0:T(8,128)(2,1)}, bf16[8,40,480]{2,1,0:T(8,128)(2,1)S(1)}, u32[]{:S(2)}) copy-start(bf16[8,40,480]{2,1,0:T(8,128)(2,1)S(1)} %all-to-all-done) | copy-start | bytes 921604
  47.1 29.4 %collective-permute-start.6 = (bf16[4,3,40,1280]{3,2,1,0:T(8,128)(2,1)}, bf16[4,3,40,1280]{3,2,1,0:T(8,128)(2,1)}, u32[]{:S(2)}, u32[]{:S(2)}) collective-permute-start(bf16[4,3,40,1280]{3,2,1,0:T(8,128)(2,1)} %all-gather.3.cloned.1.call-done), channel_id=1, source_target_pairs={{0,1},{1,0},{2,3},{3,2},{4,5},{5,4},{6,7},{7,6},{8,9},{9,8},{10,11... | collective-permute-start | bytes 3686408 | tf_op jit(solution)/shard_map/ppermute | solution.py:347
  48.6 31.7 %collective-permute-start.7 = (bf16[4,3,40,1280]{3,2,1,0:T(8,128)(2,1)}, bf16[4,3,40,1280]{3,2,1,0:T(8,128)(2,1)}, u32[]{:S(2)}, u32[]{:S(2)}) collective-permute-start(bf16[4,3,40,1280]{3,2,1,0:T(8,128)(2,1)} %all-gather.3.cloned.1.call-done), channel_id=1, source_target_pairs={{0,4},{4,0},{1,5},{5,1},{2,6},{6,2},{3,7},{7,3},{8,12},{12,8},{9,1... | collective-permute-start | bytes 3686408 | tf_op jit(solution)/shard_map/ppermute | solution.py:349
  49.7 34.7 %collective-permute-start.9 = (bf16[4,136,1280]{2,1,0:T(8,128)(2,1)}, bf16[4,136,1280]{2,1,0:T(8,128)(2,1)}, u32[]{:S(2)}, u32[]{:S(2)}) collective-permute-start(bf16[4,136,1280]{2,1,0:T(8,128)(2,1)} %pad_maximum_fusion.near_ref), channel_id=1, source_target_pairs={{0,2},{2,0},{1,3},{3,1},{4,6},{6,4},{5,7},{7,5},{8,10},{10,8},{9,1... | collective-permute-start | bytes 4177928 | tf_op jit(solution)/shard_map/ppermute | solution.py:354
  50.9 31.6 %all-to-all-start.1 = ((bf16[4,4,8,1280]{3,2,1,0:T(8,128)(2,1)}), bf16[4,4,8,1280]{3,2,1,0:T(8,128)(2,1)}, u32[]{:S(2)}, u32[]{:S(2)}) async-start(bf16[4,4,8,1280]{3,2,1,0:T(8,128)(2,1)} %bitcast.26), calls=%async_computation.1 | async-start | bytes 655360 | tf_op jit(solution)/shard_map/all_to_all | solution.py:730
  58.5 138.4 %reduce-scatter.3.cloned.1.call-start = ((), (), s32[]{:S(2)}) async-start(), calls=%async_computation.7 | async-start | bytes 1720320 | tf_op jit(solution)/shard_map/reduce_scatter | solution.py:850
  78.3 23.2 %collective-permute-start.10 = (bf16[4,3,80,1280]{3,2,1,0:T(8,128)(2,1)S(1)}, bf16[4,3,80,1280]{3,2,1,0:T(8,128)(2,1)}, u32[]{:S(2)}, u32[]{:S(2)}) collective-permute-start(bf16[4,3,80,1280]{3,2,1,0:T(8,128)(2,1)S(1)} %bitcast_select_fusion.near_rows), channel_id=1, source_target_pairs={{0,2},{2,0},{1,3},{3,1},{4,6},{6,4},{5,7},{7,5},{8,10},{10,8},{9,1... | collective-permute-start | bytes 7372808 | tf_op jit(solution)/shard_map/ppermute | solution.py:354
  82.5 19.0 %collective-permute-start.11 = (bf16[2,3,40,1280]{3,2,1,0:T(8,128)(2,1)}, bf16[2,3,40,1280]{3,2,1,0:T(8,128)(2,1)}, u32[]{:S(2)}, u32[]{:S(2)}) collective-permute-start(bf16[2,3,40,1280]{3,2,1,0:T(8,128)(2,1)} %slice.171), channel_id=1, source_target_pairs={{0,4},{4,0},{1,5},{5,1},{2,6},{6,2},{3,7},{7,3},{8,12},{12,8},{9,1... | collective-permute-start | bytes 1843208 | tf_op jit(solution)/shard_map/ppermute | solution.py:349
  83.3 18.2 %collective-permute-start.12 = (bf16[2,3,40,1280]{3,2,1,0:T(8,128)(2,1)}, bf16[2,3,40,1280]{3,2,1,0:T(8,128)(2,1)}, u32[]{:S(2)}, u32[]{:S(2)}) collective-permute-start(bf16[2,3,40,1280]{3,2,1,0:T(8,128)(2,1)} %get-tuple-element.118), channel_id=1, source_target_pairs={{0,1},{1,0},{2,3},{3,2},{4,5},{5,4},{6,7},{7,6},{8,9},{9,8},{10,11... | collective-permute-start | bytes 1843208 | tf_op jit(solution)/shard_map/ppermute | solution.py:347
  92.6 8.9 %copy-start.13 = (bf16[2,3,40,1280]{3,2,1,0:T(8,128)(2,1)S(1)}, bf16[2,3,40,1280]{3,2,1,0:T(8,128)(2,1)}, u32[]{:S(2)}) copy-start(bf16[2,3,40,1280]{3,2,1,0:T(8,128)(2,1)} %get-tuple-element.118) | copy-start | bytes 1843204
  100.1 1.4 copy-start.11
  104.5 11.3 %collective-permute-start.18 = (bf16[2,3,80,1280]{3,2,1,0:T(8,128)(2,1)}, bf16[2,3,80,1280]{3,2,1,0:T(8,128)(2,1)}, u32[]{:S(2)}, u32[]{:S(2)}) collective-permute-start(bf16[2,3,80,1280]{3,2,1,0:T(8,128)(2,1)} %get-tuple-element.221.across_b), channel_id=1, source_target_pairs={{0,2},{2,0},{1,3},{3,1},{4,6},{6,4},{5,7},{7,5},{8,10},{10,8},{9,1... | collective-permute-start | bytes 3686408 | tf_op jit(solution)/shard_map/ppermute | solution.py:354
  104.5 11.3 %collective-permute-start.17 = (bf16[2,3,80,1280]{3,2,1,0:T(8,128)(2,1)}, bf16[2,3,80,1280]{3,2,1,0:T(8,128)(2,1)}, u32[]{:S(2)}, u32[]{:S(2)}) collective-permute-start(bf16[2,3,80,1280]{3,2,1,0:T(8,128)(2,1)} %get-tuple-element.222.across_a), channel_id=1, source_target_pairs={{0,2},{2,0},{1,3},{3,1},{4,6},{6,4},{5,7},{7,5},{8,10},{10,8},{9,1... | collective-permute-start | bytes 3686408 | tf_op jit(solution)/shard_map/ppermute | solution.py:354
  105.0 7.4 %collective-permute-start.15 = (bf16[2,128,160]{2,1,0:T(8,128)(2,1)S(1)}, bf16[2,128,160]{2,1,0:T(8,128)(2,1)S(1)}, u32[]{:S(2)}, u32[]{:S(2)}) collective-permute-start(bf16[2,128,160]{2,1,0:T(8,128)(2,1)S(1)} %get-tuple-element.196), channel_id=1, source_target_pairs={{0,5},{1,4},{4,1},{5,0},{2,7},{3,6},{6,3},{7,2},{8,13},{9,12},{12,... | collective-permute-start | bytes 245768 | tf_op jit(solution)/shard_map/ppermute | solution.py:350
  105.6 8.0 %collective-permute-start.14 = (bf16[2,128,160]{2,1,0:T(8,128)(2,1)S(1)}, bf16[2,128,160]{2,1,0:T(8,128)(2,1)S(1)}, u32[]{:S(2)}, u32[]{:S(2)}) collective-permute-start(bf16[2,128,160]{2,1,0:T(8,128)(2,1)S(1)} %get-tuple-element.197), channel_id=1, source_target_pairs={{0,4},{4,0},{1,5},{5,1},{2,6},{6,2},{3,7},{7,3},{8,12},{12,8},{9,1... | collective-permute-start | bytes 245768 | tf_op jit(solution)/shard_map/ppermute | solution.py:349
  107.0 6.5 %collective-permute-start.13 = (bf16[2,128,160]{2,1,0:T(8,128)(2,1)S(1)}, bf16[2,128,160]{2,1,0:T(8,128)(2,1)S(1)}, u32[]{:S(2)}, u32[]{:S(2)}) collective-permute-start(bf16[2,128,160]{2,1,0:T(8,128)(2,1)S(1)} %get-tuple-element.198), channel_id=1, source_target_pairs={{0,1},{1,0},{2,3},{3,2},{4,5},{5,4},{6,7},{7,6},{8,9},{9,8},{10,11... | collective-permute-start | bytes 245768 | tf_op jit(solution)/shard_map/ppermute | solution.py:347
  112.4 2.0 collective-permute-start.8
  113.7 2.1 collective-permute-start.16
  124.3 8.2 %copy-start = (bf16[4,4,8,1280]{3,2,1,0:T(8,128)(2,1)}, bf16[4,4,8,1280]{3,2,1,0:T(8,128)(2,1)S(1)}, u32[]{:S(2)}) copy-start(bf16[4,4,8,1280]{3,2,1,0:T(8,128)(2,1)S(1)} %get-tuple-element.149) | copy-start | bytes 983044
  124.3 8.2 %copy-start.9 = (f32[128,1280]{1,0:T(8,128)}, f32[128,1280]{1,0:T(8,128)S(1)}, u32[]{:S(2)}) copy-start(f32[128,1280]{1,0:T(8,128)S(1)} %get-tuple-element.168.dmid_ref) | copy-start | bytes 1966084
  124.3 3.7 %collective-permute-start.19 = (bf16[4,128,1280]{2,1,0:T(8,128)(2,1)S(1)}, bf16[4,128,1280]{2,1,0:T(8,128)(2,1)S(1)}, u32[]{:S(2)}, u32[]{:S(2)}) collective-permute-start(bf16[4,128,1280]{2,1,0:T(8,128)(2,1)S(1)} %get-tuple-element.125.pack_ref), channel_id=1, source_target_pairs={{0,2},{2,0},{1,3},{3,1},{4,6},{6,4},{5,7},{7,5},{8,10},{10,8},{9,1... | collective-permute-start | bytes 3932168 | tf_op jit(solution)/shard_map/ppermute | solution.py:354
  124.5 9.0 %collective-permute-start.20 = (bf16[2,128,160]{2,1,0:T(8,128)(2,1)S(1)}, bf16[2,128,160]{2,1,0:T(8,128)(2,1)S(1)}, u32[]{:S(2)}, u32[]{:S(2)}) collective-permute-start(bf16[2,128,160]{2,1,0:T(8,128)(2,1)S(1)} %get-tuple-element.132), channel_id=1, source_target_pairs={{0,1},{1,0},{2,3},{3,2},{4,5},{5,4},{6,7},{7,6},{8,9},{9,8},{10,11... | collective-permute-start | bytes 245768 | tf_op jit(solution)/shard_map/ppermute | solution.py:347
  125.7 8.3 %collective-permute-start.21 = (bf16[2,128,160]{2,1,0:T(8,128)(2,1)S(1)}, bf16[2,128,160]{2,1,0:T(8,128)(2,1)S(1)}, u32[]{:S(2)}, u32[]{:S(2)}) collective-permute-start(bf16[2,128,160]{2,1,0:T(8,128)(2,1)S(1)} %get-tuple-element.133), channel_id=1, source_target_pairs={{0,4},{4,0},{1,5},{5,1},{2,6},{6,2},{3,7},{7,3},{8,12},{12,8},{9,1... | collective-permute-start | bytes 245768 | tf_op jit(solution)/shard_map/ppermute | solution.py:349
  126.3 10.2 %copy-start.4 = (bf16[1280,480]{1,0:T(8,128)(2,1)S(1)}, bf16[1280,480]{1,0:T(8,128)(2,1)}, u32[]{:S(2)}) copy-start(bf16[1280,480]{1,0:T(8,128)(2,1)} %all-gather.5.cloned.1.call-done.w_ref) | copy-start | bytes 3686404
  126.3 10.2 %copy-start.12 = (f32[2,4,128,480]{3,2,1,0:T(8,128)S(1)}, f32[2,4,128,480]{3,2,1,0:T(8,128)}, u32[]{:S(2)}) copy-start(f32[2,4,128,480]{3,2,1,0:T(8,128)} %copy-done.11) | copy-start | bytes 5898244
  126.3 7.7 %collective-permute-start.22 = (bf16[2,128,160]{2,1,0:T(8,128)(2,1)S(1)}, bf16[2,128,160]{2,1,0:T(8,128)(2,1)S(1)}, u32[]{:S(2)}, u32[]{:S(2)}) collective-permute-start(bf16[2,128,160]{2,1,0:T(8,128)(2,1)S(1)} %get-tuple-element.134), channel_id=1, source_target_pairs={{0,5},{1,4},{4,1},{5,0},{2,7},{3,6},{6,3},{7,2},{8,13},{9,12},{12,... | collective-permute-start | bytes 245768 | tf_op jit(solution)/shard_map/ppermute | solution.py:350
  133.5 15.8 %copy-start.6 = (bf16[2,3,2,40,1280]{4,3,2,1,0:T(8,128)(2,1)}, bf16[2,3,2,40,1280]{4,3,2,1,0:T(8,128)(2,1)S(1)}, u32[]{:S(2)}) copy-start(bf16[2,3,2,40,1280]{4,3,2,1,0:T(8,128)(2,1)S(1)} %get-tuple-element.153.mine_a) | copy-start | bytes 3686404
  134.1 2.3 collective-permute-start.25
  134.2 29.8 %collective-permute-start.23 = (bf16[2,3,2,40,1280]{4,3,2,1,0:T(8,128)(2,1)}, bf16[2,3,2,40,1280]{4,3,2,1,0:T(8,128)(2,1)}, u32[]{:S(2)}, u32[]{:S(2)}) collective-permute-start(bf16[2,3,2,40,1280]{4,3,2,1,0:T(8,128)(2,1)} %get-tuple-element.141), channel_id=1, source_target_pairs={{0,1},{1,0},{2,3},{3,2},{4,5},{5,4},{6,7},{7,6},{8,9},{9,8},{10,11... | collective-permute-start | bytes 3686408 | tf_op jit(solution)/shard_map/ppermute | solution.py:347
  135.1 29.4 %collective-permute-start.24 = (bf16[2,3,2,40,1280]{4,3,2,1,0:T(8,128)(2,1)}, bf16[2,3,2,40,1280]{4,3,2,1,0:T(8,128)(2,1)}, u32[]{:S(2)}, u32[]{:S(2)}) collective-permute-start(bf16[2,3,2,40,1280]{4,3,2,1,0:T(8,128)(2,1)} %get-tuple-element.142), channel_id=1, source_target_pairs={{0,4},{4,0},{1,5},{5,1},{2,6},{6,2},{3,7},{7,3},{8,12},{12,8},{9,1... | collective-permute-start | bytes 3686408 | tf_op jit(solution)/shard_map/ppermute | solution.py:349
  149.3 76.2 %reduce-scatter.5.cloned.1.call-start = ((), (), s32[]{:S(2)}) async-start(), calls=%async_computation.8 | async-start | bytes 1536000 | tf_op jit(solution)/shard_map/reduce_scatter | solution.py:887
  151.0 4.4 %collective-permute-start.27 = (bf16[4,8,1280]{2,1,0:T(8,128)(2,1)S(1)}, bf16[4,8,1280]{2,1,0:T(8,128)(2,1)S(1)}, u32[]{:S(2)}, u32[]{:S(2)}) collective-permute-start(bf16[4,8,1280]{2,1,0:T(8,128)(2,1)S(1)} %get-tuple-element.203), channel_id=1, source_target_pairs={{0,24},{8,0},{16,8},{24,16},{1,25},{9,1},{17,9},{25,17},{2,26},{10... | collective-permute-start | bytes 245768 | tf_op jit(solution)/shard_map/ppermute | solution.py:358
  151.9 10.2 %collective-permute-start.26 = (bf16[4,8,1280]{2,1,0:T(8,128)(2,1)S(1)}, bf16[4,8,1280]{2,1,0:T(8,128)(2,1)S(1)}, u32[]{:S(2)}, u32[]{:S(2)}) collective-permute-start(bf16[4,8,1280]{2,1,0:T(8,128)(2,1)S(1)} %get-tuple-element.204), channel_id=1, source_target_pairs={{0,8},{8,16},{16,24},{24,0},{1,9},{9,17},{17,25},{25,1},{2,10},{10... | collective-permute-start | bytes 245768 | tf_op jit(solution)/shard_map/ppermute | solution.py:358
  164.5 8.1 %collective-permute-start.28 = (bf16[4,128,1280]{2,1,0:T(8,128)(2,1)S(1)}, bf16[4,128,1280]{2,1,0:T(8,128)(2,1)S(1)}, u32[]{:S(2)}, u32[]{:S(2)}) collective-permute-start(bf16[4,128,1280]{2,1,0:T(8,128)(2,1)S(1)} %get-tuple-element.152), channel_id=1, source_target_pairs={{0,2},{2,0},{1,3},{3,1},{4,6},{6,4},{5,7},{7,5},{8,10},{10,8},{9,1... | collective-permute-start | bytes 3932168 | tf_op jit(solution)/shard_map/ppermute | solution.py:354
  168.2 16.4 %collective-permute-start.29 = (bf16[2,3,40,1280]{3,2,1,0:T(8,128)(2,1)S(1)}, bf16[2,3,40,1280]{3,2,1,0:T(8,128)(2,1)S(1)}, u32[]{:S(2)}, u32[]{:S(2)}) collective-permute-start(bf16[2,3,40,1280]{3,2,1,0:T(8,128)(2,1)S(1)} %get-tuple-element.157), channel_id=1, source_target_pairs={{0,4},{4,0},{1,5},{5,1},{2,6},{6,2},{3,7},{7,3},{8,12},{12,8},{9,1... | collective-permute-start | bytes 1843208 | tf_op jit(solution)/shard_map/ppermute | solution.py:349
  169.6 16.0 %collective-permute-start.30 = (bf16[2,3,40,1280]{3,2,1,0:T(8,128)(2,1)S(1)}, bf16[2,3,40,1280]{3,2,1,0:T(8,128)(2,1)S(1)}, u32[]{:S(2)}, u32[]{:S(2)}) collective-permute-start(bf16[2,3,40,1280]{3,2,1,0:T(8,128)(2,1)S(1)} %get-tuple-element.158), channel_id=1, source_target_pairs={{0,1},{1,0},{2,3},{3,2},{4,5},{5,4},{6,7},{7,6},{8,9},{9,8},{10,11... | collective-permute-start | bytes 1843208 | tf_op jit(solution)/shard_map/ppermute | solution.py:347
  185.6 2.1 copy-start.19
  186.9 24.9 %copy-start.10 = (f32[128,1280]{1,0:T(8,128)S(1)}, f32[128,1280]{1,0:T(8,128)}, u32[]{:S(2)}) copy-start(f32[128,1280]{1,0:T(8,128)} %copy-done.9) | copy-start | bytes 1966084
  186.9 9.9 %collective-permute-start.31 = (bf16[128,1280]{1,0:T(8,128)(2,1)}, bf16[128,1280]{1,0:T(8,128)(2,1)S(1)}, u32[]{:S(2)}, u32[]{:S(2)}) collective-permute-start(bf16[128,1280]{1,0:T(8,128)(2,1)} %get-tuple-element.159), channel_id=1, source_target_pairs={{0,1},{1,0},{2,3},{3,2},{4,5},{5,4},{6,7},{7,6},{8,9},{9,8},{10,11... | collective-permute-start | bytes 983048 | tf_op jit(solution)/shard_map/ppermute | solution.py:347
  187.7 8.2 %collective-permute-start.32 = (bf16[4,8,1280]{2,1,0:T(8,128)(2,1)S(1)}, bf16[4,8,1280]{2,1,0:T(8,128)(2,1)S(1)}, u32[]{:S(2)}, u32[]{:S(2)}) collective-permute-start(bf16[4,8,1280]{2,1,0:T(8,128)(2,1)S(1)} %copy-done.19), channel_id=1, source_target_pairs={{0,16},{8,24},{16,0},{24,8},{1,17},{9,25},{17,1},{25,9},{2,18},{10... | collective-permute-start | bytes 245768 | tf_op jit(solution)/shard_map/ppermute | solution.py:358
  192.9 18.9 %collective-permute-start.33 = (bf16[128,1280]{1,0:T(8,128)(2,1)}, bf16[128,1280]{1,0:T(8,128)(2,1)S(1)}, u32[]{:S(2)}, u32[]{:S(2)}) collective-permute-start(bf16[128,1280]{1,0:T(8,128)(2,1)} %get-tuple-element.166), channel_id=1, source_target_pairs={{0,4},{4,0},{1,5},{5,1},{2,6},{6,2},{3,7},{7,3},{8,12},{12,8},{9,1... | collective-permute-start | bytes 983048 | tf_op jit(solution)/shard_map/ppermute | solution.py:349
  193.8 17.9 %collective-permute-start.34 = (bf16[128,1280]{1,0:T(8,128)(2,1)S(1)}, bf16[128,1280]{1,0:T(8,128)(2,1)S(1)}, u32[]{:S(2)}, u32[]{:S(2)}) collective-permute-start(bf16[128,1280]{1,0:T(8,128)(2,1)S(1)} %get-tuple-element.167), channel_id=1, source_target_pairs={{0,5},{1,4},{4,1},{5,0},{2,7},{3,6},{6,3},{7,2},{8,13},{9,12},{12,... | collective-permute-start | bytes 983048 | tf_op jit(solution)/shard_map/ppermute | solution.py:350
  198.7 16.2 %all-to-all-start.2 = ((bf16[8,48,480]{2,1,0:T(8,128)(2,1)}), bf16[8,48,480]{2,1,0:T(8,128)(2,1)S(1)}, u32[]{:S(2)}, u32[]{:S(2)}) async-start(bf16[8,48,480]{2,1,0:T(8,128)(2,1)} %fold.1), calls=%async_computation.3 | async-start | bytes 786432 | tf_op jit(solution)/shard_map/all_to_all | solution.py:908
  211.8 3.2 %copy-start.21 = (f32[40]{0:T(128)S(1)}, f32[40]{0:T(128)}, u32[]{:S(2)}) copy-start(f32[40]{0:T(128)} %param.25) | copy-start | bytes 484
  212.8 11.6 %collective-permute-start.35 = (bf16[4,8,1280]{2,1,0:T(8,128)(2,1)S(1)}, bf16[4,8,1280]{2,1,0:T(8,128)(2,1)S(1)}, u32[]{:S(2)}, u32[]{:S(2)}) collective-permute-start(bf16[4,8,1280]{2,1,0:T(8,128)(2,1)S(1)} %get-tuple-element.169), channel_id=1, source_target_pairs={{0,24},{8,0},{16,8},{24,16},{1,25},{9,1},{17,9},{25,17},{2,26},{10... | collective-permute-start | bytes 245768 | tf_op jit(solution)/shard_map/ppermute | solution.py:358
  212.9 11.5 %collective-permute-start.36 = (bf16[4,8,1280]{2,1,0:T(8,128)(2,1)S(1)}, bf16[4,8,1280]{2,1,0:T(8,128)(2,1)S(1)}, u32[]{:S(2)}, u32[]{:S(2)}) collective-permute-start(bf16[4,8,1280]{2,1,0:T(8,128)(2,1)S(1)} %get-tuple-element.170), channel_id=1, source_target_pairs={{0,16},{8,24},{16,0},{24,8},{1,17},{9,25},{17,1},{25,9},{2,18},{10... | collective-permute-start | bytes 245768 | tf_op jit(solution)/shard_map/ppermute | solution.py:358
  213.0 11.4 %collective-permute-start.37 = (bf16[4,8,1280]{2,1,0:T(8,128)(2,1)S(1)}, bf16[4,8,1280]{2,1,0:T(8,128)(2,1)S(1)}, u32[]{:S(2)}, u32[]{:S(2)}) collective-permute-start(bf16[4,8,1280]{2,1,0:T(8,128)(2,1)S(1)} %get-tuple-element.176), channel_id=1, source_target_pairs={{0,8},{8,16},{16,24},{24,0},{1,9},{9,17},{17,25},{25,1},{2,10},{10... | collective-permute-start | bytes 245768 | tf_op jit(solution)/shard_map/ppermute | solution.py:358
  (7 other events, 7.7 us)
Sparse Core Ops, SparseCore 0:
  10.4 34.5 all-gather.2
  50.0 41.2 all-gather.4
  149.5 34.1 reduce-scatter.2
  187.0 35.9 reduce-scatter.4

commit v15 on v14

--- a/solution.py
+++ b/solution.py
@@ -721,6 +721,7 @@
 
     qkv = qkv.reshape(3, 40, 8, 160).transpose(2, 1, 0, 3).reshape(8, 40, 480)
     qkv = lax.all_to_all(qkv, ("y", "core", "x"), split_axis=0, concat_axis=0, tiled=True)
+    own, qkv = lax.optimization_barrier((own, qkv))
     near = jnp.stack([own] + [plane_shift(own, step) for step in (1, 2, 3)])
     big, near, cotangent, qkv = lax.optimization_barrier((big, near, cotangent, qkv.reshape(320, 480)))
     w_qkv = lax.all_gather(qkv, "z", axis=0, tiled=True)

time: 235 us -> 233 us (level)
  starting transfers between devices: 53.6 us -> 48.7 us
  waiting for transfers between devices: 89.8 us -> 93.4 us
    ppermute x8, waiting for transfers between devices: 24.2 us -> 29.6 us  [plane_shift(): return lax.ppermute(value, 'x', [(0, 1), (1, 0)])]
    all_gather x1, waiting for transfers between devices: 5.7 us -> 1.33 us  [planes(): w_qkv = lax.all_gather(qkv, 'z', axis=0, tiled=True)]
    all_to_all x1, starting transfers between devices: 7.57 us -> 4.09 us  [planes(): lax.all_to_all(cotangent.reshape(4, 4, 8, width), 'z', split_axis=0, conc...]
    ppermute x9, waiting for transfers between devices: 27.1 us -> 24.1 us  [ring_shift(): return lax.ppermute(value, 'z', [(i, (i + step) % 4) for i in range(4)])]
    ppermute x4, waiting for transfers between devices: 7.75 us -> 10.5 us  [plane_shift(): return lax.ppermute(value, ('y', 'x'), [(0, 3), (1, 2), (2, 1), (3, 0)])]
    all_to_all x1, waiting for transfers between devices: 0.39 us -> 2.84 us  [planes(): lax.all_to_all(qkv, ('y', 'core', 'x'), split_axis=0, concat_axis=0, tile...]
    unnamed x52 -> x50, local copies, waits for them, and re-layouts: 7.93 us -> 7.91 us
where the time goes in v15:
time: 233 us; the launch traced here: 232 us
  waiting for transfers between devices  93.4 us (40%)
  starting transfers between devices  48.7 us (21%)
  Pallas kernels  43 us (18%)
  local copies, waits for them, and re-layouts  19.9 us (9%)
  between operations  14.4 us (6%)
  other arithmetic  13.1 us (6%)
    ppermute x8, waiting for transfers between devices, plane_shift(): return lax.ppermute(value, 'x', [(0, 1), (1, 0)])  29.6 us
    ppermute x9, waiting for transfers between devices, ring_shift(): return lax.ppermute(value, 'z', [(i, (i + step) % 4) for i in range(4)])  24.1 us
    ppermute x8, waiting for transfers between devices, plane_shift(): return lax.ppermute(value, 'y', [(0, 1), (1, 0)])  22.4 us
    ppermute x9, starting transfers between devices, ring_shift(): return lax.ppermute(value, 'z', [(i, (i + step) % 4) for i in range(4)])  14 us
    pallas_call x1, Pallas kernels, planes(): pl.pallas_call(attend_back_kernel, grid_spec=pltpu.PrefetchScalarGridSpec...  12.9 us
    ppermute x4, waiting for transfers between devices, plane_shift(): return lax.ppermute(value, ('y', 'x'), [(0, 3), (1, 2), (2, 1), (3, 0)])  10.5 us
    pallas_call x1, Pallas kernels, planes(): pl.pallas_call(feed_kernel, in_specs=[smem] + [vmem] * 5 + [hbm] * 6, out...  8.49 us
    ppermute x8, starting transfers between devices, plane_shift(): return lax.ppermute(value, 'x', [(0, 1), (1, 0)])  8.46 us
  transfers between devices with their start and end apart: 45, of which 23 were waited for; matrix products, arithmetic and copies ran while one was open for 8% of the time, Pallas kernels for 14%

profile of v15, /device:TPU:0, one launch (start us, length us, event | category | flops | bytes accessed | tf_op | source)
XLA Modules:
  0.0 232.4 jit_solution(2431513520295412178)
XLA Ops:
  7.3 1.1 convert_bitcast_fusion.2
  8.4 1.1 convert_bitcast_fusion
  10.7 5.1 %collective-permute-start = (bf16[5,8,1280]{2,1,0:T(8,128)(2,1)S(1)}, bf16[5,8,1280]{2,1,0:T(8,128)(2,1)S(1)}, u32[]{:S(2)}, u32[]{:S(2)}) collective-permute-start(bf16[5,8,1280]{2,1,0:T(8,128)(2,1)S(1)} %get-tuple-element.108), channel_id=1, source_target_pairs={{0,24},{8,0},{16,8},{24,16},{1,25},{9,1},{17,9},{25,17},{2,26},{10... | collective-permute-start | bytes 307208 | tf_op jit(solution)/shard_map/ppermute | solution.py:358
  15.8 1.0 collective-permute-start.2
  17.9 1.1 reshape.336
  18.9 3.7 %all-to-all-start = ((bf16[8,40,480]{2,1,0:T(8,128)(2,1)}), bf16[8,40,480]{2,1,0:T(8,128)(2,1)S(1)}, u32[]{:S(2)}, u32[]{:S(2)}) async-start(bf16[8,40,480]{2,1,0:T(8,128)(2,1)} %reshape.336), calls=%async_computation | async-start | bytes 655360 | tf_op jit(solution)/shard_map/all_to_all | solution.py:723
  23.4 3.1 %collective-permute-done.1 = bf16[5,8,1280]{2,1,0:T(8,128)(2,1)S(1)} collective-permute-done((bf16[5,8,1280]{2,1,0:T(8,128)(2,1)S(1)}, bf16[5,8,1280]{2,1,0:T(8,128)(2,1)S(1)}, u32[]{:S(2)}, u32[]{:S(2)}) %collective-permute-start.1) | collective-permute-done | bytes 102432 | tf_op jit(solution)/shard_map/ppermute | solution.py:358
  27.0 2.8 %all-to-all-done = bf16[8,40,480]{2,1,0:T(8,128)(2,1)S(1)} async-done(((bf16[8,40,480]{2,1,0:T(8,128)(2,1)}), bf16[8,40,480]{2,1,0:T(8,128)(2,1)S(1)}, u32[]{:S(2)}, u32[]{:S(2)}) %all-to-all-start) | async-done | bytes 307232 | tf_op jit(solution)/shard_map/all_to_all | solution.py:723
  29.8 1.0 collective-permute-start.5
  30.8 1.5 collective-permute-start.4
  32.3 1.0 collective-permute-start.3
  33.3 8.4 %collective-permute-done.5 = bf16[136,1280]{1,0:T(8,128)(2,1)S(1)} collective-permute-done((bf16[136,1280]{1,0:T(8,128)(2,1)S(1)}, bf16[136,1280]{1,0:T(8,128)(2,1)S(1)}, u32[]{:S(2)}, u32[]{:S(2)}) %collective-permute-start.5) | collective-permute-done | bytes 348192 | tf_op jit(solution)/shard_map/ppermute | solution.py:350
  41.7 6.3 %collective-permute-done.4 = bf16[136,1280]{1,0:T(8,128)(2,1)S(1)} collective-permute-done((bf16[136,1280]{1,0:T(8,128)(2,1)S(1)}, bf16[136,1280]{1,0:T(8,128)(2,1)S(1)}, u32[]{:S(2)}, u32[]{:S(2)}) %collective-permute-start.4) | collective-permute-done | bytes 348192 | tf_op jit(solution)/shard_map/ppermute | solution.py:349
  48.1 1.3 pad_maximum_fusion.near_ref
  49.4 0.9 collective-permute-start.6
  52.2 4.1 %all-to-all-start.1 = ((bf16[4,4,8,1280]{3,2,1,0:T(8,128)(2,1)}), bf16[4,4,8,1280]{3,2,1,0:T(8,128)(2,1)}, u32[]{:S(2)}, u32[]{:S(2)}) async-start(bf16[4,4,8,1280]{3,2,1,0:T(8,128)(2,1)} %bitcast.26), calls=%async_computation.1 | async-start | bytes 655360 | tf_op jit(solution)/shard_map/all_to_all | solution.py:731
  56.4 22.1 %collective-permute-done.6 = bf16[4,3,40,1280]{3,2,1,0:T(8,128)(2,1)} collective-permute-done((bf16[4,3,40,1280]{3,2,1,0:T(8,128)(2,1)}, bf16[4,3,40,1280]{3,2,1,0:T(8,128)(2,1)}, u32[]{:S(2)}, u32[]{:S(2)}) %collective-permute-start.6) | collective-permute-done | bytes 1228832 | tf_op jit(solution)/shard_map/ppermute | solution.py:347
  78.5 1.9 bitcast_select_fusion.near_rows
  80.4 1.9 slice.171
  82.4 2.2 fusion.22
  84.5 1.2 collective-permute-start.11
  87.6 1.3 all-gather.5.cloned.1.call-done.w_ref
  89.0 1.3 copy-done.3
  90.3 7.5 %attend.1 = (f32[2,4,128,480]{3,2,1,0:T(8,128)S(1)}, bf16[4,2,128,160]{3,2,1,0:T(8,128)(2,1)S(1)}) custom-call(s32[6]{0:T(128)S(1)} %pad_add_fusion.info_ref, bf16[4,136,1280]{2,1,0:T(8,128)(2,1)} %pad_maximum_fusion.near_ref, bf16[4,136,1280]{2,1,0:T(8,128)(2,1)} %collective-permute-done.9.far_ref, f32[1,1280]{1,0:T(1,128)S(1)} %slice.143.gain_ref, ...), custom_call_target="tpu_custom_call" | custom-call | flops 8999999488 | bytes 8000000 | tf_op jit(solution)/shard_map/attend/pallas_call | solution.py:749
  97.8 1.3 copy-done.11
  99.1 2.0 collective-permute-done.11
  102.0 2.9 %bitcast_select_fusion.1 = (bf16[2,3,80,1280]{3,2,1,0:T(8,128)(2,1)}, bf16[2,3,80,1280]{3,2,1,0:T(8,128)(2,1)}) fusion(pred[80]{0:T(512)(128)(4,1)S(1)} %broadcast_in_dim.386, bf16[2,3,40,1280]{3,2,1,0:T(8,128)(2,1)} %collective-permute-done.12, bf16[2,3,40,1280]{3,2,1,0:T(8,128)(2,1)S(1)} %copy-done.13, bf16[2,3,40,1280]{3,2,1,0:T(8,128)(2,1)} %collective-permute-done.11, ...), kind=kLoop, calls=%fused_computation.2 | loop fusion | flops 1228800 | bytes 4915280 | tf_op jit(solution)/shard_map/jit(_where)/select_n | solution.py:380
  105.5 1.5 collective-permute-start.15
  107.7 1.3 collective-permute-start.13
  109.1 1.7 copy.37
  110.8 2.1 collective-permute-done.15
  112.9 1.8 collective-permute-done.14
  115.0 1.9 collective-permute-done.16.far_atts
  117.0 8.5 %feed.1 = (bf16[4,4,8,1280]{3,2,1,0:T(8,128)(2,1)S(1)}, bf16[4,128,1280]{2,1,0:T(8,128)(2,1)S(1)}, f32[128,1280]{1,0:T(8,128)S(1)}, bf16[2,128,160]{2,1,0:T(8,12...) custom-call(s32[6]{0:T(128)S(1)} %pad_add_fusion.info_ref, ...), custom_call_target="tpu_custom_call" | custom-call | flops 12000000000 | bytes 13000000 | tf_op jit(solution)/shard_map/feed/pallas_call | solution.py:786
  126.4 1.3 collective-permute-start.21
  127.7 1.5 collective-permute-start.22
  129.2 4.4 %grads.1 = (bf16[2,3,2,40,1280]{4,3,2,1,0:T(8,128)(2,1)S(1)}, bf16[2,3,2,40,1280]{4,3,2,1,0:T(8,128)(2,1)}, bf16[2,3,2,40,1280]{4,3,2,1,0:T(8,128)(2,1)S(1)}, bf16[2,3,2,40,1280]{4,3,2,1,0:T(8,128)(2,1)}) custom-call(s32[6]{0:T(128)S(1)} %pad_add_fusion.info_ref, bf16[4,128,1280]{2,1,0:T(8,128)(2,1)S(1)} %get-tuple-element.129.pack_ref, ...), custom_call_target="tpu_custom_call" | custom-call | flops 6000000000 | bytes 8000000 | tf_op jit(solution)/shard_map/grads/pallas_call | solution.py:805
  133.6 1.0 copy-done.8
  134.9 1.4 collective-permute-start.23
  137.1 12.9 %attend_back.1 = (bf16[4,128,1280]{2,1,0:T(8,128)(2,1)S(1)}, bf16[4,128,1280]{2,1,0:T(8,128)(2,1)S(1)}, bf16[4,336,480]{2,1,0:T(8,128)(2,1)}) custom-call(s32[6]{0:T(128)S(1)} %pad_add_fusion.info_ref, bf16[4,136,1280]{2,1,0:T(8,128)(2,1)} %pad_maximum_fusion.near_ref, bf16[4,136,1280]{2,1,0:T(8,128)(2,1)} %collective-permute-done.9.far_ref, ...), custom_call_target="tpu_custom_call" | custom-call | flops 15000000512 | bytes 12000000 | tf_op jit(solution)/shard_map/attend_back/pallas_call | solution.py:819
  151.6 2.8 %collective-permute-start.27 = (bf16[4,8,1280]{2,1,0:T(8,128)(2,1)S(1)}, bf16[4,8,1280]{2,1,0:T(8,128)(2,1)S(1)}, u32[]{:S(2)}, u32[]{:S(2)}) collective-permute-start(bf16[4,8,1280]{2,1,0:T(8,128)(2,1)S(1)} %get-tuple-element.205), channel_id=1, source_target_pairs={{0,24},{8,0},{16,8},{24,16},{1,25},{9,1},{17,9},{25,17},{2,26},{10... | collective-permute-start | bytes 245768 | tf_op jit(solution)/shard_map/ppermute | solution.py:358
  154.5 4.4 %collective-permute-done.27 = bf16[4,8,1280]{2,1,0:T(8,128)(2,1)S(1)} collective-permute-done((bf16[4,8,1280]{2,1,0:T(8,128)(2,1)S(1)}, bf16[4,8,1280]{2,1,0:T(8,128)(2,1)S(1)}, u32[]{:S(2)}, u32[]{:S(2)}) %collective-permute-start.27) | collective-permute-done | bytes 81952 | tf_op jit(solution)/shard_map/ppermute | solution.py:358
  158.8 3.4 %collective-permute-done.26 = bf16[4,8,1280]{2,1,0:T(8,128)(2,1)S(1)} collective-permute-done((bf16[4,8,1280]{2,1,0:T(8,128)(2,1)S(1)}, bf16[4,8,1280]{2,1,0:T(8,128)(2,1)S(1)}, u32[]{:S(2)}, u32[]{:S(2)}) %collective-permute-start.26) | collective-permute-done | bytes 81952 | tf_op jit(solution)/shard_map/ppermute | solution.py:358
  162.2 2.4 %collective-permute-done.23.from_a = bf16[2,3,2,40,1280]{4,3,2,1,0:T(8,128)(2,1)} collective-permute-done((bf16[2,3,2,40,1280]{4,3,2,1,0:T(8,128)(2,1)}, bf16[2,3,2,40,1280]{4,3,2,1,0:T(8,128)(2,1)}, u32[]{:S(2)}, u32[]{:S(2)}) %collective-permute-start.23) | collective-permute-done | bytes 1228832 | tf_op jit(solution)/shard_map/ppermute | solution.py:347
  164.6 1.1 collective-permute-done.24.from_b
  165.7 1.3 copy-done.7
  167.0 2.4 %meet.2 = (bf16[2,3,40,1280]{3,2,1,0:T(8,128)(2,1)S(1)}, bf16[2,3,40,1280]{3,2,1,0:T(8,128)(2,1)S(1)}) custom-call(s32[6]{0:T(128)S(1)} %pad_add_fusion.info_ref, bf16[2,3,2,40,1280]{4,3,2,1,0:T(8,128)(2,1)S(1)} %copy-done.7, bf16[2,3,2,40,1280]{4,3,2,1,0:T(8,128)(2,1)} %collective-permute-done.23.from_a, bf16[2,3,2,40,1280]{4,3,2,1,0:T(8,128)(2,1)} %copy-done.8, ...), custom_call_target="tpu_custom_call" | custom-call | flops 2000000000 | bytes 4000000 | tf_op jit(solution)/shard_map/meet/pallas_call | solution.py:860
  170.2 1.2 collective-permute-start.30
  171.4 2.3 %meet.3 = (bf16[2,3,40,1280]{3,2,1,0:T(8,128)(2,1)S(1)}, bf16[2,3,40,1280]{3,2,1,0:T(8,128)(2,1)S(1)}) custom-call(s32[6]{0:T(128)S(1)} %pad_add_fusion.info_ref, bf16[2,3,2,40,1280]{4,3,2,1,0:T(8,128)(2,1)S(1)} %copy-done.7, bf16[2,3,2,40,1280]{4,3,2,1,0:T(8,128)(2,1)} %collective-permute-done.23.from_a, bf16[2,3,2,40,1280]{4,3,2,1,0:T(8,128)(2,1)} %copy-done.8, ...), custom_call_target="tpu_custom_call" | custom-call | flops 2000000000 | bytes 4000000 | tf_op jit(solution)/shard_map/meet/pallas_call | solution.py:860
  173.8 1.2 fusion.3
  174.9 10.8 %collective-permute-done.29.from_a = bf16[2,3,40,1280]{3,2,1,0:T(8,128)(2,1)S(1)} collective-permute-done((bf16[2,3,40,1280]{3,2,1,0:T(8,128)(2,1)S(1)}, bf16[2,3,40,1280]{3,2,1,0:T(8,128)(2,1)S(1)}, u32[]{:S(2)}, u32[]{:S(2)}) %collective-permute-start.29) | collective-permute-done | bytes 614432 | tf_op jit(solution)/shard_map/ppermute | solution.py:349
  186.3 1.3 join.1
  187.6 1.2 collective-permute-start.31
  188.9 1.2 collective-permute-start.33
  190.0 1.5 collective-permute-start.34
  191.6 3.5 %collective-permute-done.32 = bf16[4,8,1280]{2,1,0:T(8,128)(2,1)S(1)} collective-permute-done((bf16[4,8,1280]{2,1,0:T(8,128)(2,1)S(1)}, bf16[4,8,1280]{2,1,0:T(8,128)(2,1)S(1)}, u32[]{:S(2)}, u32[]{:S(2)}) %collective-permute-start.32) | collective-permute-done | bytes 81952 | tf_op jit(solution)/shard_map/ppermute | solution.py:358
  195.0 3.5 %collective-permute-done.31.hid_1 = bf16[128,1280]{1,0:T(8,128)(2,1)S(1)} collective-permute-done((bf16[128,1280]{1,0:T(8,128)(2,1)}, bf16[128,1280]{1,0:T(8,128)(2,1)S(1)}, u32[]{:S(2)}, u32[]{:S(2)}) %collective-permute-start.31) | collective-permute-done | bytes 327712 | tf_op jit(solution)/shard_map/ppermute | solution.py:347
  198.5 1.0 copy-done.5
  200.4 3.5 %all-to-all-start.2 = ((bf16[8,48,480]{2,1,0:T(8,128)(2,1)}), bf16[8,48,480]{2,1,0:T(8,128)(2,1)S(1)}, u32[]{:S(2)}, u32[]{:S(2)}) async-start(bf16[8,48,480]{2,1,0:T(8,128)(2,1)} %fold.1), calls=%async_computation.3 | async-start | bytes 786432 | tf_op jit(solution)/shard_map/all_to_all | solution.py:909
  204.9 1.0 norm.1
  205.9 4.4 %collective-permute-start.35 = (bf16[4,8,1280]{2,1,0:T(8,128)(2,1)S(1)}, bf16[4,8,1280]{2,1,0:T(8,128)(2,1)S(1)}, u32[]{:S(2)}, u32[]{:S(2)}) collective-permute-start(bf16[4,8,1280]{2,1,0:T(8,128)(2,1)S(1)} %get-tuple-element.173), channel_id=1, source_target_pairs={{0,24},{8,0},{16,8},{24,16},{1,25},{9,1},{17,9},{25,17},{2,26},{10... | collective-permute-start | bytes 245768 | tf_op jit(solution)/shard_map/ppermute | solution.py:358
  213.2 9.8 %collective-permute-done.36 = bf16[4,8,1280]{2,1,0:T(8,128)(2,1)S(1)} collective-permute-done((bf16[4,8,1280]{2,1,0:T(8,128)(2,1)S(1)}, bf16[4,8,1280]{2,1,0:T(8,128)(2,1)S(1)}, u32[]{:S(2)}, u32[]{:S(2)}) %collective-permute-start.36) | collective-permute-done | bytes 81952 | tf_op jit(solution)/shard_map/ppermute | solution.py:358
  223.0 1.1 fusion.5
  224.1 1.0 copy-done.2
  (167 shorter events, 20.3 us)
Async XLA Ops:
  7.2 3.1 %copy-start.22 = (f32[40]{0:T(128)S(1)}, f32[40]{0:T(128)}, u32[]{:S(2)}) copy-start(f32[40]{0:T(128)} %param.23) | copy-start | bytes 484
  7.2 3.1 %copy-start.16 = (f32[40,1280]{1,0:T(8,128)S(1)}, f32[40,1280]{1,0:T(8,128)}, u32[]{:S(2)}) copy-start(f32[40,1280]{1,0:T(8,128)} %param.17) | copy-start | bytes 614404
  7.2 3.2 %copy-start.20 = (f32[40]{0:T(128)S(1)}, f32[40]{0:T(128)}, u32[]{:S(2)}) copy-start(f32[40]{0:T(128)} %param.25) | copy-start | bytes 484
  7.2 3.2 %copy-start.21 = (f32[40]{0:T(128)S(1)}, f32[40]{0:T(128)}, u32[]{:S(2)}) copy-start(f32[40]{0:T(128)} %param.24) | copy-start | bytes 484
  7.2 3.2 %copy-start.17 = (f32[40,1280]{1,0:T(8,128)S(1)}, f32[40,1280]{1,0:T(8,128)}, u32[]{:S(2)}) copy-start(f32[40,1280]{1,0:T(8,128)} %param.19) | copy-start | bytes 614404
  7.2 3.2 %copy-start.18 = (f32[40,1280]{1,0:T(8,128)S(1)}, f32[40,1280]{1,0:T(8,128)}, u32[]{:S(2)}) copy-start(f32[40,1280]{1,0:T(8,128)} %param.18) | copy-start | bytes 614404
  7.2 42.1 %all-gather.3.cloned.1.call-start = ((), (), s32[]{:S(2)}) async-start(), calls=%async_computation.5 | async-start | bytes 1536000 | tf_op jit(solution)/shard_map/all_gather | solution.py:720
  10.7 12.7 %collective-permute-start = (bf16[5,8,1280]{2,1,0:T(8,128)(2,1)S(1)}, bf16[5,8,1280]{2,1,0:T(8,128)(2,1)S(1)}, u32[]{:S(2)}, u32[]{:S(2)}) collective-permute-start(bf16[5,8,1280]{2,1,0:T(8,128)(2,1)S(1)} %get-tuple-element.108), channel_id=1, source_target_pairs={{0,24},{8,0},{16,8},{24,16},{1,25},{9,1},{17,9},{25,17},{2,26},{10... | collective-permute-start | bytes 307208 | tf_op jit(solution)/shard_map/ppermute | solution.py:358
  15.8 10.7 %collective-permute-start.1 = (bf16[5,8,1280]{2,1,0:T(8,128)(2,1)S(1)}, bf16[5,8,1280]{2,1,0:T(8,128)(2,1)S(1)}, u32[]{:S(2)}, u32[]{:S(2)}) collective-permute-start(bf16[5,8,1280]{2,1,0:T(8,128)(2,1)S(1)} %get-tuple-element.109), channel_id=1, source_target_pairs={{0,16},{8,24},{16,0},{24,8},{1,17},{9,25},{17,1},{25,9},{2,18},{10... | collective-permute-start | bytes 307208 | tf_op jit(solution)/shard_map/ppermute | solution.py:358
  15.8 10.7 %collective-permute-start.2 = (bf16[5,8,1280]{2,1,0:T(8,128)(2,1)S(1)}, bf16[5,8,1280]{2,1,0:T(8,128)(2,1)S(1)}, u32[]{:S(2)}, u32[]{:S(2)}) collective-permute-start(bf16[5,8,1280]{2,1,0:T(8,128)(2,1)S(1)} %get-tuple-element.110), channel_id=1, source_target_pairs={{0,8},{8,16},{16,24},{24,0},{1,9},{9,17},{17,25},{25,1},{2,10},{10... | collective-permute-start | bytes 307208 | tf_op jit(solution)/shard_map/ppermute | solution.py:358
  18.9 10.9 %all-to-all-start = ((bf16[8,40,480]{2,1,0:T(8,128)(2,1)}), bf16[8,40,480]{2,1,0:T(8,128)(2,1)S(1)}, u32[]{:S(2)}, u32[]{:S(2)}) async-start(bf16[8,40,480]{2,1,0:T(8,128)(2,1)} %reshape.336), calls=%async_computation | async-start | bytes 655360 | tf_op jit(solution)/shard_map/all_to_all | solution.py:723
  22.6 66.3 %all-gather.5.cloned.1.call-start = ((), (), s32[]{:S(2)}) async-start(), calls=%async_computation.6 | async-start | bytes 1638400 | tf_op jit(solution)/shard_map/all_gather | solution.py:727
  29.8 19.6 %copy-start.14 = (bf16[8,40,480]{2,1,0:T(8,128)(2,1)}, bf16[8,40,480]{2,1,0:T(8,128)(2,1)S(1)}, u32[]{:S(2)}) copy-start(bf16[8,40,480]{2,1,0:T(8,128)(2,1)S(1)} %all-to-all-done) | copy-start | bytes 921604
  29.8 11.9 %collective-permute-start.5 = (bf16[136,1280]{1,0:T(8,128)(2,1)S(1)}, bf16[136,1280]{1,0:T(8,128)(2,1)S(1)}, u32[]{:S(2)}, u32[]{:S(2)}) collective-permute-start(bf16[136,1280]{1,0:T(8,128)(2,1)S(1)} %maximum_maximum_fusion), channel_id=1, source_target_pairs={{0,5},{1,4},{4,1},{5,0},{2,7},{3,6},{6,3},{7,2},{8,13},{9,12},{12,... | collective-permute-start | bytes 1044488 | tf_op jit(solution)/shard_map/ppermute | solution.py:350
  30.8 17.2 %collective-permute-start.4 = (bf16[136,1280]{1,0:T(8,128)(2,1)S(1)}, bf16[136,1280]{1,0:T(8,128)(2,1)S(1)}, u32[]{:S(2)}, u32[]{:S(2)}) collective-permute-start(bf16[136,1280]{1,0:T(8,128)(2,1)S(1)} %maximum_maximum_fusion), channel_id=1, source_target_pairs={{0,4},{4,0},{1,5},{5,1},{2,6},{6,2},{3,7},{7,3},{8,12},{12,8},{9,1... | collective-permute-start | bytes 1044488 | tf_op jit(solution)/shard_map/ppermute | solution.py:349
  32.3 15.8 %collective-permute-start.3 = (bf16[136,1280]{1,0:T(8,128)(2,1)S(1)}, bf16[136,1280]{1,0:T(8,128)(2,1)S(1)}, u32[]{:S(2)}, u32[]{:S(2)}) collective-permute-start(bf16[136,1280]{1,0:T(8,128)(2,1)S(1)} %maximum_maximum_fusion), channel_id=1, source_target_pairs={{0,1},{1,0},{2,3},{3,2},{4,5},{5,4},{6,7},{7,6},{8,9},{9,8},{10,11... | collective-permute-start | bytes 1044488 | tf_op jit(solution)/shard_map/ppermute | solution.py:347
  48.1 3.2 %copy-start.23 = (s32[16]{0:T(128)S(1)}, s32[16]{0:T(128)}, u32[]{:S(2)}) copy-start(s32[16]{0:T(128)} %param.27) | copy-start | bytes 196
  48.1 3.2 %copy-start.24 = (s32[16]{0:T(128)S(1)}, s32[16]{0:T(128)}, u32[]{:S(2)}) copy-start(s32[16]{0:T(128)} %param.26) | copy-start | bytes 196
  49.4 29.1 %collective-permute-start.6 = (bf16[4,3,40,1280]{3,2,1,0:T(8,128)(2,1)}, bf16[4,3,40,1280]{3,2,1,0:T(8,128)(2,1)}, u32[]{:S(2)}, u32[]{:S(2)}) collective-permute-start(bf16[4,3,40,1280]{3,2,1,0:T(8,128)(2,1)} %all-gather.3.cloned.1.call-done), channel_id=1, source_target_pairs={{0,1},{1,0},{2,3},{3,2},{4,5},{5,4},{6,7},{7,6},{8,9},{9,8},{10,11... | collective-permute-start | bytes 3686408 | tf_op jit(solution)/shard_map/ppermute | solution.py:347
  50.3 32.1 %collective-permute-start.7 = (bf16[4,3,40,1280]{3,2,1,0:T(8,128)(2,1)}, bf16[4,3,40,1280]{3,2,1,0:T(8,128)(2,1)}, u32[]{:S(2)}, u32[]{:S(2)}) collective-permute-start(bf16[4,3,40,1280]{3,2,1,0:T(8,128)(2,1)} %all-gather.3.cloned.1.call-done), channel_id=1, source_target_pairs={{0,4},{4,0},{1,5},{5,1},{2,6},{6,2},{3,7},{7,3},{8,12},{12,8},{9,1... | collective-permute-start | bytes 3686408 | tf_op jit(solution)/shard_map/ppermute | solution.py:349
  51.0 35.4 %collective-permute-start.9 = (bf16[4,136,1280]{2,1,0:T(8,128)(2,1)}, bf16[4,136,1280]{2,1,0:T(8,128)(2,1)}, u32[]{:S(2)}, u32[]{:S(2)}) collective-permute-start(bf16[4,136,1280]{2,1,0:T(8,128)(2,1)} %pad_maximum_fusion.near_ref), channel_id=1, source_target_pairs={{0,2},{2,0},{1,3},{3,1},{4,6},{6,4},{5,7},{7,5},{8,10},{10,8},{9,1... | collective-permute-start | bytes 4177928 | tf_op jit(solution)/shard_map/ppermute | solution.py:354
  52.2 32.3 %all-to-all-start.1 = ((bf16[4,4,8,1280]{3,2,1,0:T(8,128)(2,1)}), bf16[4,4,8,1280]{3,2,1,0:T(8,128)(2,1)}, u32[]{:S(2)}, u32[]{:S(2)}) async-start(bf16[4,4,8,1280]{3,2,1,0:T(8,128)(2,1)} %bitcast.26), calls=%async_computation.1 | async-start | bytes 655360 | tf_op jit(solution)/shard_map/all_to_all | solution.py:731
  56.3 142.2 %reduce-scatter.3.cloned.1.call-start = ((), (), s32[]{:S(2)}) async-start(), calls=%async_computation.7 | async-start | bytes 1720320 | tf_op jit(solution)/shard_map/reduce_scatter | solution.py:851
  80.3 21.7 %collective-permute-start.10 = (bf16[4,3,80,1280]{3,2,1,0:T(8,128)(2,1)S(1)}, bf16[4,3,80,1280]{3,2,1,0:T(8,128)(2,1)}, u32[]{:S(2)}, u32[]{:S(2)}) collective-permute-start(bf16[4,3,80,1280]{3,2,1,0:T(8,128)(2,1)S(1)} %bitcast_select_fusion.near_rows), channel_id=1, source_target_pairs={{0,2},{2,0},{1,3},{3,1},{4,6},{6,4},{5,7},{7,5},{8,10},{10,8},{9,1... | collective-permute-start | bytes 7372808 | tf_op jit(solution)/shard_map/ppermute | solution.py:354
  84.5 16.6 %collective-permute-start.11 = (bf16[2,3,40,1280]{3,2,1,0:T(8,128)(2,1)}, bf16[2,3,40,1280]{3,2,1,0:T(8,128)(2,1)}, u32[]{:S(2)}, u32[]{:S(2)}) collective-permute-start(bf16[2,3,40,1280]{3,2,1,0:T(8,128)(2,1)} %slice.171), channel_id=1, source_target_pairs={{0,4},{4,0},{1,5},{5,1},{2,6},{6,2},{3,7},{7,3},{8,12},{12,8},{9,1... | collective-permute-start | bytes 1843208 | tf_op jit(solution)/shard_map/ppermute | solution.py:349
  85.7 16.3 %collective-permute-start.12 = (bf16[2,3,40,1280]{3,2,1,0:T(8,128)(2,1)}, bf16[2,3,40,1280]{3,2,1,0:T(8,128)(2,1)}, u32[]{:S(2)}, u32[]{:S(2)}) collective-permute-start(bf16[2,3,40,1280]{3,2,1,0:T(8,128)(2,1)} %get-tuple-element.122), channel_id=1, source_target_pairs={{0,1},{1,0},{2,3},{3,2},{4,5},{5,4},{6,7},{7,6},{8,9},{9,8},{10,11... | collective-permute-start | bytes 1843208 | tf_op jit(solution)/shard_map/ppermute | solution.py:347
  89.0 1.3 copy-start.3
  90.3 11.7 %copy-start.13 = (bf16[2,3,40,1280]{3,2,1,0:T(8,128)(2,1)S(1)}, bf16[2,3,40,1280]{3,2,1,0:T(8,128)(2,1)}, u32[]{:S(2)}) copy-start(bf16[2,3,40,1280]{3,2,1,0:T(8,128)(2,1)} %get-tuple-element.122) | copy-start | bytes 1843204
  97.8 1.3 copy-start.11
  105.0 12.0 %collective-permute-start.18 = (bf16[2,3,80,1280]{3,2,1,0:T(8,128)(2,1)}, bf16[2,3,80,1280]{3,2,1,0:T(8,128)(2,1)}, u32[]{:S(2)}, u32[]{:S(2)}) collective-permute-start(bf16[2,3,80,1280]{3,2,1,0:T(8,128)(2,1)} %get-tuple-element.223.across_b), channel_id=1, source_target_pairs={{0,2},{2,0},{1,3},{3,1},{4,6},{6,4},{5,7},{7,5},{8,10},{10,8},{9,1... | collective-permute-start | bytes 3686408 | tf_op jit(solution)/shard_map/ppermute | solution.py:354
  105.0 12.0 %collective-permute-start.17 = (bf16[2,3,80,1280]{3,2,1,0:T(8,128)(2,1)}, bf16[2,3,80,1280]{3,2,1,0:T(8,128)(2,1)}, u32[]{:S(2)}, u32[]{:S(2)}) collective-permute-start(bf16[2,3,80,1280]{3,2,1,0:T(8,128)(2,1)} %get-tuple-element.224.across_a), channel_id=1, source_target_pairs={{0,2},{2,0},{1,3},{3,1},{4,6},{6,4},{5,7},{7,5},{8,10},{10,8},{9,1... | collective-permute-start | bytes 3686408 | tf_op jit(solution)/shard_map/ppermute | solution.py:354
  105.5 7.3 %collective-permute-start.15 = (bf16[2,128,160]{2,1,0:T(8,128)(2,1)S(1)}, bf16[2,128,160]{2,1,0:T(8,128)(2,1)S(1)}, u32[]{:S(2)}, u32[]{:S(2)}) collective-permute-start(bf16[2,128,160]{2,1,0:T(8,128)(2,1)S(1)} %get-tuple-element.200), channel_id=1, source_target_pairs={{0,5},{1,4},{4,1},{5,0},{2,7},{3,6},{6,3},{7,2},{8,13},{9,12},{12,... | collective-permute-start | bytes 245768 | tf_op jit(solution)/shard_map/ppermute | solution.py:350
  107.0 7.7 %collective-permute-start.14 = (bf16[2,128,160]{2,1,0:T(8,128)(2,1)S(1)}, bf16[2,128,160]{2,1,0:T(8,128)(2,1)S(1)}, u32[]{:S(2)}, u32[]{:S(2)}) collective-permute-start(bf16[2,128,160]{2,1,0:T(8,128)(2,1)S(1)} %get-tuple-element.201), channel_id=1, source_target_pairs={{0,4},{4,0},{1,5},{5,1},{2,6},{6,2},{3,7},{7,3},{8,12},{12,8},{9,1... | collective-permute-start | bytes 245768 | tf_op jit(solution)/shard_map/ppermute | solution.py:349
  107.7 7.0 %collective-permute-start.13 = (bf16[2,128,160]{2,1,0:T(8,128)(2,1)S(1)}, bf16[2,128,160]{2,1,0:T(8,128)(2,1)S(1)}, u32[]{:S(2)}, u32[]{:S(2)}) collective-permute-start(bf16[2,128,160]{2,1,0:T(8,128)(2,1)S(1)} %get-tuple-element.202), channel_id=1, source_target_pairs={{0,1},{1,0},{2,3},{3,2},{4,5},{5,4},{6,7},{7,6},{8,9},{9,8},{10,11... | collective-permute-start | bytes 245768 | tf_op jit(solution)/shard_map/ppermute | solution.py:347
  112.9 2.2 collective-permute-start.8
  114.8 2.1 collective-permute-start.16
  125.5 8.1 %copy-start = (bf16[4,4,8,1280]{3,2,1,0:T(8,128)(2,1)}, bf16[4,4,8,1280]{3,2,1,0:T(8,128)(2,1)S(1)}, u32[]{:S(2)}) copy-start(bf16[4,4,8,1280]{3,2,1,0:T(8,128)(2,1)S(1)} %get-tuple-element.153) | copy-start | bytes 983044
  125.5 8.1 %copy-start.9 = (f32[128,1280]{1,0:T(8,128)}, f32[128,1280]{1,0:T(8,128)S(1)}, u32[]{:S(2)}) copy-start(f32[128,1280]{1,0:T(8,128)S(1)} %get-tuple-element.172.dmid_ref) | copy-start | bytes 1966084
  125.5 3.7 %collective-permute-start.19 = (bf16[4,128,1280]{2,1,0:T(8,128)(2,1)S(1)}, bf16[4,128,1280]{2,1,0:T(8,128)(2,1)S(1)}, u32[]{:S(2)}, u32[]{:S(2)}) collective-permute-start(bf16[4,128,1280]{2,1,0:T(8,128)(2,1)S(1)} %get-tuple-element.129.pack_ref), channel_id=1, source_target_pairs={{0,2},{2,0},{1,3},{3,1},{4,6},{6,4},{5,7},{7,5},{8,10},{10,8},{9,1... | collective-permute-start | bytes 3932168 | tf_op jit(solution)/shard_map/ppermute | solution.py:354
  125.7 9.0 %collective-permute-start.20 = (bf16[2,128,160]{2,1,0:T(8,128)(2,1)S(1)}, bf16[2,128,160]{2,1,0:T(8,128)(2,1)S(1)}, u32[]{:S(2)}, u32[]{:S(2)}) collective-permute-start(bf16[2,128,160]{2,1,0:T(8,128)(2,1)S(1)} %get-tuple-element.136), channel_id=1, source_target_pairs={{0,1},{1,0},{2,3},{3,2},{4,5},{5,4},{6,7},{7,6},{8,9},{9,8},{10,11... | collective-permute-start | bytes 245768 | tf_op jit(solution)/shard_map/ppermute | solution.py:347
  126.4 8.3 %collective-permute-start.21 = (bf16[2,128,160]{2,1,0:T(8,128)(2,1)S(1)}, bf16[2,128,160]{2,1,0:T(8,128)(2,1)S(1)}, u32[]{:S(2)}, u32[]{:S(2)}) collective-permute-start(bf16[2,128,160]{2,1,0:T(8,128)(2,1)S(1)} %get-tuple-element.137), channel_id=1, source_target_pairs={{0,4},{4,0},{1,5},{5,1},{2,6},{6,2},{3,7},{7,3},{8,12},{12,8},{9,1... | collective-permute-start | bytes 245768 | tf_op jit(solution)/shard_map/ppermute | solution.py:349
  127.7 9.4 %copy-start.4 = (bf16[1280,480]{1,0:T(8,128)(2,1)S(1)}, bf16[1280,480]{1,0:T(8,128)(2,1)}, u32[]{:S(2)}) copy-start(bf16[1280,480]{1,0:T(8,128)(2,1)} %all-gather.5.cloned.1.call-done.w_ref) | copy-start | bytes 3686404
  127.7 9.4 %copy-start.12 = (f32[2,4,128,480]{3,2,1,0:T(8,128)S(1)}, f32[2,4,128,480]{3,2,1,0:T(8,128)}, u32[]{:S(2)}) copy-start(f32[2,4,128,480]{3,2,1,0:T(8,128)} %copy-done.11) | copy-start | bytes 5898244
  127.7 7.0 %collective-permute-start.22 = (bf16[2,128,160]{2,1,0:T(8,128)(2,1)S(1)}, bf16[2,128,160]{2,1,0:T(8,128)(2,1)S(1)}, u32[]{:S(2)}, u32[]{:S(2)}) collective-permute-start(bf16[2,128,160]{2,1,0:T(8,128)(2,1)S(1)} %get-tuple-element.138), channel_id=1, source_target_pairs={{0,5},{1,4},{4,1},{5,0},{2,7},{3,6},{6,3},{7,2},{8,13},{9,12},{12,... | collective-permute-start | bytes 245768 | tf_op jit(solution)/shard_map/ppermute | solution.py:350
  134.7 15.3 %copy-start.6 = (bf16[2,3,2,40,1280]{4,3,2,1,0:T(8,128)(2,1)}, bf16[2,3,2,40,1280]{4,3,2,1,0:T(8,128)(2,1)S(1)}, u32[]{:S(2)}) copy-start(bf16[2,3,2,40,1280]{4,3,2,1,0:T(8,128)(2,1)S(1)} %get-tuple-element.157.mine_a) | copy-start | bytes 3686404
  134.8 2.3 collective-permute-start.25
  134.9 29.8 %collective-permute-start.23 = (bf16[2,3,2,40,1280]{4,3,2,1,0:T(8,128)(2,1)}, bf16[2,3,2,40,1280]{4,3,2,1,0:T(8,128)(2,1)}, u32[]{:S(2)}, u32[]{:S(2)}) collective-permute-start(bf16[2,3,2,40,1280]{4,3,2,1,0:T(8,128)(2,1)} %get-tuple-element.145), channel_id=1, source_target_pairs={{0,1},{1,0},{2,3},{3,2},{4,5},{5,4},{6,7},{7,6},{8,9},{9,8},{10,11... | collective-permute-start | bytes 3686408 | tf_op jit(solution)/shard_map/ppermute | solution.py:347
  136.3 29.4 %collective-permute-start.24 = (bf16[2,3,2,40,1280]{4,3,2,1,0:T(8,128)(2,1)}, bf16[2,3,2,40,1280]{4,3,2,1,0:T(8,128)(2,1)}, u32[]{:S(2)}, u32[]{:S(2)}) collective-permute-start(bf16[2,3,2,40,1280]{4,3,2,1,0:T(8,128)(2,1)} %get-tuple-element.146), channel_id=1, source_target_pairs={{0,4},{4,0},{1,5},{5,1},{2,6},{6,2},{3,7},{7,3},{8,12},{12,8},{9,1... | collective-permute-start | bytes 3686408 | tf_op jit(solution)/shard_map/ppermute | solution.py:349
  150.0 74.1 %reduce-scatter.5.cloned.1.call-start = ((), (), s32[]{:S(2)}) async-start(), calls=%async_computation.8 | async-start | bytes 1536000 | tf_op jit(solution)/shard_map/reduce_scatter | solution.py:888
  151.6 7.2 %collective-permute-start.27 = (bf16[4,8,1280]{2,1,0:T(8,128)(2,1)S(1)}, bf16[4,8,1280]{2,1,0:T(8,128)(2,1)S(1)}, u32[]{:S(2)}, u32[]{:S(2)}) collective-permute-start(bf16[4,8,1280]{2,1,0:T(8,128)(2,1)S(1)} %get-tuple-element.205), channel_id=1, source_target_pairs={{0,24},{8,0},{16,8},{24,16},{1,25},{9,1},{17,9},{25,17},{2,26},{10... | collective-permute-start | bytes 245768 | tf_op jit(solution)/shard_map/ppermute | solution.py:358
  154.5 7.8 %collective-permute-start.26 = (bf16[4,8,1280]{2,1,0:T(8,128)(2,1)S(1)}, bf16[4,8,1280]{2,1,0:T(8,128)(2,1)S(1)}, u32[]{:S(2)}, u32[]{:S(2)}) collective-permute-start(bf16[4,8,1280]{2,1,0:T(8,128)(2,1)S(1)} %get-tuple-element.206), channel_id=1, source_target_pairs={{0,8},{8,16},{16,24},{24,0},{1,9},{9,17},{17,25},{25,1},{2,10},{10... | collective-permute-start | bytes 245768 | tf_op jit(solution)/shard_map/ppermute | solution.py:358
  165.7 8.1 %collective-permute-start.28 = (bf16[4,128,1280]{2,1,0:T(8,128)(2,1)S(1)}, bf16[4,128,1280]{2,1,0:T(8,128)(2,1)S(1)}, u32[]{:S(2)}, u32[]{:S(2)}) collective-permute-start(bf16[4,128,1280]{2,1,0:T(8,128)(2,1)S(1)} %get-tuple-element.156), channel_id=1, source_target_pairs={{0,2},{2,0},{1,3},{3,1},{4,6},{6,4},{5,7},{7,5},{8,10},{10,8},{9,1... | collective-permute-start | bytes 3932168 | tf_op jit(solution)/shard_map/ppermute | solution.py:354
  169.4 16.3 %collective-permute-start.29 = (bf16[2,3,40,1280]{3,2,1,0:T(8,128)(2,1)S(1)}, bf16[2,3,40,1280]{3,2,1,0:T(8,128)(2,1)S(1)}, u32[]{:S(2)}, u32[]{:S(2)}) collective-permute-start(bf16[2,3,40,1280]{3,2,1,0:T(8,128)(2,1)S(1)} %get-tuple-element.161), channel_id=1, source_target_pairs={{0,4},{4,0},{1,5},{5,1},{2,6},{6,2},{3,7},{7,3},{8,12},{12,8},{9,1... | collective-permute-start | bytes 1843208 | tf_op jit(solution)/shard_map/ppermute | solution.py:349
  170.2 16.0 %collective-permute-start.30 = (bf16[2,3,40,1280]{3,2,1,0:T(8,128)(2,1)S(1)}, bf16[2,3,40,1280]{3,2,1,0:T(8,128)(2,1)S(1)}, u32[]{:S(2)}, u32[]{:S(2)}) collective-permute-start(bf16[2,3,40,1280]{3,2,1,0:T(8,128)(2,1)S(1)} %get-tuple-element.162), channel_id=1, source_target_pairs={{0,1},{1,0},{2,3},{3,2},{4,5},{5,4},{6,7},{7,6},{8,9},{9,8},{10,11... | collective-permute-start | bytes 1843208 | tf_op jit(solution)/shard_map/ppermute | solution.py:347
  186.3 2.6 %copy-start.19 = (bf16[4,8,1280]{2,1,0:T(8,128)(2,1)S(1)}, bf16[4,8,1280]{2,1,0:T(8,128)(2,1)}, u32[]{:S(2)}) copy-start(bf16[4,8,1280]{2,1,0:T(8,128)(2,1)} %get-tuple-element.165) | copy-start | bytes 245764
  187.6 17.3 %copy-start.10 = (f32[128,1280]{1,0:T(8,128)S(1)}, f32[128,1280]{1,0:T(8,128)}, u32[]{:S(2)}) copy-start(f32[128,1280]{1,0:T(8,128)} %copy-done.9) | copy-start | bytes 1966084
  187.6 10.9 %collective-permute-start.31 = (bf16[128,1280]{1,0:T(8,128)(2,1)}, bf16[128,1280]{1,0:T(8,128)(2,1)S(1)}, u32[]{:S(2)}, u32[]{:S(2)}) collective-permute-start(bf16[128,1280]{1,0:T(8,128)(2,1)} %get-tuple-element.163), channel_id=1, source_target_pairs={{0,1},{1,0},{2,3},{3,2},{4,5},{5,4},{6,7},{7,6},{8,9},{9,8},{10,11... | collective-permute-start | bytes 983048 | tf_op jit(solution)/shard_map/ppermute | solution.py:347
  188.9 6.2 %collective-permute-start.32 = (bf16[4,8,1280]{2,1,0:T(8,128)(2,1)S(1)}, bf16[4,8,1280]{2,1,0:T(8,128)(2,1)S(1)}, u32[]{:S(2)}, u32[]{:S(2)}) collective-permute-start(bf16[4,8,1280]{2,1,0:T(8,128)(2,1)S(1)} %copy-done.19), channel_id=1, source_target_pairs={{0,16},{8,24},{16,0},{24,8},{1,17},{9,25},{17,1},{25,9},{2,18},{10... | collective-permute-start | bytes 245768 | tf_op jit(solution)/shard_map/ppermute | solution.py:358
  188.9 16.0 %collective-permute-start.33 = (bf16[128,1280]{1,0:T(8,128)(2,1)}, bf16[128,1280]{1,0:T(8,128)(2,1)S(1)}, u32[]{:S(2)}, u32[]{:S(2)}) collective-permute-start(bf16[128,1280]{1,0:T(8,128)(2,1)} %get-tuple-element.170), channel_id=1, source_target_pairs={{0,4},{4,0},{1,5},{5,1},{2,6},{6,2},{3,7},{7,3},{8,12},{12,8},{9,1... | collective-permute-start | bytes 983048 | tf_op jit(solution)/shard_map/ppermute | solution.py:349
  190.0 14.9 %collective-permute-start.34 = (bf16[128,1280]{1,0:T(8,128)(2,1)S(1)}, bf16[128,1280]{1,0:T(8,128)(2,1)S(1)}, u32[]{:S(2)}, u32[]{:S(2)}) collective-permute-start(bf16[128,1280]{1,0:T(8,128)(2,1)S(1)} %get-tuple-element.171), channel_id=1, source_target_pairs={{0,5},{1,4},{4,1},{5,0},{2,7},{3,6},{6,3},{7,2},{8,13},{9,12},{12,... | collective-permute-start | bytes 983048 | tf_op jit(solution)/shard_map/ppermute | solution.py:350
  200.4 11.2 %all-to-all-start.2 = ((bf16[8,48,480]{2,1,0:T(8,128)(2,1)}), bf16[8,48,480]{2,1,0:T(8,128)(2,1)S(1)}, u32[]{:S(2)}, u32[]{:S(2)}) async-start(bf16[8,48,480]{2,1,0:T(8,128)(2,1)} %fold.1), calls=%async_computation.3 | async-start | bytes 786432 | tf_op jit(solution)/shard_map/all_to_all | solution.py:909
  205.9 17.1 %collective-permute-start.35 = (bf16[4,8,1280]{2,1,0:T(8,128)(2,1)S(1)}, bf16[4,8,1280]{2,1,0:T(8,128)(2,1)S(1)}, u32[]{:S(2)}, u32[]{:S(2)}) collective-permute-start(bf16[4,8,1280]{2,1,0:T(8,128)(2,1)S(1)} %get-tuple-element.173), channel_id=1, source_target_pairs={{0,24},{8,0},{16,8},{24,16},{1,25},{9,1},{17,9},{25,17},{2,26},{10... | collective-permute-start | bytes 245768 | tf_op jit(solution)/shard_map/ppermute | solution.py:358
  210.4 12.6 %collective-permute-start.36 = (bf16[4,8,1280]{2,1,0:T(8,128)(2,1)S(1)}, bf16[4,8,1280]{2,1,0:T(8,128)(2,1)S(1)}, u32[]{:S(2)}, u32[]{:S(2)}) collective-permute-start(bf16[4,8,1280]{2,1,0:T(8,128)(2,1)S(1)} %get-tuple-element.174), channel_id=1, source_target_pairs={{0,16},{8,24},{16,0},{24,8},{1,17},{9,25},{17,1},{25,9},{2,18},{10... | collective-permute-start | bytes 245768 | tf_op jit(solution)/shard_map/ppermute | solution.py:358
  210.5 12.5 %collective-permute-start.37 = (bf16[4,8,1280]{2,1,0:T(8,128)(2,1)S(1)}, bf16[4,8,1280]{2,1,0:T(8,128)(2,1)S(1)}, u32[]{:S(2)}, u32[]{:S(2)}) collective-permute-start(bf16[4,8,1280]{2,1,0:T(8,128)(2,1)S(1)} %get-tuple-element.180), channel_id=1, source_target_pairs={{0,8},{8,16},{16,24},{24,0},{1,9},{9,17},{17,25},{25,1},{2,10},{10... | collective-permute-start | bytes 245768 | tf_op jit(solution)/shard_map/ppermute | solution.py:358
  (6 other events, 6.4 us)
Sparse Core Ops, SparseCore 0:
  10.4 34.5 all-gather.2
  51.4 37.5 all-gather.4
  150.2 32.4 reduce-scatter.2
  187.7 34.5 reduce-scatter.4
